TPU v7x, 32 devices: a whole 2x2x4 slice. The times are simulated.
32 devices in a mesh: dp: 8 (over y, x, core), expert: 4 (over z).
Axes of the slice: x: 2, y: 2, z: 4, core: 2. Of those that a mesh axis runs over, the one named last changes fastest.
Arguments:
- context: bfloat16 [4096, 4096], P('dp'), may hold values from -6 to 6
- out_weight: bfloat16 [4096, 4096], P('dp', 'expert'), may hold values from -0.09375 to 0.09375
- residual: bfloat16 [4096, 4096], P('dp', 'expert'), may hold values from -6 to 6
- gate_weight: bfloat16 [4, 4096, 8192], P('expert', None, 'dp'), may hold values from -0.09375 to 0.09375
- up_weight: bfloat16 [4, 4096, 8192], P('expert', None, 'dp'), may hold values from -0.09375 to 0.09375
- down_weight: bfloat16 [4, 8192, 4096], P('expert', 'dp'), may hold values from -0.0625 to 0.0625
- gate_values: float32 [4, 512], P('expert'), may hold values from 0.2 to 1
- chosen_blocks: int32 [4, 4], replicated, may hold values from 0 to 31, as said below
- block_counts: int32 [4], replicated, may hold values from 1 to 4, as said below
Outputs:
- mixed: bfloat16 [4096, 4096], P('dp', 'expert')
Inputs may be any that keep to these rules, and one draw needn't show every extreme that they name: `chosen_blocks`: within one expert the 4 block numbers are distinct; slots from block_counts on are unused but hold valid block numbers. `block_counts`: some expert uses all 4 slots.
All inputs are finite; a program needn't handle non-finite values.
Results may differ from a plain program's by a relative error of at most 0.008.
Values may be sent and summed in bfloat16 or wider, within the bound.
No kernel may reach another device: no remote copies, remote signals or barrier semaphores. Data moves between devices by JAX's collectives and lax.ppermute only.
A program may use at most 128 MiB of HBM per device.

v0:
```python
import jax
import jax.numpy as jnp
from jax import lax
from jax.sharding import PartitionSpec as P

BLK = 128
CAP = 4


def spread_2(value, axis, source):
    kept = jnp.where(lax.axis_index(axis) == source, value, 0).astype(value.dtype)
    return lax.psum(kept, axis)


def spread(selected, owners):
    return jnp.stack(
        [spread_2(selected[slot], "dp", owners[slot]) for slot in range(selected.shape[0])]
    )


def expert_block(inputs, w_gate, w_up, down_split, scale):
    gate = jnp.dot(inputs, w_gate, preferred_element_type=jnp.float32)
    upper = jnp.dot(inputs, w_up, preferred_element_type=jnp.float32)
    hidden = (jax.nn.silu(gate) * upper).astype(jnp.bfloat16)
    part = jnp.einsum("rf,fcd->crd", hidden, down_split, preferred_element_type=jnp.float32)
    return (part * scale[None, :, None]).astype(jnp.bfloat16)


def body(
    context,
    out_weight,
    residual,
    gate_weight,
    up_weight,
    down_weight,
    gate_values,
    chosen_blocks,
    block_counts,
):
    n_expert = lax.axis_size("expert")
    local_tokens = context.shape[0]
    local_width = residual.shape[1]
    model_width = context.shape[1]
    local_blocks = local_tokens // BLK
    my_expert = lax.axis_index("expert")
    my_data = lax.axis_index("dp")
    projected = jnp.dot(
        context,
        lax.all_gather(out_weight, "dp", axis=0, tiled=True),
        preferred_element_type=jnp.float32,
    )
    attended = (residual.astype(jnp.float32) + projected).astype(jnp.bfloat16)
    owners = chosen_blocks // local_blocks
    offsets = chosen_blocks % local_blocks
    my_owners = lax.dynamic_index_in_dim(owners, my_expert, 0, keepdims=False)
    my_offsets = lax.dynamic_index_in_dim(offsets, my_expert, 0, keepdims=False)
    whole = lax.all_gather(attended, "expert", axis=1, tiled=True)
    selected = whole.reshape(local_blocks, BLK, model_width)[my_offsets]
    picked = spread(selected, my_owners).reshape(CAP * BLK, model_width)
    w_gate = gate_weight[0]
    w_up = up_weight[0]
    down_split = down_weight[0].reshape(down_weight.shape[1], n_expert, local_width)
    gate_row = gate_values[0]
    my_count = lax.dynamic_index_in_dim(block_counts, my_expert, 0, keepdims=False)
    live = jnp.arange(CAP * BLK) // BLK < my_count
    scale = jnp.where(live, gate_row, jnp.zeros_like(gate_row))
    partial_value = expert_block(picked, w_gate, w_up, down_split, scale)
    received = lax.all_to_all(partial_value, "expert", split_axis=0, concat_axis=0, tiled=True)
    terms = received.reshape(n_expert * CAP * BLK, local_width).astype(jnp.float32)
    expert_out = lax.psum(terms.astype(jnp.bfloat16), "dp")
    expert_out = expert_out.reshape(n_expert * CAP, BLK, local_width)
    flat_owners = owners.reshape(-1)
    flat_offsets = offsets.reshape(-1)
    selector = (flat_owners[None, :] == my_data) & (
        flat_offsets[None, :] == jnp.arange(local_blocks)[:, None]
    )
    added = jnp.einsum(
        "bs,srd->brd", selector.astype(jnp.bfloat16), expert_out, preferred_element_type=jnp.float32
    )
    total = attended.astype(jnp.float32).reshape(local_blocks, BLK, local_width) + added
    return total.reshape(local_tokens, local_width).astype(jnp.bfloat16)


def solution(mesh):
    in_specs = (
        P("dp", None),
        P("dp", "expert"),
        P("dp", "expert"),
        P("expert", None, "dp"),
        P("expert", None, "dp"),
        P("expert", "dp", None),
        P("expert", None),
        P(),
        P(),
    )
    out_specs = P("dp", "expert")
    return jax.shard_map(body, mesh=mesh, in_specs=in_specs, out_specs=out_specs, check_vma=False)
```

profile of v0, /device:TPU:0, one launch (start us, length us, event | category | flops | bytes accessed | tf_op | source)
XLA Modules:
  0.0 471.0 jit_solution(2343656891259071819)
XLA Ops:
  6.5 0.0 all-gather.3.cloned.1.call-start
  6.5 0.7 all-gather.3.cloned.1.call-update
  7.3 0.0 copy-start.2
  7.3 0.0 all-gather.5.cloned.1.call-start
  7.3 59.1 %all-gather.3.cloned.1.call-done = bf16[4096,1024]{1,0:T(8,128)(2,1)} async-done(((bf16[512,1024]{1,0:T(8,128)(2,1)}), bf16[4096,1024]{1,0:T(8,128)(2,1)}) %all-gather.3.cloned.1.call-update) | async-done | bytes 8388624 | tf_op jit(solution)/shard_map/all_gather | solution.py:49
  66.4 10.3 %add_convert_fusion = bf16[512,1024]{1,0:T(8,128)(2,1)} fusion(bf16[512,1024]{1,0:T(8,128)(2,1)} %param.11, bf16[512,4096]{1,0:T(8,128)(2,1)} %param.9, bf16[4096,1024]{1,0:T(8,128)(2,1)} %all-gather.3.cloned.1.call-done), kind=kOutput, calls=%fused_computation.13 | convolution fusion | flops 4296540160 | bytes 14680064 | tf_op jit(solution)/shard_map/dot_general | solution.py:47
  76.6 0.0 all-gather.5.cloned.1.call-update
  76.7 0.0 all-reduce.6.cloned.1.call-start
  76.7 0.0 copy-done.2
  76.8 0.6 fusion.31
  80.0 77.6 %all-gather.5.cloned.1.call-done = bf16[512,4096]{1,0:T(8,128)(2,1)} async-done(((bf16[512,1024]{1,0:T(8,128)(2,1)}), bf16[512,4096]{1,0:T(8,128)(2,1)}) %all-gather.5.cloned.1.call-update) | async-done | bytes 4194320 | tf_op jit(solution)/shard_map/all_gather | solution.py:57
  157.6 5.0 %gather_fusion = bf16[4,128,4096]{2,1,0:T(8,128)(2,1)} fusion(bf16[4,128,4096]{2,1,0:T(8,128)(2,1)} %bitcast.43, s32[1024]{0:T(1024)S(1)} %pad_clamp_fusion), kind=kCustom, calls=%fused_computation | custom fusion | bytes 8388624 | tf_op jit(solution)/shard_map/gather | solution.py:58
  162.6 4.2 slice_select_fusion.3
  166.8 0.0 copy-start.4
  166.8 0.0 all-reduce.6.cloned.1.call-update
  166.8 0.2 all-reduce.4.cloned.1.call-start
  167.0 0.4 copy-done.4
  167.4 0.6 dynamic_slice.13
  168.1 0.0 copy-start.3
  168.1 14.8 %reshape_squeeze.3 = bf16[1024,4,1024]{2,1,0:T(4,128)(2,1)} reshape(bf16[1,1024,4096]{2,1,0:T(8,128)(2,1)} %param.14) | data formatting | bytes 16777216 | tf_op jit(solution)/shard_map/reshape;squeeze | solution.py:62
  182.8 0.0 copy-done.3
  182.9 0.6 fusion.20
  183.5 63.6 %all-reduce.6.cloned.1.call-done = (bf16[1,128,4096]{2,1,0:T(8,128)(2,1)}, bf16[1,128,4096]{2,1,0:T(8,128)(2,1)}, bf16[1,128,4096]{2,1,0:T(8,128)(2,1)}, bf16[1,128,4096]{2,1,0:T(8,128)(2,1)}) async-done(((bf16[1,128,4096]{2,1,0:T(8,128)(2,1)}, bf16[1,128,4096]{2,1,0:T(8,128)(2,1)}, bf16[1,128,4096]{2,1,0:T(8,128)(2,1)}, bf16[1,128,4096]{2,1,0:T(8,128)(2,1)}), (bf16[1,128,4096]{2,1,0:T(8,128)(2,1)}, ...) | async-done | bytes 4194320 | tf_op jit(solution)/shard_map/psum | solution.py:12
  247.1 2.4 pad_maximum_fusion
  249.5 0.0 copy-start
  249.5 2.0 copy-done
  251.5 6.9 %fusion.2 = f32[512,1024]{1,0:T(8,128)S(1)} fusion(bf16[512,4096]{1,0:T(8,128)(2,1)S(1)} %bitcast.44, bf16[1,4096,1024]{2,1,0:T(8,128)(2,1)} %param.12), kind=kOutput, calls=%fused_computation.3 | convolution fusion | flops 4294967296 | bytes 14680064 | tf_op jit(solution)/shard_map/dot_general | solution.py:22
  258.3 19.1 %fusion.6 = bf16[4,512,1024]{2,1,0:T(8,128)(2,1)} fusion(f32[512]{0:T(512)S(1)} %fusion.20, bf16[1024,4,1024]{2,1,0:T(4,128)(2,1)} %reshape_squeeze.3, bf16[512,4096]{1,0:T(8,128)(2,1)} %bitcast.45, bf16[1,4096,1024]{2,1,0:T(8,128)(2,1)} %param.13, f32[512,1024]{1,0:T(8,128)S(1)} %fusion.2), kind=kOutput, calls=%fused_computation.8 | convolution fusion | flops 8597274624 | bytes 27265024 | tf_op jit(solution)/shard_map/rf,fcd->crd/dot_general | solution.py:25
  277.5 97.7 %all_to_all.5 = bf16[4,512,1024]{2,1,0:T(8,128)(2,1)S(1)} all-to-all(bf16[4,512,1024]{2,1,0:T(8,128)(2,1)} %fusion.6), channel_id=1, replica_groups=mesh['dp'=8,'expert'=4] {'expert'}, dimensions={0} | all-to-all | bytes 8388608 | tf_op jit(solution)/shard_map/all_to_all | solution.py:68
  375.1 4.3 copy.18
  379.5 0.0 all-reduce.4.cloned.1.call-update
  379.5 0.0 copy-start.1
  379.5 0.1 eq.46
  379.6 0.1 eq.45
  379.7 79.7 %all-reduce.4.cloned.1.call-done = bf16[16,128,1024]{2,0,1:T(8,128)(2,1)} async-done(((bf16[16,128,1024]{2,0,1:T(8,128)(2,1)}), bf16[16,128,1024]{2,0,1:T(8,128)(2,1)}) %all-reduce.4.cloned.1.call-update) | async-done | bytes 4194320 | tf_op jit(solution)/shard_map/psum | solution.py:70
  459.3 2.9 fusion.25
  462.3 0.0 copy-done.1
  462.3 2.2 fusion.9
  (5 shorter events, 0.1 us)
Async XLA Ops:
  6.5 59.8 %all-gather.3.cloned.1.call-start = ((), (), s32[]{:S(2)}) async-start(), calls=%async_computation.1 | async-start | bytes 9437184 | tf_op jit(solution)/shard_map/all_gather | solution.py:49
  7.3 69.5 %copy-start.2 = (s32[4,4]{1,0:T(4,128)S(1)}, s32[4,4]{1,0:T(4,128)}, u32[]{:S(2)}) copy-start(s32[4,4]{1,0:T(4,128)} %param.16) | copy-start | bytes 196
  7.3 150.3 %all-gather.5.cloned.1.call-start = ((), (), s32[]{:S(2)}) async-start(), calls=%async_computation.2 | async-start | bytes 5242880 | tf_op jit(solution)/shard_map/all_gather | solution.py:57
  76.7 170.4 %all-reduce.6.cloned.1.call-start = ((), (), s32[]{:S(2)}) async-start(), calls=%async_computation.4 | async-start | bytes 8388608 | tf_op jit(solution)/shard_map/psum | solution.py:12
  166.8 0.7 copy-start.4
  166.8 292.5 %all-reduce.4.cloned.1.call-start = ((), (), s32[]{:S(2)}) async-start(), calls=%async_computation.3 | async-start | bytes 8388608 | tf_op jit(solution)/shard_map/psum | solution.py:70
  168.1 14.8 %copy-start.3 = (f32[1,512]{1,0:T(1,128)S(1)}, f32[1,512]{1,0:T(1,128)}, u32[]{:S(2)}) copy-start(f32[1,512]{1,0:T(1,128)} %param.15) | copy-start | bytes 6148
  249.5 2.0 copy-start
  379.5 82.8 %copy-start.1 = (bf16[512,1024]{1,0:T(8,128)(2,1)S(1)}, bf16[512,1024]{1,0:T(8,128)(2,1)}, u32[]{:S(2)}) copy-start(bf16[512,1024]{1,0:T(8,128)(2,1)} %add_convert_fusion) | copy-start | bytes 3145732
Sparse Core Ops, SparseCore 0:
  9.2 57.0 all-gather.2
  76.8 80.7 all-gather.4
  166.9 80.0 all-reduce.5
  379.6 79.6 all-reduce.3
where the time goes:
time: 472 us; the launch traced here: 471 us
  waiting for transfers between devices  281 us (60%)
  blocking collectives  97.7 us (21%)
  matrix products  39.2 us (8%)
  local copies, waits for them, and re-layouts  27.9 us (6%)
  between operations  15.8 us (3%)
  other arithmetic  9.51 us (2%)
    all_to_all x1, blocking collectives, body(): lax.all_to_all(partial_value, 'expert', split_axis=0, concat_axis=0, tile...  97.7 us
    psum x1, waiting for transfers between devices, body(): expert_out = lax.psum(terms.astype(jnp.bfloat16), 'dp')  79.7 us
    all_gather x1, waiting for transfers between devices, body(): whole = lax.all_gather(attended, 'expert', axis=1, tiled=True)  77.6 us
    psum x1, waiting for transfers between devices, spread_2(): return lax.psum(kept, axis)  63.6 us
    all_gather x1, waiting for transfers between devices, body(): lax.all_gather(out_weight, 'dp', axis=0, tiled=True)  59.1 us
    dot_general x1, matrix products, expert_block(): jnp.einsum('rf,fcd->crd', hidden, down_split, preferred_element_type=jnp....  19.1 us
    another operation x1, local copies, waits for them, and re-layouts, body(): down_weight[0].reshape(down_weight.shape[1], n_expert, local_width)  14.8 us
    dot_general x1, matrix products, body(): jnp.dot(context, lax.all_gather(out_weight, 'dp', axis=0, tiled=True), pr...  10.3 us
  transfers between devices with their start and end apart: 4, of which 4 were waited for; matrix products, arithmetic and copies ran while one was open for 4% of the time, Pallas kernels for 0%

commit v1 on v0

v1 whole, which is shorter than its diff:
```python
import jax
import jax.numpy as jnp
from jax import lax
from jax.experimental import pallas as pl
from jax.experimental.pallas import tpu as pltpu
from jax.sharding import PartitionSpec as P

BLK = 128
CAP = 4
GROUPS = 2
VMEM_LIMIT = 48 * 1024 * 1024


def bit_orders(n_bits):
    forward = list(range(1, n_bits + 1))
    return forward, forward[::-1]


def step_pairs(n_dp, step):
    orders = bit_orders(n_dp.bit_length() - 2)
    return [(i, i ^ (1 << orders[i & 1][step])) for i in range(n_dp)]


def pair_pairs(n_dp):
    return [(i, i ^ 1) for i in range(n_dp)]


def masks_of(n_bits, side):
    order = bit_orders(n_bits)[side]
    return [
        sum(1 << (order[t] - 1) for t in range(n_bits) if (r >> t) & 1) for r in range(1 << n_bits)
    ]


def bit_reversed(n_bits):
    return [
        sum(1 << (n_bits - 1 - t) for t in range(n_bits) if (r >> t) & 1)
        for r in range(1 << n_bits)
    ]


def scatter_sum(buf, n_dp, n_bits):
    for step in range(n_bits - 1, -1, -1):
        half = 1 << step
        got = lax.ppermute(buf[half:], "dp", step_pairs(n_dp, step))
        buf = (buf[:half].astype(jnp.float32) + got.astype(jnp.float32)).astype(buf.dtype)
    return buf[0]


def gather_all(piece, n_dp, n_bits):
    buf = piece[None]
    for step in range(n_bits):
        got = lax.ppermute(buf, "dp", step_pairs(n_dp, step))
        buf = jnp.concatenate([buf, got], axis=0)
    return buf


def swap_planes(parts, n_expert):
    out = [parts[0]]
    for k in range(1, n_expert):
        pairs = [(i, (i + k) % n_expert) for i in range(n_expert)]
        out.append(lax.ppermute(parts[k], "expert", pairs))
    return jnp.stack(out)


def pick_kernel(idx_ref, att_ref, out_ref):
    for i in range(out_ref.shape[0]):
        idx = idx_ref[i]
        value = att_ref[jnp.maximum(idx, 0)]
        out_ref[i] = jnp.where(idx >= 0, value, jnp.zeros_like(value))


def pick(idx, attended):
    return pl.pallas_call(
        pick_kernel,
        out_shape=jax.ShapeDtypeStruct((idx.shape[0],) + attended.shape[1:], attended.dtype),
        in_specs=[
            pl.BlockSpec(memory_space=pltpu.SMEM),
            pl.BlockSpec(memory_space=pltpu.VMEM),
        ],
        out_specs=pl.BlockSpec(memory_space=pltpu.VMEM),
        compiler_params=pltpu.CompilerParams(vmem_limit_bytes=VMEM_LIMIT),
        name="pick_blocks",
    )(idx, attended)


def finish_kernel(idx_ref, att_ref, *refs):
    pieces, out_ref, acc = refs[:-2], refs[-2], refs[-1]
    acc[...] = att_ref[...].astype(jnp.float32)
    at = 0
    for piece in pieces:
        for i in range(piece.shape[0]):
            idx = idx_ref[at]
            at += 1

            @pl.when(idx >= 0)
            def _():
                acc[idx] = acc[idx] + piece[i].astype(jnp.float32)

    out_ref[...] = acc[...].astype(out_ref.dtype)


def finish(idx, attended, pieces):
    return pl.pallas_call(
        finish_kernel,
        out_shape=jax.ShapeDtypeStruct(attended.shape, attended.dtype),
        in_specs=[pl.BlockSpec(memory_space=pltpu.SMEM)]
        + [pl.BlockSpec(memory_space=pltpu.VMEM)] * (1 + len(pieces)),
        out_specs=pl.BlockSpec(memory_space=pltpu.VMEM),
        scratch_shapes=[pltpu.VMEM(attended.shape, jnp.float32)],
        compiler_params=pltpu.CompilerParams(vmem_limit_bytes=VMEM_LIMIT),
        name="add_expert_rows",
    )(idx, attended, *pieces)


def mlp_kernel(n_k, kidx, nidx, x_ref, wg_ref, wu_ref, wd_ref, scale_ref, out_ref, gate, up, hidden):
    step = pl.program_id(0)
    rows = gate.shape[0]

    @pl.when(step < n_k)
    def _():
        x = x_ref[...].reshape(rows, x_ref.shape[-1])
        g = jnp.dot(x, wg_ref[...], preferred_element_type=jnp.float32)
        u = jnp.dot(x, wu_ref[...], preferred_element_type=jnp.float32)

        @pl.when(step == 0)
        def _():
            gate[...] = g
            up[...] = u

        @pl.when(step > 0)
        def _():
            gate[...] += g
            up[...] += u

    @pl.when(step == n_k - 1)
    def _():
        v = gate[...]
        hidden[...] = (v / (1.0 + jnp.exp(-v)) * up[...]).astype(jnp.bfloat16)

    @pl.when(step >= n_k)
    def _():
        part = jnp.dot(hidden[...], wd_ref[...], preferred_element_type=jnp.float32)
        out_ref[...] = (part * scale_ref[...]).astype(out_ref.dtype).reshape(out_ref.shape)


def mlp(x, kidx, nidx, w_gate, w_up, w_down, scale):
    n_side, n_rel, n_z, rows, width = x.shape
    n_k = n_side * n_z
    ff = w_gate.shape[1]
    total = n_rel * rows

    def x_map(i, kidx, nidx):
        k = jnp.minimum(i, n_k - 1)
        return k // n_z, 0, k % n_z, 0, 0

    def k_map(i, kidx, nidx):
        return kidx[jnp.minimum(i, n_k - 1)], 0

    def n_map(i, kidx, nidx):
        return 0, nidx[jnp.maximum(i - n_k, 0)]

    def o_map(i, kidx, nidx):
        n = jnp.maximum(i - n_k, 0)
        return n // n_z, 0, n % n_z, 0, 0

    return pl.pallas_call(
        lambda *refs: mlp_kernel(n_k, *refs),
        out_shape=jax.ShapeDtypeStruct(x.shape, jnp.bfloat16),
        grid_spec=pltpu.PrefetchScalarGridSpec(
            num_scalar_prefetch=2,
            grid=(2 * n_k,),
            in_specs=[
                pl.BlockSpec((1, n_rel, 1, rows, width), x_map),
                pl.BlockSpec((width, ff), k_map),
                pl.BlockSpec((width, ff), k_map),
                pl.BlockSpec((ff, width), n_map),
                pl.BlockSpec((total, 1), lambda i, kidx, nidx: (0, 0)),
            ],
            out_specs=pl.BlockSpec((1, n_rel, 1, rows, width), o_map),
            scratch_shapes=[
                pltpu.VMEM((total, ff), jnp.float32),
                pltpu.VMEM((total, ff), jnp.float32),
                pltpu.VMEM((total, ff), jnp.bfloat16),
            ],
        ),
        compiler_params=pltpu.CompilerParams(vmem_limit_bytes=VMEM_LIMIT),
        cost_estimate=pl.CostEstimate(
            flops=6 * total * ff * n_k * width,
            bytes_accessed=6 * ff * n_k * width,
            transcendentals=total * ff,
        ),
        name="expert_mlp",
    )(kidx, nidx, x, w_gate, w_up, w_down, scale)


def body(
    context,
    out_weight,
    residual,
    gate_weight,
    up_weight,
    down_weight,
    gate_values,
    chosen_blocks,
    block_counts,
):
    n_expert = lax.axis_size("expert")
    n_dp = lax.axis_size("dp")
    n_bits = n_dp.bit_length() - 2
    n_chip = 1 << n_bits
    local_tokens, model_width = context.shape
    local_width = residual.shape[1]
    half = local_width // 2
    depth = out_weight.shape[0]
    local_blocks = local_tokens // BLK
    my_expert = lax.axis_index("expert")
    my_data = lax.axis_index("dp")
    chip, side = my_data // 2, my_data % 2
    masks = jnp.where(
        side == 0,
        jnp.array(masks_of(n_bits, 0), jnp.int32),
        jnp.array(masks_of(n_bits, 1), jnp.int32),
    )
    chips = chip ^ masks
    reverse = bit_reversed(n_bits)
    pair = pair_pairs(n_dp)

    def split_sides(value):
        own = lax.dynamic_slice_in_dim(value, side * half, half, axis=1)
        other = lax.dynamic_slice_in_dim(value, (1 - side) * half, half, axis=1)
        return own, lax.ppermute(other, "dp", pair)

    w_piece = jnp.concatenate(split_sides(out_weight), axis=0)
    pieces = [w_piece]
    for step in range(n_bits):
        pieces = pieces + [lax.ppermute(p, "dp", step_pairs(n_dp, step)) for p in pieces]
    context_pair = jnp.concatenate([context, lax.ppermute(context, "dp", pair)], axis=0)
    residual_pair = jnp.concatenate(split_sides(residual), axis=0)
    projected = jnp.zeros((2 * local_tokens, half), jnp.float32)
    for r in range(n_chip):
        columns = jnp.concatenate(
            [
                lax.dynamic_slice_in_dim(context_pair, (chips[r] * 2 + s) * depth, depth, axis=1)
                for s in (side, 1 - side)
            ],
            axis=1,
        )
        projected = projected + jnp.dot(columns, pieces[r], preferred_element_type=jnp.float32)
    attended = (residual_pair.astype(jnp.float32) + projected).astype(jnp.bfloat16)

    group_rows = CAP * BLK // GROUPS
    share = group_rows // n_chip
    grains = attended.reshape(-1, share, half)
    per_block = BLK // share

    def grain_index(group, experts):
        row = group * group_rows + chips * share
        block = chosen_blocks[experts[None, :], (row // BLK)[:, None]]
        owner = block // local_blocks
        mine = owner // 2 == chip
        first = jnp.where(owner % 2 == side, 0, local_blocks) + block % local_blocks
        index = first * per_block + ((row % BLK) // share)[:, None]
        return jnp.where(mine, index, -1).reshape(-1).astype(jnp.int32)

    ahead = (my_expert + jnp.arange(n_expert)) % n_expert
    behind = (my_expert - jnp.arange(n_expert)) % n_expert
    my_count = lax.dynamic_index_in_dim(block_counts, my_expert, 0, keepdims=False)
    live = jnp.arange(CAP * BLK) // BLK < my_count
    scale_all = jnp.where(live, gate_values[0], 0.0).reshape(GROUPS, n_chip, share)
    sides = jnp.stack([side, 1 - side])
    kidx = (behind[None, :] * 2 + sides[:, None]).reshape(-1).astype(jnp.int32)
    nidx = (ahead[None, :] * 2 + sides[:, None]).reshape(-1).astype(jnp.int32)
    w_gate, w_up, w_down = gate_weight[0], up_weight[0], down_weight[0]
    reverse_index = jnp.array(reverse)

    received = []
    for group in range(GROUPS):
        masked = pick(grain_index(group, ahead), grains).reshape(n_chip, n_expert, share, half)
        mine = scatter_sum(masked, n_dp, n_bits)
        crossed = swap_planes(mine, n_expert)
        own_half = gather_all(crossed, n_dp, n_bits)
        to_other = jnp.stack([own_half[r] for r in reverse])
        picked = jnp.stack([own_half, lax.ppermute(to_other, "dp", pair)])
        scale = scale_all[group][chips].reshape(-1, 1)
        part = mlp(picked, kidx, nidx, w_gate, w_up, w_down, scale)
        to_other = jnp.stack([part[1, r] for r in reverse])
        got = lax.ppermute(to_other, "dp", pair)
        both = (part[0].astype(jnp.float32) + got.astype(jnp.float32)).astype(jnp.bfloat16)
        mine = scatter_sum(both, n_dp, n_bits)
        crossed = swap_planes(mine, n_expert)
        received.append(gather_all(crossed, n_dp, n_bits).reshape(-1, share, half))

    index = jnp.concatenate([grain_index(group, behind) for group in range(GROUPS)])
    mixed = finish(index, grains, received).reshape(2, local_tokens, half)
    got = lax.ppermute(mixed[1], "dp", pair)
    return jnp.where(
        side == 0,
        jnp.concatenate([mixed[0], got], axis=1),
        jnp.concatenate([got, mixed[0]], axis=1),
    )


def solution(mesh):
    in_specs = (
        P("dp", None),
        P("dp", "expert"),
        P("dp", "expert"),
        P("expert", None, "dp"),
        P("expert", None, "dp"),
        P("expert", "dp", None),
        P("expert", None),
        P(),
        P(),
    )
    out_specs = P("dp", "expert")
    return jax.shard_map(body, mesh=mesh, in_specs=in_specs, out_specs=out_specs, check_vma=False)
```

time: 472 us -> 218 us (0.46)
  waiting for transfers between devices: 281 us -> 89.6 us
  blocking collectives: 97.7 us -> 0 us
  Pallas kernels: 0 us -> 41.9 us
  starting transfers between devices: 0.31 us -> 40.8 us
  matrix products: 39.2 us -> 10.3 us
  between operations: 15.8 us -> 3.04 us
  local copies, waits for them, and re-layouts: 27.9 us -> 17.9 us
    psum x2 -> x0, waiting for transfers between devices: 143 us -> none  [the longest x1 79.7 us: body(): expert_out = lax.psum(terms.astype(jnp.bfloat16), 'dp')]
    all_gather x2 -> x0, waiting for transfers between devices: 137 us -> none  [the longest x1 77.6 us: body(): whole = lax.all_gather(attended, 'expert', axis=1, tiled=True)]
    all_to_all x1 -> x0, blocking collectives: 97.7 us -> none  [body(): lax.all_to_all(partial_value, 'expert', split_axis=0, concat_axis=0, tile...]
    ppermute x0 -> x39, waiting for transfers between devices: none -> 89.6 us  [the longest x8 34.4 us: gather_all(): got = lax.ppermute(buf, 'dp', step_pairs(n_dp, step))]
    pallas_call x0 -> x5, Pallas kernels: none -> 41.9 us  [the longest x2 39.4 us: mlp(): pl.pallas_call(lambda *refs: mlp_kernel(n_k, *refs), out_shape=jax.ShapeD...]
    ppermute x0 -> x39, starting transfers between devices: none -> 40.8 us  [the longest x12 17.2 us: swap_planes(): out.append(lax.ppermute(parts[k], 'expert', pairs))]
    dot_general x4, matrix products: 39.2 us -> 10.3 us  [body(): jnp.dot(columns, pieces[r], preferred_element_type=jnp.float32)]
    another operation x1 -> x2, local copies, waits for them, and re-layouts: 14.8 us -> 0.18 us  [body(): to_other = jnp.stack([part[1, r] for r in reverse])]
  transfers between devices with their start and end apart: 4 -> 39, of which waited for: 4 -> 28; matrix products, arithmetic and copies ran while one was open for 4% -> 16% of each run, Pallas kernels for 0% -> 19%
where the time goes in v1:
time: 218 us; the launch traced here: 216 us
  waiting for transfers between devices  89.6 us (41%)
  Pallas kernels  41.9 us (19%)
  starting transfers between devices  40.8 us (19%)
  local copies, waits for them, and re-layouts  17.9 us (8%)
  other arithmetic  12.3 us (6%)
  matrix products  10.3 us (5%)
  between operations  3.04 us (1%)
    pallas_call x2, Pallas kernels, mlp(): pl.pallas_call(lambda *refs: mlp_kernel(n_k, *refs), out_shape=jax.ShapeD...  39.4 us
    ppermute x8, waiting for transfers between devices, gather_all(): got = lax.ppermute(buf, 'dp', step_pairs(n_dp, step))  34.4 us
    ppermute x8, waiting for transfers between devices, scatter_sum(): got = lax.ppermute(buf[half:], 'dp', step_pairs(n_dp, step))  29.1 us
    ppermute x12, starting transfers between devices, swap_planes(): out.append(lax.ppermute(parts[k], 'expert', pairs))  17.2 us
    dot_general x4, matrix products, body(): jnp.dot(columns, pieces[r], preferred_element_type=jnp.float32)  10.3 us
    ppermute x3, waiting for transfers between devices, body(): lax.ppermute(p, 'dp', step_pairs(n_dp, step))  8.77 us
    ppermute x3, starting transfers between devices, body(): lax.ppermute(p, 'dp', step_pairs(n_dp, step))  8.19 us
    ppermute x12, waiting for transfers between devices, swap_planes(): out.append(lax.ppermute(parts[k], 'expert', pairs))  8.03 us
  transfers between devices with their start and end apart: 39, of which 28 were waited for; matrix products, arithmetic and copies ran while one was open for 16% of the time, Pallas kernels for 19%

profile of v1, /device:TPU:0, one launch (start us, length us, event | category | flops | bytes accessed | tf_op | source)
XLA Modules:
  0.0 215.8 jit_solution(18315959125845644644)
XLA Ops:
  0.5 2.1 constant_dynamic-slice_fusion.7
  3.4 5.7 %collective-permute-done.2 = bf16[512,512]{1,0:T(8,128)(2,1)} collective-permute-done((bf16[512,512]{1,0:T(8,128)(2,1)}, bf16[512,512]{1,0:T(8,128)(2,1)}, u32[]{:S(2)}, u32[]{:S(2)}) %collective-permute-start.2) | collective-permute-done | bytes 524320 | tf_op jit(solution)/shard_map/ppermute | solution.py:232
  9.1 2.1 pad_maximum_fusion.6
  11.2 2.9 %collective-permute-start.3 = (bf16[1024,512]{1,0:T(8,128)(2,1)}, bf16[1024,512]{1,0:T(8,128)(2,1)}, u32[]{:S(2)}, u32[]{:S(2)}) collective-permute-start(bf16[1024,512]{1,0:T(8,128)(2,1)} %pad_maximum_fusion.6), channel_id=1, source_target_pairs={{0,8},{4,20},{8,0},{12,28},{16,24},{20,4},{24,16},{28,12},{1,9},{5... | collective-permute-start | bytes 3145736 | tf_op jit(solution)/shard_map/ppermute | solution.py:237
  18.1 0.7 gather_fusion.4
  19.0 0.7 gather_fusion
  19.8 0.7 gather_fusion.2
  20.7 2.7 %constant_dynamic-update-slice_fusion.1 = bf16[1024,4096]{1,0:T(8,128)(2,1)S(1)} fusion(bf16[512,4096]{1,0:T(8,128)(2,1)} %param.11), kind=kLoop, calls=%fused_computation.99 | loop fusion | bytes 8388608
  23.4 1.6 collective-permute-start.4
  25.0 3.0 %collective-permute-done.3 = bf16[1024,512]{1,0:T(8,128)(2,1)} collective-permute-done((bf16[1024,512]{1,0:T(8,128)(2,1)}, bf16[1024,512]{1,0:T(8,128)(2,1)}, u32[]{:S(2)}, u32[]{:S(2)}) %collective-permute-start.3) | collective-permute-done | bytes 1048608 | tf_op jit(solution)/shard_map/ppermute | solution.py:237
  28.0 3.7 %collective-permute-start.5 = (bf16[1024,512]{1,0:T(8,128)(2,1)}, bf16[1024,512]{1,0:T(8,128)(2,1)}, u32[]{:S(2)}, u32[]{:S(2)}) collective-permute-start(bf16[1024,512]{1,0:T(8,128)(2,1)} %collective-permute-done.3), channel_id=1, source_target_pairs={{0,16},{4,12},{8,24},{12,4},{16,0},{20,28},{24,8},{28,20},{1,17},{... | collective-permute-start | bytes 3145736 | tf_op jit(solution)/shard_map/ppermute | solution.py:237
  31.7 2.7 %constant_dynamic-update-slice_fusion = bf16[1024,4096]{1,0:T(8,128)(2,1)S(1)} fusion(bf16[1024,4096]{1,0:T(8,128)(2,1)S(1)} %constant_dynamic-update-slice_fusion.1, bf16[512,4096]{1,0:T(8,128)(2,1)} %collective-permute-done.1), kind=kLoop, calls=%fused_computation.98 | loop fusion | bytes 8388608 | tf_op jit(solution)/shard_map/concatenate | solution.py:238
  34.4 2.1 constant_dynamic-slice_fusion.1
  36.5 2.8 %fusion.4 = f32[1024,512]{1,0:T(8,128)S(1)} fusion(bf16[1024,512]{1,0:T(8,128)(2,1)} %collective-permute-done.3, bf16[1024,512]{1,0:T(8,128)(2,1)S(1)} %get-tuple-element.15, bf16[1024,512]{1,0:T(8,128)(2,1)} %get-tuple-element.16), kind=kOutput, calls=%fused_computation.10 | convolution fusion | flops 1077936128 | bytes 5242880 | tf_op jit(solution)/shard_map/dot_general | solution.py:249
  39.3 2.3 %fusion = f32[1024,512]{1,0:T(8,128)S(1)} fusion(bf16[1024,512]{1,0:T(8,128)(2,1)S(1)} %get-tuple-element.17, bf16[1024,512]{1,0:T(8,128)(2,1)S(1)} %get-tuple-element.18, bf16[512,512]{1,0:T(8,128)(2,1)} %collective-permute-done.2, bf16[512,512]{1,0:T(8,128)(2,1)S(1)} %get-tuple-element.35), kind=kOutput, calls=%fused_computation.6 | convolution fusion | flops 1080033280 | bytes 5242880 | tf_op jit(solution)/shard_map/dot_general | solution.py:249
  41.6 2.5 %fusion.8 = f32[1024,512]{1,0:T(8,128)S(1)} fusion(bf16[1024,512]{1,0:T(8,128)(2,1)} %collective-permute-done.4, bf16[1024,512]{1,0:T(8,128)(2,1)S(1)} %get-tuple-element.13, bf16[1024,512]{1,0:T(8,128)(2,1)S(1)} %get-tuple-element.14), kind=kOutput, calls=%fused_computation.14 | convolution fusion | flops 1077936128 | bytes 5242880 | tf_op jit(solution)/shard_map/dot_general | solution.py:249
  44.0 5.8 %collective-permute-done.5 = bf16[1024,512]{1,0:T(8,128)(2,1)} collective-permute-done((bf16[1024,512]{1,0:T(8,128)(2,1)}, bf16[1024,512]{1,0:T(8,128)(2,1)}, u32[]{:S(2)}, u32[]{:S(2)}) %collective-permute-start.5) | collective-permute-done | bytes 1048608 | tf_op jit(solution)/shard_map/ppermute | solution.py:237
  49.8 2.8 %add_convert_fusion = bf16[1024,512]{1,0:T(8,128)(2,1)S(1)} fusion(f32[1024,512]{1,0:T(8,128)S(1)} %fusion.8, f32[1024,512]{1,0:T(8,128)S(1)} %fusion, f32[1024,512]{1,0:T(8,128)S(1)} %fusion.4, bf16[1024,512]{1,0:T(8,128)(2,1)} %collective-permute-done.5, bf16[1024,512]{1,0:T(8,128)(2,1)S(1)} %get-tuple-element.12, ...), kind=kOutput, calls=%fused_computation.28 | convolution fusion | flops 1082654720 | bytes 11534336 | tf_op jit(solution)/shard_map/dot_general | solution.py:249
  53.4 1.6 collective-permute-start.22
  56.3 6.3 %collective-permute-done.22 = bf16[2,4,64,512]{3,2,1,0:T(8,128)(2,1)S(1)} collective-permute-done((bf16[2,4,64,512]{3,2,1,0:T(8,128)(2,1)S(1)}, bf16[2,4,64,512]{3,2,1,0:T(8,128)(2,1)S(1)}, u32[]{:S(2)}, u32[]{:S(2)}) %collective-permute-start.22) | collective-permute-done | bytes 524320 | tf_op jit(solution)/shard_map/ppermute | solution.py:45
  62.8 1.0 collective-permute-start.23
  63.8 7.2 %collective-permute-done.6 = bf16[2,4,64,512]{3,2,1,0:T(8,128)(2,1)S(1)} collective-permute-done((bf16[2,4,64,512]{3,2,1,0:T(8,128)(2,1)S(1)}, bf16[2,4,64,512]{3,2,1,0:T(8,128)(2,1)S(1)}, u32[]{:S(2)}, u32[]{:S(2)}) %collective-permute-start.6) | collective-permute-done | bytes 524320 | tf_op jit(solution)/shard_map/ppermute | solution.py:45
  71.3 1.0 collective-permute-start.7
  72.4 1.6 collective-permute-start.24
  74.0 2.6 %collective-permute-start.25 = (bf16[64,512]{1,0:T(8,128)(2,1)S(1)}, bf16[64,512]{1,0:T(8,128)(2,1)S(1)}, u32[]{:S(2)}, u32[]{:S(2)}) collective-permute-start(bf16[64,512]{1,0:T(8,128)(2,1)S(1)} %get-tuple-element.51), channel_id=1, source_target_pairs={{0,2},{1,3},{2,0},{3,1},{4,6},{5,7},{6,4},{7,5},{8,10},{9,11},{10,... | collective-permute-start | bytes 196616 | tf_op jit(solution)/shard_map/ppermute | solution.py:62
  76.6 1.3 collective-permute-start.26
  78.0 0.7 collective-permute-done.24
  79.4 1.5 collective-permute-done.26
  80.9 1.3 collective-permute-start.27
  82.4 6.5 %collective-permute-done.27 = bf16[1,4,64,512]{3,2,1,0:T(8,128)(2,1)S(1)} collective-permute-done((bf16[1,4,64,512]{3,2,1,0:T(8,128)(2,1)S(1)}, bf16[1,4,64,512]{3,2,1,0:T(8,128)(2,1)S(1)}, u32[]{:S(2)}, u32[]{:S(2)}) %collective-permute-start.27) | collective-permute-done | bytes 262176 | tf_op jit(solution)/shard_map/ppermute | solution.py:53
  89.0 1.6 collective-permute-start.28
  90.6 3.6 %collective-permute-start.9 = (bf16[64,512]{1,0:T(8,128)(2,1)S(1)}, bf16[64,512]{1,0:T(8,128)(2,1)S(1)}, u32[]{:S(2)}, u32[]{:S(2)}) collective-permute-start(bf16[64,512]{1,0:T(8,128)(2,1)S(1)} %get-tuple-element.59), channel_id=1, source_target_pairs={{0,2},{1,3},{2,0},{3,1},{4,6},{5,7},{6,4},{7,5},{8,10},{9,11},{10,... | collective-permute-start | bytes 196616 | tf_op jit(solution)/shard_map/ppermute | solution.py:62
  96.8 1.1 collective-permute-done.9
  97.9 0.7 collective-permute-done.10
  99.3 1.8 collective-permute-done.28
  101.1 1.2 fusion.21
  102.3 2.8 %collective-permute-done.11 = bf16[1,4,64,512]{3,2,1,0:T(8,128)(2,1)S(1)} collective-permute-done((bf16[1,4,64,512]{3,2,1,0:T(8,128)(2,1)S(1)}, bf16[1,4,64,512]{3,2,1,0:T(8,128)(2,1)S(1)}, u32[]{:S(2)}, u32[]{:S(2)}) %collective-permute-start.11) | collective-permute-done | bytes 262176 | tf_op jit(solution)/shard_map/ppermute | solution.py:53
  105.1 0.7 copy-done.2
  105.8 0.8 pad_maximum_fusion.11
  109.1 6.9 %collective-permute-done.12 = bf16[2,4,64,512]{3,2,1,0:T(8,128)(2,1)S(1)} collective-permute-done((bf16[2,4,64,512]{3,2,1,0:T(8,128)(2,1)}, bf16[2,4,64,512]{3,2,1,0:T(8,128)(2,1)S(1)}, u32[]{:S(2)}, u32[]{:S(2)}) %collective-permute-start.12) | collective-permute-done | bytes 524320 | tf_op jit(solution)/shard_map/ppermute | solution.py:53
  116.0 1.2 fusion.25
  117.4 1.4 pad_maximum_fusion.1.refs_2_
  118.8 19.7 %expert_mlp.3 = bf16[2,4,4,64,512]{4,3,2,1,0:T(8,128)(2,1)S(1)} custom-call(s32[8]{0:T(128)S(1)} %add.391.refs_0_, s32[8]{0:T(128)S(1)} %add.396.refs_1_, bf16[2,4,4,64,512]{4,3,2,1,0:T(8,128)(2,1)S(1)} %pad_maximum_fusion.1.refs_2_, bf16[4096,1024]{1,0:T(8,128)(2,1)} %bitcast.121, bf16[4096,1024]{1,0:T(8,128)(2,1)} %bitcast.123, ...), custom_call_target="tpu_custom_call" | custom-call | flops 6442450944 | bytes 25165824 | tf_op jit(solution)/shard_map/expert_mlp/pallas_call | solution.py:167
  139.5 19.7 %expert_mlp.2 = bf16[2,4,4,64,512]{4,3,2,1,0:T(8,128)(2,1)S(1)} custom-call(s32[8]{0:T(128)S(1)} %add.391.refs_0_, s32[8]{0:T(128)S(1)} %add.396.refs_1_, bf16[2,4,4,64,512]{4,3,2,1,0:T(8,128)(2,1)S(1)} %pad_maximum_fusion.refs_2_, bf16[4096,1024]{1,0:T(8,128)(2,1)} %bitcast.122, bf16[4096,1024]{1,0:T(8,128)(2,1)} %bitcast.124, ...), custom_call_target="tpu_custom_call" | custom-call | flops 6442450944 | bytes 25165824 | tf_op jit(solution)/shard_map/expert_mlp/pallas_call | solution.py:167
  160.4 1.7 collective-permute-done.14
  163.0 6.1 %collective-permute-done.31 = bf16[2,4,64,512]{3,2,1,0:T(8,128)(2,1)S(1)} collective-permute-done((bf16[2,4,64,512]{3,2,1,0:T(8,128)(2,1)S(1)}, bf16[2,4,64,512]{3,2,1,0:T(8,128)(2,1)S(1)}, u32[]{:S(2)}, u32[]{:S(2)}) %collective-permute-start.31) | collective-permute-done | bytes 524320 | tf_op jit(solution)/shard_map/ppermute | solution.py:45
  169.9 7.6 %collective-permute-done.15 = bf16[2,4,64,512]{3,2,1,0:T(8,128)(2,1)S(1)} collective-permute-done((bf16[2,4,64,512]{3,2,1,0:T(8,128)(2,1)S(1)}, bf16[2,4,64,512]{3,2,1,0:T(8,128)(2,1)S(1)}, u32[]{:S(2)}, u32[]{:S(2)}) %collective-permute-start.15) | collective-permute-done | bytes 524320 | tf_op jit(solution)/shard_map/ppermute | solution.py:45
  178.5 0.9 collective-permute-start.33
  179.4 2.3 %collective-permute-start.34 = (bf16[64,512]{1,0:T(8,128)(2,1)S(1)}, bf16[64,512]{1,0:T(8,128)(2,1)S(1)}, u32[]{:S(2)}, u32[]{:S(2)}) collective-permute-start(bf16[64,512]{1,0:T(8,128)(2,1)S(1)} %get-tuple-element.47), channel_id=1, source_target_pairs={{0,2},{1,3},{2,0},{3,1},{4,6},{5,7},{6,4},{7,5},{8,10},{9,11},{10,... | collective-permute-start | bytes 196616 | tf_op jit(solution)/shard_map/ppermute | solution.py:62
  182.4 1.8 collective-permute-done.16
  184.3 0.7 collective-permute-start.17
  185.0 2.3 %collective-permute-start.18 = (bf16[64,512]{1,0:T(8,128)(2,1)S(1)}, bf16[64,512]{1,0:T(8,128)(2,1)S(1)}, u32[]{:S(2)}, u32[]{:S(2)}) collective-permute-start(bf16[64,512]{1,0:T(8,128)(2,1)S(1)} %get-tuple-element.55), channel_id=1, source_target_pairs={{0,2},{1,3},{2,0},{3,1},{4,6},{5,7},{6,4},{7,5},{8,10},{9,11},{10,... | collective-permute-start | bytes 196616 | tf_op jit(solution)/shard_map/ppermute | solution.py:62
  187.3 0.8 collective-permute-start.19
  188.3 0.9 collective-permute-start.36
  189.2 1.3 collective-permute-done.17
  190.5 1.6 collective-permute-done.18
  192.2 0.9 collective-permute-start.20
  193.2 3.1 %collective-permute-done.36 = bf16[1,4,64,512]{3,2,1,0:T(8,128)(2,1)S(1)} collective-permute-done((bf16[1,4,64,512]{3,2,1,0:T(8,128)(2,1)S(1)}, bf16[1,4,64,512]{3,2,1,0:T(8,128)(2,1)S(1)}, u32[]{:S(2)}, u32[]{:S(2)}) %collective-permute-start.36) | collective-permute-done | bytes 262176 | tf_op jit(solution)/shard_map/ppermute | solution.py:53
  197.0 4.9 %collective-permute-done.20 = bf16[1,4,64,512]{3,2,1,0:T(8,128)(2,1)S(1)} collective-permute-done((bf16[1,4,64,512]{3,2,1,0:T(8,128)(2,1)S(1)}, bf16[1,4,64,512]{3,2,1,0:T(8,128)(2,1)S(1)}, u32[]{:S(2)}, u32[]{:S(2)}) %collective-permute-start.20) | collective-permute-done | bytes 262176 | tf_op jit(solution)/shard_map/ppermute | solution.py:53
  202.7 2.9 %collective-permute-done.37 = bf16[2,4,64,512]{3,2,1,0:T(8,128)(2,1)S(1)} collective-permute-done((bf16[2,4,64,512]{3,2,1,0:T(8,128)(2,1)S(1)}, bf16[2,4,64,512]{3,2,1,0:T(8,128)(2,1)S(1)}, u32[]{:S(2)}, u32[]{:S(2)}) %collective-permute-start.37) | collective-permute-done | bytes 524320 | tf_op jit(solution)/shard_map/ppermute | solution.py:53
  205.7 5.5 %collective-permute-done.21 = bf16[2,4,64,512]{3,2,1,0:T(8,128)(2,1)S(1)} collective-permute-done((bf16[2,4,64,512]{3,2,1,0:T(8,128)(2,1)S(1)}, bf16[2,4,64,512]{3,2,1,0:T(8,128)(2,1)S(1)}, u32[]{:S(2)}, u32[]{:S(2)}) %collective-permute-start.21) | collective-permute-done | bytes 524320 | tf_op jit(solution)/shard_map/ppermute | solution.py:53
  211.3 1.1 add_expert_rows.1
  212.6 1.9 collective-permute-done.38
  214.5 1.3 maximum_select_fusion
  (125 shorter events, 20.3 us)
Async XLA Ops:
  0.0 17.4 %copy-start = (s32[4,4]{1,0:T(4,128)S(1)}, s32[4,4]{1,0:T(4,128)}, u32[]{:S(2)}) copy-start(s32[4,4]{1,0:T(4,128)} %param.18) | copy-start | bytes 196
  0.0 2.7 %copy-start.3 = (bf16[512,1024]{1,0:T(8,128)(2,1)S(1)}, bf16[512,1024]{1,0:T(8,128)(2,1)}, u32[]{:S(2)}) copy-start(bf16[512,1024]{1,0:T(8,128)(2,1)} %param.13) | copy-start | bytes 3145732
  0.0 31.7 %collective-permute-start.1 = (bf16[512,4096]{1,0:T(8,128)(2,1)}, bf16[512,4096]{1,0:T(8,128)(2,1)}, u32[]{:S(2)}, u32[]{:S(2)}) collective-permute-start(bf16[512,4096]{1,0:T(8,128)(2,1)} %param.11), channel_id=1, source_target_pairs={{0,4},{4,0},{8,12},{12,8},{16,20},{20,16},{24,28},{28,24},{1,5},{5... | collective-permute-start | bytes 12582920 | tf_op jit(solution)/shard_map/ppermute | solution.py:238
  0.5 2.8 %copy-start.5 = (s32[4]{0:T(128)S(1)}, s32[4]{0:T(128)}, u32[]{:S(2)}) copy-start(s32[4]{0:T(128)} %constant.283.clone) | copy-start | bytes 52
  2.5 6.6 %collective-permute-start.2 = (bf16[512,512]{1,0:T(8,128)(2,1)}, bf16[512,512]{1,0:T(8,128)(2,1)}, u32[]{:S(2)}, u32[]{:S(2)}) collective-permute-start(bf16[512,512]{1,0:T(8,128)(2,1)} %get-tuple-element.36), channel_id=1, source_target_pairs={{0,4},{4,0},{8,12},{12,8},{16,20},{20,16},{24,28},{28,24},{1,5},{5... | collective-permute-start | bytes 1572872 | tf_op jit(solution)/shard_map/ppermute | solution.py:232
  2.8 41.3 %collective-permute-start = (bf16[512,512]{1,0:T(8,128)(2,1)S(1)}, bf16[512,512]{1,0:T(8,128)(2,1)S(1)}, u32[]{:S(2)}, u32[]{:S(2)}) collective-permute-start(bf16[512,512]{1,0:T(8,128)(2,1)S(1)} %get-tuple-element.34), channel_id=1, source_target_pairs={{0,4},{4,0},{8,12},{12,8},{16,20},{20,16},{24,28},{28,24},{1,5},{5... | collective-permute-start | bytes 1572872 | tf_op jit(solution)/shard_map/ppermute | solution.py:232
  11.2 16.8 %collective-permute-start.3 = (bf16[1024,512]{1,0:T(8,128)(2,1)}, bf16[1024,512]{1,0:T(8,128)(2,1)}, u32[]{:S(2)}, u32[]{:S(2)}) collective-permute-start(bf16[1024,512]{1,0:T(8,128)(2,1)} %pad_maximum_fusion.6), channel_id=1, source_target_pairs={{0,8},{4,20},{8,0},{12,28},{16,24},{20,4},{24,16},{28,12},{1,9},{5... | collective-permute-start | bytes 3145736 | tf_op jit(solution)/shard_map/ppermute | solution.py:237
  23.4 18.2 %collective-permute-start.4 = (bf16[1024,512]{1,0:T(8,128)(2,1)}, bf16[1024,512]{1,0:T(8,128)(2,1)}, u32[]{:S(2)}, u32[]{:S(2)}) collective-permute-start(bf16[1024,512]{1,0:T(8,128)(2,1)} %pad_maximum_fusion.6), channel_id=1, source_target_pairs={{0,16},{4,12},{8,24},{12,4},{16,0},{20,28},{24,8},{28,20},{1,17},{... | collective-permute-start | bytes 3145736 | tf_op jit(solution)/shard_map/ppermute | solution.py:237
  28.0 21.8 %collective-permute-start.5 = (bf16[1024,512]{1,0:T(8,128)(2,1)}, bf16[1024,512]{1,0:T(8,128)(2,1)}, u32[]{:S(2)}, u32[]{:S(2)}) collective-permute-start(bf16[1024,512]{1,0:T(8,128)(2,1)} %collective-permute-done.3), channel_id=1, source_target_pairs={{0,16},{4,12},{8,24},{12,4},{16,0},{20,28},{24,8},{28,20},{1,17},{... | collective-permute-start | bytes 3145736 | tf_op jit(solution)/shard_map/ppermute | solution.py:237
  53.4 9.2 %collective-permute-start.22 = (bf16[2,4,64,512]{3,2,1,0:T(8,128)(2,1)S(1)}, bf16[2,4,64,512]{3,2,1,0:T(8,128)(2,1)S(1)}, u32[]{:S(2)}, u32[]{:S(2)}) collective-permute-start(bf16[2,4,64,512]{3,2,1,0:T(8,128)(2,1)S(1)} %bitcast.132), channel_id=1, source_target_pairs={{0,16},{4,12},{8,24},{12,4},{16,0},{20,28},{24,8},{28,20},{1,17},{... | collective-permute-start | bytes 1572872 | tf_op jit(solution)/shard_map/ppermute | solution.py:45
  55.8 15.3 %collective-permute-start.6 = (bf16[2,4,64,512]{3,2,1,0:T(8,128)(2,1)S(1)}, bf16[2,4,64,512]{3,2,1,0:T(8,128)(2,1)S(1)}, u32[]{:S(2)}, u32[]{:S(2)}) collective-permute-start(bf16[2,4,64,512]{3,2,1,0:T(8,128)(2,1)S(1)} %bitcast.131), channel_id=1, source_target_pairs={{0,16},{4,12},{8,24},{12,4},{16,0},{20,28},{24,8},{28,20},{1,17},{... | collective-permute-start | bytes 1572872 | tf_op jit(solution)/shard_map/ppermute | solution.py:45
  62.8 9.5 %collective-permute-start.23 = (bf16[1,4,64,512]{3,2,1,0:T(8,128)(2,1)S(1)}, bf16[1,4,64,512]{3,2,1,0:T(8,128)(2,1)S(1)}, u32[]{:S(2)}, u32[]{:S(2)}) collective-permute-start(bf16[1,4,64,512]{3,2,1,0:T(8,128)(2,1)S(1)} %slice.303), channel_id=1, source_target_pairs={{0,8},{4,20},{8,0},{12,28},{16,24},{20,4},{24,16},{28,12},{1,9},{5... | collective-permute-start | bytes 786440 | tf_op jit(solution)/shard_map/ppermute | solution.py:45
  71.2 24.0 %copy-start.4 = (f32[1,512]{1,0:T(1,128)S(1)}, f32[1,512]{1,0:T(1,128)}, u32[]{:S(2)}) copy-start(f32[1,512]{1,0:T(1,128)} %param.17) | copy-start | bytes 6148
  71.2 24.7 %copy-start.6 = (s32[4]{0:T(128)S(1)}, s32[4]{0:T(128)}, u32[]{:S(2)}) copy-start(s32[4]{0:T(128)} %param.19) | copy-start | bytes 52
  71.3 11.1 %collective-permute-start.7 = (bf16[1,4,64,512]{3,2,1,0:T(8,128)(2,1)S(1)}, bf16[1,4,64,512]{3,2,1,0:T(8,128)(2,1)S(1)}, u32[]{:S(2)}, u32[]{:S(2)}) collective-permute-start(bf16[1,4,64,512]{3,2,1,0:T(8,128)(2,1)S(1)} %slice.280), channel_id=1, source_target_pairs={{0,8},{4,20},{8,0},{12,28},{16,24},{20,4},{24,16},{28,12},{1,9},{5... | collective-permute-start | bytes 786440 | tf_op jit(solution)/shard_map/ppermute | solution.py:45
  72.4 6.3 %collective-permute-start.24 = (bf16[64,512]{1,0:T(8,128)(2,1)S(1)}, bf16[64,512]{1,0:T(8,128)(2,1)S(1)}, u32[]{:S(2)}, u32[]{:S(2)}) collective-permute-start(bf16[64,512]{1,0:T(8,128)(2,1)S(1)} %get-tuple-element.52), channel_id=1, source_target_pairs={{0,1},{1,2},{2,3},{3,0},{4,5},{5,6},{6,7},{7,4},{8,9},{9,10},{10,1... | collective-permute-start | bytes 196616 | tf_op jit(solution)/shard_map/ppermute | solution.py:62
  74.0 5.3 %collective-permute-start.25 = (bf16[64,512]{1,0:T(8,128)(2,1)S(1)}, bf16[64,512]{1,0:T(8,128)(2,1)S(1)}, u32[]{:S(2)}, u32[]{:S(2)}) collective-permute-start(bf16[64,512]{1,0:T(8,128)(2,1)S(1)} %get-tuple-element.51), channel_id=1, source_target_pairs={{0,2},{1,3},{2,0},{3,1},{4,6},{5,7},{6,4},{7,5},{8,10},{9,11},{10,... | collective-permute-start | bytes 196616 | tf_op jit(solution)/shard_map/ppermute | solution.py:62
  76.6 4.3 %collective-permute-start.26 = (bf16[64,512]{1,0:T(8,128)(2,1)S(1)}, bf16[64,512]{1,0:T(8,128)(2,1)S(1)}, u32[]{:S(2)}, u32[]{:S(2)}) collective-permute-start(bf16[64,512]{1,0:T(8,128)(2,1)S(1)} %get-tuple-element.50), channel_id=1, source_target_pairs={{0,3},{1,0},{2,1},{3,2},{4,7},{5,4},{6,5},{7,6},{8,11},{9,8},{10,9... | collective-permute-start | bytes 196616 | tf_op jit(solution)/shard_map/ppermute | solution.py:62
  80.9 8.0 %collective-permute-start.27 = (bf16[1,4,64,512]{3,2,1,0:T(8,128)(2,1)S(1)}, bf16[1,4,64,512]{3,2,1,0:T(8,128)(2,1)S(1)}, u32[]{:S(2)}, u32[]{:S(2)}) collective-permute-start(bf16[1,4,64,512]{3,2,1,0:T(8,128)(2,1)S(1)} %maximum_bitcast_fusion.2), channel_id=1, source_target_pairs={{0,8},{4,20},{8,0},{12,28},{16,24},{20,4},{24,16},{28,12},{1,9},{5... | collective-permute-start | bytes 786440 | tf_op jit(solution)/shard_map/ppermute | solution.py:53
  89.0 12.1 %collective-permute-start.28 = (bf16[2,4,64,512]{3,2,1,0:T(8,128)(2,1)S(1)}, bf16[2,4,64,512]{3,2,1,0:T(8,128)(2,1)S(1)}, u32[]{:S(2)}, u32[]{:S(2)}) collective-permute-start(bf16[2,4,64,512]{3,2,1,0:T(8,128)(2,1)S(1)} %pad_maximum_fusion.13), channel_id=1, source_target_pairs={{0,16},{4,12},{8,24},{12,4},{16,0},{20,28},{24,8},{28,20},{1,17},{... | collective-permute-start | bytes 1572872 | tf_op jit(solution)/shard_map/ppermute | solution.py:53
  90.6 6.2 %collective-permute-start.8 = (bf16[64,512]{1,0:T(8,128)(2,1)S(1)}, bf16[64,512]{1,0:T(8,128)(2,1)S(1)}, u32[]{:S(2)}, u32[]{:S(2)}) collective-permute-start(bf16[64,512]{1,0:T(8,128)(2,1)S(1)} %get-tuple-element.60), channel_id=1, source_target_pairs={{0,1},{1,2},{2,3},{3,0},{4,5},{5,6},{6,7},{7,4},{8,9},{9,10},{10,1... | collective-permute-start | bytes 196616 | tf_op jit(solution)/shard_map/ppermute | solution.py:62
  90.6 7.3 %collective-permute-start.9 = (bf16[64,512]{1,0:T(8,128)(2,1)S(1)}, bf16[64,512]{1,0:T(8,128)(2,1)S(1)}, u32[]{:S(2)}, u32[]{:S(2)}) collective-permute-start(bf16[64,512]{1,0:T(8,128)(2,1)S(1)} %get-tuple-element.59), channel_id=1, source_target_pairs={{0,2},{1,3},{2,0},{3,1},{4,6},{5,7},{6,4},{7,5},{8,10},{9,11},{10,... | collective-permute-start | bytes 196616 | tf_op jit(solution)/shard_map/ppermute | solution.py:62
  94.3 4.3 %collective-permute-start.10 = (bf16[64,512]{1,0:T(8,128)(2,1)S(1)}, bf16[64,512]{1,0:T(8,128)(2,1)S(1)}, u32[]{:S(2)}, u32[]{:S(2)}) collective-permute-start(bf16[64,512]{1,0:T(8,128)(2,1)S(1)} %get-tuple-element.58), channel_id=1, source_target_pairs={{0,3},{1,0},{2,1},{3,2},{4,7},{5,4},{6,5},{7,6},{8,11},{9,8},{10,9... | collective-permute-start | bytes 196616 | tf_op jit(solution)/shard_map/ppermute | solution.py:62
  98.6 6.4 %collective-permute-start.11 = (bf16[1,4,64,512]{3,2,1,0:T(8,128)(2,1)S(1)}, bf16[1,4,64,512]{3,2,1,0:T(8,128)(2,1)S(1)}, u32[]{:S(2)}, u32[]{:S(2)}) collective-permute-start(bf16[1,4,64,512]{3,2,1,0:T(8,128)(2,1)S(1)} %maximum_bitcast_fusion), channel_id=1, source_target_pairs={{0,8},{4,20},{8,0},{12,28},{16,24},{20,4},{24,16},{28,12},{1,9},{5... | collective-permute-start | bytes 786440 | tf_op jit(solution)/shard_map/ppermute | solution.py:53
  102.3 15.1 %collective-permute-start.29 = (bf16[4,4,64,512]{3,2,1,0:T(8,128)(2,1)}, bf16[4,4,64,512]{3,2,1,0:T(8,128)(2,1)}, u32[]{:S(2)}, u32[]{:S(2)}) collective-permute-start(bf16[4,4,64,512]{3,2,1,0:T(8,128)(2,1)} %get-tuple-element.38), channel_id=1, source_target_pairs={{0,4},{4,0},{8,12},{12,8},{16,20},{20,16},{24,28},{28,24},{1,5},{5... | collective-permute-start | bytes 3145736 | tf_op jit(solution)/shard_map/ppermute | solution.py:284
  105.1 0.7 copy-start.2
  106.6 9.4 %collective-permute-start.12 = (bf16[2,4,64,512]{3,2,1,0:T(8,128)(2,1)}, bf16[2,4,64,512]{3,2,1,0:T(8,128)(2,1)S(1)}, u32[]{:S(2)}, u32[]{:S(2)}) collective-permute-start(bf16[2,4,64,512]{3,2,1,0:T(8,128)(2,1)} %pad_maximum_fusion.11), channel_id=1, source_target_pairs={{0,16},{4,12},{8,24},{12,4},{16,0},{20,28},{24,8},{28,20},{1,17},{... | collective-permute-start | bytes 1572872 | tf_op jit(solution)/shard_map/ppermute | solution.py:53
  117.3 22.0 %collective-permute-start.13 = (bf16[4,4,64,512]{3,2,1,0:T(8,128)(2,1)S(1)}, bf16[4,4,64,512]{3,2,1,0:T(8,128)(2,1)S(1)}, u32[]{:S(2)}, u32[]{:S(2)}) collective-permute-start(bf16[4,4,64,512]{3,2,1,0:T(8,128)(2,1)S(1)} %get-tuple-element.42), channel_id=1, source_target_pairs={{0,4},{4,0},{8,12},{12,8},{16,20},{20,16},{24,28},{28,24},{1,5},{5... | collective-permute-start | bytes 3145736 | tf_op jit(solution)/shard_map/ppermute | solution.py:284
  138.7 20.8 %collective-permute-start.30 = (bf16[4,4,64,512]{3,2,1,0:T(8,128)(2,1)S(1)}, bf16[4,4,64,512]{3,2,1,0:T(8,128)(2,1)S(1)}, u32[]{:S(2)}, u32[]{:S(2)}) collective-permute-start(bf16[4,4,64,512]{3,2,1,0:T(8,128)(2,1)S(1)} %pad_maximum_fusion.9), channel_id=1, source_target_pairs={{0,4},{4,0},{8,12},{12,8},{16,20},{20,16},{24,28},{28,24},{1,5},{5... | collective-permute-start | bytes 3145736 | tf_op jit(solution)/shard_map/ppermute | solution.py:288
  159.4 2.7 %collective-permute-start.14 = (bf16[4,4,64,512]{3,2,1,0:T(8,128)(2,1)S(1)}, bf16[4,4,64,512]{3,2,1,0:T(8,128)(2,1)S(1)}, u32[]{:S(2)}, u32[]{:S(2)}) collective-permute-start(bf16[4,4,64,512]{3,2,1,0:T(8,128)(2,1)S(1)} %pad_maximum_fusion.7), channel_id=1, source_target_pairs={{0,4},{4,0},{8,12},{12,8},{16,20},{20,16},{24,28},{28,24},{1,5},{5... | collective-permute-start | bytes 3145736 | tf_op jit(solution)/shard_map/ppermute | solution.py:288
  159.9 9.2 %collective-permute-start.31 = (bf16[2,4,64,512]{3,2,1,0:T(8,128)(2,1)S(1)}, bf16[2,4,64,512]{3,2,1,0:T(8,128)(2,1)S(1)}, u32[]{:S(2)}, u32[]{:S(2)}) collective-permute-start(bf16[2,4,64,512]{3,2,1,0:T(8,128)(2,1)S(1)} %slice.316), channel_id=1, source_target_pairs={{0,16},{4,12},{8,24},{12,4},{16,0},{20,28},{24,8},{28,20},{1,17},{... | collective-permute-start | bytes 1572872 | tf_op jit(solution)/shard_map/ppermute | solution.py:45
  162.5 15.0 %collective-permute-start.15 = (bf16[2,4,64,512]{3,2,1,0:T(8,128)(2,1)S(1)}, bf16[2,4,64,512]{3,2,1,0:T(8,128)(2,1)S(1)}, u32[]{:S(2)}, u32[]{:S(2)}) collective-permute-start(bf16[2,4,64,512]{3,2,1,0:T(8,128)(2,1)S(1)} %slice.293), channel_id=1, source_target_pairs={{0,16},{4,12},{8,24},{12,4},{16,0},{20,28},{24,8},{28,20},{1,17},{... | collective-permute-start | bytes 1572872 | tf_op jit(solution)/shard_map/ppermute | solution.py:45
  169.3 9.1 %collective-permute-start.32 = (bf16[1,4,64,512]{3,2,1,0:T(8,128)(2,1)S(1)}, bf16[1,4,64,512]{3,2,1,0:T(8,128)(2,1)S(1)}, u32[]{:S(2)}, u32[]{:S(2)}) collective-permute-start(bf16[1,4,64,512]{3,2,1,0:T(8,128)(2,1)S(1)} %slice.318), channel_id=1, source_target_pairs={{0,8},{4,20},{8,0},{12,28},{16,24},{20,4},{24,16},{28,12},{1,9},{5... | collective-permute-start | bytes 786440 | tf_op jit(solution)/shard_map/ppermute | solution.py:45
  177.8 6.4 %collective-permute-start.16 = (bf16[1,4,64,512]{3,2,1,0:T(8,128)(2,1)S(1)}, bf16[1,4,64,512]{3,2,1,0:T(8,128)(2,1)S(1)}, u32[]{:S(2)}, u32[]{:S(2)}) collective-permute-start(bf16[1,4,64,512]{3,2,1,0:T(8,128)(2,1)S(1)} %slice.295), channel_id=1, source_target_pairs={{0,8},{4,20},{8,0},{12,28},{16,24},{20,4},{24,16},{28,12},{1,9},{5... | collective-permute-start | bytes 786440 | tf_op jit(solution)/shard_map/ppermute | solution.py:45
  178.5 8.9 %collective-permute-start.33 = (bf16[64,512]{1,0:T(8,128)(2,1)S(1)}, bf16[64,512]{1,0:T(8,128)(2,1)S(1)}, u32[]{:S(2)}, u32[]{:S(2)}) collective-permute-start(bf16[64,512]{1,0:T(8,128)(2,1)S(1)} %get-tuple-element.48), channel_id=1, source_target_pairs={{0,1},{1,2},{2,3},{3,0},{4,5},{5,6},{6,7},{7,4},{8,9},{9,10},{10,1... | collective-permute-start | bytes 196616 | tf_op jit(solution)/shard_map/ppermute | solution.py:62
  179.4 8.8 %collective-permute-start.34 = (bf16[64,512]{1,0:T(8,128)(2,1)S(1)}, bf16[64,512]{1,0:T(8,128)(2,1)S(1)}, u32[]{:S(2)}, u32[]{:S(2)}) collective-permute-start(bf16[64,512]{1,0:T(8,128)(2,1)S(1)} %get-tuple-element.47), channel_id=1, source_target_pairs={{0,2},{1,3},{2,0},{3,1},{4,6},{5,7},{6,4},{7,5},{8,10},{9,11},{10,... | collective-permute-start | bytes 196616 | tf_op jit(solution)/shard_map/ppermute | solution.py:62
  181.7 6.5 %collective-permute-start.35 = (bf16[64,512]{1,0:T(8,128)(2,1)S(1)}, bf16[64,512]{1,0:T(8,128)(2,1)S(1)}, u32[]{:S(2)}, u32[]{:S(2)}) collective-permute-start(bf16[64,512]{1,0:T(8,128)(2,1)S(1)} %get-tuple-element.46), channel_id=1, source_target_pairs={{0,3},{1,0},{2,1},{3,2},{4,7},{5,4},{6,5},{7,6},{8,11},{9,8},{10,9... | collective-permute-start | bytes 196616 | tf_op jit(solution)/shard_map/ppermute | solution.py:62
  184.3 6.2 %collective-permute-start.17 = (bf16[64,512]{1,0:T(8,128)(2,1)S(1)}, bf16[64,512]{1,0:T(8,128)(2,1)S(1)}, u32[]{:S(2)}, u32[]{:S(2)}) collective-permute-start(bf16[64,512]{1,0:T(8,128)(2,1)S(1)} %get-tuple-element.56), channel_id=1, source_target_pairs={{0,1},{1,2},{2,3},{3,0},{4,5},{5,6},{6,7},{7,4},{8,9},{9,10},{10,1... | collective-permute-start | bytes 196616 | tf_op jit(solution)/shard_map/ppermute | solution.py:62
  185.0 7.1 %collective-permute-start.18 = (bf16[64,512]{1,0:T(8,128)(2,1)S(1)}, bf16[64,512]{1,0:T(8,128)(2,1)S(1)}, u32[]{:S(2)}, u32[]{:S(2)}) collective-permute-start(bf16[64,512]{1,0:T(8,128)(2,1)S(1)} %get-tuple-element.55), channel_id=1, source_target_pairs={{0,2},{1,3},{2,0},{3,1},{4,6},{5,7},{6,4},{7,5},{8,10},{9,11},{10,... | collective-permute-start | bytes 196616 | tf_op jit(solution)/shard_map/ppermute | solution.py:62
  187.3 4.8 %collective-permute-start.19 = (bf16[64,512]{1,0:T(8,128)(2,1)S(1)}, bf16[64,512]{1,0:T(8,128)(2,1)S(1)}, u32[]{:S(2)}, u32[]{:S(2)}) collective-permute-start(bf16[64,512]{1,0:T(8,128)(2,1)S(1)} %get-tuple-element.54), channel_id=1, source_target_pairs={{0,3},{1,0},{2,1},{3,2},{4,7},{5,4},{6,5},{7,6},{8,11},{9,8},{10,9... | collective-permute-start | bytes 196616 | tf_op jit(solution)/shard_map/ppermute | solution.py:62
  188.3 8.0 %collective-permute-start.36 = (bf16[1,4,64,512]{3,2,1,0:T(8,128)(2,1)S(1)}, bf16[1,4,64,512]{3,2,1,0:T(8,128)(2,1)S(1)}, u32[]{:S(2)}, u32[]{:S(2)}) collective-permute-start(bf16[1,4,64,512]{3,2,1,0:T(8,128)(2,1)S(1)} %maximum_bitcast_fusion.3), channel_id=1, source_target_pairs={{0,8},{4,20},{8,0},{12,28},{16,24},{20,4},{24,16},{28,12},{1,9},{5... | collective-permute-start | bytes 786440 | tf_op jit(solution)/shard_map/ppermute | solution.py:53
  192.2 9.7 %collective-permute-start.20 = (bf16[1,4,64,512]{3,2,1,0:T(8,128)(2,1)S(1)}, bf16[1,4,64,512]{3,2,1,0:T(8,128)(2,1)S(1)}, u32[]{:S(2)}, u32[]{:S(2)}) collective-permute-start(bf16[1,4,64,512]{3,2,1,0:T(8,128)(2,1)S(1)} %maximum_bitcast_fusion.1), channel_id=1, source_target_pairs={{0,8},{4,20},{8,0},{12,28},{16,24},{20,4},{24,16},{28,12},{1,9},{5... | collective-permute-start | bytes 786440 | tf_op jit(solution)/shard_map/ppermute | solution.py:53
  196.3 9.2 %collective-permute-start.37 = (bf16[2,4,64,512]{3,2,1,0:T(8,128)(2,1)S(1)}, bf16[2,4,64,512]{3,2,1,0:T(8,128)(2,1)S(1)}, u32[]{:S(2)}, u32[]{:S(2)}) collective-permute-start(bf16[2,4,64,512]{3,2,1,0:T(8,128)(2,1)S(1)} %pad_maximum_fusion.14), channel_id=1, source_target_pairs={{0,16},{4,12},{8,24},{12,4},{16,0},{20,28},{24,8},{28,20},{1,17},{... | collective-permute-start | bytes 1572872 | tf_op jit(solution)/shard_map/ppermute | solution.py:53
  201.9 9.2 %collective-permute-start.21 = (bf16[2,4,64,512]{3,2,1,0:T(8,128)(2,1)S(1)}, bf16[2,4,64,512]{3,2,1,0:T(8,128)(2,1)S(1)}, u32[]{:S(2)}, u32[]{:S(2)}) collective-permute-start(bf16[2,4,64,512]{3,2,1,0:T(8,128)(2,1)S(1)} %pad_maximum_fusion.12), channel_id=1, source_target_pairs={{0,16},{4,12},{8,24},{12,4},{16,0},{20,28},{24,8},{28,20},{1,17},{... | collective-permute-start | bytes 1572872 | tf_op jit(solution)/shard_map/ppermute | solution.py:53
  211.3 4.5 %copy-start.1 = (s32[4,4]{1,0:T(4,128)S(1)}, s32[4,4]{1,0:T(4,128)}, u32[]{:S(2)}) copy-start(s32[4,4]{1,0:T(4,128)} %param.18) | copy-start | bytes 196
  212.5 2.0 collective-permute-start.38

commit v2 on v1

v2 whole, which is shorter than its diff:
```python
import jax
import jax.numpy as jnp
from jax import lax
from jax.experimental import pallas as pl
from jax.experimental.pallas import tpu as pltpu
from jax.sharding import PartitionSpec as P

BLK = 128
CAP = 4
GROUPS = 2


def bit_orders(n_bits):
    forward = list(range(1, n_bits + 1))
    return forward, forward[::-1]


def step_pairs(n_dp, step):
    orders = bit_orders(n_dp.bit_length() - 2)
    return [(i, i ^ (1 << orders[i & 1][step])) for i in range(n_dp)]


def pair_pairs(n_dp):
    return [(i, i ^ 1) for i in range(n_dp)]


def masks_of(n_bits, side):
    order = bit_orders(n_bits)[side]
    return [
        sum(1 << (order[t] - 1) for t in range(n_bits) if (r >> t) & 1) for r in range(1 << n_bits)
    ]


def bit_reversed(n_bits):
    return [
        sum(1 << (n_bits - 1 - t) for t in range(n_bits) if (r >> t) & 1)
        for r in range(1 << n_bits)
    ]


SMEM = pl.BlockSpec(memory_space=pltpu.SMEM)
VMEM = pl.BlockSpec(memory_space=pltpu.VMEM)
ANY = pl.BlockSpec(memory_space=pl.ANY)
MIB = 1024 * 1024


def f32_sum(a, b):
    return (a.astype(jnp.float32) + b.astype(jnp.float32)).astype(jnp.bfloat16)


def exchange(value, n_dp, step):
    return lax.ppermute(value, "dp", step_pairs(n_dp, step))


def scatter_sum(keep, send, n_dp, n_bits):
    for step in range(n_bits - 1, -1, -1):
        got = exchange(send, n_dp, step)
        if step == 0:
            return f32_sum(keep, got)[0]
        half = 1 << (step - 1)
        keep, send = f32_sum(keep[:half], got[:half]), f32_sum(keep[half:], got[half:])


def gather_all(piece, n_dp, n_bits):
    pieces = [piece]
    for step in range(n_bits):
        pieces = pieces + [exchange(p, n_dp, step) for p in pieces]
    return pieces


def swap_planes(parts, n_expert):
    out = [parts[0]]
    for k in range(1, n_expert):
        pairs = [(i, (i + k) % n_expert) for i in range(n_expert)]
        out.append(lax.ppermute(parts[k], "expert", pairs))
    return jnp.stack(out)


def call(kernel, out_shape, in_specs, out_specs, name, limit, flops=0, moved=0, **more):
    return pl.pallas_call(
        kernel,
        out_shape=out_shape,
        in_specs=in_specs,
        out_specs=out_specs,
        compiler_params=pltpu.CompilerParams(vmem_limit_bytes=limit * MIB),
        cost_estimate=pl.CostEstimate(flops=flops, bytes_accessed=moved, transcendentals=0),
        name=name,
        **more,
    )


def load_kernel(src, after, out, sem):
    copy = pltpu.make_async_copy(src, out, sem)
    copy.start()
    copy.wait()


def load(weight, after, name):
    out = call(
        load_kernel,
        pltpu.VMEM(weight.shape, weight.dtype),
        [ANY, ANY],
        VMEM,
        name,
        1,
        moved=2 * weight.size,
        scratch_shapes=[pltpu.SemaphoreType.DMA],
    )(weight, after)
    return pltpu.with_memory_space_constraint(out, pltpu.VMEM)


def order_kernel(cidx, x_ref, after, own_ref, send_ref):
    own_ref[0] = x_ref[...]
    send_ref[0] = x_ref[...]


def order_context(context, chips, side, reverse, depth, after):
    rows, width = context.shape
    n_block = width // depth
    per_half = n_block // 2
    n_chip = n_block // 2
    r, s = jnp.arange(n_block) // 2, jnp.arange(n_block) % 2
    columns = chips[r] * 2 + (side ^ s)
    target = jnp.array(reverse)[r] * 2 + (1 - s)
    cidx = jnp.stack([columns, target]).astype(jnp.int32)
    shape = jax.ShapeDtypeStruct((2, rows, width // 2), context.dtype)
    return pl.pallas_call(
        order_kernel,
        out_shape=[shape, shape],
        grid_spec=pltpu.PrefetchScalarGridSpec(
            num_scalar_prefetch=1,
            grid=(n_block,),
            in_specs=[pl.BlockSpec((rows, depth), lambda i, c: (0, c[0, i])), ANY],
            out_specs=[
                pl.BlockSpec((1, rows, depth), lambda i, c: (i // per_half, 0, i % per_half)),
                pl.BlockSpec(
                    (1, rows, depth), lambda i, c: (c[1, i] // per_half, 0, c[1, i] % per_half)
                ),
            ],
        ),
        compiler_params=pltpu.CompilerParams(vmem_limit_bytes=12 * MIB),
        cost_estimate=pl.CostEstimate(flops=0, bytes_accessed=6 * context.size, transcendentals=0),
        name="order_context",
    )(cidx, context, after)


def project_kernel(n_w, last, *refs):
    if last:
        own, other, acc, res_own, res_other = refs[:5]
        weights, out, w_all, c_own, c_other, sems = refs[5 : 5 + n_w], *refs[5 + n_w :]
    else:
        own, other = refs[:2]
        weights, out, w_all, c_own, c_other, sems = refs[2 : 2 + n_w], *refs[2 + n_w :]
    copies = [
        pltpu.make_async_copy(own.at[int(last)], c_own, sems.at[0]),
        pltpu.make_async_copy(other.at[int(last)], c_other, sems.at[1]),
    ]
    for c in copies:
        c.start()
    depth = weights[0].shape[0]
    for i, w in enumerate(weights):
        w_all[i * depth : (i + 1) * depth, :] = w[...]
    for i, c in enumerate((c_own, c_other)):
        copies[i].wait()
        value = jnp.dot(c[...], w_all[...], preferred_element_type=jnp.float32)
        if last:
            res = (res_own, res_other)[i]
            value = value + acc[i] + res[...].astype(jnp.float32)
        out[i] = value.astype(out.dtype)


def project(own, other, weights, extra):
    last = len(extra) > 0
    rows, k = own.shape[1:]
    half = weights[0].shape[1]
    return call(
        lambda *refs: project_kernel(len(weights), last, *refs),
        jax.ShapeDtypeStruct((2, rows, half), jnp.bfloat16 if last else jnp.float32),
        [ANY, ANY] + [VMEM] * (len(extra) + len(weights)),
        VMEM,
        "project_last" if last else "project_first",
        20,
        flops=4 * rows * k * half,
        moved=6 * rows * k,
        scratch_shapes=[
            pltpu.VMEM((k, half), jnp.bfloat16),
            pltpu.VMEM((rows, k), jnp.bfloat16),
            pltpu.VMEM((rows, k), jnp.bfloat16),
            pltpu.SemaphoreType.DMA((2,)),
        ],
    )(own, other, *extra, *weights)


def pick_kernel(idx_ref, att_ref, after, keep_ref, send_ref):
    n = keep_ref.shape[0]
    for i in range(2 * n):
        idx = idx_ref[i]
        value = att_ref[jnp.maximum(idx, 0)]
        value = jnp.where(idx >= 0, value, jnp.zeros_like(value))
        if i < n:
            keep_ref[i] = value
        else:
            send_ref[i - n] = value


def pick(idx, attended, after):
    shape = jax.ShapeDtypeStruct((idx.shape[0] // 2,) + attended.shape[1:], attended.dtype)
    return call(
        pick_kernel, [shape, shape], [SMEM, VMEM, ANY], [VMEM, VMEM], "pick_blocks", 8, moved=4 * MIB
    )(idx, attended, after)


def finish_kernel(idx_ref, att_ref, *refs):
    pieces, out_ref, acc = refs[:-2], refs[-2], refs[-1]
    acc[...] = att_ref[...].astype(jnp.float32)
    at = 0
    for piece in pieces:
        for i in range(piece.shape[0]):
            idx = idx_ref[at]
            at += 1

            @pl.when(idx >= 0)
            def _():
                acc[idx] = acc[idx] + piece[i].astype(jnp.float32)

    out_ref[...] = acc[...].astype(out_ref.dtype)


def finish(idx, attended, pieces):
    return call(
        finish_kernel,
        jax.ShapeDtypeStruct(attended.shape, attended.dtype),
        [SMEM] + [VMEM] * (1 + len(pieces)),
        VMEM,
        "add_expert_rows",
        12,
        moved=4 * MIB,
        scratch_shapes=[pltpu.VMEM(attended.shape, jnp.float32)],
    )(idx, attended, *pieces)


def hidden_kernel(n, kidx, *refs):
    own, other, wg, wu, hid, xs = refs[:n], refs[n : 2 * n], *refs[2 * n :]
    n_z, rows, width = own[0].shape
    for s, pieces in enumerate((own, other)):
        for z in range(n_z):
            at = pl.ds(pl.multiple_of(kidx[s * n_z + z] * width, width), width)
            for r in range(n):
                xs[r * rows : (r + 1) * rows, at] = pieces[r][z]
    ff = wg.shape[1]
    tile = min(ff, 256)

    def one(i, carry):
        at = pl.ds(pl.multiple_of(i * tile, tile), tile)
        g = jnp.dot(xs[...], wg[:, at], preferred_element_type=jnp.float32)
        u = jnp.dot(xs[...], wu[:, at], preferred_element_type=jnp.float32)
        hid[:, at] = (g / (1.0 + jnp.exp(-g)) * u).astype(jnp.bfloat16)
        return carry

    lax.fori_loop(0, ff // tile, one, 0)


def hidden_units(own, other, kidx, w_gate, w_up):
    n = len(own)
    n_z, rows, width = own[0].shape
    model_width, ff = w_gate.shape
    return call(
        lambda *refs: hidden_kernel(n, *refs),
        jax.ShapeDtypeStruct((n * rows, ff), jnp.bfloat16),
        [SMEM] + [VMEM] * (2 * n + 2),
        VMEM,
        "expert_hidden",
        14,
        flops=4 * n * rows * ff * model_width,
        moved=2 * n * rows * model_width,
        scratch_shapes=[pltpu.VMEM((n * rows, model_width), jnp.bfloat16)],
    )(kidx, *own, *other, w_gate, w_up)


def down_kernel(order, nidx, hid, wd, scale, out):
    n, n_z, rows, width = out.shape
    for z in range(n_z):
        at = pl.ds(pl.multiple_of(nidx[z] * width, width), width)
        part = jnp.dot(hid[...], wd[:, at], preferred_element_type=jnp.float32)
        part = (part * scale[...]).astype(out.dtype)
        for r in range(n):
            out[order[r], z] = part[r * rows : (r + 1) * rows]


def down(hid, nidx, w_down, scale, order, rows, width):
    n, n_z = len(order), nidx.shape[0]
    return call(
        lambda *refs: down_kernel(order, *refs),
        jax.ShapeDtypeStruct((n, n_z, rows, width), jnp.bfloat16),
        [SMEM, VMEM, VMEM, VMEM],
        VMEM,
        "expert_down",
        10,
        flops=2 * hid.size * n_z * width,
        moved=2 * n * rows * n_z * width,
    )(nidx, hid, w_down, scale)


def body(
    context,
    out_weight,
    residual,
    gate_weight,
    up_weight,
    down_weight,
    gate_values,
    chosen_blocks,
    block_counts,
):
    n_expert = lax.axis_size("expert")
    n_dp = lax.axis_size("dp")
    n_bits = n_dp.bit_length() - 2
    n_chip = 1 << n_bits
    local_tokens, model_width = context.shape
    local_width = residual.shape[1]
    half = local_width // 2
    depth = out_weight.shape[0]
    local_blocks = local_tokens // BLK
    my_expert = lax.axis_index("expert")
    my_data = lax.axis_index("dp")
    chip, side = my_data // 2, my_data % 2
    masks = jnp.where(
        side == 0,
        jnp.array(masks_of(n_bits, 0), jnp.int32),
        jnp.array(masks_of(n_bits, 1), jnp.int32),
    )
    chips = chip ^ masks
    reverse = bit_reversed(n_bits)
    pair = pair_pairs(n_dp)

    def to_partner(value):
        return lax.ppermute(value, "dp", pair)

    def split_sides(value):
        own = lax.dynamic_slice_in_dim(value, side * half, half, axis=1)
        other = lax.dynamic_slice_in_dim(value, (1 - side) * half, half, axis=1)
        return own, to_partner(other)

    w_own, w_other = split_sides(out_weight)
    pieces = [(w_own, w_other)]
    for step in range(n_bits):
        pieces = pieces + [tuple(exchange(w, n_dp, step) for w in p) for p in pieces]
    pieces = [w for p in pieces for w in p]
    context_own, context_send = order_context(context, chips, side, reverse, depth, w_other)
    context_other = to_partner(context_send)
    residual_own, residual_other = split_sides(residual)
    first = project(context_own, context_other, pieces[:n_chip], ())
    w_gate = load(gate_weight[0], pieces[2], "load_gate")
    w_up = load(up_weight[0], pieces[2], "load_up")
    w_down = load(down_weight[0], pieces[2], "load_down")
    attended = project(
        context_own, context_other, pieces[n_chip:], (first, residual_own, residual_other)
    )

    group_rows = CAP * BLK // GROUPS
    share = group_rows // n_chip
    grains = attended.reshape(-1, share, half)
    per_block = BLK // share

    def grain_index(group, experts):
        row = group * group_rows + chips * share
        block = chosen_blocks[experts[None, :], (row // BLK)[:, None]]
        owner = block // local_blocks
        mine = owner // 2 == chip
        base = jnp.where(owner % 2 == side, 0, local_blocks) + block % local_blocks
        index = base * per_block + ((row % BLK) // share)[:, None]
        return jnp.where(mine, index, -1).reshape(-1).astype(jnp.int32)

    ahead = (my_expert + jnp.arange(n_expert)) % n_expert
    behind = (my_expert - jnp.arange(n_expert)) % n_expert
    my_count = lax.dynamic_index_in_dim(block_counts, my_expert, 0, keepdims=False)
    live = jnp.arange(CAP * BLK) // BLK < my_count
    scale_all = jnp.where(live, gate_values[0], 0.0).reshape(GROUPS, n_chip, share)
    sides = jnp.stack([side, 1 - side])
    kidx = (behind[None, :] * 2 + sides[:, None]).reshape(-1).astype(jnp.int32)
    nidx = (ahead[None, :] * 2 + sides[:, None]).astype(jnp.int32)
    plain = list(range(n_chip))

    received = []
    after = first
    for group in range(GROUPS):
        keep, send = pick(grain_index(group, ahead), grains, after)
        shape = (n_chip // 2, n_expert, share, half)
        mine = scatter_sum(keep.reshape(shape), send.reshape(shape), n_dp, n_bits)
        after = mine
        crossed = swap_planes(mine, n_expert)
        own_half = gather_all(crossed, n_dp, n_bits)
        got = [to_partner(p) for p in own_half]
        other_half = [got[r] for r in reverse]
        hid = hidden_units(own_half, other_half, kidx, w_gate, w_up)
        scale = scale_all[group][chips].reshape(-1, 1)
        to_other = down(hid, nidx[1], w_down, scale, reverse, share, half)
        got = to_partner(to_other)
        mine = down(hid, nidx[0], w_down, scale, plain, share, half)
        top = n_chip // 2
        mine = scatter_sum(
            f32_sum(mine[:top], got[:top]), f32_sum(mine[top:], got[top:]), n_dp, n_bits
        )
        crossed = swap_planes(mine, n_expert)
        received += gather_all(crossed, n_dp, n_bits)

    index = jnp.concatenate([grain_index(group, behind) for group in range(GROUPS)])
    mixed = finish(index, grains, received).reshape(2, local_tokens, half)
    got = to_partner(mixed[1])
    return jnp.where(
        side == 0,
        jnp.concatenate([mixed[0], got], axis=1),
        jnp.concatenate([got, mixed[0]], axis=1),
    )


def solution(mesh):
    in_specs = (
        P("dp", None),
        P("dp", "expert"),
        P("dp", "expert"),
        P("expert", None, "dp"),
        P("expert", None, "dp"),
        P("expert", "dp", None),
        P("expert", None),
        P(),
        P(),
    )
    out_specs = P("dp", "expert")
    return jax.shard_map(body, mesh=mesh, in_specs=in_specs, out_specs=out_specs, check_vma=False)
```

time: 218 us -> 214 us (0.982)
  starting transfers between devices: 40.8 us -> 51.6 us
  matrix products: 10.3 us -> 0 us
  local copies, waits for them, and re-layouts: 17.9 us -> 25.5 us
  other arithmetic: 12.3 us -> 6.48 us
  Pallas kernels: 41.9 us -> 38.1 us
  between operations: 3.04 us -> 0.5 us
    unnamed x16 -> x27, local copies, waits for them, and re-layouts: 3.91 us -> 15.7 us
    dot_general x4 -> x0, matrix products: 10.3 us -> none  [body(): jnp.dot(columns, pieces[r], preferred_element_type=jnp.float32)]
    ppermute x27 -> x40, starting transfers between devices: 23.6 us -> 33.5 us  [the longest x26 30.4 us: exchange(): return lax.ppermute(value, 'dp', step_pairs(n_dp, step))]
    another operation x6 -> x5, other arithmetic: 4.33 us -> 0.15 us  [the longest x4 0.14 us: swap_planes(): return jnp.stack(out)]
    pallas_call x5 -> x15, Pallas kernels: 41.9 us -> 38.1 us  [the longest x2 13.1 us: hidden_units(): call(lambda *refs: hidden_kernel(n, *refs), jax.ShapeDtypeStruct((n * row...]
    ppermute x12, waiting for transfers between devices: 8.03 us -> 11.6 us  [swap_planes(): out.append(lax.ppermute(parts[k], 'expert', pairs))]
    concatenate x7 -> x0, other arithmetic: 3.27 us -> none  [the longest x1 2.08 us: body(): w_piece = jnp.concatenate(split_sides(out_weight), axis=0)]
    concatenate x1 -> x0, local copies, waits for them, and re-layouts: 2.67 us -> none  [body(): jnp.concatenate([context, lax.ppermute(context, 'dp', pair)], axis=0)]
  transfers between devices with their start and end apart: 39 -> 52, of which waited for: 28 -> 25; matrix products, arithmetic and copies ran while one was open for 16% -> 6% of each run, Pallas kernels for 19% -> 12%
where the time goes in v2:
time: 214 us; the launch traced here: 213 us
  waiting for transfers between devices  91.3 us (43%)
  starting transfers between devices  51.6 us (24%)
  Pallas kernels  38.1 us (18%)
  local copies, waits for them, and re-layouts  25.5 us (12%)
  other arithmetic  6.48 us (3%)
    ppermute x26, waiting for transfers between devices, exchange(): return lax.ppermute(value, 'dp', step_pairs(n_dp, step))  77.8 us
    ppermute x26, starting transfers between devices, exchange(): return lax.ppermute(value, 'dp', step_pairs(n_dp, step))  30.4 us
    ppermute x12, starting transfers between devices, swap_planes(): out.append(lax.ppermute(parts[k], 'expert', pairs))  18.1 us
    unnamed x27, local copies, waits for them, and re-layouts  15.7 us
    pallas_call x2, Pallas kernels, hidden_units(): call(lambda *refs: hidden_kernel(n, *refs), jax.ShapeDtypeStruct((n * row...  13.1 us
    ppermute x12, waiting for transfers between devices, swap_planes(): out.append(lax.ppermute(parts[k], 'expert', pairs))  11.6 us
    pallas_call x2, Pallas kernels, project(): call(lambda *refs: project_kernel(len(weights), last, *refs), jax.ShapeDt...  8.62 us
    pallas_call x4, Pallas kernels, down(): call(lambda *refs: down_kernel(order, *refs), jax.ShapeDtypeStruct((n, n_...  7.31 us
  transfers between devices with their start and end apart: 52, of which 25 were waited for; matrix products, arithmetic and copies ran while one was open for 6% of the time, Pallas kernels for 12%

profile of v2, /device:TPU:0, one launch (start us, length us, event | category | flops | bytes accessed | tf_op | source)
XLA Modules:
  0.0 213.5 jit_solution(4274730282792038754)
XLA Ops:
  0.0 1.3 constant_dynamic-slice_fusion.2
  1.8 1.3 gather_fusion.3
  3.8 2.2 %copy-done.7 = bf16[512,4096]{1,0:T(8,128)(2,1)S(1)} copy-done((bf16[512,4096]{1,0:T(8,128)(2,1)S(1)}, bf16[512,4096]{1,0:T(8,128)(2,1)}, u32[]{:S(2)}) %copy-start.7) | copy-done | bytes 4194328
  6.0 4.9 %order_context.1 = (bf16[2,512,2048]{2,1,0:T(8,128)(2,1)S(1)}, bf16[2,512,2048]{2,1,0:T(8,128)(2,1)}) custom-call(s32[2,8]{1,0:T(2,128)S(1)} %pad_add_fusion.cidx, bf16[512,4096]{1,0:T(8,128)(2,1)S(1)} %copy-done.7, bf16[512,512]{1,0:T(8,128)(2,1)S(1)} %collective-permute-done.after.refs_3_), custom_call_target="tpu_custom_call" | custom-call | bytes 12582912 | tf_op jit(solution)/shard_map/order_context/pallas_call | solution.py:127
  10.9 2.0 copy-done.2
  13.7 2.9 %collective-permute-start.2 = (bf16[512,512]{1,0:T(8,128)(2,1)S(1)}, bf16[512,512]{1,0:T(8,128)(2,1)S(1)}, u32[]{:S(2)}, u32[]{:S(2)}) collective-permute-start(bf16[512,512]{1,0:T(8,128)(2,1)S(1)} %get-tuple-element.31.refs_2_), channel_id=1, source_target_pairs={{0,8},{4,20},{8,0},{12,28},{16,24},{20,4},{24,16},{28,12},{1,9},{5... | collective-permute-start | bytes 1572872 | tf_op jit(solution)/shard_map/ppermute | solution.py:52
  16.6 1.5 collective-permute-start.5
  19.7 9.0 %collective-permute-done.2.refs_4_.after = bf16[512,512]{1,0:T(8,128)(2,1)S(1)} collective-permute-done((bf16[512,512]{1,0:T(8,128)(2,1)S(1)}, bf16[512,512]{1,0:T(8,128)(2,1)S(1)}, u32[]{:S(2)}, u32[]{:S(2)}) %collective-permute-start.2) | collective-permute-done | bytes 524320 | tf_op jit(solution)/shard_map/ppermute | solution.py:52
  28.7 1.8 collective-permute-start.6
  30.5 9.2 %collective-permute-done.3.refs_5_ = bf16[512,512]{1,0:T(8,128)(2,1)} collective-permute-done((bf16[512,512]{1,0:T(8,128)(2,1)S(1)}, bf16[512,512]{1,0:T(8,128)(2,1)}, u32[]{:S(2)}, u32[]{:S(2)}) %collective-permute-start.3) | collective-permute-done | bytes 524320 | tf_op jit(solution)/shard_map/ppermute | solution.py:52
  39.6 1.2 collective-permute-start.7
  43.4 2.2 %copy-done.3 = bf16[2,512,2048]{2,1,0:T(8,128)(2,1)S(1)} copy-done((bf16[2,512,2048]{2,1,0:T(8,128)(2,1)S(1)}, bf16[2,512,2048]{2,1,0:T(8,128)(2,1)}, u32[]{:S(2)}) %copy-start.3) | copy-done | bytes 4194328
  45.6 4.3 %project_first.1.refs_2_.after = f32[2,512,512]{2,1,0:T(8,128)S(1)} custom-call(bf16[2,512,2048]{2,1,0:T(8,128)(2,1)S(1)} %copy-done.3, bf16[2,512,2048]{2,1,0:T(8,128)(2,1)} %collective-permute-done.1.refs_1_, bf16[512,512]{1,0:T(8,128)(2,1)S(1)} %get-tuple-element.31.refs_2_, bf16[512,512]{1,0:T(8,128)(2,1)S(1)} %collective-permute-done.after.refs_3_, ...), custom_call_target="tpu_custom_call" | custom-call | flops 2147483648 | bytes 6291456 | tf_op jit(solution)/shard_map/project_first/pallas_call | solution.py:176
  49.9 4.6 %collective-permute-done.8.refs_8_ = bf16[512,512]{1,0:T(8,128)(2,1)} collective-permute-done((bf16[512,512]{1,0:T(8,128)(2,1)}, bf16[512,512]{1,0:T(8,128)(2,1)}, u32[]{:S(2)}, u32[]{:S(2)}) %collective-permute-start.8) | collective-permute-done | bytes 524320 | tf_op jit(solution)/shard_map/ppermute | solution.py:52
  54.6 4.4 %project_last.1 = bf16[2,512,512]{2,1,0:T(8,128)(2,1)S(1)} custom-call(bf16[2,512,2048]{2,1,0:T(8,128)(2,1)S(1)} %copy-done.4, bf16[2,512,2048]{2,1,0:T(8,128)(2,1)} %collective-permute-done.1.refs_1_, f32[2,512,512]{2,1,0:T(8,128)S(1)} %project_first.1.refs_2_.after, bf16[512,512]{1,0:T(8,128)(2,1)S(1)} %get-tuple-element.30.refs_3_, ...), custom_call_target="tpu_custom_call" | custom-call | flops 2147483648 | bytes 6291456 | tf_op jit(solution)/shard_map/project_last/pallas_call | solution.py:176
  59.6 1.3 collective-permute-start.9
  60.9 8.2 %collective-permute-done.9 = bf16[2,4,64,512]{3,2,1,0:T(8,128)(2,1)S(1)} collective-permute-done((bf16[2,4,64,512]{3,2,1,0:T(8,128)(2,1)S(1)}, bf16[2,4,64,512]{3,2,1,0:T(8,128)(2,1)S(1)}, u32[]{:S(2)}, u32[]{:S(2)}) %collective-permute-start.9) | collective-permute-done | bytes 524320 | tf_op jit(solution)/shard_map/ppermute | solution.py:52
  69.2 2.9 %collective-permute-start.10 = (bf16[1,4,64,512]{3,2,1,0:T(8,128)(2,1)S(1)}, bf16[1,4,64,512]{3,2,1,0:T(8,128)(2,1)S(1)}, u32[]{:S(2)}, u32[]{:S(2)}) collective-permute-start(bf16[1,4,64,512]{3,2,1,0:T(8,128)(2,1)S(1)} %fusion.2), channel_id=1, source_target_pairs={{0,8},{4,20},{8,0},{12,28},{16,24},{20,4},{24,16},{28,12},{1,9},{5... | collective-permute-start | bytes 786440 | tf_op jit(solution)/shard_map/ppermute | solution.py:52
  73.9 3.5 %collective-permute-done.10 = bf16[1,4,64,512]{3,2,1,0:T(8,128)(2,1)S(1)} collective-permute-done((bf16[1,4,64,512]{3,2,1,0:T(8,128)(2,1)S(1)}, bf16[1,4,64,512]{3,2,1,0:T(8,128)(2,1)S(1)}, u32[]{:S(2)}, u32[]{:S(2)}) %collective-permute-start.10) | collective-permute-done | bytes 262176 | tf_op jit(solution)/shard_map/ppermute | solution.py:52
  78.1 1.0 collective-permute-start.30
  81.6 7.2 %collective-permute-done.30 = bf16[2,4,64,512]{3,2,1,0:T(8,128)(2,1)} collective-permute-done((bf16[2,4,64,512]{3,2,1,0:T(8,128)(2,1)S(1)}, bf16[2,4,64,512]{3,2,1,0:T(8,128)(2,1)}, u32[]{:S(2)}, u32[]{:S(2)}) %collective-permute-start.30) | collective-permute-done | bytes 524320 | tf_op jit(solution)/shard_map/ppermute | solution.py:52
  88.8 1.0 fusion
  89.8 2.6 %collective-permute-start.31 = (bf16[1,4,64,512]{3,2,1,0:T(8,128)(2,1)S(1)}, bf16[1,4,64,512]{3,2,1,0:T(8,128)(2,1)S(1)}, u32[]{:S(2)}, u32[]{:S(2)}) collective-permute-start(bf16[1,4,64,512]{3,2,1,0:T(8,128)(2,1)S(1)} %fusion), channel_id=1, source_target_pairs={{0,8},{4,20},{8,0},{12,28},{16,24},{20,4},{24,16},{28,12},{1,9},{5... | collective-permute-start | bytes 786440 | tf_op jit(solution)/shard_map/ppermute | solution.py:52
  92.5 6.2 %collective-permute-start.13 = (bf16[64,512]{1,0:T(8,128)(2,1)S(1)}, bf16[64,512]{1,0:T(8,128)(2,1)S(1)}, u32[]{:S(2)}, u32[]{:S(2)}) collective-permute-start(bf16[64,512]{1,0:T(8,128)(2,1)S(1)} %get-tuple-element.46), channel_id=1, source_target_pairs={{0,3},{1,0},{2,1},{3,2},{4,7},{5,4},{6,5},{7,6},{8,11},{9,8},{10,9... | collective-permute-start | bytes 196616 | tf_op jit(solution)/shard_map/ppermute | solution.py:75
  98.7 1.0 collective-permute-start.11
  100.6 3.3 %collective-permute-done.12 = bf16[64,512]{1,0:T(8,128)(2,1)S(1)} collective-permute-done((bf16[64,512]{1,0:T(8,128)(2,1)S(1)}, bf16[64,512]{1,0:T(8,128)(2,1)S(1)}, u32[]{:S(2)}, u32[]{:S(2)}) %collective-permute-start.12) | collective-permute-done | bytes 65568 | tf_op jit(solution)/shard_map/ppermute | solution.py:75
  104.8 1.4 collective-permute-start.14
  106.3 1.1 add_convert_fusion.7
  107.3 1.5 collective-permute-start.34
  108.8 1.9 collective-permute-start.32
  111.7 1.2 collective-permute-start.16
  112.9 2.5 %collective-permute-done.33 = bf16[64,512]{1,0:T(8,128)(2,1)S(1)} collective-permute-done((bf16[64,512]{1,0:T(8,128)(2,1)S(1)}, bf16[64,512]{1,0:T(8,128)(2,1)S(1)}, u32[]{:S(2)}, u32[]{:S(2)}) %collective-permute-start.33) | collective-permute-done | bytes 65568 | tf_op jit(solution)/shard_map/ppermute | solution.py:75
  116.2 2.6 %collective-permute-done.15.refs_3_ = bf16[4,64,512]{2,1,0:T(8,128)(2,1)S(1)} collective-permute-done((bf16[4,64,512]{2,1,0:T(8,128)(2,1)S(1)}, bf16[4,64,512]{2,1,0:T(8,128)(2,1)S(1)}, u32[]{:S(2)}, u32[]{:S(2)}) %collective-permute-start.15) | collective-permute-done | bytes 262176 | tf_op jit(solution)/shard_map/ppermute | solution.py:52
  118.8 4.1 %collective-permute-done.16.refs_4_ = bf16[4,64,512]{2,1,0:T(8,128)(2,1)} collective-permute-done((bf16[4,64,512]{2,1,0:T(8,128)(2,1)S(1)}, bf16[4,64,512]{2,1,0:T(8,128)(2,1)}, u32[]{:S(2)}, u32[]{:S(2)}) %collective-permute-start.16) | collective-permute-done | bytes 262176 | tf_op jit(solution)/shard_map/ppermute | solution.py:52
  123.5 1.5 collective-permute-start.37
  126.5 3.4 %copy-done.5 = bf16[1,4096,1024]{2,1,0:T(8,128)(2,1)S(1)} copy-done((bf16[1,4096,1024]{2,1,0:T(8,128)(2,1)S(1)}, bf16[1,4096,1024]{2,1,0:T(8,128)(2,1)}, u32[]{:S(2)}) %copy-start.5) | copy-done | bytes 8388632
  130.4 3.7 %copy-done.6 = bf16[1,4096,1024]{2,1,0:T(8,128)(2,1)S(1)} copy-done((bf16[1,4096,1024]{2,1,0:T(8,128)(2,1)S(1)}, bf16[1,4096,1024]{2,1,0:T(8,128)(2,1)}, u32[]{:S(2)}) %copy-start.6) | copy-done | bytes 8388632
  134.7 1.7 slice-done.1
  138.0 6.6 %expert_hidden.2.refs_1_ = bf16[256,1024]{1,0:T(8,128)(2,1)S(1)} custom-call(s32[8]{0:T(128)S(1)} %add.393.refs_0_, bf16[4,64,512]{2,1,0:T(8,128)(2,1)S(1)} %pad_maximum_fusion.refs_1_, bf16[4,64,512]{2,1,0:T(8,128)(2,1)S(1)} %collective-permute-done.14.refs_2_, bf16[4,64,512]{2,1,0:T(8,128)(2,1)S(1)} %collective-permute-done.15.refs_3_, ...), custom_call_target="tpu_custom_call" | custom-call | flops 4294967296 | bytes 2097152 | tf_op jit(solution)/shard_map/expert_hidden/pallas_call | solution.py:267
  144.7 1.8 expert_down.5
  146.7 6.5 %expert_hidden.3.refs_1_ = bf16[256,1024]{1,0:T(8,128)(2,1)S(1)} custom-call(s32[8]{0:T(128)S(1)} %add.393.refs_0_, bf16[4,64,512]{2,1,0:T(8,128)(2,1)S(1)} %pad_maximum_fusion.2.refs_1_, bf16[4,64,512]{2,1,0:T(8,128)(2,1)S(1)} %collective-permute-done.35.refs_2_, bf16[4,64,512]{2,1,0:T(8,128)(2,1)} %collective-permute-done.36.refs_3_, ...), custom_call_target="tpu_custom_call" | custom-call | flops 4294967296 | bytes 2097152 | tf_op jit(solution)/shard_map/expert_hidden/pallas_call | solution.py:267
  153.2 1.8 expert_down.7
  155.5 1.8 expert_down.4
  157.3 1.8 expert_down.6
  160.5 1.5 collective-permute-start.43
  162.0 6.7 %collective-permute-done.22 = bf16[2,4,64,512]{3,2,1,0:T(8,128)(2,1)S(1)} collective-permute-done((bf16[2,4,64,512]{3,2,1,0:T(8,128)(2,1)S(1)}, bf16[2,4,64,512]{3,2,1,0:T(8,128)(2,1)S(1)}, u32[]{:S(2)}, u32[]{:S(2)}) %collective-permute-start.22) | collective-permute-done | bytes 524320 | tf_op jit(solution)/shard_map/ppermute | solution.py:52
  169.4 7.7 %collective-permute-done.43 = bf16[2,4,64,512]{3,2,1,0:T(8,128)(2,1)S(1)} collective-permute-done((bf16[2,4,64,512]{3,2,1,0:T(8,128)(2,1)S(1)}, bf16[2,4,64,512]{3,2,1,0:T(8,128)(2,1)S(1)}, u32[]{:S(2)}, u32[]{:S(2)}) %collective-permute-start.43) | collective-permute-done | bytes 524320 | tf_op jit(solution)/shard_map/ppermute | solution.py:52
  178.0 2.1 collective-permute-start.26
  180.0 1.1 collective-permute-start.25
  181.8 1.9 collective-permute-done.44
  183.8 2.0 collective-permute-start.47
  185.8 1.1 collective-permute-start.46
  187.5 1.1 collective-permute-done.25
  188.7 1.6 collective-permute-start.27
  190.3 1.1 collective-permute-done.46
  191.4 1.6 collective-permute-done.45
  193.8 3.2 %collective-permute-done.27.refs_1_ = bf16[4,64,512]{2,1,0:T(8,128)(2,1)S(1)} collective-permute-done((bf16[4,64,512]{2,1,0:T(8,128)(2,1)S(1)}, bf16[4,64,512]{2,1,0:T(8,128)(2,1)S(1)}, u32[]{:S(2)}, u32[]{:S(2)}) %collective-permute-start.27) | collective-permute-done | bytes 262176 | tf_op jit(solution)/shard_map/ppermute | solution.py:52
  197.0 2.0 collective-permute-start.49
  199.0 3.6 %collective-permute-done.48.refs_5_ = bf16[4,64,512]{2,1,0:T(8,128)(2,1)S(1)} collective-permute-done((bf16[4,64,512]{2,1,0:T(8,128)(2,1)S(1)}, bf16[4,64,512]{2,1,0:T(8,128)(2,1)S(1)}, u32[]{:S(2)}, u32[]{:S(2)}) %collective-permute-start.48) | collective-permute-done | bytes 262176 | tf_op jit(solution)/shard_map/ppermute | solution.py:52
  203.4 2.8 %collective-permute-done.49.refs_6_ = bf16[4,64,512]{2,1,0:T(8,128)(2,1)S(1)} collective-permute-done((bf16[4,64,512]{2,1,0:T(8,128)(2,1)S(1)}, bf16[4,64,512]{2,1,0:T(8,128)(2,1)S(1)}, u32[]{:S(2)}, u32[]{:S(2)}) %collective-permute-start.49) | collective-permute-done | bytes 262176 | tf_op jit(solution)/shard_map/ppermute | solution.py:52
  206.2 2.8 %collective-permute-done.50.refs_7_ = bf16[4,64,512]{2,1,0:T(8,128)(2,1)S(1)} collective-permute-done((bf16[4,64,512]{2,1,0:T(8,128)(2,1)S(1)}, bf16[4,64,512]{2,1,0:T(8,128)(2,1)S(1)}, u32[]{:S(2)}, u32[]{:S(2)}) %collective-permute-start.50) | collective-permute-done | bytes 262176 | tf_op jit(solution)/shard_map/ppermute | solution.py:52
  209.0 1.1 add_expert_rows.1
  210.4 1.8 collective-permute-done.51
  212.2 1.3 maximum_select_fusion
  (146 shorter events, 26.9 us)
Async XLA Ops:
  0.0 42.0 %copy-start = (s32[4,4]{1,0:T(4,128)S(1)}, s32[4,4]{1,0:T(4,128)}, u32[]{:S(2)}) copy-start(s32[4,4]{1,0:T(4,128)} %param.19) | copy-start | bytes 196
  1.3 2.5 %collective-permute-start = (bf16[512,512]{1,0:T(8,128)(2,1)S(1)}, bf16[512,512]{1,0:T(8,128)(2,1)S(1)}, u32[]{:S(2)}, u32[]{:S(2)}) collective-permute-start(bf16[512,512]{1,0:T(8,128)(2,1)S(1)} %get-tuple-element.32), channel_id=1, source_target_pairs={{0,4},{4,0},{8,12},{12,8},{16,20},{20,16},{24,28},{28,24},{1,5},{5... | collective-permute-start | bytes 1572872 | tf_op jit(solution)/shard_map/ppermute | solution.py:337
  3.8 2.2 %copy-start.7 = (bf16[512,4096]{1,0:T(8,128)(2,1)S(1)}, bf16[512,4096]{1,0:T(8,128)(2,1)}, u32[]{:S(2)}) copy-start(bf16[512,4096]{1,0:T(8,128)(2,1)} %x_ref.1) | copy-start | bytes 12582916
  6.0 12.1 %copy-start.8 = (bf16[512,1024]{1,0:T(8,128)(2,1)S(1)}, bf16[512,1024]{1,0:T(8,128)(2,1)}, u32[]{:S(2)}) copy-start(bf16[512,1024]{1,0:T(8,128)(2,1)} %param.14) | copy-start | bytes 3145732
  13.0 27.9 %collective-permute-start.1 = (bf16[2,512,2048]{2,1,0:T(8,128)(2,1)}, bf16[2,512,2048]{2,1,0:T(8,128)(2,1)}, u32[]{:S(2)}, u32[]{:S(2)}) collective-permute-start(bf16[2,512,2048]{2,1,0:T(8,128)(2,1)} %get-tuple-element.12), channel_id=1, source_target_pairs={{0,4},{4,0},{8,12},{12,8},{16,20},{20,16},{24,28},{28,24},{1,5},{5... | collective-permute-start | bytes 12582920 | tf_op jit(solution)/shard_map/ppermute | solution.py:337
  13.7 15.0 %collective-permute-start.2 = (bf16[512,512]{1,0:T(8,128)(2,1)S(1)}, bf16[512,512]{1,0:T(8,128)(2,1)S(1)}, u32[]{:S(2)}, u32[]{:S(2)}) collective-permute-start(bf16[512,512]{1,0:T(8,128)(2,1)S(1)} %get-tuple-element.31.refs_2_), channel_id=1, source_target_pairs={{0,8},{4,20},{8,0},{12,28},{16,24},{20,4},{24,16},{28,12},{1,9},{5... | collective-permute-start | bytes 1572872 | tf_op jit(solution)/shard_map/ppermute | solution.py:52
  16.6 33.3 %collective-permute-start.5 = (bf16[512,512]{1,0:T(8,128)(2,1)S(1)}, bf16[512,512]{1,0:T(8,128)(2,1)S(1)}, u32[]{:S(2)}, u32[]{:S(2)}) collective-permute-start(bf16[512,512]{1,0:T(8,128)(2,1)S(1)} %get-tuple-element.31.refs_2_), channel_id=1, source_target_pairs={{0,16},{4,12},{8,24},{12,4},{16,0},{20,28},{24,8},{28,20},{1,17},{... | collective-permute-start | bytes 1572872 | tf_op jit(solution)/shard_map/ppermute | solution.py:52
  19.0 30.9 %collective-permute-start.4 = (bf16[512,512]{1,0:T(8,128)(2,1)}, bf16[512,512]{1,0:T(8,128)(2,1)S(1)}, u32[]{:S(2)}, u32[]{:S(2)}) collective-permute-start(bf16[512,512]{1,0:T(8,128)(2,1)} %get-tuple-element.29), channel_id=1, source_target_pairs={{0,4},{4,0},{8,12},{12,8},{16,20},{20,16},{24,28},{28,24},{1,5},{5... | collective-permute-start | bytes 1572872 | tf_op jit(solution)/shard_map/ppermute | solution.py:337
  19.0 20.6 %collective-permute-start.3 = (bf16[512,512]{1,0:T(8,128)(2,1)S(1)}, bf16[512,512]{1,0:T(8,128)(2,1)}, u32[]{:S(2)}, u32[]{:S(2)}) collective-permute-start(bf16[512,512]{1,0:T(8,128)(2,1)S(1)} %collective-permute-done.after.refs_3_), channel_id=1, source_target_pairs={{0,8},{4,20},{8,0},{12,28},{16,24},{20,4},{24,16},{28,12},{1,9},{5... | collective-permute-start | bytes 1572872 | tf_op jit(solution)/shard_map/ppermute | solution.py:52
  28.7 21.3 %collective-permute-start.6 = (bf16[512,512]{1,0:T(8,128)(2,1)S(1)}, bf16[512,512]{1,0:T(8,128)(2,1)}, u32[]{:S(2)}, u32[]{:S(2)}) collective-permute-start(bf16[512,512]{1,0:T(8,128)(2,1)S(1)} %collective-permute-done.after.refs_3_), channel_id=1, source_target_pairs={{0,16},{4,12},{8,24},{12,4},{16,0},{20,28},{24,8},{28,20},{1,17},{... | collective-permute-start | bytes 1572872 | tf_op jit(solution)/shard_map/ppermute | solution.py:52
  39.6 10.3 %collective-permute-start.7 = (bf16[512,512]{1,0:T(8,128)(2,1)S(1)}, bf16[512,512]{1,0:T(8,128)(2,1)}, u32[]{:S(2)}, u32[]{:S(2)}) collective-permute-start(bf16[512,512]{1,0:T(8,128)(2,1)S(1)} %collective-permute-done.2.refs_4_.after), channel_id=1, source_target_pairs={{0,16},{4,12},{8,24},{12,4},{16,0},{20,28},{24,8},{28,20},{1,17},{... | collective-permute-start | bytes 1572872 | tf_op jit(solution)/shard_map/ppermute | solution.py:52
  40.9 13.7 %collective-permute-start.8 = (bf16[512,512]{1,0:T(8,128)(2,1)}, bf16[512,512]{1,0:T(8,128)(2,1)}, u32[]{:S(2)}, u32[]{:S(2)}) collective-permute-start(bf16[512,512]{1,0:T(8,128)(2,1)} %collective-permute-done.3.refs_5_), channel_id=1, source_target_pairs={{0,16},{4,12},{8,24},{12,4},{16,0},{20,28},{24,8},{28,20},{1,17},{... | collective-permute-start | bytes 1572872 | tf_op jit(solution)/shard_map/ppermute | solution.py:52
  43.4 2.2 %copy-start.3 = (bf16[2,512,2048]{2,1,0:T(8,128)(2,1)S(1)}, bf16[2,512,2048]{2,1,0:T(8,128)(2,1)}, u32[]{:S(2)}) copy-start(bf16[2,512,2048]{2,1,0:T(8,128)(2,1)} %copy-done.2) | copy-start | bytes 12582916
  45.6 8.9 %copy-start.4 = (bf16[2,512,2048]{2,1,0:T(8,128)(2,1)S(1)}, bf16[2,512,2048]{2,1,0:T(8,128)(2,1)}, u32[]{:S(2)}) copy-start(bf16[2,512,2048]{2,1,0:T(8,128)(2,1)} %copy-done.2) | copy-start | bytes 12582916
  59.6 20.0 %copy-start.9 = (f32[1,512]{1,0:T(1,128)S(1)}, f32[1,512]{1,0:T(1,128)}, u32[]{:S(2)}) copy-start(f32[1,512]{1,0:T(1,128)} %param.18) | copy-start | bytes 6148
  59.6 20.8 %copy-start.10 = (s32[4]{0:T(128)S(1)}, s32[4]{0:T(128)}, u32[]{:S(2)}) copy-start(s32[4]{0:T(128)} %param.20) | copy-start | bytes 52
  59.6 9.5 %collective-permute-start.9 = (bf16[2,4,64,512]{3,2,1,0:T(8,128)(2,1)S(1)}, bf16[2,4,64,512]{3,2,1,0:T(8,128)(2,1)S(1)}, u32[]{:S(2)}, u32[]{:S(2)}) collective-permute-start(bf16[2,4,64,512]{3,2,1,0:T(8,128)(2,1)S(1)} %bitcast.96), channel_id=1, source_target_pairs={{0,16},{4,12},{8,24},{12,4},{16,0},{20,28},{24,8},{28,20},{1,17},{... | collective-permute-start | bytes 1572872 | tf_op jit(solution)/shard_map/ppermute | solution.py:52
  69.2 8.2 %collective-permute-start.10 = (bf16[1,4,64,512]{3,2,1,0:T(8,128)(2,1)S(1)}, bf16[1,4,64,512]{3,2,1,0:T(8,128)(2,1)S(1)}, u32[]{:S(2)}, u32[]{:S(2)}) collective-permute-start(bf16[1,4,64,512]{3,2,1,0:T(8,128)(2,1)S(1)} %fusion.2), channel_id=1, source_target_pairs={{0,8},{4,20},{8,0},{12,28},{16,24},{20,4},{24,16},{28,12},{1,9},{5... | collective-permute-start | bytes 786440 | tf_op jit(solution)/shard_map/ppermute | solution.py:52
  78.1 10.7 %collective-permute-start.30 = (bf16[2,4,64,512]{3,2,1,0:T(8,128)(2,1)S(1)}, bf16[2,4,64,512]{3,2,1,0:T(8,128)(2,1)}, u32[]{:S(2)}, u32[]{:S(2)}) collective-permute-start(bf16[2,4,64,512]{3,2,1,0:T(8,128)(2,1)S(1)} %bitcast.95), channel_id=1, source_target_pairs={{0,16},{4,12},{8,24},{12,4},{16,0},{20,28},{24,8},{28,20},{1,17},{... | collective-permute-start | bytes 1572872 | tf_op jit(solution)/shard_map/ppermute | solution.py:52
  89.8 16.4 %collective-permute-start.31 = (bf16[1,4,64,512]{3,2,1,0:T(8,128)(2,1)S(1)}, bf16[1,4,64,512]{3,2,1,0:T(8,128)(2,1)S(1)}, u32[]{:S(2)}, u32[]{:S(2)}) collective-permute-start(bf16[1,4,64,512]{3,2,1,0:T(8,128)(2,1)S(1)} %fusion), channel_id=1, source_target_pairs={{0,8},{4,20},{8,0},{12,28},{16,24},{20,4},{24,16},{28,12},{1,9},{5... | collective-permute-start | bytes 786440 | tf_op jit(solution)/shard_map/ppermute | solution.py:52
  92.5 8.1 %collective-permute-start.13 = (bf16[64,512]{1,0:T(8,128)(2,1)S(1)}, bf16[64,512]{1,0:T(8,128)(2,1)S(1)}, u32[]{:S(2)}, u32[]{:S(2)}) collective-permute-start(bf16[64,512]{1,0:T(8,128)(2,1)S(1)} %get-tuple-element.46), channel_id=1, source_target_pairs={{0,3},{1,0},{2,1},{3,2},{4,7},{5,4},{6,5},{7,6},{8,11},{9,8},{10,9... | collective-permute-start | bytes 196616 | tf_op jit(solution)/shard_map/ppermute | solution.py:75
  98.7 5.2 %collective-permute-start.12 = (bf16[64,512]{1,0:T(8,128)(2,1)S(1)}, bf16[64,512]{1,0:T(8,128)(2,1)S(1)}, u32[]{:S(2)}, u32[]{:S(2)}) collective-permute-start(bf16[64,512]{1,0:T(8,128)(2,1)S(1)} %get-tuple-element.47), channel_id=1, source_target_pairs={{0,2},{1,3},{2,0},{3,1},{4,6},{5,7},{6,4},{7,5},{8,10},{9,11},{10,... | collective-permute-start | bytes 196616 | tf_op jit(solution)/shard_map/ppermute | solution.py:75
  98.7 6.1 %collective-permute-start.11 = (bf16[64,512]{1,0:T(8,128)(2,1)S(1)}, bf16[64,512]{1,0:T(8,128)(2,1)S(1)}, u32[]{:S(2)}, u32[]{:S(2)}) collective-permute-start(bf16[64,512]{1,0:T(8,128)(2,1)S(1)} %get-tuple-element.48), channel_id=1, source_target_pairs={{0,1},{1,2},{2,3},{3,0},{4,5},{5,6},{6,7},{7,4},{8,9},{9,10},{10,1... | collective-permute-start | bytes 196616 | tf_op jit(solution)/shard_map/ppermute | solution.py:75
  104.8 6.5 %collective-permute-start.14 = (bf16[4,64,512]{2,1,0:T(8,128)(2,1)S(1)}, bf16[4,64,512]{2,1,0:T(8,128)(2,1)S(1)}, u32[]{:S(2)}, u32[]{:S(2)}) collective-permute-start(bf16[4,64,512]{2,1,0:T(8,128)(2,1)S(1)} %pad_maximum_fusion.refs_1_), channel_id=1, source_target_pairs={{0,8},{4,20},{8,0},{12,28},{16,24},{20,4},{24,16},{28,12},{1,9},{5... | collective-permute-start | bytes 786440 | tf_op jit(solution)/shard_map/ppermute | solution.py:52
  107.3 4.3 %collective-permute-start.34 = (bf16[64,512]{1,0:T(8,128)(2,1)S(1)}, bf16[64,512]{1,0:T(8,128)(2,1)S(1)}, u32[]{:S(2)}, u32[]{:S(2)}) collective-permute-start(bf16[64,512]{1,0:T(8,128)(2,1)S(1)} %get-tuple-element.38), channel_id=1, source_target_pairs={{0,3},{1,0},{2,1},{3,2},{4,7},{5,4},{6,5},{7,6},{8,11},{9,8},{10,9... | collective-permute-start | bytes 196616 | tf_op jit(solution)/shard_map/ppermute | solution.py:75
  108.8 6.6 %collective-permute-start.33 = (bf16[64,512]{1,0:T(8,128)(2,1)S(1)}, bf16[64,512]{1,0:T(8,128)(2,1)S(1)}, u32[]{:S(2)}, u32[]{:S(2)}) collective-permute-start(bf16[64,512]{1,0:T(8,128)(2,1)S(1)} %get-tuple-element.39), channel_id=1, source_target_pairs={{0,2},{1,3},{2,0},{3,1},{4,6},{5,7},{6,4},{7,5},{8,10},{9,11},{10,... | collective-permute-start | bytes 196616 | tf_op jit(solution)/shard_map/ppermute | solution.py:75
  108.8 6.6 %collective-permute-start.32 = (bf16[64,512]{1,0:T(8,128)(2,1)S(1)}, bf16[64,512]{1,0:T(8,128)(2,1)S(1)}, u32[]{:S(2)}, u32[]{:S(2)}) collective-permute-start(bf16[64,512]{1,0:T(8,128)(2,1)S(1)} %get-tuple-element.40), channel_id=1, source_target_pairs={{0,1},{1,2},{2,3},{3,0},{4,5},{5,6},{6,7},{7,4},{8,9},{9,10},{10,1... | collective-permute-start | bytes 196616 | tf_op jit(solution)/shard_map/ppermute | solution.py:75
  110.8 7.9 %collective-permute-start.15 = (bf16[4,64,512]{2,1,0:T(8,128)(2,1)S(1)}, bf16[4,64,512]{2,1,0:T(8,128)(2,1)S(1)}, u32[]{:S(2)}, u32[]{:S(2)}) collective-permute-start(bf16[4,64,512]{2,1,0:T(8,128)(2,1)S(1)} %pad_maximum_fusion.refs_1_), channel_id=1, source_target_pairs={{0,16},{4,12},{8,24},{12,4},{16,0},{20,28},{24,8},{28,20},{1,17},{... | collective-permute-start | bytes 786440 | tf_op jit(solution)/shard_map/ppermute | solution.py:52
  111.4 11.5 %collective-permute-start.17 = (bf16[4,64,512]{2,1,0:T(8,128)(2,1)S(1)}, bf16[4,64,512]{2,1,0:T(8,128)(2,1)S(1)}, u32[]{:S(2)}, u32[]{:S(2)}) collective-permute-start(bf16[4,64,512]{2,1,0:T(8,128)(2,1)S(1)} %pad_maximum_fusion.refs_1_), channel_id=1, source_target_pairs={{0,4},{4,0},{8,12},{12,8},{16,20},{20,16},{24,28},{28,24},{1,5},{5... | collective-permute-start | bytes 786440 | tf_op jit(solution)/shard_map/ppermute | solution.py:337
  111.7 11.2 %collective-permute-start.16 = (bf16[4,64,512]{2,1,0:T(8,128)(2,1)S(1)}, bf16[4,64,512]{2,1,0:T(8,128)(2,1)}, u32[]{:S(2)}, u32[]{:S(2)}) collective-permute-start(bf16[4,64,512]{2,1,0:T(8,128)(2,1)S(1)} %collective-permute-done.14.refs_2_), channel_id=1, source_target_pairs={{0,16},{4,12},{8,24},{12,4},{16,0},{20,28},{24,8},{28,20},{1,17},{... | collective-permute-start | bytes 786440 | tf_op jit(solution)/shard_map/ppermute | solution.py:52
  115.4 8.0 %collective-permute-start.35 = (bf16[4,64,512]{2,1,0:T(8,128)(2,1)S(1)}, bf16[4,64,512]{2,1,0:T(8,128)(2,1)S(1)}, u32[]{:S(2)}, u32[]{:S(2)}) collective-permute-start(bf16[4,64,512]{2,1,0:T(8,128)(2,1)S(1)} %pad_maximum_fusion.2.refs_1_), channel_id=1, source_target_pairs={{0,8},{4,20},{8,0},{12,28},{16,24},{20,4},{24,16},{28,12},{1,9},{5... | collective-permute-start | bytes 786440 | tf_op jit(solution)/shard_map/ppermute | solution.py:52
  116.2 20.8 %collective-permute-start.19 = (bf16[4,64,512]{2,1,0:T(8,128)(2,1)S(1)}, bf16[4,64,512]{2,1,0:T(8,128)(2,1)}, u32[]{:S(2)}, u32[]{:S(2)}) collective-permute-start(bf16[4,64,512]{2,1,0:T(8,128)(2,1)S(1)} %collective-permute-done.14.refs_2_), channel_id=1, source_target_pairs={{0,4},{4,0},{8,12},{12,8},{16,20},{20,16},{24,28},{28,24},{1,5},{5... | collective-permute-start | bytes 786440 | tf_op jit(solution)/shard_map/ppermute | solution.py:337
  118.7 18.2 %collective-permute-start.18 = (bf16[4,64,512]{2,1,0:T(8,128)(2,1)S(1)}, bf16[4,64,512]{2,1,0:T(8,128)(2,1)}, u32[]{:S(2)}, u32[]{:S(2)}) collective-permute-start(bf16[4,64,512]{2,1,0:T(8,128)(2,1)S(1)} %collective-permute-done.15.refs_3_), channel_id=1, source_target_pairs={{0,4},{4,0},{8,12},{12,8},{16,20},{20,16},{24,28},{28,24},{1,5},{5... | collective-permute-start | bytes 786440 | tf_op jit(solution)/shard_map/ppermute | solution.py:337
  122.9 15.1 %collective-permute-start.20 = (bf16[4,64,512]{2,1,0:T(8,128)(2,1)}, bf16[4,64,512]{2,1,0:T(8,128)(2,1)}, u32[]{:S(2)}, u32[]{:S(2)}) collective-permute-start(bf16[4,64,512]{2,1,0:T(8,128)(2,1)} %collective-permute-done.16.refs_4_), channel_id=1, source_target_pairs={{0,4},{4,0},{8,12},{12,8},{16,20},{20,16},{24,28},{28,24},{1,5},{5... | collective-permute-start | bytes 786440 | tf_op jit(solution)/shard_map/ppermute | solution.py:337
  122.9 14.6 %collective-permute-start.36 = (bf16[4,64,512]{2,1,0:T(8,128)(2,1)S(1)}, bf16[4,64,512]{2,1,0:T(8,128)(2,1)}, u32[]{:S(2)}, u32[]{:S(2)}) collective-permute-start(bf16[4,64,512]{2,1,0:T(8,128)(2,1)S(1)} %pad_maximum_fusion.2.refs_1_), channel_id=1, source_target_pairs={{0,16},{4,12},{8,24},{12,4},{16,0},{20,28},{24,8},{28,20},{1,17},{... | collective-permute-start | bytes 786440 | tf_op jit(solution)/shard_map/ppermute | solution.py:52
  123.5 14.1 %collective-permute-start.37 = (bf16[4,64,512]{2,1,0:T(8,128)(2,1)S(1)}, bf16[4,64,512]{2,1,0:T(8,128)(2,1)}, u32[]{:S(2)}, u32[]{:S(2)}) collective-permute-start(bf16[4,64,512]{2,1,0:T(8,128)(2,1)S(1)} %collective-permute-done.35.refs_2_), channel_id=1, source_target_pairs={{0,16},{4,12},{8,24},{12,4},{16,0},{20,28},{24,8},{28,20},{1,17},{... | collective-permute-start | bytes 786440 | tf_op jit(solution)/shard_map/ppermute | solution.py:52
  126.4 3.4 %copy-start.5 = (bf16[1,4096,1024]{2,1,0:T(8,128)(2,1)S(1)}, bf16[1,4096,1024]{2,1,0:T(8,128)(2,1)}, u32[]{:S(2)}) copy-start(bf16[1,4096,1024]{2,1,0:T(8,128)(2,1)} %param.15) | copy-start | bytes 25165828
  129.8 4.8 %slice-start = ((s8[8388608]{0:T(1024)(128)(4,1)}), s8[4194304]{0:T(1024)(128)(4,1)S(1)}, s32[]{:S(2)}) async-start(s8[8388608]{0:T(1024)(128)(4,1)} %bitcast.91), calls=%async_computation | async-start | bytes 8388608
  130.4 3.7 %copy-start.6 = (bf16[1,4096,1024]{2,1,0:T(8,128)(2,1)S(1)}, bf16[1,4096,1024]{2,1,0:T(8,128)(2,1)}, u32[]{:S(2)}) copy-start(bf16[1,4096,1024]{2,1,0:T(8,128)(2,1)} %param.16) | copy-start | bytes 25165828
  134.1 2.3 %slice-start.1 = ((s8[8388608]{0:T(1024)(128)(4,1)}), s8[4194304]{0:T(1024)(128)(4,1)S(1)}, s32[]{:S(2)}) async-start(s8[8388608]{0:T(1024)(128)(4,1)} %bitcast.91), calls=%async_computation.1 | async-start | bytes 8388608
  136.9 9.8 %collective-permute-start.38 = (bf16[4,64,512]{2,1,0:T(8,128)(2,1)S(1)}, bf16[4,64,512]{2,1,0:T(8,128)(2,1)S(1)}, u32[]{:S(2)}, u32[]{:S(2)}) collective-permute-start(bf16[4,64,512]{2,1,0:T(8,128)(2,1)S(1)} %pad_maximum_fusion.2.refs_1_), channel_id=1, source_target_pairs={{0,4},{4,0},{8,12},{12,8},{16,20},{20,16},{24,28},{28,24},{1,5},{5... | collective-permute-start | bytes 786440 | tf_op jit(solution)/shard_map/ppermute | solution.py:337
  137.0 9.7 %collective-permute-start.40 = (bf16[4,64,512]{2,1,0:T(8,128)(2,1)S(1)}, bf16[4,64,512]{2,1,0:T(8,128)(2,1)S(1)}, u32[]{:S(2)}, u32[]{:S(2)}) collective-permute-start(bf16[4,64,512]{2,1,0:T(8,128)(2,1)S(1)} %collective-permute-done.35.refs_2_), channel_id=1, source_target_pairs={{0,4},{4,0},{8,12},{12,8},{16,20},{20,16},{24,28},{28,24},{1,5},{5... | collective-permute-start | bytes 786440 | tf_op jit(solution)/shard_map/ppermute | solution.py:337
  137.5 9.2 %collective-permute-start.39 = (bf16[4,64,512]{2,1,0:T(8,128)(2,1)}, bf16[4,64,512]{2,1,0:T(8,128)(2,1)S(1)}, u32[]{:S(2)}, u32[]{:S(2)}) collective-permute-start(bf16[4,64,512]{2,1,0:T(8,128)(2,1)} %collective-permute-done.36.refs_3_), channel_id=1, source_target_pairs={{0,4},{4,0},{8,12},{12,8},{16,20},{20,16},{24,28},{28,24},{1,5},{5... | collective-permute-start | bytes 786440 | tf_op jit(solution)/shard_map/ppermute | solution.py:337
  137.6 9.1 %collective-permute-start.41 = (bf16[4,64,512]{2,1,0:T(8,128)(2,1)}, bf16[4,64,512]{2,1,0:T(8,128)(2,1)S(1)}, u32[]{:S(2)}, u32[]{:S(2)}) collective-permute-start(bf16[4,64,512]{2,1,0:T(8,128)(2,1)} %collective-permute-done.37.refs_4_), channel_id=1, source_target_pairs={{0,4},{4,0},{8,12},{12,8},{16,20},{20,16},{24,28},{28,24},{1,5},{5... | collective-permute-start | bytes 786440 | tf_op jit(solution)/shard_map/ppermute | solution.py:337
  146.5 12.6 %collective-permute-start.21 = (bf16[4,4,64,512]{3,2,1,0:T(8,128)(2,1)S(1)}, bf16[4,4,64,512]{3,2,1,0:T(8,128)(2,1)S(1)}, u32[]{:S(2)}, u32[]{:S(2)}) collective-permute-start(bf16[4,4,64,512]{3,2,1,0:T(8,128)(2,1)S(1)} %expert_down.5), channel_id=1, source_target_pairs={{0,4},{4,0},{8,12},{12,8},{16,20},{20,16},{24,28},{28,24},{1,5},{5... | collective-permute-start | bytes 3145736 | tf_op jit(solution)/shard_map/ppermute | solution.py:337
  155.0 5.1 %collective-permute-start.42 = (bf16[4,4,64,512]{3,2,1,0:T(8,128)(2,1)S(1)}, bf16[4,4,64,512]{3,2,1,0:T(8,128)(2,1)S(1)}, u32[]{:S(2)}, u32[]{:S(2)}) collective-permute-start(bf16[4,4,64,512]{3,2,1,0:T(8,128)(2,1)S(1)} %expert_down.7), channel_id=1, source_target_pairs={{0,4},{4,0},{8,12},{12,8},{16,20},{20,16},{24,28},{28,24},{1,5},{5... | collective-permute-start | bytes 3145736 | tf_op jit(solution)/shard_map/ppermute | solution.py:337
  159.5 9.2 %collective-permute-start.22 = (bf16[2,4,64,512]{3,2,1,0:T(8,128)(2,1)S(1)}, bf16[2,4,64,512]{3,2,1,0:T(8,128)(2,1)S(1)}, u32[]{:S(2)}, u32[]{:S(2)}) collective-permute-start(bf16[2,4,64,512]{3,2,1,0:T(8,128)(2,1)S(1)} %get-tuple-element.26), channel_id=1, source_target_pairs={{0,16},{4,12},{8,24},{12,4},{16,0},{20,28},{24,8},{28,20},{1,17},{... | collective-permute-start | bytes 1572872 | tf_op jit(solution)/shard_map/ppermute | solution.py:52
  160.5 16.7 %collective-permute-start.43 = (bf16[2,4,64,512]{3,2,1,0:T(8,128)(2,1)S(1)}, bf16[2,4,64,512]{3,2,1,0:T(8,128)(2,1)S(1)}, u32[]{:S(2)}, u32[]{:S(2)}) collective-permute-start(bf16[2,4,64,512]{3,2,1,0:T(8,128)(2,1)S(1)} %get-tuple-element.24), channel_id=1, source_target_pairs={{0,16},{4,12},{8,24},{12,4},{16,0},{20,28},{24,8},{28,20},{1,17},{... | collective-permute-start | bytes 1572872 | tf_op jit(solution)/shard_map/ppermute | solution.py:52
  168.8 9.0 %collective-permute-start.23 = (bf16[1,4,64,512]{3,2,1,0:T(8,128)(2,1)S(1)}, bf16[1,4,64,512]{3,2,1,0:T(8,128)(2,1)S(1)}, u32[]{:S(2)}, u32[]{:S(2)}) collective-permute-start(bf16[1,4,64,512]{3,2,1,0:T(8,128)(2,1)S(1)} %add_convert_fusion.9), channel_id=1, source_target_pairs={{0,8},{4,20},{8,0},{12,28},{16,24},{20,4},{24,16},{28,12},{1,9},{5... | collective-permute-start | bytes 786440 | tf_op jit(solution)/shard_map/ppermute | solution.py:52
  177.2 6.4 %collective-permute-start.44 = (bf16[1,4,64,512]{3,2,1,0:T(8,128)(2,1)S(1)}, bf16[1,4,64,512]{3,2,1,0:T(8,128)(2,1)S(1)}, u32[]{:S(2)}, u32[]{:S(2)}) collective-permute-start(bf16[1,4,64,512]{3,2,1,0:T(8,128)(2,1)S(1)} %add_convert_fusion.5), channel_id=1, source_target_pairs={{0,8},{4,20},{8,0},{12,28},{16,24},{20,4},{24,16},{28,12},{1,9},{5... | collective-permute-start | bytes 786440 | tf_op jit(solution)/shard_map/ppermute | solution.py:52
  178.0 8.9 %collective-permute-start.26 = (bf16[64,512]{1,0:T(8,128)(2,1)S(1)}, bf16[64,512]{1,0:T(8,128)(2,1)S(1)}, u32[]{:S(2)}, u32[]{:S(2)}) collective-permute-start(bf16[64,512]{1,0:T(8,128)(2,1)S(1)} %get-tuple-element.42), channel_id=1, source_target_pairs={{0,3},{1,0},{2,1},{3,2},{4,7},{5,4},{6,5},{7,6},{8,11},{9,8},{10,9... | collective-permute-start | bytes 196616 | tf_op jit(solution)/shard_map/ppermute | solution.py:75
  180.0 8.6 %collective-permute-start.25 = (bf16[64,512]{1,0:T(8,128)(2,1)S(1)}, bf16[64,512]{1,0:T(8,128)(2,1)S(1)}, u32[]{:S(2)}, u32[]{:S(2)}) collective-permute-start(bf16[64,512]{1,0:T(8,128)(2,1)S(1)} %get-tuple-element.43), channel_id=1, source_target_pairs={{0,2},{1,3},{2,0},{3,1},{4,6},{5,7},{6,4},{7,5},{8,10},{9,11},{10,... | collective-permute-start | bytes 196616 | tf_op jit(solution)/shard_map/ppermute | solution.py:75
  181.1 7.5 %collective-permute-start.24 = (bf16[64,512]{1,0:T(8,128)(2,1)S(1)}, bf16[64,512]{1,0:T(8,128)(2,1)S(1)}, u32[]{:S(2)}, u32[]{:S(2)}) collective-permute-start(bf16[64,512]{1,0:T(8,128)(2,1)S(1)} %get-tuple-element.44), channel_id=1, source_target_pairs={{0,1},{1,2},{2,3},{3,0},{4,5},{5,6},{6,7},{7,4},{8,9},{9,10},{10,1... | collective-permute-start | bytes 196616 | tf_op jit(solution)/shard_map/ppermute | solution.py:75
  183.8 6.5 %collective-permute-start.47 = (bf16[64,512]{1,0:T(8,128)(2,1)S(1)}, bf16[64,512]{1,0:T(8,128)(2,1)S(1)}, u32[]{:S(2)}, u32[]{:S(2)}) collective-permute-start(bf16[64,512]{1,0:T(8,128)(2,1)S(1)} %get-tuple-element.34), channel_id=1, source_target_pairs={{0,3},{1,0},{2,1},{3,2},{4,7},{5,4},{6,5},{7,6},{8,11},{9,8},{10,9... | collective-permute-start | bytes 196616 | tf_op jit(solution)/shard_map/ppermute | solution.py:75
  185.8 5.6 %collective-permute-start.46 = (bf16[64,512]{1,0:T(8,128)(2,1)S(1)}, bf16[64,512]{1,0:T(8,128)(2,1)S(1)}, u32[]{:S(2)}, u32[]{:S(2)}) collective-permute-start(bf16[64,512]{1,0:T(8,128)(2,1)S(1)} %get-tuple-element.35), channel_id=1, source_target_pairs={{0,2},{1,3},{2,0},{3,1},{4,6},{5,7},{6,4},{7,5},{8,10},{9,11},{10,... | collective-permute-start | bytes 196616 | tf_op jit(solution)/shard_map/ppermute | solution.py:75
  186.9 6.1 %collective-permute-start.45 = (bf16[64,512]{1,0:T(8,128)(2,1)S(1)}, bf16[64,512]{1,0:T(8,128)(2,1)S(1)}, u32[]{:S(2)}, u32[]{:S(2)}) collective-permute-start(bf16[64,512]{1,0:T(8,128)(2,1)S(1)} %get-tuple-element.36), channel_id=1, source_target_pairs={{0,1},{1,2},{2,3},{3,0},{4,5},{5,6},{6,7},{7,4},{8,9},{9,10},{10,1... | collective-permute-start | bytes 196616 | tf_op jit(solution)/shard_map/ppermute | solution.py:75
  188.7 8.3 %collective-permute-start.27 = (bf16[4,64,512]{2,1,0:T(8,128)(2,1)S(1)}, bf16[4,64,512]{2,1,0:T(8,128)(2,1)S(1)}, u32[]{:S(2)}, u32[]{:S(2)}) collective-permute-start(bf16[4,64,512]{2,1,0:T(8,128)(2,1)S(1)} %pad_maximum_fusion.1.refs_0_), channel_id=1, source_target_pairs={{0,8},{4,20},{8,0},{12,28},{16,24},{20,4},{24,16},{28,12},{1,9},{5... | collective-permute-start | bytes 786440 | tf_op jit(solution)/shard_map/ppermute | solution.py:52
  193.0 9.6 %collective-permute-start.48 = (bf16[4,64,512]{2,1,0:T(8,128)(2,1)S(1)}, bf16[4,64,512]{2,1,0:T(8,128)(2,1)S(1)}, u32[]{:S(2)}, u32[]{:S(2)}) collective-permute-start(bf16[4,64,512]{2,1,0:T(8,128)(2,1)S(1)} %pad_maximum_fusion.3.refs_4_), channel_id=1, source_target_pairs={{0,8},{4,20},{8,0},{12,28},{16,24},{20,4},{24,16},{28,12},{1,9},{5... | collective-permute-start | bytes 786440 | tf_op jit(solution)/shard_map/ppermute | solution.py:52
  193.7 9.0 %collective-permute-start.28 = (bf16[4,64,512]{2,1,0:T(8,128)(2,1)S(1)}, bf16[4,64,512]{2,1,0:T(8,128)(2,1)S(1)}, u32[]{:S(2)}, u32[]{:S(2)}) collective-permute-start(bf16[4,64,512]{2,1,0:T(8,128)(2,1)S(1)} %pad_maximum_fusion.1.refs_0_), channel_id=1, source_target_pairs={{0,16},{4,12},{8,24},{12,4},{16,0},{20,28},{24,8},{28,20},{1,17},{... | collective-permute-start | bytes 786440 | tf_op jit(solution)/shard_map/ppermute | solution.py:52
  197.0 6.4 %collective-permute-start.29 = (bf16[4,64,512]{2,1,0:T(8,128)(2,1)S(1)}, bf16[4,64,512]{2,1,0:T(8,128)(2,1)S(1)}, u32[]{:S(2)}, u32[]{:S(2)}) collective-permute-start(bf16[4,64,512]{2,1,0:T(8,128)(2,1)S(1)} %collective-permute-done.27.refs_1_), channel_id=1, source_target_pairs={{0,16},{4,12},{8,24},{12,4},{16,0},{20,28},{24,8},{28,20},{1,17},{... | collective-permute-start | bytes 786440 | tf_op jit(solution)/shard_map/ppermute | solution.py:52
  197.0 9.2 %collective-permute-start.49 = (bf16[4,64,512]{2,1,0:T(8,128)(2,1)S(1)}, bf16[4,64,512]{2,1,0:T(8,128)(2,1)S(1)}, u32[]{:S(2)}, u32[]{:S(2)}) collective-permute-start(bf16[4,64,512]{2,1,0:T(8,128)(2,1)S(1)} %pad_maximum_fusion.3.refs_4_), channel_id=1, source_target_pairs={{0,16},{4,12},{8,24},{12,4},{16,0},{20,28},{24,8},{28,20},{1,17},{... | collective-permute-start | bytes 786440 | tf_op jit(solution)/shard_map/ppermute | solution.py:52
  202.6 6.4 %collective-permute-start.50 = (bf16[4,64,512]{2,1,0:T(8,128)(2,1)S(1)}, bf16[4,64,512]{2,1,0:T(8,128)(2,1)S(1)}, u32[]{:S(2)}, u32[]{:S(2)}) collective-permute-start(bf16[4,64,512]{2,1,0:T(8,128)(2,1)S(1)} %collective-permute-done.48.refs_5_), channel_id=1, source_target_pairs={{0,16},{4,12},{8,24},{12,4},{16,0},{20,28},{24,8},{28,20},{1,17},{... | collective-permute-start | bytes 786440 | tf_op jit(solution)/shard_map/ppermute | solution.py:52
  202.6 10.8 %copy-start.1 = (s32[4,4]{1,0:T(4,128)S(1)}, s32[4,4]{1,0:T(4,128)}, u32[]{:S(2)}) copy-start(s32[4,4]{1,0:T(4,128)} %param.19) | copy-start | bytes 196
  210.2 2.0 collective-permute-start.51
  (1 other events, 2.0 us)

commit v3 on v2

v3 whole, which is shorter than its diff:
```python
import jax
import jax.numpy as jnp
from jax import lax
from jax.experimental import pallas as pl
from jax.experimental.pallas import tpu as pltpu
from jax.sharding import PartitionSpec as P

BLK = 128
CAP = 4
GROUPS = 2


def bit_orders(n_bits):
    forward = list(range(1, n_bits + 1))
    return forward, forward[::-1]


def step_pairs(n_dp, step):
    orders = bit_orders(n_dp.bit_length() - 2)
    return [(i, i ^ (1 << orders[i & 1][step])) for i in range(n_dp)]


def pair_pairs(n_dp):
    return [(i, i ^ 1) for i in range(n_dp)]


def masks_of(n_bits, side):
    order = bit_orders(n_bits)[side]
    return [
        sum(1 << (order[t] - 1) for t in range(n_bits) if (r >> t) & 1) for r in range(1 << n_bits)
    ]


def bit_reversed(n_bits):
    return [
        sum(1 << (n_bits - 1 - t) for t in range(n_bits) if (r >> t) & 1)
        for r in range(1 << n_bits)
    ]


SMEM = pl.BlockSpec(memory_space=pltpu.SMEM)
VMEM = pl.BlockSpec(memory_space=pltpu.VMEM)
ANY = pl.BlockSpec(memory_space=pl.ANY)
MIB = 1024 * 1024


def f32_sum(a, b):
    return (a.astype(jnp.float32) + b.astype(jnp.float32)).astype(jnp.bfloat16)


def exchange(value, n_dp, step):
    return lax.ppermute(value, "dp", step_pairs(n_dp, step))


def scatter_sum(keep, send, n_dp, n_bits, afters=()):
    seen = []
    for i, step in enumerate(range(n_bits - 1, -1, -1)):
        got = exchange(send, n_dp, step)
        keep, send = add_split(keep, got, afters[i] if i < len(afters) else None, step > 0)
        seen.append(keep)
    return keep[0], seen


def gather_all(piece, n_dp, n_bits):
    pieces = [piece]
    for step in range(n_bits):
        pieces = pieces + [exchange(p, n_dp, step) for p in pieces]
    return pieces


def swap_planes(parts, n_expert, after=None):
    out = [parts[0]]
    for k in range(1, n_expert):
        pairs = [(i, (i + k) % n_expert) for i in range(n_expert)]
        out.append(lax.ppermute(parts[k], "expert", pairs))
    return stack(out, after)


def call(kernel, out_shape, in_specs, out_specs, name, limit, flops=0, moved=0, **more):
    return pl.pallas_call(
        kernel,
        out_shape=out_shape,
        in_specs=in_specs,
        out_specs=out_specs,
        compiler_params=pltpu.CompilerParams(vmem_limit_bytes=limit * MIB),
        cost_estimate=pl.CostEstimate(flops=flops, bytes_accessed=moved, transcendentals=0),
        name=name,
        **more,
    )


def add_split_kernel(split, keep, got, *refs):
    out = refs[1:] if len(refs) > (2 if split else 1) else refs
    n = out[0].shape[0]
    for i in range(keep.shape[0]):
        value = f32_sum(keep[i], got[i])
        if i < n:
            out[0][i] = value
        else:
            out[1][i - n] = value


def add_split(keep, got, after, split):
    n = keep.shape[0]
    shape = jax.ShapeDtypeStruct((n // 2 if split else n,) + keep.shape[1:], keep.dtype)
    extra = [] if after is None else [after]
    out = call(
        lambda *refs: add_split_kernel(split, *refs),
        [shape] * (2 if split else 1),
        [VMEM, VMEM] + [ANY] * len(extra),
        [VMEM] * (2 if split else 1),
        "add_halves",
        8,
        moved=2 * keep.size,
    )(keep, got, *extra)
    return out if split else (out[0], None)


def stack_kernel(n, *refs):
    for i in range(n):
        refs[-1][i] = refs[i][...]


def stack(parts, after):
    extra = [] if after is None else [after]
    return call(
        lambda *refs: stack_kernel(len(parts), *refs),
        jax.ShapeDtypeStruct((len(parts),) + parts[0].shape, parts[0].dtype),
        [VMEM] * len(parts) + [ANY] * len(extra),
        VMEM,
        "stack_planes",
        8,
        moved=2 * len(parts) * parts[0].size,
    )(*parts, *extra)


class Place:
    def __init__(self, n_bits, n_expert):
        data = lax.axis_index("dp")
        self.chip, self.side = lax.div(data, 2), lax.rem(data, 2)
        self.expert = lax.axis_index("expert")
        self.n_expert = n_expert
        self.n_bits = n_bits

    def chip_at(self, r):
        first, second = (masks_of(self.n_bits, s)[r] for s in (0, 1))
        return self.chip ^ jnp.where(self.side == 0, first, second)

    def ahead(self, k):
        return lax.rem(self.expert + k, self.n_expert)

    def behind(self, k):
        return lax.rem(self.expert + (self.n_expert - k), self.n_expert)


class Layout:
    def __init__(self, group, n_chip, local_blocks):
        self.rows = CAP * BLK // GROUPS
        self.share = self.rows // n_chip
        self.group, self.local_blocks = group, local_blocks

    def first_row(self, place, r):
        return self.group * self.rows + place.chip_at(r) * self.share

    def grain(self, place, chosen, r, expert):
        row = self.first_row(place, r)
        block = chosen[expert, lax.div(row, BLK)]
        owner = lax.div(block, self.local_blocks)
        base = jnp.where(lax.rem(owner, 2) == place.side, 0, self.local_blocks)
        base = base + lax.rem(block, self.local_blocks)
        index = base * (BLK // self.share) + lax.div(lax.rem(row, BLK), self.share)
        return index, lax.div(owner, 2) == place.chip


def load_kernel(src, after, out, sem):
    copy = pltpu.make_async_copy(src, out, sem)
    copy.start()
    copy.wait()


def load(weight, after, name):
    out = call(
        load_kernel,
        pltpu.VMEM(weight.shape, weight.dtype),
        [ANY, ANY],
        VMEM,
        name,
        1,
        moved=2 * weight.size,
        scratch_shapes=[pltpu.SemaphoreType.DMA],
    )(weight, after)
    return pltpu.with_memory_space_constraint(out, pltpu.VMEM)


def project_kernel(make_place, parts, n_w, n_res, *refs):
    context, other = refs[:2]
    weights = refs[2 : 2 + n_w]
    extra = refs[2 + n_w : 2 + n_w + n_res]
    out, w_all, c_own, c_other, sems = refs[-5:]
    depth = weights[0].shape[0]
    place = make_place()
    copies = []
    for i, (src, dst) in enumerate(((context, c_own), (other, c_other))):
        for j, r in enumerate(parts):
            for s in range(2):
                at = (place.chip_at(r) * 2 + (place.side ^ s)) * depth
                at = pl.ds(pl.multiple_of(at, depth), depth)
                n = 2 * j + s
                copies.append(
                    pltpu.make_async_copy(
                        src.at[:, at], dst.at[:, n * depth : (n + 1) * depth], sems.at[i, n]
                    )
                )
    for c in copies:
        c.start()
    for i, w in enumerate(weights):
        w_all[i * depth : (i + 1) * depth, :] = w[...]
    for i, c in enumerate((c_own, c_other)):
        for copy in copies[i * n_w : (i + 1) * n_w]:
            copy.wait()
        value = jnp.dot(c[...], w_all[...], preferred_element_type=jnp.float32)
        if n_res:
            acc, *res = extra
            value = value + acc[i] + res[i][...].astype(jnp.float32)
        out[i] = value.astype(out.dtype)


def project(make_place, parts, own, other, weights, extra, held):
    last = len(extra) > 0
    rows = own.shape[0]
    depth, half = weights[0].shape
    k = depth * len(weights)
    return call(
        lambda *refs: project_kernel(make_place, parts, len(weights), len(extra), *refs),
        jax.ShapeDtypeStruct((2, rows, half), jnp.bfloat16 if last else jnp.float32),
        [ANY, ANY] + [VMEM] * (len(weights) + len(extra) + len(held)),
        VMEM,
        "project_last" if last else "project_first",
        20,
        flops=4 * rows * k * half,
        moved=6 * rows * k,
        scratch_shapes=[
            pltpu.VMEM((k, half), jnp.bfloat16),
            pltpu.VMEM((rows, k), jnp.bfloat16),
            pltpu.VMEM((rows, k), jnp.bfloat16),
            pltpu.SemaphoreType.DMA((2, len(weights))),
        ],
    )(own, other, *weights, *extra, *held)


def pick_kernel(make_place, layout, n_chip, chosen, att_ref, *refs):
    place = make_place()
    keep_ref, send_ref = refs[-2:]
    top = n_chip // 2
    for r in range(n_chip):
        for k in range(place.n_expert):
            index, mine = layout.grain(place, chosen, r, place.ahead(k))
            value = att_ref[jnp.where(mine, index, 0)]
            value = jnp.where(mine, value, jnp.zeros_like(value))
            if r < top:
                keep_ref[r, k] = value
            else:
                send_ref[r - top, k] = value


def pick(make_place, layout, n_chip, n_expert, chosen, grains, after):
    shape = (n_chip // 2, n_expert) + grains.shape[1:]
    shape = jax.ShapeDtypeStruct(shape, grains.dtype)
    extra = [] if after is None else [after]
    return call(
        lambda *refs: pick_kernel(make_place, layout, n_chip, *refs),
        [shape, shape],
        [SMEM, VMEM] + [ANY] * len(extra),
        [VMEM, VMEM],
        "pick_blocks",
        8,
        moved=4 * MIB,
    )(chosen, grains, *extra)


def finish_kernel(make_place, layouts, n_chip, chosen, att_ref, *refs):
    pieces, out_ref, acc = refs[:-2], refs[-2], refs[-1]
    place = make_place()
    acc[...] = att_ref[...].astype(jnp.float32)
    for g, layout in enumerate(layouts):
        for r in range(n_chip):
            piece = pieces[g * n_chip + r]
            for k in range(place.n_expert):
                index, mine = layout.grain(place, chosen, r, place.behind(k))

                @pl.when(mine)
                def _():
                    acc[index] = acc[index] + piece[k].astype(jnp.float32)

    out_ref[...] = acc[...].astype(out_ref.dtype)


def finish(make_place, layouts, n_chip, chosen, grains, pieces):
    return call(
        lambda *refs: finish_kernel(make_place, layouts, n_chip, *refs),
        jax.ShapeDtypeStruct(grains.shape, grains.dtype),
        [SMEM] + [VMEM] * (1 + len(pieces)),
        VMEM,
        "add_expert_rows",
        12,
        moved=4 * MIB,
        scratch_shapes=[pltpu.VMEM(grains.shape, jnp.float32)],
    )(chosen, grains, *pieces)


def hidden_kernel(make_place, n, *refs):
    own, other, wg, wu, hid, xs = refs[:n], refs[n : 2 * n], *refs[2 * n : 2 * n + 2], *refs[-2:]
    n_z, rows, width = own[0].shape
    place = make_place()
    for s, pieces in enumerate((own, other)):
        for z in range(n_z):
            at = (place.behind(z) * 2 + (place.side ^ s)) * width
            at = pl.ds(pl.multiple_of(at, width), width)
            for r in range(n):
                xs[r * rows : (r + 1) * rows, at] = pieces[r][z]
    ff = wg.shape[1]
    tile = min(ff, 256)

    def one(i, carry):
        at = pl.ds(pl.multiple_of(i * tile, tile), tile)
        g = jnp.dot(xs[...], wg[:, at], preferred_element_type=jnp.float32)
        u = jnp.dot(xs[...], wu[:, at], preferred_element_type=jnp.float32)
        hid[:, at] = (g / (1.0 + jnp.exp(-g)) * u).astype(jnp.bfloat16)
        return carry

    lax.fori_loop(0, ff // tile, one, 0)


def hidden_units(make_place, own, other, w_gate, w_up, after):
    n = len(own)
    n_z, rows, width = own[0].shape
    model_width, ff = w_gate.shape
    extra = [] if after is None else [after]
    return call(
        lambda *refs: hidden_kernel(make_place, n, *refs),
        jax.ShapeDtypeStruct((n * rows, ff), jnp.bfloat16),
        [VMEM] * (2 * n + 2) + [ANY] * len(extra),
        VMEM,
        "expert_hidden",
        14,
        flops=4 * n * rows * ff * model_width,
        moved=2 * n * rows * model_width,
        scratch_shapes=[pltpu.VMEM((n * rows, model_width), jnp.bfloat16)],
    )(*own, *other, w_gate, w_up, *extra)


def down_kernel(make_place, layout, order, s, counts, hid, wd, values, *refs):
    out = refs[-1]
    n, n_z, rows, width = out.shape
    place = make_place()
    count = counts[place.expert]
    scale = []
    for r in range(n):
        row = layout.first_row(place, r)
        value = values[pl.ds(pl.multiple_of(row, rows), rows), :]
        scale.append(jnp.where(lax.div(row, BLK) < count, value, jnp.zeros_like(value)))
    for z in range(n_z):
        at = (place.ahead(z) * 2 + (place.side ^ s)) * width
        at = pl.ds(pl.multiple_of(at, width), width)
        part = jnp.dot(hid[...], wd[:, at], preferred_element_type=jnp.float32)
        for r in range(n):
            out[order[r], z] = (part[r * rows : (r + 1) * rows] * scale[r]).astype(out.dtype)


def down(make_place, layout, order, s, n_z, width, counts, hid, w_down, values, after):
    n = len(order)
    extra = [] if after is None else [after]
    return call(
        lambda *refs: down_kernel(make_place, layout, order, s, *refs),
        jax.ShapeDtypeStruct((n, n_z, layout.share, width), jnp.bfloat16),
        [SMEM] + [VMEM] * 3 + [ANY] * len(extra),
        VMEM,
        "expert_down",
        10,
        flops=2 * hid.size * n_z * width,
        moved=2 * n * layout.share * n_z * width,
    )(counts, hid, w_down, values, *extra)


def body(
    context,
    out_weight,
    residual,
    gate_weight,
    up_weight,
    down_weight,
    gate_values,
    chosen_blocks,
    block_counts,
):
    n_expert = lax.axis_size("expert")
    n_dp = lax.axis_size("dp")
    n_bits = n_dp.bit_length() - 2
    n_chip = 1 << n_bits
    local_tokens, model_width = context.shape
    local_width = residual.shape[1]
    half = local_width // 2
    depth = out_weight.shape[0]
    local_blocks = local_tokens // BLK
    place = Place(n_bits, n_expert)
    side = place.side
    reverse = bit_reversed(n_bits)
    pair = pair_pairs(n_dp)

    def to_partner(value):
        return lax.ppermute(value, "dp", pair)

    def split_sides(value):
        own = lax.dynamic_slice_in_dim(value, side * half, half, axis=1)
        other = lax.dynamic_slice_in_dim(value, (1 - side) * half, half, axis=1)
        return own, to_partner(other)

    w_own, w_other = split_sides(out_weight)
    pieces = [(w_own, w_other)]
    for step in range(n_bits):
        pieces = pieces + [tuple(exchange(w, n_dp, step) for w in p) for p in pieces]
    pieces = [w for p in pieces for w in p]
    context_other = to_partner(context)
    residual_own, residual_other = split_sides(residual)
    w_gate = load(gate_weight[0], w_other, "load_gate")
    w_up = load(up_weight[0], w_other, "load_up")
    w_down = load(down_weight[0], w_other, "load_down")
    plain = list(range(n_chip))
    top = n_chip // 2

    def make_place():
        return Place(n_bits, n_expert)

    first = project(
        make_place, plain[:top], context, context_other, pieces[:n_chip], (), (w_gate, w_up, w_down)
    )
    attended = project(
        make_place,
        plain[top:],
        context,
        context_other,
        pieces[n_chip:],
        (first, residual_own, residual_other),
        (),
    )

    layouts = [Layout(group, n_chip, local_blocks) for group in range(GROUPS)]
    share = layouts[0].share
    grains = attended.reshape(-1, share, half)
    values = gate_values.reshape(-1, 1)

    received = []
    after_pick, after_add, after_stack, after_hidden, after_down = None, None, None, None, None
    for layout in layouts:
        keep, send = pick(make_place, layout, n_chip, n_expert, chosen_blocks, grains, after_pick)
        mine, sums = scatter_sum(keep, send, n_dp, n_bits, [after_add])
        after_pick = mine
        crossed = swap_planes(mine, n_expert, after_stack)
        after_add = crossed
        own_half = gather_all(crossed, n_dp, n_bits)
        got = [to_partner(p) for p in own_half]
        other_half = [got[r] for r in reverse]
        hid = hidden_units(make_place, own_half, other_half, w_gate, w_up, after_hidden)
        after_stack = hid

        def downs(order, s, after):
            return down(
                make_place, layout, order, s, n_expert, half, block_counts, hid, w_down, values, after
            )

        got = to_partner(downs(reverse, 1, after_down))
        mine = downs(plain, 0, after_down)
        keep, send = add_split(mine, got, None, True)
        after_hidden = keep
        mine, sums = scatter_sum(keep, send, n_dp, n_bits)
        after_down = sums[0]
        crossed = swap_planes(mine, n_expert)
        received += gather_all(crossed, n_dp, n_bits)

    mixed = finish(make_place, layouts, n_chip, chosen_blocks, grains, received).reshape(2, local_tokens, half)
    got = to_partner(mixed[1])
    return jnp.where(
        side == 0,
        jnp.concatenate([mixed[0], got], axis=1),
        jnp.concatenate([got, mixed[0]], axis=1),
    )


def solution(mesh):
    in_specs = (
        P("dp", None),
        P("dp", "expert"),
        P("dp", "expert"),
        P("expert", None, "dp"),
        P("expert", None, "dp"),
        P("expert", "dp", None),
        P("expert", None),
        P(),
        P(),
    )
    out_specs = P("dp", "expert")
    return jax.shard_map(body, mesh=mesh, in_specs=in_specs, out_specs=out_specs, check_vma=False)
```

time: 214 us -> 202 us (0.944)
  waiting for transfers between devices: 91.3 us -> 84.1 us
  other arithmetic: 6.48 us -> 1.26 us
  starting transfers between devices: 51.6 us -> 56.6 us
  Pallas kernels: 38.1 us -> 34.5 us
    ppermute x26, waiting for transfers between devices: 77.8 us -> 67.2 us  [exchange(): return lax.ppermute(value, 'dp', step_pairs(n_dp, step))]
    unnamed x27 -> x34, local copies, waits for them, and re-layouts: 15.7 us -> 22.2 us
    gather x8 -> x0, local copies, waits for them, and re-layouts: 5.82 us -> none  [the longest x4 2.76 us: grain_index(): block = chosen_blocks[experts[None, :], (row // BLK)[:, None]]]
    ppermute x26, starting transfers between devices: 30.4 us -> 35.8 us  [exchange(): return lax.ppermute(value, 'dp', step_pairs(n_dp, step))]
    ppermute x14, waiting for transfers between devices: 1.83 us -> 5.6 us  [to_partner(): return lax.ppermute(value, 'dp', pair)]
    pallas_call x12 -> x25, Pallas kernels: 36.4 us -> 32.8 us  [the longest x2 12.1 us: hidden_units(): call(lambda *refs: hidden_kernel(make_place, n, *refs), jax.ShapeDtypeStr...]
    convert_element_type x10 -> x0, other arithmetic: 3.29 us -> none  [f32_sum(): return (a.astype(jnp.float32) + b.astype(jnp.float32)).astype(jnp.bfloat16)]
  transfers between devices with their start and end apart: 52 -> 52, of which waited for: 25 -> 26; matrix products, arithmetic and copies ran while one was open for 6% -> 1% of each run, Pallas kernels for 12% -> 13%
where the time goes in v3:
time: 202 us
  waiting for transfers between devices  84.1 us (42%)
  starting transfers between devices  56.6 us (28%)
  Pallas kernels  34.5 us (17%)
  local copies, waits for them, and re-layouts  25.1 us (12%)
    ppermute x26, waiting for transfers between devices, exchange(): return lax.ppermute(value, 'dp', step_pairs(n_dp, step))  67.2 us
    ppermute x26, starting transfers between devices, exchange(): return lax.ppermute(value, 'dp', step_pairs(n_dp, step))  35.8 us
    unnamed x34, local copies, waits for them, and re-layouts  22.2 us
    ppermute x12, starting transfers between devices, swap_planes(): out.append(lax.ppermute(parts[k], 'expert', pairs))  17.6 us
    pallas_call x2, Pallas kernels, hidden_units(): call(lambda *refs: hidden_kernel(make_place, n, *refs), jax.ShapeDtypeStr...  12.1 us
    ppermute x12, waiting for transfers between devices, swap_planes(): out.append(lax.ppermute(parts[k], 'expert', pairs))  11.4 us
    pallas_call x2, Pallas kernels, project(): call(lambda *refs: project_kernel(make_place, parts, len(weights), len(ex...  8.34 us
    pallas_call x4, Pallas kernels, down(): call(lambda *refs: down_kernel(make_place, layout, order, s, *refs), jax....  7.28 us
  transfers between devices with their start and end apart: 52, of which 26 were waited for; matrix products, arithmetic and copies ran while one was open for 1% of the time, Pallas kernels for 13%

profile of v3, /device:TPU:0, one launch (start us, length us, event | category | flops | bytes accessed | tf_op | source)
XLA Modules:
  0.0 202.0 jit_solution(13131418171702476878)
XLA Ops:
  0.5 1.3 constant_dynamic-slice_fusion.2
  1.8 2.9 %collective-permute-start.4 = (bf16[512,512]{1,0:T(8,128)(2,1)S(1)}, bf16[512,512]{1,0:T(8,128)(2,1)S(1)}, u32[]{:S(2)}, u32[]{:S(2)}) collective-permute-start(bf16[512,512]{1,0:T(8,128)(2,1)S(1)} %get-tuple-element.42.refs_2_), channel_id=1, source_target_pairs={{0,8},{4,20},{8,0},{12,28},{16,24},{20,4},{24,16},{28,12},{1,9},{5... | collective-permute-start | bytes 1572872 | tf_op jit(solution)/shard_map/ppermute | solution.py:52
  4.8 3.2 %collective-permute-done.2.after.refs_3_ = bf16[512,512]{1,0:T(8,128)(2,1)S(1)} collective-permute-done((bf16[512,512]{1,0:T(8,128)(2,1)S(1)}, bf16[512,512]{1,0:T(8,128)(2,1)S(1)}, u32[]{:S(2)}, u32[]{:S(2)}) %collective-permute-start.2) | collective-permute-done | bytes 524320 | tf_op jit(solution)/shard_map/ppermute | solution.py:411
  8.0 2.9 %collective-permute-start.6 = (bf16[512,512]{1,0:T(8,128)(2,1)S(1)}, bf16[512,512]{1,0:T(8,128)(2,1)S(1)}, u32[]{:S(2)}, u32[]{:S(2)}) collective-permute-start(bf16[512,512]{1,0:T(8,128)(2,1)S(1)} %collective-permute-done.2.after.refs_3_), channel_id=1, source_target_pairs={{0,8},{4,20},{8,0},{12,28},{16,24},{20,4},{24,16},{28,12},{1,9},{5... | collective-permute-start | bytes 1572872 | tf_op jit(solution)/shard_map/ppermute | solution.py:52
  10.8 1.5 collective-permute-start.1
  12.4 1.3 constant_dynamic-slice_fusion
  14.3 8.5 %collective-permute-done.6.refs_5_ = bf16[512,512]{1,0:T(8,128)(2,1)S(1)} collective-permute-done((bf16[512,512]{1,0:T(8,128)(2,1)S(1)}, bf16[512,512]{1,0:T(8,128)(2,1)S(1)}, u32[]{:S(2)}, u32[]{:S(2)}) %collective-permute-start.6) | collective-permute-done | bytes 524320 | tf_op jit(solution)/shard_map/ppermute | solution.py:52
  22.8 2.8 %collective-permute-start.5 = (bf16[512,512]{1,0:T(8,128)(2,1)S(1)}, bf16[512,512]{1,0:T(8,128)(2,1)S(1)}, u32[]{:S(2)}, u32[]{:S(2)}) collective-permute-start(bf16[512,512]{1,0:T(8,128)(2,1)S(1)} %collective-permute-done.4.refs_4_), channel_id=1, source_target_pairs={{0,16},{4,12},{8,24},{12,4},{16,0},{20,28},{24,8},{28,20},{1,17},{... | collective-permute-start | bytes 1572872 | tf_op jit(solution)/shard_map/ppermute | solution.py:52
  25.7 3.4 %copy-done.6 = bf16[1,1024,4096]{2,1,0:T(8,128)(2,1)S(1)} copy-done((bf16[1,1024,4096]{2,1,0:T(8,128)(2,1)S(1)}, bf16[1,1024,4096]{2,1,0:T(8,128)(2,1)}, u32[]{:S(2)}) %copy-start.6) | copy-done | bytes 8388632
  29.7 5.8 %copy-done.7 = bf16[1,4096,1024]{2,1,0:T(8,128)(2,1)S(1)} copy-done((bf16[1,4096,1024]{2,1,0:T(8,128)(2,1)S(1)}, bf16[1,4096,1024]{2,1,0:T(8,128)(2,1)}, u32[]{:S(2)}) %copy-start.7) | copy-done | bytes 8388632
  36.7 3.4 %slice-done.5 = s8[4194304]{0:T(1024)(128)(4,1)S(1)} async-done(((s8[8388608]{0:T(1024)(128)(4,1)}), s8[4194304]{0:T(1024)(128)(4,1)S(1)}, s32[]{:S(2)}) %slice-start.5) | async-done | bytes 4194328
  40.7 1.6 copy-done.5
  42.3 5.0 %project_first.1.refs_6_ = f32[2,512,512]{2,1,0:T(8,128)S(1)} custom-call(bf16[512,4096]{1,0:T(8,128)(2,1)S(1)} %copy-done.5, bf16[512,4096]{1,0:T(8,128)(2,1)} %collective-permute-done.refs_1_, bf16[512,512]{1,0:T(8,128)(2,1)S(1)} %get-tuple-element.42.refs_2_, bf16[512,512]{1,0:T(8,128)(2,1)S(1)} %collective-permute-done.2.after.refs_3_, ...), custom_call_target="tpu_custom_call" | custom-call | flops 2147483648 | bytes 6291456 | tf_op jit(solution)/shard_map/project_first/pallas_call | solution.py:233
  47.3 3.4 %project_last.1 = bf16[2,512,512]{2,1,0:T(8,128)(2,1)S(1)} custom-call(bf16[512,4096]{1,0:T(8,128)(2,1)S(1)} %copy-done.5, bf16[512,4096]{1,0:T(8,128)(2,1)} %collective-permute-done.refs_1_, bf16[512,512]{1,0:T(8,128)(2,1)S(1)} %collective-permute-done.1.refs_2_, bf16[512,512]{1,0:T(8,128)(2,1)S(1)} %collective-permute-done.3.refs_3_, ...), custom_call_target="tpu_custom_call" | custom-call | flops 2147483648 | bytes 6291456 | tf_op jit(solution)/shard_map/project_last/pallas_call | solution.py:233
  51.6 2.1 %collective-permute-start.9 = (bf16[2,4,64,512]{3,2,1,0:T(8,128)(2,1)S(1)}, bf16[2,4,64,512]{3,2,1,0:T(8,128)(2,1)S(1)}, u32[]{:S(2)}, u32[]{:S(2)}) collective-permute-start(bf16[2,4,64,512]{3,2,1,0:T(8,128)(2,1)S(1)} %get-tuple-element.22), channel_id=1, source_target_pairs={{0,16},{4,12},{8,24},{12,4},{16,0},{20,28},{24,8},{28,20},{1,17},{... | collective-permute-start | bytes 1572872 | tf_op jit(solution)/shard_map/ppermute | solution.py:52
  53.6 8.1 %collective-permute-done.9.refs_1_ = bf16[2,4,64,512]{3,2,1,0:T(8,128)(2,1)S(1)} collective-permute-done((bf16[2,4,64,512]{3,2,1,0:T(8,128)(2,1)S(1)}, bf16[2,4,64,512]{3,2,1,0:T(8,128)(2,1)S(1)}, u32[]{:S(2)}, u32[]{:S(2)}) %collective-permute-start.9) | collective-permute-done | bytes 524320 | tf_op jit(solution)/shard_map/ppermute | solution.py:52
  62.2 6.0 %collective-permute-done.10.refs_1_ = bf16[1,4,64,512]{3,2,1,0:T(8,128)(2,1)S(1)} collective-permute-done((bf16[1,4,64,512]{3,2,1,0:T(8,128)(2,1)S(1)}, bf16[1,4,64,512]{3,2,1,0:T(8,128)(2,1)S(1)}, u32[]{:S(2)}, u32[]{:S(2)}) %collective-permute-start.10) | collective-permute-done | bytes 262176 | tf_op jit(solution)/shard_map/ppermute | solution.py:52
  68.3 2.0 collective-permute-start.11
  70.3 2.6 %collective-permute-start.12 = (bf16[64,512]{1,0:T(8,128)(2,1)S(1)}, bf16[64,512]{1,0:T(8,128)(2,1)S(1)}, u32[]{:S(2)}, u32[]{:S(2)}) collective-permute-start(bf16[64,512]{1,0:T(8,128)(2,1)S(1)} %get-tuple-element.56), channel_id=1, source_target_pairs={{0,2},{1,3},{2,0},{3,1},{4,6},{5,7},{6,4},{7,5},{8,10},{9,11},{10,... | collective-permute-start | bytes 196616 | tf_op jit(solution)/shard_map/ppermute | solution.py:75
  72.9 1.3 collective-permute-start.13
  75.5 1.7 collective-permute-done.13.refs_3_
  77.6 1.6 pick_blocks.3
  79.2 2.1 %collective-permute-start.30 = (bf16[2,4,64,512]{3,2,1,0:T(8,128)(2,1)}, bf16[2,4,64,512]{3,2,1,0:T(8,128)(2,1)S(1)}, u32[]{:S(2)}, u32[]{:S(2)}) collective-permute-start(bf16[2,4,64,512]{3,2,1,0:T(8,128)(2,1)} %get-tuple-element.30), channel_id=1, source_target_pairs={{0,16},{4,12},{8,24},{12,4},{16,0},{20,28},{24,8},{28,20},{1,17},{... | collective-permute-start | bytes 1572872 | tf_op jit(solution)/shard_map/ppermute | solution.py:52
  81.3 5.2 %collective-permute-done.14.refs_1_ = bf16[4,64,512]{2,1,0:T(8,128)(2,1)S(1)} collective-permute-done((bf16[4,64,512]{2,1,0:T(8,128)(2,1)S(1)}, bf16[4,64,512]{2,1,0:T(8,128)(2,1)S(1)}, u32[]{:S(2)}, u32[]{:S(2)}) %collective-permute-start.14) | collective-permute-done | bytes 262176 | tf_op jit(solution)/shard_map/ppermute | solution.py:52
  86.5 2.1 %collective-permute-start.16 = (bf16[4,64,512]{2,1,0:T(8,128)(2,1)S(1)}, bf16[4,64,512]{2,1,0:T(8,128)(2,1)S(1)}, u32[]{:S(2)}, u32[]{:S(2)}) collective-permute-start(bf16[4,64,512]{2,1,0:T(8,128)(2,1)S(1)} %collective-permute-done.14.refs_1_), channel_id=1, source_target_pairs={{0,16},{4,12},{8,24},{12,4},{16,0},{20,28},{24,8},{28,20},{1,17},{... | collective-permute-start | bytes 786440 | tf_op jit(solution)/shard_map/ppermute | solution.py:52
  89.1 2.3 %collective-permute-done.15.refs_2_ = bf16[4,64,512]{2,1,0:T(8,128)(2,1)S(1)} collective-permute-done((bf16[4,64,512]{2,1,0:T(8,128)(2,1)S(1)}, bf16[4,64,512]{2,1,0:T(8,128)(2,1)S(1)}, u32[]{:S(2)}, u32[]{:S(2)}) %collective-permute-start.15) | collective-permute-done | bytes 262176 | tf_op jit(solution)/shard_map/ppermute | solution.py:52
  91.5 2.8 %collective-permute-done.16.refs_3_ = bf16[4,64,512]{2,1,0:T(8,128)(2,1)S(1)} collective-permute-done((bf16[4,64,512]{2,1,0:T(8,128)(2,1)S(1)}, bf16[4,64,512]{2,1,0:T(8,128)(2,1)S(1)}, u32[]{:S(2)}, u32[]{:S(2)}) %collective-permute-start.16) | collective-permute-done | bytes 262176 | tf_op jit(solution)/shard_map/ppermute | solution.py:52
  94.6 1.7 collective-permute-start.31
  96.4 3.9 %copy-done.2 = bf16[4096,1024]{1,0:T(8,128)(2,1)S(1)} copy-done((bf16[4096,1024]{1,0:T(8,128)(2,1)S(1)}, bf16[4096,1024]{1,0:T(8,128)(2,1)}, u32[]{:S(2)}) %copy-start.2) | copy-done | bytes 8388632
  100.3 3.4 %copy-done.4 = bf16[4096,1024]{1,0:T(8,128)(2,1)S(1)} copy-done((bf16[4096,1024]{1,0:T(8,128)(2,1)S(1)}, bf16[4096,1024]{1,0:T(8,128)(2,1)}, u32[]{:S(2)}) %copy-start.4) | copy-done | bytes 8388632
  103.7 6.6 %expert_hidden.2.refs_1_.refs_4_ = bf16[256,1024]{1,0:T(8,128)(2,1)S(1)} custom-call(bf16[4,64,512]{2,1,0:T(8,128)(2,1)S(1)} %stack_planes.4.refs_0_.refs_2_, bf16[4,64,512]{2,1,0:T(8,128)(2,1)S(1)} %collective-permute-done.14.refs_1_, bf16[4,64,512]{2,1,0:T(8,128)(2,1)S(1)} %collective-permute-done.15.refs_2_, ...), custom_call_target="tpu_custom_call" | custom-call | flops 4294967296 | bytes 2097152 | tf_op jit(solution)/shard_map/expert_hidden/pallas_call | solution.py:339
  110.4 1.8 expert_down.5
  113.5 3.1 %collective-permute-start.33 = (bf16[64,512]{1,0:T(8,128)(2,1)S(1)}, bf16[64,512]{1,0:T(8,128)(2,1)S(1)}, u32[]{:S(2)}, u32[]{:S(2)}) collective-permute-start(bf16[64,512]{1,0:T(8,128)(2,1)S(1)} %get-tuple-element.48), channel_id=1, source_target_pairs={{0,2},{1,3},{2,0},{3,1},{4,6},{5,7},{6,4},{7,5},{8,10},{9,11},{10,... | collective-permute-start | bytes 196616 | tf_op jit(solution)/shard_map/ppermute | solution.py:75
  116.8 3.1 %collective-permute-done.32.refs_1_ = bf16[64,512]{1,0:T(8,128)(2,1)S(1)} collective-permute-done((bf16[64,512]{1,0:T(8,128)(2,1)S(1)}, bf16[64,512]{1,0:T(8,128)(2,1)S(1)}, u32[]{:S(2)}, u32[]{:S(2)}) %collective-permute-start.32) | collective-permute-done | bytes 65568 | tf_op jit(solution)/shard_map/ppermute | solution.py:75
  119.8 1.8 collective-permute-done.33.refs_2_
  121.9 1.7 collective-permute-start.35
  123.6 1.6 collective-permute-start.36
  125.2 5.7 %collective-permute-done.35.refs_1_ = bf16[4,64,512]{2,1,0:T(8,128)(2,1)S(1)} collective-permute-done((bf16[4,64,512]{2,1,0:T(8,128)(2,1)S(1)}, bf16[4,64,512]{2,1,0:T(8,128)(2,1)S(1)}, u32[]{:S(2)}, u32[]{:S(2)}) %collective-permute-start.35) | collective-permute-done | bytes 262176 | tf_op jit(solution)/shard_map/ppermute | solution.py:52
  132.3 4.9 %collective-permute-done.37.refs_3_ = bf16[4,64,512]{2,1,0:T(8,128)(2,1)S(1)} collective-permute-done((bf16[4,64,512]{2,1,0:T(8,128)(2,1)S(1)}, bf16[4,64,512]{2,1,0:T(8,128)(2,1)S(1)}, u32[]{:S(2)}, u32[]{:S(2)}) %collective-permute-start.37) | collective-permute-done | bytes 262176 | tf_op jit(solution)/shard_map/ppermute | solution.py:52
  137.2 1.8 expert_down.4.refs_0_
  140.4 5.5 %expert_hidden.3.refs_1_ = bf16[256,1024]{1,0:T(8,128)(2,1)S(1)} custom-call(bf16[4,64,512]{2,1,0:T(8,128)(2,1)S(1)} %stack_planes.6.refs_0_, bf16[4,64,512]{2,1,0:T(8,128)(2,1)S(1)} %collective-permute-done.35.refs_1_, bf16[4,64,512]{2,1,0:T(8,128)(2,1)S(1)} %collective-permute-done.36.refs_2_, bf16[4,64,512]{2,1,0:T(8,128)(2,1)S(1)} %collective-permute-done.37.refs_3_, ...), custom_call_target="tpu_custom_call" | custom-call | flops 4294967296 | bytes 2097152 | tf_op jit(solution)/shard_map/expert_hidden/pallas_call | solution.py:339
  145.8 2.7 %collective-permute-done.22.refs_1_ = bf16[2,4,64,512]{3,2,1,0:T(8,128)(2,1)S(1)} collective-permute-done((bf16[2,4,64,512]{3,2,1,0:T(8,128)(2,1)S(1)}, bf16[2,4,64,512]{3,2,1,0:T(8,128)(2,1)S(1)}, u32[]{:S(2)}, u32[]{:S(2)}) %collective-permute-start.22) | collective-permute-done | bytes 524320 | tf_op jit(solution)/shard_map/ppermute | solution.py:52
  148.7 1.8 expert_down.7
  150.6 1.8 expert_down.6.refs_0_
  154.5 1.4 collective-permute-start.23
  155.9 9.7 %collective-permute-done.43.refs_1_ = bf16[2,4,64,512]{3,2,1,0:T(8,128)(2,1)S(1)} collective-permute-done((bf16[2,4,64,512]{3,2,1,0:T(8,128)(2,1)S(1)}, bf16[2,4,64,512]{3,2,1,0:T(8,128)(2,1)S(1)}, u32[]{:S(2)}, u32[]{:S(2)}) %collective-permute-start.43) | collective-permute-done | bytes 524320 | tf_op jit(solution)/shard_map/ppermute | solution.py:52
  165.7 1.3 collective-permute-start.44
  167.0 1.3 collective-permute-start.24
  168.4 1.7 collective-permute-start.25
  170.9 1.2 collective-permute-done.44.refs_1_
  172.2 1.3 collective-permute-start.45
  173.5 2.0 %collective-permute-start.46 = (bf16[64,512]{1,0:T(8,128)(2,1)S(1)}, bf16[64,512]{1,0:T(8,128)(2,1)S(1)}, u32[]{:S(2)}, u32[]{:S(2)}) collective-permute-start(bf16[64,512]{1,0:T(8,128)(2,1)S(1)} %get-tuple-element.44), channel_id=1, source_target_pairs={{0,2},{1,3},{2,0},{3,1},{4,6},{5,7},{6,4},{7,5},{8,10},{9,11},{10,... | collective-permute-start | bytes 196616 | tf_op jit(solution)/shard_map/ppermute | solution.py:75
  176.1 1.3 collective-permute-start.27
  178.4 2.2 %collective-permute-done.46.refs_2_ = bf16[64,512]{1,0:T(8,128)(2,1)S(1)} collective-permute-done((bf16[64,512]{1,0:T(8,128)(2,1)S(1)}, bf16[64,512]{1,0:T(8,128)(2,1)S(1)}, u32[]{:S(2)}, u32[]{:S(2)}) %collective-permute-start.46) | collective-permute-done | bytes 65568 | tf_op jit(solution)/shard_map/ppermute | solution.py:75
  180.7 1.3 collective-permute-start.48
  182.0 1.3 collective-permute-start.28
  183.3 1.3 collective-permute-start.29
  185.3 4.6 %collective-permute-done.48.refs_7_ = bf16[4,64,512]{2,1,0:T(8,128)(2,1)S(1)} collective-permute-done((bf16[4,64,512]{2,1,0:T(8,128)(2,1)S(1)}, bf16[4,64,512]{2,1,0:T(8,128)(2,1)S(1)}, u32[]{:S(2)}, u32[]{:S(2)}) %collective-permute-start.48) | collective-permute-done | bytes 262176 | tf_op jit(solution)/shard_map/ppermute | solution.py:52
  189.9 1.5 collective-permute-start.50
  191.4 2.6 %collective-permute-done.49.refs_8_ = bf16[4,64,512]{2,1,0:T(8,128)(2,1)S(1)} collective-permute-done((bf16[4,64,512]{2,1,0:T(8,128)(2,1)S(1)}, bf16[4,64,512]{2,1,0:T(8,128)(2,1)S(1)}, u32[]{:S(2)}, u32[]{:S(2)}) %collective-permute-start.49) | collective-permute-done | bytes 262176 | tf_op jit(solution)/shard_map/ppermute | solution.py:52
  194.0 2.8 %collective-permute-done.50.refs_9_ = bf16[4,64,512]{2,1,0:T(8,128)(2,1)S(1)} collective-permute-done((bf16[4,64,512]{2,1,0:T(8,128)(2,1)S(1)}, bf16[4,64,512]{2,1,0:T(8,128)(2,1)S(1)}, u32[]{:S(2)}, u32[]{:S(2)}) %collective-permute-start.50) | collective-permute-done | bytes 262176 | tf_op jit(solution)/shard_map/ppermute | solution.py:52
  196.8 1.4 add_expert_rows.1
  199.2 1.5 collective-permute-done.51
  200.8 1.3 maximum_select_fusion
  (114 shorter events, 18.8 us)
Async XLA Ops:
  0.0 25.7 %collective-permute-start = (bf16[512,4096]{1,0:T(8,128)(2,1)}, bf16[512,4096]{1,0:T(8,128)(2,1)}, u32[]{:S(2)}, u32[]{:S(2)}) collective-permute-start(bf16[512,4096]{1,0:T(8,128)(2,1)} %refs_0_.10), channel_id=1, source_target_pairs={{0,4},{4,0},{8,12},{12,8},{16,20},{20,16},{24,28},{28,24},{1,5},{5... | collective-permute-start | bytes 12582920 | tf_op jit(solution)/shard_map/ppermute | solution.py:411
  1.7 6.3 %collective-permute-start.2 = (bf16[512,512]{1,0:T(8,128)(2,1)S(1)}, bf16[512,512]{1,0:T(8,128)(2,1)S(1)}, u32[]{:S(2)}, u32[]{:S(2)}) collective-permute-start(bf16[512,512]{1,0:T(8,128)(2,1)S(1)} %get-tuple-element.41), channel_id=1, source_target_pairs={{0,4},{4,0},{8,12},{12,8},{16,20},{20,16},{24,28},{28,24},{1,5},{5... | collective-permute-start | bytes 1572872 | tf_op jit(solution)/shard_map/ppermute | solution.py:411
  1.8 11.9 %collective-permute-start.4 = (bf16[512,512]{1,0:T(8,128)(2,1)S(1)}, bf16[512,512]{1,0:T(8,128)(2,1)S(1)}, u32[]{:S(2)}, u32[]{:S(2)}) collective-permute-start(bf16[512,512]{1,0:T(8,128)(2,1)S(1)} %get-tuple-element.42.refs_2_), channel_id=1, source_target_pairs={{0,8},{4,20},{8,0},{12,28},{16,24},{20,4},{24,16},{28,12},{1,9},{5... | collective-permute-start | bytes 1572872 | tf_op jit(solution)/shard_map/ppermute | solution.py:52
  8.0 14.9 %collective-permute-start.6 = (bf16[512,512]{1,0:T(8,128)(2,1)S(1)}, bf16[512,512]{1,0:T(8,128)(2,1)S(1)}, u32[]{:S(2)}, u32[]{:S(2)}) collective-permute-start(bf16[512,512]{1,0:T(8,128)(2,1)S(1)} %collective-permute-done.2.after.refs_3_), channel_id=1, source_target_pairs={{0,8},{4,20},{8,0},{12,28},{16,24},{20,4},{24,16},{28,12},{1,9},{5... | collective-permute-start | bytes 1572872 | tf_op jit(solution)/shard_map/ppermute | solution.py:52
  10.8 36.4 %collective-permute-start.1 = (bf16[512,512]{1,0:T(8,128)(2,1)S(1)}, bf16[512,512]{1,0:T(8,128)(2,1)S(1)}, u32[]{:S(2)}, u32[]{:S(2)}) collective-permute-start(bf16[512,512]{1,0:T(8,128)(2,1)S(1)} %get-tuple-element.42.refs_2_), channel_id=1, source_target_pairs={{0,16},{4,12},{8,24},{12,4},{16,0},{20,28},{24,8},{28,20},{1,17},{... | collective-permute-start | bytes 1572872 | tf_op jit(solution)/shard_map/ppermute | solution.py:52
  13.7 33.6 %collective-permute-start.8 = (bf16[512,512]{1,0:T(8,128)(2,1)S(1)}, bf16[512,512]{1,0:T(8,128)(2,1)S(1)}, u32[]{:S(2)}, u32[]{:S(2)}) collective-permute-start(bf16[512,512]{1,0:T(8,128)(2,1)S(1)} %get-tuple-element.39), channel_id=1, source_target_pairs={{0,4},{4,0},{8,12},{12,8},{16,20},{20,16},{24,28},{28,24},{1,5},{5... | collective-permute-start | bytes 1572872 | tf_op jit(solution)/shard_map/ppermute | solution.py:411
  13.7 33.6 %collective-permute-start.3 = (bf16[512,512]{1,0:T(8,128)(2,1)S(1)}, bf16[512,512]{1,0:T(8,128)(2,1)S(1)}, u32[]{:S(2)}, u32[]{:S(2)}) collective-permute-start(bf16[512,512]{1,0:T(8,128)(2,1)S(1)} %collective-permute-done.2.after.refs_3_), channel_id=1, source_target_pairs={{0,16},{4,12},{8,24},{12,4},{16,0},{20,28},{24,8},{28,20},{1,17},{... | collective-permute-start | bytes 1572872 | tf_op jit(solution)/shard_map/ppermute | solution.py:52
  22.8 24.5 %collective-permute-start.5 = (bf16[512,512]{1,0:T(8,128)(2,1)S(1)}, bf16[512,512]{1,0:T(8,128)(2,1)S(1)}, u32[]{:S(2)}, u32[]{:S(2)}) collective-permute-start(bf16[512,512]{1,0:T(8,128)(2,1)S(1)} %collective-permute-done.4.refs_4_), channel_id=1, source_target_pairs={{0,16},{4,12},{8,24},{12,4},{16,0},{20,28},{24,8},{28,20},{1,17},{... | collective-permute-start | bytes 1572872 | tf_op jit(solution)/shard_map/ppermute | solution.py:52
  25.7 21.7 %collective-permute-start.7 = (bf16[512,512]{1,0:T(8,128)(2,1)S(1)}, bf16[512,512]{1,0:T(8,128)(2,1)S(1)}, u32[]{:S(2)}, u32[]{:S(2)}) collective-permute-start(bf16[512,512]{1,0:T(8,128)(2,1)S(1)} %collective-permute-done.6.refs_5_), channel_id=1, source_target_pairs={{0,16},{4,12},{8,24},{12,4},{16,0},{20,28},{24,8},{28,20},{1,17},{... | collective-permute-start | bytes 1572872 | tf_op jit(solution)/shard_map/ppermute | solution.py:52
  29.1 6.4 %copy-start.7 = (bf16[1,4096,1024]{2,1,0:T(8,128)(2,1)S(1)}, bf16[1,4096,1024]{2,1,0:T(8,128)(2,1)}, u32[]{:S(2)}) copy-start(bf16[1,4096,1024]{2,1,0:T(8,128)(2,1)} %param.12) | copy-start | bytes 25165828
  29.1 7.6 %slice-start.4 = ((s8[8388608]{0:T(1024)(128)(4,1)}), s8[4194304]{0:T(1024)(128)(4,1)S(1)}, s32[]{:S(2)}) async-start(s8[8388608]{0:T(1024)(128)(4,1)} %bitcast.49), calls=%async_computation.4 | async-start | bytes 8388608
  29.6 11.0 %copy-start = (bf16[1024,4096]{1,0:T(8,128)(2,1)}, bf16[1024,4096]{1,0:T(8,128)(2,1)S(1)}, u32[]{:S(2)}) copy-start(bf16[1024,4096]{1,0:T(8,128)(2,1)S(1)} %load_down.1.refs_8_.refs_2_) | copy-start | bytes 25165828
  35.5 4.6 %slice-start.5 = ((s8[8388608]{0:T(1024)(128)(4,1)}), s8[4194304]{0:T(1024)(128)(4,1)S(1)}, s32[]{:S(2)}) async-start(s8[8388608]{0:T(1024)(128)(4,1)} %bitcast.49), calls=%async_computation.5 | async-start | bytes 8388608
  36.1 4.6 %copy-start.1 = (bf16[4096,1024]{1,0:T(8,128)(2,1)}, bf16[4096,1024]{1,0:T(8,128)(2,1)S(1)}, u32[]{:S(2)}) copy-start(bf16[4096,1024]{1,0:T(8,128)(2,1)S(1)} %load_gate.1.refs_6_.refs_8_) | copy-start | bytes 25165828
  42.3 5.0 %copy-start.3 = (bf16[4096,1024]{1,0:T(8,128)(2,1)}, bf16[4096,1024]{1,0:T(8,128)(2,1)S(1)}, u32[]{:S(2)}) copy-start(bf16[4096,1024]{1,0:T(8,128)(2,1)S(1)} %load_up.1.refs_7_.refs_9_) | copy-start | bytes 25165828
  50.7 43.6 %copy-start.10 = (f32[1,512]{1,0:T(1,128)S(1)}, f32[1,512]{1,0:T(1,128)}, u32[]{:S(2)}) copy-start(f32[1,512]{1,0:T(1,128)} %param.15) | copy-start | bytes 6148
  51.6 10.1 %collective-permute-start.9 = (bf16[2,4,64,512]{3,2,1,0:T(8,128)(2,1)S(1)}, bf16[2,4,64,512]{3,2,1,0:T(8,128)(2,1)S(1)}, u32[]{:S(2)}, u32[]{:S(2)}) collective-permute-start(bf16[2,4,64,512]{3,2,1,0:T(8,128)(2,1)S(1)} %get-tuple-element.22), channel_id=1, source_target_pairs={{0,16},{4,12},{8,24},{12,4},{16,0},{20,28},{24,8},{28,20},{1,17},{... | collective-permute-start | bytes 1572872 | tf_op jit(solution)/shard_map/ppermute | solution.py:52
  61.8 6.4 %collective-permute-start.10 = (bf16[1,4,64,512]{3,2,1,0:T(8,128)(2,1)S(1)}, bf16[1,4,64,512]{3,2,1,0:T(8,128)(2,1)S(1)}, u32[]{:S(2)}, u32[]{:S(2)}) collective-permute-start(bf16[1,4,64,512]{3,2,1,0:T(8,128)(2,1)S(1)} %get-tuple-element.24), channel_id=1, source_target_pairs={{0,8},{4,20},{8,0},{12,28},{16,24},{20,4},{24,16},{28,12},{1,9},{5... | collective-permute-start | bytes 786440 | tf_op jit(solution)/shard_map/ppermute | solution.py:52
  68.3 6.3 %collective-permute-start.11 = (bf16[64,512]{1,0:T(8,128)(2,1)S(1)}, bf16[64,512]{1,0:T(8,128)(2,1)S(1)}, u32[]{:S(2)}, u32[]{:S(2)}) collective-permute-start(bf16[64,512]{1,0:T(8,128)(2,1)S(1)} %get-tuple-element.57), channel_id=1, source_target_pairs={{0,1},{1,2},{2,3},{3,0},{4,5},{5,6},{6,7},{7,4},{8,9},{9,10},{10,1... | collective-permute-start | bytes 196616 | tf_op jit(solution)/shard_map/ppermute | solution.py:75
  70.3 5.2 %collective-permute-start.12 = (bf16[64,512]{1,0:T(8,128)(2,1)S(1)}, bf16[64,512]{1,0:T(8,128)(2,1)S(1)}, u32[]{:S(2)}, u32[]{:S(2)}) collective-permute-start(bf16[64,512]{1,0:T(8,128)(2,1)S(1)} %get-tuple-element.56), channel_id=1, source_target_pairs={{0,2},{1,3},{2,0},{3,1},{4,6},{5,7},{6,4},{7,5},{8,10},{9,11},{10,... | collective-permute-start | bytes 196616 | tf_op jit(solution)/shard_map/ppermute | solution.py:75
  72.9 4.3 %collective-permute-start.13 = (bf16[64,512]{1,0:T(8,128)(2,1)S(1)}, bf16[64,512]{1,0:T(8,128)(2,1)S(1)}, u32[]{:S(2)}, u32[]{:S(2)}) collective-permute-start(bf16[64,512]{1,0:T(8,128)(2,1)S(1)} %get-tuple-element.55), channel_id=1, source_target_pairs={{0,3},{1,0},{2,1},{3,2},{4,7},{5,4},{6,5},{7,6},{8,11},{9,8},{10,9... | collective-permute-start | bytes 196616 | tf_op jit(solution)/shard_map/ppermute | solution.py:75
  77.2 9.3 %collective-permute-start.14 = (bf16[4,64,512]{2,1,0:T(8,128)(2,1)S(1)}, bf16[4,64,512]{2,1,0:T(8,128)(2,1)S(1)}, u32[]{:S(2)}, u32[]{:S(2)}) collective-permute-start(bf16[4,64,512]{2,1,0:T(8,128)(2,1)S(1)} %stack_planes.4.refs_0_.refs_2_), channel_id=1, source_target_pairs={{0,8},{4,20},{8,0},{12,28},{16,24},{20,4},{24,16},{28,12},{1,9},{5... | collective-permute-start | bytes 786440 | tf_op jit(solution)/shard_map/ppermute | solution.py:52
  79.2 15.2 %collective-permute-start.30 = (bf16[2,4,64,512]{3,2,1,0:T(8,128)(2,1)}, bf16[2,4,64,512]{3,2,1,0:T(8,128)(2,1)S(1)}, u32[]{:S(2)}, u32[]{:S(2)}) collective-permute-start(bf16[2,4,64,512]{3,2,1,0:T(8,128)(2,1)} %get-tuple-element.30), channel_id=1, source_target_pairs={{0,16},{4,12},{8,24},{12,4},{16,0},{20,28},{24,8},{28,20},{1,17},{... | collective-permute-start | bytes 1572872 | tf_op jit(solution)/shard_map/ppermute | solution.py:52
  81.3 10.2 %collective-permute-start.15 = (bf16[4,64,512]{2,1,0:T(8,128)(2,1)S(1)}, bf16[4,64,512]{2,1,0:T(8,128)(2,1)S(1)}, u32[]{:S(2)}, u32[]{:S(2)}) collective-permute-start(bf16[4,64,512]{2,1,0:T(8,128)(2,1)S(1)} %stack_planes.4.refs_0_.refs_2_), channel_id=1, source_target_pairs={{0,16},{4,12},{8,24},{12,4},{16,0},{20,28},{24,8},{28,20},{1,17},{... | collective-permute-start | bytes 786440 | tf_op jit(solution)/shard_map/ppermute | solution.py:52
  86.5 7.7 %collective-permute-start.16 = (bf16[4,64,512]{2,1,0:T(8,128)(2,1)S(1)}, bf16[4,64,512]{2,1,0:T(8,128)(2,1)S(1)}, u32[]{:S(2)}, u32[]{:S(2)}) collective-permute-start(bf16[4,64,512]{2,1,0:T(8,128)(2,1)S(1)} %collective-permute-done.14.refs_1_), channel_id=1, source_target_pairs={{0,16},{4,12},{8,24},{12,4},{16,0},{20,28},{24,8},{28,20},{1,17},{... | collective-permute-start | bytes 786440 | tf_op jit(solution)/shard_map/ppermute | solution.py:52
  88.6 7.7 %collective-permute-start.17 = (bf16[4,64,512]{2,1,0:T(8,128)(2,1)S(1)}, bf16[4,64,512]{2,1,0:T(8,128)(2,1)}, u32[]{:S(2)}, u32[]{:S(2)}) collective-permute-start(bf16[4,64,512]{2,1,0:T(8,128)(2,1)S(1)} %stack_planes.4.refs_0_.refs_2_), channel_id=1, source_target_pairs={{0,4},{4,0},{8,12},{12,8},{16,20},{20,16},{24,28},{28,24},{1,5},{5... | collective-permute-start | bytes 786440 | tf_op jit(solution)/shard_map/ppermute | solution.py:411
  88.6 7.7 %collective-permute-start.19 = (bf16[4,64,512]{2,1,0:T(8,128)(2,1)S(1)}, bf16[4,64,512]{2,1,0:T(8,128)(2,1)}, u32[]{:S(2)}, u32[]{:S(2)}) collective-permute-start(bf16[4,64,512]{2,1,0:T(8,128)(2,1)S(1)} %collective-permute-done.14.refs_1_), channel_id=1, source_target_pairs={{0,4},{4,0},{8,12},{12,8},{16,20},{20,16},{24,28},{28,24},{1,5},{5... | collective-permute-start | bytes 786440 | tf_op jit(solution)/shard_map/ppermute | solution.py:411
  91.5 4.9 %collective-permute-start.18 = (bf16[4,64,512]{2,1,0:T(8,128)(2,1)S(1)}, bf16[4,64,512]{2,1,0:T(8,128)(2,1)}, u32[]{:S(2)}, u32[]{:S(2)}) collective-permute-start(bf16[4,64,512]{2,1,0:T(8,128)(2,1)S(1)} %collective-permute-done.15.refs_2_), channel_id=1, source_target_pairs={{0,4},{4,0},{8,12},{12,8},{16,20},{20,16},{24,28},{28,24},{1,5},{5... | collective-permute-start | bytes 786440 | tf_op jit(solution)/shard_map/ppermute | solution.py:411
  94.3 2.1 %collective-permute-start.20 = (bf16[4,64,512]{2,1,0:T(8,128)(2,1)S(1)}, bf16[4,64,512]{2,1,0:T(8,128)(2,1)}, u32[]{:S(2)}, u32[]{:S(2)}) collective-permute-start(bf16[4,64,512]{2,1,0:T(8,128)(2,1)S(1)} %collective-permute-done.16.refs_3_), channel_id=1, source_target_pairs={{0,4},{4,0},{8,12},{12,8},{16,20},{20,16},{24,28},{28,24},{1,5},{5... | collective-permute-start | bytes 786440 | tf_op jit(solution)/shard_map/ppermute | solution.py:411
  94.4 15.9 %copy-start.9 = (s32[4]{0:T(128)S(1)}, s32[4]{0:T(128)}, u32[]{:S(2)}) copy-start(s32[4]{0:T(128)} %refs_0_.16) | copy-start | bytes 52
  94.5 15.9 %slice-start = ((s8[8388608]{0:T(1024)(128)(4,1)}), s8[4194304]{0:T(1024)(128)(4,1)S(1)}, s32[]{:S(2)}) async-start(s8[8388608]{0:T(1024)(128)(4,1)} %bitcast.40), calls=%async_computation | async-start | bytes 8388608
  94.6 15.8 %slice-start.1 = ((s8[8388608]{0:T(1024)(128)(4,1)}), s8[4194304]{0:T(1024)(128)(4,1)S(1)}, s32[]{:S(2)}) async-start(s8[8388608]{0:T(1024)(128)(4,1)} %bitcast.40), calls=%async_computation.1 | async-start | bytes 8388608
  94.6 18.2 %collective-permute-start.31 = (bf16[1,4,64,512]{3,2,1,0:T(8,128)(2,1)S(1)}, bf16[1,4,64,512]{3,2,1,0:T(8,128)(2,1)S(1)}, u32[]{:S(2)}, u32[]{:S(2)}) collective-permute-start(bf16[1,4,64,512]{3,2,1,0:T(8,128)(2,1)S(1)} %get-tuple-element.32), channel_id=1, source_target_pairs={{0,8},{4,20},{8,0},{12,28},{16,24},{20,4},{24,16},{28,12},{1,9},{5... | collective-permute-start | bytes 786440 | tf_op jit(solution)/shard_map/ppermute | solution.py:52
  110.4 30.0 %slice-start.2 = ((s8[8388608]{0:T(1024)(128)(4,1)}), s8[4194304]{0:T(1024)(128)(4,1)S(1)}, s32[]{:S(2)}) async-start(s8[8388608]{0:T(1024)(128)(4,1)} %bitcast.42), calls=%async_computation.2 | async-start | bytes 8388608
  112.2 26.8 %collective-permute-start.21 = (bf16[4,4,64,512]{3,2,1,0:T(8,128)(2,1)S(1)}, bf16[4,4,64,512]{3,2,1,0:T(8,128)(2,1)S(1)}, u32[]{:S(2)}, u32[]{:S(2)}) collective-permute-start(bf16[4,4,64,512]{3,2,1,0:T(8,128)(2,1)S(1)} %expert_down.5), channel_id=1, source_target_pairs={{0,4},{4,0},{8,12},{12,8},{16,20},{20,16},{24,28},{28,24},{1,5},{5... | collective-permute-start | bytes 3145736 | tf_op jit(solution)/shard_map/ppermute | solution.py:411
  112.9 7.0 %collective-permute-start.32 = (bf16[64,512]{1,0:T(8,128)(2,1)S(1)}, bf16[64,512]{1,0:T(8,128)(2,1)S(1)}, u32[]{:S(2)}, u32[]{:S(2)}) collective-permute-start(bf16[64,512]{1,0:T(8,128)(2,1)S(1)} %get-tuple-element.49), channel_id=1, source_target_pairs={{0,1},{1,2},{2,3},{3,0},{4,5},{5,6},{6,7},{7,4},{8,9},{9,10},{10,1... | collective-permute-start | bytes 196616 | tf_op jit(solution)/shard_map/ppermute | solution.py:75
  113.5 8.2 %collective-permute-start.33 = (bf16[64,512]{1,0:T(8,128)(2,1)S(1)}, bf16[64,512]{1,0:T(8,128)(2,1)S(1)}, u32[]{:S(2)}, u32[]{:S(2)}) collective-permute-start(bf16[64,512]{1,0:T(8,128)(2,1)S(1)} %get-tuple-element.48), channel_id=1, source_target_pairs={{0,2},{1,3},{2,0},{3,1},{4,6},{5,7},{6,4},{7,5},{8,10},{9,11},{10,... | collective-permute-start | bytes 196616 | tf_op jit(solution)/shard_map/ppermute | solution.py:75
  116.6 5.2 %collective-permute-start.34 = (bf16[64,512]{1,0:T(8,128)(2,1)S(1)}, bf16[64,512]{1,0:T(8,128)(2,1)S(1)}, u32[]{:S(2)}, u32[]{:S(2)}) collective-permute-start(bf16[64,512]{1,0:T(8,128)(2,1)S(1)} %get-tuple-element.47), channel_id=1, source_target_pairs={{0,3},{1,0},{2,1},{3,2},{4,7},{5,4},{6,5},{7,6},{8,11},{9,8},{10,9... | collective-permute-start | bytes 196616 | tf_op jit(solution)/shard_map/ppermute | solution.py:75
  121.9 18.5 %slice-start.3 = ((s8[8388608]{0:T(1024)(128)(4,1)}), s8[4194304]{0:T(1024)(128)(4,1)S(1)}, s32[]{:S(2)}) async-start(s8[8388608]{0:T(1024)(128)(4,1)} %bitcast.42), calls=%async_computation.3 | async-start | bytes 8388608
  121.9 8.9 %collective-permute-start.35 = (bf16[4,64,512]{2,1,0:T(8,128)(2,1)S(1)}, bf16[4,64,512]{2,1,0:T(8,128)(2,1)S(1)}, u32[]{:S(2)}, u32[]{:S(2)}) collective-permute-start(bf16[4,64,512]{2,1,0:T(8,128)(2,1)S(1)} %stack_planes.6.refs_0_), channel_id=1, source_target_pairs={{0,8},{4,20},{8,0},{12,28},{16,24},{20,4},{24,16},{28,12},{1,9},{5... | collective-permute-start | bytes 786440 | tf_op jit(solution)/shard_map/ppermute | solution.py:52
  123.6 8.7 %collective-permute-start.36 = (bf16[4,64,512]{2,1,0:T(8,128)(2,1)S(1)}, bf16[4,64,512]{2,1,0:T(8,128)(2,1)S(1)}, u32[]{:S(2)}, u32[]{:S(2)}) collective-permute-start(bf16[4,64,512]{2,1,0:T(8,128)(2,1)S(1)} %stack_planes.6.refs_0_), channel_id=1, source_target_pairs={{0,16},{4,12},{8,24},{12,4},{16,0},{20,28},{24,8},{28,20},{1,17},{... | collective-permute-start | bytes 786440 | tf_op jit(solution)/shard_map/ppermute | solution.py:52
  130.8 6.4 %collective-permute-start.37 = (bf16[4,64,512]{2,1,0:T(8,128)(2,1)S(1)}, bf16[4,64,512]{2,1,0:T(8,128)(2,1)S(1)}, u32[]{:S(2)}, u32[]{:S(2)}) collective-permute-start(bf16[4,64,512]{2,1,0:T(8,128)(2,1)S(1)} %collective-permute-done.35.refs_1_), channel_id=1, source_target_pairs={{0,16},{4,12},{8,24},{12,4},{16,0},{20,28},{24,8},{28,20},{1,17},{... | collective-permute-start | bytes 786440 | tf_op jit(solution)/shard_map/ppermute | solution.py:52
  131.8 8.5 %collective-permute-start.38 = (bf16[4,64,512]{2,1,0:T(8,128)(2,1)S(1)}, bf16[4,64,512]{2,1,0:T(8,128)(2,1)S(1)}, u32[]{:S(2)}, u32[]{:S(2)}) collective-permute-start(bf16[4,64,512]{2,1,0:T(8,128)(2,1)S(1)} %stack_planes.6.refs_0_), channel_id=1, source_target_pairs={{0,4},{4,0},{8,12},{12,8},{16,20},{20,16},{24,28},{28,24},{1,5},{5... | collective-permute-start | bytes 786440 | tf_op jit(solution)/shard_map/ppermute | solution.py:411
  131.8 8.5 %collective-permute-start.40 = (bf16[4,64,512]{2,1,0:T(8,128)(2,1)S(1)}, bf16[4,64,512]{2,1,0:T(8,128)(2,1)S(1)}, u32[]{:S(2)}, u32[]{:S(2)}) collective-permute-start(bf16[4,64,512]{2,1,0:T(8,128)(2,1)S(1)} %collective-permute-done.35.refs_1_), channel_id=1, source_target_pairs={{0,4},{4,0},{8,12},{12,8},{16,20},{20,16},{24,28},{28,24},{1,5},{5... | collective-permute-start | bytes 786440 | tf_op jit(solution)/shard_map/ppermute | solution.py:411
  132.3 8.0 %collective-permute-start.39 = (bf16[4,64,512]{2,1,0:T(8,128)(2,1)S(1)}, bf16[4,64,512]{2,1,0:T(8,128)(2,1)S(1)}, u32[]{:S(2)}, u32[]{:S(2)}) collective-permute-start(bf16[4,64,512]{2,1,0:T(8,128)(2,1)S(1)} %collective-permute-done.36.refs_2_), channel_id=1, source_target_pairs={{0,4},{4,0},{8,12},{12,8},{16,20},{20,16},{24,28},{28,24},{1,5},{5... | collective-permute-start | bytes 786440 | tf_op jit(solution)/shard_map/ppermute | solution.py:411
  137.2 3.1 %collective-permute-start.41 = (bf16[4,64,512]{2,1,0:T(8,128)(2,1)S(1)}, bf16[4,64,512]{2,1,0:T(8,128)(2,1)S(1)}, u32[]{:S(2)}, u32[]{:S(2)}) collective-permute-start(bf16[4,64,512]{2,1,0:T(8,128)(2,1)S(1)} %collective-permute-done.37.refs_3_), channel_id=1, source_target_pairs={{0,4},{4,0},{8,12},{12,8},{16,20},{20,16},{24,28},{28,24},{1,5},{5... | collective-permute-start | bytes 786440 | tf_op jit(solution)/shard_map/ppermute | solution.py:411
  139.3 9.2 %collective-permute-start.22 = (bf16[2,4,64,512]{3,2,1,0:T(8,128)(2,1)S(1)}, bf16[2,4,64,512]{3,2,1,0:T(8,128)(2,1)S(1)}, u32[]{:S(2)}, u32[]{:S(2)}) collective-permute-start(bf16[2,4,64,512]{3,2,1,0:T(8,128)(2,1)S(1)} %get-tuple-element.26), channel_id=1, source_target_pairs={{0,16},{4,12},{8,24},{12,4},{16,0},{20,28},{24,8},{28,20},{1,17},{... | collective-permute-start | bytes 1572872 | tf_op jit(solution)/shard_map/ppermute | solution.py:52
  150.5 2.7 %collective-permute-start.42 = (bf16[4,4,64,512]{3,2,1,0:T(8,128)(2,1)S(1)}, bf16[4,4,64,512]{3,2,1,0:T(8,128)(2,1)S(1)}, u32[]{:S(2)}, u32[]{:S(2)}) collective-permute-start(bf16[4,4,64,512]{3,2,1,0:T(8,128)(2,1)S(1)} %expert_down.7), channel_id=1, source_target_pairs={{0,4},{4,0},{8,12},{12,8},{16,20},{20,16},{24,28},{28,24},{1,5},{5... | collective-permute-start | bytes 3145736 | tf_op jit(solution)/shard_map/ppermute | solution.py:411
  153.5 12.1 %collective-permute-start.43 = (bf16[2,4,64,512]{3,2,1,0:T(8,128)(2,1)S(1)}, bf16[2,4,64,512]{3,2,1,0:T(8,128)(2,1)S(1)}, u32[]{:S(2)}, u32[]{:S(2)}) collective-permute-start(bf16[2,4,64,512]{3,2,1,0:T(8,128)(2,1)S(1)} %get-tuple-element.34), channel_id=1, source_target_pairs={{0,16},{4,12},{8,24},{12,4},{16,0},{20,28},{24,8},{28,20},{1,17},{... | collective-permute-start | bytes 1572872 | tf_op jit(solution)/shard_map/ppermute | solution.py:52
  154.5 12.4 %collective-permute-start.23 = (bf16[1,4,64,512]{3,2,1,0:T(8,128)(2,1)S(1)}, bf16[1,4,64,512]{3,2,1,0:T(8,128)(2,1)S(1)}, u32[]{:S(2)}, u32[]{:S(2)}) collective-permute-start(bf16[1,4,64,512]{3,2,1,0:T(8,128)(2,1)S(1)} %get-tuple-element.28), channel_id=1, source_target_pairs={{0,8},{4,20},{8,0},{12,28},{16,24},{20,4},{24,16},{28,12},{1,9},{5... | collective-permute-start | bytes 786440 | tf_op jit(solution)/shard_map/ppermute | solution.py:52
  165.7 6.4 %collective-permute-start.44 = (bf16[1,4,64,512]{3,2,1,0:T(8,128)(2,1)S(1)}, bf16[1,4,64,512]{3,2,1,0:T(8,128)(2,1)S(1)}, u32[]{:S(2)}, u32[]{:S(2)}) collective-permute-start(bf16[1,4,64,512]{3,2,1,0:T(8,128)(2,1)S(1)} %get-tuple-element.36), channel_id=1, source_target_pairs={{0,8},{4,20},{8,0},{12,28},{16,24},{20,4},{24,16},{28,12},{1,9},{5... | collective-permute-start | bytes 786440 | tf_op jit(solution)/shard_map/ppermute | solution.py:52
  167.0 8.5 %collective-permute-start.24 = (bf16[64,512]{1,0:T(8,128)(2,1)S(1)}, bf16[64,512]{1,0:T(8,128)(2,1)S(1)}, u32[]{:S(2)}, u32[]{:S(2)}) collective-permute-start(bf16[64,512]{1,0:T(8,128)(2,1)S(1)} %get-tuple-element.53), channel_id=1, source_target_pairs={{0,1},{1,2},{2,3},{3,0},{4,5},{5,6},{6,7},{7,4},{8,9},{9,10},{10,1... | collective-permute-start | bytes 196616 | tf_op jit(solution)/shard_map/ppermute | solution.py:75
  168.4 7.7 %collective-permute-start.25 = (bf16[64,512]{1,0:T(8,128)(2,1)S(1)}, bf16[64,512]{1,0:T(8,128)(2,1)S(1)}, u32[]{:S(2)}, u32[]{:S(2)}) collective-permute-start(bf16[64,512]{1,0:T(8,128)(2,1)S(1)} %get-tuple-element.52), channel_id=1, source_target_pairs={{0,2},{1,3},{2,0},{3,1},{4,6},{5,7},{6,4},{7,5},{8,10},{9,11},{10,... | collective-permute-start | bytes 196616 | tf_op jit(solution)/shard_map/ppermute | solution.py:75
  170.1 6.0 %collective-permute-start.26 = (bf16[64,512]{1,0:T(8,128)(2,1)S(1)}, bf16[64,512]{1,0:T(8,128)(2,1)S(1)}, u32[]{:S(2)}, u32[]{:S(2)}) collective-permute-start(bf16[64,512]{1,0:T(8,128)(2,1)S(1)} %get-tuple-element.51), channel_id=1, source_target_pairs={{0,3},{1,0},{2,1},{3,2},{4,7},{5,4},{6,5},{7,6},{8,11},{9,8},{10,9... | collective-permute-start | bytes 196616 | tf_op jit(solution)/shard_map/ppermute | solution.py:75
  172.2 6.2 %collective-permute-start.45 = (bf16[64,512]{1,0:T(8,128)(2,1)S(1)}, bf16[64,512]{1,0:T(8,128)(2,1)S(1)}, u32[]{:S(2)}, u32[]{:S(2)}) collective-permute-start(bf16[64,512]{1,0:T(8,128)(2,1)S(1)} %get-tuple-element.45), channel_id=1, source_target_pairs={{0,1},{1,2},{2,3},{3,0},{4,5},{5,6},{6,7},{7,4},{8,9},{9,10},{10,1... | collective-permute-start | bytes 196616 | tf_op jit(solution)/shard_map/ppermute | solution.py:75
  173.5 7.1 %collective-permute-start.46 = (bf16[64,512]{1,0:T(8,128)(2,1)S(1)}, bf16[64,512]{1,0:T(8,128)(2,1)S(1)}, u32[]{:S(2)}, u32[]{:S(2)}) collective-permute-start(bf16[64,512]{1,0:T(8,128)(2,1)S(1)} %get-tuple-element.44), channel_id=1, source_target_pairs={{0,2},{1,3},{2,0},{3,1},{4,6},{5,7},{6,4},{7,5},{8,10},{9,11},{10,... | collective-permute-start | bytes 196616 | tf_op jit(solution)/shard_map/ppermute | solution.py:75
  175.5 5.2 %collective-permute-start.47 = (bf16[64,512]{1,0:T(8,128)(2,1)S(1)}, bf16[64,512]{1,0:T(8,128)(2,1)S(1)}, u32[]{:S(2)}, u32[]{:S(2)}) collective-permute-start(bf16[64,512]{1,0:T(8,128)(2,1)S(1)} %get-tuple-element.43), channel_id=1, source_target_pairs={{0,3},{1,0},{2,1},{3,2},{4,7},{5,4},{6,5},{7,6},{8,11},{9,8},{10,9... | collective-permute-start | bytes 196616 | tf_op jit(solution)/shard_map/ppermute | solution.py:75
  176.1 7.2 %collective-permute-start.27 = (bf16[4,64,512]{2,1,0:T(8,128)(2,1)S(1)}, bf16[4,64,512]{2,1,0:T(8,128)(2,1)S(1)}, u32[]{:S(2)}, u32[]{:S(2)}) collective-permute-start(bf16[4,64,512]{2,1,0:T(8,128)(2,1)S(1)} %stack_planes.5.refs_2_), channel_id=1, source_target_pairs={{0,8},{4,20},{8,0},{12,28},{16,24},{20,4},{24,16},{28,12},{1,9},{5... | collective-permute-start | bytes 786440 | tf_op jit(solution)/shard_map/ppermute | solution.py:52
  180.7 9.2 %collective-permute-start.48 = (bf16[4,64,512]{2,1,0:T(8,128)(2,1)S(1)}, bf16[4,64,512]{2,1,0:T(8,128)(2,1)S(1)}, u32[]{:S(2)}, u32[]{:S(2)}) collective-permute-start(bf16[4,64,512]{2,1,0:T(8,128)(2,1)S(1)} %stack_planes.7.refs_6_), channel_id=1, source_target_pairs={{0,8},{4,20},{8,0},{12,28},{16,24},{20,4},{24,16},{28,12},{1,9},{5... | collective-permute-start | bytes 786440 | tf_op jit(solution)/shard_map/ppermute | solution.py:52
  182.0 9.4 %collective-permute-start.28 = (bf16[4,64,512]{2,1,0:T(8,128)(2,1)S(1)}, bf16[4,64,512]{2,1,0:T(8,128)(2,1)S(1)}, u32[]{:S(2)}, u32[]{:S(2)}) collective-permute-start(bf16[4,64,512]{2,1,0:T(8,128)(2,1)S(1)} %stack_planes.5.refs_2_), channel_id=1, source_target_pairs={{0,16},{4,12},{8,24},{12,4},{16,0},{20,28},{24,8},{28,20},{1,17},{... | collective-permute-start | bytes 786440 | tf_op jit(solution)/shard_map/ppermute | solution.py:52
  183.3 8.1 %collective-permute-start.29 = (bf16[4,64,512]{2,1,0:T(8,128)(2,1)S(1)}, bf16[4,64,512]{2,1,0:T(8,128)(2,1)S(1)}, u32[]{:S(2)}, u32[]{:S(2)}) collective-permute-start(bf16[4,64,512]{2,1,0:T(8,128)(2,1)S(1)} %collective-permute-done.27.refs_3_), channel_id=1, source_target_pairs={{0,16},{4,12},{8,24},{12,4},{16,0},{20,28},{24,8},{28,20},{1,17},{... | collective-permute-start | bytes 786440 | tf_op jit(solution)/shard_map/ppermute | solution.py:52
  184.5 9.5 %collective-permute-start.49 = (bf16[4,64,512]{2,1,0:T(8,128)(2,1)S(1)}, bf16[4,64,512]{2,1,0:T(8,128)(2,1)S(1)}, u32[]{:S(2)}, u32[]{:S(2)}) collective-permute-start(bf16[4,64,512]{2,1,0:T(8,128)(2,1)S(1)} %stack_planes.7.refs_6_), channel_id=1, source_target_pairs={{0,16},{4,12},{8,24},{12,4},{16,0},{20,28},{24,8},{28,20},{1,17},{... | collective-permute-start | bytes 786440 | tf_op jit(solution)/shard_map/ppermute | solution.py:52
  189.9 6.9 %collective-permute-start.50 = (bf16[4,64,512]{2,1,0:T(8,128)(2,1)S(1)}, bf16[4,64,512]{2,1,0:T(8,128)(2,1)S(1)}, u32[]{:S(2)}, u32[]{:S(2)}) collective-permute-start(bf16[4,64,512]{2,1,0:T(8,128)(2,1)S(1)} %collective-permute-done.48.refs_7_), channel_id=1, source_target_pairs={{0,16},{4,12},{8,24},{12,4},{16,0},{20,28},{24,8},{28,20},{1,17},{... | collective-permute-start | bytes 786440 | tf_op jit(solution)/shard_map/ppermute | solution.py:52
  198.3 2.4 %collective-permute-start.51 = (bf16[512,512]{1,0:T(8,128)(2,1)S(1)}, bf16[512,512]{1,0:T(8,128)(2,1)S(1)}, u32[]{:S(2)}, u32[]{:S(2)}) collective-permute-start(bf16[512,512]{1,0:T(8,128)(2,1)S(1)} %bitcast.54), channel_id=1, source_target_pairs={{0,4},{4,0},{8,12},{12,8},{16,20},{20,16},{24,28},{28,24},{1,5},{5... | collective-permute-start | bytes 1572872 | tf_op jit(solution)/shard_map/ppermute | solution.py:411
  (5 other events, 16.3 us)

commit v4 on v3

--- a/solution.py
+++ b/solution.py
@@ -41,6 +41,7 @@
 SMEM = pl.BlockSpec(memory_space=pltpu.SMEM)
 VMEM = pl.BlockSpec(memory_space=pltpu.VMEM)
 ANY = pl.BlockSpec(memory_space=pl.ANY)
+HBM = pl.BlockSpec(memory_space=pltpu.HBM)
 MIB = 1024 * 1024
 
 
@@ -50,15 +51,6 @@
 
 def exchange(value, n_dp, step):
     return lax.ppermute(value, "dp", step_pairs(n_dp, step))
-
-
-def scatter_sum(keep, send, n_dp, n_bits, afters=()):
-    seen = []
-    for i, step in enumerate(range(n_bits - 1, -1, -1)):
-        got = exchange(send, n_dp, step)
-        keep, send = add_split(keep, got, afters[i] if i < len(afters) else None, step > 0)
-        seen.append(keep)
-    return keep[0], seen
 
 
 def gather_all(piece, n_dp, n_bits):
@@ -83,7 +75,6 @@
         in_specs=in_specs,
         out_specs=out_specs,
         compiler_params=pltpu.CompilerParams(vmem_limit_bytes=limit * MIB),
-        cost_estimate=pl.CostEstimate(flops=flops, bytes_accessed=moved, transcendentals=0),
         name=name,
         **more,
     )
@@ -170,26 +161,6 @@
         base = base + lax.rem(block, self.local_blocks)
         index = base * (BLK // self.share) + lax.div(lax.rem(row, BLK), self.share)
         return index, lax.div(owner, 2) == place.chip
-
-
-def load_kernel(src, after, out, sem):
-    copy = pltpu.make_async_copy(src, out, sem)
-    copy.start()
-    copy.wait()
-
-
-def load(weight, after, name):
-    out = call(
-        load_kernel,
-        pltpu.VMEM(weight.shape, weight.dtype),
-        [ANY, ANY],
-        VMEM,
-        name,
-        1,
-        moved=2 * weight.size,
-        scratch_shapes=[pltpu.SemaphoreType.DMA],
-    )(weight, after)
-    return pltpu.with_memory_space_constraint(out, pltpu.VMEM)
 
 
 def project_kernel(make_place, parts, n_w, n_res, *refs):
@@ -225,7 +196,7 @@
         out[i] = value.astype(out.dtype)
 
 
-def project(make_place, parts, own, other, weights, extra, held):
+def project(make_place, parts, own, other, weights, extra):
     last = len(extra) > 0
     rows = own.shape[0]
     depth, half = weights[0].shape
@@ -233,7 +204,7 @@
     return call(
         lambda *refs: project_kernel(make_place, parts, len(weights), len(extra), *refs),
         jax.ShapeDtypeStruct((2, rows, half), jnp.bfloat16 if last else jnp.float32),
-        [ANY, ANY] + [VMEM] * (len(weights) + len(extra) + len(held)),
+        [ANY, ANY] + [VMEM] * (len(weights) + len(extra)),
         VMEM,
         "project_last" if last else "project_first",
         20,
@@ -245,7 +216,7 @@
             pltpu.VMEM((rows, k), jnp.bfloat16),
             pltpu.SemaphoreType.DMA((2, len(weights))),
         ],
-    )(own, other, *weights, *extra, *held)
+    )(own, other, *weights, *extra)
 
 
 def pick_kernel(make_place, layout, n_chip, chosen, att_ref, *refs):
@@ -309,50 +280,85 @@
 
 
 def hidden_kernel(make_place, n, *refs):
-    own, other, wg, wu, hid, xs = refs[:n], refs[n : 2 * n], *refs[2 * n : 2 * n + 2], *refs[-2:]
+    own, other, wg, wu = refs[:n], refs[n : 2 * n], *refs[2 * n : 2 * n + 2]
+    hid, xs, wgs, wus, sems = refs[-5:]
     n_z, rows, width = own[0].shape
     place = make_place()
+    n_tile, _, tile = wgs.shape
+
+    def copies(i):
+        at = pl.ds(pl.multiple_of(i * tile, tile), tile)
+        return (
+            pltpu.make_async_copy(wg.at[:, at], wgs.at[i], sems.at[0, i]),
+            pltpu.make_async_copy(wu.at[:, at], wus.at[i], sems.at[1, i]),
+        )
+
+    def start(i):
+        for c in copies(i):
+            c.start()
+
+    start(0)
+    if n_tile > 1:
+        start(1)
     for s, pieces in enumerate((own, other)):
         for z in range(n_z):
             at = (place.behind(z) * 2 + (place.side ^ s)) * width
             at = pl.ds(pl.multiple_of(at, width), width)
             for r in range(n):
                 xs[r * rows : (r + 1) * rows, at] = pieces[r][z]
-    ff = wg.shape[1]
-    tile = min(ff, 256)
 
     def one(i, carry):
+        for c in copies(i):
+            c.wait()
+
+        @pl.when(i + 2 < n_tile)
+        def _():
+            start(i + 2)
+
         at = pl.ds(pl.multiple_of(i * tile, tile), tile)
-        g = jnp.dot(xs[...], wg[:, at], preferred_element_type=jnp.float32)
-        u = jnp.dot(xs[...], wu[:, at], preferred_element_type=jnp.float32)
+        g = jnp.dot(xs[...], wgs[i], preferred_element_type=jnp.float32)
+        u = jnp.dot(xs[...], wus[i], preferred_element_type=jnp.float32)
         hid[:, at] = (g / (1.0 + jnp.exp(-g)) * u).astype(jnp.bfloat16)
         return carry
 
-    lax.fori_loop(0, ff // tile, one, 0)
+    lax.fori_loop(0, n_tile, one, 0)
 
 
 def hidden_units(make_place, own, other, w_gate, w_up, after):
     n = len(own)
     n_z, rows, width = own[0].shape
     model_width, ff = w_gate.shape
+    tile = min(ff, 256)
     extra = [] if after is None else [after]
     return call(
         lambda *refs: hidden_kernel(make_place, n, *refs),
         jax.ShapeDtypeStruct((n * rows, ff), jnp.bfloat16),
-        [VMEM] * (2 * n + 2) + [ANY] * len(extra),
+        [VMEM] * (2 * n) + [HBM] * 2 + [ANY] * len(extra),
         VMEM,
         "expert_hidden",
-        14,
+        28,
         flops=4 * n * rows * ff * model_width,
-        moved=2 * n * rows * model_width,
-        scratch_shapes=[pltpu.VMEM((n * rows, model_width), jnp.bfloat16)],
+        moved=4 * model_width * ff,
+        scratch_shapes=[
+            pltpu.VMEM((n * rows, model_width), jnp.bfloat16),
+            pltpu.VMEM((ff // tile, model_width, tile), jnp.bfloat16),
+            pltpu.VMEM((ff // tile, model_width, tile), jnp.bfloat16),
+            pltpu.SemaphoreType.DMA((2, ff // tile)),
+        ],
     )(*own, *other, w_gate, w_up, *extra)
 
 
 def down_kernel(make_place, layout, order, s, counts, hid, wd, values, *refs):
-    out = refs[-1]
+    out, wds, sems = refs[-3:]
     n, n_z, rows, width = out.shape
     place = make_place()
+    copies = []
+    for z in range(n_z):
+        at = (place.ahead(z) * 2 + (place.side ^ s)) * width
+        at = pl.ds(pl.multiple_of(at, width), width)
+        copies.append(pltpu.make_async_copy(wd.at[:, at], wds.at[z], sems.at[z]))
+    for c in copies:
+        c.start()
     count = counts[place.expert]
     scale = []
     for r in range(n):
@@ -360,26 +366,73 @@
         value = values[pl.ds(pl.multiple_of(row, rows), rows), :]
         scale.append(jnp.where(lax.div(row, BLK) < count, value, jnp.zeros_like(value)))
     for z in range(n_z):
-        at = (place.ahead(z) * 2 + (place.side ^ s)) * width
-        at = pl.ds(pl.multiple_of(at, width), width)
-        part = jnp.dot(hid[...], wd[:, at], preferred_element_type=jnp.float32)
+        copies[z].wait()
+        part = jnp.dot(hid[...], wds[z], preferred_element_type=jnp.float32)
         for r in range(n):
             out[order[r], z] = (part[r * rows : (r + 1) * rows] * scale[r]).astype(out.dtype)
 
 
 def down(make_place, layout, order, s, n_z, width, counts, hid, w_down, values, after):
     n = len(order)
+    ff = hid.shape[1]
     extra = [] if after is None else [after]
     return call(
         lambda *refs: down_kernel(make_place, layout, order, s, *refs),
         jax.ShapeDtypeStruct((n, n_z, layout.share, width), jnp.bfloat16),
-        [SMEM] + [VMEM] * 3 + [ANY] * len(extra),
+        [SMEM, VMEM, HBM, VMEM] + [ANY] * len(extra),
         VMEM,
         "expert_down",
-        10,
+        12,
         flops=2 * hid.size * n_z * width,
-        moved=2 * n * layout.share * n_z * width,
+        moved=2 * ff * n_z * width,
+        scratch_shapes=[
+            pltpu.VMEM((n_z, ff, width), jnp.bfloat16),
+            pltpu.SemaphoreType.DMA((n_z,)),
+        ],
     )(counts, hid, w_down, values, *extra)
+
+
+def group_steps(layout, scope, tables, grains):
+    make_place, n_dp, n_bits, n_expert, half, reverse, to_partner = scope
+    chosen, counts, values, w_gate, w_up, w_down = tables
+    n_chip = 1 << n_bits
+    plain = list(range(n_chip))
+    after = yield
+    keep, send = pick(make_place, layout, n_chip, n_expert, chosen, grains, after)
+    after = yield keep, None
+    for step in range(n_bits - 1, -1, -1):
+        keep, send = add_split(keep, exchange(send, n_dp, step), after, step > 0)
+        after = yield keep, None
+    crossed = swap_planes(keep[0], n_expert, after)
+    own_half = gather_all(crossed, n_dp, n_bits)
+    after = yield (own_half[1] if layout.group == GROUPS - 1 else crossed), None
+    got = [to_partner(p) for p in own_half]
+    other_half = [got[r] for r in reverse]
+    hid = hidden_units(make_place, own_half, other_half, w_gate, w_up, after)
+    after = yield hid, None
+
+    def downs(order, s):
+        return down(
+            make_place, layout, order, s, n_expert, half, counts, hid, w_down, values, after
+        )
+
+    theirs = downs(reverse, 1)
+    after = yield theirs, None
+    mine = downs(plain, 0)
+    after = yield mine, None
+    keep, send = add_split(mine, to_partner(theirs), after, True)
+    after = yield keep, None
+    for step in range(n_bits - 1, -1, -1):
+        keep, send = add_split(keep, exchange(send, n_dp, step), after, step > 0)
+        after = yield keep, None
+    crossed = swap_planes(keep[0], n_expert, after)
+    yield crossed, gather_all(crossed, n_dp, n_bits)
+
+
+def kernel_order(n_bits):
+    order = [0, 0] + [1, 0] * n_bits + [1, 1]
+    order += [0] * 4 + [1] * 2 + [0]
+    return order + [1, 1] + [0, 1] * n_bits + [1]
 
 
 def body(
@@ -422,17 +475,16 @@
     pieces = [w for p in pieces for w in p]
     context_other = to_partner(context)
     residual_own, residual_other = split_sides(residual)
-    w_gate = load(gate_weight[0], w_other, "load_gate")
-    w_up = load(up_weight[0], w_other, "load_up")
-    w_down = load(down_weight[0], w_other, "load_down")
+    w_gate, w_up, w_down = gate_weight[0], up_weight[0], down_weight[0]
     plain = list(range(n_chip))
     top = n_chip // 2
+    share = CAP * BLK // GROUPS // n_chip
 
     def make_place():
         return Place(n_bits, n_expert)
 
     first = project(
-        make_place, plain[:top], context, context_other, pieces[:n_chip], (), (w_gate, w_up, w_down)
+        make_place, plain[:top], context, context_other, pieces[:n_chip], ()
     )
     attended = project(
         make_place,
@@ -441,41 +493,22 @@
         context_other,
         pieces[n_chip:],
         (first, residual_own, residual_other),
-        (),
     )
 
     layouts = [Layout(group, n_chip, local_blocks) for group in range(GROUPS)]
-    share = layouts[0].share
     grains = attended.reshape(-1, share, half)
     values = gate_values.reshape(-1, 1)
 
-    received = []
-    after_pick, after_add, after_stack, after_hidden, after_down = None, None, None, None, None
-    for layout in layouts:
-        keep, send = pick(make_place, layout, n_chip, n_expert, chosen_blocks, grains, after_pick)
-        mine, sums = scatter_sum(keep, send, n_dp, n_bits, [after_add])
-        after_pick = mine
-        crossed = swap_planes(mine, n_expert, after_stack)
-        after_add = crossed
-        own_half = gather_all(crossed, n_dp, n_bits)
-        got = [to_partner(p) for p in own_half]
-        other_half = [got[r] for r in reverse]
-        hid = hidden_units(make_place, own_half, other_half, w_gate, w_up, after_hidden)
-        after_stack = hid
-
-        def downs(order, s, after):
-            return down(
-                make_place, layout, order, s, n_expert, half, block_counts, hid, w_down, values, after
-            )
-
-        got = to_partner(downs(reverse, 1, after_down))
-        mine = downs(plain, 0, after_down)
-        keep, send = add_split(mine, got, None, True)
-        after_hidden = keep
-        mine, sums = scatter_sum(keep, send, n_dp, n_bits)
-        after_down = sums[0]
-        crossed = swap_planes(mine, n_expert)
-        received += gather_all(crossed, n_dp, n_bits)
+    scope = (make_place, n_dp, n_bits, n_expert, half, reverse, to_partner)
+    tables = (chosen_blocks, block_counts, values, w_gate, w_up, w_down)
+    groups = [group_steps(layout, scope, tables, grains) for layout in layouts]
+    for group in groups:
+        next(group)
+    after, received = None, [None] * GROUPS
+    for g in kernel_order(n_bits):
+        after, done = groups[g].send(after)
+        received[g] = done
+    received = [piece for pieces in received for piece in pieces]
 
     mixed = finish(make_place, layouts, n_chip, chosen_blocks, grains, received).reshape(2, local_tokens, half)
     got = to_partner(mixed[1])

time: 202 us -> 205 us (1.015)
  local copies, waits for them, and re-layouts: 25.1 us -> 13.2 us
  waiting for transfers between devices: 84.1 us -> 90 us
  Pallas kernels: 34.5 us -> 39.4 us
  starting transfers between devices: 56.6 us -> 60.3 us
    unnamed x34 -> x26, local copies, waits for them, and re-layouts: 22.2 us -> 10.2 us
    ppermute x26, waiting for transfers between devices: 67.2 us -> 75.1 us  [exchange(): return lax.ppermute(value, 'dp', step_pairs(n_dp, step))]
    pallas_call x4, Pallas kernels: 7.28 us -> 12.1 us  [down(): call(lambda *refs: down_kernel(make_place, layout, order, s, *refs), jax....]
    pallas_call x2, Pallas kernels: 12.1 us -> 16.2 us  [hidden_units(): call(lambda *refs: hidden_kernel(make_place, n, *refs), jax.ShapeDtypeStr...]
    ppermute x12, starting transfers between devices: 17.6 us -> 20.2 us  [swap_planes(): out.append(lax.ppermute(parts[k], 'expert', pairs))]
  transfers between devices with their start and end apart: 52 -> 52, of which waited for: 26 -> 28; matrix products, arithmetic and copies ran while one was open for 1% -> 1% of each run, Pallas kernels for 13% -> 5%
where the time goes in v4:
time: 205 us
  waiting for transfers between devices  90 us (44%)
  starting transfers between devices  60.3 us (29%)
  Pallas kernels  39.4 us (19%)
  local copies, waits for them, and re-layouts  13.2 us (6%)
    ppermute x26, waiting for transfers between devices, exchange(): return lax.ppermute(value, 'dp', step_pairs(n_dp, step))  75.1 us
    ppermute x26, starting transfers between devices, exchange(): return lax.ppermute(value, 'dp', step_pairs(n_dp, step))  37.1 us
    ppermute x12, starting transfers between devices, swap_planes(): out.append(lax.ppermute(parts[k], 'expert', pairs))  20.2 us
    pallas_call x2, Pallas kernels, hidden_units(): call(lambda *refs: hidden_kernel(make_place, n, *refs), jax.ShapeDtypeStr...  16.2 us
    pallas_call x4, Pallas kernels, down(): call(lambda *refs: down_kernel(make_place, layout, order, s, *refs), jax....  12.1 us
    ppermute x12, waiting for transfers between devices, swap_planes(): out.append(lax.ppermute(parts[k], 'expert', pairs))  10.3 us
    unnamed x26, local copies, waits for them, and re-layouts  10.2 us
    pallas_call x2, Pallas kernels, project(): call(lambda *refs: project_kernel(make_place, parts, len(weights), len(ex...  6.7 us
  transfers between devices with their start and end apart: 52, of which 28 were waited for; matrix products, arithmetic and copies ran while one was open for 1% of the time, Pallas kernels for 5%

profile of v4, /device:TPU:0, one launch (start us, length us, event | category | flops | bytes accessed | tf_op | source)
XLA Modules:
  0.0 204.6 jit_solution(17882717118820531762)
XLA Ops:
  0.5 1.4 constant_dynamic-slice_fusion.2
  2.0 2.9 %collective-permute-start.4 = (bf16[512,512]{1,0:T(8,128)(2,1)S(1)}, bf16[512,512]{1,0:T(8,128)(2,1)S(1)}, u32[]{:S(2)}, u32[]{:S(2)}) collective-permute-start(bf16[512,512]{1,0:T(8,128)(2,1)S(1)} %get-tuple-element.42.refs_2_), channel_id=1, source_target_pairs={{0,8},{4,20},{8,0},{12,28},{16,24},{20,4},{24,16},{28,12},{1,9},{5... | collective-permute-start | bytes 1572872 | tf_op jit(solution)/shard_map/ppermute | solution.py:53
  4.9 3.1 %collective-permute-done.2.refs_3_ = bf16[512,512]{1,0:T(8,128)(2,1)S(1)} collective-permute-done((bf16[512,512]{1,0:T(8,128)(2,1)S(1)}, bf16[512,512]{1,0:T(8,128)(2,1)S(1)}, u32[]{:S(2)}, u32[]{:S(2)}) %collective-permute-start.2) | collective-permute-done | bytes 524320 | tf_op jit(solution)/shard_map/ppermute | solution.py:464
  8.0 2.9 %collective-permute-start.6 = (bf16[512,512]{1,0:T(8,128)(2,1)S(1)}, bf16[512,512]{1,0:T(8,128)(2,1)S(1)}, u32[]{:S(2)}, u32[]{:S(2)}) collective-permute-start(bf16[512,512]{1,0:T(8,128)(2,1)S(1)} %collective-permute-done.2.refs_3_), channel_id=1, source_target_pairs={{0,8},{4,20},{8,0},{12,28},{16,24},{20,4},{24,16},{28,12},{1,9},{5... | collective-permute-start | bytes 1572872 | tf_op jit(solution)/shard_map/ppermute | solution.py:53
  10.8 1.5 collective-permute-start.1
  12.4 1.3 constant_dynamic-slice_fusion
  14.6 8.2 %collective-permute-done.6.refs_5_ = bf16[512,512]{1,0:T(8,128)(2,1)S(1)} collective-permute-done((bf16[512,512]{1,0:T(8,128)(2,1)S(1)}, bf16[512,512]{1,0:T(8,128)(2,1)S(1)}, u32[]{:S(2)}, u32[]{:S(2)}) %collective-permute-start.6) | collective-permute-done | bytes 524320 | tf_op jit(solution)/shard_map/ppermute | solution.py:53
  22.8 3.0 %collective-permute-start.5 = (bf16[512,512]{1,0:T(8,128)(2,1)S(1)}, bf16[512,512]{1,0:T(8,128)(2,1)S(1)}, u32[]{:S(2)}, u32[]{:S(2)}) collective-permute-start(bf16[512,512]{1,0:T(8,128)(2,1)S(1)} %collective-permute-done.4.refs_4_), channel_id=1, source_target_pairs={{0,16},{4,12},{8,24},{12,4},{16,0},{20,28},{24,8},{28,20},{1,17},{... | collective-permute-start | bytes 1572872 | tf_op jit(solution)/shard_map/ppermute | solution.py:53
  25.9 3.3 %project_first.1.refs_6_ = f32[2,512,512]{2,1,0:T(8,128)S(1)} custom-call(bf16[512,4096]{1,0:T(8,128)(2,1)S(1)} %copy-done.3, bf16[512,4096]{1,0:T(8,128)(2,1)} %collective-permute-done.refs_1_, bf16[512,512]{1,0:T(8,128)(2,1)S(1)} %get-tuple-element.42.refs_2_, bf16[512,512]{1,0:T(8,128)(2,1)S(1)} %collective-permute-done.2.refs_3_, ...), custom_call_target="tpu_custom_call" | custom-call | tf_op jit(solution)/shard_map/project_first/pallas_call | solution.py:204
  29.3 5.1 %collective-permute-done.5.refs_4_ = bf16[512,512]{1,0:T(8,128)(2,1)S(1)} collective-permute-done((bf16[512,512]{1,0:T(8,128)(2,1)S(1)}, bf16[512,512]{1,0:T(8,128)(2,1)S(1)}, u32[]{:S(2)}, u32[]{:S(2)}) %collective-permute-start.5) | collective-permute-done | bytes 524320 | tf_op jit(solution)/shard_map/ppermute | solution.py:53
  34.3 5.6 %collective-permute-done.7.refs_5_ = bf16[512,512]{1,0:T(8,128)(2,1)S(1)} collective-permute-done((bf16[512,512]{1,0:T(8,128)(2,1)S(1)}, bf16[512,512]{1,0:T(8,128)(2,1)S(1)}, u32[]{:S(2)}, u32[]{:S(2)}) %collective-permute-start.7) | collective-permute-done | bytes 524320 | tf_op jit(solution)/shard_map/ppermute | solution.py:53
  40.0 3.4 %project_last.1 = bf16[2,512,512]{2,1,0:T(8,128)(2,1)S(1)} custom-call(bf16[512,4096]{1,0:T(8,128)(2,1)S(1)} %copy-done.3, bf16[512,4096]{1,0:T(8,128)(2,1)} %collective-permute-done.refs_1_, bf16[512,512]{1,0:T(8,128)(2,1)S(1)} %collective-permute-done.1.refs_2_, bf16[512,512]{1,0:T(8,128)(2,1)S(1)} %collective-permute-done.3.refs_3_, ...), custom_call_target="tpu_custom_call" | custom-call | tf_op jit(solution)/shard_map/project_last/pallas_call | solution.py:204
  44.1 1.8 collective-permute-start.9
  45.9 7.4 %collective-permute-done.9.refs_1_ = bf16[2,4,64,512]{3,2,1,0:T(8,128)(2,1)S(1)} collective-permute-done((bf16[2,4,64,512]{3,2,1,0:T(8,128)(2,1)S(1)}, bf16[2,4,64,512]{3,2,1,0:T(8,128)(2,1)S(1)}, u32[]{:S(2)}, u32[]{:S(2)}) %collective-permute-start.9) | collective-permute-done | bytes 524320 | tf_op jit(solution)/shard_map/ppermute | solution.py:53
  53.5 1.6 collective-permute-start.10
  55.9 1.6 collective-permute-start.14
  57.5 4.7 %collective-permute-done.10.refs_1_ = bf16[1,4,64,512]{3,2,1,0:T(8,128)(2,1)S(1)} collective-permute-done((bf16[1,4,64,512]{3,2,1,0:T(8,128)(2,1)S(1)}, bf16[1,4,64,512]{3,2,1,0:T(8,128)(2,1)S(1)}, u32[]{:S(2)}, u32[]{:S(2)}) %collective-permute-start.10) | collective-permute-done | bytes 262176 | tf_op jit(solution)/shard_map/ppermute | solution.py:53
  62.2 2.1 %collective-permute-start.11 = (bf16[64,512]{1,0:T(8,128)(2,1)S(1)}, bf16[64,512]{1,0:T(8,128)(2,1)S(1)}, u32[]{:S(2)}, u32[]{:S(2)}) collective-permute-start(bf16[64,512]{1,0:T(8,128)(2,1)S(1)} %get-tuple-element.57), channel_id=1, source_target_pairs={{0,1},{1,2},{2,3},{3,0},{4,5},{5,6},{6,7},{7,4},{8,9},{9,10},{10,1... | collective-permute-start | bytes 196616 | tf_op jit(solution)/shard_map/ppermute | solution.py:67
  64.4 2.6 %collective-permute-start.12 = (bf16[64,512]{1,0:T(8,128)(2,1)S(1)}, bf16[64,512]{1,0:T(8,128)(2,1)S(1)}, u32[]{:S(2)}, u32[]{:S(2)}) collective-permute-start(bf16[64,512]{1,0:T(8,128)(2,1)S(1)} %get-tuple-element.56), channel_id=1, source_target_pairs={{0,2},{1,3},{2,0},{3,1},{4,6},{5,7},{6,4},{7,5},{8,10},{9,11},{10,... | collective-permute-start | bytes 196616 | tf_op jit(solution)/shard_map/ppermute | solution.py:67
  67.0 1.3 collective-permute-start.13
  69.5 1.7 collective-permute-done.13.refs_3_
  71.2 1.1 collective-permute-start.15
  72.3 2.1 %collective-permute-start.16 = (bf16[4,64,512]{2,1,0:T(8,128)(2,1)S(1)}, bf16[4,64,512]{2,1,0:T(8,128)(2,1)S(1)}, u32[]{:S(2)}, u32[]{:S(2)}) collective-permute-start(bf16[4,64,512]{2,1,0:T(8,128)(2,1)S(1)} %stack_planes.4.refs_2_.refs_0_), channel_id=1, source_target_pairs={{0,16},{4,12},{8,24},{12,4},{16,0},{20,28},{24,8},{28,20},{1,17},{... | collective-permute-start | bytes 786440 | tf_op jit(solution)/shard_map/ppermute | solution.py:53
  75.4 4.3 %collective-permute-done.15.refs_1_ = bf16[4,64,512]{2,1,0:T(8,128)(2,1)S(1)} collective-permute-done((bf16[4,64,512]{2,1,0:T(8,128)(2,1)S(1)}, bf16[4,64,512]{2,1,0:T(8,128)(2,1)S(1)}, u32[]{:S(2)}, u32[]{:S(2)}) %collective-permute-start.15) | collective-permute-done | bytes 262176 | tf_op jit(solution)/shard_map/ppermute | solution.py:53
  79.8 1.4 collective-permute-start.17
  81.2 1.7 collective-permute-start.23
  82.9 1.7 collective-permute-start.24
  84.6 2.2 %collective-permute-start.25 = (bf16[64,512]{1,0:T(8,128)(2,1)S(1)}, bf16[64,512]{1,0:T(8,128)(2,1)S(1)}, u32[]{:S(2)}, u32[]{:S(2)}) collective-permute-start(bf16[64,512]{1,0:T(8,128)(2,1)S(1)} %get-tuple-element.51), channel_id=1, source_target_pairs={{0,3},{1,0},{2,1},{3,2},{4,7},{5,4},{6,5},{7,6},{8,11},{9,8},{10,9... | collective-permute-start | bytes 196616 | tf_op jit(solution)/shard_map/ppermute | solution.py:67
  88.9 1.4 collective-permute-start.26
  90.5 4.8 %collective-permute-done.26.refs_10_.refs_1_ = bf16[4,64,512]{2,1,0:T(8,128)(2,1)S(1)} collective-permute-done((bf16[4,64,512]{2,1,0:T(8,128)(2,1)S(1)}, bf16[4,64,512]{2,1,0:T(8,128)(2,1)S(1)}, u32[]{:S(2)}, u32[]{:S(2)}) %collective-permute-start.26) | collective-permute-done | bytes 262176 | tf_op jit(solution)/shard_map/ppermute | solution.py:53
  95.4 3.4 %copy-done.1 = bf16[1,4096,1024]{2,1,0:T(8,128)(2,1)S(1)} copy-done((bf16[1,4096,1024]{2,1,0:T(8,128)(2,1)S(1)}, bf16[1,4096,1024]{2,1,0:T(8,128)(2,1)}, u32[]{:S(2)}) %copy-start.1) | copy-done | bytes 8388632
  98.7 3.4 %copy-done.2 = bf16[1,4096,1024]{2,1,0:T(8,128)(2,1)S(1)} copy-done((bf16[1,4096,1024]{2,1,0:T(8,128)(2,1)S(1)}, bf16[1,4096,1024]{2,1,0:T(8,128)(2,1)}, u32[]{:S(2)}) %copy-start.2) | copy-done | bytes 8388632
  102.1 8.5 %expert_hidden.2.refs_1_.refs_4_ = bf16[256,1024]{1,0:T(8,128)(2,1)S(1)} custom-call(bf16[4,64,512]{2,1,0:T(8,128)(2,1)S(1)} %stack_planes.4.refs_2_.refs_0_, bf16[4,64,512]{2,1,0:T(8,128)(2,1)S(1)} %collective-permute-done.15.refs_1_, bf16[4,64,512]{2,1,0:T(8,128)(2,1)S(1)} %collective-permute-done.16.refs_2_, ...), custom_call_target="tpu_custom_call" | custom-call | tf_op jit(solution)/shard_map/expert_hidden/pallas_call | solution.py:333
  110.7 3.4 %copy-done = bf16[1,1024,4096]{2,1,0:T(8,128)(2,1)S(1)} copy-done((bf16[1,1024,4096]{2,1,0:T(8,128)(2,1)S(1)}, bf16[1,1024,4096]{2,1,0:T(8,128)(2,1)}, u32[]{:S(2)}) %copy-start) | copy-done | bytes 8388632
  114.1 2.9 %expert_down.4.refs_4_ = bf16[4,4,64,512]{3,2,1,0:T(8,128)(2,1)S(1)} custom-call(s32[4]{0:T(128)S(1)} %copy-done.5, bf16[256,1024]{1,0:T(8,128)(2,1)S(1)} %expert_hidden.2.refs_1_.refs_4_, bf16[1024,4096]{1,0:T(8,128)(2,1)S(1)} %bitcast.39, f32[512,1]{1,0:T(8,128)S(1)} %copy.11.refs_3_, bf16[256,1024]{1,0:T(8,128)(2,1)S(1)} %expert_hidden.2.refs_1_.refs_4_), custom_call_target="tpu_custom_call" | custom-call | tf_op jit(solution)/shard_map/expert_down/pallas_call | solution.py:379
  117.8 1.4 collective-permute-start.30
  119.7 3.8 %collective-permute-done.29.refs_2_ = bf16[4,64,512]{2,1,0:T(8,128)(2,1)S(1)} collective-permute-done((bf16[4,64,512]{2,1,0:T(8,128)(2,1)S(1)}, bf16[4,64,512]{2,1,0:T(8,128)(2,1)S(1)}, u32[]{:S(2)}, u32[]{:S(2)}) %collective-permute-start.29) | collective-permute-done | bytes 262176 | tf_op jit(solution)/shard_map/ppermute | solution.py:53
  123.5 2.8 %collective-permute-done.30.refs_3_ = bf16[4,64,512]{2,1,0:T(8,128)(2,1)S(1)} collective-permute-done((bf16[4,64,512]{2,1,0:T(8,128)(2,1)S(1)}, bf16[4,64,512]{2,1,0:T(8,128)(2,1)S(1)}, u32[]{:S(2)}, u32[]{:S(2)}) %collective-permute-start.30) | collective-permute-done | bytes 262176 | tf_op jit(solution)/shard_map/ppermute | solution.py:53
  126.4 2.9 %expert_down.5.refs_0_.refs_2_ = bf16[4,4,64,512]{3,2,1,0:T(8,128)(2,1)S(1)} custom-call(s32[4]{0:T(128)S(1)} %copy-done.5, bf16[256,1024]{1,0:T(8,128)(2,1)S(1)} %expert_hidden.2.refs_1_.refs_4_, bf16[1024,4096]{1,0:T(8,128)(2,1)S(1)} %bitcast.40, f32[512,1]{1,0:T(8,128)S(1)} %copy.11.refs_3_, bf16[4,4,64,512]{3,2,1,0:T(8,128)(2,1)S(1)} %expert_down.4.refs_4_), custom_call_target="tpu_custom_call" | custom-call | tf_op jit(solution)/shard_map/expert_down/pallas_call | solution.py:379
  129.7 7.6 %expert_hidden.3.refs_1_.refs_4_ = bf16[256,1024]{1,0:T(8,128)(2,1)S(1)} custom-call(bf16[4,64,512]{2,1,0:T(8,128)(2,1)S(1)} %stack_planes.5.refs_0_, bf16[4,64,512]{2,1,0:T(8,128)(2,1)S(1)} %collective-permute-done.26.refs_10_.refs_1_, bf16[4,64,512]{2,1,0:T(8,128)(2,1)S(1)} %collective-permute-done.29.refs_2_, ...), custom_call_target="tpu_custom_call" | custom-call | tf_op jit(solution)/shard_map/expert_hidden/pallas_call | solution.py:333
  137.3 3.0 %expert_down.6.refs_2_ = bf16[4,4,64,512]{3,2,1,0:T(8,128)(2,1)S(1)} custom-call(s32[4]{0:T(128)S(1)} %copy-done.5, bf16[256,1024]{1,0:T(8,128)(2,1)S(1)} %expert_hidden.3.refs_1_.refs_4_, bf16[1024,4096]{1,0:T(8,128)(2,1)S(1)} %bitcast.43, f32[512,1]{1,0:T(8,128)S(1)} %copy.11.refs_3_, bf16[256,1024]{1,0:T(8,128)(2,1)S(1)} %expert_hidden.3.refs_1_.refs_4_), custom_call_target="tpu_custom_call" | custom-call | tf_op jit(solution)/shard_map/expert_down/pallas_call | solution.py:379
  141.6 8.5 %collective-permute-done.28.refs_1_ = bf16[2,4,64,512]{3,2,1,0:T(8,128)(2,1)S(1)} collective-permute-done((bf16[2,4,64,512]{3,2,1,0:T(8,128)(2,1)S(1)}, bf16[2,4,64,512]{3,2,1,0:T(8,128)(2,1)S(1)}, u32[]{:S(2)}, u32[]{:S(2)}) %collective-permute-start.28) | collective-permute-done | bytes 524320 | tf_op jit(solution)/shard_map/ppermute | solution.py:53
  150.2 3.2 %expert_down.7.refs_0_.refs_2_ = bf16[4,4,64,512]{3,2,1,0:T(8,128)(2,1)S(1)} custom-call(s32[4]{0:T(128)S(1)} %copy-done.5, bf16[256,1024]{1,0:T(8,128)(2,1)S(1)} %expert_hidden.3.refs_1_.refs_4_, bf16[1024,4096]{1,0:T(8,128)(2,1)S(1)} %bitcast.44, f32[512,1]{1,0:T(8,128)S(1)} %copy.11.refs_3_, bf16[1,4,64,512]{3,2,1,0:T(8,128)(2,1)S(1)} %get-tuple-element.31.refs_4_.refs_0_), custom_call_target="tpu_custom_call" | custom-call | tf_op jit(solution)/shard_map/expert_down/pallas_call | solution.py:379
  154.5 1.3 collective-permute-start.35
  155.8 7.9 %collective-permute-done.35.refs_1_ = bf16[1,4,64,512]{3,2,1,0:T(8,128)(2,1)S(1)} collective-permute-done((bf16[1,4,64,512]{3,2,1,0:T(8,128)(2,1)S(1)}, bf16[1,4,64,512]{3,2,1,0:T(8,128)(2,1)S(1)}, u32[]{:S(2)}, u32[]{:S(2)}) %collective-permute-start.35) | collective-permute-done | bytes 262176 | tf_op jit(solution)/shard_map/ppermute | solution.py:53
  163.8 1.4 collective-permute-done.40.refs_1_
  166.0 1.5 collective-permute-start.37
  167.5 3.1 %collective-permute-start.38 = (bf16[64,512]{1,0:T(8,128)(2,1)S(1)}, bf16[64,512]{1,0:T(8,128)(2,1)S(1)}, u32[]{:S(2)}, u32[]{:S(2)}) collective-permute-start(bf16[64,512]{1,0:T(8,128)(2,1)S(1)} %get-tuple-element.48), channel_id=1, source_target_pairs={{0,2},{1,3},{2,0},{3,1},{4,6},{5,7},{6,4},{7,5},{8,10},{9,11},{10,... | collective-permute-start | bytes 196616 | tf_op jit(solution)/shard_map/ppermute | solution.py:67
  170.6 1.8 collective-permute-done.37.refs_1_
  172.5 1.7 collective-permute-done.38.refs_2_
  175.7 2.5 %collective-permute-start.46 = (bf16[64,512]{1,0:T(8,128)(2,1)S(1)}, bf16[64,512]{1,0:T(8,128)(2,1)S(1)}, u32[]{:S(2)}, u32[]{:S(2)}) collective-permute-start(bf16[64,512]{1,0:T(8,128)(2,1)S(1)} %get-tuple-element.44), channel_id=1, source_target_pairs={{0,2},{1,3},{2,0},{3,1},{4,6},{5,7},{6,4},{7,5},{8,10},{9,11},{10,... | collective-permute-start | bytes 196616 | tf_op jit(solution)/shard_map/ppermute | solution.py:67
  179.0 1.5 collective-permute-start.41
  181.3 1.1 collective-permute-done.46.refs_2_
  182.7 1.6 collective-permute-start.48
  184.3 1.6 collective-permute-start.42
  186.3 1.6 collective-permute-start.49
  187.9 4.1 %collective-permute-done.48.refs_7_ = bf16[4,64,512]{2,1,0:T(8,128)(2,1)S(1)} collective-permute-done((bf16[4,64,512]{2,1,0:T(8,128)(2,1)S(1)}, bf16[4,64,512]{2,1,0:T(8,128)(2,1)S(1)}, u32[]{:S(2)}, u32[]{:S(2)}) %collective-permute-start.48) | collective-permute-done | bytes 262176 | tf_op jit(solution)/shard_map/ppermute | solution.py:53
  192.0 1.7 collective-permute-start.50
  193.6 2.6 %collective-permute-done.49.refs_8_ = bf16[4,64,512]{2,1,0:T(8,128)(2,1)S(1)} collective-permute-done((bf16[4,64,512]{2,1,0:T(8,128)(2,1)S(1)}, bf16[4,64,512]{2,1,0:T(8,128)(2,1)S(1)}, u32[]{:S(2)}, u32[]{:S(2)}) %collective-permute-start.49) | collective-permute-done | bytes 262176 | tf_op jit(solution)/shard_map/ppermute | solution.py:53
  196.3 2.8 %collective-permute-done.50.refs_9_ = bf16[4,64,512]{2,1,0:T(8,128)(2,1)S(1)} collective-permute-done((bf16[4,64,512]{2,1,0:T(8,128)(2,1)S(1)}, bf16[4,64,512]{2,1,0:T(8,128)(2,1)S(1)}, u32[]{:S(2)}, u32[]{:S(2)}) %collective-permute-start.50) | collective-permute-done | bytes 262176 | tf_op jit(solution)/shard_map/ppermute | solution.py:53
  199.1 1.5 add_expert_rows.1
  200.6 1.2 collective-permute-start.51
  201.8 1.5 collective-permute-done.51
  203.4 1.3 maximum_select_fusion
  (103 shorter events, 16.7 us)
Async XLA Ops:
  0.0 25.9 %collective-permute-start = (bf16[512,4096]{1,0:T(8,128)(2,1)}, bf16[512,4096]{1,0:T(8,128)(2,1)}, u32[]{:S(2)}, u32[]{:S(2)}) collective-permute-start(bf16[512,4096]{1,0:T(8,128)(2,1)} %refs_0_.10), channel_id=1, source_target_pairs={{0,4},{4,0},{8,12},{12,8},{16,20},{20,16},{24,28},{28,24},{1,5},{5... | collective-permute-start | bytes 12582920 | tf_op jit(solution)/shard_map/ppermute | solution.py:464
  0.5 25.4 %copy-start.3 = (bf16[512,4096]{1,0:T(8,128)(2,1)S(1)}, bf16[512,4096]{1,0:T(8,128)(2,1)}, u32[]{:S(2)}) copy-start(bf16[512,4096]{1,0:T(8,128)(2,1)} %refs_0_.10) | copy-start | bytes 12582916
  1.9 6.1 %collective-permute-start.2 = (bf16[512,512]{1,0:T(8,128)(2,1)S(1)}, bf16[512,512]{1,0:T(8,128)(2,1)S(1)}, u32[]{:S(2)}, u32[]{:S(2)}) collective-permute-start(bf16[512,512]{1,0:T(8,128)(2,1)S(1)} %get-tuple-element.41), channel_id=1, source_target_pairs={{0,4},{4,0},{8,12},{12,8},{16,20},{20,16},{24,28},{28,24},{1,5},{5... | collective-permute-start | bytes 1572872 | tf_op jit(solution)/shard_map/ppermute | solution.py:464
  2.0 11.7 %collective-permute-start.4 = (bf16[512,512]{1,0:T(8,128)(2,1)S(1)}, bf16[512,512]{1,0:T(8,128)(2,1)S(1)}, u32[]{:S(2)}, u32[]{:S(2)}) collective-permute-start(bf16[512,512]{1,0:T(8,128)(2,1)S(1)} %get-tuple-element.42.refs_2_), channel_id=1, source_target_pairs={{0,8},{4,20},{8,0},{12,28},{16,24},{20,4},{24,16},{28,12},{1,9},{5... | collective-permute-start | bytes 1572872 | tf_op jit(solution)/shard_map/ppermute | solution.py:53
  8.0 14.9 %collective-permute-start.6 = (bf16[512,512]{1,0:T(8,128)(2,1)S(1)}, bf16[512,512]{1,0:T(8,128)(2,1)S(1)}, u32[]{:S(2)}, u32[]{:S(2)}) collective-permute-start(bf16[512,512]{1,0:T(8,128)(2,1)S(1)} %collective-permute-done.2.refs_3_), channel_id=1, source_target_pairs={{0,8},{4,20},{8,0},{12,28},{16,24},{20,4},{24,16},{28,12},{1,9},{5... | collective-permute-start | bytes 1572872 | tf_op jit(solution)/shard_map/ppermute | solution.py:53
  10.8 18.4 %collective-permute-start.1 = (bf16[512,512]{1,0:T(8,128)(2,1)S(1)}, bf16[512,512]{1,0:T(8,128)(2,1)S(1)}, u32[]{:S(2)}, u32[]{:S(2)}) collective-permute-start(bf16[512,512]{1,0:T(8,128)(2,1)S(1)} %get-tuple-element.42.refs_2_), channel_id=1, source_target_pairs={{0,16},{4,12},{8,24},{12,4},{16,0},{20,28},{24,8},{28,20},{1,17},{... | collective-permute-start | bytes 1572872 | tf_op jit(solution)/shard_map/ppermute | solution.py:53
  13.7 15.6 %collective-permute-start.8 = (bf16[512,512]{1,0:T(8,128)(2,1)S(1)}, bf16[512,512]{1,0:T(8,128)(2,1)S(1)}, u32[]{:S(2)}, u32[]{:S(2)}) collective-permute-start(bf16[512,512]{1,0:T(8,128)(2,1)S(1)} %get-tuple-element.39), channel_id=1, source_target_pairs={{0,4},{4,0},{8,12},{12,8},{16,20},{20,16},{24,28},{28,24},{1,5},{5... | collective-permute-start | bytes 1572872 | tf_op jit(solution)/shard_map/ppermute | solution.py:464
  13.7 20.6 %collective-permute-start.3 = (bf16[512,512]{1,0:T(8,128)(2,1)S(1)}, bf16[512,512]{1,0:T(8,128)(2,1)S(1)}, u32[]{:S(2)}, u32[]{:S(2)}) collective-permute-start(bf16[512,512]{1,0:T(8,128)(2,1)S(1)} %collective-permute-done.2.refs_3_), channel_id=1, source_target_pairs={{0,16},{4,12},{8,24},{12,4},{16,0},{20,28},{24,8},{28,20},{1,17},{... | collective-permute-start | bytes 1572872 | tf_op jit(solution)/shard_map/ppermute | solution.py:53
  22.8 11.5 %collective-permute-start.5 = (bf16[512,512]{1,0:T(8,128)(2,1)S(1)}, bf16[512,512]{1,0:T(8,128)(2,1)S(1)}, u32[]{:S(2)}, u32[]{:S(2)}) collective-permute-start(bf16[512,512]{1,0:T(8,128)(2,1)S(1)} %collective-permute-done.4.refs_4_), channel_id=1, source_target_pairs={{0,16},{4,12},{8,24},{12,4},{16,0},{20,28},{24,8},{28,20},{1,17},{... | collective-permute-start | bytes 1572872 | tf_op jit(solution)/shard_map/ppermute | solution.py:53
  25.9 14.1 %collective-permute-start.7 = (bf16[512,512]{1,0:T(8,128)(2,1)S(1)}, bf16[512,512]{1,0:T(8,128)(2,1)S(1)}, u32[]{:S(2)}, u32[]{:S(2)}) collective-permute-start(bf16[512,512]{1,0:T(8,128)(2,1)S(1)} %collective-permute-done.6.refs_5_), channel_id=1, source_target_pairs={{0,16},{4,12},{8,24},{12,4},{16,0},{20,28},{24,8},{28,20},{1,17},{... | collective-permute-start | bytes 1572872 | tf_op jit(solution)/shard_map/ppermute | solution.py:53
  44.1 9.2 %collective-permute-start.9 = (bf16[2,4,64,512]{3,2,1,0:T(8,128)(2,1)S(1)}, bf16[2,4,64,512]{3,2,1,0:T(8,128)(2,1)S(1)}, u32[]{:S(2)}, u32[]{:S(2)}) collective-permute-start(bf16[2,4,64,512]{3,2,1,0:T(8,128)(2,1)S(1)} %get-tuple-element.22), channel_id=1, source_target_pairs={{0,16},{4,12},{8,24},{12,4},{16,0},{20,28},{24,8},{28,20},{1,17},{... | collective-permute-start | bytes 1572872 | tf_op jit(solution)/shard_map/ppermute | solution.py:53
  53.5 8.6 %collective-permute-start.10 = (bf16[1,4,64,512]{3,2,1,0:T(8,128)(2,1)S(1)}, bf16[1,4,64,512]{3,2,1,0:T(8,128)(2,1)S(1)}, u32[]{:S(2)}, u32[]{:S(2)}) collective-permute-start(bf16[1,4,64,512]{3,2,1,0:T(8,128)(2,1)S(1)} %get-tuple-element.24), channel_id=1, source_target_pairs={{0,8},{4,20},{8,0},{12,28},{16,24},{20,4},{24,16},{28,12},{1,9},{5... | collective-permute-start | bytes 786440 | tf_op jit(solution)/shard_map/ppermute | solution.py:53
  55.9 12.4 %collective-permute-start.14 = (bf16[2,4,64,512]{3,2,1,0:T(8,128)(2,1)S(1)}, bf16[2,4,64,512]{3,2,1,0:T(8,128)(2,1)S(1)}, u32[]{:S(2)}, u32[]{:S(2)}) collective-permute-start(bf16[2,4,64,512]{3,2,1,0:T(8,128)(2,1)S(1)} %get-tuple-element.26), channel_id=1, source_target_pairs={{0,16},{4,12},{8,24},{12,4},{16,0},{20,28},{24,8},{28,20},{1,17},{... | collective-permute-start | bytes 1572872 | tf_op jit(solution)/shard_map/ppermute | solution.py:53
  62.2 7.2 %collective-permute-start.11 = (bf16[64,512]{1,0:T(8,128)(2,1)S(1)}, bf16[64,512]{1,0:T(8,128)(2,1)S(1)}, u32[]{:S(2)}, u32[]{:S(2)}) collective-permute-start(bf16[64,512]{1,0:T(8,128)(2,1)S(1)} %get-tuple-element.57), channel_id=1, source_target_pairs={{0,1},{1,2},{2,3},{3,0},{4,5},{5,6},{6,7},{7,4},{8,9},{9,10},{10,1... | collective-permute-start | bytes 196616 | tf_op jit(solution)/shard_map/ppermute | solution.py:67
  64.4 5.2 %collective-permute-start.12 = (bf16[64,512]{1,0:T(8,128)(2,1)S(1)}, bf16[64,512]{1,0:T(8,128)(2,1)S(1)}, u32[]{:S(2)}, u32[]{:S(2)}) collective-permute-start(bf16[64,512]{1,0:T(8,128)(2,1)S(1)} %get-tuple-element.56), channel_id=1, source_target_pairs={{0,2},{1,3},{2,0},{3,1},{4,6},{5,7},{6,4},{7,5},{8,10},{9,11},{10,... | collective-permute-start | bytes 196616 | tf_op jit(solution)/shard_map/ppermute | solution.py:67
  66.9 23.4 %copy-start.6 = (f32[1,512]{1,0:T(1,128)S(1)}, f32[1,512]{1,0:T(1,128)}, u32[]{:S(2)}) copy-start(f32[1,512]{1,0:T(1,128)} %param.15) | copy-start | bytes 6148
  67.0 4.3 %collective-permute-start.13 = (bf16[64,512]{1,0:T(8,128)(2,1)S(1)}, bf16[64,512]{1,0:T(8,128)(2,1)S(1)}, u32[]{:S(2)}, u32[]{:S(2)}) collective-permute-start(bf16[64,512]{1,0:T(8,128)(2,1)S(1)} %get-tuple-element.55), channel_id=1, source_target_pairs={{0,3},{1,0},{2,1},{3,2},{4,7},{5,4},{6,5},{7,6},{8,11},{9,8},{10,9... | collective-permute-start | bytes 196616 | tf_op jit(solution)/shard_map/ppermute | solution.py:67
  68.4 6.9 %collective-permute-start.22 = (bf16[1,4,64,512]{3,2,1,0:T(8,128)(2,1)S(1)}, bf16[1,4,64,512]{3,2,1,0:T(8,128)(2,1)S(1)}, u32[]{:S(2)}, u32[]{:S(2)}) collective-permute-start(bf16[1,4,64,512]{3,2,1,0:T(8,128)(2,1)S(1)} %get-tuple-element.28), channel_id=1, source_target_pairs={{0,8},{4,20},{8,0},{12,28},{16,24},{20,4},{24,16},{28,12},{1,9},{5... | collective-permute-start | bytes 786440 | tf_op jit(solution)/shard_map/ppermute | solution.py:53
  71.2 8.5 %collective-permute-start.15 = (bf16[4,64,512]{2,1,0:T(8,128)(2,1)S(1)}, bf16[4,64,512]{2,1,0:T(8,128)(2,1)S(1)}, u32[]{:S(2)}, u32[]{:S(2)}) collective-permute-start(bf16[4,64,512]{2,1,0:T(8,128)(2,1)S(1)} %stack_planes.4.refs_2_.refs_0_), channel_id=1, source_target_pairs={{0,8},{4,20},{8,0},{12,28},{16,24},{20,4},{24,16},{28,12},{1,9},{5... | collective-permute-start | bytes 786440 | tf_op jit(solution)/shard_map/ppermute | solution.py:53
  72.3 14.5 %collective-permute-start.16 = (bf16[4,64,512]{2,1,0:T(8,128)(2,1)S(1)}, bf16[4,64,512]{2,1,0:T(8,128)(2,1)S(1)}, u32[]{:S(2)}, u32[]{:S(2)}) collective-permute-start(bf16[4,64,512]{2,1,0:T(8,128)(2,1)S(1)} %stack_planes.4.refs_2_.refs_0_), channel_id=1, source_target_pairs={{0,16},{4,12},{8,24},{12,4},{16,0},{20,28},{24,8},{28,20},{1,17},{... | collective-permute-start | bytes 786440 | tf_op jit(solution)/shard_map/ppermute | solution.py:53
  79.8 10.6 %collective-permute-start.17 = (bf16[4,64,512]{2,1,0:T(8,128)(2,1)S(1)}, bf16[4,64,512]{2,1,0:T(8,128)(2,1)S(1)}, u32[]{:S(2)}, u32[]{:S(2)}) collective-permute-start(bf16[4,64,512]{2,1,0:T(8,128)(2,1)S(1)} %collective-permute-done.15.refs_1_), channel_id=1, source_target_pairs={{0,16},{4,12},{8,24},{12,4},{16,0},{20,28},{24,8},{28,20},{1,17},{... | collective-permute-start | bytes 786440 | tf_op jit(solution)/shard_map/ppermute | solution.py:53
  81.2 6.1 %collective-permute-start.23 = (bf16[64,512]{1,0:T(8,128)(2,1)S(1)}, bf16[64,512]{1,0:T(8,128)(2,1)S(1)}, u32[]{:S(2)}, u32[]{:S(2)}) collective-permute-start(bf16[64,512]{1,0:T(8,128)(2,1)S(1)} %get-tuple-element.53), channel_id=1, source_target_pairs={{0,1},{1,2},{2,3},{3,0},{4,5},{5,6},{6,7},{7,4},{8,9},{9,10},{10,1... | collective-permute-start | bytes 196616 | tf_op jit(solution)/shard_map/ppermute | solution.py:67
  82.9 5.2 %collective-permute-start.24 = (bf16[64,512]{1,0:T(8,128)(2,1)S(1)}, bf16[64,512]{1,0:T(8,128)(2,1)S(1)}, u32[]{:S(2)}, u32[]{:S(2)}) collective-permute-start(bf16[64,512]{1,0:T(8,128)(2,1)S(1)} %get-tuple-element.52), channel_id=1, source_target_pairs={{0,2},{1,3},{2,0},{3,1},{4,6},{5,7},{6,4},{7,5},{8,10},{9,11},{10,... | collective-permute-start | bytes 196616 | tf_op jit(solution)/shard_map/ppermute | solution.py:67
  84.6 4.3 %collective-permute-start.25 = (bf16[64,512]{1,0:T(8,128)(2,1)S(1)}, bf16[64,512]{1,0:T(8,128)(2,1)S(1)}, u32[]{:S(2)}, u32[]{:S(2)}) collective-permute-start(bf16[64,512]{1,0:T(8,128)(2,1)S(1)} %get-tuple-element.51), channel_id=1, source_target_pairs={{0,3},{1,0},{2,1},{3,2},{4,7},{5,4},{6,5},{7,6},{8,11},{9,8},{10,9... | collective-permute-start | bytes 196616 | tf_op jit(solution)/shard_map/ppermute | solution.py:67
  86.8 3.7 %collective-permute-start.18 = (bf16[4,64,512]{2,1,0:T(8,128)(2,1)S(1)}, bf16[4,64,512]{2,1,0:T(8,128)(2,1)S(1)}, u32[]{:S(2)}, u32[]{:S(2)}) collective-permute-start(bf16[4,64,512]{2,1,0:T(8,128)(2,1)S(1)} %stack_planes.4.refs_2_.refs_0_), channel_id=1, source_target_pairs={{0,4},{4,0},{8,12},{12,8},{16,20},{20,16},{24,28},{28,24},{1,5},{5... | collective-permute-start | bytes 786440 | tf_op jit(solution)/shard_map/ppermute | solution.py:464
  87.3 3.2 %collective-permute-start.20 = (bf16[4,64,512]{2,1,0:T(8,128)(2,1)S(1)}, bf16[4,64,512]{2,1,0:T(8,128)(2,1)S(1)}, u32[]{:S(2)}, u32[]{:S(2)}) collective-permute-start(bf16[4,64,512]{2,1,0:T(8,128)(2,1)S(1)} %collective-permute-done.15.refs_1_), channel_id=1, source_target_pairs={{0,4},{4,0},{8,12},{12,8},{16,20},{20,16},{24,28},{28,24},{1,5},{5... | collective-permute-start | bytes 786440 | tf_op jit(solution)/shard_map/ppermute | solution.py:464
  88.0 2.5 %collective-permute-start.19 = (bf16[4,64,512]{2,1,0:T(8,128)(2,1)S(1)}, bf16[4,64,512]{2,1,0:T(8,128)(2,1)}, u32[]{:S(2)}, u32[]{:S(2)}) collective-permute-start(bf16[4,64,512]{2,1,0:T(8,128)(2,1)S(1)} %collective-permute-done.16.refs_2_), channel_id=1, source_target_pairs={{0,4},{4,0},{8,12},{12,8},{16,20},{20,16},{24,28},{28,24},{1,5},{5... | collective-permute-start | bytes 786440 | tf_op jit(solution)/shard_map/ppermute | solution.py:464
  88.9 6.4 %collective-permute-start.26 = (bf16[4,64,512]{2,1,0:T(8,128)(2,1)S(1)}, bf16[4,64,512]{2,1,0:T(8,128)(2,1)S(1)}, u32[]{:S(2)}, u32[]{:S(2)}) collective-permute-start(bf16[4,64,512]{2,1,0:T(8,128)(2,1)S(1)} %stack_planes.5.refs_0_), channel_id=1, source_target_pairs={{0,8},{4,20},{8,0},{12,28},{16,24},{20,4},{24,16},{28,12},{1,9},{5... | collective-permute-start | bytes 786440 | tf_op jit(solution)/shard_map/ppermute | solution.py:53
  90.4 5.0 %collective-permute-start.21 = (bf16[4,64,512]{2,1,0:T(8,128)(2,1)S(1)}, bf16[4,64,512]{2,1,0:T(8,128)(2,1)}, u32[]{:S(2)}, u32[]{:S(2)}) collective-permute-start(bf16[4,64,512]{2,1,0:T(8,128)(2,1)S(1)} %collective-permute-done.17.refs_3_), channel_id=1, source_target_pairs={{0,4},{4,0},{8,12},{12,8},{16,20},{20,16},{24,28},{28,24},{1,5},{5... | collective-permute-start | bytes 786440 | tf_op jit(solution)/shard_map/ppermute | solution.py:464
  95.3 3.4 %copy-start.1 = (bf16[1,4096,1024]{2,1,0:T(8,128)(2,1)S(1)}, bf16[1,4096,1024]{2,1,0:T(8,128)(2,1)}, u32[]{:S(2)}) copy-start(bf16[1,4096,1024]{2,1,0:T(8,128)(2,1)} %param.12) | copy-start | bytes 25165828
  98.7 3.4 %copy-start.2 = (bf16[1,4096,1024]{2,1,0:T(8,128)(2,1)S(1)}, bf16[1,4096,1024]{2,1,0:T(8,128)(2,1)}, u32[]{:S(2)}) copy-start(bf16[1,4096,1024]{2,1,0:T(8,128)(2,1)} %param.13) | copy-start | bytes 25165828
  102.1 8.5 %copy-start.5 = (s32[4]{0:T(128)S(1)}, s32[4]{0:T(128)}, u32[]{:S(2)}) copy-start(s32[4]{0:T(128)} %refs_0_.16) | copy-start | bytes 52
  110.7 3.4 %copy-start = (bf16[1,1024,4096]{2,1,0:T(8,128)(2,1)S(1)}, bf16[1,1024,4096]{2,1,0:T(8,128)(2,1)}, u32[]{:S(2)}) copy-start(bf16[1,1024,4096]{2,1,0:T(8,128)(2,1)} %param.14) | copy-start | bytes 25165828
  114.0 15.6 %slice-start.2 = ((s8[8388608]{0:T(1024)(128)(4,1)}), s8[4194304]{0:T(1024)(128)(4,1)S(1)}, s32[]{:S(2)}) async-start(s8[8388608]{0:T(1024)(128)(4,1)} %bitcast.46), calls=%async_computation.2 | async-start | bytes 8388608
  114.1 15.6 %slice-start.4 = ((s8[8388608]{0:T(1024)(128)(4,1)}), s8[4194304]{0:T(1024)(128)(4,1)S(1)}, s32[]{:S(2)}) async-start(s8[8388608]{0:T(1024)(128)(4,1)} %bitcast.50), calls=%async_computation.4 | async-start | bytes 8388608
  117.0 12.6 %slice-start.3 = ((s8[8388608]{0:T(1024)(128)(4,1)}), s8[4194304]{0:T(1024)(128)(4,1)S(1)}, s32[]{:S(2)}) async-start(s8[8388608]{0:T(1024)(128)(4,1)} %bitcast.46), calls=%async_computation.3 | async-start | bytes 8388608
  117.0 12.6 %slice-start.5 = ((s8[8388608]{0:T(1024)(128)(4,1)}), s8[4194304]{0:T(1024)(128)(4,1)S(1)}, s32[]{:S(2)}) async-start(s8[8388608]{0:T(1024)(128)(4,1)} %bitcast.50), calls=%async_computation.5 | async-start | bytes 8388608
  117.0 12.3 %collective-permute-start.27 = (bf16[4,4,64,512]{3,2,1,0:T(8,128)(2,1)S(1)}, bf16[4,4,64,512]{3,2,1,0:T(8,128)(2,1)S(1)}, u32[]{:S(2)}, u32[]{:S(2)}) collective-permute-start(bf16[4,4,64,512]{3,2,1,0:T(8,128)(2,1)S(1)} %expert_down.4.refs_4_), channel_id=1, source_target_pairs={{0,4},{4,0},{8,12},{12,8},{16,20},{20,16},{24,28},{28,24},{1,5},{5... | collective-permute-start | bytes 3145736 | tf_op jit(solution)/shard_map/ppermute | solution.py:464
  117.1 6.4 %collective-permute-start.29 = (bf16[4,64,512]{2,1,0:T(8,128)(2,1)S(1)}, bf16[4,64,512]{2,1,0:T(8,128)(2,1)S(1)}, u32[]{:S(2)}, u32[]{:S(2)}) collective-permute-start(bf16[4,64,512]{2,1,0:T(8,128)(2,1)S(1)} %stack_planes.5.refs_0_), channel_id=1, source_target_pairs={{0,16},{4,12},{8,24},{12,4},{16,0},{20,28},{24,8},{28,20},{1,17},{... | collective-permute-start | bytes 786440 | tf_op jit(solution)/shard_map/ppermute | solution.py:53
  117.8 8.5 %collective-permute-start.30 = (bf16[4,64,512]{2,1,0:T(8,128)(2,1)S(1)}, bf16[4,64,512]{2,1,0:T(8,128)(2,1)S(1)}, u32[]{:S(2)}, u32[]{:S(2)}) collective-permute-start(bf16[4,64,512]{2,1,0:T(8,128)(2,1)S(1)} %collective-permute-done.26.refs_10_.refs_1_), channel_id=1, source_target_pairs={{0,16},{4,12},{8,24},{12,4},{16,0},{20,28},{24,8},{28,20},{1,17},{... | collective-permute-start | bytes 786440 | tf_op jit(solution)/shard_map/ppermute | solution.py:53
  119.2 10.4 %collective-permute-start.31 = (bf16[4,64,512]{2,1,0:T(8,128)(2,1)S(1)}, bf16[4,64,512]{2,1,0:T(8,128)(2,1)S(1)}, u32[]{:S(2)}, u32[]{:S(2)}) collective-permute-start(bf16[4,64,512]{2,1,0:T(8,128)(2,1)S(1)} %stack_planes.5.refs_0_), channel_id=1, source_target_pairs={{0,4},{4,0},{8,12},{12,8},{16,20},{20,16},{24,28},{28,24},{1,5},{5... | collective-permute-start | bytes 786440 | tf_op jit(solution)/shard_map/ppermute | solution.py:464
  119.2 10.4 %collective-permute-start.33 = (bf16[4,64,512]{2,1,0:T(8,128)(2,1)S(1)}, bf16[4,64,512]{2,1,0:T(8,128)(2,1)S(1)}, u32[]{:S(2)}, u32[]{:S(2)}) collective-permute-start(bf16[4,64,512]{2,1,0:T(8,128)(2,1)S(1)} %collective-permute-done.26.refs_10_.refs_1_), channel_id=1, source_target_pairs={{0,4},{4,0},{8,12},{12,8},{16,20},{20,16},{24,28},{28,24},{1,5},{5... | collective-permute-start | bytes 786440 | tf_op jit(solution)/shard_map/ppermute | solution.py:464
  123.5 6.0 %collective-permute-start.32 = (bf16[4,64,512]{2,1,0:T(8,128)(2,1)S(1)}, bf16[4,64,512]{2,1,0:T(8,128)(2,1)S(1)}, u32[]{:S(2)}, u32[]{:S(2)}) collective-permute-start(bf16[4,64,512]{2,1,0:T(8,128)(2,1)S(1)} %collective-permute-done.29.refs_2_), channel_id=1, source_target_pairs={{0,4},{4,0},{8,12},{12,8},{16,20},{20,16},{24,28},{28,24},{1,5},{5... | collective-permute-start | bytes 786440 | tf_op jit(solution)/shard_map/ppermute | solution.py:464
  126.4 3.2 %collective-permute-start.34 = (bf16[4,64,512]{2,1,0:T(8,128)(2,1)S(1)}, bf16[4,64,512]{2,1,0:T(8,128)(2,1)S(1)}, u32[]{:S(2)}, u32[]{:S(2)}) collective-permute-start(bf16[4,64,512]{2,1,0:T(8,128)(2,1)S(1)} %collective-permute-done.30.refs_3_), channel_id=1, source_target_pairs={{0,4},{4,0},{8,12},{12,8},{16,20},{20,16},{24,28},{28,24},{1,5},{5... | collective-permute-start | bytes 786440 | tf_op jit(solution)/shard_map/ppermute | solution.py:464
  129.3 8.0 %slice-start = ((s8[8388608]{0:T(1024)(128)(4,1)}), s8[4194304]{0:T(1024)(128)(4,1)S(1)}, s32[]{:S(2)}) async-start(s8[8388608]{0:T(1024)(128)(4,1)} %bitcast.41), calls=%async_computation | async-start | bytes 8388608
  129.7 7.7 %slice-start.1 = ((s8[8388608]{0:T(1024)(128)(4,1)}), s8[4194304]{0:T(1024)(128)(4,1)S(1)}, s32[]{:S(2)}) async-start(s8[8388608]{0:T(1024)(128)(4,1)} %bitcast.41), calls=%async_computation.1 | async-start | bytes 8388608
  140.4 13.1 %collective-permute-start.36 = (bf16[4,4,64,512]{3,2,1,0:T(8,128)(2,1)S(1)}, bf16[4,4,64,512]{3,2,1,0:T(8,128)(2,1)S(1)}, u32[]{:S(2)}, u32[]{:S(2)}) collective-permute-start(bf16[4,4,64,512]{3,2,1,0:T(8,128)(2,1)S(1)} %expert_down.6.refs_2_), channel_id=1, source_target_pairs={{0,4},{4,0},{8,12},{12,8},{16,20},{20,16},{24,28},{28,24},{1,5},{5... | collective-permute-start | bytes 3145736 | tf_op jit(solution)/shard_map/ppermute | solution.py:464
  140.9 9.2 %collective-permute-start.28 = (bf16[2,4,64,512]{3,2,1,0:T(8,128)(2,1)S(1)}, bf16[2,4,64,512]{3,2,1,0:T(8,128)(2,1)S(1)}, u32[]{:S(2)}, u32[]{:S(2)}) collective-permute-start(bf16[2,4,64,512]{3,2,1,0:T(8,128)(2,1)S(1)} %get-tuple-element.30), channel_id=1, source_target_pairs={{0,16},{4,12},{8,24},{12,4},{16,0},{20,28},{24,8},{28,20},{1,17},{... | collective-permute-start | bytes 1572872 | tf_op jit(solution)/shard_map/ppermute | solution.py:53
  153.8 11.4 %collective-permute-start.40 = (bf16[2,4,64,512]{3,2,1,0:T(8,128)(2,1)S(1)}, bf16[2,4,64,512]{3,2,1,0:T(8,128)(2,1)S(1)}, u32[]{:S(2)}, u32[]{:S(2)}) collective-permute-start(bf16[2,4,64,512]{3,2,1,0:T(8,128)(2,1)S(1)} %get-tuple-element.34), channel_id=1, source_target_pairs={{0,16},{4,12},{8,24},{12,4},{16,0},{20,28},{24,8},{28,20},{1,17},{... | collective-permute-start | bytes 1572872 | tf_op jit(solution)/shard_map/ppermute | solution.py:53
  154.5 9.2 %collective-permute-start.35 = (bf16[1,4,64,512]{3,2,1,0:T(8,128)(2,1)S(1)}, bf16[1,4,64,512]{3,2,1,0:T(8,128)(2,1)S(1)}, u32[]{:S(2)}, u32[]{:S(2)}) collective-permute-start(bf16[1,4,64,512]{3,2,1,0:T(8,128)(2,1)S(1)} %get-tuple-element.32), channel_id=1, source_target_pairs={{0,8},{4,20},{8,0},{12,28},{16,24},{20,4},{24,16},{28,12},{1,9},{5... | collective-permute-start | bytes 786440 | tf_op jit(solution)/shard_map/ppermute | solution.py:53
  165.3 9.7 %collective-permute-start.44 = (bf16[1,4,64,512]{3,2,1,0:T(8,128)(2,1)S(1)}, bf16[1,4,64,512]{3,2,1,0:T(8,128)(2,1)S(1)}, u32[]{:S(2)}, u32[]{:S(2)}) collective-permute-start(bf16[1,4,64,512]{3,2,1,0:T(8,128)(2,1)S(1)} %get-tuple-element.36), channel_id=1, source_target_pairs={{0,8},{4,20},{8,0},{12,28},{16,24},{20,4},{24,16},{28,12},{1,9},{5... | collective-permute-start | bytes 786440 | tf_op jit(solution)/shard_map/ppermute | solution.py:53
  166.0 6.5 %collective-permute-start.37 = (bf16[64,512]{1,0:T(8,128)(2,1)S(1)}, bf16[64,512]{1,0:T(8,128)(2,1)S(1)}, u32[]{:S(2)}, u32[]{:S(2)}) collective-permute-start(bf16[64,512]{1,0:T(8,128)(2,1)S(1)} %get-tuple-element.49), channel_id=1, source_target_pairs={{0,1},{1,2},{2,3},{3,0},{4,5},{5,6},{6,7},{7,4},{8,9},{9,10},{10,1... | collective-permute-start | bytes 196616 | tf_op jit(solution)/shard_map/ppermute | solution.py:67
  167.5 6.7 %collective-permute-start.38 = (bf16[64,512]{1,0:T(8,128)(2,1)S(1)}, bf16[64,512]{1,0:T(8,128)(2,1)S(1)}, u32[]{:S(2)}, u32[]{:S(2)}) collective-permute-start(bf16[64,512]{1,0:T(8,128)(2,1)S(1)} %get-tuple-element.48), channel_id=1, source_target_pairs={{0,2},{1,3},{2,0},{3,1},{4,6},{5,7},{6,4},{7,5},{8,10},{9,11},{10,... | collective-permute-start | bytes 196616 | tf_op jit(solution)/shard_map/ppermute | solution.py:67
  170.6 4.3 %collective-permute-start.39 = (bf16[64,512]{1,0:T(8,128)(2,1)S(1)}, bf16[64,512]{1,0:T(8,128)(2,1)S(1)}, u32[]{:S(2)}, u32[]{:S(2)}) collective-permute-start(bf16[64,512]{1,0:T(8,128)(2,1)S(1)} %get-tuple-element.47), channel_id=1, source_target_pairs={{0,3},{1,0},{2,1},{3,2},{4,7},{5,4},{6,5},{7,6},{8,11},{9,8},{10,9... | collective-permute-start | bytes 196616 | tf_op jit(solution)/shard_map/ppermute | solution.py:67
  175.1 6.2 %collective-permute-start.45 = (bf16[64,512]{1,0:T(8,128)(2,1)S(1)}, bf16[64,512]{1,0:T(8,128)(2,1)S(1)}, u32[]{:S(2)}, u32[]{:S(2)}) collective-permute-start(bf16[64,512]{1,0:T(8,128)(2,1)S(1)} %get-tuple-element.45), channel_id=1, source_target_pairs={{0,1},{1,2},{2,3},{3,0},{4,5},{5,6},{6,7},{7,4},{8,9},{9,10},{10,1... | collective-permute-start | bytes 196616 | tf_op jit(solution)/shard_map/ppermute | solution.py:67
  175.7 6.7 %collective-permute-start.46 = (bf16[64,512]{1,0:T(8,128)(2,1)S(1)}, bf16[64,512]{1,0:T(8,128)(2,1)S(1)}, u32[]{:S(2)}, u32[]{:S(2)}) collective-permute-start(bf16[64,512]{1,0:T(8,128)(2,1)S(1)} %get-tuple-element.44), channel_id=1, source_target_pairs={{0,2},{1,3},{2,0},{3,1},{4,6},{5,7},{6,4},{7,5},{8,10},{9,11},{10,... | collective-permute-start | bytes 196616 | tf_op jit(solution)/shard_map/ppermute | solution.py:67
  178.2 4.5 %collective-permute-start.47 = (bf16[64,512]{1,0:T(8,128)(2,1)S(1)}, bf16[64,512]{1,0:T(8,128)(2,1)S(1)}, u32[]{:S(2)}, u32[]{:S(2)}) collective-permute-start(bf16[64,512]{1,0:T(8,128)(2,1)S(1)} %get-tuple-element.43), channel_id=1, source_target_pairs={{0,3},{1,0},{2,1},{3,2},{4,7},{5,4},{6,5},{7,6},{8,11},{9,8},{10,9... | collective-permute-start | bytes 196616 | tf_op jit(solution)/shard_map/ppermute | solution.py:67
  179.0 6.9 %collective-permute-start.41 = (bf16[4,64,512]{2,1,0:T(8,128)(2,1)S(1)}, bf16[4,64,512]{2,1,0:T(8,128)(2,1)S(1)}, u32[]{:S(2)}, u32[]{:S(2)}) collective-permute-start(bf16[4,64,512]{2,1,0:T(8,128)(2,1)S(1)} %stack_planes.6.refs_2_), channel_id=1, source_target_pairs={{0,8},{4,20},{8,0},{12,28},{16,24},{20,4},{24,16},{28,12},{1,9},{5... | collective-permute-start | bytes 786440 | tf_op jit(solution)/shard_map/ppermute | solution.py:53
  182.7 9.2 %collective-permute-start.48 = (bf16[4,64,512]{2,1,0:T(8,128)(2,1)S(1)}, bf16[4,64,512]{2,1,0:T(8,128)(2,1)S(1)}, u32[]{:S(2)}, u32[]{:S(2)}) collective-permute-start(bf16[4,64,512]{2,1,0:T(8,128)(2,1)S(1)} %stack_planes.7.refs_6_), channel_id=1, source_target_pairs={{0,8},{4,20},{8,0},{12,28},{16,24},{20,4},{24,16},{28,12},{1,9},{5... | collective-permute-start | bytes 786440 | tf_op jit(solution)/shard_map/ppermute | solution.py:53
  184.3 9.4 %collective-permute-start.42 = (bf16[4,64,512]{2,1,0:T(8,128)(2,1)S(1)}, bf16[4,64,512]{2,1,0:T(8,128)(2,1)S(1)}, u32[]{:S(2)}, u32[]{:S(2)}) collective-permute-start(bf16[4,64,512]{2,1,0:T(8,128)(2,1)S(1)} %stack_planes.6.refs_2_), channel_id=1, source_target_pairs={{0,16},{4,12},{8,24},{12,4},{16,0},{20,28},{24,8},{28,20},{1,17},{... | collective-permute-start | bytes 786440 | tf_op jit(solution)/shard_map/ppermute | solution.py:53
  185.9 7.8 %collective-permute-start.43 = (bf16[4,64,512]{2,1,0:T(8,128)(2,1)S(1)}, bf16[4,64,512]{2,1,0:T(8,128)(2,1)S(1)}, u32[]{:S(2)}, u32[]{:S(2)}) collective-permute-start(bf16[4,64,512]{2,1,0:T(8,128)(2,1)S(1)} %collective-permute-done.41.refs_3_), channel_id=1, source_target_pairs={{0,16},{4,12},{8,24},{12,4},{16,0},{20,28},{24,8},{28,20},{1,17},{... | collective-permute-start | bytes 786440 | tf_op jit(solution)/shard_map/ppermute | solution.py:53
  186.3 10.0 %collective-permute-start.49 = (bf16[4,64,512]{2,1,0:T(8,128)(2,1)S(1)}, bf16[4,64,512]{2,1,0:T(8,128)(2,1)S(1)}, u32[]{:S(2)}, u32[]{:S(2)}) collective-permute-start(bf16[4,64,512]{2,1,0:T(8,128)(2,1)S(1)} %stack_planes.7.refs_6_), channel_id=1, source_target_pairs={{0,16},{4,12},{8,24},{12,4},{16,0},{20,28},{24,8},{28,20},{1,17},{... | collective-permute-start | bytes 786440 | tf_op jit(solution)/shard_map/ppermute | solution.py:53
  192.0 7.1 %collective-permute-start.50 = (bf16[4,64,512]{2,1,0:T(8,128)(2,1)S(1)}, bf16[4,64,512]{2,1,0:T(8,128)(2,1)S(1)}, u32[]{:S(2)}, u32[]{:S(2)}) collective-permute-start(bf16[4,64,512]{2,1,0:T(8,128)(2,1)S(1)} %collective-permute-done.48.refs_7_), channel_id=1, source_target_pairs={{0,16},{4,12},{8,24},{12,4},{16,0},{20,28},{24,8},{28,20},{1,17},{... | collective-permute-start | bytes 786440 | tf_op jit(solution)/shard_map/ppermute | solution.py:53
  200.6 2.7 %collective-permute-start.51 = (bf16[512,512]{1,0:T(8,128)(2,1)S(1)}, bf16[512,512]{1,0:T(8,128)(2,1)S(1)}, u32[]{:S(2)}, u32[]{:S(2)}) collective-permute-start(bf16[512,512]{1,0:T(8,128)(2,1)S(1)} %bitcast.57), channel_id=1, source_target_pairs={{0,4},{4,0},{8,12},{12,8},{16,20},{20,16},{24,28},{28,24},{1,5},{5... | collective-permute-start | bytes 1572872 | tf_op jit(solution)/shard_map/ppermute | solution.py:464
  (1 other events, 3.4 us)

commit v5 on v4

--- a/solution.py
+++ b/solution.py
@@ -41,12 +41,7 @@
 SMEM = pl.BlockSpec(memory_space=pltpu.SMEM)
 VMEM = pl.BlockSpec(memory_space=pltpu.VMEM)
 ANY = pl.BlockSpec(memory_space=pl.ANY)
-HBM = pl.BlockSpec(memory_space=pltpu.HBM)
 MIB = 1024 * 1024
-
-
-def f32_sum(a, b):
-    return (a.astype(jnp.float32) + b.astype(jnp.float32)).astype(jnp.bfloat16)
 
 
 def exchange(value, n_dp, step):
@@ -68,7 +63,7 @@
     return stack(out, after)
 
 
-def call(kernel, out_shape, in_specs, out_specs, name, limit, flops=0, moved=0, **more):
+def call(kernel, out_shape, in_specs, out_specs, name, limit, **more):
     return pl.pallas_call(
         kernel,
         out_shape=out_shape,
@@ -80,31 +75,27 @@
     )
 
 
-def add_split_kernel(split, keep, got, *refs):
-    out = refs[1:] if len(refs) > (2 if split else 1) else refs
-    n = out[0].shape[0]
-    for i in range(keep.shape[0]):
-        value = f32_sum(keep[i], got[i])
-        if i < n:
-            out[0][i] = value
-        else:
-            out[1][i - n] = value
-
-
-def add_split(keep, got, after, split):
-    n = keep.shape[0]
-    shape = jax.ShapeDtypeStruct((n // 2 if split else n,) + keep.shape[1:], keep.dtype)
-    extra = [] if after is None else [after]
-    out = call(
-        lambda *refs: add_split_kernel(split, *refs),
-        [shape] * (2 if split else 1),
-        [VMEM, VMEM] + [ANY] * len(extra),
-        [VMEM] * (2 if split else 1),
-        "add_halves",
+def add_kernel(counts, *refs):
+    at, outs = sum(counts), refs[-len(counts) :]
+    terms = iter(refs[:at])
+    for n, out in zip(counts, outs):
+        total = next(terms)[...].astype(jnp.float32)
+        for _ in range(n - 1):
+            total = total + next(terms)[...].astype(jnp.float32)
+        out[...] = total.astype(out.dtype)
+
+
+def add_terms(terms, after):
+    counts = [len(t) for t in terms]
+    shapes = [jax.ShapeDtypeStruct(t[0].shape, t[0].dtype) for t in terms]
+    return call(
+        lambda *refs: add_kernel(counts, *refs),
+        shapes,
+        [VMEM] * sum(counts) + [ANY],
+        [VMEM] * len(counts),
+        "add_terms",
         8,
-        moved=2 * keep.size,
-    )(keep, got, *extra)
-    return out if split else (out[0], None)
+    )(*[x for t in terms for x in t], after)
 
 
 def stack_kernel(n, *refs):
@@ -121,7 +112,6 @@
         VMEM,
         "stack_planes",
         8,
-        moved=2 * len(parts) * parts[0].size,
     )(*parts, *extra)
 
 
@@ -208,8 +198,6 @@
         VMEM,
         "project_last" if last else "project_first",
         20,
-        flops=4 * rows * k * half,
-        moved=6 * rows * k,
         scratch_shapes=[
             pltpu.VMEM((k, half), jnp.bfloat16),
             pltpu.VMEM((rows, k), jnp.bfloat16),
@@ -221,31 +209,24 @@
 
 def pick_kernel(make_place, layout, n_chip, chosen, att_ref, *refs):
     place = make_place()
-    keep_ref, send_ref = refs[-2:]
-    top = n_chip // 2
+    outs = refs[-n_chip:]
     for r in range(n_chip):
         for k in range(place.n_expert):
             index, mine = layout.grain(place, chosen, r, place.ahead(k))
             value = att_ref[jnp.where(mine, index, 0)]
-            value = jnp.where(mine, value, jnp.zeros_like(value))
-            if r < top:
-                keep_ref[r, k] = value
-            else:
-                send_ref[r - top, k] = value
+            outs[r][k] = jnp.where(mine, value, jnp.zeros_like(value))
 
 
 def pick(make_place, layout, n_chip, n_expert, chosen, grains, after):
-    shape = (n_chip // 2, n_expert) + grains.shape[1:]
-    shape = jax.ShapeDtypeStruct(shape, grains.dtype)
+    shape = jax.ShapeDtypeStruct((n_expert,) + grains.shape[1:], grains.dtype)
     extra = [] if after is None else [after]
     return call(
         lambda *refs: pick_kernel(make_place, layout, n_chip, *refs),
-        [shape, shape],
+        [shape] * n_chip,
         [SMEM, VMEM] + [ANY] * len(extra),
-        [VMEM, VMEM],
+        [VMEM] * n_chip,
         "pick_blocks",
         8,
-        moved=4 * MIB,
     )(chosen, grains, *extra)
 
 
@@ -274,7 +255,6 @@
         VMEM,
         "add_expert_rows",
         12,
-        moved=4 * MIB,
         scratch_shapes=[pltpu.VMEM(grains.shape, jnp.float32)],
     )(chosen, grains, *pieces)
 
@@ -333,12 +313,10 @@
     return call(
         lambda *refs: hidden_kernel(make_place, n, *refs),
         jax.ShapeDtypeStruct((n * rows, ff), jnp.bfloat16),
-        [VMEM] * (2 * n) + [HBM] * 2 + [ANY] * len(extra),
+        [VMEM] * (2 * n) + [ANY] * 2 + [ANY] * len(extra),
         VMEM,
         "expert_hidden",
         28,
-        flops=4 * n * rows * ff * model_width,
-        moved=4 * model_width * ff,
         scratch_shapes=[
             pltpu.VMEM((n * rows, model_width), jnp.bfloat16),
             pltpu.VMEM((ff // tile, model_width, tile), jnp.bfloat16),
@@ -349,8 +327,9 @@
 
 
 def down_kernel(make_place, layout, order, s, counts, hid, wd, values, *refs):
-    out, wds, sems = refs[-3:]
-    n, n_z, rows, width = out.shape
+    outs, wds, sems = refs[-2 - len(order) : -2], refs[-2], refs[-1]
+    n = len(order)
+    n_z, rows, width = outs[0].shape
     place = make_place()
     copies = []
     for z in range(n_z):
@@ -369,7 +348,8 @@
         copies[z].wait()
         part = jnp.dot(hid[...], wds[z], preferred_element_type=jnp.float32)
         for r in range(n):
-            out[order[r], z] = (part[r * rows : (r + 1) * rows] * scale[r]).astype(out.dtype)
+            value = part[r * rows : (r + 1) * rows] * scale[r]
+            outs[order[r]][z] = value.astype(jnp.bfloat16)
 
 
 def down(make_place, layout, order, s, n_z, width, counts, hid, w_down, values, after):
@@ -378,13 +358,11 @@
     extra = [] if after is None else [after]
     return call(
         lambda *refs: down_kernel(make_place, layout, order, s, *refs),
-        jax.ShapeDtypeStruct((n, n_z, layout.share, width), jnp.bfloat16),
-        [SMEM, VMEM, HBM, VMEM] + [ANY] * len(extra),
-        VMEM,
+        [jax.ShapeDtypeStruct((n_z, layout.share, width), jnp.bfloat16)] * n,
+        [SMEM, VMEM, ANY, VMEM] + [ANY] * len(extra),
+        [VMEM] * n,
         "expert_down",
         12,
-        flops=2 * hid.size * n_z * width,
-        moved=2 * ff * n_z * width,
         scratch_shapes=[
             pltpu.VMEM((n_z, ff, width), jnp.bfloat16),
             pltpu.SemaphoreType.DMA((n_z,)),
@@ -398,12 +376,18 @@
     n_chip = 1 << n_bits
     plain = list(range(n_chip))
     after = yield
-    keep, send = pick(make_place, layout, n_chip, n_expert, chosen, grains, after)
-    after = yield keep, None
+    terms = [[p] for p in pick(make_place, layout, n_chip, n_expert, chosen, grains, after)]
+    after = yield terms[0][0], None
     for step in range(n_bits - 1, -1, -1):
-        keep, send = add_split(keep, exchange(send, n_dp, step), after, step > 0)
-        after = yield keep, None
-    crossed = swap_planes(keep[0], n_expert, after)
+        half_way = 1 << step
+        send = [t[0] for t in terms[half_way:]]
+        if len(terms[half_way]) > 1:
+            send = add_terms(terms[half_way:], after)
+            after = yield send[0], None
+        terms = [t + [exchange(s, n_dp, step)] for t, s in zip(terms, send)]
+    mine = add_terms(terms, after)[0]
+    after = yield mine, None
+    crossed = swap_planes(mine, n_expert, after)
     own_half = gather_all(crossed, n_dp, n_bits)
     after = yield (own_half[1] if layout.group == GROUPS - 1 else crossed), None
     got = [to_partner(p) for p in own_half]
@@ -417,15 +401,17 @@
         )
 
     theirs = downs(reverse, 1)
-    after = yield theirs, None
+    after = yield theirs[0], None
     mine = downs(plain, 0)
+    after = yield mine[0], None
+    terms = [[m, to_partner(t)] for m, t in zip(mine, theirs)]
+    for step in range(n_bits - 1, -1, -1):
+        send = add_terms(terms[1 << step :], after)
+        after = yield send[0], None
+        terms = [t + [exchange(s, n_dp, step)] for t, s in zip(terms, send)]
+    mine = add_terms(terms, after)[0]
     after = yield mine, None
-    keep, send = add_split(mine, to_partner(theirs), after, True)
-    after = yield keep, None
-    for step in range(n_bits - 1, -1, -1):
-        keep, send = add_split(keep, exchange(send, n_dp, step), after, step > 0)
-        after = yield keep, None
-    crossed = swap_planes(keep[0], n_expert, after)
+    crossed = swap_planes(mine, n_expert, after)
     yield crossed, gather_all(crossed, n_dp, n_bits)
 
 

time: 205 us -> 195 us (0.951)
  waiting for transfers between devices: 90 us -> 73.4 us
  starting transfers between devices: 60.3 us -> 63.2 us
  local copies, waits for them, and re-layouts: 13.2 us -> 15.9 us
    ppermute x26 -> x30, waiting for transfers between devices: 75.1 us -> 54.6 us  [exchange(): return lax.ppermute(value, 'dp', step_pairs(n_dp, step))]
    ppermute x14 -> x20, starting transfers between devices: 3.05 us -> 6.33 us  [to_partner(): return lax.ppermute(value, 'dp', pair)]
    ppermute x12, waiting for transfers between devices: 10.3 us -> 13.4 us  [swap_planes(): out.append(lax.ppermute(parts[k], 'expert', pairs))]
    unnamed x26 -> x38, local copies, waits for them, and re-layouts: 10.2 us -> 12.2 us
    ppermute x26 -> x30, starting transfers between devices: 37.1 us -> 38 us  [exchange(): return lax.ppermute(value, 'dp', step_pairs(n_dp, step))]
    ppermute x14 -> x20, waiting for transfers between devices: 4.62 us -> 5.4 us  [to_partner(): return lax.ppermute(value, 'dp', pair)]
  transfers between devices with their start and end apart: 52 -> 62, of which waited for: 28 -> 25; matrix products, arithmetic and copies ran while one was open for 1% -> 2% of each run, Pallas kernels for 5% -> 18%
where the time goes in v5:
time: 195 us; the launch traced here: 194 us
  waiting for transfers between devices  73.4 us (38%)
  starting transfers between devices  63.2 us (32%)
  Pallas kernels  39.9 us (20%)
  local copies, waits for them, and re-layouts  15.9 us (8%)
    ppermute x30, waiting for transfers between devices, exchange(): return lax.ppermute(value, 'dp', step_pairs(n_dp, step))  54.6 us
    ppermute x30, starting transfers between devices, exchange(): return lax.ppermute(value, 'dp', step_pairs(n_dp, step))  38 us
    ppermute x12, starting transfers between devices, swap_planes(): out.append(lax.ppermute(parts[k], 'expert', pairs))  18.9 us
    pallas_call x2, Pallas kernels, hidden_units(): call(lambda *refs: hidden_kernel(make_place, n, *refs), jax.ShapeDtypeStr...  16.2 us
    ppermute x12, waiting for transfers between devices, swap_planes(): out.append(lax.ppermute(parts[k], 'expert', pairs))  13.4 us
    unnamed x38, local copies, waits for them, and re-layouts  12.2 us
    pallas_call x4, Pallas kernels, down(): call(lambda *refs: down_kernel(make_place, layout, order, s, *refs), [jax...  12.2 us
    pallas_call x2, Pallas kernels, project(): call(lambda *refs: project_kernel(make_place, parts, len(weights), len(ex...  6.7 us
  transfers between devices with their start and end apart: 62, of which 25 were waited for; matrix products, arithmetic and copies ran while one was open for 2% of the time, Pallas kernels for 18%

profile of v5, /device:TPU:0, one launch (start us, length us, event | category | flops | bytes accessed | tf_op | source)
XLA Modules:
  0.0 194.3 jit_solution(9206829552568790029)
XLA Ops:
  0.5 1.4 constant_dynamic-slice_fusion.2
  2.0 2.9 %collective-permute-start.4 = (bf16[512,512]{1,0:T(8,128)(2,1)S(1)}, bf16[512,512]{1,0:T(8,128)(2,1)S(1)}, u32[]{:S(2)}, u32[]{:S(2)}) collective-permute-start(bf16[512,512]{1,0:T(8,128)(2,1)S(1)} %get-tuple-element.66.refs_2_), channel_id=1, source_target_pairs={{0,8},{4,20},{8,0},{12,28},{16,24},{20,4},{24,16},{28,12},{1,9},{5... | collective-permute-start | bytes 1572872 | tf_op jit(solution)/shard_map/ppermute | solution.py:48
  4.9 3.1 %collective-permute-done.2.refs_3_ = bf16[512,512]{1,0:T(8,128)(2,1)S(1)} collective-permute-done((bf16[512,512]{1,0:T(8,128)(2,1)S(1)}, bf16[512,512]{1,0:T(8,128)(2,1)S(1)}, u32[]{:S(2)}, u32[]{:S(2)}) %collective-permute-start.2) | collective-permute-done | bytes 524320 | tf_op jit(solution)/shard_map/ppermute | solution.py:450
  8.0 2.9 %collective-permute-start.6 = (bf16[512,512]{1,0:T(8,128)(2,1)S(1)}, bf16[512,512]{1,0:T(8,128)(2,1)S(1)}, u32[]{:S(2)}, u32[]{:S(2)}) collective-permute-start(bf16[512,512]{1,0:T(8,128)(2,1)S(1)} %collective-permute-done.2.refs_3_), channel_id=1, source_target_pairs={{0,8},{4,20},{8,0},{12,28},{16,24},{20,4},{24,16},{28,12},{1,9},{5... | collective-permute-start | bytes 1572872 | tf_op jit(solution)/shard_map/ppermute | solution.py:48
  10.8 1.5 collective-permute-start.1
  12.4 1.3 constant_dynamic-slice_fusion
  14.6 8.2 %collective-permute-done.6.refs_5_ = bf16[512,512]{1,0:T(8,128)(2,1)S(1)} collective-permute-done((bf16[512,512]{1,0:T(8,128)(2,1)S(1)}, bf16[512,512]{1,0:T(8,128)(2,1)S(1)}, u32[]{:S(2)}, u32[]{:S(2)}) %collective-permute-start.6) | collective-permute-done | bytes 524320 | tf_op jit(solution)/shard_map/ppermute | solution.py:48
  22.8 3.0 %collective-permute-start.5 = (bf16[512,512]{1,0:T(8,128)(2,1)S(1)}, bf16[512,512]{1,0:T(8,128)(2,1)S(1)}, u32[]{:S(2)}, u32[]{:S(2)}) collective-permute-start(bf16[512,512]{1,0:T(8,128)(2,1)S(1)} %collective-permute-done.4.refs_4_), channel_id=1, source_target_pairs={{0,16},{4,12},{8,24},{12,4},{16,0},{20,28},{24,8},{28,20},{1,17},{... | collective-permute-start | bytes 1572872 | tf_op jit(solution)/shard_map/ppermute | solution.py:48
  25.9 3.3 %project_first.1.refs_6_ = f32[2,512,512]{2,1,0:T(8,128)S(1)} custom-call(bf16[512,4096]{1,0:T(8,128)(2,1)S(1)} %copy-done.3, bf16[512,4096]{1,0:T(8,128)(2,1)} %collective-permute-done.refs_1_, bf16[512,512]{1,0:T(8,128)(2,1)S(1)} %get-tuple-element.66.refs_2_, bf16[512,512]{1,0:T(8,128)(2,1)S(1)} %collective-permute-done.2.refs_3_, ...), custom_call_target="tpu_custom_call" | custom-call | tf_op jit(solution)/shard_map/project_first/pallas_call | solution.py:194
  29.3 5.1 %collective-permute-done.5.refs_4_ = bf16[512,512]{1,0:T(8,128)(2,1)S(1)} collective-permute-done((bf16[512,512]{1,0:T(8,128)(2,1)S(1)}, bf16[512,512]{1,0:T(8,128)(2,1)S(1)}, u32[]{:S(2)}, u32[]{:S(2)}) %collective-permute-start.5) | collective-permute-done | bytes 524320 | tf_op jit(solution)/shard_map/ppermute | solution.py:48
  34.3 5.6 %collective-permute-done.7.refs_5_ = bf16[512,512]{1,0:T(8,128)(2,1)S(1)} collective-permute-done((bf16[512,512]{1,0:T(8,128)(2,1)S(1)}, bf16[512,512]{1,0:T(8,128)(2,1)S(1)}, u32[]{:S(2)}, u32[]{:S(2)}) %collective-permute-start.7) | collective-permute-done | bytes 524320 | tf_op jit(solution)/shard_map/ppermute | solution.py:48
  40.0 3.4 %project_last.1 = bf16[2,512,512]{2,1,0:T(8,128)(2,1)S(1)} custom-call(bf16[512,4096]{1,0:T(8,128)(2,1)S(1)} %copy-done.3, bf16[512,4096]{1,0:T(8,128)(2,1)} %collective-permute-done.refs_1_, bf16[512,512]{1,0:T(8,128)(2,1)S(1)} %collective-permute-done.1.refs_2_, bf16[512,512]{1,0:T(8,128)(2,1)S(1)} %collective-permute-done.3.refs_3_, ...), custom_call_target="tpu_custom_call" | custom-call | tf_op jit(solution)/shard_map/project_last/pallas_call | solution.py:194
  44.1 1.8 collective-permute-start.10
  46.2 4.3 %collective-permute-done.10.refs_1_ = bf16[4,64,512]{2,1,0:T(8,128)(2,1)S(1)} collective-permute-done((bf16[4,64,512]{2,1,0:T(8,128)(2,1)S(1)}, bf16[4,64,512]{2,1,0:T(8,128)(2,1)S(1)}, u32[]{:S(2)}, u32[]{:S(2)}) %collective-permute-start.10) | collective-permute-done | bytes 262176 | tf_op jit(solution)/shard_map/ppermute | solution.py:48
  50.6 1.6 collective-permute-start.11
  53.0 1.6 collective-permute-start.15
  54.6 4.7 %collective-permute-done.11.refs_2_ = bf16[4,64,512]{2,1,0:T(8,128)(2,1)S(1)} collective-permute-done((bf16[4,64,512]{2,1,0:T(8,128)(2,1)S(1)}, bf16[4,64,512]{2,1,0:T(8,128)(2,1)S(1)}, u32[]{:S(2)}, u32[]{:S(2)}) %collective-permute-start.11) | collective-permute-done | bytes 262176 | tf_op jit(solution)/shard_map/ppermute | solution.py:48
  59.4 2.1 %collective-permute-start.12 = (bf16[64,512]{1,0:T(8,128)(2,1)S(1)}, bf16[64,512]{1,0:T(8,128)(2,1)S(1)}, u32[]{:S(2)}, u32[]{:S(2)}) collective-permute-start(bf16[64,512]{1,0:T(8,128)(2,1)S(1)} %get-tuple-element.81), channel_id=1, source_target_pairs={{0,1},{1,2},{2,3},{3,0},{4,5},{5,6},{6,7},{7,4},{8,9},{9,10},{10,1... | collective-permute-start | bytes 196616 | tf_op jit(solution)/shard_map/ppermute | solution.py:62
  61.5 2.6 %collective-permute-start.13 = (bf16[64,512]{1,0:T(8,128)(2,1)S(1)}, bf16[64,512]{1,0:T(8,128)(2,1)S(1)}, u32[]{:S(2)}, u32[]{:S(2)}) collective-permute-start(bf16[64,512]{1,0:T(8,128)(2,1)S(1)} %get-tuple-element.80), channel_id=1, source_target_pairs={{0,2},{1,3},{2,0},{3,1},{4,6},{5,7},{6,4},{7,5},{8,10},{9,11},{10,... | collective-permute-start | bytes 196616 | tf_op jit(solution)/shard_map/ppermute | solution.py:62
  64.1 1.3 collective-permute-start.14
  65.5 1.6 collective-permute-start.23
  67.1 1.6 collective-permute-start.24
  69.5 2.1 %collective-permute-start.17 = (bf16[4,64,512]{2,1,0:T(8,128)(2,1)S(1)}, bf16[4,64,512]{2,1,0:T(8,128)(2,1)S(1)}, u32[]{:S(2)}, u32[]{:S(2)}) collective-permute-start(bf16[4,64,512]{2,1,0:T(8,128)(2,1)S(1)} %stack_planes.4.refs_3_.refs_0_), channel_id=1, source_target_pairs={{0,16},{4,12},{8,24},{12,4},{16,0},{20,28},{24,8},{28,20},{1,17},{... | collective-permute-start | bytes 786440 | tf_op jit(solution)/shard_map/ppermute | solution.py:48
  71.5 2.2 %collective-permute-done.23.refs_1_ = bf16[4,64,512]{2,1,0:T(8,128)(2,1)S(1)} collective-permute-done((bf16[4,64,512]{2,1,0:T(8,128)(2,1)S(1)}, bf16[4,64,512]{2,1,0:T(8,128)(2,1)S(1)}, u32[]{:S(2)}, u32[]{:S(2)}) %collective-permute-start.23) | collective-permute-done | bytes 262176 | tf_op jit(solution)/shard_map/ppermute | solution.py:48
  73.8 3.5 %collective-permute-done.16.refs_1_ = bf16[4,64,512]{2,1,0:T(8,128)(2,1)S(1)} collective-permute-done((bf16[4,64,512]{2,1,0:T(8,128)(2,1)S(1)}, bf16[4,64,512]{2,1,0:T(8,128)(2,1)S(1)}, u32[]{:S(2)}, u32[]{:S(2)}) %collective-permute-start.16) | collective-permute-done | bytes 262176 | tf_op jit(solution)/shard_map/ppermute | solution.py:48
  78.2 2.9 %collective-permute-start.26 = (bf16[64,512]{1,0:T(8,128)(2,1)S(1)}, bf16[64,512]{1,0:T(8,128)(2,1)S(1)}, u32[]{:S(2)}, u32[]{:S(2)}) collective-permute-start(bf16[64,512]{1,0:T(8,128)(2,1)S(1)} %get-tuple-element.76), channel_id=1, source_target_pairs={{0,2},{1,3},{2,0},{3,1},{4,6},{5,7},{6,4},{7,5},{8,10},{9,11},{10,... | collective-permute-start | bytes 196616 | tf_op jit(solution)/shard_map/ppermute | solution.py:62
  81.3 2.3 %collective-permute-done.25.refs_1_ = bf16[64,512]{1,0:T(8,128)(2,1)S(1)} collective-permute-done((bf16[64,512]{1,0:T(8,128)(2,1)S(1)}, bf16[64,512]{1,0:T(8,128)(2,1)S(1)}, u32[]{:S(2)}, u32[]{:S(2)}) %collective-permute-start.25) | collective-permute-done | bytes 65568 | tf_op jit(solution)/shard_map/ppermute | solution.py:62
  83.6 1.1 collective-permute-done.26.refs_2_
  86.1 1.8 collective-permute-start.28
  89.4 2.0 %collective-permute-start.35 = (bf16[4,64,512]{2,1,0:T(8,128)(2,1)}, bf16[4,64,512]{2,1,0:T(8,128)(2,1)S(1)}, u32[]{:S(2)}, u32[]{:S(2)}) collective-permute-start(bf16[4,64,512]{2,1,0:T(8,128)(2,1)} %stack_planes.5.refs_0_), channel_id=1, source_target_pairs={{0,16},{4,12},{8,24},{12,4},{16,0},{20,28},{24,8},{28,20},{1,17},{... | collective-permute-start | bytes 786440 | tf_op jit(solution)/shard_map/ppermute | solution.py:48
  91.4 1.8 collective-permute-done.28.refs_10_.refs_1_
  93.2 2.5 %collective-permute-start.36 = (bf16[4,64,512]{2,1,0:T(8,128)(2,1)}, bf16[4,64,512]{2,1,0:T(8,128)(2,1)S(1)}, u32[]{:S(2)}, u32[]{:S(2)}) collective-permute-start(bf16[4,64,512]{2,1,0:T(8,128)(2,1)} %collective-permute-done.28.refs_10_.refs_1_), channel_id=1, source_target_pairs={{0,16},{4,12},{8,24},{12,4},{16,0},{20,28},{24,8},{28,20},{1,17},{... | collective-permute-start | bytes 786440 | tf_op jit(solution)/shard_map/ppermute | solution.py:48
  95.8 3.4 %copy-done.1 = bf16[1,4096,1024]{2,1,0:T(8,128)(2,1)S(1)} copy-done((bf16[1,4096,1024]{2,1,0:T(8,128)(2,1)S(1)}, bf16[1,4096,1024]{2,1,0:T(8,128)(2,1)}, u32[]{:S(2)}) %copy-start.1) | copy-done | bytes 8388632
  99.1 3.4 %copy-done.2 = bf16[1,4096,1024]{2,1,0:T(8,128)(2,1)S(1)} copy-done((bf16[1,4096,1024]{2,1,0:T(8,128)(2,1)S(1)}, bf16[1,4096,1024]{2,1,0:T(8,128)(2,1)}, u32[]{:S(2)}) %copy-start.2) | copy-done | bytes 8388632
  102.5 7.5 %expert_hidden.2.refs_1_.refs_4_ = bf16[256,1024]{1,0:T(8,128)(2,1)S(1)} custom-call(bf16[4,64,512]{2,1,0:T(8,128)(2,1)S(1)} %stack_planes.4.refs_3_.refs_0_, bf16[4,64,512]{2,1,0:T(8,128)(2,1)S(1)} %collective-permute-done.16.refs_1_, bf16[4,64,512]{2,1,0:T(8,128)(2,1)S(1)} %collective-permute-done.17.refs_2_, ...), custom_call_target="tpu_custom_call" | custom-call | tf_op jit(solution)/shard_map/expert_hidden/pallas_call | solution.py:313
  110.1 3.4 %copy-done = bf16[1,1024,4096]{2,1,0:T(8,128)(2,1)S(1)} copy-done((bf16[1,1024,4096]{2,1,0:T(8,128)(2,1)S(1)}, bf16[1,1024,4096]{2,1,0:T(8,128)(2,1)}, u32[]{:S(2)}) %copy-start) | copy-done | bytes 8388632
  113.5 2.9 %expert_down.4 = (bf16[4,64,512]{2,1,0:T(8,128)(2,1)S(1)}, bf16[4,64,512]{2,1,0:T(8,128)(2,1)S(1)}, bf16[4,64,512]{2,1,0:T(8,128)(2,1)S(1)}, bf16[4,64,512]{2,1,0:T(8,128)(2,1)S(1)}) custom-call(s32[4]{0:T(128)S(1)} %copy-done.11, bf16[256,1024]{1,0:T(8,128)(2,1)S(1)} %expert_hidden.2.refs_1_.refs_4_, bf16[1024,4096]{1,0:T(8,128)(2,1)S(1)} %bitcast.39, ...), custom_call_target="tpu_custom_call" | custom-call | tf_op jit(solution)/shard_map/expert_down/pallas_call | solution.py:359
  118.2 2.9 %expert_down.5 = (bf16[4,64,512]{2,1,0:T(8,128)(2,1)S(1)}, bf16[4,64,512]{2,1,0:T(8,128)(2,1)S(1)}, bf16[4,64,512]{2,1,0:T(8,128)(2,1)S(1)}, bf16[4,64,512]{2,1,0:T(8,128)(2,1)S(1)}) custom-call(s32[4]{0:T(128)S(1)} %copy-done.11, bf16[256,1024]{1,0:T(8,128)(2,1)S(1)} %expert_hidden.2.refs_1_.refs_4_, bf16[1024,4096]{1,0:T(8,128)(2,1)S(1)} %bitcast.40, ...), custom_call_target="tpu_custom_call" | custom-call | tf_op jit(solution)/shard_map/expert_down/pallas_call | solution.py:359
  121.9 1.1 copy-done.7
  123.0 0.9 copy-done.9
  123.9 8.7 %expert_hidden.3.refs_1_.refs_4_ = bf16[256,1024]{1,0:T(8,128)(2,1)S(1)} custom-call(bf16[4,64,512]{2,1,0:T(8,128)(2,1)} %stack_planes.5.refs_0_, bf16[4,64,512]{2,1,0:T(8,128)(2,1)} %collective-permute-done.28.refs_10_.refs_1_, bf16[4,64,512]{2,1,0:T(8,128)(2,1)S(1)} %copy-done.7, bf16[4,64,512]{2,1,0:T(8,128)(2,1)S(1)} %copy-done.9, ...), custom_call_target="tpu_custom_call" | custom-call | tf_op jit(solution)/shard_map/expert_hidden/pallas_call | solution.py:313
  132.7 3.0 %expert_down.6 = (bf16[4,64,512]{2,1,0:T(8,128)(2,1)S(1)}, bf16[4,64,512]{2,1,0:T(8,128)(2,1)S(1)}, bf16[4,64,512]{2,1,0:T(8,128)(2,1)S(1)}, bf16[4,64,512]{2,1,0:T(8,128)(2,1)S(1)}) custom-call(s32[4]{0:T(128)S(1)} %copy-done.11, bf16[256,1024]{1,0:T(8,128)(2,1)S(1)} %expert_hidden.3.refs_1_.refs_4_, bf16[1024,4096]{1,0:T(8,128)(2,1)S(1)} %bitcast.43, ...), custom_call_target="tpu_custom_call" | custom-call | tf_op jit(solution)/shard_map/expert_down/pallas_call | solution.py:359
  135.7 2.2 %collective-permute-start.42 = (bf16[4,64,512]{2,1,0:T(8,128)(2,1)S(1)}, bf16[4,64,512]{2,1,0:T(8,128)(2,1)S(1)}, u32[]{:S(2)}, u32[]{:S(2)}) collective-permute-start(bf16[4,64,512]{2,1,0:T(8,128)(2,1)S(1)} %get-tuple-element.53), channel_id=1, source_target_pairs={{0,4},{4,0},{8,12},{12,8},{16,20},{20,16},{24,28},{28,24},{1,5},{5... | collective-permute-start | bytes 786440 | tf_op jit(solution)/shard_map/ppermute | solution.py:450
  139.1 3.3 %expert_down.7 = (bf16[4,64,512]{2,1,0:T(8,128)(2,1)S(1)}, bf16[4,64,512]{2,1,0:T(8,128)(2,1)S(1)}, bf16[4,64,512]{2,1,0:T(8,128)(2,1)S(1)}, bf16[4,64,512]{2,1,0:T(8,128)(2,1)S(1)}) custom-call(s32[4]{0:T(128)S(1)} %copy-done.11, bf16[256,1024]{1,0:T(8,128)(2,1)S(1)} %expert_hidden.3.refs_1_.refs_4_, bf16[1024,4096]{1,0:T(8,128)(2,1)S(1)} %bitcast.44, ...), custom_call_target="tpu_custom_call" | custom-call | tf_op jit(solution)/shard_map/expert_down/pallas_call | solution.py:359
  142.4 1.8 collective-permute-start.41
  144.9 1.6 collective-permute-start.53
  146.4 4.4 %collective-permute-done.41.refs_3_ = bf16[4,64,512]{2,1,0:T(8,128)(2,1)S(1)} collective-permute-done((bf16[4,64,512]{2,1,0:T(8,128)(2,1)S(1)}, bf16[4,64,512]{2,1,0:T(8,128)(2,1)S(1)}, u32[]{:S(2)}, u32[]{:S(2)}) %collective-permute-start.41) | collective-permute-done | bytes 262176 | tf_op jit(solution)/shard_map/ppermute | solution.py:48
  151.1 2.5 %collective-permute-start.54 = (bf16[4,64,512]{2,1,0:T(8,128)(2,1)S(1)}, bf16[4,64,512]{2,1,0:T(8,128)(2,1)S(1)}, u32[]{:S(2)}, u32[]{:S(2)}) collective-permute-start(bf16[4,64,512]{2,1,0:T(8,128)(2,1)S(1)} %add_terms.18.refs_4_), channel_id=1, source_target_pairs={{0,8},{4,20},{8,0},{12,28},{16,24},{20,4},{24,16},{28,12},{1,9},{5... | collective-permute-start | bytes 786440 | tf_op jit(solution)/shard_map/ppermute | solution.py:48
  153.7 1.5 collective-permute-start.44
  155.1 2.0 %collective-permute-start.45 = (bf16[64,512]{1,0:T(8,128)(2,1)S(1)}, bf16[64,512]{1,0:T(8,128)(2,1)S(1)}, u32[]{:S(2)}, u32[]{:S(2)}) collective-permute-start(bf16[64,512]{1,0:T(8,128)(2,1)S(1)} %get-tuple-element.72), channel_id=1, source_target_pairs={{0,2},{1,3},{2,0},{3,1},{4,6},{5,7},{6,4},{7,5},{8,10},{9,11},{10,... | collective-permute-start | bytes 196616 | tf_op jit(solution)/shard_map/ppermute | solution.py:62
  157.1 2.7 %collective-permute-done.44.refs_1_ = bf16[64,512]{1,0:T(8,128)(2,1)S(1)} collective-permute-done((bf16[64,512]{1,0:T(8,128)(2,1)S(1)}, bf16[64,512]{1,0:T(8,128)(2,1)S(1)}, u32[]{:S(2)}, u32[]{:S(2)}) %collective-permute-start.44) | collective-permute-done | bytes 65568 | tf_op jit(solution)/shard_map/ppermute | solution.py:62
  159.8 1.4 collective-permute-start.46
  162.0 2.1 %collective-permute-done.46.refs_3_ = bf16[64,512]{1,0:T(8,128)(2,1)S(1)} collective-permute-done((bf16[64,512]{1,0:T(8,128)(2,1)S(1)}, bf16[64,512]{1,0:T(8,128)(2,1)S(1)}, u32[]{:S(2)}, u32[]{:S(2)}) %collective-permute-start.46) | collective-permute-done | bytes 65568 | tf_op jit(solution)/shard_map/ppermute | solution.py:62
  164.4 3.9 %collective-permute-start.56 = (bf16[64,512]{1,0:T(8,128)(2,1)S(1)}, bf16[64,512]{1,0:T(8,128)(2,1)S(1)}, u32[]{:S(2)}, u32[]{:S(2)}) collective-permute-start(bf16[64,512]{1,0:T(8,128)(2,1)S(1)} %get-tuple-element.68), channel_id=1, source_target_pairs={{0,2},{1,3},{2,0},{3,1},{4,6},{5,7},{6,4},{7,5},{8,10},{9,11},{10,... | collective-permute-start | bytes 196616 | tf_op jit(solution)/shard_map/ppermute | solution.py:62
  168.9 1.6 collective-permute-done.55.refs_1_
  170.5 1.3 collective-permute-done.56.refs_2_
  172.7 2.1 %collective-permute-start.50 = (bf16[4,64,512]{2,1,0:T(8,128)(2,1)S(1)}, bf16[4,64,512]{2,1,0:T(8,128)(2,1)S(1)}, u32[]{:S(2)}, u32[]{:S(2)}) collective-permute-start(bf16[4,64,512]{2,1,0:T(8,128)(2,1)S(1)} %stack_planes.6.refs_4_.refs_2_), channel_id=1, source_target_pairs={{0,16},{4,12},{8,24},{12,4},{16,0},{20,28},{24,8},{28,20},{1,17},{... | collective-permute-start | bytes 786440 | tf_op jit(solution)/shard_map/ppermute | solution.py:48
  174.9 2.6 %collective-permute-done.49.refs_3_ = bf16[4,64,512]{2,1,0:T(8,128)(2,1)S(1)} collective-permute-done((bf16[4,64,512]{2,1,0:T(8,128)(2,1)S(1)}, bf16[4,64,512]{2,1,0:T(8,128)(2,1)S(1)}, u32[]{:S(2)}, u32[]{:S(2)}) %collective-permute-start.49) | collective-permute-done | bytes 262176 | tf_op jit(solution)/shard_map/ppermute | solution.py:48
  177.5 5.6 %collective-permute-done.58.refs_7_ = bf16[4,64,512]{2,1,0:T(8,128)(2,1)S(1)} collective-permute-done((bf16[4,64,512]{2,1,0:T(8,128)(2,1)S(1)}, bf16[4,64,512]{2,1,0:T(8,128)(2,1)S(1)}, u32[]{:S(2)}, u32[]{:S(2)}) %collective-permute-start.58) | collective-permute-done | bytes 262176 | tf_op jit(solution)/shard_map/ppermute | solution.py:48
  183.2 1.7 collective-permute-done.51.refs_5_
  184.8 4.7 %collective-permute-done.60.refs_9_ = bf16[4,64,512]{2,1,0:T(8,128)(2,1)S(1)} collective-permute-done((bf16[4,64,512]{2,1,0:T(8,128)(2,1)S(1)}, bf16[4,64,512]{2,1,0:T(8,128)(2,1)S(1)}, u32[]{:S(2)}, u32[]{:S(2)}) %collective-permute-start.60) | collective-permute-done | bytes 262176 | tf_op jit(solution)/shard_map/ppermute | solution.py:48
  189.5 1.4 add_expert_rows.1
  191.1 1.9 collective-permute-done.61
  193.0 1.3 maximum_select_fusion
  (135 shorter events, 15.7 us)
Async XLA Ops:
  0.0 25.9 %collective-permute-start = (bf16[512,4096]{1,0:T(8,128)(2,1)}, bf16[512,4096]{1,0:T(8,128)(2,1)}, u32[]{:S(2)}, u32[]{:S(2)}) collective-permute-start(bf16[512,4096]{1,0:T(8,128)(2,1)} %refs_0_.10), channel_id=1, source_target_pairs={{0,4},{4,0},{8,12},{12,8},{16,20},{20,16},{24,28},{28,24},{1,5},{5... | collective-permute-start | bytes 12582920 | tf_op jit(solution)/shard_map/ppermute | solution.py:450
  0.5 25.4 %copy-start.3 = (bf16[512,4096]{1,0:T(8,128)(2,1)S(1)}, bf16[512,4096]{1,0:T(8,128)(2,1)}, u32[]{:S(2)}) copy-start(bf16[512,4096]{1,0:T(8,128)(2,1)} %refs_0_.10) | copy-start | bytes 12582916
  1.9 6.1 %collective-permute-start.2 = (bf16[512,512]{1,0:T(8,128)(2,1)S(1)}, bf16[512,512]{1,0:T(8,128)(2,1)S(1)}, u32[]{:S(2)}, u32[]{:S(2)}) collective-permute-start(bf16[512,512]{1,0:T(8,128)(2,1)S(1)} %get-tuple-element.65), channel_id=1, source_target_pairs={{0,4},{4,0},{8,12},{12,8},{16,20},{20,16},{24,28},{28,24},{1,5},{5... | collective-permute-start | bytes 1572872 | tf_op jit(solution)/shard_map/ppermute | solution.py:450
  2.0 11.7 %collective-permute-start.4 = (bf16[512,512]{1,0:T(8,128)(2,1)S(1)}, bf16[512,512]{1,0:T(8,128)(2,1)S(1)}, u32[]{:S(2)}, u32[]{:S(2)}) collective-permute-start(bf16[512,512]{1,0:T(8,128)(2,1)S(1)} %get-tuple-element.66.refs_2_), channel_id=1, source_target_pairs={{0,8},{4,20},{8,0},{12,28},{16,24},{20,4},{24,16},{28,12},{1,9},{5... | collective-permute-start | bytes 1572872 | tf_op jit(solution)/shard_map/ppermute | solution.py:48
  8.0 14.9 %collective-permute-start.6 = (bf16[512,512]{1,0:T(8,128)(2,1)S(1)}, bf16[512,512]{1,0:T(8,128)(2,1)S(1)}, u32[]{:S(2)}, u32[]{:S(2)}) collective-permute-start(bf16[512,512]{1,0:T(8,128)(2,1)S(1)} %collective-permute-done.2.refs_3_), channel_id=1, source_target_pairs={{0,8},{4,20},{8,0},{12,28},{16,24},{20,4},{24,16},{28,12},{1,9},{5... | collective-permute-start | bytes 1572872 | tf_op jit(solution)/shard_map/ppermute | solution.py:48
  10.8 18.4 %collective-permute-start.1 = (bf16[512,512]{1,0:T(8,128)(2,1)S(1)}, bf16[512,512]{1,0:T(8,128)(2,1)S(1)}, u32[]{:S(2)}, u32[]{:S(2)}) collective-permute-start(bf16[512,512]{1,0:T(8,128)(2,1)S(1)} %get-tuple-element.66.refs_2_), channel_id=1, source_target_pairs={{0,16},{4,12},{8,24},{12,4},{16,0},{20,28},{24,8},{28,20},{1,17},{... | collective-permute-start | bytes 1572872 | tf_op jit(solution)/shard_map/ppermute | solution.py:48
  13.7 15.6 %collective-permute-start.8 = (bf16[512,512]{1,0:T(8,128)(2,1)S(1)}, bf16[512,512]{1,0:T(8,128)(2,1)S(1)}, u32[]{:S(2)}, u32[]{:S(2)}) collective-permute-start(bf16[512,512]{1,0:T(8,128)(2,1)S(1)} %get-tuple-element.63), channel_id=1, source_target_pairs={{0,4},{4,0},{8,12},{12,8},{16,20},{20,16},{24,28},{28,24},{1,5},{5... | collective-permute-start | bytes 1572872 | tf_op jit(solution)/shard_map/ppermute | solution.py:450
  13.7 20.6 %collective-permute-start.3 = (bf16[512,512]{1,0:T(8,128)(2,1)S(1)}, bf16[512,512]{1,0:T(8,128)(2,1)S(1)}, u32[]{:S(2)}, u32[]{:S(2)}) collective-permute-start(bf16[512,512]{1,0:T(8,128)(2,1)S(1)} %collective-permute-done.2.refs_3_), channel_id=1, source_target_pairs={{0,16},{4,12},{8,24},{12,4},{16,0},{20,28},{24,8},{28,20},{1,17},{... | collective-permute-start | bytes 1572872 | tf_op jit(solution)/shard_map/ppermute | solution.py:48
  22.8 11.5 %collective-permute-start.5 = (bf16[512,512]{1,0:T(8,128)(2,1)S(1)}, bf16[512,512]{1,0:T(8,128)(2,1)S(1)}, u32[]{:S(2)}, u32[]{:S(2)}) collective-permute-start(bf16[512,512]{1,0:T(8,128)(2,1)S(1)} %collective-permute-done.4.refs_4_), channel_id=1, source_target_pairs={{0,16},{4,12},{8,24},{12,4},{16,0},{20,28},{24,8},{28,20},{1,17},{... | collective-permute-start | bytes 1572872 | tf_op jit(solution)/shard_map/ppermute | solution.py:48
  25.9 14.1 %collective-permute-start.7 = (bf16[512,512]{1,0:T(8,128)(2,1)S(1)}, bf16[512,512]{1,0:T(8,128)(2,1)S(1)}, u32[]{:S(2)}, u32[]{:S(2)}) collective-permute-start(bf16[512,512]{1,0:T(8,128)(2,1)S(1)} %collective-permute-done.6.refs_5_), channel_id=1, source_target_pairs={{0,16},{4,12},{8,24},{12,4},{16,0},{20,28},{24,8},{28,20},{1,17},{... | collective-permute-start | bytes 1572872 | tf_op jit(solution)/shard_map/ppermute | solution.py:48
  44.1 6.4 %collective-permute-start.10 = (bf16[4,64,512]{2,1,0:T(8,128)(2,1)S(1)}, bf16[4,64,512]{2,1,0:T(8,128)(2,1)S(1)}, u32[]{:S(2)}, u32[]{:S(2)}) collective-permute-start(bf16[4,64,512]{2,1,0:T(8,128)(2,1)S(1)} %get-tuple-element.36), channel_id=1, source_target_pairs={{0,16},{4,12},{8,24},{12,4},{16,0},{20,28},{24,8},{28,20},{1,17},{... | collective-permute-start | bytes 786440 | tf_op jit(solution)/shard_map/ppermute | solution.py:48
  45.9 8.7 %collective-permute-start.9 = (bf16[4,64,512]{2,1,0:T(8,128)(2,1)S(1)}, bf16[4,64,512]{2,1,0:T(8,128)(2,1)S(1)}, u32[]{:S(2)}, u32[]{:S(2)}) collective-permute-start(bf16[4,64,512]{2,1,0:T(8,128)(2,1)S(1)} %get-tuple-element.34), channel_id=1, source_target_pairs={{0,16},{4,12},{8,24},{12,4},{16,0},{20,28},{24,8},{28,20},{1,17},{... | collective-permute-start | bytes 786440 | tf_op jit(solution)/shard_map/ppermute | solution.py:48
  50.6 8.6 %collective-permute-start.11 = (bf16[4,64,512]{2,1,0:T(8,128)(2,1)S(1)}, bf16[4,64,512]{2,1,0:T(8,128)(2,1)S(1)}, u32[]{:S(2)}, u32[]{:S(2)}) collective-permute-start(bf16[4,64,512]{2,1,0:T(8,128)(2,1)S(1)} %add_terms.10.refs_2_), channel_id=1, source_target_pairs={{0,8},{4,20},{8,0},{12,28},{16,24},{20,4},{24,16},{28,12},{1,9},{5... | collective-permute-start | bytes 786440 | tf_op jit(solution)/shard_map/ppermute | solution.py:48
  53.0 14.0 %collective-permute-start.15 = (bf16[4,64,512]{2,1,0:T(8,128)(2,1)S(1)}, bf16[4,64,512]{2,1,0:T(8,128)(2,1)S(1)}, u32[]{:S(2)}, u32[]{:S(2)}) collective-permute-start(bf16[4,64,512]{2,1,0:T(8,128)(2,1)S(1)} %get-tuple-element.39), channel_id=1, source_target_pairs={{0,16},{4,12},{8,24},{12,4},{16,0},{20,28},{24,8},{28,20},{1,17},{... | collective-permute-start | bytes 786440 | tf_op jit(solution)/shard_map/ppermute | solution.py:48
  59.4 9.3 %collective-permute-start.12 = (bf16[64,512]{1,0:T(8,128)(2,1)S(1)}, bf16[64,512]{1,0:T(8,128)(2,1)S(1)}, u32[]{:S(2)}, u32[]{:S(2)}) collective-permute-start(bf16[64,512]{1,0:T(8,128)(2,1)S(1)} %get-tuple-element.81), channel_id=1, source_target_pairs={{0,1},{1,2},{2,3},{3,0},{4,5},{5,6},{6,7},{7,4},{8,9},{9,10},{10,1... | collective-permute-start | bytes 196616 | tf_op jit(solution)/shard_map/ppermute | solution.py:62
  61.5 7.2 %collective-permute-start.13 = (bf16[64,512]{1,0:T(8,128)(2,1)S(1)}, bf16[64,512]{1,0:T(8,128)(2,1)S(1)}, u32[]{:S(2)}, u32[]{:S(2)}) collective-permute-start(bf16[64,512]{1,0:T(8,128)(2,1)S(1)} %get-tuple-element.80), channel_id=1, source_target_pairs={{0,2},{1,3},{2,0},{3,1},{4,6},{5,7},{6,4},{7,5},{8,10},{9,11},{10,... | collective-permute-start | bytes 196616 | tf_op jit(solution)/shard_map/ppermute | solution.py:62
  64.1 4.6 %collective-permute-start.14 = (bf16[64,512]{1,0:T(8,128)(2,1)S(1)}, bf16[64,512]{1,0:T(8,128)(2,1)S(1)}, u32[]{:S(2)}, u32[]{:S(2)}) collective-permute-start(bf16[64,512]{1,0:T(8,128)(2,1)S(1)} %get-tuple-element.79), channel_id=1, source_target_pairs={{0,3},{1,0},{2,1},{3,2},{4,7},{5,4},{6,5},{7,6},{8,11},{9,8},{10,9... | collective-permute-start | bytes 196616 | tf_op jit(solution)/shard_map/ppermute | solution.py:62
  65.5 8.3 %collective-permute-start.23 = (bf16[4,64,512]{2,1,0:T(8,128)(2,1)S(1)}, bf16[4,64,512]{2,1,0:T(8,128)(2,1)S(1)}, u32[]{:S(2)}, u32[]{:S(2)}) collective-permute-start(bf16[4,64,512]{2,1,0:T(8,128)(2,1)S(1)} %get-tuple-element.40), channel_id=1, source_target_pairs={{0,16},{4,12},{8,24},{12,4},{16,0},{20,28},{24,8},{28,20},{1,17},{... | collective-permute-start | bytes 786440 | tf_op jit(solution)/shard_map/ppermute | solution.py:48
  67.0 21.5 %copy-start.12 = (f32[1,512]{1,0:T(1,128)S(1)}, f32[1,512]{1,0:T(1,128)}, u32[]{:S(2)}) copy-start(f32[1,512]{1,0:T(1,128)} %param.15) | copy-start | bytes 6148
  67.1 6.6 %collective-permute-start.24 = (bf16[4,64,512]{2,1,0:T(8,128)(2,1)S(1)}, bf16[4,64,512]{2,1,0:T(8,128)(2,1)S(1)}, u32[]{:S(2)}, u32[]{:S(2)}) collective-permute-start(bf16[4,64,512]{2,1,0:T(8,128)(2,1)S(1)} %add_terms.12.refs_4_), channel_id=1, source_target_pairs={{0,8},{4,20},{8,0},{12,28},{16,24},{20,4},{24,16},{28,12},{1,9},{5... | collective-permute-start | bytes 786440 | tf_op jit(solution)/shard_map/ppermute | solution.py:48
  68.7 8.7 %collective-permute-start.16 = (bf16[4,64,512]{2,1,0:T(8,128)(2,1)S(1)}, bf16[4,64,512]{2,1,0:T(8,128)(2,1)S(1)}, u32[]{:S(2)}, u32[]{:S(2)}) collective-permute-start(bf16[4,64,512]{2,1,0:T(8,128)(2,1)S(1)} %stack_planes.4.refs_3_.refs_0_), channel_id=1, source_target_pairs={{0,8},{4,20},{8,0},{12,28},{16,24},{20,4},{24,16},{28,12},{1,9},{5... | collective-permute-start | bytes 786440 | tf_op jit(solution)/shard_map/ppermute | solution.py:48
  69.5 18.5 %collective-permute-start.17 = (bf16[4,64,512]{2,1,0:T(8,128)(2,1)S(1)}, bf16[4,64,512]{2,1,0:T(8,128)(2,1)S(1)}, u32[]{:S(2)}, u32[]{:S(2)}) collective-permute-start(bf16[4,64,512]{2,1,0:T(8,128)(2,1)S(1)} %stack_planes.4.refs_3_.refs_0_), channel_id=1, source_target_pairs={{0,16},{4,12},{8,24},{12,4},{16,0},{20,28},{24,8},{28,20},{1,17},{... | collective-permute-start | bytes 786440 | tf_op jit(solution)/shard_map/ppermute | solution.py:48
  77.4 11.0 %collective-permute-start.18 = (bf16[4,64,512]{2,1,0:T(8,128)(2,1)S(1)}, bf16[4,64,512]{2,1,0:T(8,128)(2,1)S(1)}, u32[]{:S(2)}, u32[]{:S(2)}) collective-permute-start(bf16[4,64,512]{2,1,0:T(8,128)(2,1)S(1)} %collective-permute-done.16.refs_1_), channel_id=1, source_target_pairs={{0,16},{4,12},{8,24},{12,4},{16,0},{20,28},{24,8},{28,20},{1,17},{... | collective-permute-start | bytes 786440 | tf_op jit(solution)/shard_map/ppermute | solution.py:48
  77.4 6.2 %collective-permute-start.25 = (bf16[64,512]{1,0:T(8,128)(2,1)S(1)}, bf16[64,512]{1,0:T(8,128)(2,1)S(1)}, u32[]{:S(2)}, u32[]{:S(2)}) collective-permute-start(bf16[64,512]{1,0:T(8,128)(2,1)S(1)} %get-tuple-element.77), channel_id=1, source_target_pairs={{0,1},{1,2},{2,3},{3,0},{4,5},{5,6},{6,7},{7,4},{8,9},{9,10},{10,1... | collective-permute-start | bytes 196616 | tf_op jit(solution)/shard_map/ppermute | solution.py:62
  78.2 6.6 %collective-permute-start.26 = (bf16[64,512]{1,0:T(8,128)(2,1)S(1)}, bf16[64,512]{1,0:T(8,128)(2,1)S(1)}, u32[]{:S(2)}, u32[]{:S(2)}) collective-permute-start(bf16[64,512]{1,0:T(8,128)(2,1)S(1)} %get-tuple-element.76), channel_id=1, source_target_pairs={{0,2},{1,3},{2,0},{3,1},{4,6},{5,7},{6,4},{7,5},{8,10},{9,11},{10,... | collective-permute-start | bytes 196616 | tf_op jit(solution)/shard_map/ppermute | solution.py:62
  81.1 4.4 %collective-permute-start.27 = (bf16[64,512]{1,0:T(8,128)(2,1)S(1)}, bf16[64,512]{1,0:T(8,128)(2,1)S(1)}, u32[]{:S(2)}, u32[]{:S(2)}) collective-permute-start(bf16[64,512]{1,0:T(8,128)(2,1)S(1)} %get-tuple-element.75), channel_id=1, source_target_pairs={{0,3},{1,0},{2,1},{3,2},{4,7},{5,4},{6,5},{7,6},{8,11},{9,8},{10,9... | collective-permute-start | bytes 196616 | tf_op jit(solution)/shard_map/ppermute | solution.py:62
  83.6 5.7 %collective-permute-start.19 = (bf16[4,64,512]{2,1,0:T(8,128)(2,1)S(1)}, bf16[4,64,512]{2,1,0:T(8,128)(2,1)S(1)}, u32[]{:S(2)}, u32[]{:S(2)}) collective-permute-start(bf16[4,64,512]{2,1,0:T(8,128)(2,1)S(1)} %stack_planes.4.refs_3_.refs_0_), channel_id=1, source_target_pairs={{0,4},{4,0},{8,12},{12,8},{16,20},{20,16},{24,28},{28,24},{1,5},{5... | collective-permute-start | bytes 786440 | tf_op jit(solution)/shard_map/ppermute | solution.py:450
  86.1 7.1 %collective-permute-start.28 = (bf16[4,64,512]{2,1,0:T(8,128)(2,1)}, bf16[4,64,512]{2,1,0:T(8,128)(2,1)}, u32[]{:S(2)}, u32[]{:S(2)}) collective-permute-start(bf16[4,64,512]{2,1,0:T(8,128)(2,1)} %stack_planes.5.refs_0_), channel_id=1, source_target_pairs={{0,8},{4,20},{8,0},{12,28},{16,24},{20,4},{24,16},{28,12},{1,9},{5... | collective-permute-start | bytes 786440 | tf_op jit(solution)/shard_map/ppermute | solution.py:48
  87.9 7.8 %collective-permute-start.21 = (bf16[4,64,512]{2,1,0:T(8,128)(2,1)S(1)}, bf16[4,64,512]{2,1,0:T(8,128)(2,1)S(1)}, u32[]{:S(2)}, u32[]{:S(2)}) collective-permute-start(bf16[4,64,512]{2,1,0:T(8,128)(2,1)S(1)} %collective-permute-done.16.refs_1_), channel_id=1, source_target_pairs={{0,4},{4,0},{8,12},{12,8},{16,20},{20,16},{24,28},{28,24},{1,5},{5... | collective-permute-start | bytes 786440 | tf_op jit(solution)/shard_map/ppermute | solution.py:450
  87.9 7.8 %collective-permute-start.20 = (bf16[4,64,512]{2,1,0:T(8,128)(2,1)S(1)}, bf16[4,64,512]{2,1,0:T(8,128)(2,1)S(1)}, u32[]{:S(2)}, u32[]{:S(2)}) collective-permute-start(bf16[4,64,512]{2,1,0:T(8,128)(2,1)S(1)} %collective-permute-done.17.refs_2_), channel_id=1, source_target_pairs={{0,4},{4,0},{8,12},{12,8},{16,20},{20,16},{24,28},{28,24},{1,5},{5... | collective-permute-start | bytes 786440 | tf_op jit(solution)/shard_map/ppermute | solution.py:450
  88.4 7.3 %collective-permute-start.22 = (bf16[4,64,512]{2,1,0:T(8,128)(2,1)S(1)}, bf16[4,64,512]{2,1,0:T(8,128)(2,1)S(1)}, u32[]{:S(2)}, u32[]{:S(2)}) collective-permute-start(bf16[4,64,512]{2,1,0:T(8,128)(2,1)S(1)} %collective-permute-done.18.refs_3_), channel_id=1, source_target_pairs={{0,4},{4,0},{8,12},{12,8},{16,20},{20,16},{24,28},{28,24},{1,5},{5... | collective-permute-start | bytes 786440 | tf_op jit(solution)/shard_map/ppermute | solution.py:450
  89.4 27.7 %collective-permute-start.35 = (bf16[4,64,512]{2,1,0:T(8,128)(2,1)}, bf16[4,64,512]{2,1,0:T(8,128)(2,1)S(1)}, u32[]{:S(2)}, u32[]{:S(2)}) collective-permute-start(bf16[4,64,512]{2,1,0:T(8,128)(2,1)} %stack_planes.5.refs_0_), channel_id=1, source_target_pairs={{0,16},{4,12},{8,24},{12,4},{16,0},{20,28},{24,8},{28,20},{1,17},{... | collective-permute-start | bytes 786440 | tf_op jit(solution)/shard_map/ppermute | solution.py:48
  93.2 24.3 %collective-permute-start.36 = (bf16[4,64,512]{2,1,0:T(8,128)(2,1)}, bf16[4,64,512]{2,1,0:T(8,128)(2,1)S(1)}, u32[]{:S(2)}, u32[]{:S(2)}) collective-permute-start(bf16[4,64,512]{2,1,0:T(8,128)(2,1)} %collective-permute-done.28.refs_10_.refs_1_), channel_id=1, source_target_pairs={{0,16},{4,12},{8,24},{12,4},{16,0},{20,28},{24,8},{28,20},{1,17},{... | collective-permute-start | bytes 786440 | tf_op jit(solution)/shard_map/ppermute | solution.py:48
  116.4 1.6 collective-permute-start.30
  116.5 4.6 %collective-permute-start.31 = (bf16[4,64,512]{2,1,0:T(8,128)(2,1)S(1)}, bf16[4,64,512]{2,1,0:T(8,128)(2,1)S(1)}, u32[]{:S(2)}, u32[]{:S(2)}) collective-permute-start(bf16[4,64,512]{2,1,0:T(8,128)(2,1)S(1)} %get-tuple-element.46), channel_id=1, source_target_pairs={{0,4},{4,0},{8,12},{12,8},{16,20},{20,16},{24,28},{28,24},{1,5},{5... | collective-permute-start | bytes 786440 | tf_op jit(solution)/shard_map/ppermute | solution.py:450
  117.0 4.7 %collective-permute-start.37 = (bf16[4,64,512]{2,1,0:T(8,128)(2,1)}, bf16[4,64,512]{2,1,0:T(8,128)(2,1)S(1)}, u32[]{:S(2)}, u32[]{:S(2)}) collective-permute-start(bf16[4,64,512]{2,1,0:T(8,128)(2,1)} %stack_planes.5.refs_0_), channel_id=1, source_target_pairs={{0,4},{4,0},{8,12},{12,8},{16,20},{20,16},{24,28},{28,24},{1,5},{5... | collective-permute-start | bytes 786440 | tf_op jit(solution)/shard_map/ppermute | solution.py:450
  117.1 4.7 %collective-permute-start.39 = (bf16[4,64,512]{2,1,0:T(8,128)(2,1)}, bf16[4,64,512]{2,1,0:T(8,128)(2,1)S(1)}, u32[]{:S(2)}, u32[]{:S(2)}) collective-permute-start(bf16[4,64,512]{2,1,0:T(8,128)(2,1)} %collective-permute-done.28.refs_10_.refs_1_), channel_id=1, source_target_pairs={{0,4},{4,0},{8,12},{12,8},{16,20},{20,16},{24,28},{28,24},{1,5},{5... | collective-permute-start | bytes 786440 | tf_op jit(solution)/shard_map/ppermute | solution.py:450
  117.5 4.3 %collective-permute-start.38 = (bf16[4,64,512]{2,1,0:T(8,128)(2,1)S(1)}, bf16[4,64,512]{2,1,0:T(8,128)(2,1)S(1)}, u32[]{:S(2)}, u32[]{:S(2)}) collective-permute-start(bf16[4,64,512]{2,1,0:T(8,128)(2,1)S(1)} %collective-permute-done.35.refs_2_), channel_id=1, source_target_pairs={{0,4},{4,0},{8,12},{12,8},{16,20},{20,16},{24,28},{28,24},{1,5},{5... | collective-permute-start | bytes 786440 | tf_op jit(solution)/shard_map/ppermute | solution.py:450
  118.0 3.8 %collective-permute-start.40 = (bf16[4,64,512]{2,1,0:T(8,128)(2,1)S(1)}, bf16[4,64,512]{2,1,0:T(8,128)(2,1)S(1)}, u32[]{:S(2)}, u32[]{:S(2)}) collective-permute-start(bf16[4,64,512]{2,1,0:T(8,128)(2,1)S(1)} %collective-permute-done.36.refs_3_), channel_id=1, source_target_pairs={{0,4},{4,0},{8,12},{12,8},{16,20},{20,16},{24,28},{28,24},{1,5},{5... | collective-permute-start | bytes 786440 | tf_op jit(solution)/shard_map/ppermute | solution.py:450
  121.1 17.3 %collective-permute-start.33 = (bf16[4,64,512]{2,1,0:T(8,128)(2,1)S(1)}, bf16[4,64,512]{2,1,0:T(8,128)(2,1)S(1)}, u32[]{:S(2)}, u32[]{:S(2)}) collective-permute-start(bf16[4,64,512]{2,1,0:T(8,128)(2,1)S(1)} %get-tuple-element.49), channel_id=1, source_target_pairs={{0,4},{4,0},{8,12},{12,8},{16,20},{20,16},{24,28},{28,24},{1,5},{5... | collective-permute-start | bytes 786440 | tf_op jit(solution)/shard_map/ppermute | solution.py:450
  121.7 16.8 %collective-permute-start.34 = (bf16[4,64,512]{2,1,0:T(8,128)(2,1)S(1)}, bf16[4,64,512]{2,1,0:T(8,128)(2,1)S(1)}, u32[]{:S(2)}, u32[]{:S(2)}) collective-permute-start(bf16[4,64,512]{2,1,0:T(8,128)(2,1)S(1)} %get-tuple-element.50), channel_id=1, source_target_pairs={{0,16},{4,12},{8,24},{12,4},{16,0},{20,28},{24,8},{28,20},{1,17},{... | collective-permute-start | bytes 786440 | tf_op jit(solution)/shard_map/ppermute | solution.py:48
  135.7 6.7 %collective-permute-start.42 = (bf16[4,64,512]{2,1,0:T(8,128)(2,1)S(1)}, bf16[4,64,512]{2,1,0:T(8,128)(2,1)S(1)}, u32[]{:S(2)}, u32[]{:S(2)}) collective-permute-start(bf16[4,64,512]{2,1,0:T(8,128)(2,1)S(1)} %get-tuple-element.53), channel_id=1, source_target_pairs={{0,4},{4,0},{8,12},{12,8},{16,20},{20,16},{24,28},{28,24},{1,5},{5... | collective-permute-start | bytes 786440 | tf_op jit(solution)/shard_map/ppermute | solution.py:450
  138.0 6.2 %collective-permute-start.43 = (bf16[4,64,512]{2,1,0:T(8,128)(2,1)S(1)}, bf16[4,64,512]{2,1,0:T(8,128)(2,1)S(1)}, u32[]{:S(2)}, u32[]{:S(2)}) collective-permute-start(bf16[4,64,512]{2,1,0:T(8,128)(2,1)S(1)} %get-tuple-element.55), channel_id=1, source_target_pairs={{0,4},{4,0},{8,12},{12,8},{16,20},{20,16},{24,28},{28,24},{1,5},{5... | collective-permute-start | bytes 786440 | tf_op jit(solution)/shard_map/ppermute | solution.py:450
  138.0 6.8 %collective-permute-start.29 = (bf16[4,64,512]{2,1,0:T(8,128)(2,1)S(1)}, bf16[4,64,512]{2,1,0:T(8,128)(2,1)S(1)}, u32[]{:S(2)}, u32[]{:S(2)}) collective-permute-start(bf16[4,64,512]{2,1,0:T(8,128)(2,1)S(1)} %get-tuple-element.41.refs_4_), channel_id=1, source_target_pairs={{0,4},{4,0},{8,12},{12,8},{16,20},{20,16},{24,28},{28,24},{1,5},{5... | collective-permute-start | bytes 786440 | tf_op jit(solution)/shard_map/ppermute | solution.py:450
  138.5 6.4 %collective-permute-start.32 = (bf16[4,64,512]{2,1,0:T(8,128)(2,1)S(1)}, bf16[4,64,512]{2,1,0:T(8,128)(2,1)S(1)}, u32[]{:S(2)}, u32[]{:S(2)}) collective-permute-start(bf16[4,64,512]{2,1,0:T(8,128)(2,1)S(1)} %get-tuple-element.47.refs_10_), channel_id=1, source_target_pairs={{0,16},{4,12},{8,24},{12,4},{16,0},{20,28},{24,8},{28,20},{1,17},{... | collective-permute-start | bytes 786440 | tf_op jit(solution)/shard_map/ppermute | solution.py:48
  138.5 12.5 %collective-permute-start.47 = (bf16[4,64,512]{2,1,0:T(8,128)(2,1)S(1)}, bf16[4,64,512]{2,1,0:T(8,128)(2,1)S(1)}, u32[]{:S(2)}, u32[]{:S(2)}) collective-permute-start(bf16[4,64,512]{2,1,0:T(8,128)(2,1)S(1)} %get-tuple-element.59), channel_id=1, source_target_pairs={{0,4},{4,0},{8,12},{12,8},{16,20},{20,16},{24,28},{28,24},{1,5},{5... | collective-permute-start | bytes 786440 | tf_op jit(solution)/shard_map/ppermute | solution.py:450
  142.4 8.5 %collective-permute-start.41 = (bf16[4,64,512]{2,1,0:T(8,128)(2,1)S(1)}, bf16[4,64,512]{2,1,0:T(8,128)(2,1)S(1)}, u32[]{:S(2)}, u32[]{:S(2)}) collective-permute-start(bf16[4,64,512]{2,1,0:T(8,128)(2,1)S(1)} %add_terms.15.refs_4_), channel_id=1, source_target_pairs={{0,8},{4,20},{8,0},{12,28},{16,24},{20,4},{24,16},{28,12},{1,9},{5... | collective-permute-start | bytes 786440 | tf_op jit(solution)/shard_map/ppermute | solution.py:48
  144.3 6.7 %collective-permute-start.48 = (bf16[4,64,512]{2,1,0:T(8,128)(2,1)S(1)}, bf16[4,64,512]{2,1,0:T(8,128)(2,1)S(1)}, u32[]{:S(2)}, u32[]{:S(2)}) collective-permute-start(bf16[4,64,512]{2,1,0:T(8,128)(2,1)S(1)} %get-tuple-element.60), channel_id=1, source_target_pairs={{0,16},{4,12},{8,24},{12,4},{16,0},{20,28},{24,8},{28,20},{1,17},{... | collective-permute-start | bytes 786440 | tf_op jit(solution)/shard_map/ppermute | solution.py:48
  144.8 19.2 %collective-permute-start.52 = (bf16[4,64,512]{2,1,0:T(8,128)(2,1)S(1)}, bf16[4,64,512]{2,1,0:T(8,128)(2,1)S(1)}, u32[]{:S(2)}, u32[]{:S(2)}) collective-permute-start(bf16[4,64,512]{2,1,0:T(8,128)(2,1)S(1)} %get-tuple-element.51.refs_3_), channel_id=1, source_target_pairs={{0,4},{4,0},{8,12},{12,8},{16,20},{20,16},{24,28},{28,24},{1,5},{5... | collective-permute-start | bytes 786440 | tf_op jit(solution)/shard_map/ppermute | solution.py:450
  144.9 19.2 %collective-permute-start.53 = (bf16[4,64,512]{2,1,0:T(8,128)(2,1)S(1)}, bf16[4,64,512]{2,1,0:T(8,128)(2,1)S(1)}, u32[]{:S(2)}, u32[]{:S(2)}) collective-permute-start(bf16[4,64,512]{2,1,0:T(8,128)(2,1)S(1)} %get-tuple-element.57.refs_4_), channel_id=1, source_target_pairs={{0,16},{4,12},{8,24},{12,4},{16,0},{20,28},{24,8},{28,20},{1,17},{... | collective-permute-start | bytes 786440 | tf_op jit(solution)/shard_map/ppermute | solution.py:48
  151.1 13.0 %collective-permute-start.54 = (bf16[4,64,512]{2,1,0:T(8,128)(2,1)S(1)}, bf16[4,64,512]{2,1,0:T(8,128)(2,1)S(1)}, u32[]{:S(2)}, u32[]{:S(2)}) collective-permute-start(bf16[4,64,512]{2,1,0:T(8,128)(2,1)S(1)} %add_terms.18.refs_4_), channel_id=1, source_target_pairs={{0,8},{4,20},{8,0},{12,28},{16,24},{20,4},{24,16},{28,12},{1,9},{5... | collective-permute-start | bytes 786440 | tf_op jit(solution)/shard_map/ppermute | solution.py:48
  153.7 6.1 %collective-permute-start.44 = (bf16[64,512]{1,0:T(8,128)(2,1)S(1)}, bf16[64,512]{1,0:T(8,128)(2,1)S(1)}, u32[]{:S(2)}, u32[]{:S(2)}) collective-permute-start(bf16[64,512]{1,0:T(8,128)(2,1)S(1)} %get-tuple-element.73), channel_id=1, source_target_pairs={{0,1},{1,2},{2,3},{3,0},{4,5},{5,6},{6,7},{7,4},{8,9},{9,10},{10,1... | collective-permute-start | bytes 196616 | tf_op jit(solution)/shard_map/ppermute | solution.py:62
  155.1 6.8 %collective-permute-start.45 = (bf16[64,512]{1,0:T(8,128)(2,1)S(1)}, bf16[64,512]{1,0:T(8,128)(2,1)S(1)}, u32[]{:S(2)}, u32[]{:S(2)}) collective-permute-start(bf16[64,512]{1,0:T(8,128)(2,1)S(1)} %get-tuple-element.72), channel_id=1, source_target_pairs={{0,2},{1,3},{2,0},{3,1},{4,6},{5,7},{6,4},{7,5},{8,10},{9,11},{10,... | collective-permute-start | bytes 196616 | tf_op jit(solution)/shard_map/ppermute | solution.py:62
  159.8 4.3 %collective-permute-start.46 = (bf16[64,512]{1,0:T(8,128)(2,1)S(1)}, bf16[64,512]{1,0:T(8,128)(2,1)S(1)}, u32[]{:S(2)}, u32[]{:S(2)}) collective-permute-start(bf16[64,512]{1,0:T(8,128)(2,1)S(1)} %get-tuple-element.71), channel_id=1, source_target_pairs={{0,3},{1,0},{2,1},{3,2},{4,7},{5,4},{6,5},{7,6},{8,11},{9,8},{10,9... | collective-permute-start | bytes 196616 | tf_op jit(solution)/shard_map/ppermute | solution.py:62
  164.3 6.2 %collective-permute-start.55 = (bf16[64,512]{1,0:T(8,128)(2,1)S(1)}, bf16[64,512]{1,0:T(8,128)(2,1)S(1)}, u32[]{:S(2)}, u32[]{:S(2)}) collective-permute-start(bf16[64,512]{1,0:T(8,128)(2,1)S(1)} %get-tuple-element.69), channel_id=1, source_target_pairs={{0,1},{1,2},{2,3},{3,0},{4,5},{5,6},{6,7},{7,4},{8,9},{9,10},{10,1... | collective-permute-start | bytes 196616 | tf_op jit(solution)/shard_map/ppermute | solution.py:62
  164.4 7.4 %collective-permute-start.56 = (bf16[64,512]{1,0:T(8,128)(2,1)S(1)}, bf16[64,512]{1,0:T(8,128)(2,1)S(1)}, u32[]{:S(2)}, u32[]{:S(2)}) collective-permute-start(bf16[64,512]{1,0:T(8,128)(2,1)S(1)} %get-tuple-element.68), channel_id=1, source_target_pairs={{0,2},{1,3},{2,0},{3,1},{4,6},{5,7},{6,4},{7,5},{8,10},{9,11},{10,... | collective-permute-start | bytes 196616 | tf_op jit(solution)/shard_map/ppermute | solution.py:62
  168.4 4.3 %collective-permute-start.57 = (bf16[64,512]{1,0:T(8,128)(2,1)S(1)}, bf16[64,512]{1,0:T(8,128)(2,1)S(1)}, u32[]{:S(2)}, u32[]{:S(2)}) collective-permute-start(bf16[64,512]{1,0:T(8,128)(2,1)S(1)} %get-tuple-element.67), channel_id=1, source_target_pairs={{0,3},{1,0},{2,1},{3,2},{4,7},{5,4},{6,5},{7,6},{8,11},{9,8},{10,9... | collective-permute-start | bytes 196616 | tf_op jit(solution)/shard_map/ppermute | solution.py:62
  168.4 9.2 %collective-permute-start.49 = (bf16[4,64,512]{2,1,0:T(8,128)(2,1)S(1)}, bf16[4,64,512]{2,1,0:T(8,128)(2,1)S(1)}, u32[]{:S(2)}, u32[]{:S(2)}) collective-permute-start(bf16[4,64,512]{2,1,0:T(8,128)(2,1)S(1)} %stack_planes.6.refs_4_.refs_2_), channel_id=1, source_target_pairs={{0,8},{4,20},{8,0},{12,28},{16,24},{20,4},{24,16},{28,12},{1,9},{5... | collective-permute-start | bytes 786440 | tf_op jit(solution)/shard_map/ppermute | solution.py:48
  172.6 10.5 %collective-permute-start.58 = (bf16[4,64,512]{2,1,0:T(8,128)(2,1)S(1)}, bf16[4,64,512]{2,1,0:T(8,128)(2,1)S(1)}, u32[]{:S(2)}, u32[]{:S(2)}) collective-permute-start(bf16[4,64,512]{2,1,0:T(8,128)(2,1)S(1)} %stack_planes.7.refs_6_), channel_id=1, source_target_pairs={{0,8},{4,20},{8,0},{12,28},{16,24},{20,4},{24,16},{28,12},{1,9},{5... | collective-permute-start | bytes 786440 | tf_op jit(solution)/shard_map/ppermute | solution.py:48
  172.7 10.4 %collective-permute-start.50 = (bf16[4,64,512]{2,1,0:T(8,128)(2,1)S(1)}, bf16[4,64,512]{2,1,0:T(8,128)(2,1)S(1)}, u32[]{:S(2)}, u32[]{:S(2)}) collective-permute-start(bf16[4,64,512]{2,1,0:T(8,128)(2,1)S(1)} %stack_planes.6.refs_4_.refs_2_), channel_id=1, source_target_pairs={{0,16},{4,12},{8,24},{12,4},{16,0},{20,28},{24,8},{28,20},{1,17},{... | collective-permute-start | bytes 786440 | tf_op jit(solution)/shard_map/ppermute | solution.py:48
  174.9 8.3 %collective-permute-start.59 = (bf16[4,64,512]{2,1,0:T(8,128)(2,1)S(1)}, bf16[4,64,512]{2,1,0:T(8,128)(2,1)S(1)}, u32[]{:S(2)}, u32[]{:S(2)}) collective-permute-start(bf16[4,64,512]{2,1,0:T(8,128)(2,1)S(1)} %stack_planes.7.refs_6_), channel_id=1, source_target_pairs={{0,16},{4,12},{8,24},{12,4},{16,0},{20,28},{24,8},{28,20},{1,17},{... | collective-permute-start | bytes 786440 | tf_op jit(solution)/shard_map/ppermute | solution.py:48
  177.5 7.3 %collective-permute-start.51 = (bf16[4,64,512]{2,1,0:T(8,128)(2,1)S(1)}, bf16[4,64,512]{2,1,0:T(8,128)(2,1)S(1)}, u32[]{:S(2)}, u32[]{:S(2)}) collective-permute-start(bf16[4,64,512]{2,1,0:T(8,128)(2,1)S(1)} %collective-permute-done.49.refs_3_), channel_id=1, source_target_pairs={{0,16},{4,12},{8,24},{12,4},{16,0},{20,28},{24,8},{28,20},{1,17},{... | collective-permute-start | bytes 786440 | tf_op jit(solution)/shard_map/ppermute | solution.py:48
  183.2 6.4 %collective-permute-start.60 = (bf16[4,64,512]{2,1,0:T(8,128)(2,1)S(1)}, bf16[4,64,512]{2,1,0:T(8,128)(2,1)S(1)}, u32[]{:S(2)}, u32[]{:S(2)}) collective-permute-start(bf16[4,64,512]{2,1,0:T(8,128)(2,1)S(1)} %collective-permute-done.58.refs_7_), channel_id=1, source_target_pairs={{0,16},{4,12},{8,24},{12,4},{16,0},{20,28},{24,8},{28,20},{1,17},{... | collective-permute-start | bytes 786440 | tf_op jit(solution)/shard_map/ppermute | solution.py:48
  191.0 2.0 %collective-permute-start.61 = (bf16[512,512]{1,0:T(8,128)(2,1)S(1)}, bf16[512,512]{1,0:T(8,128)(2,1)S(1)}, u32[]{:S(2)}, u32[]{:S(2)}) collective-permute-start(bf16[512,512]{1,0:T(8,128)(2,1)S(1)} %bitcast.57), channel_id=1, source_target_pairs={{0,4},{4,0},{8,12},{12,8},{16,20},{20,16},{24,28},{28,24},{1,5},{5... | collective-permute-start | bytes 1572872 | tf_op jit(solution)/shard_map/ppermute | solution.py:450
  (17 other events, 106.6 us)

commit v6 on v5

--- a/solution.py
+++ b/solution.py
@@ -186,7 +186,7 @@
         out[i] = value.astype(out.dtype)
 
 
-def project(make_place, parts, own, other, weights, extra):
+def project(make_place, parts, own, other, weights, extra, unread):
     last = len(extra) > 0
     rows = own.shape[0]
     depth, half = weights[0].shape
@@ -194,17 +194,17 @@
     return call(
         lambda *refs: project_kernel(make_place, parts, len(weights), len(extra), *refs),
         jax.ShapeDtypeStruct((2, rows, half), jnp.bfloat16 if last else jnp.float32),
-        [ANY, ANY] + [VMEM] * (len(weights) + len(extra)),
+        [ANY, ANY] + [VMEM] * (len(weights) + len(extra)) + [ANY] * len(unread),
         VMEM,
         "project_last" if last else "project_first",
-        20,
+        12,
         scratch_shapes=[
             pltpu.VMEM((k, half), jnp.bfloat16),
             pltpu.VMEM((rows, k), jnp.bfloat16),
             pltpu.VMEM((rows, k), jnp.bfloat16),
             pltpu.SemaphoreType.DMA((2, len(weights))),
         ],
-    )(own, other, *weights, *extra)
+    )(own, other, *weights, *extra, *unread)
 
 
 def pick_kernel(make_place, layout, n_chip, chosen, att_ref, *refs):
@@ -231,7 +231,7 @@
 
 
 def finish_kernel(make_place, layouts, n_chip, chosen, att_ref, *refs):
-    pieces, out_ref, acc = refs[:-2], refs[-2], refs[-1]
+    pieces, outs, acc = refs[:-3], refs[-3:-1], refs[-1]
     place = make_place()
     acc[...] = att_ref[...].astype(jnp.float32)
     for g, layout in enumerate(layouts):
@@ -244,109 +244,98 @@
                 def _():
                     acc[index] = acc[index] + piece[k].astype(jnp.float32)
 
-    out_ref[...] = acc[...].astype(out_ref.dtype)
+    n = outs[0].shape[0]
+    for s, out in enumerate(outs):
+        out[...] = acc[s * n : (s + 1) * n].astype(out.dtype)
 
 
 def finish(make_place, layouts, n_chip, chosen, grains, pieces):
     return call(
         lambda *refs: finish_kernel(make_place, layouts, n_chip, *refs),
-        jax.ShapeDtypeStruct(grains.shape, grains.dtype),
+        [jax.ShapeDtypeStruct((grains.shape[0] // 2,) + grains.shape[1:], grains.dtype)] * 2,
         [SMEM] + [VMEM] * (1 + len(pieces)),
-        VMEM,
+        [VMEM] * 2,
         "add_expert_rows",
         12,
         scratch_shapes=[pltpu.VMEM(grains.shape, jnp.float32)],
     )(chosen, grains, *pieces)
 
 
+def join_kernel(make_place, own, other, out):
+    side = make_place().side
+    rows, half = out.shape[0], out.shape[1] // 2
+    for s, value in enumerate((own, other)):
+        at = pl.ds(pl.multiple_of((side ^ s) * half, half), half)
+        out[:, at] = value[...].reshape(rows, half)
+
+
+def join(make_place, own, other, rows):
+    return call(
+        lambda *refs: join_kernel(make_place, *refs),
+        jax.ShapeDtypeStruct((rows, 2 * own.shape[-1]), own.dtype),
+        [VMEM, VMEM],
+        VMEM,
+        "join_halves",
+        8,
+    )(own, other)
+
+
 def hidden_kernel(make_place, n, *refs):
     own, other, wg, wu = refs[:n], refs[n : 2 * n], *refs[2 * n : 2 * n + 2]
-    hid, xs, wgs, wus, sems = refs[-5:]
+    hid, xs = refs[-2:]
     n_z, rows, width = own[0].shape
     place = make_place()
-    n_tile, _, tile = wgs.shape
-
-    def copies(i):
-        at = pl.ds(pl.multiple_of(i * tile, tile), tile)
-        return (
-            pltpu.make_async_copy(wg.at[:, at], wgs.at[i], sems.at[0, i]),
-            pltpu.make_async_copy(wu.at[:, at], wus.at[i], sems.at[1, i]),
-        )
-
-    def start(i):
-        for c in copies(i):
-            c.start()
-
-    start(0)
-    if n_tile > 1:
-        start(1)
     for s, pieces in enumerate((own, other)):
         for z in range(n_z):
             at = (place.behind(z) * 2 + (place.side ^ s)) * width
             at = pl.ds(pl.multiple_of(at, width), width)
             for r in range(n):
                 xs[r * rows : (r + 1) * rows, at] = pieces[r][z]
+    ff = wg.shape[1]
+    tile = min(ff, 256)
 
     def one(i, carry):
-        for c in copies(i):
-            c.wait()
-
-        @pl.when(i + 2 < n_tile)
-        def _():
-            start(i + 2)
-
         at = pl.ds(pl.multiple_of(i * tile, tile), tile)
-        g = jnp.dot(xs[...], wgs[i], preferred_element_type=jnp.float32)
-        u = jnp.dot(xs[...], wus[i], preferred_element_type=jnp.float32)
+        g = jnp.dot(xs[...], wg[:, at], preferred_element_type=jnp.float32)
+        u = jnp.dot(xs[...], wu[:, at], preferred_element_type=jnp.float32)
         hid[:, at] = (g / (1.0 + jnp.exp(-g)) * u).astype(jnp.bfloat16)
         return carry
 
-    lax.fori_loop(0, n_tile, one, 0)
+    lax.fori_loop(0, ff // tile, one, 0)
 
 
 def hidden_units(make_place, own, other, w_gate, w_up, after):
     n = len(own)
     n_z, rows, width = own[0].shape
     model_width, ff = w_gate.shape
-    tile = min(ff, 256)
-    extra = [] if after is None else [after]
     return call(
         lambda *refs: hidden_kernel(make_place, n, *refs),
         jax.ShapeDtypeStruct((n * rows, ff), jnp.bfloat16),
-        [VMEM] * (2 * n) + [ANY] * 2 + [ANY] * len(extra),
+        [VMEM] * (2 * n + 2) + [ANY],
         VMEM,
         "expert_hidden",
-        28,
-        scratch_shapes=[
-            pltpu.VMEM((n * rows, model_width), jnp.bfloat16),
-            pltpu.VMEM((ff // tile, model_width, tile), jnp.bfloat16),
-            pltpu.VMEM((ff // tile, model_width, tile), jnp.bfloat16),
-            pltpu.SemaphoreType.DMA((2, ff // tile)),
-        ],
-    )(*own, *other, w_gate, w_up, *extra)
-
-
-def down_kernel(make_place, layout, order, s, counts, hid, wd, values, *refs):
-    outs, wds, sems = refs[-2 - len(order) : -2], refs[-2], refs[-1]
+        12,
+        scratch_shapes=[pltpu.VMEM((n * rows, model_width), jnp.bfloat16)],
+    )(*own, *other, w_gate, w_up, after)
+
+
+def down_kernel(make_place, layout, order, s, counts, hid, wd, values, after, *outs):
     n = len(order)
     n_z, rows, width = outs[0].shape
     place = make_place()
-    copies = []
+    count = counts[place.expert]
+    n_row = values.shape[1]
+    row_of = lax.broadcasted_iota(jnp.int32, (rows, n_row), 0)
+    at_of = lax.broadcasted_iota(jnp.int32, (rows, n_row), 1)
+    scale = []
+    for r in range(n):
+        row = layout.first_row(place, r)
+        chosen = (at_of == row_of + row) & (lax.div(row, BLK) < count)
+        scale.append(jnp.sum(jnp.where(chosen, values[...], 0.0), axis=1, keepdims=True))
     for z in range(n_z):
         at = (place.ahead(z) * 2 + (place.side ^ s)) * width
         at = pl.ds(pl.multiple_of(at, width), width)
-        copies.append(pltpu.make_async_copy(wd.at[:, at], wds.at[z], sems.at[z]))
-    for c in copies:
-        c.start()
-    count = counts[place.expert]
-    scale = []
-    for r in range(n):
-        row = layout.first_row(place, r)
-        value = values[pl.ds(pl.multiple_of(row, rows), rows), :]
-        scale.append(jnp.where(lax.div(row, BLK) < count, value, jnp.zeros_like(value)))
-    for z in range(n_z):
-        copies[z].wait()
-        part = jnp.dot(hid[...], wds[z], preferred_element_type=jnp.float32)
+        part = jnp.dot(hid[...], wd[:, at], preferred_element_type=jnp.float32)
         for r in range(n):
             value = part[r * rows : (r + 1) * rows] * scale[r]
             outs[order[r]][z] = value.astype(jnp.bfloat16)
@@ -354,20 +343,14 @@
 
 def down(make_place, layout, order, s, n_z, width, counts, hid, w_down, values, after):
     n = len(order)
-    ff = hid.shape[1]
-    extra = [] if after is None else [after]
     return call(
         lambda *refs: down_kernel(make_place, layout, order, s, *refs),
         [jax.ShapeDtypeStruct((n_z, layout.share, width), jnp.bfloat16)] * n,
-        [SMEM, VMEM, ANY, VMEM] + [ANY] * len(extra),
+        [SMEM] + [VMEM] * 3 + [ANY],
         [VMEM] * n,
         "expert_down",
-        12,
-        scratch_shapes=[
-            pltpu.VMEM((n_z, ff, width), jnp.bfloat16),
-            pltpu.SemaphoreType.DMA((n_z,)),
-        ],
-    )(counts, hid, w_down, values, *extra)
+        8,
+    )(counts, hid, w_down, values, after)
 
 
 def group_steps(layout, scope, tables, grains):
@@ -470,7 +453,13 @@
         return Place(n_bits, n_expert)
 
     first = project(
-        make_place, plain[:top], context, context_other, pieces[:n_chip], ()
+        make_place,
+        plain[:top],
+        context,
+        context_other,
+        pieces[:n_chip],
+        (),
+        (),
     )
     attended = project(
         make_place,
@@ -479,11 +468,12 @@
         context_other,
         pieces[n_chip:],
         (first, residual_own, residual_other),
+        (),
     )
 
     layouts = [Layout(group, n_chip, local_blocks) for group in range(GROUPS)]
     grains = attended.reshape(-1, share, half)
-    values = gate_values.reshape(-1, 1)
+    values = gate_values
 
     scope = (make_place, n_dp, n_bits, n_expert, half, reverse, to_partner)
     tables = (chosen_blocks, block_counts, values, w_gate, w_up, w_down)
@@ -496,13 +486,8 @@
         received[g] = done
     received = [piece for pieces in received for piece in pieces]
 
-    mixed = finish(make_place, layouts, n_chip, chosen_blocks, grains, received).reshape(2, local_tokens, half)
-    got = to_partner(mixed[1])
-    return jnp.where(
-        side == 0,
-        jnp.concatenate([mixed[0], got], axis=1),
-        jnp.concatenate([got, mixed[0]], axis=1),
-    )
+    own, other = finish(make_place, layouts, n_chip, chosen_blocks, grains, received)
+    return join(make_place, own, to_partner(other), local_tokens)
 
 
 def solution(mesh):

time: 195 us -> 172 us (0.88)
  local copies, waits for them, and re-layouts: 15.9 us -> 4.84 us
  Pallas kernels: 39.9 us -> 30.4 us
    unnamed x38 -> x20, local copies, waits for them, and re-layouts: 12.2 us -> 2.23 us
    pallas_call x2, Pallas kernels: 16.2 us -> 10.9 us  [hidden_units(): call(lambda *refs: hidden_kernel(make_place, n, *refs), jax.ShapeDtypeStr...]
    pallas_call x4, Pallas kernels: 12.2 us -> 7.3 us  [down(): call(lambda *refs: down_kernel(make_place, layout, order, s, *refs), [jax...]
  transfers between devices with their start and end apart: 62 -> 62, of which waited for: 25 -> 27; matrix products, arithmetic and copies ran while one was open for 2% -> 2% of each run, Pallas kernels for 18% -> 14%
where the time goes in v6:
time: 172 us
  waiting for transfers between devices  74.9 us (44%)
  starting transfers between devices  61.5 us (36%)
  Pallas kernels  30.4 us (18%)
  local copies, waits for them, and re-layouts  4.84 us (3%)
    ppermute x30, waiting for transfers between devices, exchange(): return lax.ppermute(value, 'dp', step_pairs(n_dp, step))  55.8 us
    ppermute x30, starting transfers between devices, exchange(): return lax.ppermute(value, 'dp', step_pairs(n_dp, step))  36.4 us
    ppermute x12, starting transfers between devices, swap_planes(): out.append(lax.ppermute(parts[k], 'expert', pairs))  18.8 us
    ppermute x12, waiting for transfers between devices, swap_planes(): out.append(lax.ppermute(parts[k], 'expert', pairs))  13.5 us
    pallas_call x2, Pallas kernels, hidden_units(): call(lambda *refs: hidden_kernel(make_place, n, *refs), jax.ShapeDtypeStr...  10.9 us
    pallas_call x4, Pallas kernels, down(): call(lambda *refs: down_kernel(make_place, layout, order, s, *refs), [jax...  7.3 us
    pallas_call x2, Pallas kernels, project(): call(lambda *refs: project_kernel(make_place, parts, len(weights), len(ex...  6.98 us
    ppermute x20, starting transfers between devices, to_partner(): return lax.ppermute(value, 'dp', pair)  6.34 us
  transfers between devices with their start and end apart: 62, of which 27 were waited for; matrix products, arithmetic and copies ran while one was open for 2% of the time, Pallas kernels for 14%

profile of v6, /device:TPU:0, one launch (start us, length us, event | category | flops | bytes accessed | tf_op | source)
XLA Modules:
  0.0 172.1 jit_solution(16780270072441671862)
XLA Ops:
  0.5 1.3 constant_dynamic-slice_fusion.2
  1.8 2.9 %collective-permute-start.4 = (bf16[512,512]{1,0:T(8,128)(2,1)S(1)}, bf16[512,512]{1,0:T(8,128)(2,1)S(1)}, u32[]{:S(2)}, u32[]{:S(2)}) collective-permute-start(bf16[512,512]{1,0:T(8,128)(2,1)S(1)} %get-tuple-element.68.refs_2_), channel_id=1, source_target_pairs={{0,8},{4,20},{8,0},{12,28},{16,24},{20,4},{24,16},{28,12},{1,9},{5... | collective-permute-start | bytes 1572872 | tf_op jit(solution)/shard_map/ppermute | solution.py:48
  4.8 3.2 %collective-permute-done.2.refs_3_ = bf16[512,512]{1,0:T(8,128)(2,1)S(1)} collective-permute-done((bf16[512,512]{1,0:T(8,128)(2,1)S(1)}, bf16[512,512]{1,0:T(8,128)(2,1)S(1)}, u32[]{:S(2)}, u32[]{:S(2)}) %collective-permute-start.2) | collective-permute-done | bytes 524320 | tf_op jit(solution)/shard_map/ppermute | solution.py:433
  8.0 2.9 %collective-permute-start.6 = (bf16[512,512]{1,0:T(8,128)(2,1)S(1)}, bf16[512,512]{1,0:T(8,128)(2,1)S(1)}, u32[]{:S(2)}, u32[]{:S(2)}) collective-permute-start(bf16[512,512]{1,0:T(8,128)(2,1)S(1)} %collective-permute-done.2.refs_3_), channel_id=1, source_target_pairs={{0,8},{4,20},{8,0},{12,28},{16,24},{20,4},{24,16},{28,12},{1,9},{5... | collective-permute-start | bytes 1572872 | tf_op jit(solution)/shard_map/ppermute | solution.py:48
  10.8 1.5 collective-permute-start.1
  12.4 1.3 constant_dynamic-slice_fusion
  14.3 8.5 %collective-permute-done.6.refs_5_ = bf16[512,512]{1,0:T(8,128)(2,1)S(1)} collective-permute-done((bf16[512,512]{1,0:T(8,128)(2,1)S(1)}, bf16[512,512]{1,0:T(8,128)(2,1)S(1)}, u32[]{:S(2)}, u32[]{:S(2)}) %collective-permute-start.6) | collective-permute-done | bytes 524320 | tf_op jit(solution)/shard_map/ppermute | solution.py:48
  22.8 2.8 %collective-permute-start.5 = (bf16[512,512]{1,0:T(8,128)(2,1)S(1)}, bf16[512,512]{1,0:T(8,128)(2,1)S(1)}, u32[]{:S(2)}, u32[]{:S(2)}) collective-permute-start(bf16[512,512]{1,0:T(8,128)(2,1)S(1)} %collective-permute-done.4.refs_4_), channel_id=1, source_target_pairs={{0,16},{4,12},{8,24},{12,4},{16,0},{20,28},{24,8},{28,20},{1,17},{... | collective-permute-start | bytes 1572872 | tf_op jit(solution)/shard_map/ppermute | solution.py:48
  25.7 2.2 %copy-done = bf16[512,4096]{1,0:T(8,128)(2,1)S(1)} copy-done((bf16[512,4096]{1,0:T(8,128)(2,1)S(1)}, bf16[512,4096]{1,0:T(8,128)(2,1)}, u32[]{:S(2)}) %copy-start) | copy-done | bytes 4194328
  27.9 3.3 %project_first.1.refs_6_ = f32[2,512,512]{2,1,0:T(8,128)S(1)} custom-call(bf16[512,4096]{1,0:T(8,128)(2,1)S(1)} %copy-done, bf16[512,4096]{1,0:T(8,128)(2,1)} %collective-permute-done.refs_1_, bf16[512,512]{1,0:T(8,128)(2,1)S(1)} %get-tuple-element.68.refs_2_, bf16[512,512]{1,0:T(8,128)(2,1)S(1)} %collective-permute-done.2.refs_3_, ...), custom_call_target="tpu_custom_call" | custom-call | tf_op jit(solution)/shard_map/project_first/pallas_call | solution.py:194
  31.3 3.1 %collective-permute-done.5.refs_4_ = bf16[512,512]{1,0:T(8,128)(2,1)S(1)} collective-permute-done((bf16[512,512]{1,0:T(8,128)(2,1)S(1)}, bf16[512,512]{1,0:T(8,128)(2,1)S(1)}, u32[]{:S(2)}, u32[]{:S(2)}) %collective-permute-start.5) | collective-permute-done | bytes 524320 | tf_op jit(solution)/shard_map/ppermute | solution.py:48
  34.3 5.6 %collective-permute-done.7.refs_5_ = bf16[512,512]{1,0:T(8,128)(2,1)S(1)} collective-permute-done((bf16[512,512]{1,0:T(8,128)(2,1)S(1)}, bf16[512,512]{1,0:T(8,128)(2,1)S(1)}, u32[]{:S(2)}, u32[]{:S(2)}) %collective-permute-start.7) | collective-permute-done | bytes 524320 | tf_op jit(solution)/shard_map/ppermute | solution.py:48
  40.0 3.6 %project_last.1 = bf16[2,512,512]{2,1,0:T(8,128)(2,1)S(1)} custom-call(bf16[512,4096]{1,0:T(8,128)(2,1)S(1)} %copy-done, bf16[512,4096]{1,0:T(8,128)(2,1)} %collective-permute-done.refs_1_, bf16[512,512]{1,0:T(8,128)(2,1)S(1)} %collective-permute-done.1.refs_2_, bf16[512,512]{1,0:T(8,128)(2,1)S(1)} %collective-permute-done.3.refs_3_, ...), custom_call_target="tpu_custom_call" | custom-call | tf_op jit(solution)/shard_map/project_last/pallas_call | solution.py:194
  44.4 1.8 %collective-permute-start.10 = (bf16[4,64,512]{2,1,0:T(8,128)(2,1)S(1)}, bf16[4,64,512]{2,1,0:T(8,128)(2,1)S(1)}, u32[]{:S(2)}, u32[]{:S(2)}) collective-permute-start(bf16[4,64,512]{2,1,0:T(8,128)(2,1)S(1)} %get-tuple-element.38), channel_id=1, source_target_pairs={{0,16},{4,12},{8,24},{12,4},{16,0},{20,28},{24,8},{28,20},{1,17},{... | collective-permute-start | bytes 786440 | tf_op jit(solution)/shard_map/ppermute | solution.py:48
  46.5 4.3 %collective-permute-done.10.refs_1_ = bf16[4,64,512]{2,1,0:T(8,128)(2,1)S(1)} collective-permute-done((bf16[4,64,512]{2,1,0:T(8,128)(2,1)S(1)}, bf16[4,64,512]{2,1,0:T(8,128)(2,1)S(1)}, u32[]{:S(2)}, u32[]{:S(2)}) %collective-permute-start.10) | collective-permute-done | bytes 262176 | tf_op jit(solution)/shard_map/ppermute | solution.py:48
  50.9 1.5 collective-permute-start.11
  52.4 0.8 pick_blocks.3
  53.2 1.6 collective-permute-start.15
  54.8 5.1 %collective-permute-done.11.refs_2_ = bf16[4,64,512]{2,1,0:T(8,128)(2,1)S(1)} collective-permute-done((bf16[4,64,512]{2,1,0:T(8,128)(2,1)S(1)}, bf16[4,64,512]{2,1,0:T(8,128)(2,1)S(1)}, u32[]{:S(2)}, u32[]{:S(2)}) %collective-permute-start.11) | collective-permute-done | bytes 262176 | tf_op jit(solution)/shard_map/ppermute | solution.py:48
  60.0 2.0 %collective-permute-start.12 = (bf16[64,512]{1,0:T(8,128)(2,1)S(1)}, bf16[64,512]{1,0:T(8,128)(2,1)S(1)}, u32[]{:S(2)}, u32[]{:S(2)}) collective-permute-start(bf16[64,512]{1,0:T(8,128)(2,1)S(1)} %get-tuple-element.83), channel_id=1, source_target_pairs={{0,1},{1,2},{2,3},{3,0},{4,5},{5,6},{6,7},{7,4},{8,9},{9,10},{10,1... | collective-permute-start | bytes 196616 | tf_op jit(solution)/shard_map/ppermute | solution.py:62
  62.0 2.6 %collective-permute-start.13 = (bf16[64,512]{1,0:T(8,128)(2,1)S(1)}, bf16[64,512]{1,0:T(8,128)(2,1)S(1)}, u32[]{:S(2)}, u32[]{:S(2)}) collective-permute-start(bf16[64,512]{1,0:T(8,128)(2,1)S(1)} %get-tuple-element.82), channel_id=1, source_target_pairs={{0,2},{1,3},{2,0},{3,1},{4,6},{5,7},{6,4},{7,5},{8,10},{9,11},{10,... | collective-permute-start | bytes 196616 | tf_op jit(solution)/shard_map/ppermute | solution.py:62
  64.6 1.3 collective-permute-start.14
  65.9 1.3 collective-permute-start.23
  67.3 1.6 collective-permute-start.24
  68.9 0.9 collective-permute-start.16
  69.8 1.9 %collective-permute-start.17 = (bf16[4,64,512]{2,1,0:T(8,128)(2,1)S(1)}, bf16[4,64,512]{2,1,0:T(8,128)(2,1)S(1)}, u32[]{:S(2)}, u32[]{:S(2)}) collective-permute-start(bf16[4,64,512]{2,1,0:T(8,128)(2,1)S(1)} %stack_planes.4.refs_3_.refs_0_), channel_id=1, source_target_pairs={{0,16},{4,12},{8,24},{12,4},{16,0},{20,28},{24,8},{28,20},{1,17},{... | collective-permute-start | bytes 786440 | tf_op jit(solution)/shard_map/ppermute | solution.py:48
  71.7 2.1 %collective-permute-done.23.refs_1_ = bf16[4,64,512]{2,1,0:T(8,128)(2,1)S(1)} collective-permute-done((bf16[4,64,512]{2,1,0:T(8,128)(2,1)S(1)}, bf16[4,64,512]{2,1,0:T(8,128)(2,1)S(1)}, u32[]{:S(2)}, u32[]{:S(2)}) %collective-permute-start.23) | collective-permute-done | bytes 262176 | tf_op jit(solution)/shard_map/ppermute | solution.py:48
  73.9 3.9 %collective-permute-done.16.refs_1_ = bf16[4,64,512]{2,1,0:T(8,128)(2,1)S(1)} collective-permute-done((bf16[4,64,512]{2,1,0:T(8,128)(2,1)S(1)}, bf16[4,64,512]{2,1,0:T(8,128)(2,1)S(1)}, u32[]{:S(2)}, u32[]{:S(2)}) %collective-permute-start.16) | collective-permute-done | bytes 262176 | tf_op jit(solution)/shard_map/ppermute | solution.py:48
  78.6 2.8 %collective-permute-start.26 = (bf16[64,512]{1,0:T(8,128)(2,1)S(1)}, bf16[64,512]{1,0:T(8,128)(2,1)S(1)}, u32[]{:S(2)}, u32[]{:S(2)}) collective-permute-start(bf16[64,512]{1,0:T(8,128)(2,1)S(1)} %get-tuple-element.78), channel_id=1, source_target_pairs={{0,2},{1,3},{2,0},{3,1},{4,6},{5,7},{6,4},{7,5},{8,10},{9,11},{10,... | collective-permute-start | bytes 196616 | tf_op jit(solution)/shard_map/ppermute | solution.py:62
  81.8 2.3 %collective-permute-done.25.refs_1_ = bf16[64,512]{1,0:T(8,128)(2,1)S(1)} collective-permute-done((bf16[64,512]{1,0:T(8,128)(2,1)S(1)}, bf16[64,512]{1,0:T(8,128)(2,1)S(1)}, u32[]{:S(2)}, u32[]{:S(2)}) %collective-permute-start.25) | collective-permute-done | bytes 65568 | tf_op jit(solution)/shard_map/ppermute | solution.py:62
  84.1 1.1 collective-permute-done.26.refs_2_
  85.9 1.7 %collective-permute-start.28 = (bf16[4,64,512]{2,1,0:T(8,128)(2,1)S(1)}, bf16[4,64,512]{2,1,0:T(8,128)(2,1)S(1)}, u32[]{:S(2)}, u32[]{:S(2)}) collective-permute-start(bf16[4,64,512]{2,1,0:T(8,128)(2,1)S(1)} %stack_planes.5.refs_0_), channel_id=1, source_target_pairs={{0,8},{4,20},{8,0},{12,28},{16,24},{20,4},{24,16},{28,12},{1,9},{5... | collective-permute-start | bytes 786440 | tf_op jit(solution)/shard_map/ppermute | solution.py:48
  88.2 2.0 %collective-permute-start.35 = (bf16[4,64,512]{2,1,0:T(8,128)(2,1)S(1)}, bf16[4,64,512]{2,1,0:T(8,128)(2,1)S(1)}, u32[]{:S(2)}, u32[]{:S(2)}) collective-permute-start(bf16[4,64,512]{2,1,0:T(8,128)(2,1)S(1)} %stack_planes.5.refs_0_), channel_id=1, source_target_pairs={{0,16},{4,12},{8,24},{12,4},{16,0},{20,28},{24,8},{28,20},{1,17},{... | collective-permute-start | bytes 786440 | tf_op jit(solution)/shard_map/ppermute | solution.py:48
  90.2 3.3 %collective-permute-done.28.refs_10_.refs_1_ = bf16[4,64,512]{2,1,0:T(8,128)(2,1)S(1)} collective-permute-done((bf16[4,64,512]{2,1,0:T(8,128)(2,1)S(1)}, bf16[4,64,512]{2,1,0:T(8,128)(2,1)S(1)}, u32[]{:S(2)}, u32[]{:S(2)}) %collective-permute-start.28) | collective-permute-done | bytes 262176 | tf_op jit(solution)/shard_map/ppermute | solution.py:48
  93.5 2.5 %collective-permute-start.36 = (bf16[4,64,512]{2,1,0:T(8,128)(2,1)S(1)}, bf16[4,64,512]{2,1,0:T(8,128)(2,1)S(1)}, u32[]{:S(2)}, u32[]{:S(2)}) collective-permute-start(bf16[4,64,512]{2,1,0:T(8,128)(2,1)S(1)} %collective-permute-done.28.refs_10_.refs_1_), channel_id=1, source_target_pairs={{0,16},{4,12},{8,24},{12,4},{16,0},{20,28},{24,8},{28,20},{1,17},{... | collective-permute-start | bytes 786440 | tf_op jit(solution)/shard_map/ppermute | solution.py:48
  96.1 5.4 %expert_hidden.2.refs_1_.refs_4_ = bf16[256,1024]{1,0:T(8,128)(2,1)S(1)} custom-call(bf16[4,64,512]{2,1,0:T(8,128)(2,1)S(1)} %stack_planes.4.refs_3_.refs_0_, bf16[4,64,512]{2,1,0:T(8,128)(2,1)S(1)} %collective-permute-done.16.refs_1_, bf16[4,64,512]{2,1,0:T(8,128)(2,1)S(1)} %collective-permute-done.17.refs_2_, ...), custom_call_target="tpu_custom_call" | custom-call | tf_op jit(solution)/shard_map/expert_hidden/pallas_call | solution.py:311
  101.6 1.8 %expert_down.4 = (bf16[4,64,512]{2,1,0:T(8,128)(2,1)S(1)}, bf16[4,64,512]{2,1,0:T(8,128)(2,1)S(1)}, bf16[4,64,512]{2,1,0:T(8,128)(2,1)S(1)}, bf16[4,64,512]{2,1,0:T(8,128)(2,1)S(1)}) custom-call(s32[4]{0:T(128)S(1)} %copy-done.3, bf16[256,1024]{1,0:T(8,128)(2,1)S(1)} %expert_hidden.2.refs_1_.refs_4_, bf16[1024,4096]{1,0:T(8,128)(2,1)S(1)} %bitcast.38, ...), custom_call_target="tpu_custom_call" | custom-call | tf_op jit(solution)/shard_map/expert_down/pallas_call | solution.py:346
  105.2 1.8 %expert_down.5 = (bf16[4,64,512]{2,1,0:T(8,128)(2,1)S(1)}, bf16[4,64,512]{2,1,0:T(8,128)(2,1)S(1)}, bf16[4,64,512]{2,1,0:T(8,128)(2,1)S(1)}, bf16[4,64,512]{2,1,0:T(8,128)(2,1)S(1)}) custom-call(s32[4]{0:T(128)S(1)} %copy-done.3, bf16[256,1024]{1,0:T(8,128)(2,1)S(1)} %expert_hidden.2.refs_1_.refs_4_, bf16[1024,4096]{1,0:T(8,128)(2,1)S(1)} %bitcast.39, ...), custom_call_target="tpu_custom_call" | custom-call | tf_op jit(solution)/shard_map/expert_down/pallas_call | solution.py:346
  107.7 5.4 %expert_hidden.3.refs_1_.refs_4_ = bf16[256,1024]{1,0:T(8,128)(2,1)S(1)} custom-call(bf16[4,64,512]{2,1,0:T(8,128)(2,1)S(1)} %stack_planes.5.refs_0_, bf16[4,64,512]{2,1,0:T(8,128)(2,1)S(1)} %collective-permute-done.28.refs_10_.refs_1_, bf16[4,64,512]{2,1,0:T(8,128)(2,1)S(1)} %collective-permute-done.35.refs_2_, ...), custom_call_target="tpu_custom_call" | custom-call | tf_op jit(solution)/shard_map/expert_hidden/pallas_call | solution.py:311
  113.2 1.8 %expert_down.6 = (bf16[4,64,512]{2,1,0:T(8,128)(2,1)S(1)}, bf16[4,64,512]{2,1,0:T(8,128)(2,1)S(1)}, bf16[4,64,512]{2,1,0:T(8,128)(2,1)S(1)}, bf16[4,64,512]{2,1,0:T(8,128)(2,1)S(1)}) custom-call(s32[4]{0:T(128)S(1)} %copy-done.3, bf16[256,1024]{1,0:T(8,128)(2,1)S(1)} %expert_hidden.3.refs_1_.refs_4_, bf16[1024,4096]{1,0:T(8,128)(2,1)S(1)} %bitcast.40, ...), custom_call_target="tpu_custom_call" | custom-call | tf_op jit(solution)/shard_map/expert_down/pallas_call | solution.py:346
  115.0 2.3 %collective-permute-start.42 = (bf16[4,64,512]{2,1,0:T(8,128)(2,1)S(1)}, bf16[4,64,512]{2,1,0:T(8,128)(2,1)S(1)}, u32[]{:S(2)}, u32[]{:S(2)}) collective-permute-start(bf16[4,64,512]{2,1,0:T(8,128)(2,1)S(1)} %get-tuple-element.55), channel_id=1, source_target_pairs={{0,4},{4,0},{8,12},{12,8},{16,20},{20,16},{24,28},{28,24},{1,5},{5... | collective-permute-start | bytes 786440 | tf_op jit(solution)/shard_map/ppermute | solution.py:433
  118.4 1.8 %expert_down.7 = (bf16[4,64,512]{2,1,0:T(8,128)(2,1)S(1)}, bf16[4,64,512]{2,1,0:T(8,128)(2,1)S(1)}, bf16[4,64,512]{2,1,0:T(8,128)(2,1)S(1)}, bf16[4,64,512]{2,1,0:T(8,128)(2,1)S(1)}) custom-call(s32[4]{0:T(128)S(1)} %copy-done.3, bf16[256,1024]{1,0:T(8,128)(2,1)S(1)} %expert_hidden.3.refs_1_.refs_4_, bf16[1024,4096]{1,0:T(8,128)(2,1)S(1)} %bitcast.41, ...), custom_call_target="tpu_custom_call" | custom-call | tf_op jit(solution)/shard_map/expert_down/pallas_call | solution.py:346
  120.3 1.9 %collective-permute-start.41 = (bf16[4,64,512]{2,1,0:T(8,128)(2,1)S(1)}, bf16[4,64,512]{2,1,0:T(8,128)(2,1)S(1)}, u32[]{:S(2)}, u32[]{:S(2)}) collective-permute-start(bf16[4,64,512]{2,1,0:T(8,128)(2,1)S(1)} %add_terms.15.refs_4_), channel_id=1, source_target_pairs={{0,8},{4,20},{8,0},{12,28},{16,24},{20,4},{24,16},{28,12},{1,9},{5... | collective-permute-start | bytes 786440 | tf_op jit(solution)/shard_map/ppermute | solution.py:48
  122.9 2.3 %collective-permute-done.32.refs_2_ = bf16[4,64,512]{2,1,0:T(8,128)(2,1)S(1)} collective-permute-done((bf16[4,64,512]{2,1,0:T(8,128)(2,1)S(1)}, bf16[4,64,512]{2,1,0:T(8,128)(2,1)S(1)}, u32[]{:S(2)}, u32[]{:S(2)}) %collective-permute-start.32) | collective-permute-done | bytes 262176 | tf_op jit(solution)/shard_map/ppermute | solution.py:48
  125.1 3.7 %collective-permute-done.41.refs_3_ = bf16[4,64,512]{2,1,0:T(8,128)(2,1)S(1)} collective-permute-done((bf16[4,64,512]{2,1,0:T(8,128)(2,1)S(1)}, bf16[4,64,512]{2,1,0:T(8,128)(2,1)S(1)}, u32[]{:S(2)}, u32[]{:S(2)}) %collective-permute-start.41) | collective-permute-done | bytes 262176 | tf_op jit(solution)/shard_map/ppermute | solution.py:48
  129.0 0.8 collective-permute-done.48.refs_2_
  130.0 1.7 %collective-permute-start.54 = (bf16[4,64,512]{2,1,0:T(8,128)(2,1)S(1)}, bf16[4,64,512]{2,1,0:T(8,128)(2,1)S(1)}, u32[]{:S(2)}, u32[]{:S(2)}) collective-permute-start(bf16[4,64,512]{2,1,0:T(8,128)(2,1)S(1)} %add_terms.18.refs_4_), channel_id=1, source_target_pairs={{0,8},{4,20},{8,0},{12,28},{16,24},{20,4},{24,16},{28,12},{1,9},{5... | collective-permute-start | bytes 786440 | tf_op jit(solution)/shard_map/ppermute | solution.py:48
  131.7 1.5 collective-permute-start.44
  133.3 1.8 %collective-permute-start.45 = (bf16[64,512]{1,0:T(8,128)(2,1)S(1)}, bf16[64,512]{1,0:T(8,128)(2,1)S(1)}, u32[]{:S(2)}, u32[]{:S(2)}) collective-permute-start(bf16[64,512]{1,0:T(8,128)(2,1)S(1)} %get-tuple-element.74), channel_id=1, source_target_pairs={{0,2},{1,3},{2,0},{3,1},{4,6},{5,7},{6,4},{7,5},{8,10},{9,11},{10,... | collective-permute-start | bytes 196616 | tf_op jit(solution)/shard_map/ppermute | solution.py:62
  135.1 2.8 %collective-permute-done.44.refs_1_ = bf16[64,512]{1,0:T(8,128)(2,1)S(1)} collective-permute-done((bf16[64,512]{1,0:T(8,128)(2,1)S(1)}, bf16[64,512]{1,0:T(8,128)(2,1)S(1)}, u32[]{:S(2)}, u32[]{:S(2)}) %collective-permute-start.44) | collective-permute-done | bytes 65568 | tf_op jit(solution)/shard_map/ppermute | solution.py:62
  137.8 1.5 collective-permute-start.46
  140.0 2.1 %collective-permute-done.46.refs_3_ = bf16[64,512]{1,0:T(8,128)(2,1)S(1)} collective-permute-done((bf16[64,512]{1,0:T(8,128)(2,1)S(1)}, bf16[64,512]{1,0:T(8,128)(2,1)S(1)}, u32[]{:S(2)}, u32[]{:S(2)}) %collective-permute-start.46) | collective-permute-done | bytes 65568 | tf_op jit(solution)/shard_map/ppermute | solution.py:62
  142.4 4.0 %collective-permute-start.56 = (bf16[64,512]{1,0:T(8,128)(2,1)S(1)}, bf16[64,512]{1,0:T(8,128)(2,1)S(1)}, u32[]{:S(2)}, u32[]{:S(2)}) collective-permute-start(bf16[64,512]{1,0:T(8,128)(2,1)S(1)} %get-tuple-element.70), channel_id=1, source_target_pairs={{0,2},{1,3},{2,0},{3,1},{4,6},{5,7},{6,4},{7,5},{8,10},{9,11},{10,... | collective-permute-start | bytes 196616 | tf_op jit(solution)/shard_map/ppermute | solution.py:62
  146.9 1.6 collective-permute-done.55.refs_1_
  148.5 1.4 collective-permute-done.56.refs_2_
  149.8 0.9 collective-permute-done.57.refs_3_
  151.1 1.8 %collective-permute-start.50 = (bf16[4,64,512]{2,1,0:T(8,128)(2,1)S(1)}, bf16[4,64,512]{2,1,0:T(8,128)(2,1)S(1)}, u32[]{:S(2)}, u32[]{:S(2)}) collective-permute-start(bf16[4,64,512]{2,1,0:T(8,128)(2,1)S(1)} %stack_planes.6.refs_4_.refs_2_), channel_id=1, source_target_pairs={{0,16},{4,12},{8,24},{12,4},{16,0},{20,28},{24,8},{28,20},{1,17},{... | collective-permute-start | bytes 786440 | tf_op jit(solution)/shard_map/ppermute | solution.py:48
  153.1 2.5 %collective-permute-done.49.refs_3_ = bf16[4,64,512]{2,1,0:T(8,128)(2,1)S(1)} collective-permute-done((bf16[4,64,512]{2,1,0:T(8,128)(2,1)S(1)}, bf16[4,64,512]{2,1,0:T(8,128)(2,1)S(1)}, u32[]{:S(2)}, u32[]{:S(2)}) %collective-permute-start.49) | collective-permute-done | bytes 262176 | tf_op jit(solution)/shard_map/ppermute | solution.py:48
  156.4 4.9 %collective-permute-done.58.refs_7_ = bf16[4,64,512]{2,1,0:T(8,128)(2,1)S(1)} collective-permute-done((bf16[4,64,512]{2,1,0:T(8,128)(2,1)S(1)}, bf16[4,64,512]{2,1,0:T(8,128)(2,1)S(1)}, u32[]{:S(2)}, u32[]{:S(2)}) %collective-permute-start.58) | collective-permute-done | bytes 262176 | tf_op jit(solution)/shard_map/ppermute | solution.py:48
  162.0 1.1 collective-permute-done.51.refs_5_
  163.1 4.5 %collective-permute-done.60.refs_9_ = bf16[4,64,512]{2,1,0:T(8,128)(2,1)S(1)} collective-permute-done((bf16[4,64,512]{2,1,0:T(8,128)(2,1)S(1)}, bf16[4,64,512]{2,1,0:T(8,128)(2,1)S(1)}, u32[]{:S(2)}, u32[]{:S(2)}) %collective-permute-start.60) | collective-permute-done | bytes 262176 | tf_op jit(solution)/shard_map/ppermute | solution.py:48
  167.6 1.4 add_expert_rows.1
  169.1 1.9 %collective-permute-done.61.refs_1_ = bf16[8,64,512]{2,1,0:T(8,128)(2,1)S(1)} collective-permute-done((bf16[8,64,512]{2,1,0:T(8,128)(2,1)S(1)}, bf16[8,64,512]{2,1,0:T(8,128)(2,1)S(1)}, u32[]{:S(2)}, u32[]{:S(2)}) %collective-permute-start.61) | collective-permute-done | bytes 524320 | tf_op jit(solution)/shard_map/ppermute | solution.py:433
  171.0 1.1 join_halves.1
  (115 shorter events, 13.1 us)
Async XLA Ops:
  0.0 25.7 %collective-permute-start = (bf16[512,4096]{1,0:T(8,128)(2,1)}, bf16[512,4096]{1,0:T(8,128)(2,1)}, u32[]{:S(2)}, u32[]{:S(2)}) collective-permute-start(bf16[512,4096]{1,0:T(8,128)(2,1)} %refs_0_.10), channel_id=1, source_target_pairs={{0,4},{4,0},{8,12},{12,8},{16,20},{20,16},{24,28},{28,24},{1,5},{5... | collective-permute-start | bytes 12582920 | tf_op jit(solution)/shard_map/ppermute | solution.py:433
  1.7 6.3 %collective-permute-start.2 = (bf16[512,512]{1,0:T(8,128)(2,1)S(1)}, bf16[512,512]{1,0:T(8,128)(2,1)S(1)}, u32[]{:S(2)}, u32[]{:S(2)}) collective-permute-start(bf16[512,512]{1,0:T(8,128)(2,1)S(1)} %get-tuple-element.67), channel_id=1, source_target_pairs={{0,4},{4,0},{8,12},{12,8},{16,20},{20,16},{24,28},{28,24},{1,5},{5... | collective-permute-start | bytes 1572872 | tf_op jit(solution)/shard_map/ppermute | solution.py:433
  1.8 11.9 %collective-permute-start.4 = (bf16[512,512]{1,0:T(8,128)(2,1)S(1)}, bf16[512,512]{1,0:T(8,128)(2,1)S(1)}, u32[]{:S(2)}, u32[]{:S(2)}) collective-permute-start(bf16[512,512]{1,0:T(8,128)(2,1)S(1)} %get-tuple-element.68.refs_2_), channel_id=1, source_target_pairs={{0,8},{4,20},{8,0},{12,28},{16,24},{20,4},{24,16},{28,12},{1,9},{5... | collective-permute-start | bytes 1572872 | tf_op jit(solution)/shard_map/ppermute | solution.py:48
  8.0 14.9 %collective-permute-start.6 = (bf16[512,512]{1,0:T(8,128)(2,1)S(1)}, bf16[512,512]{1,0:T(8,128)(2,1)S(1)}, u32[]{:S(2)}, u32[]{:S(2)}) collective-permute-start(bf16[512,512]{1,0:T(8,128)(2,1)S(1)} %collective-permute-done.2.refs_3_), channel_id=1, source_target_pairs={{0,8},{4,20},{8,0},{12,28},{16,24},{20,4},{24,16},{28,12},{1,9},{5... | collective-permute-start | bytes 1572872 | tf_op jit(solution)/shard_map/ppermute | solution.py:48
  10.8 20.4 %collective-permute-start.1 = (bf16[512,512]{1,0:T(8,128)(2,1)S(1)}, bf16[512,512]{1,0:T(8,128)(2,1)S(1)}, u32[]{:S(2)}, u32[]{:S(2)}) collective-permute-start(bf16[512,512]{1,0:T(8,128)(2,1)S(1)} %get-tuple-element.68.refs_2_), channel_id=1, source_target_pairs={{0,16},{4,12},{8,24},{12,4},{16,0},{20,28},{24,8},{28,20},{1,17},{... | collective-permute-start | bytes 1572872 | tf_op jit(solution)/shard_map/ppermute | solution.py:48
  13.7 17.6 %collective-permute-start.8 = (bf16[512,512]{1,0:T(8,128)(2,1)S(1)}, bf16[512,512]{1,0:T(8,128)(2,1)S(1)}, u32[]{:S(2)}, u32[]{:S(2)}) collective-permute-start(bf16[512,512]{1,0:T(8,128)(2,1)S(1)} %get-tuple-element.65), channel_id=1, source_target_pairs={{0,4},{4,0},{8,12},{12,8},{16,20},{20,16},{24,28},{28,24},{1,5},{5... | collective-permute-start | bytes 1572872 | tf_op jit(solution)/shard_map/ppermute | solution.py:433
  13.7 20.6 %collective-permute-start.3 = (bf16[512,512]{1,0:T(8,128)(2,1)S(1)}, bf16[512,512]{1,0:T(8,128)(2,1)S(1)}, u32[]{:S(2)}, u32[]{:S(2)}) collective-permute-start(bf16[512,512]{1,0:T(8,128)(2,1)S(1)} %collective-permute-done.2.refs_3_), channel_id=1, source_target_pairs={{0,16},{4,12},{8,24},{12,4},{16,0},{20,28},{24,8},{28,20},{1,17},{... | collective-permute-start | bytes 1572872 | tf_op jit(solution)/shard_map/ppermute | solution.py:48
  22.8 11.5 %collective-permute-start.5 = (bf16[512,512]{1,0:T(8,128)(2,1)S(1)}, bf16[512,512]{1,0:T(8,128)(2,1)S(1)}, u32[]{:S(2)}, u32[]{:S(2)}) collective-permute-start(bf16[512,512]{1,0:T(8,128)(2,1)S(1)} %collective-permute-done.4.refs_4_), channel_id=1, source_target_pairs={{0,16},{4,12},{8,24},{12,4},{16,0},{20,28},{24,8},{28,20},{1,17},{... | collective-permute-start | bytes 1572872 | tf_op jit(solution)/shard_map/ppermute | solution.py:48
  25.7 14.3 %collective-permute-start.7 = (bf16[512,512]{1,0:T(8,128)(2,1)S(1)}, bf16[512,512]{1,0:T(8,128)(2,1)S(1)}, u32[]{:S(2)}, u32[]{:S(2)}) collective-permute-start(bf16[512,512]{1,0:T(8,128)(2,1)S(1)} %collective-permute-done.6.refs_5_), channel_id=1, source_target_pairs={{0,16},{4,12},{8,24},{12,4},{16,0},{20,28},{24,8},{28,20},{1,17},{... | collective-permute-start | bytes 1572872 | tf_op jit(solution)/shard_map/ppermute | solution.py:48
  40.0 56.1 %slice-start.3 = ((s8[8388608]{0:T(1024)(128)(4,1)}), s8[4194304]{0:T(1024)(128)(4,1)S(1)}, s32[]{:S(2)}) async-start(s8[8388608]{0:T(1024)(128)(4,1)} %bitcast.42), calls=%async_computation.3 | async-start | bytes 8388608
  40.0 56.1 %slice-start.5 = ((s8[8388608]{0:T(1024)(128)(4,1)}), s8[4194304]{0:T(1024)(128)(4,1)S(1)}, s32[]{:S(2)}) async-start(s8[8388608]{0:T(1024)(128)(4,1)} %bitcast.46), calls=%async_computation.5 | async-start | bytes 8388608
  44.4 6.4 %collective-permute-start.10 = (bf16[4,64,512]{2,1,0:T(8,128)(2,1)S(1)}, bf16[4,64,512]{2,1,0:T(8,128)(2,1)S(1)}, u32[]{:S(2)}, u32[]{:S(2)}) collective-permute-start(bf16[4,64,512]{2,1,0:T(8,128)(2,1)S(1)} %get-tuple-element.38), channel_id=1, source_target_pairs={{0,16},{4,12},{8,24},{12,4},{16,0},{20,28},{24,8},{28,20},{1,17},{... | collective-permute-start | bytes 786440 | tf_op jit(solution)/shard_map/ppermute | solution.py:48
  46.2 8.6 %collective-permute-start.9 = (bf16[4,64,512]{2,1,0:T(8,128)(2,1)S(1)}, bf16[4,64,512]{2,1,0:T(8,128)(2,1)S(1)}, u32[]{:S(2)}, u32[]{:S(2)}) collective-permute-start(bf16[4,64,512]{2,1,0:T(8,128)(2,1)S(1)} %get-tuple-element.36), channel_id=1, source_target_pairs={{0,16},{4,12},{8,24},{12,4},{16,0},{20,28},{24,8},{28,20},{1,17},{... | collective-permute-start | bytes 786440 | tf_op jit(solution)/shard_map/ppermute | solution.py:48
  50.9 8.9 %collective-permute-start.11 = (bf16[4,64,512]{2,1,0:T(8,128)(2,1)S(1)}, bf16[4,64,512]{2,1,0:T(8,128)(2,1)S(1)}, u32[]{:S(2)}, u32[]{:S(2)}) collective-permute-start(bf16[4,64,512]{2,1,0:T(8,128)(2,1)S(1)} %add_terms.10.refs_2_), channel_id=1, source_target_pairs={{0,8},{4,20},{8,0},{12,28},{16,24},{20,4},{24,16},{28,12},{1,9},{5... | collective-permute-start | bytes 786440 | tf_op jit(solution)/shard_map/ppermute | solution.py:48
  53.2 14.0 %collective-permute-start.15 = (bf16[4,64,512]{2,1,0:T(8,128)(2,1)S(1)}, bf16[4,64,512]{2,1,0:T(8,128)(2,1)S(1)}, u32[]{:S(2)}, u32[]{:S(2)}) collective-permute-start(bf16[4,64,512]{2,1,0:T(8,128)(2,1)S(1)} %get-tuple-element.41), channel_id=1, source_target_pairs={{0,16},{4,12},{8,24},{12,4},{16,0},{20,28},{24,8},{28,20},{1,17},{... | collective-permute-start | bytes 786440 | tf_op jit(solution)/shard_map/ppermute | solution.py:48
  60.0 8.9 %collective-permute-start.12 = (bf16[64,512]{1,0:T(8,128)(2,1)S(1)}, bf16[64,512]{1,0:T(8,128)(2,1)S(1)}, u32[]{:S(2)}, u32[]{:S(2)}) collective-permute-start(bf16[64,512]{1,0:T(8,128)(2,1)S(1)} %get-tuple-element.83), channel_id=1, source_target_pairs={{0,1},{1,2},{2,3},{3,0},{4,5},{5,6},{6,7},{7,4},{8,9},{9,10},{10,1... | collective-permute-start | bytes 196616 | tf_op jit(solution)/shard_map/ppermute | solution.py:62
  62.0 6.9 %collective-permute-start.13 = (bf16[64,512]{1,0:T(8,128)(2,1)S(1)}, bf16[64,512]{1,0:T(8,128)(2,1)S(1)}, u32[]{:S(2)}, u32[]{:S(2)}) collective-permute-start(bf16[64,512]{1,0:T(8,128)(2,1)S(1)} %get-tuple-element.82), channel_id=1, source_target_pairs={{0,2},{1,3},{2,0},{3,1},{4,6},{5,7},{6,4},{7,5},{8,10},{9,11},{10,... | collective-permute-start | bytes 196616 | tf_op jit(solution)/shard_map/ppermute | solution.py:62
  64.6 4.3 %collective-permute-start.14 = (bf16[64,512]{1,0:T(8,128)(2,1)S(1)}, bf16[64,512]{1,0:T(8,128)(2,1)S(1)}, u32[]{:S(2)}, u32[]{:S(2)}) collective-permute-start(bf16[64,512]{1,0:T(8,128)(2,1)S(1)} %get-tuple-element.81), channel_id=1, source_target_pairs={{0,3},{1,0},{2,1},{3,2},{4,7},{5,4},{6,5},{7,6},{8,11},{9,8},{10,9... | collective-permute-start | bytes 196616 | tf_op jit(solution)/shard_map/ppermute | solution.py:62
  65.9 7.9 %collective-permute-start.23 = (bf16[4,64,512]{2,1,0:T(8,128)(2,1)S(1)}, bf16[4,64,512]{2,1,0:T(8,128)(2,1)S(1)}, u32[]{:S(2)}, u32[]{:S(2)}) collective-permute-start(bf16[4,64,512]{2,1,0:T(8,128)(2,1)S(1)} %get-tuple-element.42), channel_id=1, source_target_pairs={{0,16},{4,12},{8,24},{12,4},{16,0},{20,28},{24,8},{28,20},{1,17},{... | collective-permute-start | bytes 786440 | tf_op jit(solution)/shard_map/ppermute | solution.py:48
  67.3 6.5 %collective-permute-start.24 = (bf16[4,64,512]{2,1,0:T(8,128)(2,1)S(1)}, bf16[4,64,512]{2,1,0:T(8,128)(2,1)S(1)}, u32[]{:S(2)}, u32[]{:S(2)}) collective-permute-start(bf16[4,64,512]{2,1,0:T(8,128)(2,1)S(1)} %add_terms.12.refs_4_), channel_id=1, source_target_pairs={{0,8},{4,20},{8,0},{12,28},{16,24},{20,4},{24,16},{28,12},{1,9},{5... | collective-permute-start | bytes 786440 | tf_op jit(solution)/shard_map/ppermute | solution.py:48
  68.9 8.9 %collective-permute-start.16 = (bf16[4,64,512]{2,1,0:T(8,128)(2,1)S(1)}, bf16[4,64,512]{2,1,0:T(8,128)(2,1)S(1)}, u32[]{:S(2)}, u32[]{:S(2)}) collective-permute-start(bf16[4,64,512]{2,1,0:T(8,128)(2,1)S(1)} %stack_planes.4.refs_3_.refs_0_), channel_id=1, source_target_pairs={{0,8},{4,20},{8,0},{12,28},{16,24},{20,4},{24,16},{28,12},{1,9},{5... | collective-permute-start | bytes 786440 | tf_op jit(solution)/shard_map/ppermute | solution.py:48
  69.8 17.8 %collective-permute-start.17 = (bf16[4,64,512]{2,1,0:T(8,128)(2,1)S(1)}, bf16[4,64,512]{2,1,0:T(8,128)(2,1)S(1)}, u32[]{:S(2)}, u32[]{:S(2)}) collective-permute-start(bf16[4,64,512]{2,1,0:T(8,128)(2,1)S(1)} %stack_planes.4.refs_3_.refs_0_), channel_id=1, source_target_pairs={{0,16},{4,12},{8,24},{12,4},{16,0},{20,28},{24,8},{28,20},{1,17},{... | collective-permute-start | bytes 786440 | tf_op jit(solution)/shard_map/ppermute | solution.py:48
  77.8 10.3 %collective-permute-start.18 = (bf16[4,64,512]{2,1,0:T(8,128)(2,1)S(1)}, bf16[4,64,512]{2,1,0:T(8,128)(2,1)S(1)}, u32[]{:S(2)}, u32[]{:S(2)}) collective-permute-start(bf16[4,64,512]{2,1,0:T(8,128)(2,1)S(1)} %collective-permute-done.16.refs_1_), channel_id=1, source_target_pairs={{0,16},{4,12},{8,24},{12,4},{16,0},{20,28},{24,8},{28,20},{1,17},{... | collective-permute-start | bytes 786440 | tf_op jit(solution)/shard_map/ppermute | solution.py:48
  77.9 6.2 %collective-permute-start.25 = (bf16[64,512]{1,0:T(8,128)(2,1)S(1)}, bf16[64,512]{1,0:T(8,128)(2,1)S(1)}, u32[]{:S(2)}, u32[]{:S(2)}) collective-permute-start(bf16[64,512]{1,0:T(8,128)(2,1)S(1)} %get-tuple-element.79), channel_id=1, source_target_pairs={{0,1},{1,2},{2,3},{3,0},{4,5},{5,6},{6,7},{7,4},{8,9},{9,10},{10,1... | collective-permute-start | bytes 196616 | tf_op jit(solution)/shard_map/ppermute | solution.py:62
  78.6 6.6 %collective-permute-start.26 = (bf16[64,512]{1,0:T(8,128)(2,1)S(1)}, bf16[64,512]{1,0:T(8,128)(2,1)S(1)}, u32[]{:S(2)}, u32[]{:S(2)}) collective-permute-start(bf16[64,512]{1,0:T(8,128)(2,1)S(1)} %get-tuple-element.78), channel_id=1, source_target_pairs={{0,2},{1,3},{2,0},{3,1},{4,6},{5,7},{6,4},{7,5},{8,10},{9,11},{10,... | collective-permute-start | bytes 196616 | tf_op jit(solution)/shard_map/ppermute | solution.py:62
  81.4 4.4 %collective-permute-start.27 = (bf16[64,512]{1,0:T(8,128)(2,1)S(1)}, bf16[64,512]{1,0:T(8,128)(2,1)S(1)}, u32[]{:S(2)}, u32[]{:S(2)}) collective-permute-start(bf16[64,512]{1,0:T(8,128)(2,1)S(1)} %get-tuple-element.77), channel_id=1, source_target_pairs={{0,3},{1,0},{2,1},{3,2},{4,7},{5,4},{6,5},{7,6},{8,11},{9,8},{10,9... | collective-permute-start | bytes 196616 | tf_op jit(solution)/shard_map/ppermute | solution.py:62
  84.1 4.1 %collective-permute-start.19 = (bf16[4,64,512]{2,1,0:T(8,128)(2,1)S(1)}, bf16[4,64,512]{2,1,0:T(8,128)(2,1)S(1)}, u32[]{:S(2)}, u32[]{:S(2)}) collective-permute-start(bf16[4,64,512]{2,1,0:T(8,128)(2,1)S(1)} %stack_planes.4.refs_3_.refs_0_), channel_id=1, source_target_pairs={{0,4},{4,0},{8,12},{12,8},{16,20},{20,16},{24,28},{28,24},{1,5},{5... | collective-permute-start | bytes 786440 | tf_op jit(solution)/shard_map/ppermute | solution.py:433
  85.9 7.6 %collective-permute-start.28 = (bf16[4,64,512]{2,1,0:T(8,128)(2,1)S(1)}, bf16[4,64,512]{2,1,0:T(8,128)(2,1)S(1)}, u32[]{:S(2)}, u32[]{:S(2)}) collective-permute-start(bf16[4,64,512]{2,1,0:T(8,128)(2,1)S(1)} %stack_planes.5.refs_0_), channel_id=1, source_target_pairs={{0,8},{4,20},{8,0},{12,28},{16,24},{20,4},{24,16},{28,12},{1,9},{5... | collective-permute-start | bytes 786440 | tf_op jit(solution)/shard_map/ppermute | solution.py:48
  87.6 8.4 %collective-permute-start.21 = (bf16[4,64,512]{2,1,0:T(8,128)(2,1)S(1)}, bf16[4,64,512]{2,1,0:T(8,128)(2,1)S(1)}, u32[]{:S(2)}, u32[]{:S(2)}) collective-permute-start(bf16[4,64,512]{2,1,0:T(8,128)(2,1)S(1)} %collective-permute-done.16.refs_1_), channel_id=1, source_target_pairs={{0,4},{4,0},{8,12},{12,8},{16,20},{20,16},{24,28},{28,24},{1,5},{5... | collective-permute-start | bytes 786440 | tf_op jit(solution)/shard_map/ppermute | solution.py:433
  87.6 8.4 %collective-permute-start.20 = (bf16[4,64,512]{2,1,0:T(8,128)(2,1)S(1)}, bf16[4,64,512]{2,1,0:T(8,128)(2,1)S(1)}, u32[]{:S(2)}, u32[]{:S(2)}) collective-permute-start(bf16[4,64,512]{2,1,0:T(8,128)(2,1)S(1)} %collective-permute-done.17.refs_2_), channel_id=1, source_target_pairs={{0,4},{4,0},{8,12},{12,8},{16,20},{20,16},{24,28},{28,24},{1,5},{5... | collective-permute-start | bytes 786440 | tf_op jit(solution)/shard_map/ppermute | solution.py:433
  88.1 7.9 %collective-permute-start.22 = (bf16[4,64,512]{2,1,0:T(8,128)(2,1)S(1)}, bf16[4,64,512]{2,1,0:T(8,128)(2,1)S(1)}, u32[]{:S(2)}, u32[]{:S(2)}) collective-permute-start(bf16[4,64,512]{2,1,0:T(8,128)(2,1)S(1)} %collective-permute-done.18.refs_3_), channel_id=1, source_target_pairs={{0,4},{4,0},{8,12},{12,8},{16,20},{20,16},{24,28},{28,24},{1,5},{5... | collective-permute-start | bytes 786440 | tf_op jit(solution)/shard_map/ppermute | solution.py:433
  88.2 15.9 %collective-permute-start.35 = (bf16[4,64,512]{2,1,0:T(8,128)(2,1)S(1)}, bf16[4,64,512]{2,1,0:T(8,128)(2,1)S(1)}, u32[]{:S(2)}, u32[]{:S(2)}) collective-permute-start(bf16[4,64,512]{2,1,0:T(8,128)(2,1)S(1)} %stack_planes.5.refs_0_), channel_id=1, source_target_pairs={{0,16},{4,12},{8,24},{12,4},{16,0},{20,28},{24,8},{28,20},{1,17},{... | collective-permute-start | bytes 786440 | tf_op jit(solution)/shard_map/ppermute | solution.py:48
  93.5 11.0 %collective-permute-start.36 = (bf16[4,64,512]{2,1,0:T(8,128)(2,1)S(1)}, bf16[4,64,512]{2,1,0:T(8,128)(2,1)S(1)}, u32[]{:S(2)}, u32[]{:S(2)}) collective-permute-start(bf16[4,64,512]{2,1,0:T(8,128)(2,1)S(1)} %collective-permute-done.28.refs_10_.refs_1_), channel_id=1, source_target_pairs={{0,16},{4,12},{8,24},{12,4},{16,0},{20,28},{24,8},{28,20},{1,17},{... | collective-permute-start | bytes 786440 | tf_op jit(solution)/shard_map/ppermute | solution.py:48
  103.5 1.6 collective-permute-start.30
  103.5 3.5 %collective-permute-start.31 = (bf16[4,64,512]{2,1,0:T(8,128)(2,1)S(1)}, bf16[4,64,512]{2,1,0:T(8,128)(2,1)S(1)}, u32[]{:S(2)}, u32[]{:S(2)}) collective-permute-start(bf16[4,64,512]{2,1,0:T(8,128)(2,1)S(1)} %get-tuple-element.48), channel_id=1, source_target_pairs={{0,4},{4,0},{8,12},{12,8},{16,20},{20,16},{24,28},{28,24},{1,5},{5... | collective-permute-start | bytes 786440 | tf_op jit(solution)/shard_map/ppermute | solution.py:433
  104.0 3.6 %collective-permute-start.37 = (bf16[4,64,512]{2,1,0:T(8,128)(2,1)S(1)}, bf16[4,64,512]{2,1,0:T(8,128)(2,1)S(1)}, u32[]{:S(2)}, u32[]{:S(2)}) collective-permute-start(bf16[4,64,512]{2,1,0:T(8,128)(2,1)S(1)} %stack_planes.5.refs_0_), channel_id=1, source_target_pairs={{0,4},{4,0},{8,12},{12,8},{16,20},{20,16},{24,28},{28,24},{1,5},{5... | collective-permute-start | bytes 786440 | tf_op jit(solution)/shard_map/ppermute | solution.py:433
  104.1 3.6 %collective-permute-start.39 = (bf16[4,64,512]{2,1,0:T(8,128)(2,1)S(1)}, bf16[4,64,512]{2,1,0:T(8,128)(2,1)S(1)}, u32[]{:S(2)}, u32[]{:S(2)}) collective-permute-start(bf16[4,64,512]{2,1,0:T(8,128)(2,1)S(1)} %collective-permute-done.28.refs_10_.refs_1_), channel_id=1, source_target_pairs={{0,4},{4,0},{8,12},{12,8},{16,20},{20,16},{24,28},{28,24},{1,5},{5... | collective-permute-start | bytes 786440 | tf_op jit(solution)/shard_map/ppermute | solution.py:433
  104.6 3.2 %collective-permute-start.38 = (bf16[4,64,512]{2,1,0:T(8,128)(2,1)S(1)}, bf16[4,64,512]{2,1,0:T(8,128)(2,1)S(1)}, u32[]{:S(2)}, u32[]{:S(2)}) collective-permute-start(bf16[4,64,512]{2,1,0:T(8,128)(2,1)S(1)} %collective-permute-done.35.refs_2_), channel_id=1, source_target_pairs={{0,4},{4,0},{8,12},{12,8},{16,20},{20,16},{24,28},{28,24},{1,5},{5... | collective-permute-start | bytes 786440 | tf_op jit(solution)/shard_map/ppermute | solution.py:433
  105.1 2.7 %collective-permute-start.40 = (bf16[4,64,512]{2,1,0:T(8,128)(2,1)S(1)}, bf16[4,64,512]{2,1,0:T(8,128)(2,1)S(1)}, u32[]{:S(2)}, u32[]{:S(2)}) collective-permute-start(bf16[4,64,512]{2,1,0:T(8,128)(2,1)S(1)} %collective-permute-done.36.refs_3_), channel_id=1, source_target_pairs={{0,4},{4,0},{8,12},{12,8},{16,20},{20,16},{24,28},{28,24},{1,5},{5... | collective-permute-start | bytes 786440 | tf_op jit(solution)/shard_map/ppermute | solution.py:433
  107.0 10.9 %collective-permute-start.33 = (bf16[4,64,512]{2,1,0:T(8,128)(2,1)S(1)}, bf16[4,64,512]{2,1,0:T(8,128)(2,1)S(1)}, u32[]{:S(2)}, u32[]{:S(2)}) collective-permute-start(bf16[4,64,512]{2,1,0:T(8,128)(2,1)S(1)} %get-tuple-element.51), channel_id=1, source_target_pairs={{0,4},{4,0},{8,12},{12,8},{16,20},{20,16},{24,28},{28,24},{1,5},{5... | collective-permute-start | bytes 786440 | tf_op jit(solution)/shard_map/ppermute | solution.py:433
  107.6 10.3 %collective-permute-start.34 = (bf16[4,64,512]{2,1,0:T(8,128)(2,1)S(1)}, bf16[4,64,512]{2,1,0:T(8,128)(2,1)S(1)}, u32[]{:S(2)}, u32[]{:S(2)}) collective-permute-start(bf16[4,64,512]{2,1,0:T(8,128)(2,1)S(1)} %get-tuple-element.52), channel_id=1, source_target_pairs={{0,16},{4,12},{8,24},{12,4},{16,0},{20,28},{24,8},{28,20},{1,17},{... | collective-permute-start | bytes 786440 | tf_op jit(solution)/shard_map/ppermute | solution.py:48
  115.0 5.2 %collective-permute-start.42 = (bf16[4,64,512]{2,1,0:T(8,128)(2,1)S(1)}, bf16[4,64,512]{2,1,0:T(8,128)(2,1)S(1)}, u32[]{:S(2)}, u32[]{:S(2)}) collective-permute-start(bf16[4,64,512]{2,1,0:T(8,128)(2,1)S(1)} %get-tuple-element.55), channel_id=1, source_target_pairs={{0,4},{4,0},{8,12},{12,8},{16,20},{20,16},{24,28},{28,24},{1,5},{5... | collective-permute-start | bytes 786440 | tf_op jit(solution)/shard_map/ppermute | solution.py:433
  117.4 4.8 %collective-permute-start.43 = (bf16[4,64,512]{2,1,0:T(8,128)(2,1)S(1)}, bf16[4,64,512]{2,1,0:T(8,128)(2,1)S(1)}, u32[]{:S(2)}, u32[]{:S(2)}) collective-permute-start(bf16[4,64,512]{2,1,0:T(8,128)(2,1)S(1)} %get-tuple-element.57), channel_id=1, source_target_pairs={{0,4},{4,0},{8,12},{12,8},{16,20},{20,16},{24,28},{28,24},{1,5},{5... | collective-permute-start | bytes 786440 | tf_op jit(solution)/shard_map/ppermute | solution.py:433
  117.4 5.4 %collective-permute-start.29 = (bf16[4,64,512]{2,1,0:T(8,128)(2,1)S(1)}, bf16[4,64,512]{2,1,0:T(8,128)(2,1)S(1)}, u32[]{:S(2)}, u32[]{:S(2)}) collective-permute-start(bf16[4,64,512]{2,1,0:T(8,128)(2,1)S(1)} %get-tuple-element.43.refs_4_), channel_id=1, source_target_pairs={{0,4},{4,0},{8,12},{12,8},{16,20},{20,16},{24,28},{28,24},{1,5},{5... | collective-permute-start | bytes 786440 | tf_op jit(solution)/shard_map/ppermute | solution.py:433
  117.9 7.3 %collective-permute-start.32 = (bf16[4,64,512]{2,1,0:T(8,128)(2,1)S(1)}, bf16[4,64,512]{2,1,0:T(8,128)(2,1)S(1)}, u32[]{:S(2)}, u32[]{:S(2)}) collective-permute-start(bf16[4,64,512]{2,1,0:T(8,128)(2,1)S(1)} %get-tuple-element.49.refs_10_), channel_id=1, source_target_pairs={{0,16},{4,12},{8,24},{12,4},{16,0},{20,28},{24,8},{28,20},{1,17},{... | collective-permute-start | bytes 786440 | tf_op jit(solution)/shard_map/ppermute | solution.py:48
  117.9 11.1 %collective-permute-start.47 = (bf16[4,64,512]{2,1,0:T(8,128)(2,1)S(1)}, bf16[4,64,512]{2,1,0:T(8,128)(2,1)S(1)}, u32[]{:S(2)}, u32[]{:S(2)}) collective-permute-start(bf16[4,64,512]{2,1,0:T(8,128)(2,1)S(1)} %get-tuple-element.61), channel_id=1, source_target_pairs={{0,4},{4,0},{8,12},{12,8},{16,20},{20,16},{24,28},{28,24},{1,5},{5... | collective-permute-start | bytes 786440 | tf_op jit(solution)/shard_map/ppermute | solution.py:433
  120.3 8.6 %collective-permute-start.41 = (bf16[4,64,512]{2,1,0:T(8,128)(2,1)S(1)}, bf16[4,64,512]{2,1,0:T(8,128)(2,1)S(1)}, u32[]{:S(2)}, u32[]{:S(2)}) collective-permute-start(bf16[4,64,512]{2,1,0:T(8,128)(2,1)S(1)} %add_terms.15.refs_4_), channel_id=1, source_target_pairs={{0,8},{4,20},{8,0},{12,28},{16,24},{20,4},{24,16},{28,12},{1,9},{5... | collective-permute-start | bytes 786440 | tf_op jit(solution)/shard_map/ppermute | solution.py:48
  122.3 7.6 %collective-permute-start.48 = (bf16[4,64,512]{2,1,0:T(8,128)(2,1)S(1)}, bf16[4,64,512]{2,1,0:T(8,128)(2,1)S(1)}, u32[]{:S(2)}, u32[]{:S(2)}) collective-permute-start(bf16[4,64,512]{2,1,0:T(8,128)(2,1)S(1)} %get-tuple-element.62), channel_id=1, source_target_pairs={{0,16},{4,12},{8,24},{12,4},{16,0},{20,28},{24,8},{28,20},{1,17},{... | collective-permute-start | bytes 786440 | tf_op jit(solution)/shard_map/ppermute | solution.py:48
  122.9 19.2 %collective-permute-start.52 = (bf16[4,64,512]{2,1,0:T(8,128)(2,1)S(1)}, bf16[4,64,512]{2,1,0:T(8,128)(2,1)S(1)}, u32[]{:S(2)}, u32[]{:S(2)}) collective-permute-start(bf16[4,64,512]{2,1,0:T(8,128)(2,1)S(1)} %get-tuple-element.53.refs_3_), channel_id=1, source_target_pairs={{0,4},{4,0},{8,12},{12,8},{16,20},{20,16},{24,28},{28,24},{1,5},{5... | collective-permute-start | bytes 786440 | tf_op jit(solution)/shard_map/ppermute | solution.py:433
  125.1 17.0 %collective-permute-start.53 = (bf16[4,64,512]{2,1,0:T(8,128)(2,1)S(1)}, bf16[4,64,512]{2,1,0:T(8,128)(2,1)S(1)}, u32[]{:S(2)}, u32[]{:S(2)}) collective-permute-start(bf16[4,64,512]{2,1,0:T(8,128)(2,1)S(1)} %get-tuple-element.59.refs_4_), channel_id=1, source_target_pairs={{0,16},{4,12},{8,24},{12,4},{16,0},{20,28},{24,8},{28,20},{1,17},{... | collective-permute-start | bytes 786440 | tf_op jit(solution)/shard_map/ppermute | solution.py:48
  130.0 12.2 %collective-permute-start.54 = (bf16[4,64,512]{2,1,0:T(8,128)(2,1)S(1)}, bf16[4,64,512]{2,1,0:T(8,128)(2,1)S(1)}, u32[]{:S(2)}, u32[]{:S(2)}) collective-permute-start(bf16[4,64,512]{2,1,0:T(8,128)(2,1)S(1)} %add_terms.18.refs_4_), channel_id=1, source_target_pairs={{0,8},{4,20},{8,0},{12,28},{16,24},{20,4},{24,16},{28,12},{1,9},{5... | collective-permute-start | bytes 786440 | tf_op jit(solution)/shard_map/ppermute | solution.py:48
  131.7 6.1 %collective-permute-start.44 = (bf16[64,512]{1,0:T(8,128)(2,1)S(1)}, bf16[64,512]{1,0:T(8,128)(2,1)S(1)}, u32[]{:S(2)}, u32[]{:S(2)}) collective-permute-start(bf16[64,512]{1,0:T(8,128)(2,1)S(1)} %get-tuple-element.75), channel_id=1, source_target_pairs={{0,1},{1,2},{2,3},{3,0},{4,5},{5,6},{6,7},{7,4},{8,9},{9,10},{10,1... | collective-permute-start | bytes 196616 | tf_op jit(solution)/shard_map/ppermute | solution.py:62
  133.3 6.7 %collective-permute-start.45 = (bf16[64,512]{1,0:T(8,128)(2,1)S(1)}, bf16[64,512]{1,0:T(8,128)(2,1)S(1)}, u32[]{:S(2)}, u32[]{:S(2)}) collective-permute-start(bf16[64,512]{1,0:T(8,128)(2,1)S(1)} %get-tuple-element.74), channel_id=1, source_target_pairs={{0,2},{1,3},{2,0},{3,1},{4,6},{5,7},{6,4},{7,5},{8,10},{9,11},{10,... | collective-permute-start | bytes 196616 | tf_op jit(solution)/shard_map/ppermute | solution.py:62
  137.8 4.3 %collective-permute-start.46 = (bf16[64,512]{1,0:T(8,128)(2,1)S(1)}, bf16[64,512]{1,0:T(8,128)(2,1)S(1)}, u32[]{:S(2)}, u32[]{:S(2)}) collective-permute-start(bf16[64,512]{1,0:T(8,128)(2,1)S(1)} %get-tuple-element.73), channel_id=1, source_target_pairs={{0,3},{1,0},{2,1},{3,2},{4,7},{5,4},{6,5},{7,6},{8,11},{9,8},{10,9... | collective-permute-start | bytes 196616 | tf_op jit(solution)/shard_map/ppermute | solution.py:62
  142.3 6.2 %collective-permute-start.55 = (bf16[64,512]{1,0:T(8,128)(2,1)S(1)}, bf16[64,512]{1,0:T(8,128)(2,1)S(1)}, u32[]{:S(2)}, u32[]{:S(2)}) collective-permute-start(bf16[64,512]{1,0:T(8,128)(2,1)S(1)} %get-tuple-element.71), channel_id=1, source_target_pairs={{0,1},{1,2},{2,3},{3,0},{4,5},{5,6},{6,7},{7,4},{8,9},{9,10},{10,1... | collective-permute-start | bytes 196616 | tf_op jit(solution)/shard_map/ppermute | solution.py:62
  142.4 7.4 %collective-permute-start.56 = (bf16[64,512]{1,0:T(8,128)(2,1)S(1)}, bf16[64,512]{1,0:T(8,128)(2,1)S(1)}, u32[]{:S(2)}, u32[]{:S(2)}) collective-permute-start(bf16[64,512]{1,0:T(8,128)(2,1)S(1)} %get-tuple-element.70), channel_id=1, source_target_pairs={{0,2},{1,3},{2,0},{3,1},{4,6},{5,7},{6,4},{7,5},{8,10},{9,11},{10,... | collective-permute-start | bytes 196616 | tf_op jit(solution)/shard_map/ppermute | solution.py:62
  146.5 4.3 %collective-permute-start.57 = (bf16[64,512]{1,0:T(8,128)(2,1)S(1)}, bf16[64,512]{1,0:T(8,128)(2,1)S(1)}, u32[]{:S(2)}, u32[]{:S(2)}) collective-permute-start(bf16[64,512]{1,0:T(8,128)(2,1)S(1)} %get-tuple-element.69), channel_id=1, source_target_pairs={{0,3},{1,0},{2,1},{3,2},{4,7},{5,4},{6,5},{7,6},{8,11},{9,8},{10,9... | collective-permute-start | bytes 196616 | tf_op jit(solution)/shard_map/ppermute | solution.py:62
  146.5 9.2 %collective-permute-start.49 = (bf16[4,64,512]{2,1,0:T(8,128)(2,1)S(1)}, bf16[4,64,512]{2,1,0:T(8,128)(2,1)S(1)}, u32[]{:S(2)}, u32[]{:S(2)}) collective-permute-start(bf16[4,64,512]{2,1,0:T(8,128)(2,1)S(1)} %stack_planes.6.refs_4_.refs_2_), channel_id=1, source_target_pairs={{0,8},{4,20},{8,0},{12,28},{16,24},{20,4},{24,16},{28,12},{1,9},{5... | collective-permute-start | bytes 786440 | tf_op jit(solution)/shard_map/ppermute | solution.py:48
  150.7 10.5 %collective-permute-start.58 = (bf16[4,64,512]{2,1,0:T(8,128)(2,1)S(1)}, bf16[4,64,512]{2,1,0:T(8,128)(2,1)S(1)}, u32[]{:S(2)}, u32[]{:S(2)}) collective-permute-start(bf16[4,64,512]{2,1,0:T(8,128)(2,1)S(1)} %stack_planes.7.refs_6_), channel_id=1, source_target_pairs={{0,8},{4,20},{8,0},{12,28},{16,24},{20,4},{24,16},{28,12},{1,9},{5... | collective-permute-start | bytes 786440 | tf_op jit(solution)/shard_map/ppermute | solution.py:48
  151.1 10.9 %collective-permute-start.50 = (bf16[4,64,512]{2,1,0:T(8,128)(2,1)S(1)}, bf16[4,64,512]{2,1,0:T(8,128)(2,1)S(1)}, u32[]{:S(2)}, u32[]{:S(2)}) collective-permute-start(bf16[4,64,512]{2,1,0:T(8,128)(2,1)S(1)} %stack_planes.6.refs_4_.refs_2_), channel_id=1, source_target_pairs={{0,16},{4,12},{8,24},{12,4},{16,0},{20,28},{24,8},{28,20},{1,17},{... | collective-permute-start | bytes 786440 | tf_op jit(solution)/shard_map/ppermute | solution.py:48
  152.9 9.0 %collective-permute-start.59 = (bf16[4,64,512]{2,1,0:T(8,128)(2,1)S(1)}, bf16[4,64,512]{2,1,0:T(8,128)(2,1)S(1)}, u32[]{:S(2)}, u32[]{:S(2)}) collective-permute-start(bf16[4,64,512]{2,1,0:T(8,128)(2,1)S(1)} %stack_planes.7.refs_6_), channel_id=1, source_target_pairs={{0,16},{4,12},{8,24},{12,4},{16,0},{20,28},{24,8},{28,20},{1,17},{... | collective-permute-start | bytes 786440 | tf_op jit(solution)/shard_map/ppermute | solution.py:48
  155.6 7.5 %collective-permute-start.51 = (bf16[4,64,512]{2,1,0:T(8,128)(2,1)S(1)}, bf16[4,64,512]{2,1,0:T(8,128)(2,1)S(1)}, u32[]{:S(2)}, u32[]{:S(2)}) collective-permute-start(bf16[4,64,512]{2,1,0:T(8,128)(2,1)S(1)} %collective-permute-done.49.refs_3_), channel_id=1, source_target_pairs={{0,16},{4,12},{8,24},{12,4},{16,0},{20,28},{24,8},{28,20},{1,17},{... | collective-permute-start | bytes 786440 | tf_op jit(solution)/shard_map/ppermute | solution.py:48
  161.2 6.4 %collective-permute-start.60 = (bf16[4,64,512]{2,1,0:T(8,128)(2,1)S(1)}, bf16[4,64,512]{2,1,0:T(8,128)(2,1)S(1)}, u32[]{:S(2)}, u32[]{:S(2)}) collective-permute-start(bf16[4,64,512]{2,1,0:T(8,128)(2,1)S(1)} %collective-permute-done.58.refs_7_), channel_id=1, source_target_pairs={{0,16},{4,12},{8,24},{12,4},{16,0},{20,28},{24,8},{28,20},{1,17},{... | collective-permute-start | bytes 786440 | tf_op jit(solution)/shard_map/ppermute | solution.py:48
  169.0 2.0 %collective-permute-start.61 = (bf16[8,64,512]{2,1,0:T(8,128)(2,1)S(1)}, bf16[8,64,512]{2,1,0:T(8,128)(2,1)S(1)}, u32[]{:S(2)}, u32[]{:S(2)}) collective-permute-start(bf16[8,64,512]{2,1,0:T(8,128)(2,1)S(1)} %get-tuple-element.64), channel_id=1, source_target_pairs={{0,4},{4,0},{8,12},{12,8},{16,20},{20,16},{24,28},{28,24},{1,5},{5... | collective-permute-start | bytes 1572872 | tf_op jit(solution)/shard_map/ppermute | solution.py:433
  (8 other events, 158.9 us)

commit v7 on v6

--- a/solution.py
+++ b/solution.py
@@ -8,6 +8,10 @@
 BLK = 128
 CAP = 4
 GROUPS = 2
+DIRECT = ((0, 0, 0, 0), (0, 1, 1, 0))
+PICK_WAIT = (0, 0)
+HOP_WAIT = ((0, 1), (0, 0))
+ORDER = '001010110010001011101011'
 
 
 def bit_orders(n_bits):
@@ -48,11 +52,52 @@
     return lax.ppermute(value, "dp", step_pairs(n_dp, step))
 
 
-def gather_all(piece, n_dp, n_bits):
+def gather_steps(piece, n_dp, n_bits):
     pieces = [piece]
     for step in range(n_bits):
         pieces = pieces + [exchange(p, n_dp, step) for p in pieces]
     return pieces
+
+
+def gather(piece, n_dp, n_bits, at_once):
+    if at_once:
+        return direct([piece] * (1 << n_bits), n_dp, n_bits)
+    return gather_steps(piece, n_dp, n_bits)
+
+
+def scatter(terms, n_dp, n_bits, at_once, hop_wait, wait, after):
+    if at_once:
+        if len(terms[0]) > 1:
+            terms = [[t] for t in add_terms(terms, [after])]
+            after = yield terms[0][0], None
+        got = direct([t[0] for t in terms], n_dp, n_bits)
+        if wait:
+            after = yield got[1], None
+        mine = add_terms([got], [after])[0]
+        after = yield mine, None
+        return mine, after
+    for step in range(n_bits - 1, -1, -1):
+        half_way = 1 << step
+        send = [t[0] for t in terms[half_way:]]
+        if len(terms[half_way]) > 1:
+            others = [t[-1] for t in terms[:half_way]] if hop_wait else []
+            send = add_terms(terms[half_way:], [after] + others)
+            after = yield send[0], None
+        terms = [t + [exchange(s, n_dp, step)] for t, s in zip(terms, send)]
+        if wait and step == n_bits - 1:
+            after = yield terms[half_way - 1][-1], None
+    mine = add_terms(terms, [after])[0]
+    after = yield mine, None
+    return mine, after
+
+
+def direct(values, n_dp, n_bits):
+    masks = [masks_of(n_bits, side) for side in (0, 1)]
+    out = []
+    for r, value in enumerate(values):
+        pairs = [(i, i ^ (masks[i & 1][r] << 1)) for i in range(n_dp)]
+        out.append(lax.ppermute(value, "dp", pairs) if r else value)
+    return out
 
 
 def swap_planes(parts, n_expert, after=None):
@@ -85,17 +130,17 @@
         out[...] = total.astype(out.dtype)
 
 
-def add_terms(terms, after):
+def add_terms(terms, unread):
     counts = [len(t) for t in terms]
     shapes = [jax.ShapeDtypeStruct(t[0].shape, t[0].dtype) for t in terms]
     return call(
         lambda *refs: add_kernel(counts, *refs),
         shapes,
-        [VMEM] * sum(counts) + [ANY],
+        [VMEM] * sum(counts) + [ANY] * len(unread),
         [VMEM] * len(counts),
         "add_terms",
         8,
-    )(*[x for t in terms for x in t], after)
+    )(*[x for t in terms for x in t], *unread)
 
 
 def stack_kernel(n, *refs):
@@ -180,23 +225,23 @@
         for copy in copies[i * n_w : (i + 1) * n_w]:
             copy.wait()
         value = jnp.dot(c[...], w_all[...], preferred_element_type=jnp.float32)
-        if n_res:
-            acc, *res = extra
-            value = value + acc[i] + res[i][...].astype(jnp.float32)
+        if n_res > 0:
+            value = value + extra[0][i]
+        if n_res > 1:
+            value = value + extra[1 + i][...].astype(jnp.float32)
         out[i] = value.astype(out.dtype)
 
 
-def project(make_place, parts, own, other, weights, extra, unread):
-    last = len(extra) > 0
+def project(make_place, parts, own, other, weights, extra):
     rows = own.shape[0]
     depth, half = weights[0].shape
     k = depth * len(weights)
     return call(
         lambda *refs: project_kernel(make_place, parts, len(weights), len(extra), *refs),
-        jax.ShapeDtypeStruct((2, rows, half), jnp.bfloat16 if last else jnp.float32),
-        [ANY, ANY] + [VMEM] * (len(weights) + len(extra)) + [ANY] * len(unread),
+        jax.ShapeDtypeStruct((2, rows, half), jnp.bfloat16 if len(extra) > 1 else jnp.float32),
+        [ANY, ANY] + [VMEM] * (len(weights) + len(extra)),
         VMEM,
-        "project_last" if last else "project_first",
+        "project",
         12,
         scratch_shapes=[
             pltpu.VMEM((k, half), jnp.bfloat16),
@@ -204,7 +249,7 @@
             pltpu.VMEM((rows, k), jnp.bfloat16),
             pltpu.SemaphoreType.DMA((2, len(weights))),
         ],
-    )(own, other, *weights, *extra, *unread)
+    )(own, other, *weights, *extra)
 
 
 def pick_kernel(make_place, layout, n_chip, chosen, att_ref, *refs):
@@ -230,35 +275,35 @@
     )(chosen, grains, *extra)
 
 
-def finish_kernel(make_place, layouts, n_chip, chosen, att_ref, *refs):
-    pieces, outs, acc = refs[:-3], refs[-3:-1], refs[-1]
+def finish_kernel(make_place, layout, n_chip, lo, hi, chosen, *refs):
+    pieces, old, out = refs[:n_chip], refs[n_chip], refs[n_chip + 1]
+    acc = refs[-1]
     place = make_place()
-    acc[...] = att_ref[...].astype(jnp.float32)
-    for g, layout in enumerate(layouts):
-        for r in range(n_chip):
-            piece = pieces[g * n_chip + r]
-            for k in range(place.n_expert):
-                index, mine = layout.grain(place, chosen, r, place.behind(k))
-
-                @pl.when(mine)
-                def _():
-                    acc[index] = acc[index] + piece[k].astype(jnp.float32)
-
-    n = outs[0].shape[0]
-    for s, out in enumerate(outs):
-        out[...] = acc[s * n : (s + 1) * n].astype(out.dtype)
-
-
-def finish(make_place, layouts, n_chip, chosen, grains, pieces):
-    return call(
-        lambda *refs: finish_kernel(make_place, layouts, n_chip, *refs),
-        [jax.ShapeDtypeStruct((grains.shape[0] // 2,) + grains.shape[1:], grains.dtype)] * 2,
-        [SMEM] + [VMEM] * (1 + len(pieces)),
-        [VMEM] * 2,
+    acc[...] = old[lo:hi].astype(jnp.float32)
+    for r in range(n_chip):
+        for k in range(place.n_expert):
+            index, mine = layout.grain(place, chosen, r, place.behind(k))
+
+            @pl.when(mine & (index >= lo) & (index < hi))
+            def _():
+                acc[index - lo] = acc[index - lo] + pieces[r][k].astype(jnp.float32)
+
+    if acc is not out:
+        out[...] = acc[...].astype(out.dtype)
+
+
+def finish(make_place, layout, n_chip, chosen, old, pieces, lo, hi, last):
+    dtype = jnp.bfloat16 if last else jnp.float32
+    shape = (hi - lo,) + old.shape[1:]
+    return call(
+        lambda *refs: finish_kernel(make_place, layout, n_chip, lo, hi, *refs),
+        jax.ShapeDtypeStruct(shape, dtype),
+        [SMEM] + [VMEM] * (len(pieces) + 1),
+        VMEM,
         "add_expert_rows",
-        12,
-        scratch_shapes=[pltpu.VMEM(grains.shape, jnp.float32)],
-    )(chosen, grains, *pieces)
+        8,
+        scratch_shapes=[pltpu.VMEM(shape, jnp.float32)] if last else (),
+    )(chosen, *pieces, old)
 
 
 def join_kernel(make_place, own, other, out):
@@ -280,17 +325,16 @@
     )(own, other)
 
 
-def hidden_kernel(make_place, n, *refs):
-    own, other, wg, wu = refs[:n], refs[n : 2 * n], *refs[2 * n : 2 * n + 2]
-    hid, xs = refs[-2:]
-    n_z, rows, width = own[0].shape
+def hidden_kernel(make_place, reverse, own, other, wg, wu, after, hid, xs):
+    n_z, rows, width = own.shape[1:]
     place = make_place()
     for s, pieces in enumerate((own, other)):
         for z in range(n_z):
             at = (place.behind(z) * 2 + (place.side ^ s)) * width
             at = pl.ds(pl.multiple_of(at, width), width)
-            for r in range(n):
-                xs[r * rows : (r + 1) * rows, at] = pieces[r][z]
+            for r, to in enumerate(reverse):
+                to = to if s else r
+                xs[to * rows : (to + 1) * rows, at] = pieces[r, z]
     ff = wg.shape[1]
     tile = min(ff, 256)
 
@@ -304,19 +348,18 @@
     lax.fori_loop(0, ff // tile, one, 0)
 
 
-def hidden_units(make_place, own, other, w_gate, w_up, after):
-    n = len(own)
-    n_z, rows, width = own[0].shape
+def hidden_units(make_place, reverse, own, other, w_gate, w_up, after):
+    n_row = own.shape[0] * own.shape[2]
     model_width, ff = w_gate.shape
     return call(
-        lambda *refs: hidden_kernel(make_place, n, *refs),
-        jax.ShapeDtypeStruct((n * rows, ff), jnp.bfloat16),
-        [VMEM] * (2 * n + 2) + [ANY],
+        lambda *refs: hidden_kernel(make_place, reverse, *refs),
+        jax.ShapeDtypeStruct((n_row, ff), jnp.bfloat16),
+        [VMEM] * 4 + [ANY],
         VMEM,
         "expert_hidden",
         12,
-        scratch_shapes=[pltpu.VMEM((n * rows, model_width), jnp.bfloat16)],
-    )(*own, *other, w_gate, w_up, after)
+        scratch_shapes=[pltpu.VMEM((n_row, model_width), jnp.bfloat16)],
+    )(own, other, w_gate, w_up, after)
 
 
 def down_kernel(make_place, layout, order, s, counts, hid, wd, values, after, *outs):
@@ -359,23 +402,20 @@
     n_chip = 1 << n_bits
     plain = list(range(n_chip))
     after = yield
+    modes, hop_wait = DIRECT[layout.group], HOP_WAIT[layout.group]
     terms = [[p] for p in pick(make_place, layout, n_chip, n_expert, chosen, grains, after)]
-    after = yield terms[0][0], None
-    for step in range(n_bits - 1, -1, -1):
-        half_way = 1 << step
-        send = [t[0] for t in terms[half_way:]]
-        if len(terms[half_way]) > 1:
-            send = add_terms(terms[half_way:], after)
-            after = yield send[0], None
-        terms = [t + [exchange(s, n_dp, step)] for t, s in zip(terms, send)]
-    mine = add_terms(terms, after)[0]
-    after = yield mine, None
+    if not PICK_WAIT[layout.group]:
+        after = yield terms[0][0], None
+    mine, after = yield from scatter(
+        terms, n_dp, n_bits, modes[0], hop_wait[0], PICK_WAIT[layout.group], after
+    )
     crossed = swap_planes(mine, n_expert, after)
-    own_half = gather_all(crossed, n_dp, n_bits)
-    after = yield (own_half[1] if layout.group == GROUPS - 1 else crossed), None
-    got = [to_partner(p) for p in own_half]
-    other_half = [got[r] for r in reverse]
-    hid = hidden_units(make_place, own_half, other_half, w_gate, w_up, after)
+    own_half = gather(crossed, n_dp, n_bits, modes[1])
+    after = yield crossed, None
+    own = stack(own_half, after)
+    other = to_partner(own)
+    after = yield own, None
+    hid = hidden_units(make_place, reverse, own, other, w_gate, w_up, after)
     after = yield hid, None
 
     def downs(order, s):
@@ -388,20 +428,9 @@
     mine = downs(plain, 0)
     after = yield mine[0], None
     terms = [[m, to_partner(t)] for m, t in zip(mine, theirs)]
-    for step in range(n_bits - 1, -1, -1):
-        send = add_terms(terms[1 << step :], after)
-        after = yield send[0], None
-        terms = [t + [exchange(s, n_dp, step)] for t, s in zip(terms, send)]
-    mine = add_terms(terms, after)[0]
-    after = yield mine, None
+    mine, after = yield from scatter(terms, n_dp, n_bits, modes[2], hop_wait[1], 0, after)
     crossed = swap_planes(mine, n_expert, after)
-    yield crossed, gather_all(crossed, n_dp, n_bits)
-
-
-def kernel_order(n_bits):
-    order = [0, 0] + [1, 0] * n_bits + [1, 1]
-    order += [0] * 4 + [1] * 2 + [0]
-    return order + [1, 1] + [0, 1] * n_bits + [1]
+    yield crossed, gather(crossed, n_dp, n_bits, modes[3])
 
 
 def body(
@@ -452,24 +481,14 @@
     def make_place():
         return Place(n_bits, n_expert)
 
-    first = project(
-        make_place,
-        plain[:top],
-        context,
-        context_other,
-        pieces[:n_chip],
-        (),
-        (),
-    )
-    attended = project(
-        make_place,
-        plain[top:],
-        context,
-        context_other,
-        pieces[n_chip:],
-        (first, residual_own, residual_other),
-        (),
-    )
+    bounds = [0, top, n_chip - 1, n_chip]
+    total = ()
+    for lo, hi in zip(bounds[:-1], bounds[1:]):
+        if hi == n_chip:
+            total = total + (residual_own, residual_other)
+        part = pieces[2 * lo : 2 * hi]
+        total = (project(make_place, plain[lo:hi], context, context_other, part, total),)
+    attended = total[0]
 
     layouts = [Layout(group, n_chip, local_blocks) for group in range(GROUPS)]
     grains = attended.reshape(-1, share, half)
@@ -481,12 +500,19 @@
     for group in groups:
         next(group)
     after, received = None, [None] * GROUPS
-    for g in kernel_order(n_bits):
-        after, done = groups[g].send(after)
-        received[g] = done
-    received = [piece for pieces in received for piece in pieces]
-
-    own, other = finish(make_place, layouts, n_chip, chosen_blocks, grains, received)
+    turn = 0
+    while any(done is None for done in received):
+        g = int(ORDER[turn]) if turn < len(ORDER) else turn % GROUPS
+        turn += 1
+        if received[g] is None:
+            after, received[g] = groups[g].send(after)
+
+    total, n = grains, grains.shape[0]
+    for layout, got in zip(layouts[:-1], received[:-1]):
+        total = finish(make_place, layout, n_chip, chosen_blocks, total, got, 0, n, False)
+    last = (make_place, layouts[-1], n_chip, chosen_blocks, total, received[-1])
+    other = finish(*last, n // 2, n, True)
+    own = finish(*last, 0, n // 2, True)
     return join(make_place, own, to_partner(other), local_tokens)
 
 

time: 172 us -> 165 us (0.959)
  waiting for transfers between devices: 74.9 us -> 61.4 us
  starting transfers between devices: 61.5 us -> 67.3 us
  Pallas kernels: 30.4 us -> 33.1 us
  local copies, waits for them, and re-layouts: 4.84 us -> 2.81 us
    ppermute x30 -> x24, waiting for transfers between devices: 55.8 us -> 40.1 us  [exchange(): return lax.ppermute(value, 'dp', step_pairs(n_dp, step))]
    ppermute x0 -> x6, waiting for transfers between devices: none -> 10.6 us  [direct(): out.append(lax.ppermute(value, 'dp', pairs) if r else value)]
    ppermute x0 -> x6, starting transfers between devices: none -> 7.64 us  [direct(): out.append(lax.ppermute(value, 'dp', pairs) if r else value)]
    ppermute x12, waiting for transfers between devices: 13.5 us -> 6.86 us  [swap_planes(): out.append(lax.ppermute(parts[k], 'expert', pairs))]
    ppermute x20 -> x14, starting transfers between devices: 6.34 us -> 3.04 us  [to_partner(): return lax.ppermute(value, 'dp', pair)]
    unnamed x20, local copies, waits for them, and re-layouts: 2.23 us -> 0.05 us
    pallas_call x3 -> x5, Pallas kernels: 12.3 us -> 14.1 us  [the longest x2 10.9 us: hidden_units(): call(lambda *refs: hidden_kernel(make_place, reverse, *refs), jax.ShapeDt...]
    ppermute x20 -> x14, waiting for transfers between devices: 5.57 us -> 3.94 us  [to_partner(): return lax.ppermute(value, 'dp', pair)]
  transfers between devices with their start and end apart: 62 -> 56, of which waited for: 27 -> 22; matrix products, arithmetic and copies ran while one was open for 2% -> 2% of each run, Pallas kernels for 14% -> 16%
where the time goes in v7:
time: 165 us
  starting transfers between devices  67.3 us (41%)
  waiting for transfers between devices  61.4 us (37%)
  Pallas kernels  33.1 us (20%)
  local copies, waits for them, and re-layouts  2.81 us (2%)
    ppermute x24, waiting for transfers between devices, exchange(): return lax.ppermute(value, 'dp', step_pairs(n_dp, step))  40.1 us
    ppermute x24, starting transfers between devices, exchange(): return lax.ppermute(value, 'dp', step_pairs(n_dp, step))  36.9 us
    ppermute x12, starting transfers between devices, swap_planes(): out.append(lax.ppermute(parts[k], 'expert', pairs))  19.7 us
    pallas_call x2, Pallas kernels, hidden_units(): call(lambda *refs: hidden_kernel(make_place, reverse, *refs), jax.ShapeDt...  10.9 us
    ppermute x6, waiting for transfers between devices, direct(): out.append(lax.ppermute(value, 'dp', pairs) if r else value)  10.6 us
    pallas_call x3, Pallas kernels, project(): call(lambda *refs: project_kernel(make_place, parts, len(weights), len(ex...  7.82 us
    ppermute x6, starting transfers between devices, direct(): out.append(lax.ppermute(value, 'dp', pairs) if r else value)  7.64 us
    pallas_call x4, Pallas kernels, down(): call(lambda *refs: down_kernel(make_place, layout, order, s, *refs), [jax...  7.3 us
  transfers between devices with their start and end apart: 56, of which 22 were waited for; matrix products, arithmetic and copies ran while one was open for 2% of the time, Pallas kernels for 16%

profile of v7, /device:TPU:0, one launch (start us, length us, event | category | flops | bytes accessed | tf_op | source)
XLA Modules:
  0.0 165.3 jit_solution(2198062872720820580)
XLA Ops:
  0.5 1.4 constant_dynamic-slice_fusion.2
  2.0 2.9 %collective-permute-start.1 = (bf16[512,512]{1,0:T(8,128)(2,1)S(1)}, bf16[512,512]{1,0:T(8,128)(2,1)S(1)}, u32[]{:S(2)}, u32[]{:S(2)}) collective-permute-start(bf16[512,512]{1,0:T(8,128)(2,1)S(1)} %get-tuple-element.68.refs_2_), channel_id=1, source_target_pairs={{0,8},{4,20},{8,0},{12,28},{16,24},{20,4},{24,16},{28,12},{1,9},{5... | collective-permute-start | bytes 1572872 | tf_op jit(solution)/shard_map/ppermute | solution.py:52
  4.9 3.1 %collective-permute-done.3.refs_3_ = bf16[512,512]{1,0:T(8,128)(2,1)S(1)} collective-permute-done((bf16[512,512]{1,0:T(8,128)(2,1)S(1)}, bf16[512,512]{1,0:T(8,128)(2,1)S(1)}, u32[]{:S(2)}, u32[]{:S(2)}) %collective-permute-start.3) | collective-permute-done | bytes 524320 | tf_op jit(solution)/shard_map/ppermute | solution.py:462
  8.0 2.9 %collective-permute-start.4 = (bf16[512,512]{1,0:T(8,128)(2,1)S(1)}, bf16[512,512]{1,0:T(8,128)(2,1)S(1)}, u32[]{:S(2)}, u32[]{:S(2)}) collective-permute-start(bf16[512,512]{1,0:T(8,128)(2,1)S(1)} %collective-permute-done.3.refs_3_), channel_id=1, source_target_pairs={{0,8},{4,20},{8,0},{12,28},{16,24},{20,4},{24,16},{28,12},{1,9},{5... | collective-permute-start | bytes 1572872 | tf_op jit(solution)/shard_map/ppermute | solution.py:52
  10.8 1.5 collective-permute-start.6
  12.4 1.3 constant_dynamic-slice_fusion
  13.7 0.9 collective-permute-start.7
  14.6 8.2 %collective-permute-done.4.refs_5_ = bf16[512,512]{1,0:T(8,128)(2,1)S(1)} collective-permute-done((bf16[512,512]{1,0:T(8,128)(2,1)S(1)}, bf16[512,512]{1,0:T(8,128)(2,1)S(1)}, u32[]{:S(2)}, u32[]{:S(2)}) %collective-permute-start.4) | collective-permute-done | bytes 524320 | tf_op jit(solution)/shard_map/ppermute | solution.py:52
  22.8 3.0 %collective-permute-start.2 = (bf16[512,512]{1,0:T(8,128)(2,1)S(1)}, bf16[512,512]{1,0:T(8,128)(2,1)S(1)}, u32[]{:S(2)}, u32[]{:S(2)}) collective-permute-start(bf16[512,512]{1,0:T(8,128)(2,1)S(1)} %collective-permute-done.1.refs_4_), channel_id=1, source_target_pairs={{0,16},{4,12},{8,24},{12,4},{16,0},{20,28},{24,8},{28,20},{1,17},{... | collective-permute-start | bytes 1572872 | tf_op jit(solution)/shard_map/ppermute | solution.py:52
  25.9 3.3 %project.3.refs_4_ = f32[2,512,512]{2,1,0:T(8,128)S(1)} custom-call(bf16[512,4096]{1,0:T(8,128)(2,1)S(1)} %copy-done, bf16[512,4096]{1,0:T(8,128)(2,1)} %collective-permute-done.refs_1_, bf16[512,512]{1,0:T(8,128)(2,1)S(1)} %get-tuple-element.68.refs_2_, bf16[512,512]{1,0:T(8,128)(2,1)S(1)} %collective-permute-done.3.refs_3_, ...), custom_call_target="tpu_custom_call" | custom-call | tf_op jit(solution)/shard_map/project/pallas_call | solution.py:239
  29.3 2.2 %project.4.refs_4_ = f32[2,512,512]{2,1,0:T(8,128)S(1)} custom-call(bf16[512,4096]{1,0:T(8,128)(2,1)S(1)} %copy-done, bf16[512,4096]{1,0:T(8,128)(2,1)} %collective-permute-done.refs_1_, bf16[512,512]{1,0:T(8,128)(2,1)S(1)} %collective-permute-done.6.refs_2_, bf16[512,512]{1,0:T(8,128)(2,1)S(1)} %collective-permute-done.7.refs_3_, ...), custom_call_target="tpu_custom_call" | custom-call | tf_op jit(solution)/shard_map/project/pallas_call | solution.py:239
  31.5 2.9 %collective-permute-done.2.refs_2_ = bf16[512,512]{1,0:T(8,128)(2,1)S(1)} collective-permute-done((bf16[512,512]{1,0:T(8,128)(2,1)S(1)}, bf16[512,512]{1,0:T(8,128)(2,1)S(1)}, u32[]{:S(2)}, u32[]{:S(2)}) %collective-permute-start.2) | collective-permute-done | bytes 524320 | tf_op jit(solution)/shard_map/ppermute | solution.py:52
  34.3 5.6 %collective-permute-done.5.refs_3_ = bf16[512,512]{1,0:T(8,128)(2,1)S(1)} collective-permute-done((bf16[512,512]{1,0:T(8,128)(2,1)S(1)}, bf16[512,512]{1,0:T(8,128)(2,1)S(1)}, u32[]{:S(2)}, u32[]{:S(2)}) %collective-permute-start.5) | collective-permute-done | bytes 524320 | tf_op jit(solution)/shard_map/ppermute | solution.py:52
  40.0 2.3 %project.5 = bf16[2,512,512]{2,1,0:T(8,128)(2,1)S(1)} custom-call(bf16[512,4096]{1,0:T(8,128)(2,1)S(1)} %copy-done, bf16[512,4096]{1,0:T(8,128)(2,1)} %collective-permute-done.refs_1_, bf16[512,512]{1,0:T(8,128)(2,1)S(1)} %collective-permute-done.2.refs_2_, bf16[512,512]{1,0:T(8,128)(2,1)S(1)} %collective-permute-done.5.refs_3_, ...), custom_call_target="tpu_custom_call" | custom-call | tf_op jit(solution)/shard_map/project/pallas_call | solution.py:239
  43.1 1.8 %collective-permute-start.9 = (bf16[4,64,512]{2,1,0:T(8,128)(2,1)S(1)}, bf16[4,64,512]{2,1,0:T(8,128)(2,1)S(1)}, u32[]{:S(2)}, u32[]{:S(2)}) collective-permute-start(bf16[4,64,512]{2,1,0:T(8,128)(2,1)S(1)} %get-tuple-element.36), channel_id=1, source_target_pairs={{0,16},{4,12},{8,24},{12,4},{16,0},{20,28},{24,8},{28,20},{1,17},{... | collective-permute-start | bytes 786440 | tf_op jit(solution)/shard_map/ppermute | solution.py:52
  45.2 4.3 %collective-permute-done.9.refs_1_ = bf16[4,64,512]{2,1,0:T(8,128)(2,1)S(1)} collective-permute-done((bf16[4,64,512]{2,1,0:T(8,128)(2,1)S(1)}, bf16[4,64,512]{2,1,0:T(8,128)(2,1)S(1)}, u32[]{:S(2)}, u32[]{:S(2)}) %collective-permute-start.9) | collective-permute-done | bytes 262176 | tf_op jit(solution)/shard_map/ppermute | solution.py:52
  49.6 1.8 %collective-permute-start.13 = (bf16[4,64,512]{2,1,0:T(8,128)(2,1)S(1)}, bf16[4,64,512]{2,1,0:T(8,128)(2,1)S(1)}, u32[]{:S(2)}, u32[]{:S(2)}) collective-permute-start(bf16[4,64,512]{2,1,0:T(8,128)(2,1)S(1)} %add_terms.9.refs_2_), channel_id=1, source_target_pairs={{0,8},{4,20},{8,0},{12,28},{16,24},{20,4},{24,16},{28,12},{1,9},{5... | collective-permute-start | bytes 786440 | tf_op jit(solution)/shard_map/ppermute | solution.py:52
  52.2 1.6 collective-permute-start.11
  53.8 4.3 %collective-permute-done.13.refs_2_ = bf16[4,64,512]{2,1,0:T(8,128)(2,1)S(1)} collective-permute-done((bf16[4,64,512]{2,1,0:T(8,128)(2,1)S(1)}, bf16[4,64,512]{2,1,0:T(8,128)(2,1)S(1)}, u32[]{:S(2)}, u32[]{:S(2)}) %collective-permute-start.13) | collective-permute-done | bytes 262176 | tf_op jit(solution)/shard_map/ppermute | solution.py:52
  58.2 2.1 %collective-permute-start.15 = (bf16[64,512]{1,0:T(8,128)(2,1)S(1)}, bf16[64,512]{1,0:T(8,128)(2,1)S(1)}, u32[]{:S(2)}, u32[]{:S(2)}) collective-permute-start(bf16[64,512]{1,0:T(8,128)(2,1)S(1)} %get-tuple-element.83), channel_id=1, source_target_pairs={{0,1},{1,2},{2,3},{3,0},{4,5},{5,6},{6,7},{7,4},{8,9},{9,10},{10,1... | collective-permute-start | bytes 196616 | tf_op jit(solution)/shard_map/ppermute | solution.py:107
  60.3 2.6 %collective-permute-start.16 = (bf16[64,512]{1,0:T(8,128)(2,1)S(1)}, bf16[64,512]{1,0:T(8,128)(2,1)S(1)}, u32[]{:S(2)}, u32[]{:S(2)}) collective-permute-start(bf16[64,512]{1,0:T(8,128)(2,1)S(1)} %get-tuple-element.82), channel_id=1, source_target_pairs={{0,2},{1,3},{2,0},{3,1},{4,6},{5,7},{6,4},{7,5},{8,10},{9,11},{10,... | collective-permute-start | bytes 196616 | tf_op jit(solution)/shard_map/ppermute | solution.py:107
  62.9 1.3 collective-permute-start.17
  64.2 2.0 %collective-permute-start.10 = (bf16[4,64,512]{2,1,0:T(8,128)(2,1)S(1)}, bf16[4,64,512]{2,1,0:T(8,128)(2,1)S(1)}, u32[]{:S(2)}, u32[]{:S(2)}) collective-permute-start(bf16[4,64,512]{2,1,0:T(8,128)(2,1)S(1)} %get-tuple-element.39), channel_id=1, source_target_pairs={{0,16},{4,12},{8,24},{12,4},{16,0},{20,28},{24,8},{28,20},{1,17},{... | collective-permute-start | bytes 786440 | tf_op jit(solution)/shard_map/ppermute | solution.py:52
  66.3 1.6 collective-permute-start.14
  67.9 0.9 collective-permute-start.24
  68.7 2.0 %collective-permute-start.25 = (bf16[4,64,512]{2,1,0:T(8,128)(2,1)S(1)}, bf16[4,64,512]{2,1,0:T(8,128)(2,1)S(1)}, u32[]{:S(2)}, u32[]{:S(2)}) collective-permute-start(bf16[4,64,512]{2,1,0:T(8,128)(2,1)S(1)} %stack_planes.6.refs_3_.refs_0_), channel_id=1, source_target_pairs={{0,16},{4,12},{8,24},{12,4},{16,0},{20,28},{24,8},{28,20},{1,17},{... | collective-permute-start | bytes 786440 | tf_op jit(solution)/shard_map/ppermute | solution.py:52
  70.7 2.5 %collective-permute-done.10.refs_1_ = bf16[4,64,512]{2,1,0:T(8,128)(2,1)S(1)} collective-permute-done((bf16[4,64,512]{2,1,0:T(8,128)(2,1)S(1)}, bf16[4,64,512]{2,1,0:T(8,128)(2,1)S(1)}, u32[]{:S(2)}, u32[]{:S(2)}) %collective-permute-start.10) | collective-permute-done | bytes 262176 | tf_op jit(solution)/shard_map/ppermute | solution.py:52
  73.3 2.3 %collective-permute-done.24.refs_1_ = bf16[4,64,512]{2,1,0:T(8,128)(2,1)S(1)} collective-permute-done((bf16[4,64,512]{2,1,0:T(8,128)(2,1)S(1)}, bf16[4,64,512]{2,1,0:T(8,128)(2,1)S(1)}, u32[]{:S(2)}, u32[]{:S(2)}) %collective-permute-start.24) | collective-permute-done | bytes 262176 | tf_op jit(solution)/shard_map/ppermute | solution.py:52
  77.1 3.4 %collective-permute-start.19 = (bf16[64,512]{1,0:T(8,128)(2,1)S(1)}, bf16[64,512]{1,0:T(8,128)(2,1)S(1)}, u32[]{:S(2)}, u32[]{:S(2)}) collective-permute-start(bf16[64,512]{1,0:T(8,128)(2,1)S(1)} %get-tuple-element.78), channel_id=1, source_target_pairs={{0,2},{1,3},{2,0},{3,1},{4,6},{5,7},{6,4},{7,5},{8,10},{9,11},{10,... | collective-permute-start | bytes 196616 | tf_op jit(solution)/shard_map/ppermute | solution.py:107
  80.4 2.0 %collective-permute-done.18.refs_1_ = bf16[64,512]{1,0:T(8,128)(2,1)S(1)} collective-permute-done((bf16[64,512]{1,0:T(8,128)(2,1)S(1)}, bf16[64,512]{1,0:T(8,128)(2,1)S(1)}, u32[]{:S(2)}, u32[]{:S(2)}) %collective-permute-start.18) | collective-permute-done | bytes 65568 | tf_op jit(solution)/shard_map/ppermute | solution.py:107
  82.4 1.4 collective-permute-done.19.refs_2_
  83.8 0.9 collective-permute-done.20.refs_3_
  84.9 2.1 %collective-permute-start.21 = (bf16[4,64,512]{2,1,0:T(8,128)(2,1)S(1)}, bf16[4,64,512]{2,1,0:T(8,128)(2,1)S(1)}, u32[]{:S(2)}, u32[]{:S(2)}) collective-permute-start(bf16[4,64,512]{2,1,0:T(8,128)(2,1)S(1)} %stack_planes.7.refs_4_.refs_0_), channel_id=1, source_target_pairs={{0,8},{4,20},{8,0},{12,28},{16,24},{20,4},{24,16},{28,12},{1,9},{5... | collective-permute-start | bytes 786440 | tf_op jit(solution)/shard_map/ppermute | solution.py:99
  87.0 2.0 %collective-permute-start.22 = (bf16[4,64,512]{2,1,0:T(8,128)(2,1)S(1)}, bf16[4,64,512]{2,1,0:T(8,128)(2,1)S(1)}, u32[]{:S(2)}, u32[]{:S(2)}) collective-permute-start(bf16[4,64,512]{2,1,0:T(8,128)(2,1)S(1)} %stack_planes.7.refs_4_.refs_0_), channel_id=1, source_target_pairs={{0,16},{4,12},{8,24},{12,4},{16,0},{20,28},{24,8},{28,20},{1,17},{... | collective-permute-start | bytes 786440 | tf_op jit(solution)/shard_map/ppermute | solution.py:99
  89.1 5.4 %expert_hidden.2.refs_4_.refs_1_ = bf16[256,1024]{1,0:T(8,128)(2,1)S(1)} custom-call(bf16[4,4,64,512]{3,2,1,0:T(8,128)(2,1)S(1)} %stack_planes.8.refs_0_.refs_4_, bf16[4,4,64,512]{3,2,1,0:T(8,128)(2,1)S(1)} %collective-permute-done.27.refs_1_, bf16[4096,1024]{1,0:T(8,128)(2,1)S(1)} %bitcast.44, bf16[4096,1024]{1,0:T(8,128)(2,1)S(1)} %bitcast.48, ...), custom_call_target="tpu_custom_call" | custom-call | tf_op jit(solution)/shard_map/expert_hidden/pallas_call | solution.py:354
  94.6 6.4 %collective-permute-done.23.refs_3_ = bf16[4,64,512]{2,1,0:T(8,128)(2,1)S(1)} collective-permute-done((bf16[4,64,512]{2,1,0:T(8,128)(2,1)S(1)}, bf16[4,64,512]{2,1,0:T(8,128)(2,1)S(1)}, u32[]{:S(2)}, u32[]{:S(2)}) %collective-permute-start.23) | collective-permute-done | bytes 262176 | tf_op jit(solution)/shard_map/ppermute | solution.py:99
  101.1 1.8 %expert_down.4 = (bf16[4,64,512]{2,1,0:T(8,128)(2,1)S(1)}, bf16[4,64,512]{2,1,0:T(8,128)(2,1)S(1)}, bf16[4,64,512]{2,1,0:T(8,128)(2,1)S(1)}, bf16[4,64,512]{2,1,0:T(8,128)(2,1)S(1)}) custom-call(s32[4]{0:T(128)S(1)} %copy-done.3, bf16[256,1024]{1,0:T(8,128)(2,1)S(1)} %expert_hidden.2.refs_4_.refs_1_, bf16[1024,4096]{1,0:T(8,128)(2,1)S(1)} %bitcast.38, ...), custom_call_target="tpu_custom_call" | custom-call | tf_op jit(solution)/shard_map/expert_down/pallas_call | solution.py:389
  104.1 1.8 %expert_down.5 = (bf16[4,64,512]{2,1,0:T(8,128)(2,1)S(1)}, bf16[4,64,512]{2,1,0:T(8,128)(2,1)S(1)}, bf16[4,64,512]{2,1,0:T(8,128)(2,1)S(1)}, bf16[4,64,512]{2,1,0:T(8,128)(2,1)S(1)}) custom-call(s32[4]{0:T(128)S(1)} %copy-done.3, bf16[256,1024]{1,0:T(8,128)(2,1)S(1)} %expert_hidden.2.refs_4_.refs_1_, bf16[1024,4096]{1,0:T(8,128)(2,1)S(1)} %bitcast.39, ...), custom_call_target="tpu_custom_call" | custom-call | tf_op jit(solution)/shard_map/expert_down/pallas_call | solution.py:389
  106.2 1.9 %collective-permute-start.34 = (bf16[4,64,512]{2,1,0:T(8,128)(2,1)S(1)}, bf16[4,64,512]{2,1,0:T(8,128)(2,1)S(1)}, u32[]{:S(2)}, u32[]{:S(2)}) collective-permute-start(bf16[4,64,512]{2,1,0:T(8,128)(2,1)S(1)} %get-tuple-element.50.refs_4_), channel_id=1, source_target_pairs={{0,16},{4,12},{8,24},{12,4},{16,0},{20,28},{24,8},{28,20},{1,17},{... | collective-permute-start | bytes 786440 | tf_op jit(solution)/shard_map/ppermute | solution.py:52
  108.2 5.5 %expert_hidden.3.refs_3_.refs_1_ = bf16[256,1024]{1,0:T(8,128)(2,1)S(1)} custom-call(bf16[4,4,64,512]{3,2,1,0:T(8,128)(2,1)S(1)} %stack_planes.9.refs_4_.refs_0_, bf16[4,4,64,512]{3,2,1,0:T(8,128)(2,1)S(1)} %collective-permute-done.28.refs_1_, bf16[4096,1024]{1,0:T(8,128)(2,1)S(1)} %bitcast.45, bf16[4096,1024]{1,0:T(8,128)(2,1)S(1)} %bitcast.49, ...), custom_call_target="tpu_custom_call" | custom-call | tf_op jit(solution)/shard_map/expert_hidden/pallas_call | solution.py:354
  113.7 1.7 %collective-permute-done.34.refs_4_.refs_2_ = bf16[4,64,512]{2,1,0:T(8,128)(2,1)S(1)} collective-permute-done((bf16[4,64,512]{2,1,0:T(8,128)(2,1)S(1)}, bf16[4,64,512]{2,1,0:T(8,128)(2,1)S(1)}, u32[]{:S(2)}, u32[]{:S(2)}) %collective-permute-start.34) | collective-permute-done | bytes 262176 | tf_op jit(solution)/shard_map/ppermute | solution.py:52
  115.4 1.8 %expert_down.6 = (bf16[4,64,512]{2,1,0:T(8,128)(2,1)S(1)}, bf16[4,64,512]{2,1,0:T(8,128)(2,1)S(1)}, bf16[4,64,512]{2,1,0:T(8,128)(2,1)S(1)}, bf16[4,64,512]{2,1,0:T(8,128)(2,1)S(1)}) custom-call(s32[4]{0:T(128)S(1)} %copy-done.3, bf16[256,1024]{1,0:T(8,128)(2,1)S(1)} %expert_hidden.3.refs_3_.refs_1_, bf16[1024,4096]{1,0:T(8,128)(2,1)S(1)} %bitcast.40, ...), custom_call_target="tpu_custom_call" | custom-call | tf_op jit(solution)/shard_map/expert_down/pallas_call | solution.py:389
  118.4 1.7 %collective-permute-start.42 = (bf16[4,64,512]{2,1,0:T(8,128)(2,1)S(1)}, bf16[4,64,512]{2,1,0:T(8,128)(2,1)S(1)}, u32[]{:S(2)}, u32[]{:S(2)}) collective-permute-start(bf16[4,64,512]{2,1,0:T(8,128)(2,1)S(1)} %add_terms.14.refs_4_), channel_id=1, source_target_pairs={{0,8},{4,20},{8,0},{12,28},{16,24},{20,4},{24,16},{28,12},{1,9},{5... | collective-permute-start | bytes 786440 | tf_op jit(solution)/shard_map/ppermute | solution.py:52
  120.1 1.8 %expert_down.7 = (bf16[4,64,512]{2,1,0:T(8,128)(2,1)S(1)}, bf16[4,64,512]{2,1,0:T(8,128)(2,1)S(1)}, bf16[4,64,512]{2,1,0:T(8,128)(2,1)S(1)}, bf16[4,64,512]{2,1,0:T(8,128)(2,1)S(1)}) custom-call(s32[4]{0:T(128)S(1)} %copy-done.3, bf16[256,1024]{1,0:T(8,128)(2,1)S(1)} %expert_hidden.3.refs_3_.refs_1_, bf16[1024,4096]{1,0:T(8,128)(2,1)S(1)} %bitcast.41, ...), custom_call_target="tpu_custom_call" | custom-call | tf_op jit(solution)/shard_map/expert_down/pallas_call | solution.py:389
  122.7 3.1 %collective-permute-start.41 = (bf16[4,64,512]{2,1,0:T(8,128)(2,1)S(1)}, bf16[4,64,512]{2,1,0:T(8,128)(2,1)S(1)}, u32[]{:S(2)}, u32[]{:S(2)}) collective-permute-start(bf16[4,64,512]{2,1,0:T(8,128)(2,1)S(1)} %get-tuple-element.64), channel_id=1, source_target_pairs={{0,24},{4,28},{8,16},{12,20},{16,8},{20,12},{24,0},{28,4},{1,25},{... | collective-permute-start | bytes 786440 | tf_op jit(solution)/shard_map/ppermute | solution.py:99
  126.2 2.9 %collective-permute-start.47 = (bf16[64,512]{1,0:T(8,128)(2,1)S(1)}, bf16[64,512]{1,0:T(8,128)(2,1)S(1)}, u32[]{:S(2)}, u32[]{:S(2)}) collective-permute-start(bf16[64,512]{1,0:T(8,128)(2,1)S(1)} %get-tuple-element.70), channel_id=1, source_target_pairs={{0,2},{1,3},{2,0},{3,1},{4,6},{5,7},{6,4},{7,5},{8,10},{9,11},{10,... | collective-permute-start | bytes 196616 | tf_op jit(solution)/shard_map/ppermute | solution.py:107
  129.1 2.4 %collective-permute-done.39.refs_1_ = bf16[4,64,512]{2,1,0:T(8,128)(2,1)S(1)} collective-permute-done((bf16[4,64,512]{2,1,0:T(8,128)(2,1)S(1)}, bf16[4,64,512]{2,1,0:T(8,128)(2,1)S(1)}, u32[]{:S(2)}, u32[]{:S(2)}) %collective-permute-start.39) | collective-permute-done | bytes 262176 | tf_op jit(solution)/shard_map/ppermute | solution.py:99
  131.5 2.5 %collective-permute-start.48 = (bf16[64,512]{1,0:T(8,128)(2,1)S(1)}, bf16[64,512]{1,0:T(8,128)(2,1)S(1)}, u32[]{:S(2)}, u32[]{:S(2)}) collective-permute-start(bf16[64,512]{1,0:T(8,128)(2,1)S(1)} %get-tuple-element.69), channel_id=1, source_target_pairs={{0,3},{1,0},{2,1},{3,2},{4,7},{5,4},{6,5},{7,6},{8,11},{9,8},{10,9... | collective-permute-start | bytes 196616 | tf_op jit(solution)/shard_map/ppermute | solution.py:107
  134.0 1.8 %collective-permute-done.41.refs_3_ = bf16[4,64,512]{2,1,0:T(8,128)(2,1)S(1)} collective-permute-done((bf16[4,64,512]{2,1,0:T(8,128)(2,1)S(1)}, bf16[4,64,512]{2,1,0:T(8,128)(2,1)S(1)}, u32[]{:S(2)}, u32[]{:S(2)}) %collective-permute-start.41) | collective-permute-done | bytes 262176 | tf_op jit(solution)/shard_map/ppermute | solution.py:99
  136.3 2.7 %collective-permute-start.44 = (bf16[64,512]{1,0:T(8,128)(2,1)S(1)}, bf16[64,512]{1,0:T(8,128)(2,1)S(1)}, u32[]{:S(2)}, u32[]{:S(2)}) collective-permute-start(bf16[64,512]{1,0:T(8,128)(2,1)S(1)} %get-tuple-element.74), channel_id=1, source_target_pairs={{0,2},{1,3},{2,0},{3,1},{4,6},{5,7},{6,4},{7,5},{8,10},{9,11},{10,... | collective-permute-start | bytes 196616 | tf_op jit(solution)/shard_map/ppermute | solution.py:107
  139.8 1.7 %collective-permute-start.52 = (bf16[4,64,512]{2,1,0:T(8,128)(2,1)S(1)}, bf16[4,64,512]{2,1,0:T(8,128)(2,1)S(1)}, u32[]{:S(2)}, u32[]{:S(2)}) collective-permute-start(bf16[4,64,512]{2,1,0:T(8,128)(2,1)S(1)} %stack_planes.10.refs_4_.refs_1_), channel_id=1, source_target_pairs={{0,8},{4,20},{8,0},{12,28},{16,24},{20,4},{24,16},{28,12},{1,9},{5... | collective-permute-start | bytes 786440 | tf_op jit(solution)/shard_map/ppermute | solution.py:52
  141.6 1.3 collective-permute-done.43.refs_1_
  142.8 1.3 collective-permute-done.44.refs_2_
  144.2 2.2 %collective-permute-start.49 = (bf16[4,64,512]{2,1,0:T(8,128)(2,1)S(1)}, bf16[4,64,512]{2,1,0:T(8,128)(2,1)S(1)}, u32[]{:S(2)}, u32[]{:S(2)}) collective-permute-start(bf16[4,64,512]{2,1,0:T(8,128)(2,1)S(1)} %stack_planes.11.refs_1_), channel_id=1, source_target_pairs={{0,8},{4,20},{8,0},{12,28},{16,24},{20,4},{24,16},{28,12},{1,9},{5... | collective-permute-start | bytes 786440 | tf_op jit(solution)/shard_map/ppermute | solution.py:52
  146.4 1.7 %collective-permute-start.53 = (bf16[4,64,512]{2,1,0:T(8,128)(2,1)S(1)}, bf16[4,64,512]{2,1,0:T(8,128)(2,1)S(1)}, u32[]{:S(2)}, u32[]{:S(2)}) collective-permute-start(bf16[4,64,512]{2,1,0:T(8,128)(2,1)S(1)} %stack_planes.10.refs_4_.refs_1_), channel_id=1, source_target_pairs={{0,16},{4,12},{8,24},{12,4},{16,0},{20,28},{24,8},{28,20},{1,17},{... | collective-permute-start | bytes 786440 | tf_op jit(solution)/shard_map/ppermute | solution.py:52
  148.7 1.4 collective-permute-start.50
  150.1 3.4 %collective-permute-done.49.refs_2_ = bf16[4,64,512]{2,1,0:T(8,128)(2,1)S(1)} collective-permute-done((bf16[4,64,512]{2,1,0:T(8,128)(2,1)S(1)}, bf16[4,64,512]{2,1,0:T(8,128)(2,1)S(1)}, u32[]{:S(2)}, u32[]{:S(2)}) %collective-permute-start.49) | collective-permute-done | bytes 262176 | tf_op jit(solution)/shard_map/ppermute | solution.py:52
  153.5 1.8 %collective-permute-start.51 = (bf16[4,64,512]{2,1,0:T(8,128)(2,1)S(1)}, bf16[4,64,512]{2,1,0:T(8,128)(2,1)S(1)}, u32[]{:S(2)}, u32[]{:S(2)}) collective-permute-start(bf16[4,64,512]{2,1,0:T(8,128)(2,1)S(1)} %collective-permute-done.49.refs_2_), channel_id=1, source_target_pairs={{0,16},{4,12},{8,24},{12,4},{16,0},{20,28},{24,8},{28,20},{1,17},{... | collective-permute-start | bytes 786440 | tf_op jit(solution)/shard_map/ppermute | solution.py:52
  155.5 1.1 add_expert_rows.3.refs_5_
  156.6 1.7 %collective-permute-done.50.refs_3_ = bf16[4,64,512]{2,1,0:T(8,128)(2,1)S(1)} collective-permute-done((bf16[4,64,512]{2,1,0:T(8,128)(2,1)S(1)}, bf16[4,64,512]{2,1,0:T(8,128)(2,1)S(1)}, u32[]{:S(2)}, u32[]{:S(2)}) %collective-permute-start.50) | collective-permute-done | bytes 262176 | tf_op jit(solution)/shard_map/ppermute | solution.py:52
  158.3 2.8 %collective-permute-done.51.refs_4_ = bf16[4,64,512]{2,1,0:T(8,128)(2,1)S(1)} collective-permute-done((bf16[4,64,512]{2,1,0:T(8,128)(2,1)S(1)}, bf16[4,64,512]{2,1,0:T(8,128)(2,1)S(1)}, u32[]{:S(2)}, u32[]{:S(2)}) %collective-permute-start.51) | collective-permute-done | bytes 262176 | tf_op jit(solution)/shard_map/ppermute | solution.py:52
  161.2 1.1 add_expert_rows.5
  162.3 1.0 add_expert_rows.4.refs_0_
  164.2 1.1 join_halves.1
  (107 shorter events, 11.6 us)
Async XLA Ops:
  0.0 25.9 %collective-permute-start = (bf16[512,4096]{1,0:T(8,128)(2,1)}, bf16[512,4096]{1,0:T(8,128)(2,1)}, u32[]{:S(2)}, u32[]{:S(2)}) collective-permute-start(bf16[512,4096]{1,0:T(8,128)(2,1)} %refs_0_.14), channel_id=1, source_target_pairs={{0,4},{4,0},{8,12},{12,8},{16,20},{20,16},{24,28},{28,24},{1,5},{5... | collective-permute-start | bytes 12582920 | tf_op jit(solution)/shard_map/ppermute | solution.py:462
  0.5 25.4 %copy-start = (bf16[512,4096]{1,0:T(8,128)(2,1)S(1)}, bf16[512,4096]{1,0:T(8,128)(2,1)}, u32[]{:S(2)}) copy-start(bf16[512,4096]{1,0:T(8,128)(2,1)} %refs_0_.14) | copy-start | bytes 12582916
  1.9 6.1 %collective-permute-start.3 = (bf16[512,512]{1,0:T(8,128)(2,1)S(1)}, bf16[512,512]{1,0:T(8,128)(2,1)S(1)}, u32[]{:S(2)}, u32[]{:S(2)}) collective-permute-start(bf16[512,512]{1,0:T(8,128)(2,1)S(1)} %get-tuple-element.67), channel_id=1, source_target_pairs={{0,4},{4,0},{8,12},{12,8},{16,20},{20,16},{24,28},{28,24},{1,5},{5... | collective-permute-start | bytes 1572872 | tf_op jit(solution)/shard_map/ppermute | solution.py:462
  2.0 11.7 %collective-permute-start.1 = (bf16[512,512]{1,0:T(8,128)(2,1)S(1)}, bf16[512,512]{1,0:T(8,128)(2,1)S(1)}, u32[]{:S(2)}, u32[]{:S(2)}) collective-permute-start(bf16[512,512]{1,0:T(8,128)(2,1)S(1)} %get-tuple-element.68.refs_2_), channel_id=1, source_target_pairs={{0,8},{4,20},{8,0},{12,28},{16,24},{20,4},{24,16},{28,12},{1,9},{5... | collective-permute-start | bytes 1572872 | tf_op jit(solution)/shard_map/ppermute | solution.py:52
  8.0 14.9 %collective-permute-start.4 = (bf16[512,512]{1,0:T(8,128)(2,1)S(1)}, bf16[512,512]{1,0:T(8,128)(2,1)S(1)}, u32[]{:S(2)}, u32[]{:S(2)}) collective-permute-start(bf16[512,512]{1,0:T(8,128)(2,1)S(1)} %collective-permute-done.3.refs_3_), channel_id=1, source_target_pairs={{0,8},{4,20},{8,0},{12,28},{16,24},{20,4},{24,16},{28,12},{1,9},{5... | collective-permute-start | bytes 1572872 | tf_op jit(solution)/shard_map/ppermute | solution.py:52
  10.8 18.4 %collective-permute-start.6 = (bf16[512,512]{1,0:T(8,128)(2,1)S(1)}, bf16[512,512]{1,0:T(8,128)(2,1)S(1)}, u32[]{:S(2)}, u32[]{:S(2)}) collective-permute-start(bf16[512,512]{1,0:T(8,128)(2,1)S(1)} %get-tuple-element.68.refs_2_), channel_id=1, source_target_pairs={{0,16},{4,12},{8,24},{12,4},{16,0},{20,28},{24,8},{28,20},{1,17},{... | collective-permute-start | bytes 1572872 | tf_op jit(solution)/shard_map/ppermute | solution.py:52
  13.7 17.8 %collective-permute-start.8 = (bf16[512,512]{1,0:T(8,128)(2,1)S(1)}, bf16[512,512]{1,0:T(8,128)(2,1)S(1)}, u32[]{:S(2)}, u32[]{:S(2)}) collective-permute-start(bf16[512,512]{1,0:T(8,128)(2,1)S(1)} %get-tuple-element.65), channel_id=1, source_target_pairs={{0,4},{4,0},{8,12},{12,8},{16,20},{20,16},{24,28},{28,24},{1,5},{5... | collective-permute-start | bytes 1572872 | tf_op jit(solution)/shard_map/ppermute | solution.py:462
  13.7 15.5 %collective-permute-start.7 = (bf16[512,512]{1,0:T(8,128)(2,1)S(1)}, bf16[512,512]{1,0:T(8,128)(2,1)S(1)}, u32[]{:S(2)}, u32[]{:S(2)}) collective-permute-start(bf16[512,512]{1,0:T(8,128)(2,1)S(1)} %collective-permute-done.3.refs_3_), channel_id=1, source_target_pairs={{0,16},{4,12},{8,24},{12,4},{16,0},{20,28},{24,8},{28,20},{1,17},{... | collective-permute-start | bytes 1572872 | tf_op jit(solution)/shard_map/ppermute | solution.py:52
  22.8 11.5 %collective-permute-start.2 = (bf16[512,512]{1,0:T(8,128)(2,1)S(1)}, bf16[512,512]{1,0:T(8,128)(2,1)S(1)}, u32[]{:S(2)}, u32[]{:S(2)}) collective-permute-start(bf16[512,512]{1,0:T(8,128)(2,1)S(1)} %collective-permute-done.1.refs_4_), channel_id=1, source_target_pairs={{0,16},{4,12},{8,24},{12,4},{16,0},{20,28},{24,8},{28,20},{1,17},{... | collective-permute-start | bytes 1572872 | tf_op jit(solution)/shard_map/ppermute | solution.py:52
  25.9 14.1 %collective-permute-start.5 = (bf16[512,512]{1,0:T(8,128)(2,1)S(1)}, bf16[512,512]{1,0:T(8,128)(2,1)S(1)}, u32[]{:S(2)}, u32[]{:S(2)}) collective-permute-start(bf16[512,512]{1,0:T(8,128)(2,1)S(1)} %collective-permute-done.4.refs_5_), channel_id=1, source_target_pairs={{0,16},{4,12},{8,24},{12,4},{16,0},{20,28},{24,8},{28,20},{1,17},{... | collective-permute-start | bytes 1572872 | tf_op jit(solution)/shard_map/ppermute | solution.py:52
  29.3 13.0 %copy-start.1 = (s32[4,4]{1,0:T(4,128)S(1)}, s32[4,4]{1,0:T(4,128)}, u32[]{:S(2)}) copy-start(s32[4,4]{1,0:T(4,128)} %refs_0_.23) | copy-start | bytes 196
  40.0 49.0 %slice-start.2 = ((s8[8388608]{0:T(1024)(128)(4,1)}), s8[4194304]{0:T(1024)(128)(4,1)S(1)}, s32[]{:S(2)}) async-start(s8[8388608]{0:T(1024)(128)(4,1)} %bitcast.42), calls=%async_computation.2 | async-start | bytes 8388608
  40.0 49.1 %slice-start.4 = ((s8[8388608]{0:T(1024)(128)(4,1)}), s8[4194304]{0:T(1024)(128)(4,1)S(1)}, s32[]{:S(2)}) async-start(s8[8388608]{0:T(1024)(128)(4,1)} %bitcast.46), calls=%async_computation.4 | async-start | bytes 8388608
  40.0 49.1 %slice-start.3 = ((s8[8388608]{0:T(1024)(128)(4,1)}), s8[4194304]{0:T(1024)(128)(4,1)S(1)}, s32[]{:S(2)}) async-start(s8[8388608]{0:T(1024)(128)(4,1)} %bitcast.42), calls=%async_computation.3 | async-start | bytes 8388608
  40.0 49.1 %slice-start.5 = ((s8[8388608]{0:T(1024)(128)(4,1)}), s8[4194304]{0:T(1024)(128)(4,1)S(1)}, s32[]{:S(2)}) async-start(s8[8388608]{0:T(1024)(128)(4,1)} %bitcast.46), calls=%async_computation.5 | async-start | bytes 8388608
  43.1 6.4 %collective-permute-start.9 = (bf16[4,64,512]{2,1,0:T(8,128)(2,1)S(1)}, bf16[4,64,512]{2,1,0:T(8,128)(2,1)S(1)}, u32[]{:S(2)}, u32[]{:S(2)}) collective-permute-start(bf16[4,64,512]{2,1,0:T(8,128)(2,1)S(1)} %get-tuple-element.36), channel_id=1, source_target_pairs={{0,16},{4,12},{8,24},{12,4},{16,0},{20,28},{24,8},{28,20},{1,17},{... | collective-permute-start | bytes 786440 | tf_op jit(solution)/shard_map/ppermute | solution.py:52
  44.9 8.9 %collective-permute-start.12 = (bf16[4,64,512]{2,1,0:T(8,128)(2,1)S(1)}, bf16[4,64,512]{2,1,0:T(8,128)(2,1)S(1)}, u32[]{:S(2)}, u32[]{:S(2)}) collective-permute-start(bf16[4,64,512]{2,1,0:T(8,128)(2,1)S(1)} %get-tuple-element.42), channel_id=1, source_target_pairs={{0,16},{4,12},{8,24},{12,4},{16,0},{20,28},{24,8},{28,20},{1,17},{... | collective-permute-start | bytes 786440 | tf_op jit(solution)/shard_map/ppermute | solution.py:52
  49.6 8.4 %collective-permute-start.13 = (bf16[4,64,512]{2,1,0:T(8,128)(2,1)S(1)}, bf16[4,64,512]{2,1,0:T(8,128)(2,1)S(1)}, u32[]{:S(2)}, u32[]{:S(2)}) collective-permute-start(bf16[4,64,512]{2,1,0:T(8,128)(2,1)S(1)} %add_terms.9.refs_2_), channel_id=1, source_target_pairs={{0,8},{4,20},{8,0},{12,28},{16,24},{20,4},{24,16},{28,12},{1,9},{5... | collective-permute-start | bytes 786440 | tf_op jit(solution)/shard_map/ppermute | solution.py:52
  52.2 14.0 %collective-permute-start.11 = (bf16[4,64,512]{2,1,0:T(8,128)(2,1)S(1)}, bf16[4,64,512]{2,1,0:T(8,128)(2,1)S(1)}, u32[]{:S(2)}, u32[]{:S(2)}) collective-permute-start(bf16[4,64,512]{2,1,0:T(8,128)(2,1)S(1)} %get-tuple-element.41), channel_id=1, source_target_pairs={{0,16},{4,12},{8,24},{12,4},{16,0},{20,28},{24,8},{28,20},{1,17},{... | collective-permute-start | bytes 786440 | tf_op jit(solution)/shard_map/ppermute | solution.py:52
  58.2 9.6 %collective-permute-start.15 = (bf16[64,512]{1,0:T(8,128)(2,1)S(1)}, bf16[64,512]{1,0:T(8,128)(2,1)S(1)}, u32[]{:S(2)}, u32[]{:S(2)}) collective-permute-start(bf16[64,512]{1,0:T(8,128)(2,1)S(1)} %get-tuple-element.83), channel_id=1, source_target_pairs={{0,1},{1,2},{2,3},{3,0},{4,5},{5,6},{6,7},{7,4},{8,9},{9,10},{10,1... | collective-permute-start | bytes 196616 | tf_op jit(solution)/shard_map/ppermute | solution.py:107
  60.3 7.5 %collective-permute-start.16 = (bf16[64,512]{1,0:T(8,128)(2,1)S(1)}, bf16[64,512]{1,0:T(8,128)(2,1)S(1)}, u32[]{:S(2)}, u32[]{:S(2)}) collective-permute-start(bf16[64,512]{1,0:T(8,128)(2,1)S(1)} %get-tuple-element.82), channel_id=1, source_target_pairs={{0,2},{1,3},{2,0},{3,1},{4,6},{5,7},{6,4},{7,5},{8,10},{9,11},{10,... | collective-permute-start | bytes 196616 | tf_op jit(solution)/shard_map/ppermute | solution.py:107
  62.9 4.9 %collective-permute-start.17 = (bf16[64,512]{1,0:T(8,128)(2,1)S(1)}, bf16[64,512]{1,0:T(8,128)(2,1)S(1)}, u32[]{:S(2)}, u32[]{:S(2)}) collective-permute-start(bf16[64,512]{1,0:T(8,128)(2,1)S(1)} %get-tuple-element.81), channel_id=1, source_target_pairs={{0,3},{1,0},{2,1},{3,2},{4,7},{5,4},{6,5},{7,6},{8,11},{9,8},{10,9... | collective-permute-start | bytes 196616 | tf_op jit(solution)/shard_map/ppermute | solution.py:107
  64.2 8.9 %collective-permute-start.10 = (bf16[4,64,512]{2,1,0:T(8,128)(2,1)S(1)}, bf16[4,64,512]{2,1,0:T(8,128)(2,1)S(1)}, u32[]{:S(2)}, u32[]{:S(2)}) collective-permute-start(bf16[4,64,512]{2,1,0:T(8,128)(2,1)S(1)} %get-tuple-element.39), channel_id=1, source_target_pairs={{0,16},{4,12},{8,24},{12,4},{16,0},{20,28},{24,8},{28,20},{1,17},{... | collective-permute-start | bytes 786440 | tf_op jit(solution)/shard_map/ppermute | solution.py:52
  66.3 6.9 %collective-permute-start.14 = (bf16[4,64,512]{2,1,0:T(8,128)(2,1)S(1)}, bf16[4,64,512]{2,1,0:T(8,128)(2,1)S(1)}, u32[]{:S(2)}, u32[]{:S(2)}) collective-permute-start(bf16[4,64,512]{2,1,0:T(8,128)(2,1)S(1)} %add_terms.11.refs_4_), channel_id=1, source_target_pairs={{0,8},{4,20},{8,0},{12,28},{16,24},{20,4},{24,16},{28,12},{1,9},{5... | collective-permute-start | bytes 786440 | tf_op jit(solution)/shard_map/ppermute | solution.py:52
  67.9 7.8 %collective-permute-start.24 = (bf16[4,64,512]{2,1,0:T(8,128)(2,1)S(1)}, bf16[4,64,512]{2,1,0:T(8,128)(2,1)S(1)}, u32[]{:S(2)}, u32[]{:S(2)}) collective-permute-start(bf16[4,64,512]{2,1,0:T(8,128)(2,1)S(1)} %stack_planes.6.refs_3_.refs_0_), channel_id=1, source_target_pairs={{0,8},{4,20},{8,0},{12,28},{16,24},{20,4},{24,16},{28,12},{1,9},{5... | collective-permute-start | bytes 786440 | tf_op jit(solution)/shard_map/ppermute | solution.py:52
  68.7 16.0 %collective-permute-start.25 = (bf16[4,64,512]{2,1,0:T(8,128)(2,1)S(1)}, bf16[4,64,512]{2,1,0:T(8,128)(2,1)S(1)}, u32[]{:S(2)}, u32[]{:S(2)}) collective-permute-start(bf16[4,64,512]{2,1,0:T(8,128)(2,1)S(1)} %stack_planes.6.refs_3_.refs_0_), channel_id=1, source_target_pairs={{0,16},{4,12},{8,24},{12,4},{16,0},{20,28},{24,8},{28,20},{1,17},{... | collective-permute-start | bytes 786440 | tf_op jit(solution)/shard_map/ppermute | solution.py:52
  75.6 9.1 %collective-permute-start.26 = (bf16[4,64,512]{2,1,0:T(8,128)(2,1)S(1)}, bf16[4,64,512]{2,1,0:T(8,128)(2,1)S(1)}, u32[]{:S(2)}, u32[]{:S(2)}) collective-permute-start(bf16[4,64,512]{2,1,0:T(8,128)(2,1)S(1)} %collective-permute-done.24.refs_1_), channel_id=1, source_target_pairs={{0,16},{4,12},{8,24},{12,4},{16,0},{20,28},{24,8},{28,20},{1,17},{... | collective-permute-start | bytes 786440 | tf_op jit(solution)/shard_map/ppermute | solution.py:52
  76.3 6.2 %collective-permute-start.18 = (bf16[64,512]{1,0:T(8,128)(2,1)S(1)}, bf16[64,512]{1,0:T(8,128)(2,1)S(1)}, u32[]{:S(2)}, u32[]{:S(2)}) collective-permute-start(bf16[64,512]{1,0:T(8,128)(2,1)S(1)} %get-tuple-element.79), channel_id=1, source_target_pairs={{0,1},{1,2},{2,3},{3,0},{4,5},{5,6},{6,7},{7,4},{8,9},{9,10},{10,1... | collective-permute-start | bytes 196616 | tf_op jit(solution)/shard_map/ppermute | solution.py:107
  77.1 6.7 %collective-permute-start.19 = (bf16[64,512]{1,0:T(8,128)(2,1)S(1)}, bf16[64,512]{1,0:T(8,128)(2,1)S(1)}, u32[]{:S(2)}, u32[]{:S(2)}) collective-permute-start(bf16[64,512]{1,0:T(8,128)(2,1)S(1)} %get-tuple-element.78), channel_id=1, source_target_pairs={{0,2},{1,3},{2,0},{3,1},{4,6},{5,7},{6,4},{7,5},{8,10},{9,11},{10,... | collective-permute-start | bytes 196616 | tf_op jit(solution)/shard_map/ppermute | solution.py:107
  80.4 4.3 %collective-permute-start.20 = (bf16[64,512]{1,0:T(8,128)(2,1)S(1)}, bf16[64,512]{1,0:T(8,128)(2,1)S(1)}, u32[]{:S(2)}, u32[]{:S(2)}) collective-permute-start(bf16[64,512]{1,0:T(8,128)(2,1)S(1)} %get-tuple-element.77), channel_id=1, source_target_pairs={{0,3},{1,0},{2,1},{3,2},{4,7},{5,4},{6,5},{7,6},{8,11},{9,8},{10,9... | collective-permute-start | bytes 196616 | tf_op jit(solution)/shard_map/ppermute | solution.py:107
  84.8 4.2 %collective-permute-start.27 = (bf16[4,4,64,512]{3,2,1,0:T(8,128)(2,1)S(1)}, bf16[4,4,64,512]{3,2,1,0:T(8,128)(2,1)S(1)}, u32[]{:S(2)}, u32[]{:S(2)}) collective-permute-start(bf16[4,4,64,512]{3,2,1,0:T(8,128)(2,1)S(1)} %stack_planes.8.refs_0_.refs_4_), channel_id=1, source_target_pairs={{0,4},{4,0},{8,12},{12,8},{16,20},{20,16},{24,28},{28,24},{1,5},{5... | collective-permute-start | bytes 3145736 | tf_op jit(solution)/shard_map/ppermute | solution.py:462
  84.9 9.6 %collective-permute-start.21 = (bf16[4,64,512]{2,1,0:T(8,128)(2,1)S(1)}, bf16[4,64,512]{2,1,0:T(8,128)(2,1)S(1)}, u32[]{:S(2)}, u32[]{:S(2)}) collective-permute-start(bf16[4,64,512]{2,1,0:T(8,128)(2,1)S(1)} %stack_planes.7.refs_4_.refs_0_), channel_id=1, source_target_pairs={{0,8},{4,20},{8,0},{12,28},{16,24},{20,4},{24,16},{28,12},{1,9},{5... | collective-permute-start | bytes 786440 | tf_op jit(solution)/shard_map/ppermute | solution.py:99
  87.0 7.6 %collective-permute-start.22 = (bf16[4,64,512]{2,1,0:T(8,128)(2,1)S(1)}, bf16[4,64,512]{2,1,0:T(8,128)(2,1)S(1)}, u32[]{:S(2)}, u32[]{:S(2)}) collective-permute-start(bf16[4,64,512]{2,1,0:T(8,128)(2,1)S(1)} %stack_planes.7.refs_4_.refs_0_), channel_id=1, source_target_pairs={{0,16},{4,12},{8,24},{12,4},{16,0},{20,28},{24,8},{28,20},{1,17},{... | collective-permute-start | bytes 786440 | tf_op jit(solution)/shard_map/ppermute | solution.py:99
  89.0 12.0 %collective-permute-start.23 = (bf16[4,64,512]{2,1,0:T(8,128)(2,1)S(1)}, bf16[4,64,512]{2,1,0:T(8,128)(2,1)S(1)}, u32[]{:S(2)}, u32[]{:S(2)}) collective-permute-start(bf16[4,64,512]{2,1,0:T(8,128)(2,1)S(1)} %stack_planes.7.refs_4_.refs_0_), channel_id=1, source_target_pairs={{0,24},{4,28},{8,16},{12,20},{16,8},{20,12},{24,0},{28,4},{1,25},{... | collective-permute-start | bytes 786440 | tf_op jit(solution)/shard_map/ppermute | solution.py:99
  89.0 12.1 %slice-start = ((s8[8388608]{0:T(1024)(128)(4,1)}), s8[4194304]{0:T(1024)(128)(4,1)S(1)}, s32[]{:S(2)}) async-start(s8[8388608]{0:T(1024)(128)(4,1)} %bitcast.36), calls=%async_computation | async-start | bytes 8388608
  89.1 12.1 %slice-start.1 = ((s8[8388608]{0:T(1024)(128)(4,1)}), s8[4194304]{0:T(1024)(128)(4,1)S(1)}, s32[]{:S(2)}) async-start(s8[8388608]{0:T(1024)(128)(4,1)} %bitcast.36), calls=%async_computation.1 | async-start | bytes 8388608
  101.0 7.2 %collective-permute-start.28 = (bf16[4,4,64,512]{3,2,1,0:T(8,128)(2,1)S(1)}, bf16[4,4,64,512]{3,2,1,0:T(8,128)(2,1)S(1)}, u32[]{:S(2)}, u32[]{:S(2)}) collective-permute-start(bf16[4,4,64,512]{3,2,1,0:T(8,128)(2,1)S(1)} %stack_planes.9.refs_4_.refs_0_), channel_id=1, source_target_pairs={{0,4},{4,0},{8,12},{12,8},{16,20},{20,16},{24,28},{28,24},{1,5},{5... | collective-permute-start | bytes 3145736 | tf_op jit(solution)/shard_map/ppermute | solution.py:462
  103.0 2.9 %collective-permute-start.29 = (bf16[4,64,512]{2,1,0:T(8,128)(2,1)S(1)}, bf16[4,64,512]{2,1,0:T(8,128)(2,1)S(1)}, u32[]{:S(2)}, u32[]{:S(2)}) collective-permute-start(bf16[4,64,512]{2,1,0:T(8,128)(2,1)S(1)} %get-tuple-element.45), channel_id=1, source_target_pairs={{0,4},{4,0},{8,12},{12,8},{16,20},{20,16},{24,28},{28,24},{1,5},{5... | collective-permute-start | bytes 786440 | tf_op jit(solution)/shard_map/ppermute | solution.py:462
  103.5 2.4 %collective-permute-start.30 = (bf16[4,64,512]{2,1,0:T(8,128)(2,1)S(1)}, bf16[4,64,512]{2,1,0:T(8,128)(2,1)S(1)}, u32[]{:S(2)}, u32[]{:S(2)}) collective-permute-start(bf16[4,64,512]{2,1,0:T(8,128)(2,1)S(1)} %get-tuple-element.47), channel_id=1, source_target_pairs={{0,4},{4,0},{8,12},{12,8},{16,20},{20,16},{24,28},{28,24},{1,5},{5... | collective-permute-start | bytes 786440 | tf_op jit(solution)/shard_map/ppermute | solution.py:462
  103.6 2.4 %collective-permute-start.31 = (bf16[4,64,512]{2,1,0:T(8,128)(2,1)S(1)}, bf16[4,64,512]{2,1,0:T(8,128)(2,1)S(1)}, u32[]{:S(2)}, u32[]{:S(2)}) collective-permute-start(bf16[4,64,512]{2,1,0:T(8,128)(2,1)S(1)} %get-tuple-element.43.refs_4_), channel_id=1, source_target_pairs={{0,4},{4,0},{8,12},{12,8},{16,20},{20,16},{24,28},{28,24},{1,5},{5... | collective-permute-start | bytes 786440 | tf_op jit(solution)/shard_map/ppermute | solution.py:462
  104.0 1.9 %collective-permute-start.32 = (bf16[4,64,512]{2,1,0:T(8,128)(2,1)S(1)}, bf16[4,64,512]{2,1,0:T(8,128)(2,1)S(1)}, u32[]{:S(2)}, u32[]{:S(2)}) collective-permute-start(bf16[4,64,512]{2,1,0:T(8,128)(2,1)S(1)} %get-tuple-element.49), channel_id=1, source_target_pairs={{0,4},{4,0},{8,12},{12,8},{16,20},{20,16},{24,28},{28,24},{1,5},{5... | collective-permute-start | bytes 786440 | tf_op jit(solution)/shard_map/ppermute | solution.py:462
  106.1 7.6 %collective-permute-start.33 = (bf16[4,64,512]{2,1,0:T(8,128)(2,1)S(1)}, bf16[4,64,512]{2,1,0:T(8,128)(2,1)S(1)}, u32[]{:S(2)}, u32[]{:S(2)}) collective-permute-start(bf16[4,64,512]{2,1,0:T(8,128)(2,1)S(1)} %get-tuple-element.52), channel_id=1, source_target_pairs={{0,16},{4,12},{8,24},{12,4},{16,0},{20,28},{24,8},{28,20},{1,17},{... | collective-permute-start | bytes 786440 | tf_op jit(solution)/shard_map/ppermute | solution.py:52
  106.2 9.1 %collective-permute-start.34 = (bf16[4,64,512]{2,1,0:T(8,128)(2,1)S(1)}, bf16[4,64,512]{2,1,0:T(8,128)(2,1)S(1)}, u32[]{:S(2)}, u32[]{:S(2)}) collective-permute-start(bf16[4,64,512]{2,1,0:T(8,128)(2,1)S(1)} %get-tuple-element.50.refs_4_), channel_id=1, source_target_pairs={{0,16},{4,12},{8,24},{12,4},{16,0},{20,28},{24,8},{28,20},{1,17},{... | collective-permute-start | bytes 786440 | tf_op jit(solution)/shard_map/ppermute | solution.py:52
  117.3 4.7 %collective-permute-start.35 = (bf16[4,64,512]{2,1,0:T(8,128)(2,1)S(1)}, bf16[4,64,512]{2,1,0:T(8,128)(2,1)S(1)}, u32[]{:S(2)}, u32[]{:S(2)}) collective-permute-start(bf16[4,64,512]{2,1,0:T(8,128)(2,1)S(1)} %get-tuple-element.53.refs_4_), channel_id=1, source_target_pairs={{0,4},{4,0},{8,12},{12,8},{16,20},{20,16},{24,28},{28,24},{1,5},{5... | collective-permute-start | bytes 786440 | tf_op jit(solution)/shard_map/ppermute | solution.py:462
  117.4 4.6 %collective-permute-start.36 = (bf16[4,64,512]{2,1,0:T(8,128)(2,1)S(1)}, bf16[4,64,512]{2,1,0:T(8,128)(2,1)S(1)}, u32[]{:S(2)}, u32[]{:S(2)}) collective-permute-start(bf16[4,64,512]{2,1,0:T(8,128)(2,1)S(1)} %get-tuple-element.56), channel_id=1, source_target_pairs={{0,4},{4,0},{8,12},{12,8},{16,20},{20,16},{24,28},{28,24},{1,5},{5... | collective-permute-start | bytes 786440 | tf_op jit(solution)/shard_map/ppermute | solution.py:462
  117.9 4.1 %collective-permute-start.37 = (bf16[4,64,512]{2,1,0:T(8,128)(2,1)S(1)}, bf16[4,64,512]{2,1,0:T(8,128)(2,1)S(1)}, u32[]{:S(2)}, u32[]{:S(2)}) collective-permute-start(bf16[4,64,512]{2,1,0:T(8,128)(2,1)S(1)} %get-tuple-element.58), channel_id=1, source_target_pairs={{0,4},{4,0},{8,12},{12,8},{16,20},{20,16},{24,28},{28,24},{1,5},{5... | collective-permute-start | bytes 786440 | tf_op jit(solution)/shard_map/ppermute | solution.py:462
  117.9 4.0 %collective-permute-start.38 = (bf16[4,64,512]{2,1,0:T(8,128)(2,1)S(1)}, bf16[4,64,512]{2,1,0:T(8,128)(2,1)S(1)}, u32[]{:S(2)}, u32[]{:S(2)}) collective-permute-start(bf16[4,64,512]{2,1,0:T(8,128)(2,1)S(1)} %get-tuple-element.60), channel_id=1, source_target_pairs={{0,4},{4,0},{8,12},{12,8},{16,20},{20,16},{24,28},{28,24},{1,5},{5... | collective-permute-start | bytes 786440 | tf_op jit(solution)/shard_map/ppermute | solution.py:462
  118.4 7.4 %collective-permute-start.42 = (bf16[4,64,512]{2,1,0:T(8,128)(2,1)S(1)}, bf16[4,64,512]{2,1,0:T(8,128)(2,1)S(1)}, u32[]{:S(2)}, u32[]{:S(2)}) collective-permute-start(bf16[4,64,512]{2,1,0:T(8,128)(2,1)S(1)} %add_terms.14.refs_4_), channel_id=1, source_target_pairs={{0,8},{4,20},{8,0},{12,28},{16,24},{20,4},{24,16},{28,12},{1,9},{5... | collective-permute-start | bytes 786440 | tf_op jit(solution)/shard_map/ppermute | solution.py:52
  122.2 9.3 %collective-permute-start.39 = (bf16[4,64,512]{2,1,0:T(8,128)(2,1)S(1)}, bf16[4,64,512]{2,1,0:T(8,128)(2,1)S(1)}, u32[]{:S(2)}, u32[]{:S(2)}) collective-permute-start(bf16[4,64,512]{2,1,0:T(8,128)(2,1)S(1)} %get-tuple-element.62), channel_id=1, source_target_pairs={{0,8},{4,20},{8,0},{12,28},{16,24},{20,4},{24,16},{28,12},{1,9},{5... | collective-permute-start | bytes 786440 | tf_op jit(solution)/shard_map/ppermute | solution.py:99
  122.6 11.4 %collective-permute-start.40 = (bf16[4,64,512]{2,1,0:T(8,128)(2,1)S(1)}, bf16[4,64,512]{2,1,0:T(8,128)(2,1)S(1)}, u32[]{:S(2)}, u32[]{:S(2)}) collective-permute-start(bf16[4,64,512]{2,1,0:T(8,128)(2,1)S(1)} %get-tuple-element.63), channel_id=1, source_target_pairs={{0,16},{4,12},{8,24},{12,4},{16,0},{20,28},{24,8},{28,20},{1,17},{... | collective-permute-start | bytes 786440 | tf_op jit(solution)/shard_map/ppermute | solution.py:99
  122.7 13.0 %collective-permute-start.41 = (bf16[4,64,512]{2,1,0:T(8,128)(2,1)S(1)}, bf16[4,64,512]{2,1,0:T(8,128)(2,1)S(1)}, u32[]{:S(2)}, u32[]{:S(2)}) collective-permute-start(bf16[4,64,512]{2,1,0:T(8,128)(2,1)S(1)} %get-tuple-element.64), channel_id=1, source_target_pairs={{0,24},{4,28},{8,16},{12,20},{16,8},{20,12},{24,0},{28,4},{1,25},{... | collective-permute-start | bytes 786440 | tf_op jit(solution)/shard_map/ppermute | solution.py:99
  125.9 13.1 %collective-permute-start.46 = (bf16[64,512]{1,0:T(8,128)(2,1)S(1)}, bf16[64,512]{1,0:T(8,128)(2,1)S(1)}, u32[]{:S(2)}, u32[]{:S(2)}) collective-permute-start(bf16[64,512]{1,0:T(8,128)(2,1)S(1)} %get-tuple-element.71), channel_id=1, source_target_pairs={{0,1},{1,2},{2,3},{3,0},{4,5},{5,6},{6,7},{7,4},{8,9},{9,10},{10,1... | collective-permute-start | bytes 196616 | tf_op jit(solution)/shard_map/ppermute | solution.py:107
  126.2 13.6 %collective-permute-start.47 = (bf16[64,512]{1,0:T(8,128)(2,1)S(1)}, bf16[64,512]{1,0:T(8,128)(2,1)S(1)}, u32[]{:S(2)}, u32[]{:S(2)}) collective-permute-start(bf16[64,512]{1,0:T(8,128)(2,1)S(1)} %get-tuple-element.70), channel_id=1, source_target_pairs={{0,2},{1,3},{2,0},{3,1},{4,6},{5,7},{6,4},{7,5},{8,10},{9,11},{10,... | collective-permute-start | bytes 196616 | tf_op jit(solution)/shard_map/ppermute | solution.py:107
  131.5 8.3 %collective-permute-start.48 = (bf16[64,512]{1,0:T(8,128)(2,1)S(1)}, bf16[64,512]{1,0:T(8,128)(2,1)S(1)}, u32[]{:S(2)}, u32[]{:S(2)}) collective-permute-start(bf16[64,512]{1,0:T(8,128)(2,1)S(1)} %get-tuple-element.69), channel_id=1, source_target_pairs={{0,3},{1,0},{2,1},{3,2},{4,7},{5,4},{6,5},{7,6},{8,11},{9,8},{10,9... | collective-permute-start | bytes 196616 | tf_op jit(solution)/shard_map/ppermute | solution.py:107
  135.9 6.9 %collective-permute-start.43 = (bf16[64,512]{1,0:T(8,128)(2,1)S(1)}, bf16[64,512]{1,0:T(8,128)(2,1)S(1)}, u32[]{:S(2)}, u32[]{:S(2)}) collective-permute-start(bf16[64,512]{1,0:T(8,128)(2,1)S(1)} %get-tuple-element.75), channel_id=1, source_target_pairs={{0,1},{1,2},{2,3},{3,0},{4,5},{5,6},{6,7},{7,4},{8,9},{9,10},{10,1... | collective-permute-start | bytes 196616 | tf_op jit(solution)/shard_map/ppermute | solution.py:107
  136.3 7.8 %collective-permute-start.44 = (bf16[64,512]{1,0:T(8,128)(2,1)S(1)}, bf16[64,512]{1,0:T(8,128)(2,1)S(1)}, u32[]{:S(2)}, u32[]{:S(2)}) collective-permute-start(bf16[64,512]{1,0:T(8,128)(2,1)S(1)} %get-tuple-element.74), channel_id=1, source_target_pairs={{0,2},{1,3},{2,0},{3,1},{4,6},{5,7},{6,4},{7,5},{8,10},{9,11},{10,... | collective-permute-start | bytes 196616 | tf_op jit(solution)/shard_map/ppermute | solution.py:107
  139.0 5.1 %collective-permute-start.45 = (bf16[64,512]{1,0:T(8,128)(2,1)S(1)}, bf16[64,512]{1,0:T(8,128)(2,1)S(1)}, u32[]{:S(2)}, u32[]{:S(2)}) collective-permute-start(bf16[64,512]{1,0:T(8,128)(2,1)S(1)} %get-tuple-element.73), channel_id=1, source_target_pairs={{0,3},{1,0},{2,1},{3,2},{4,7},{5,4},{6,5},{7,6},{8,11},{9,8},{10,9... | collective-permute-start | bytes 196616 | tf_op jit(solution)/shard_map/ppermute | solution.py:107
  139.8 8.3 %collective-permute-start.52 = (bf16[4,64,512]{2,1,0:T(8,128)(2,1)S(1)}, bf16[4,64,512]{2,1,0:T(8,128)(2,1)S(1)}, u32[]{:S(2)}, u32[]{:S(2)}) collective-permute-start(bf16[4,64,512]{2,1,0:T(8,128)(2,1)S(1)} %stack_planes.10.refs_4_.refs_1_), channel_id=1, source_target_pairs={{0,8},{4,20},{8,0},{12,28},{16,24},{20,4},{24,16},{28,12},{1,9},{5... | collective-permute-start | bytes 786440 | tf_op jit(solution)/shard_map/ppermute | solution.py:52
  144.2 9.4 %collective-permute-start.49 = (bf16[4,64,512]{2,1,0:T(8,128)(2,1)S(1)}, bf16[4,64,512]{2,1,0:T(8,128)(2,1)S(1)}, u32[]{:S(2)}, u32[]{:S(2)}) collective-permute-start(bf16[4,64,512]{2,1,0:T(8,128)(2,1)S(1)} %stack_planes.11.refs_1_), channel_id=1, source_target_pairs={{0,8},{4,20},{8,0},{12,28},{16,24},{20,4},{24,16},{28,12},{1,9},{5... | collective-permute-start | bytes 786440 | tf_op jit(solution)/shard_map/ppermute | solution.py:52
  146.4 8.9 %collective-permute-start.53 = (bf16[4,64,512]{2,1,0:T(8,128)(2,1)S(1)}, bf16[4,64,512]{2,1,0:T(8,128)(2,1)S(1)}, u32[]{:S(2)}, u32[]{:S(2)}) collective-permute-start(bf16[4,64,512]{2,1,0:T(8,128)(2,1)S(1)} %stack_planes.10.refs_4_.refs_1_), channel_id=1, source_target_pairs={{0,16},{4,12},{8,24},{12,4},{16,0},{20,28},{24,8},{28,20},{1,17},{... | collective-permute-start | bytes 786440 | tf_op jit(solution)/shard_map/ppermute | solution.py:52
  148.1 7.5 %collective-permute-start.54 = (bf16[4,64,512]{2,1,0:T(8,128)(2,1)S(1)}, bf16[4,64,512]{2,1,0:T(8,128)(2,1)S(1)}, u32[]{:S(2)}, u32[]{:S(2)}) collective-permute-start(bf16[4,64,512]{2,1,0:T(8,128)(2,1)S(1)} %collective-permute-done.52.refs_2_), channel_id=1, source_target_pairs={{0,16},{4,12},{8,24},{12,4},{16,0},{20,28},{24,8},{28,20},{1,17},{... | collective-permute-start | bytes 786440 | tf_op jit(solution)/shard_map/ppermute | solution.py:52
  148.7 9.7 %collective-permute-start.50 = (bf16[4,64,512]{2,1,0:T(8,128)(2,1)S(1)}, bf16[4,64,512]{2,1,0:T(8,128)(2,1)S(1)}, u32[]{:S(2)}, u32[]{:S(2)}) collective-permute-start(bf16[4,64,512]{2,1,0:T(8,128)(2,1)S(1)} %stack_planes.11.refs_1_), channel_id=1, source_target_pairs={{0,16},{4,12},{8,24},{12,4},{16,0},{20,28},{24,8},{28,20},{1,17},{... | collective-permute-start | bytes 786440 | tf_op jit(solution)/shard_map/ppermute | solution.py:52
  153.5 7.6 %collective-permute-start.51 = (bf16[4,64,512]{2,1,0:T(8,128)(2,1)S(1)}, bf16[4,64,512]{2,1,0:T(8,128)(2,1)S(1)}, u32[]{:S(2)}, u32[]{:S(2)}) collective-permute-start(bf16[4,64,512]{2,1,0:T(8,128)(2,1)S(1)} %collective-permute-done.49.refs_2_), channel_id=1, source_target_pairs={{0,16},{4,12},{8,24},{12,4},{16,0},{20,28},{24,8},{28,20},{1,17},{... | collective-permute-start | bytes 786440 | tf_op jit(solution)/shard_map/ppermute | solution.py:52
  162.2 2.0 %collective-permute-start.55 = (bf16[8,64,512]{2,1,0:T(8,128)(2,1)S(1)}, bf16[8,64,512]{2,1,0:T(8,128)(2,1)S(1)}, u32[]{:S(2)}, u32[]{:S(2)}) collective-permute-start(bf16[8,64,512]{2,1,0:T(8,128)(2,1)S(1)} %add_expert_rows.5), channel_id=1, source_target_pairs={{0,4},{4,0},{8,12},{12,8},{16,20},{20,16},{24,28},{28,24},{1,5},{5... | collective-permute-start | bytes 1572872 | tf_op jit(solution)/shard_map/ppermute | solution.py:462
  (2 other events, 24.1 us)

commit v8 on v7

--- a/solution.py
+++ b/solution.py
@@ -10,8 +10,8 @@
 GROUPS = 2
 DIRECT = ((0, 0, 0, 0), (0, 1, 1, 0))
 PICK_WAIT = (0, 0)
-HOP_WAIT = ((0, 1), (0, 0))
-ORDER = '001010110010001011101011'
+HOP_WAIT = ((0, 1), (1, 0))
+ORDER = '001010110001001101101011'
 
 
 def bit_orders(n_bits):
@@ -336,7 +336,7 @@
                 to = to if s else r
                 xs[to * rows : (to + 1) * rows, at] = pieces[r, z]
     ff = wg.shape[1]
-    tile = min(ff, 256)
+    tile = min(ff, 1024)
 
     def one(i, carry):
         at = pl.ds(pl.multiple_of(i * tile, tile), tile)

time: 165 us -> 163 us (0.988)
    ppermute x24, starting transfers between devices: 36.9 us -> 33.6 us  [exchange(): return lax.ppermute(value, 'dp', step_pairs(n_dp, step))]
    ppermute x12, starting transfers between devices: 19.7 us -> 22.4 us  [swap_planes(): out.append(lax.ppermute(parts[k], 'expert', pairs))]
  transfers between devices with their start and end apart: 56 -> 56, of which waited for: 22 -> 26; matrix products, arithmetic and copies ran while one was open for 2% -> 2% of each run, Pallas kernels for 16% -> 16%
where the time goes in v8:
time: 163 us
  starting transfers between devices  66.4 us (41%)
  waiting for transfers between devices  61.8 us (38%)
  Pallas kernels  31.5 us (19%)
  local copies, waits for them, and re-layouts  2.82 us (2%)
    ppermute x24, waiting for transfers between devices, exchange(): return lax.ppermute(value, 'dp', step_pairs(n_dp, step))  41.4 us
    ppermute x24, starting transfers between devices, exchange(): return lax.ppermute(value, 'dp', step_pairs(n_dp, step))  33.6 us
    ppermute x12, starting transfers between devices, swap_planes(): out.append(lax.ppermute(parts[k], 'expert', pairs))  22.4 us
    ppermute x6, waiting for transfers between devices, direct(): out.append(lax.ppermute(value, 'dp', pairs) if r else value)  9.34 us
    pallas_call x2, Pallas kernels, hidden_units(): call(lambda *refs: hidden_kernel(make_place, reverse, *refs), jax.ShapeDt...  9.29 us
    pallas_call x3, Pallas kernels, project(): call(lambda *refs: project_kernel(make_place, parts, len(weights), len(ex...  7.82 us
    pallas_call x4, Pallas kernels, down(): call(lambda *refs: down_kernel(make_place, layout, order, s, *refs), [jax...  7.29 us
    ppermute x6, starting transfers between devices, direct(): out.append(lax.ppermute(value, 'dp', pairs) if r else value)  7.11 us
  transfers between devices with their start and end apart: 56, of which 26 were waited for; matrix products, arithmetic and copies ran while one was open for 2% of the time, Pallas kernels for 16%

profile of v8, /device:TPU:0, one launch (start us, length us, event | category | flops | bytes accessed | tf_op | source)
XLA Modules:
  0.0 163.0 jit_solution(12489664874437474153)
XLA Ops:
  0.5 1.4 constant_dynamic-slice_fusion.2
  2.0 2.9 %collective-permute-start.1 = (bf16[512,512]{1,0:T(8,128)(2,1)S(1)}, bf16[512,512]{1,0:T(8,128)(2,1)S(1)}, u32[]{:S(2)}, u32[]{:S(2)}) collective-permute-start(bf16[512,512]{1,0:T(8,128)(2,1)S(1)} %get-tuple-element.68.refs_2_), channel_id=1, source_target_pairs={{0,8},{4,20},{8,0},{12,28},{16,24},{20,4},{24,16},{28,12},{1,9},{5... | collective-permute-start | bytes 1572872 | tf_op jit(solution)/shard_map/ppermute | solution.py:52
  4.9 3.1 %collective-permute-done.3.refs_3_ = bf16[512,512]{1,0:T(8,128)(2,1)S(1)} collective-permute-done((bf16[512,512]{1,0:T(8,128)(2,1)S(1)}, bf16[512,512]{1,0:T(8,128)(2,1)S(1)}, u32[]{:S(2)}, u32[]{:S(2)}) %collective-permute-start.3) | collective-permute-done | bytes 524320 | tf_op jit(solution)/shard_map/ppermute | solution.py:462
  8.0 2.9 %collective-permute-start.4 = (bf16[512,512]{1,0:T(8,128)(2,1)S(1)}, bf16[512,512]{1,0:T(8,128)(2,1)S(1)}, u32[]{:S(2)}, u32[]{:S(2)}) collective-permute-start(bf16[512,512]{1,0:T(8,128)(2,1)S(1)} %collective-permute-done.3.refs_3_), channel_id=1, source_target_pairs={{0,8},{4,20},{8,0},{12,28},{16,24},{20,4},{24,16},{28,12},{1,9},{5... | collective-permute-start | bytes 1572872 | tf_op jit(solution)/shard_map/ppermute | solution.py:52
  10.8 1.5 collective-permute-start.6
  12.4 1.3 constant_dynamic-slice_fusion
  13.7 0.9 collective-permute-start.7
  14.6 8.2 %collective-permute-done.4.refs_5_ = bf16[512,512]{1,0:T(8,128)(2,1)S(1)} collective-permute-done((bf16[512,512]{1,0:T(8,128)(2,1)S(1)}, bf16[512,512]{1,0:T(8,128)(2,1)S(1)}, u32[]{:S(2)}, u32[]{:S(2)}) %collective-permute-start.4) | collective-permute-done | bytes 524320 | tf_op jit(solution)/shard_map/ppermute | solution.py:52
  22.8 3.0 %collective-permute-start.2 = (bf16[512,512]{1,0:T(8,128)(2,1)S(1)}, bf16[512,512]{1,0:T(8,128)(2,1)S(1)}, u32[]{:S(2)}, u32[]{:S(2)}) collective-permute-start(bf16[512,512]{1,0:T(8,128)(2,1)S(1)} %collective-permute-done.1.refs_4_), channel_id=1, source_target_pairs={{0,16},{4,12},{8,24},{12,4},{16,0},{20,28},{24,8},{28,20},{1,17},{... | collective-permute-start | bytes 1572872 | tf_op jit(solution)/shard_map/ppermute | solution.py:52
  25.9 3.3 %project.3.refs_4_ = f32[2,512,512]{2,1,0:T(8,128)S(1)} custom-call(bf16[512,4096]{1,0:T(8,128)(2,1)S(1)} %copy-done, bf16[512,4096]{1,0:T(8,128)(2,1)} %collective-permute-done.refs_1_, bf16[512,512]{1,0:T(8,128)(2,1)S(1)} %get-tuple-element.68.refs_2_, bf16[512,512]{1,0:T(8,128)(2,1)S(1)} %collective-permute-done.3.refs_3_, ...), custom_call_target="tpu_custom_call" | custom-call | tf_op jit(solution)/shard_map/project/pallas_call | solution.py:239
  29.3 2.2 %project.4.refs_4_ = f32[2,512,512]{2,1,0:T(8,128)S(1)} custom-call(bf16[512,4096]{1,0:T(8,128)(2,1)S(1)} %copy-done, bf16[512,4096]{1,0:T(8,128)(2,1)} %collective-permute-done.refs_1_, bf16[512,512]{1,0:T(8,128)(2,1)S(1)} %collective-permute-done.6.refs_2_, bf16[512,512]{1,0:T(8,128)(2,1)S(1)} %collective-permute-done.7.refs_3_, ...), custom_call_target="tpu_custom_call" | custom-call | tf_op jit(solution)/shard_map/project/pallas_call | solution.py:239
  31.5 2.9 %collective-permute-done.2.refs_2_ = bf16[512,512]{1,0:T(8,128)(2,1)S(1)} collective-permute-done((bf16[512,512]{1,0:T(8,128)(2,1)S(1)}, bf16[512,512]{1,0:T(8,128)(2,1)S(1)}, u32[]{:S(2)}, u32[]{:S(2)}) %collective-permute-start.2) | collective-permute-done | bytes 524320 | tf_op jit(solution)/shard_map/ppermute | solution.py:52
  34.3 5.6 %collective-permute-done.5.refs_3_ = bf16[512,512]{1,0:T(8,128)(2,1)S(1)} collective-permute-done((bf16[512,512]{1,0:T(8,128)(2,1)S(1)}, bf16[512,512]{1,0:T(8,128)(2,1)S(1)}, u32[]{:S(2)}, u32[]{:S(2)}) %collective-permute-start.5) | collective-permute-done | bytes 524320 | tf_op jit(solution)/shard_map/ppermute | solution.py:52
  40.0 2.3 %project.5 = bf16[2,512,512]{2,1,0:T(8,128)(2,1)S(1)} custom-call(bf16[512,4096]{1,0:T(8,128)(2,1)S(1)} %copy-done, bf16[512,4096]{1,0:T(8,128)(2,1)} %collective-permute-done.refs_1_, bf16[512,512]{1,0:T(8,128)(2,1)S(1)} %collective-permute-done.2.refs_2_, bf16[512,512]{1,0:T(8,128)(2,1)S(1)} %collective-permute-done.5.refs_3_, ...), custom_call_target="tpu_custom_call" | custom-call | tf_op jit(solution)/shard_map/project/pallas_call | solution.py:239
  42.3 0.8 pick_blocks.2
  43.1 1.8 %collective-permute-start.9 = (bf16[4,64,512]{2,1,0:T(8,128)(2,1)S(1)}, bf16[4,64,512]{2,1,0:T(8,128)(2,1)S(1)}, u32[]{:S(2)}, u32[]{:S(2)}) collective-permute-start(bf16[4,64,512]{2,1,0:T(8,128)(2,1)S(1)} %get-tuple-element.36), channel_id=1, source_target_pairs={{0,16},{4,12},{8,24},{12,4},{16,0},{20,28},{24,8},{28,20},{1,17},{... | collective-permute-start | bytes 786440 | tf_op jit(solution)/shard_map/ppermute | solution.py:52
  45.2 4.3 %collective-permute-done.9.refs_1_ = bf16[4,64,512]{2,1,0:T(8,128)(2,1)S(1)} collective-permute-done((bf16[4,64,512]{2,1,0:T(8,128)(2,1)S(1)}, bf16[4,64,512]{2,1,0:T(8,128)(2,1)S(1)}, u32[]{:S(2)}, u32[]{:S(2)}) %collective-permute-start.9) | collective-permute-done | bytes 262176 | tf_op jit(solution)/shard_map/ppermute | solution.py:52
  49.6 1.8 %collective-permute-start.13 = (bf16[4,64,512]{2,1,0:T(8,128)(2,1)S(1)}, bf16[4,64,512]{2,1,0:T(8,128)(2,1)S(1)}, u32[]{:S(2)}, u32[]{:S(2)}) collective-permute-start(bf16[4,64,512]{2,1,0:T(8,128)(2,1)S(1)} %add_terms.9.refs_2_), channel_id=1, source_target_pairs={{0,8},{4,20},{8,0},{12,28},{16,24},{20,4},{24,16},{28,12},{1,9},{5... | collective-permute-start | bytes 786440 | tf_op jit(solution)/shard_map/ppermute | solution.py:52
  51.4 0.8 pick_blocks.3
  52.2 1.6 collective-permute-start.10
  54.3 3.7 %collective-permute-done.13.refs_2_ = bf16[4,64,512]{2,1,0:T(8,128)(2,1)S(1)} collective-permute-done((bf16[4,64,512]{2,1,0:T(8,128)(2,1)S(1)}, bf16[4,64,512]{2,1,0:T(8,128)(2,1)S(1)}, u32[]{:S(2)}, u32[]{:S(2)}) %collective-permute-start.13) | collective-permute-done | bytes 262176 | tf_op jit(solution)/shard_map/ppermute | solution.py:52
  58.2 2.1 %collective-permute-start.15 = (bf16[64,512]{1,0:T(8,128)(2,1)S(1)}, bf16[64,512]{1,0:T(8,128)(2,1)S(1)}, u32[]{:S(2)}, u32[]{:S(2)}) collective-permute-start(bf16[64,512]{1,0:T(8,128)(2,1)S(1)} %get-tuple-element.83), channel_id=1, source_target_pairs={{0,1},{1,2},{2,3},{3,0},{4,5},{5,6},{6,7},{7,4},{8,9},{9,10},{10,1... | collective-permute-start | bytes 196616 | tf_op jit(solution)/shard_map/ppermute | solution.py:107
  60.3 2.6 %collective-permute-start.16 = (bf16[64,512]{1,0:T(8,128)(2,1)S(1)}, bf16[64,512]{1,0:T(8,128)(2,1)S(1)}, u32[]{:S(2)}, u32[]{:S(2)}) collective-permute-start(bf16[64,512]{1,0:T(8,128)(2,1)S(1)} %get-tuple-element.82), channel_id=1, source_target_pairs={{0,2},{1,3},{2,0},{3,1},{4,6},{5,7},{6,4},{7,5},{8,10},{9,11},{10,... | collective-permute-start | bytes 196616 | tf_op jit(solution)/shard_map/ppermute | solution.py:107
  62.9 1.3 collective-permute-start.17
  64.3 1.6 collective-permute-start.14
  65.9 1.3 collective-permute-done.17.refs_3_
  67.2 1.6 collective-permute-start.24
  68.7 2.1 %collective-permute-start.25 = (bf16[4,64,512]{2,1,0:T(8,128)(2,1)S(1)}, bf16[4,64,512]{2,1,0:T(8,128)(2,1)S(1)}, u32[]{:S(2)}, u32[]{:S(2)}) collective-permute-start(bf16[4,64,512]{2,1,0:T(8,128)(2,1)S(1)} %stack_planes.6.refs_3_.refs_0_), channel_id=1, source_target_pairs={{0,16},{4,12},{8,24},{12,4},{16,0},{20,28},{24,8},{28,20},{1,17},{... | collective-permute-start | bytes 786440 | tf_op jit(solution)/shard_map/ppermute | solution.py:52
  70.8 1.3 collective-permute-done.14.refs_2_
  72.2 5.0 %collective-permute-done.24.refs_1_ = bf16[4,64,512]{2,1,0:T(8,128)(2,1)S(1)} collective-permute-done((bf16[4,64,512]{2,1,0:T(8,128)(2,1)S(1)}, bf16[4,64,512]{2,1,0:T(8,128)(2,1)S(1)}, u32[]{:S(2)}, u32[]{:S(2)}) %collective-permute-start.24) | collective-permute-done | bytes 262176 | tf_op jit(solution)/shard_map/ppermute | solution.py:52
  77.4 1.7 %collective-permute-start.18 = (bf16[64,512]{1,0:T(8,128)(2,1)S(1)}, bf16[64,512]{1,0:T(8,128)(2,1)S(1)}, u32[]{:S(2)}, u32[]{:S(2)}) collective-permute-start(bf16[64,512]{1,0:T(8,128)(2,1)S(1)} %get-tuple-element.79), channel_id=1, source_target_pairs={{0,1},{1,2},{2,3},{3,0},{4,5},{5,6},{6,7},{7,4},{8,9},{9,10},{10,1... | collective-permute-start | bytes 196616 | tf_op jit(solution)/shard_map/ppermute | solution.py:107
  79.1 1.4 collective-permute-start.19
  80.5 2.5 %collective-permute-start.20 = (bf16[64,512]{1,0:T(8,128)(2,1)S(1)}, bf16[64,512]{1,0:T(8,128)(2,1)S(1)}, u32[]{:S(2)}, u32[]{:S(2)}) collective-permute-start(bf16[64,512]{1,0:T(8,128)(2,1)S(1)} %get-tuple-element.77), channel_id=1, source_target_pairs={{0,3},{1,0},{2,1},{3,2},{4,7},{5,4},{6,5},{7,6},{8,11},{9,8},{10,9... | collective-permute-start | bytes 196616 | tf_op jit(solution)/shard_map/ppermute | solution.py:107
  85.2 1.7 %collective-permute-start.21 = (bf16[4,64,512]{2,1,0:T(8,128)(2,1)S(1)}, bf16[4,64,512]{2,1,0:T(8,128)(2,1)S(1)}, u32[]{:S(2)}, u32[]{:S(2)}) collective-permute-start(bf16[4,64,512]{2,1,0:T(8,128)(2,1)S(1)} %stack_planes.7.refs_4_.refs_0_), channel_id=1, source_target_pairs={{0,8},{4,20},{8,0},{12,28},{16,24},{20,4},{24,16},{28,12},{1,9},{5... | collective-permute-start | bytes 786440 | tf_op jit(solution)/shard_map/ppermute | solution.py:99
  86.9 1.4 collective-permute-start.22
  88.8 4.6 %expert_hidden.2.refs_1_.refs_4_ = bf16[256,1024]{1,0:T(8,128)(2,1)S(1)} custom-call(bf16[4,4,64,512]{3,2,1,0:T(8,128)(2,1)S(1)} %stack_planes.8.refs_0_.refs_4_, bf16[4,4,64,512]{3,2,1,0:T(8,128)(2,1)S(1)} %collective-permute-done.27.refs_1_, bf16[4096,1024]{1,0:T(8,128)(2,1)S(1)} %bitcast.44, bf16[4096,1024]{1,0:T(8,128)(2,1)S(1)} %bitcast.48, ...), custom_call_target="tpu_custom_call" | custom-call | tf_op jit(solution)/shard_map/expert_hidden/pallas_call | solution.py:354
  93.5 1.8 %expert_down.4 = (bf16[4,64,512]{2,1,0:T(8,128)(2,1)S(1)}, bf16[4,64,512]{2,1,0:T(8,128)(2,1)S(1)}, bf16[4,64,512]{2,1,0:T(8,128)(2,1)S(1)}, bf16[4,64,512]{2,1,0:T(8,128)(2,1)S(1)}) custom-call(s32[4]{0:T(128)S(1)} %copy-done.3, bf16[256,1024]{1,0:T(8,128)(2,1)S(1)} %expert_hidden.2.refs_1_.refs_4_, bf16[1024,4096]{1,0:T(8,128)(2,1)S(1)} %bitcast.38, ...), custom_call_target="tpu_custom_call" | custom-call | tf_op jit(solution)/shard_map/expert_down/pallas_call | solution.py:389
  95.4 5.3 %collective-permute-done.23.refs_3_ = bf16[4,64,512]{2,1,0:T(8,128)(2,1)S(1)} collective-permute-done((bf16[4,64,512]{2,1,0:T(8,128)(2,1)S(1)}, bf16[4,64,512]{2,1,0:T(8,128)(2,1)S(1)}, u32[]{:S(2)}, u32[]{:S(2)}) %collective-permute-start.23) | collective-permute-done | bytes 262176 | tf_op jit(solution)/shard_map/ppermute | solution.py:99
  101.9 1.8 %expert_down.5 = (bf16[4,64,512]{2,1,0:T(8,128)(2,1)S(1)}, bf16[4,64,512]{2,1,0:T(8,128)(2,1)S(1)}, bf16[4,64,512]{2,1,0:T(8,128)(2,1)S(1)}, bf16[4,64,512]{2,1,0:T(8,128)(2,1)S(1)}) custom-call(s32[4]{0:T(128)S(1)} %copy-done.3, bf16[256,1024]{1,0:T(8,128)(2,1)S(1)} %expert_hidden.2.refs_1_.refs_4_, bf16[1024,4096]{1,0:T(8,128)(2,1)S(1)} %bitcast.39, ...), custom_call_target="tpu_custom_call" | custom-call | tf_op jit(solution)/shard_map/expert_down/pallas_call | solution.py:389
  105.6 1.6 %collective-permute-start.34 = (bf16[4,64,512]{2,1,0:T(8,128)(2,1)S(1)}, bf16[4,64,512]{2,1,0:T(8,128)(2,1)S(1)}, u32[]{:S(2)}, u32[]{:S(2)}) collective-permute-start(bf16[4,64,512]{2,1,0:T(8,128)(2,1)S(1)} %get-tuple-element.50.refs_4_), channel_id=1, source_target_pairs={{0,16},{4,12},{8,24},{12,4},{16,0},{20,28},{24,8},{28,20},{1,17},{... | collective-permute-start | bytes 786440 | tf_op jit(solution)/shard_map/ppermute | solution.py:52
  107.2 4.6 %expert_hidden.3.refs_1_.refs_4_ = bf16[256,1024]{1,0:T(8,128)(2,1)S(1)} custom-call(bf16[4,4,64,512]{3,2,1,0:T(8,128)(2,1)S(1)} %stack_planes.9.refs_4_.refs_0_, bf16[4,4,64,512]{3,2,1,0:T(8,128)(2,1)S(1)} %collective-permute-done.28.refs_1_, bf16[4096,1024]{1,0:T(8,128)(2,1)S(1)} %bitcast.45, bf16[4096,1024]{1,0:T(8,128)(2,1)S(1)} %bitcast.49, ...), custom_call_target="tpu_custom_call" | custom-call | tf_op jit(solution)/shard_map/expert_hidden/pallas_call | solution.py:354
  111.9 1.8 %expert_down.6 = (bf16[4,64,512]{2,1,0:T(8,128)(2,1)S(1)}, bf16[4,64,512]{2,1,0:T(8,128)(2,1)S(1)}, bf16[4,64,512]{2,1,0:T(8,128)(2,1)S(1)}, bf16[4,64,512]{2,1,0:T(8,128)(2,1)S(1)}) custom-call(s32[4]{0:T(128)S(1)} %copy-done.3, bf16[256,1024]{1,0:T(8,128)(2,1)S(1)} %expert_hidden.3.refs_1_.refs_4_, bf16[1024,4096]{1,0:T(8,128)(2,1)S(1)} %bitcast.40, ...), custom_call_target="tpu_custom_call" | custom-call | tf_op jit(solution)/shard_map/expert_down/pallas_call | solution.py:389
  114.9 1.7 %collective-permute-start.42 = (bf16[4,64,512]{2,1,0:T(8,128)(2,1)S(1)}, bf16[4,64,512]{2,1,0:T(8,128)(2,1)S(1)}, u32[]{:S(2)}, u32[]{:S(2)}) collective-permute-start(bf16[4,64,512]{2,1,0:T(8,128)(2,1)S(1)} %add_terms.14.refs_4_), channel_id=1, source_target_pairs={{0,8},{4,20},{8,0},{12,28},{16,24},{20,4},{24,16},{28,12},{1,9},{5... | collective-permute-start | bytes 786440 | tf_op jit(solution)/shard_map/ppermute | solution.py:52
  116.6 1.8 %expert_down.7 = (bf16[4,64,512]{2,1,0:T(8,128)(2,1)S(1)}, bf16[4,64,512]{2,1,0:T(8,128)(2,1)S(1)}, bf16[4,64,512]{2,1,0:T(8,128)(2,1)S(1)}, bf16[4,64,512]{2,1,0:T(8,128)(2,1)S(1)}) custom-call(s32[4]{0:T(128)S(1)} %copy-done.3, bf16[256,1024]{1,0:T(8,128)(2,1)S(1)} %expert_hidden.3.refs_1_.refs_4_, bf16[1024,4096]{1,0:T(8,128)(2,1)S(1)} %bitcast.41, ...), custom_call_target="tpu_custom_call" | custom-call | tf_op jit(solution)/shard_map/expert_down/pallas_call | solution.py:389
  119.5 2.7 %collective-permute-start.41 = (bf16[4,64,512]{2,1,0:T(8,128)(2,1)S(1)}, bf16[4,64,512]{2,1,0:T(8,128)(2,1)S(1)}, u32[]{:S(2)}, u32[]{:S(2)}) collective-permute-start(bf16[4,64,512]{2,1,0:T(8,128)(2,1)S(1)} %get-tuple-element.64), channel_id=1, source_target_pairs={{0,24},{4,28},{8,16},{12,20},{16,8},{20,12},{24,0},{28,4},{1,25},{... | collective-permute-start | bytes 786440 | tf_op jit(solution)/shard_map/ppermute | solution.py:99
  122.5 1.5 collective-permute-start.46
  123.9 1.8 %collective-permute-start.47 = (bf16[64,512]{1,0:T(8,128)(2,1)S(1)}, bf16[64,512]{1,0:T(8,128)(2,1)S(1)}, u32[]{:S(2)}, u32[]{:S(2)}) collective-permute-start(bf16[64,512]{1,0:T(8,128)(2,1)S(1)} %get-tuple-element.70), channel_id=1, source_target_pairs={{0,2},{1,3},{2,0},{3,1},{4,6},{5,7},{6,4},{7,5},{8,10},{9,11},{10,... | collective-permute-start | bytes 196616 | tf_op jit(solution)/shard_map/ppermute | solution.py:107
  125.7 2.3 %collective-permute-done.39.refs_1_ = bf16[4,64,512]{2,1,0:T(8,128)(2,1)S(1)} collective-permute-done((bf16[4,64,512]{2,1,0:T(8,128)(2,1)S(1)}, bf16[4,64,512]{2,1,0:T(8,128)(2,1)S(1)}, u32[]{:S(2)}, u32[]{:S(2)}) %collective-permute-start.39) | collective-permute-done | bytes 262176 | tf_op jit(solution)/shard_map/ppermute | solution.py:99
  128.0 2.6 %collective-permute-start.48 = (bf16[64,512]{1,0:T(8,128)(2,1)S(1)}, bf16[64,512]{1,0:T(8,128)(2,1)S(1)}, u32[]{:S(2)}, u32[]{:S(2)}) collective-permute-start(bf16[64,512]{1,0:T(8,128)(2,1)S(1)} %get-tuple-element.69), channel_id=1, source_target_pairs={{0,3},{1,0},{2,1},{3,2},{4,7},{5,4},{6,5},{7,6},{8,11},{9,8},{10,9... | collective-permute-start | bytes 196616 | tf_op jit(solution)/shard_map/ppermute | solution.py:107
  130.6 1.8 %collective-permute-done.41.refs_3_ = bf16[4,64,512]{2,1,0:T(8,128)(2,1)S(1)} collective-permute-done((bf16[4,64,512]{2,1,0:T(8,128)(2,1)S(1)}, bf16[4,64,512]{2,1,0:T(8,128)(2,1)S(1)}, u32[]{:S(2)}, u32[]{:S(2)}) %collective-permute-start.41) | collective-permute-done | bytes 262176 | tf_op jit(solution)/shard_map/ppermute | solution.py:99
  132.5 1.6 collective-permute-start.43
  134.1 3.1 %collective-permute-start.44 = (bf16[64,512]{1,0:T(8,128)(2,1)S(1)}, bf16[64,512]{1,0:T(8,128)(2,1)S(1)}, u32[]{:S(2)}, u32[]{:S(2)}) collective-permute-start(bf16[64,512]{1,0:T(8,128)(2,1)S(1)} %get-tuple-element.74), channel_id=1, source_target_pairs={{0,2},{1,3},{2,0},{3,1},{4,6},{5,7},{6,4},{7,5},{8,10},{9,11},{10,... | collective-permute-start | bytes 196616 | tf_op jit(solution)/shard_map/ppermute | solution.py:107
  137.5 1.5 collective-permute-start.52
  139.6 1.8 %collective-permute-done.44.refs_2_ = bf16[64,512]{1,0:T(8,128)(2,1)S(1)} collective-permute-done((bf16[64,512]{1,0:T(8,128)(2,1)S(1)}, bf16[64,512]{1,0:T(8,128)(2,1)S(1)}, u32[]{:S(2)}, u32[]{:S(2)}) %collective-permute-start.44) | collective-permute-done | bytes 65568 | tf_op jit(solution)/shard_map/ppermute | solution.py:107
  141.8 2.3 %collective-permute-start.49 = (bf16[4,64,512]{2,1,0:T(8,128)(2,1)S(1)}, bf16[4,64,512]{2,1,0:T(8,128)(2,1)S(1)}, u32[]{:S(2)}, u32[]{:S(2)}) collective-permute-start(bf16[4,64,512]{2,1,0:T(8,128)(2,1)S(1)} %stack_planes.11.refs_1_), channel_id=1, source_target_pairs={{0,8},{4,20},{8,0},{12,28},{16,24},{20,4},{24,16},{28,12},{1,9},{5... | collective-permute-start | bytes 786440 | tf_op jit(solution)/shard_map/ppermute | solution.py:52
  144.8 1.4 collective-permute-start.54
  146.8 4.4 %collective-permute-done.49.refs_2_ = bf16[4,64,512]{2,1,0:T(8,128)(2,1)S(1)} collective-permute-done((bf16[4,64,512]{2,1,0:T(8,128)(2,1)S(1)}, bf16[4,64,512]{2,1,0:T(8,128)(2,1)S(1)}, u32[]{:S(2)}, u32[]{:S(2)}) %collective-permute-start.49) | collective-permute-done | bytes 262176 | tf_op jit(solution)/shard_map/ppermute | solution.py:52
  151.9 1.4 collective-permute-done.54.refs_4_
  153.3 1.1 add_expert_rows.3.refs_5_
  154.4 1.7 %collective-permute-done.50.refs_3_ = bf16[4,64,512]{2,1,0:T(8,128)(2,1)S(1)} collective-permute-done((bf16[4,64,512]{2,1,0:T(8,128)(2,1)S(1)}, bf16[4,64,512]{2,1,0:T(8,128)(2,1)S(1)}, u32[]{:S(2)}, u32[]{:S(2)}) %collective-permute-start.50) | collective-permute-done | bytes 262176 | tf_op jit(solution)/shard_map/ppermute | solution.py:52
  156.1 2.8 %collective-permute-done.51.refs_4_ = bf16[4,64,512]{2,1,0:T(8,128)(2,1)S(1)} collective-permute-done((bf16[4,64,512]{2,1,0:T(8,128)(2,1)S(1)}, bf16[4,64,512]{2,1,0:T(8,128)(2,1)S(1)}, u32[]{:S(2)}, u32[]{:S(2)}) %collective-permute-start.51) | collective-permute-done | bytes 262176 | tf_op jit(solution)/shard_map/ppermute | solution.py:52
  158.9 1.0 add_expert_rows.5
  160.2 1.0 add_expert_rows.4.refs_0_
  161.9 1.1 join_halves.1
  (107 shorter events, 14.7 us)
Async XLA Ops:
  0.0 25.9 %collective-permute-start = (bf16[512,4096]{1,0:T(8,128)(2,1)}, bf16[512,4096]{1,0:T(8,128)(2,1)}, u32[]{:S(2)}, u32[]{:S(2)}) collective-permute-start(bf16[512,4096]{1,0:T(8,128)(2,1)} %refs_0_.14), channel_id=1, source_target_pairs={{0,4},{4,0},{8,12},{12,8},{16,20},{20,16},{24,28},{28,24},{1,5},{5... | collective-permute-start | bytes 12582920 | tf_op jit(solution)/shard_map/ppermute | solution.py:462
  0.5 25.4 %copy-start = (bf16[512,4096]{1,0:T(8,128)(2,1)S(1)}, bf16[512,4096]{1,0:T(8,128)(2,1)}, u32[]{:S(2)}) copy-start(bf16[512,4096]{1,0:T(8,128)(2,1)} %refs_0_.14) | copy-start | bytes 12582916
  1.9 6.1 %collective-permute-start.3 = (bf16[512,512]{1,0:T(8,128)(2,1)S(1)}, bf16[512,512]{1,0:T(8,128)(2,1)S(1)}, u32[]{:S(2)}, u32[]{:S(2)}) collective-permute-start(bf16[512,512]{1,0:T(8,128)(2,1)S(1)} %get-tuple-element.67), channel_id=1, source_target_pairs={{0,4},{4,0},{8,12},{12,8},{16,20},{20,16},{24,28},{28,24},{1,5},{5... | collective-permute-start | bytes 1572872 | tf_op jit(solution)/shard_map/ppermute | solution.py:462
  2.0 11.7 %collective-permute-start.1 = (bf16[512,512]{1,0:T(8,128)(2,1)S(1)}, bf16[512,512]{1,0:T(8,128)(2,1)S(1)}, u32[]{:S(2)}, u32[]{:S(2)}) collective-permute-start(bf16[512,512]{1,0:T(8,128)(2,1)S(1)} %get-tuple-element.68.refs_2_), channel_id=1, source_target_pairs={{0,8},{4,20},{8,0},{12,28},{16,24},{20,4},{24,16},{28,12},{1,9},{5... | collective-permute-start | bytes 1572872 | tf_op jit(solution)/shard_map/ppermute | solution.py:52
  8.0 14.9 %collective-permute-start.4 = (bf16[512,512]{1,0:T(8,128)(2,1)S(1)}, bf16[512,512]{1,0:T(8,128)(2,1)S(1)}, u32[]{:S(2)}, u32[]{:S(2)}) collective-permute-start(bf16[512,512]{1,0:T(8,128)(2,1)S(1)} %collective-permute-done.3.refs_3_), channel_id=1, source_target_pairs={{0,8},{4,20},{8,0},{12,28},{16,24},{20,4},{24,16},{28,12},{1,9},{5... | collective-permute-start | bytes 1572872 | tf_op jit(solution)/shard_map/ppermute | solution.py:52
  10.8 18.4 %collective-permute-start.6 = (bf16[512,512]{1,0:T(8,128)(2,1)S(1)}, bf16[512,512]{1,0:T(8,128)(2,1)S(1)}, u32[]{:S(2)}, u32[]{:S(2)}) collective-permute-start(bf16[512,512]{1,0:T(8,128)(2,1)S(1)} %get-tuple-element.68.refs_2_), channel_id=1, source_target_pairs={{0,16},{4,12},{8,24},{12,4},{16,0},{20,28},{24,8},{28,20},{1,17},{... | collective-permute-start | bytes 1572872 | tf_op jit(solution)/shard_map/ppermute | solution.py:52
  13.7 17.8 %collective-permute-start.8 = (bf16[512,512]{1,0:T(8,128)(2,1)S(1)}, bf16[512,512]{1,0:T(8,128)(2,1)S(1)}, u32[]{:S(2)}, u32[]{:S(2)}) collective-permute-start(bf16[512,512]{1,0:T(8,128)(2,1)S(1)} %get-tuple-element.65), channel_id=1, source_target_pairs={{0,4},{4,0},{8,12},{12,8},{16,20},{20,16},{24,28},{28,24},{1,5},{5... | collective-permute-start | bytes 1572872 | tf_op jit(solution)/shard_map/ppermute | solution.py:462
  13.7 15.5 %collective-permute-start.7 = (bf16[512,512]{1,0:T(8,128)(2,1)S(1)}, bf16[512,512]{1,0:T(8,128)(2,1)S(1)}, u32[]{:S(2)}, u32[]{:S(2)}) collective-permute-start(bf16[512,512]{1,0:T(8,128)(2,1)S(1)} %collective-permute-done.3.refs_3_), channel_id=1, source_target_pairs={{0,16},{4,12},{8,24},{12,4},{16,0},{20,28},{24,8},{28,20},{1,17},{... | collective-permute-start | bytes 1572872 | tf_op jit(solution)/shard_map/ppermute | solution.py:52
  22.8 11.5 %collective-permute-start.2 = (bf16[512,512]{1,0:T(8,128)(2,1)S(1)}, bf16[512,512]{1,0:T(8,128)(2,1)S(1)}, u32[]{:S(2)}, u32[]{:S(2)}) collective-permute-start(bf16[512,512]{1,0:T(8,128)(2,1)S(1)} %collective-permute-done.1.refs_4_), channel_id=1, source_target_pairs={{0,16},{4,12},{8,24},{12,4},{16,0},{20,28},{24,8},{28,20},{1,17},{... | collective-permute-start | bytes 1572872 | tf_op jit(solution)/shard_map/ppermute | solution.py:52
  25.9 14.1 %collective-permute-start.5 = (bf16[512,512]{1,0:T(8,128)(2,1)S(1)}, bf16[512,512]{1,0:T(8,128)(2,1)S(1)}, u32[]{:S(2)}, u32[]{:S(2)}) collective-permute-start(bf16[512,512]{1,0:T(8,128)(2,1)S(1)} %collective-permute-done.4.refs_5_), channel_id=1, source_target_pairs={{0,16},{4,12},{8,24},{12,4},{16,0},{20,28},{24,8},{28,20},{1,17},{... | collective-permute-start | bytes 1572872 | tf_op jit(solution)/shard_map/ppermute | solution.py:52
  29.3 13.0 %copy-start.1 = (s32[4,4]{1,0:T(4,128)S(1)}, s32[4,4]{1,0:T(4,128)}, u32[]{:S(2)}) copy-start(s32[4,4]{1,0:T(4,128)} %refs_0_.23) | copy-start | bytes 196
  40.0 48.8 %slice-start.2 = ((s8[8388608]{0:T(1024)(128)(4,1)}), s8[4194304]{0:T(1024)(128)(4,1)S(1)}, s32[]{:S(2)}) async-start(s8[8388608]{0:T(1024)(128)(4,1)} %bitcast.42), calls=%async_computation.2 | async-start | bytes 8388608
  40.0 48.8 %slice-start.4 = ((s8[8388608]{0:T(1024)(128)(4,1)}), s8[4194304]{0:T(1024)(128)(4,1)S(1)}, s32[]{:S(2)}) async-start(s8[8388608]{0:T(1024)(128)(4,1)} %bitcast.46), calls=%async_computation.4 | async-start | bytes 8388608
  40.0 48.8 %slice-start.3 = ((s8[8388608]{0:T(1024)(128)(4,1)}), s8[4194304]{0:T(1024)(128)(4,1)S(1)}, s32[]{:S(2)}) async-start(s8[8388608]{0:T(1024)(128)(4,1)} %bitcast.42), calls=%async_computation.3 | async-start | bytes 8388608
  40.0 48.8 %slice-start.5 = ((s8[8388608]{0:T(1024)(128)(4,1)}), s8[4194304]{0:T(1024)(128)(4,1)S(1)}, s32[]{:S(2)}) async-start(s8[8388608]{0:T(1024)(128)(4,1)} %bitcast.46), calls=%async_computation.5 | async-start | bytes 8388608
  43.1 6.4 %collective-permute-start.9 = (bf16[4,64,512]{2,1,0:T(8,128)(2,1)S(1)}, bf16[4,64,512]{2,1,0:T(8,128)(2,1)S(1)}, u32[]{:S(2)}, u32[]{:S(2)}) collective-permute-start(bf16[4,64,512]{2,1,0:T(8,128)(2,1)S(1)} %get-tuple-element.36), channel_id=1, source_target_pairs={{0,16},{4,12},{8,24},{12,4},{16,0},{20,28},{24,8},{28,20},{1,17},{... | collective-permute-start | bytes 786440 | tf_op jit(solution)/shard_map/ppermute | solution.py:52
  44.9 9.4 %collective-permute-start.12 = (bf16[4,64,512]{2,1,0:T(8,128)(2,1)S(1)}, bf16[4,64,512]{2,1,0:T(8,128)(2,1)S(1)}, u32[]{:S(2)}, u32[]{:S(2)}) collective-permute-start(bf16[4,64,512]{2,1,0:T(8,128)(2,1)S(1)} %get-tuple-element.42), channel_id=1, source_target_pairs={{0,16},{4,12},{8,24},{12,4},{16,0},{20,28},{24,8},{28,20},{1,17},{... | collective-permute-start | bytes 786440 | tf_op jit(solution)/shard_map/ppermute | solution.py:52
  49.6 8.4 %collective-permute-start.13 = (bf16[4,64,512]{2,1,0:T(8,128)(2,1)S(1)}, bf16[4,64,512]{2,1,0:T(8,128)(2,1)S(1)}, u32[]{:S(2)}, u32[]{:S(2)}) collective-permute-start(bf16[4,64,512]{2,1,0:T(8,128)(2,1)S(1)} %add_terms.9.refs_2_), channel_id=1, source_target_pairs={{0,8},{4,20},{8,0},{12,28},{16,24},{20,4},{24,16},{28,12},{1,9},{5... | collective-permute-start | bytes 786440 | tf_op jit(solution)/shard_map/ppermute | solution.py:52
  52.2 12.0 %collective-permute-start.10 = (bf16[4,64,512]{2,1,0:T(8,128)(2,1)S(1)}, bf16[4,64,512]{2,1,0:T(8,128)(2,1)S(1)}, u32[]{:S(2)}, u32[]{:S(2)}) collective-permute-start(bf16[4,64,512]{2,1,0:T(8,128)(2,1)S(1)} %get-tuple-element.39), channel_id=1, source_target_pairs={{0,16},{4,12},{8,24},{12,4},{16,0},{20,28},{24,8},{28,20},{1,17},{... | collective-permute-start | bytes 786440 | tf_op jit(solution)/shard_map/ppermute | solution.py:52
  53.8 10.4 %collective-permute-start.11 = (bf16[4,64,512]{2,1,0:T(8,128)(2,1)S(1)}, bf16[4,64,512]{2,1,0:T(8,128)(2,1)S(1)}, u32[]{:S(2)}, u32[]{:S(2)}) collective-permute-start(bf16[4,64,512]{2,1,0:T(8,128)(2,1)S(1)} %get-tuple-element.41), channel_id=1, source_target_pairs={{0,16},{4,12},{8,24},{12,4},{16,0},{20,28},{24,8},{28,20},{1,17},{... | collective-permute-start | bytes 786440 | tf_op jit(solution)/shard_map/ppermute | solution.py:52
  58.2 7.7 %collective-permute-start.15 = (bf16[64,512]{1,0:T(8,128)(2,1)S(1)}, bf16[64,512]{1,0:T(8,128)(2,1)S(1)}, u32[]{:S(2)}, u32[]{:S(2)}) collective-permute-start(bf16[64,512]{1,0:T(8,128)(2,1)S(1)} %get-tuple-element.83), channel_id=1, source_target_pairs={{0,1},{1,2},{2,3},{3,0},{4,5},{5,6},{6,7},{7,4},{8,9},{9,10},{10,1... | collective-permute-start | bytes 196616 | tf_op jit(solution)/shard_map/ppermute | solution.py:107
  60.3 5.6 %collective-permute-start.16 = (bf16[64,512]{1,0:T(8,128)(2,1)S(1)}, bf16[64,512]{1,0:T(8,128)(2,1)S(1)}, u32[]{:S(2)}, u32[]{:S(2)}) collective-permute-start(bf16[64,512]{1,0:T(8,128)(2,1)S(1)} %get-tuple-element.82), channel_id=1, source_target_pairs={{0,2},{1,3},{2,0},{3,1},{4,6},{5,7},{6,4},{7,5},{8,10},{9,11},{10,... | collective-permute-start | bytes 196616 | tf_op jit(solution)/shard_map/ppermute | solution.py:107
  62.9 4.3 %collective-permute-start.17 = (bf16[64,512]{1,0:T(8,128)(2,1)S(1)}, bf16[64,512]{1,0:T(8,128)(2,1)S(1)}, u32[]{:S(2)}, u32[]{:S(2)}) collective-permute-start(bf16[64,512]{1,0:T(8,128)(2,1)S(1)} %get-tuple-element.81), channel_id=1, source_target_pairs={{0,3},{1,0},{2,1},{3,2},{4,7},{5,4},{6,5},{7,6},{8,11},{9,8},{10,9... | collective-permute-start | bytes 196616 | tf_op jit(solution)/shard_map/ppermute | solution.py:107
  64.3 7.8 %collective-permute-start.14 = (bf16[4,64,512]{2,1,0:T(8,128)(2,1)S(1)}, bf16[4,64,512]{2,1,0:T(8,128)(2,1)S(1)}, u32[]{:S(2)}, u32[]{:S(2)}) collective-permute-start(bf16[4,64,512]{2,1,0:T(8,128)(2,1)S(1)} %add_terms.11.refs_4_), channel_id=1, source_target_pairs={{0,8},{4,20},{8,0},{12,28},{16,24},{20,4},{24,16},{28,12},{1,9},{5... | collective-permute-start | bytes 786440 | tf_op jit(solution)/shard_map/ppermute | solution.py:52
  67.2 10.0 %collective-permute-start.24 = (bf16[4,64,512]{2,1,0:T(8,128)(2,1)S(1)}, bf16[4,64,512]{2,1,0:T(8,128)(2,1)S(1)}, u32[]{:S(2)}, u32[]{:S(2)}) collective-permute-start(bf16[4,64,512]{2,1,0:T(8,128)(2,1)S(1)} %stack_planes.6.refs_3_.refs_0_), channel_id=1, source_target_pairs={{0,8},{4,20},{8,0},{12,28},{16,24},{20,4},{24,16},{28,12},{1,9},{5... | collective-permute-start | bytes 786440 | tf_op jit(solution)/shard_map/ppermute | solution.py:52
  68.7 16.3 %collective-permute-start.25 = (bf16[4,64,512]{2,1,0:T(8,128)(2,1)S(1)}, bf16[4,64,512]{2,1,0:T(8,128)(2,1)S(1)}, u32[]{:S(2)}, u32[]{:S(2)}) collective-permute-start(bf16[4,64,512]{2,1,0:T(8,128)(2,1)S(1)} %stack_planes.6.refs_3_.refs_0_), channel_id=1, source_target_pairs={{0,16},{4,12},{8,24},{12,4},{16,0},{20,28},{24,8},{28,20},{1,17},{... | collective-permute-start | bytes 786440 | tf_op jit(solution)/shard_map/ppermute | solution.py:52
  77.2 7.8 %collective-permute-start.26 = (bf16[4,64,512]{2,1,0:T(8,128)(2,1)S(1)}, bf16[4,64,512]{2,1,0:T(8,128)(2,1)S(1)}, u32[]{:S(2)}, u32[]{:S(2)}) collective-permute-start(bf16[4,64,512]{2,1,0:T(8,128)(2,1)S(1)} %collective-permute-done.24.refs_1_), channel_id=1, source_target_pairs={{0,16},{4,12},{8,24},{12,4},{16,0},{20,28},{24,8},{28,20},{1,17},{... | collective-permute-start | bytes 786440 | tf_op jit(solution)/shard_map/ppermute | solution.py:52
  77.4 6.1 %collective-permute-start.18 = (bf16[64,512]{1,0:T(8,128)(2,1)S(1)}, bf16[64,512]{1,0:T(8,128)(2,1)S(1)}, u32[]{:S(2)}, u32[]{:S(2)}) collective-permute-start(bf16[64,512]{1,0:T(8,128)(2,1)S(1)} %get-tuple-element.79), channel_id=1, source_target_pairs={{0,1},{1,2},{2,3},{3,0},{4,5},{5,6},{6,7},{7,4},{8,9},{9,10},{10,1... | collective-permute-start | bytes 196616 | tf_op jit(solution)/shard_map/ppermute | solution.py:107
  79.1 5.2 %collective-permute-start.19 = (bf16[64,512]{1,0:T(8,128)(2,1)S(1)}, bf16[64,512]{1,0:T(8,128)(2,1)S(1)}, u32[]{:S(2)}, u32[]{:S(2)}) collective-permute-start(bf16[64,512]{1,0:T(8,128)(2,1)S(1)} %get-tuple-element.78), channel_id=1, source_target_pairs={{0,2},{1,3},{2,0},{3,1},{4,6},{5,7},{6,4},{7,5},{8,10},{9,11},{10,... | collective-permute-start | bytes 196616 | tf_op jit(solution)/shard_map/ppermute | solution.py:107
  80.5 4.4 %collective-permute-start.20 = (bf16[64,512]{1,0:T(8,128)(2,1)S(1)}, bf16[64,512]{1,0:T(8,128)(2,1)S(1)}, u32[]{:S(2)}, u32[]{:S(2)}) collective-permute-start(bf16[64,512]{1,0:T(8,128)(2,1)S(1)} %get-tuple-element.77), channel_id=1, source_target_pairs={{0,3},{1,0},{2,1},{3,2},{4,7},{5,4},{6,5},{7,6},{8,11},{9,8},{10,9... | collective-permute-start | bytes 196616 | tf_op jit(solution)/shard_map/ppermute | solution.py:107
  85.0 8.5 %slice-start = ((s8[8388608]{0:T(1024)(128)(4,1)}), s8[4194304]{0:T(1024)(128)(4,1)S(1)}, s32[]{:S(2)}) async-start(s8[8388608]{0:T(1024)(128)(4,1)} %bitcast.36), calls=%async_computation | async-start | bytes 8388608
  85.1 3.6 %collective-permute-start.27 = (bf16[4,4,64,512]{3,2,1,0:T(8,128)(2,1)S(1)}, bf16[4,4,64,512]{3,2,1,0:T(8,128)(2,1)S(1)}, u32[]{:S(2)}, u32[]{:S(2)}) collective-permute-start(bf16[4,4,64,512]{3,2,1,0:T(8,128)(2,1)S(1)} %stack_planes.8.refs_0_.refs_4_), channel_id=1, source_target_pairs={{0,4},{4,0},{8,12},{12,8},{16,20},{20,16},{24,28},{28,24},{1,5},{5... | collective-permute-start | bytes 3145736 | tf_op jit(solution)/shard_map/ppermute | solution.py:462
  85.2 10.2 %collective-permute-start.21 = (bf16[4,64,512]{2,1,0:T(8,128)(2,1)S(1)}, bf16[4,64,512]{2,1,0:T(8,128)(2,1)S(1)}, u32[]{:S(2)}, u32[]{:S(2)}) collective-permute-start(bf16[4,64,512]{2,1,0:T(8,128)(2,1)S(1)} %stack_planes.7.refs_4_.refs_0_), channel_id=1, source_target_pairs={{0,8},{4,20},{8,0},{12,28},{16,24},{20,4},{24,16},{28,12},{1,9},{5... | collective-permute-start | bytes 786440 | tf_op jit(solution)/shard_map/ppermute | solution.py:99
  86.9 8.5 %collective-permute-start.22 = (bf16[4,64,512]{2,1,0:T(8,128)(2,1)S(1)}, bf16[4,64,512]{2,1,0:T(8,128)(2,1)S(1)}, u32[]{:S(2)}, u32[]{:S(2)}) collective-permute-start(bf16[4,64,512]{2,1,0:T(8,128)(2,1)S(1)} %stack_planes.7.refs_4_.refs_0_), channel_id=1, source_target_pairs={{0,16},{4,12},{8,24},{12,4},{16,0},{20,28},{24,8},{28,20},{1,17},{... | collective-permute-start | bytes 786440 | tf_op jit(solution)/shard_map/ppermute | solution.py:99
  88.3 12.4 %collective-permute-start.23 = (bf16[4,64,512]{2,1,0:T(8,128)(2,1)S(1)}, bf16[4,64,512]{2,1,0:T(8,128)(2,1)S(1)}, u32[]{:S(2)}, u32[]{:S(2)}) collective-permute-start(bf16[4,64,512]{2,1,0:T(8,128)(2,1)S(1)} %stack_planes.7.refs_4_.refs_0_), channel_id=1, source_target_pairs={{0,24},{4,28},{8,16},{12,20},{16,8},{20,12},{24,0},{28,4},{1,25},{... | collective-permute-start | bytes 786440 | tf_op jit(solution)/shard_map/ppermute | solution.py:99
  88.8 4.7 %slice-start.1 = ((s8[8388608]{0:T(1024)(128)(4,1)}), s8[4194304]{0:T(1024)(128)(4,1)S(1)}, s32[]{:S(2)}) async-start(s8[8388608]{0:T(1024)(128)(4,1)} %bitcast.36), calls=%async_computation.1 | async-start | bytes 8388608
  100.8 6.4 %collective-permute-start.28 = (bf16[4,4,64,512]{3,2,1,0:T(8,128)(2,1)S(1)}, bf16[4,4,64,512]{3,2,1,0:T(8,128)(2,1)S(1)}, u32[]{:S(2)}, u32[]{:S(2)}) collective-permute-start(bf16[4,4,64,512]{3,2,1,0:T(8,128)(2,1)S(1)} %stack_planes.9.refs_4_.refs_0_), channel_id=1, source_target_pairs={{0,4},{4,0},{8,12},{12,8},{16,20},{20,16},{24,28},{28,24},{1,5},{5... | collective-permute-start | bytes 3145736 | tf_op jit(solution)/shard_map/ppermute | solution.py:462
  100.8 3.8 %collective-permute-start.31 = (bf16[4,64,512]{2,1,0:T(8,128)(2,1)S(1)}, bf16[4,64,512]{2,1,0:T(8,128)(2,1)S(1)}, u32[]{:S(2)}, u32[]{:S(2)}) collective-permute-start(bf16[4,64,512]{2,1,0:T(8,128)(2,1)S(1)} %get-tuple-element.43.refs_4_), channel_id=1, source_target_pairs={{0,4},{4,0},{8,12},{12,8},{16,20},{20,16},{24,28},{28,24},{1,5},{5... | collective-permute-start | bytes 786440 | tf_op jit(solution)/shard_map/ppermute | solution.py:462
  101.3 2.9 %collective-permute-start.29 = (bf16[4,64,512]{2,1,0:T(8,128)(2,1)S(1)}, bf16[4,64,512]{2,1,0:T(8,128)(2,1)S(1)}, u32[]{:S(2)}, u32[]{:S(2)}) collective-permute-start(bf16[4,64,512]{2,1,0:T(8,128)(2,1)S(1)} %get-tuple-element.45), channel_id=1, source_target_pairs={{0,4},{4,0},{8,12},{12,8},{16,20},{20,16},{24,28},{28,24},{1,5},{5... | collective-permute-start | bytes 786440 | tf_op jit(solution)/shard_map/ppermute | solution.py:462
  101.4 3.2 %collective-permute-start.30 = (bf16[4,64,512]{2,1,0:T(8,128)(2,1)S(1)}, bf16[4,64,512]{2,1,0:T(8,128)(2,1)S(1)}, u32[]{:S(2)}, u32[]{:S(2)}) collective-permute-start(bf16[4,64,512]{2,1,0:T(8,128)(2,1)S(1)} %get-tuple-element.47), channel_id=1, source_target_pairs={{0,4},{4,0},{8,12},{12,8},{16,20},{20,16},{24,28},{28,24},{1,5},{5... | collective-permute-start | bytes 786440 | tf_op jit(solution)/shard_map/ppermute | solution.py:462
  101.8 3.1 %collective-permute-start.32 = (bf16[4,64,512]{2,1,0:T(8,128)(2,1)S(1)}, bf16[4,64,512]{2,1,0:T(8,128)(2,1)S(1)}, u32[]{:S(2)}, u32[]{:S(2)}) collective-permute-start(bf16[4,64,512]{2,1,0:T(8,128)(2,1)S(1)} %get-tuple-element.49), channel_id=1, source_target_pairs={{0,4},{4,0},{8,12},{12,8},{16,20},{20,16},{24,28},{28,24},{1,5},{5... | collective-permute-start | bytes 786440 | tf_op jit(solution)/shard_map/ppermute | solution.py:462
  105.1 9.2 %collective-permute-start.33 = (bf16[4,64,512]{2,1,0:T(8,128)(2,1)S(1)}, bf16[4,64,512]{2,1,0:T(8,128)(2,1)S(1)}, u32[]{:S(2)}, u32[]{:S(2)}) collective-permute-start(bf16[4,64,512]{2,1,0:T(8,128)(2,1)S(1)} %get-tuple-element.52), channel_id=1, source_target_pairs={{0,16},{4,12},{8,24},{12,4},{16,0},{20,28},{24,8},{28,20},{1,17},{... | collective-permute-start | bytes 786440 | tf_op jit(solution)/shard_map/ppermute | solution.py:52
  105.6 9.2 %collective-permute-start.34 = (bf16[4,64,512]{2,1,0:T(8,128)(2,1)S(1)}, bf16[4,64,512]{2,1,0:T(8,128)(2,1)S(1)}, u32[]{:S(2)}, u32[]{:S(2)}) collective-permute-start(bf16[4,64,512]{2,1,0:T(8,128)(2,1)S(1)} %get-tuple-element.50.refs_4_), channel_id=1, source_target_pairs={{0,16},{4,12},{8,24},{12,4},{16,0},{20,28},{24,8},{28,20},{1,17},{... | collective-permute-start | bytes 786440 | tf_op jit(solution)/shard_map/ppermute | solution.py:52
  113.7 4.7 %collective-permute-start.35 = (bf16[4,64,512]{2,1,0:T(8,128)(2,1)S(1)}, bf16[4,64,512]{2,1,0:T(8,128)(2,1)S(1)}, u32[]{:S(2)}, u32[]{:S(2)}) collective-permute-start(bf16[4,64,512]{2,1,0:T(8,128)(2,1)S(1)} %get-tuple-element.53.refs_3_), channel_id=1, source_target_pairs={{0,4},{4,0},{8,12},{12,8},{16,20},{20,16},{24,28},{28,24},{1,5},{5... | collective-permute-start | bytes 786440 | tf_op jit(solution)/shard_map/ppermute | solution.py:462
  113.8 4.7 %collective-permute-start.36 = (bf16[4,64,512]{2,1,0:T(8,128)(2,1)S(1)}, bf16[4,64,512]{2,1,0:T(8,128)(2,1)S(1)}, u32[]{:S(2)}, u32[]{:S(2)}) collective-permute-start(bf16[4,64,512]{2,1,0:T(8,128)(2,1)S(1)} %get-tuple-element.56), channel_id=1, source_target_pairs={{0,4},{4,0},{8,12},{12,8},{16,20},{20,16},{24,28},{28,24},{1,5},{5... | collective-permute-start | bytes 786440 | tf_op jit(solution)/shard_map/ppermute | solution.py:462
  114.3 4.2 %collective-permute-start.37 = (bf16[4,64,512]{2,1,0:T(8,128)(2,1)S(1)}, bf16[4,64,512]{2,1,0:T(8,128)(2,1)S(1)}, u32[]{:S(2)}, u32[]{:S(2)}) collective-permute-start(bf16[4,64,512]{2,1,0:T(8,128)(2,1)S(1)} %get-tuple-element.58), channel_id=1, source_target_pairs={{0,4},{4,0},{8,12},{12,8},{16,20},{20,16},{24,28},{28,24},{1,5},{5... | collective-permute-start | bytes 786440 | tf_op jit(solution)/shard_map/ppermute | solution.py:462
  114.4 4.1 %collective-permute-start.38 = (bf16[4,64,512]{2,1,0:T(8,128)(2,1)S(1)}, bf16[4,64,512]{2,1,0:T(8,128)(2,1)S(1)}, u32[]{:S(2)}, u32[]{:S(2)}) collective-permute-start(bf16[4,64,512]{2,1,0:T(8,128)(2,1)S(1)} %get-tuple-element.60), channel_id=1, source_target_pairs={{0,4},{4,0},{8,12},{12,8},{16,20},{20,16},{24,28},{28,24},{1,5},{5... | collective-permute-start | bytes 786440 | tf_op jit(solution)/shard_map/ppermute | solution.py:462
  114.9 7.4 %collective-permute-start.42 = (bf16[4,64,512]{2,1,0:T(8,128)(2,1)S(1)}, bf16[4,64,512]{2,1,0:T(8,128)(2,1)S(1)}, u32[]{:S(2)}, u32[]{:S(2)}) collective-permute-start(bf16[4,64,512]{2,1,0:T(8,128)(2,1)S(1)} %add_terms.14.refs_4_), channel_id=1, source_target_pairs={{0,8},{4,20},{8,0},{12,28},{16,24},{20,4},{24,16},{28,12},{1,9},{5... | collective-permute-start | bytes 786440 | tf_op jit(solution)/shard_map/ppermute | solution.py:52
  118.7 9.2 %collective-permute-start.39 = (bf16[4,64,512]{2,1,0:T(8,128)(2,1)S(1)}, bf16[4,64,512]{2,1,0:T(8,128)(2,1)S(1)}, u32[]{:S(2)}, u32[]{:S(2)}) collective-permute-start(bf16[4,64,512]{2,1,0:T(8,128)(2,1)S(1)} %get-tuple-element.62), channel_id=1, source_target_pairs={{0,8},{4,20},{8,0},{12,28},{16,24},{20,4},{24,16},{28,12},{1,9},{5... | collective-permute-start | bytes 786440 | tf_op jit(solution)/shard_map/ppermute | solution.py:99
  119.2 11.4 %collective-permute-start.40 = (bf16[4,64,512]{2,1,0:T(8,128)(2,1)S(1)}, bf16[4,64,512]{2,1,0:T(8,128)(2,1)S(1)}, u32[]{:S(2)}, u32[]{:S(2)}) collective-permute-start(bf16[4,64,512]{2,1,0:T(8,128)(2,1)S(1)} %get-tuple-element.63), channel_id=1, source_target_pairs={{0,16},{4,12},{8,24},{12,4},{16,0},{20,28},{24,8},{28,20},{1,17},{... | collective-permute-start | bytes 786440 | tf_op jit(solution)/shard_map/ppermute | solution.py:99
  119.5 12.8 %collective-permute-start.41 = (bf16[4,64,512]{2,1,0:T(8,128)(2,1)S(1)}, bf16[4,64,512]{2,1,0:T(8,128)(2,1)S(1)}, u32[]{:S(2)}, u32[]{:S(2)}) collective-permute-start(bf16[4,64,512]{2,1,0:T(8,128)(2,1)S(1)} %get-tuple-element.64), channel_id=1, source_target_pairs={{0,24},{4,28},{8,16},{12,20},{16,8},{20,12},{24,0},{28,4},{1,25},{... | collective-permute-start | bytes 786440 | tf_op jit(solution)/shard_map/ppermute | solution.py:99
  122.5 14.8 %collective-permute-start.46 = (bf16[64,512]{1,0:T(8,128)(2,1)S(1)}, bf16[64,512]{1,0:T(8,128)(2,1)S(1)}, u32[]{:S(2)}, u32[]{:S(2)}) collective-permute-start(bf16[64,512]{1,0:T(8,128)(2,1)S(1)} %get-tuple-element.71), channel_id=1, source_target_pairs={{0,1},{1,2},{2,3},{3,0},{4,5},{5,6},{6,7},{7,4},{8,9},{9,10},{10,1... | collective-permute-start | bytes 196616 | tf_op jit(solution)/shard_map/ppermute | solution.py:107
  123.9 13.5 %collective-permute-start.47 = (bf16[64,512]{1,0:T(8,128)(2,1)S(1)}, bf16[64,512]{1,0:T(8,128)(2,1)S(1)}, u32[]{:S(2)}, u32[]{:S(2)}) collective-permute-start(bf16[64,512]{1,0:T(8,128)(2,1)S(1)} %get-tuple-element.70), channel_id=1, source_target_pairs={{0,2},{1,3},{2,0},{3,1},{4,6},{5,7},{6,4},{7,5},{8,10},{9,11},{10,... | collective-permute-start | bytes 196616 | tf_op jit(solution)/shard_map/ppermute | solution.py:107
  128.0 9.5 %collective-permute-start.48 = (bf16[64,512]{1,0:T(8,128)(2,1)S(1)}, bf16[64,512]{1,0:T(8,128)(2,1)S(1)}, u32[]{:S(2)}, u32[]{:S(2)}) collective-permute-start(bf16[64,512]{1,0:T(8,128)(2,1)S(1)} %get-tuple-element.69), channel_id=1, source_target_pairs={{0,3},{1,0},{2,1},{3,2},{4,7},{5,4},{6,5},{7,6},{8,11},{9,8},{10,9... | collective-permute-start | bytes 196616 | tf_op jit(solution)/shard_map/ppermute | solution.py:107
  132.5 7.0 %collective-permute-start.43 = (bf16[64,512]{1,0:T(8,128)(2,1)S(1)}, bf16[64,512]{1,0:T(8,128)(2,1)S(1)}, u32[]{:S(2)}, u32[]{:S(2)}) collective-permute-start(bf16[64,512]{1,0:T(8,128)(2,1)S(1)} %get-tuple-element.75), channel_id=1, source_target_pairs={{0,1},{1,2},{2,3},{3,0},{4,5},{5,6},{6,7},{7,4},{8,9},{9,10},{10,1... | collective-permute-start | bytes 196616 | tf_op jit(solution)/shard_map/ppermute | solution.py:107
  134.1 7.2 %collective-permute-start.44 = (bf16[64,512]{1,0:T(8,128)(2,1)S(1)}, bf16[64,512]{1,0:T(8,128)(2,1)S(1)}, u32[]{:S(2)}, u32[]{:S(2)}) collective-permute-start(bf16[64,512]{1,0:T(8,128)(2,1)S(1)} %get-tuple-element.74), channel_id=1, source_target_pairs={{0,2},{1,3},{2,0},{3,1},{4,6},{5,7},{6,4},{7,5},{8,10},{9,11},{10,... | collective-permute-start | bytes 196616 | tf_op jit(solution)/shard_map/ppermute | solution.py:107
  137.2 4.6 %collective-permute-start.45 = (bf16[64,512]{1,0:T(8,128)(2,1)S(1)}, bf16[64,512]{1,0:T(8,128)(2,1)S(1)}, u32[]{:S(2)}, u32[]{:S(2)}) collective-permute-start(bf16[64,512]{1,0:T(8,128)(2,1)S(1)} %get-tuple-element.73), channel_id=1, source_target_pairs={{0,3},{1,0},{2,1},{3,2},{4,7},{5,4},{6,5},{7,6},{8,11},{9,8},{10,9... | collective-permute-start | bytes 196616 | tf_op jit(solution)/shard_map/ppermute | solution.py:107
  137.5 7.3 %collective-permute-start.52 = (bf16[4,64,512]{2,1,0:T(8,128)(2,1)S(1)}, bf16[4,64,512]{2,1,0:T(8,128)(2,1)S(1)}, u32[]{:S(2)}, u32[]{:S(2)}) collective-permute-start(bf16[4,64,512]{2,1,0:T(8,128)(2,1)S(1)} %stack_planes.10.refs_4_.refs_1_), channel_id=1, source_target_pairs={{0,8},{4,20},{8,0},{12,28},{16,24},{20,4},{24,16},{28,12},{1,9},{5... | collective-permute-start | bytes 786440 | tf_op jit(solution)/shard_map/ppermute | solution.py:52
  141.8 9.4 %collective-permute-start.49 = (bf16[4,64,512]{2,1,0:T(8,128)(2,1)S(1)}, bf16[4,64,512]{2,1,0:T(8,128)(2,1)S(1)}, u32[]{:S(2)}, u32[]{:S(2)}) collective-permute-start(bf16[4,64,512]{2,1,0:T(8,128)(2,1)S(1)} %stack_planes.11.refs_1_), channel_id=1, source_target_pairs={{0,8},{4,20},{8,0},{12,28},{16,24},{20,4},{24,16},{28,12},{1,9},{5... | collective-permute-start | bytes 786440 | tf_op jit(solution)/shard_map/ppermute | solution.py:52
  144.1 7.8 %collective-permute-start.53 = (bf16[4,64,512]{2,1,0:T(8,128)(2,1)S(1)}, bf16[4,64,512]{2,1,0:T(8,128)(2,1)S(1)}, u32[]{:S(2)}, u32[]{:S(2)}) collective-permute-start(bf16[4,64,512]{2,1,0:T(8,128)(2,1)S(1)} %stack_planes.10.refs_4_.refs_1_), channel_id=1, source_target_pairs={{0,16},{4,12},{8,24},{12,4},{16,0},{20,28},{24,8},{28,20},{1,17},{... | collective-permute-start | bytes 786440 | tf_op jit(solution)/shard_map/ppermute | solution.py:52
  144.8 8.5 %collective-permute-start.54 = (bf16[4,64,512]{2,1,0:T(8,128)(2,1)S(1)}, bf16[4,64,512]{2,1,0:T(8,128)(2,1)S(1)}, u32[]{:S(2)}, u32[]{:S(2)}) collective-permute-start(bf16[4,64,512]{2,1,0:T(8,128)(2,1)S(1)} %collective-permute-done.52.refs_2_), channel_id=1, source_target_pairs={{0,16},{4,12},{8,24},{12,4},{16,0},{20,28},{24,8},{28,20},{1,17},{... | collective-permute-start | bytes 786440 | tf_op jit(solution)/shard_map/ppermute | solution.py:52
  146.2 10.0 %collective-permute-start.50 = (bf16[4,64,512]{2,1,0:T(8,128)(2,1)S(1)}, bf16[4,64,512]{2,1,0:T(8,128)(2,1)S(1)}, u32[]{:S(2)}, u32[]{:S(2)}) collective-permute-start(bf16[4,64,512]{2,1,0:T(8,128)(2,1)S(1)} %stack_planes.11.refs_1_), channel_id=1, source_target_pairs={{0,16},{4,12},{8,24},{12,4},{16,0},{20,28},{24,8},{28,20},{1,17},{... | collective-permute-start | bytes 786440 | tf_op jit(solution)/shard_map/ppermute | solution.py:52
  151.2 7.7 %collective-permute-start.51 = (bf16[4,64,512]{2,1,0:T(8,128)(2,1)S(1)}, bf16[4,64,512]{2,1,0:T(8,128)(2,1)S(1)}, u32[]{:S(2)}, u32[]{:S(2)}) collective-permute-start(bf16[4,64,512]{2,1,0:T(8,128)(2,1)S(1)} %collective-permute-done.49.refs_2_), channel_id=1, source_target_pairs={{0,16},{4,12},{8,24},{12,4},{16,0},{20,28},{24,8},{28,20},{1,17},{... | collective-permute-start | bytes 786440 | tf_op jit(solution)/shard_map/ppermute | solution.py:52
  159.9 2.0 %collective-permute-start.55 = (bf16[8,64,512]{2,1,0:T(8,128)(2,1)S(1)}, bf16[8,64,512]{2,1,0:T(8,128)(2,1)S(1)}, u32[]{:S(2)}, u32[]{:S(2)}) collective-permute-start(bf16[8,64,512]{2,1,0:T(8,128)(2,1)S(1)} %add_expert_rows.5), channel_id=1, source_target_pairs={{0,4},{4,0},{8,12},{12,8},{16,20},{20,16},{24,28},{28,24},{1,5},{5... | collective-permute-start | bytes 1572872 | tf_op jit(solution)/shard_map/ppermute | solution.py:462
  (2 other events, 9.4 us)

commit v9 on v8

--- a/solution.py
+++ b/solution.py
@@ -198,27 +198,35 @@
         return index, lax.div(owner, 2) == place.chip
 
 
-def project_kernel(make_place, parts, n_w, n_res, *refs):
+def project_kernel(make_place, parts, ahead, n_w, n_res, *refs):
     context, other = refs[:2]
     weights = refs[2 : 2 + n_w]
     extra = refs[2 + n_w : 2 + n_w + n_res]
-    out, w_all, c_own, c_other, sems = refs[-5:]
+    outs, (w_all, c_own, c_other, sems) = refs[2 + n_w + n_res : -4], refs[-4:]
     depth = weights[0].shape[0]
     place = make_place()
+
+    def fetch(r, src, dst, at, sem):
+        copies = []
+        for s in range(2):
+            column = (place.chip_at(r) * 2 + (place.side ^ s)) * depth
+            column = pl.ds(pl.multiple_of(column, depth), depth)
+            n = at + s
+            copy = pltpu.make_async_copy(
+                src.at[:, column], dst.at[:, n * depth : (n + 1) * depth], sem.at[n]
+            )
+            copy.start()
+            copies.append(copy)
+        return copies
+
     copies = []
     for i, (src, dst) in enumerate(((context, c_own), (other, c_other))):
         for j, r in enumerate(parts):
-            for s in range(2):
-                at = (place.chip_at(r) * 2 + (place.side ^ s)) * depth
-                at = pl.ds(pl.multiple_of(at, depth), depth)
-                n = 2 * j + s
-                copies.append(
-                    pltpu.make_async_copy(
-                        src.at[:, at], dst.at[:, n * depth : (n + 1) * depth], sems.at[i, n]
-                    )
-                )
-    for c in copies:
-        c.start()
+            copies += fetch(r, src, dst, 2 * j, sems.at[i])
+    later = []
+    if ahead is not None:
+        for i, src in enumerate((context, other)):
+            later += fetch(ahead, src, outs[1].at[i], 0, sems.at[2 + i])
     for i, w in enumerate(weights):
         w_all[i * depth : (i + 1) * depth, :] = w[...]
     for i, c in enumerate((c_own, c_other)):
@@ -227,29 +235,55 @@
         value = jnp.dot(c[...], w_all[...], preferred_element_type=jnp.float32)
         if n_res > 0:
             value = value + extra[0][i]
-        if n_res > 1:
-            value = value + extra[1 + i][...].astype(jnp.float32)
-        out[i] = value.astype(out.dtype)
-
-
-def project(make_place, parts, own, other, weights, extra):
+        outs[0][i] = value
+    for copy in later:
+        copy.wait()
+
+
+def project(make_place, parts, ahead, own, other, weights, extra):
     rows = own.shape[0]
     depth, half = weights[0].shape
     k = depth * len(weights)
-    return call(
-        lambda *refs: project_kernel(make_place, parts, len(weights), len(extra), *refs),
-        jax.ShapeDtypeStruct((2, rows, half), jnp.bfloat16 if len(extra) > 1 else jnp.float32),
+    shapes = [jax.ShapeDtypeStruct((2, rows, half), jnp.float32)]
+    if ahead is not None:
+        shapes.append(jax.ShapeDtypeStruct((2, rows, 2 * depth), own.dtype))
+    return call(
+        lambda *refs: project_kernel(make_place, parts, ahead, len(weights), len(extra), *refs),
+        shapes,
         [ANY, ANY] + [VMEM] * (len(weights) + len(extra)),
-        VMEM,
+        [VMEM] * len(shapes),
         "project",
         12,
         scratch_shapes=[
             pltpu.VMEM((k, half), jnp.bfloat16),
             pltpu.VMEM((rows, k), jnp.bfloat16),
             pltpu.VMEM((rows, k), jnp.bfloat16),
-            pltpu.SemaphoreType.DMA((2, len(weights))),
+            pltpu.SemaphoreType.DMA((4, len(weights))),
         ],
     )(own, other, *weights, *extra)
+
+
+def project_last_kernel(columns, total, own, other, *refs):
+    weights, out, w_all = refs[:-2], refs[-2], refs[-1]
+    depth = weights[0].shape[0]
+    for i, w in enumerate(weights):
+        w_all[i * depth : (i + 1) * depth, :] = w[...]
+    for i, res in enumerate((own, other)):
+        value = jnp.dot(columns[i], w_all[...], preferred_element_type=jnp.float32)
+        out[i] = (value + total[i] + res[...].astype(jnp.float32)).astype(out.dtype)
+
+
+def project_last(columns, total, own, other, weights):
+    depth, half = weights[0].shape
+    return call(
+        project_last_kernel,
+        jax.ShapeDtypeStruct(total.shape, jnp.bfloat16),
+        [VMEM] * (4 + len(weights)),
+        VMEM,
+        "project_last",
+        12,
+        scratch_shapes=[pltpu.VMEM((depth * len(weights), half), jnp.bfloat16)],
+    )(columns, total, own, other, *weights)
 
 
 def pick_kernel(make_place, layout, n_chip, chosen, att_ref, *refs):
@@ -481,14 +515,13 @@
     def make_place():
         return Place(n_bits, n_expert)
 
-    bounds = [0, top, n_chip - 1, n_chip]
-    total = ()
-    for lo, hi in zip(bounds[:-1], bounds[1:]):
-        if hi == n_chip:
-            total = total + (residual_own, residual_other)
-        part = pieces[2 * lo : 2 * hi]
-        total = (project(make_place, plain[lo:hi], context, context_other, part, total),)
-    attended = total[0]
+    last = n_chip - 1
+    sides = (context, context_other)
+    (total,) = project(make_place, plain[:top], None, *sides, pieces[: 2 * top], ())
+    total, columns = project(
+        make_place, plain[top:last], last, *sides, pieces[2 * top : 2 * last], (total,)
+    )
+    attended = project_last(columns, total, residual_own, residual_other, pieces[2 * last :])
 
     layouts = [Layout(group, n_chip, local_blocks) for group in range(GROUPS)]
     grains = attended.reshape(-1, share, half)

time: 163 us -> 162 us (level)
  no operation moved by 1% of the time
where the time goes in v9:
time: 162 us
  starting transfers between devices  66.4 us (41%)
  waiting for transfers between devices  61.4 us (38%)
  Pallas kernels  30.7 us (19%)
  local copies, waits for them, and re-layouts  2.82 us (2%)
    ppermute x24, waiting for transfers between devices, exchange(): return lax.ppermute(value, 'dp', step_pairs(n_dp, step))  40.9 us
    ppermute x24, starting transfers between devices, exchange(): return lax.ppermute(value, 'dp', step_pairs(n_dp, step))  33.6 us
    ppermute x12, starting transfers between devices, swap_planes(): out.append(lax.ppermute(parts[k], 'expert', pairs))  22.6 us
    ppermute x6, waiting for transfers between devices, direct(): out.append(lax.ppermute(value, 'dp', pairs) if r else value)  9.46 us
    pallas_call x2, Pallas kernels, hidden_units(): call(lambda *refs: hidden_kernel(make_place, reverse, *refs), jax.ShapeDt...  9.29 us
    pallas_call x4, Pallas kernels, down(): call(lambda *refs: down_kernel(make_place, layout, order, s, *refs), [jax...  7.29 us
    ppermute x6, starting transfers between devices, direct(): out.append(lax.ppermute(value, 'dp', pairs) if r else value)  7.11 us
    ppermute x12, waiting for transfers between devices, swap_planes(): out.append(lax.ppermute(parts[k], 'expert', pairs))  6.08 us
  transfers between devices with their start and end apart: 56, of which 26 were waited for; matrix products, arithmetic and copies ran while one was open for 2% of the time, Pallas kernels for 16%

profile of v9, /device:TPU:0, one launch (start us, length us, event | category | flops | bytes accessed | tf_op | source)
XLA Modules:
  0.0 161.9 jit_solution(7113328306350385592)
XLA Ops:
  0.5 1.4 constant_dynamic-slice_fusion.2
  2.0 2.9 %collective-permute-start.4 = (bf16[512,512]{1,0:T(8,128)(2,1)S(1)}, bf16[512,512]{1,0:T(8,128)(2,1)S(1)}, u32[]{:S(2)}, u32[]{:S(2)}) collective-permute-start(bf16[512,512]{1,0:T(8,128)(2,1)S(1)} %get-tuple-element.72.refs_2_), channel_id=1, source_target_pairs={{0,8},{4,20},{8,0},{12,28},{16,24},{20,4},{24,16},{28,12},{1,9},{5... | collective-permute-start | bytes 1572872 | tf_op jit(solution)/shard_map/ppermute | solution.py:52
  4.9 3.1 %collective-permute-done.2.refs_3_ = bf16[512,512]{1,0:T(8,128)(2,1)S(1)} collective-permute-done((bf16[512,512]{1,0:T(8,128)(2,1)S(1)}, bf16[512,512]{1,0:T(8,128)(2,1)S(1)}, u32[]{:S(2)}, u32[]{:S(2)}) %collective-permute-start.2) | collective-permute-done | bytes 524320 | tf_op jit(solution)/shard_map/ppermute | solution.py:496
  8.0 2.9 %collective-permute-start.5 = (bf16[512,512]{1,0:T(8,128)(2,1)S(1)}, bf16[512,512]{1,0:T(8,128)(2,1)S(1)}, u32[]{:S(2)}, u32[]{:S(2)}) collective-permute-start(bf16[512,512]{1,0:T(8,128)(2,1)S(1)} %collective-permute-done.2.refs_3_), channel_id=1, source_target_pairs={{0,8},{4,20},{8,0},{12,28},{16,24},{20,4},{24,16},{28,12},{1,9},{5... | collective-permute-start | bytes 1572872 | tf_op jit(solution)/shard_map/ppermute | solution.py:52
  10.8 1.5 collective-permute-start.1
  12.4 1.3 constant_dynamic-slice_fusion
  13.7 0.9 collective-permute-start.3
  14.6 8.2 %collective-permute-done.5.refs_5_ = bf16[512,512]{1,0:T(8,128)(2,1)S(1)} collective-permute-done((bf16[512,512]{1,0:T(8,128)(2,1)S(1)}, bf16[512,512]{1,0:T(8,128)(2,1)S(1)}, u32[]{:S(2)}, u32[]{:S(2)}) %collective-permute-start.5) | collective-permute-done | bytes 524320 | tf_op jit(solution)/shard_map/ppermute | solution.py:52
  22.8 3.0 %collective-permute-start.7 = (bf16[512,512]{1,0:T(8,128)(2,1)S(1)}, bf16[512,512]{1,0:T(8,128)(2,1)S(1)}, u32[]{:S(2)}, u32[]{:S(2)}) collective-permute-start(bf16[512,512]{1,0:T(8,128)(2,1)S(1)} %collective-permute-done.4.refs_4_), channel_id=1, source_target_pairs={{0,16},{4,12},{8,24},{12,4},{16,0},{20,28},{24,8},{28,20},{1,17},{... | collective-permute-start | bytes 1572872 | tf_op jit(solution)/shard_map/ppermute | solution.py:52
  25.9 3.4 %project.2.refs_4_ = f32[2,512,512]{2,1,0:T(8,128)S(1)} custom-call(bf16[512,4096]{1,0:T(8,128)(2,1)S(1)} %copy-done, bf16[512,4096]{1,0:T(8,128)(2,1)} %collective-permute-done.refs_1_, bf16[512,512]{1,0:T(8,128)(2,1)S(1)} %get-tuple-element.72.refs_2_, bf16[512,512]{1,0:T(8,128)(2,1)S(1)} %collective-permute-done.2.refs_3_, ...), custom_call_target="tpu_custom_call" | custom-call | tf_op jit(solution)/shard_map/project/pallas_call | solution.py:250
  29.4 2.4 %project.3 = (f32[2,512,512]{2,1,0:T(8,128)S(1)}, bf16[2,512,1024]{2,1,0:T(8,128)(2,1)S(1)}) custom-call(bf16[512,4096]{1,0:T(8,128)(2,1)S(1)} %copy-done, bf16[512,4096]{1,0:T(8,128)(2,1)} %collective-permute-done.refs_1_, bf16[512,512]{1,0:T(8,128)(2,1)S(1)} %collective-permute-done.1.refs_2_, bf16[512,512]{1,0:T(8,128)(2,1)S(1)} %collective-permute-done.3.refs_3_, ...), custom_call_target="tpu_custom_call" | custom-call | tf_op jit(solution)/shard_map/project/pallas_call | solution.py:250
  31.7 2.6 %collective-permute-done.7.refs_0_ = bf16[512,512]{1,0:T(8,128)(2,1)S(1)} collective-permute-done((bf16[512,512]{1,0:T(8,128)(2,1)S(1)}, bf16[512,512]{1,0:T(8,128)(2,1)S(1)}, u32[]{:S(2)}, u32[]{:S(2)}) %collective-permute-start.7) | collective-permute-done | bytes 524320 | tf_op jit(solution)/shard_map/ppermute | solution.py:52
  34.3 5.6 %collective-permute-done.8.refs_1_ = bf16[512,512]{1,0:T(8,128)(2,1)S(1)} collective-permute-done((bf16[512,512]{1,0:T(8,128)(2,1)S(1)}, bf16[512,512]{1,0:T(8,128)(2,1)S(1)}, u32[]{:S(2)}, u32[]{:S(2)}) %collective-permute-start.8) | collective-permute-done | bytes 524320 | tf_op jit(solution)/shard_map/ppermute | solution.py:52
  40.0 1.2 project_last.1
  42.0 1.8 %collective-permute-start.9 = (bf16[4,64,512]{2,1,0:T(8,128)(2,1)S(1)}, bf16[4,64,512]{2,1,0:T(8,128)(2,1)S(1)}, u32[]{:S(2)}, u32[]{:S(2)}) collective-permute-start(bf16[4,64,512]{2,1,0:T(8,128)(2,1)S(1)} %get-tuple-element.40), channel_id=1, source_target_pairs={{0,16},{4,12},{8,24},{12,4},{16,0},{20,28},{24,8},{28,20},{1,17},{... | collective-permute-start | bytes 786440 | tf_op jit(solution)/shard_map/ppermute | solution.py:52
  44.1 4.3 %collective-permute-done.9.refs_1_ = bf16[4,64,512]{2,1,0:T(8,128)(2,1)S(1)} collective-permute-done((bf16[4,64,512]{2,1,0:T(8,128)(2,1)S(1)}, bf16[4,64,512]{2,1,0:T(8,128)(2,1)S(1)}, u32[]{:S(2)}, u32[]{:S(2)}) %collective-permute-start.9) | collective-permute-done | bytes 262176 | tf_op jit(solution)/shard_map/ppermute | solution.py:52
  48.6 1.8 %collective-permute-start.13 = (bf16[4,64,512]{2,1,0:T(8,128)(2,1)S(1)}, bf16[4,64,512]{2,1,0:T(8,128)(2,1)S(1)}, u32[]{:S(2)}, u32[]{:S(2)}) collective-permute-start(bf16[4,64,512]{2,1,0:T(8,128)(2,1)S(1)} %add_terms.9.refs_2_), channel_id=1, source_target_pairs={{0,8},{4,20},{8,0},{12,28},{16,24},{20,4},{24,16},{28,12},{1,9},{5... | collective-permute-start | bytes 786440 | tf_op jit(solution)/shard_map/ppermute | solution.py:52
  50.3 0.8 pick_blocks.3
  51.2 1.6 collective-permute-start.10
  53.3 3.7 %collective-permute-done.13.refs_2_ = bf16[4,64,512]{2,1,0:T(8,128)(2,1)S(1)} collective-permute-done((bf16[4,64,512]{2,1,0:T(8,128)(2,1)S(1)}, bf16[4,64,512]{2,1,0:T(8,128)(2,1)S(1)}, u32[]{:S(2)}, u32[]{:S(2)}) %collective-permute-start.13) | collective-permute-done | bytes 262176 | tf_op jit(solution)/shard_map/ppermute | solution.py:52
  57.1 2.1 %collective-permute-start.15 = (bf16[64,512]{1,0:T(8,128)(2,1)S(1)}, bf16[64,512]{1,0:T(8,128)(2,1)S(1)}, u32[]{:S(2)}, u32[]{:S(2)}) collective-permute-start(bf16[64,512]{1,0:T(8,128)(2,1)S(1)} %get-tuple-element.87), channel_id=1, source_target_pairs={{0,1},{1,2},{2,3},{3,0},{4,5},{5,6},{6,7},{7,4},{8,9},{9,10},{10,1... | collective-permute-start | bytes 196616 | tf_op jit(solution)/shard_map/ppermute | solution.py:107
  59.2 2.6 %collective-permute-start.16 = (bf16[64,512]{1,0:T(8,128)(2,1)S(1)}, bf16[64,512]{1,0:T(8,128)(2,1)S(1)}, u32[]{:S(2)}, u32[]{:S(2)}) collective-permute-start(bf16[64,512]{1,0:T(8,128)(2,1)S(1)} %get-tuple-element.86), channel_id=1, source_target_pairs={{0,2},{1,3},{2,0},{3,1},{4,6},{5,7},{6,4},{7,5},{8,10},{9,11},{10,... | collective-permute-start | bytes 196616 | tf_op jit(solution)/shard_map/ppermute | solution.py:107
  61.8 1.3 collective-permute-start.17
  63.2 1.6 collective-permute-start.14
  64.7 1.3 collective-permute-done.17.refs_3_
  66.0 1.6 collective-permute-start.24
  67.6 2.1 %collective-permute-start.25 = (bf16[4,64,512]{2,1,0:T(8,128)(2,1)S(1)}, bf16[4,64,512]{2,1,0:T(8,128)(2,1)S(1)}, u32[]{:S(2)}, u32[]{:S(2)}) collective-permute-start(bf16[4,64,512]{2,1,0:T(8,128)(2,1)S(1)} %stack_planes.6.refs_3_.refs_0_), channel_id=1, source_target_pairs={{0,16},{4,12},{8,24},{12,4},{16,0},{20,28},{24,8},{28,20},{1,17},{... | collective-permute-start | bytes 786440 | tf_op jit(solution)/shard_map/ppermute | solution.py:52
  69.7 1.3 collective-permute-done.14.refs_2_
  71.1 4.9 %collective-permute-done.24.refs_1_ = bf16[4,64,512]{2,1,0:T(8,128)(2,1)S(1)} collective-permute-done((bf16[4,64,512]{2,1,0:T(8,128)(2,1)S(1)}, bf16[4,64,512]{2,1,0:T(8,128)(2,1)S(1)}, u32[]{:S(2)}, u32[]{:S(2)}) %collective-permute-start.24) | collective-permute-done | bytes 262176 | tf_op jit(solution)/shard_map/ppermute | solution.py:52
  76.4 1.7 %collective-permute-start.18 = (bf16[64,512]{1,0:T(8,128)(2,1)S(1)}, bf16[64,512]{1,0:T(8,128)(2,1)S(1)}, u32[]{:S(2)}, u32[]{:S(2)}) collective-permute-start(bf16[64,512]{1,0:T(8,128)(2,1)S(1)} %get-tuple-element.83), channel_id=1, source_target_pairs={{0,1},{1,2},{2,3},{3,0},{4,5},{5,6},{6,7},{7,4},{8,9},{9,10},{10,1... | collective-permute-start | bytes 196616 | tf_op jit(solution)/shard_map/ppermute | solution.py:107
  78.1 1.3 collective-permute-start.19
  79.4 2.6 %collective-permute-start.20 = (bf16[64,512]{1,0:T(8,128)(2,1)S(1)}, bf16[64,512]{1,0:T(8,128)(2,1)S(1)}, u32[]{:S(2)}, u32[]{:S(2)}) collective-permute-start(bf16[64,512]{1,0:T(8,128)(2,1)S(1)} %get-tuple-element.81), channel_id=1, source_target_pairs={{0,3},{1,0},{2,1},{3,2},{4,7},{5,4},{6,5},{7,6},{8,11},{9,8},{10,9... | collective-permute-start | bytes 196616 | tf_op jit(solution)/shard_map/ppermute | solution.py:107
  84.2 1.6 collective-permute-start.21
  85.8 1.4 collective-permute-start.22
  87.8 4.6 %expert_hidden.2.refs_1_.refs_4_ = bf16[256,1024]{1,0:T(8,128)(2,1)S(1)} custom-call(bf16[4,4,64,512]{3,2,1,0:T(8,128)(2,1)S(1)} %stack_planes.8.refs_0_.refs_4_, bf16[4,4,64,512]{3,2,1,0:T(8,128)(2,1)S(1)} %collective-permute-done.27.refs_1_, bf16[4096,1024]{1,0:T(8,128)(2,1)S(1)} %bitcast.44, bf16[4096,1024]{1,0:T(8,128)(2,1)S(1)} %bitcast.48, ...), custom_call_target="tpu_custom_call" | custom-call | tf_op jit(solution)/shard_map/expert_hidden/pallas_call | solution.py:388
  92.5 1.8 %expert_down.4 = (bf16[4,64,512]{2,1,0:T(8,128)(2,1)S(1)}, bf16[4,64,512]{2,1,0:T(8,128)(2,1)S(1)}, bf16[4,64,512]{2,1,0:T(8,128)(2,1)S(1)}, bf16[4,64,512]{2,1,0:T(8,128)(2,1)S(1)}) custom-call(s32[4]{0:T(128)S(1)} %copy-done.3, bf16[256,1024]{1,0:T(8,128)(2,1)S(1)} %expert_hidden.2.refs_1_.refs_4_, bf16[1024,4096]{1,0:T(8,128)(2,1)S(1)} %bitcast.38, ...), custom_call_target="tpu_custom_call" | custom-call | tf_op jit(solution)/shard_map/expert_down/pallas_call | solution.py:423
  94.4 5.3 %collective-permute-done.23.refs_3_ = bf16[4,64,512]{2,1,0:T(8,128)(2,1)S(1)} collective-permute-done((bf16[4,64,512]{2,1,0:T(8,128)(2,1)S(1)}, bf16[4,64,512]{2,1,0:T(8,128)(2,1)S(1)}, u32[]{:S(2)}, u32[]{:S(2)}) %collective-permute-start.23) | collective-permute-done | bytes 262176 | tf_op jit(solution)/shard_map/ppermute | solution.py:99
  100.9 1.8 %expert_down.5 = (bf16[4,64,512]{2,1,0:T(8,128)(2,1)S(1)}, bf16[4,64,512]{2,1,0:T(8,128)(2,1)S(1)}, bf16[4,64,512]{2,1,0:T(8,128)(2,1)S(1)}, bf16[4,64,512]{2,1,0:T(8,128)(2,1)S(1)}) custom-call(s32[4]{0:T(128)S(1)} %copy-done.3, bf16[256,1024]{1,0:T(8,128)(2,1)S(1)} %expert_hidden.2.refs_1_.refs_4_, bf16[1024,4096]{1,0:T(8,128)(2,1)S(1)} %bitcast.39, ...), custom_call_target="tpu_custom_call" | custom-call | tf_op jit(solution)/shard_map/expert_down/pallas_call | solution.py:423
  104.6 1.6 collective-permute-start.34
  106.2 4.6 %expert_hidden.3.refs_1_.refs_4_ = bf16[256,1024]{1,0:T(8,128)(2,1)S(1)} custom-call(bf16[4,4,64,512]{3,2,1,0:T(8,128)(2,1)S(1)} %stack_planes.9.refs_4_.refs_0_, bf16[4,4,64,512]{3,2,1,0:T(8,128)(2,1)S(1)} %collective-permute-done.28.refs_1_, bf16[4096,1024]{1,0:T(8,128)(2,1)S(1)} %bitcast.45, bf16[4096,1024]{1,0:T(8,128)(2,1)S(1)} %bitcast.49, ...), custom_call_target="tpu_custom_call" | custom-call | tf_op jit(solution)/shard_map/expert_hidden/pallas_call | solution.py:388
  110.9 1.8 %expert_down.6 = (bf16[4,64,512]{2,1,0:T(8,128)(2,1)S(1)}, bf16[4,64,512]{2,1,0:T(8,128)(2,1)S(1)}, bf16[4,64,512]{2,1,0:T(8,128)(2,1)S(1)}, bf16[4,64,512]{2,1,0:T(8,128)(2,1)S(1)}) custom-call(s32[4]{0:T(128)S(1)} %copy-done.3, bf16[256,1024]{1,0:T(8,128)(2,1)S(1)} %expert_hidden.3.refs_1_.refs_4_, bf16[1024,4096]{1,0:T(8,128)(2,1)S(1)} %bitcast.40, ...), custom_call_target="tpu_custom_call" | custom-call | tf_op jit(solution)/shard_map/expert_down/pallas_call | solution.py:423
  113.9 1.6 collective-permute-start.42
  115.5 1.8 %expert_down.7 = (bf16[4,64,512]{2,1,0:T(8,128)(2,1)S(1)}, bf16[4,64,512]{2,1,0:T(8,128)(2,1)S(1)}, bf16[4,64,512]{2,1,0:T(8,128)(2,1)S(1)}, bf16[4,64,512]{2,1,0:T(8,128)(2,1)S(1)}) custom-call(s32[4]{0:T(128)S(1)} %copy-done.3, bf16[256,1024]{1,0:T(8,128)(2,1)S(1)} %expert_hidden.3.refs_1_.refs_4_, bf16[1024,4096]{1,0:T(8,128)(2,1)S(1)} %bitcast.41, ...), custom_call_target="tpu_custom_call" | custom-call | tf_op jit(solution)/shard_map/expert_down/pallas_call | solution.py:423
  118.6 2.5 %collective-permute-start.41 = (bf16[4,64,512]{2,1,0:T(8,128)(2,1)S(1)}, bf16[4,64,512]{2,1,0:T(8,128)(2,1)S(1)}, u32[]{:S(2)}, u32[]{:S(2)}) collective-permute-start(bf16[4,64,512]{2,1,0:T(8,128)(2,1)S(1)} %get-tuple-element.68), channel_id=1, source_target_pairs={{0,24},{4,28},{8,16},{12,20},{16,8},{20,12},{24,0},{28,4},{1,25},{... | collective-permute-start | bytes 786440 | tf_op jit(solution)/shard_map/ppermute | solution.py:99
  121.3 1.6 collective-permute-start.46
  122.9 1.7 %collective-permute-start.47 = (bf16[64,512]{1,0:T(8,128)(2,1)S(1)}, bf16[64,512]{1,0:T(8,128)(2,1)S(1)}, u32[]{:S(2)}, u32[]{:S(2)}) collective-permute-start(bf16[64,512]{1,0:T(8,128)(2,1)S(1)} %get-tuple-element.74), channel_id=1, source_target_pairs={{0,2},{1,3},{2,0},{3,1},{4,6},{5,7},{6,4},{7,5},{8,10},{9,11},{10,... | collective-permute-start | bytes 196616 | tf_op jit(solution)/shard_map/ppermute | solution.py:107
  124.6 2.2 %collective-permute-done.39.refs_1_ = bf16[4,64,512]{2,1,0:T(8,128)(2,1)S(1)} collective-permute-done((bf16[4,64,512]{2,1,0:T(8,128)(2,1)S(1)}, bf16[4,64,512]{2,1,0:T(8,128)(2,1)S(1)}, u32[]{:S(2)}, u32[]{:S(2)}) %collective-permute-start.39) | collective-permute-done | bytes 262176 | tf_op jit(solution)/shard_map/ppermute | solution.py:99
  126.8 2.7 %collective-permute-start.48 = (bf16[64,512]{1,0:T(8,128)(2,1)S(1)}, bf16[64,512]{1,0:T(8,128)(2,1)S(1)}, u32[]{:S(2)}, u32[]{:S(2)}) collective-permute-start(bf16[64,512]{1,0:T(8,128)(2,1)S(1)} %get-tuple-element.73), channel_id=1, source_target_pairs={{0,3},{1,0},{2,1},{3,2},{4,7},{5,4},{6,5},{7,6},{8,11},{9,8},{10,9... | collective-permute-start | bytes 196616 | tf_op jit(solution)/shard_map/ppermute | solution.py:107
  129.5 1.9 %collective-permute-done.41.refs_3_ = bf16[4,64,512]{2,1,0:T(8,128)(2,1)S(1)} collective-permute-done((bf16[4,64,512]{2,1,0:T(8,128)(2,1)S(1)}, bf16[4,64,512]{2,1,0:T(8,128)(2,1)S(1)}, u32[]{:S(2)}, u32[]{:S(2)}) %collective-permute-start.41) | collective-permute-done | bytes 262176 | tf_op jit(solution)/shard_map/ppermute | solution.py:99
  131.6 1.5 collective-permute-start.43
  133.1 3.1 %collective-permute-start.44 = (bf16[64,512]{1,0:T(8,128)(2,1)S(1)}, bf16[64,512]{1,0:T(8,128)(2,1)S(1)}, u32[]{:S(2)}, u32[]{:S(2)}) collective-permute-start(bf16[64,512]{1,0:T(8,128)(2,1)S(1)} %get-tuple-element.78), channel_id=1, source_target_pairs={{0,2},{1,3},{2,0},{3,1},{4,6},{5,7},{6,4},{7,5},{8,10},{9,11},{10,... | collective-permute-start | bytes 196616 | tf_op jit(solution)/shard_map/ppermute | solution.py:107
  136.6 1.3 collective-permute-start.52
  138.7 1.7 %collective-permute-done.44.refs_2_ = bf16[64,512]{1,0:T(8,128)(2,1)S(1)} collective-permute-done((bf16[64,512]{1,0:T(8,128)(2,1)S(1)}, bf16[64,512]{1,0:T(8,128)(2,1)S(1)}, u32[]{:S(2)}, u32[]{:S(2)}) %collective-permute-start.44) | collective-permute-done | bytes 65568 | tf_op jit(solution)/shard_map/ppermute | solution.py:107
  140.8 2.2 %collective-permute-start.49 = (bf16[4,64,512]{2,1,0:T(8,128)(2,1)S(1)}, bf16[4,64,512]{2,1,0:T(8,128)(2,1)S(1)}, u32[]{:S(2)}, u32[]{:S(2)}) collective-permute-start(bf16[4,64,512]{2,1,0:T(8,128)(2,1)S(1)} %stack_planes.11.refs_1_), channel_id=1, source_target_pairs={{0,8},{4,20},{8,0},{12,28},{16,24},{20,4},{24,16},{28,12},{1,9},{5... | collective-permute-start | bytes 786440 | tf_op jit(solution)/shard_map/ppermute | solution.py:52
  143.6 1.4 collective-permute-start.54
  145.7 4.4 %collective-permute-done.49.refs_2_ = bf16[4,64,512]{2,1,0:T(8,128)(2,1)S(1)} collective-permute-done((bf16[4,64,512]{2,1,0:T(8,128)(2,1)S(1)}, bf16[4,64,512]{2,1,0:T(8,128)(2,1)S(1)}, u32[]{:S(2)}, u32[]{:S(2)}) %collective-permute-start.49) | collective-permute-done | bytes 262176 | tf_op jit(solution)/shard_map/ppermute | solution.py:52
  150.1 0.9 collective-permute-start.51
  151.0 1.2 collective-permute-done.54.refs_4_
  152.2 1.1 add_expert_rows.3.refs_5_
  153.3 1.7 %collective-permute-done.50.refs_3_ = bf16[4,64,512]{2,1,0:T(8,128)(2,1)S(1)} collective-permute-done((bf16[4,64,512]{2,1,0:T(8,128)(2,1)S(1)}, bf16[4,64,512]{2,1,0:T(8,128)(2,1)S(1)}, u32[]{:S(2)}, u32[]{:S(2)}) %collective-permute-start.50) | collective-permute-done | bytes 262176 | tf_op jit(solution)/shard_map/ppermute | solution.py:52
  155.0 2.8 %collective-permute-done.51.refs_4_ = bf16[4,64,512]{2,1,0:T(8,128)(2,1)S(1)} collective-permute-done((bf16[4,64,512]{2,1,0:T(8,128)(2,1)S(1)}, bf16[4,64,512]{2,1,0:T(8,128)(2,1)S(1)}, u32[]{:S(2)}, u32[]{:S(2)}) %collective-permute-start.51) | collective-permute-done | bytes 262176 | tf_op jit(solution)/shard_map/ppermute | solution.py:52
  157.8 1.0 add_expert_rows.5
  159.1 1.0 add_expert_rows.4.refs_0_
  160.8 1.1 join_halves.1
  (107 shorter events, 15.3 us)
Async XLA Ops:
  0.0 25.9 %collective-permute-start = (bf16[512,4096]{1,0:T(8,128)(2,1)}, bf16[512,4096]{1,0:T(8,128)(2,1)}, u32[]{:S(2)}, u32[]{:S(2)}) collective-permute-start(bf16[512,4096]{1,0:T(8,128)(2,1)} %refs_0_.12), channel_id=1, source_target_pairs={{0,4},{4,0},{8,12},{12,8},{16,20},{20,16},{24,28},{28,24},{1,5},{5... | collective-permute-start | bytes 12582920 | tf_op jit(solution)/shard_map/ppermute | solution.py:496
  0.5 25.4 %copy-start = (bf16[512,4096]{1,0:T(8,128)(2,1)S(1)}, bf16[512,4096]{1,0:T(8,128)(2,1)}, u32[]{:S(2)}) copy-start(bf16[512,4096]{1,0:T(8,128)(2,1)} %refs_0_.12) | copy-start | bytes 12582916
  1.9 6.1 %collective-permute-start.2 = (bf16[512,512]{1,0:T(8,128)(2,1)S(1)}, bf16[512,512]{1,0:T(8,128)(2,1)S(1)}, u32[]{:S(2)}, u32[]{:S(2)}) collective-permute-start(bf16[512,512]{1,0:T(8,128)(2,1)S(1)} %get-tuple-element.71), channel_id=1, source_target_pairs={{0,4},{4,0},{8,12},{12,8},{16,20},{20,16},{24,28},{28,24},{1,5},{5... | collective-permute-start | bytes 1572872 | tf_op jit(solution)/shard_map/ppermute | solution.py:496
  2.0 11.7 %collective-permute-start.4 = (bf16[512,512]{1,0:T(8,128)(2,1)S(1)}, bf16[512,512]{1,0:T(8,128)(2,1)S(1)}, u32[]{:S(2)}, u32[]{:S(2)}) collective-permute-start(bf16[512,512]{1,0:T(8,128)(2,1)S(1)} %get-tuple-element.72.refs_2_), channel_id=1, source_target_pairs={{0,8},{4,20},{8,0},{12,28},{16,24},{20,4},{24,16},{28,12},{1,9},{5... | collective-permute-start | bytes 1572872 | tf_op jit(solution)/shard_map/ppermute | solution.py:52
  8.0 14.9 %collective-permute-start.5 = (bf16[512,512]{1,0:T(8,128)(2,1)S(1)}, bf16[512,512]{1,0:T(8,128)(2,1)S(1)}, u32[]{:S(2)}, u32[]{:S(2)}) collective-permute-start(bf16[512,512]{1,0:T(8,128)(2,1)S(1)} %collective-permute-done.2.refs_3_), channel_id=1, source_target_pairs={{0,8},{4,20},{8,0},{12,28},{16,24},{20,4},{24,16},{28,12},{1,9},{5... | collective-permute-start | bytes 1572872 | tf_op jit(solution)/shard_map/ppermute | solution.py:52
  10.8 18.5 %collective-permute-start.1 = (bf16[512,512]{1,0:T(8,128)(2,1)S(1)}, bf16[512,512]{1,0:T(8,128)(2,1)S(1)}, u32[]{:S(2)}, u32[]{:S(2)}) collective-permute-start(bf16[512,512]{1,0:T(8,128)(2,1)S(1)} %get-tuple-element.72.refs_2_), channel_id=1, source_target_pairs={{0,16},{4,12},{8,24},{12,4},{16,0},{20,28},{24,8},{28,20},{1,17},{... | collective-permute-start | bytes 1572872 | tf_op jit(solution)/shard_map/ppermute | solution.py:52
  13.7 18.1 %collective-permute-start.6 = (bf16[512,512]{1,0:T(8,128)(2,1)S(1)}, bf16[512,512]{1,0:T(8,128)(2,1)S(1)}, u32[]{:S(2)}, u32[]{:S(2)}) collective-permute-start(bf16[512,512]{1,0:T(8,128)(2,1)S(1)} %get-tuple-element.69), channel_id=1, source_target_pairs={{0,4},{4,0},{8,12},{12,8},{16,20},{20,16},{24,28},{28,24},{1,5},{5... | collective-permute-start | bytes 1572872 | tf_op jit(solution)/shard_map/ppermute | solution.py:496
  13.7 15.6 %collective-permute-start.3 = (bf16[512,512]{1,0:T(8,128)(2,1)S(1)}, bf16[512,512]{1,0:T(8,128)(2,1)S(1)}, u32[]{:S(2)}, u32[]{:S(2)}) collective-permute-start(bf16[512,512]{1,0:T(8,128)(2,1)S(1)} %collective-permute-done.2.refs_3_), channel_id=1, source_target_pairs={{0,16},{4,12},{8,24},{12,4},{16,0},{20,28},{24,8},{28,20},{1,17},{... | collective-permute-start | bytes 1572872 | tf_op jit(solution)/shard_map/ppermute | solution.py:52
  22.8 11.5 %collective-permute-start.7 = (bf16[512,512]{1,0:T(8,128)(2,1)S(1)}, bf16[512,512]{1,0:T(8,128)(2,1)S(1)}, u32[]{:S(2)}, u32[]{:S(2)}) collective-permute-start(bf16[512,512]{1,0:T(8,128)(2,1)S(1)} %collective-permute-done.4.refs_4_), channel_id=1, source_target_pairs={{0,16},{4,12},{8,24},{12,4},{16,0},{20,28},{24,8},{28,20},{1,17},{... | collective-permute-start | bytes 1572872 | tf_op jit(solution)/shard_map/ppermute | solution.py:52
  25.9 14.1 %collective-permute-start.8 = (bf16[512,512]{1,0:T(8,128)(2,1)S(1)}, bf16[512,512]{1,0:T(8,128)(2,1)S(1)}, u32[]{:S(2)}, u32[]{:S(2)}) collective-permute-start(bf16[512,512]{1,0:T(8,128)(2,1)S(1)} %collective-permute-done.5.refs_5_), channel_id=1, source_target_pairs={{0,16},{4,12},{8,24},{12,4},{16,0},{20,28},{24,8},{28,20},{1,17},{... | collective-permute-start | bytes 1572872 | tf_op jit(solution)/shard_map/ppermute | solution.py:52
  29.3 58.4 %slice-start.4 = ((s8[8388608]{0:T(1024)(128)(4,1)}), s8[4194304]{0:T(1024)(128)(4,1)S(1)}, s32[]{:S(2)}) async-start(s8[8388608]{0:T(1024)(128)(4,1)} %bitcast.46), calls=%async_computation.4 | async-start | bytes 8388608
  31.7 9.5 %copy-start.1 = (s32[4,4]{1,0:T(4,128)S(1)}, s32[4,4]{1,0:T(4,128)}, u32[]{:S(2)}) copy-start(s32[4,4]{1,0:T(4,128)} %refs_0_.21) | copy-start | bytes 196
  40.0 47.8 %slice-start.2 = ((s8[8388608]{0:T(1024)(128)(4,1)}), s8[4194304]{0:T(1024)(128)(4,1)S(1)}, s32[]{:S(2)}) async-start(s8[8388608]{0:T(1024)(128)(4,1)} %bitcast.42), calls=%async_computation.2 | async-start | bytes 8388608
  40.0 47.8 %slice-start.5 = ((s8[8388608]{0:T(1024)(128)(4,1)}), s8[4194304]{0:T(1024)(128)(4,1)S(1)}, s32[]{:S(2)}) async-start(s8[8388608]{0:T(1024)(128)(4,1)} %bitcast.46), calls=%async_computation.5 | async-start | bytes 8388608
  42.0 6.4 %collective-permute-start.9 = (bf16[4,64,512]{2,1,0:T(8,128)(2,1)S(1)}, bf16[4,64,512]{2,1,0:T(8,128)(2,1)S(1)}, u32[]{:S(2)}, u32[]{:S(2)}) collective-permute-start(bf16[4,64,512]{2,1,0:T(8,128)(2,1)S(1)} %get-tuple-element.40), channel_id=1, source_target_pairs={{0,16},{4,12},{8,24},{12,4},{16,0},{20,28},{24,8},{28,20},{1,17},{... | collective-permute-start | bytes 786440 | tf_op jit(solution)/shard_map/ppermute | solution.py:52
  43.9 9.4 %collective-permute-start.12 = (bf16[4,64,512]{2,1,0:T(8,128)(2,1)S(1)}, bf16[4,64,512]{2,1,0:T(8,128)(2,1)S(1)}, u32[]{:S(2)}, u32[]{:S(2)}) collective-permute-start(bf16[4,64,512]{2,1,0:T(8,128)(2,1)S(1)} %get-tuple-element.46), channel_id=1, source_target_pairs={{0,16},{4,12},{8,24},{12,4},{16,0},{20,28},{24,8},{28,20},{1,17},{... | collective-permute-start | bytes 786440 | tf_op jit(solution)/shard_map/ppermute | solution.py:52
  48.5 39.2 %slice-start.3 = ((s8[8388608]{0:T(1024)(128)(4,1)}), s8[4194304]{0:T(1024)(128)(4,1)S(1)}, s32[]{:S(2)}) async-start(s8[8388608]{0:T(1024)(128)(4,1)} %bitcast.42), calls=%async_computation.3 | async-start | bytes 8388608
  48.6 8.4 %collective-permute-start.13 = (bf16[4,64,512]{2,1,0:T(8,128)(2,1)S(1)}, bf16[4,64,512]{2,1,0:T(8,128)(2,1)S(1)}, u32[]{:S(2)}, u32[]{:S(2)}) collective-permute-start(bf16[4,64,512]{2,1,0:T(8,128)(2,1)S(1)} %add_terms.9.refs_2_), channel_id=1, source_target_pairs={{0,8},{4,20},{8,0},{12,28},{16,24},{20,4},{24,16},{28,12},{1,9},{5... | collective-permute-start | bytes 786440 | tf_op jit(solution)/shard_map/ppermute | solution.py:52
  51.2 12.0 %collective-permute-start.10 = (bf16[4,64,512]{2,1,0:T(8,128)(2,1)S(1)}, bf16[4,64,512]{2,1,0:T(8,128)(2,1)S(1)}, u32[]{:S(2)}, u32[]{:S(2)}) collective-permute-start(bf16[4,64,512]{2,1,0:T(8,128)(2,1)S(1)} %get-tuple-element.43), channel_id=1, source_target_pairs={{0,16},{4,12},{8,24},{12,4},{16,0},{20,28},{24,8},{28,20},{1,17},{... | collective-permute-start | bytes 786440 | tf_op jit(solution)/shard_map/ppermute | solution.py:52
  52.7 10.4 %collective-permute-start.11 = (bf16[4,64,512]{2,1,0:T(8,128)(2,1)S(1)}, bf16[4,64,512]{2,1,0:T(8,128)(2,1)S(1)}, u32[]{:S(2)}, u32[]{:S(2)}) collective-permute-start(bf16[4,64,512]{2,1,0:T(8,128)(2,1)S(1)} %get-tuple-element.45), channel_id=1, source_target_pairs={{0,16},{4,12},{8,24},{12,4},{16,0},{20,28},{24,8},{28,20},{1,17},{... | collective-permute-start | bytes 786440 | tf_op jit(solution)/shard_map/ppermute | solution.py:52
  57.1 7.7 %collective-permute-start.15 = (bf16[64,512]{1,0:T(8,128)(2,1)S(1)}, bf16[64,512]{1,0:T(8,128)(2,1)S(1)}, u32[]{:S(2)}, u32[]{:S(2)}) collective-permute-start(bf16[64,512]{1,0:T(8,128)(2,1)S(1)} %get-tuple-element.87), channel_id=1, source_target_pairs={{0,1},{1,2},{2,3},{3,0},{4,5},{5,6},{6,7},{7,4},{8,9},{9,10},{10,1... | collective-permute-start | bytes 196616 | tf_op jit(solution)/shard_map/ppermute | solution.py:107
  59.2 5.6 %collective-permute-start.16 = (bf16[64,512]{1,0:T(8,128)(2,1)S(1)}, bf16[64,512]{1,0:T(8,128)(2,1)S(1)}, u32[]{:S(2)}, u32[]{:S(2)}) collective-permute-start(bf16[64,512]{1,0:T(8,128)(2,1)S(1)} %get-tuple-element.86), channel_id=1, source_target_pairs={{0,2},{1,3},{2,0},{3,1},{4,6},{5,7},{6,4},{7,5},{8,10},{9,11},{10,... | collective-permute-start | bytes 196616 | tf_op jit(solution)/shard_map/ppermute | solution.py:107
  61.8 4.3 %collective-permute-start.17 = (bf16[64,512]{1,0:T(8,128)(2,1)S(1)}, bf16[64,512]{1,0:T(8,128)(2,1)S(1)}, u32[]{:S(2)}, u32[]{:S(2)}) collective-permute-start(bf16[64,512]{1,0:T(8,128)(2,1)S(1)} %get-tuple-element.85), channel_id=1, source_target_pairs={{0,3},{1,0},{2,1},{3,2},{4,7},{5,4},{6,5},{7,6},{8,11},{9,8},{10,9... | collective-permute-start | bytes 196616 | tf_op jit(solution)/shard_map/ppermute | solution.py:107
  63.2 7.9 %collective-permute-start.14 = (bf16[4,64,512]{2,1,0:T(8,128)(2,1)S(1)}, bf16[4,64,512]{2,1,0:T(8,128)(2,1)S(1)}, u32[]{:S(2)}, u32[]{:S(2)}) collective-permute-start(bf16[4,64,512]{2,1,0:T(8,128)(2,1)S(1)} %add_terms.11.refs_4_), channel_id=1, source_target_pairs={{0,8},{4,20},{8,0},{12,28},{16,24},{20,4},{24,16},{28,12},{1,9},{5... | collective-permute-start | bytes 786440 | tf_op jit(solution)/shard_map/ppermute | solution.py:52
  66.0 10.0 %collective-permute-start.24 = (bf16[4,64,512]{2,1,0:T(8,128)(2,1)S(1)}, bf16[4,64,512]{2,1,0:T(8,128)(2,1)S(1)}, u32[]{:S(2)}, u32[]{:S(2)}) collective-permute-start(bf16[4,64,512]{2,1,0:T(8,128)(2,1)S(1)} %stack_planes.6.refs_3_.refs_0_), channel_id=1, source_target_pairs={{0,8},{4,20},{8,0},{12,28},{16,24},{20,4},{24,16},{28,12},{1,9},{5... | collective-permute-start | bytes 786440 | tf_op jit(solution)/shard_map/ppermute | solution.py:52
  67.6 16.4 %collective-permute-start.25 = (bf16[4,64,512]{2,1,0:T(8,128)(2,1)S(1)}, bf16[4,64,512]{2,1,0:T(8,128)(2,1)S(1)}, u32[]{:S(2)}, u32[]{:S(2)}) collective-permute-start(bf16[4,64,512]{2,1,0:T(8,128)(2,1)S(1)} %stack_planes.6.refs_3_.refs_0_), channel_id=1, source_target_pairs={{0,16},{4,12},{8,24},{12,4},{16,0},{20,28},{24,8},{28,20},{1,17},{... | collective-permute-start | bytes 786440 | tf_op jit(solution)/shard_map/ppermute | solution.py:52
  76.1 7.9 %collective-permute-start.26 = (bf16[4,64,512]{2,1,0:T(8,128)(2,1)S(1)}, bf16[4,64,512]{2,1,0:T(8,128)(2,1)S(1)}, u32[]{:S(2)}, u32[]{:S(2)}) collective-permute-start(bf16[4,64,512]{2,1,0:T(8,128)(2,1)S(1)} %collective-permute-done.24.refs_1_), channel_id=1, source_target_pairs={{0,16},{4,12},{8,24},{12,4},{16,0},{20,28},{24,8},{28,20},{1,17},{... | collective-permute-start | bytes 786440 | tf_op jit(solution)/shard_map/ppermute | solution.py:52
  76.4 6.1 %collective-permute-start.18 = (bf16[64,512]{1,0:T(8,128)(2,1)S(1)}, bf16[64,512]{1,0:T(8,128)(2,1)S(1)}, u32[]{:S(2)}, u32[]{:S(2)}) collective-permute-start(bf16[64,512]{1,0:T(8,128)(2,1)S(1)} %get-tuple-element.83), channel_id=1, source_target_pairs={{0,1},{1,2},{2,3},{3,0},{4,5},{5,6},{6,7},{7,4},{8,9},{9,10},{10,1... | collective-permute-start | bytes 196616 | tf_op jit(solution)/shard_map/ppermute | solution.py:107
  78.1 5.2 %collective-permute-start.19 = (bf16[64,512]{1,0:T(8,128)(2,1)S(1)}, bf16[64,512]{1,0:T(8,128)(2,1)S(1)}, u32[]{:S(2)}, u32[]{:S(2)}) collective-permute-start(bf16[64,512]{1,0:T(8,128)(2,1)S(1)} %get-tuple-element.82), channel_id=1, source_target_pairs={{0,2},{1,3},{2,0},{3,1},{4,6},{5,7},{6,4},{7,5},{8,10},{9,11},{10,... | collective-permute-start | bytes 196616 | tf_op jit(solution)/shard_map/ppermute | solution.py:107
  79.4 4.5 %collective-permute-start.20 = (bf16[64,512]{1,0:T(8,128)(2,1)S(1)}, bf16[64,512]{1,0:T(8,128)(2,1)S(1)}, u32[]{:S(2)}, u32[]{:S(2)}) collective-permute-start(bf16[64,512]{1,0:T(8,128)(2,1)S(1)} %get-tuple-element.81), channel_id=1, source_target_pairs={{0,3},{1,0},{2,1},{3,2},{4,7},{5,4},{6,5},{7,6},{8,11},{9,8},{10,9... | collective-permute-start | bytes 196616 | tf_op jit(solution)/shard_map/ppermute | solution.py:107
  84.0 8.5 %slice-start = ((s8[8388608]{0:T(1024)(128)(4,1)}), s8[4194304]{0:T(1024)(128)(4,1)S(1)}, s32[]{:S(2)}) async-start(s8[8388608]{0:T(1024)(128)(4,1)} %bitcast.36), calls=%async_computation | async-start | bytes 8388608
  84.1 3.6 %collective-permute-start.27 = (bf16[4,4,64,512]{3,2,1,0:T(8,128)(2,1)S(1)}, bf16[4,4,64,512]{3,2,1,0:T(8,128)(2,1)S(1)}, u32[]{:S(2)}, u32[]{:S(2)}) collective-permute-start(bf16[4,4,64,512]{3,2,1,0:T(8,128)(2,1)S(1)} %stack_planes.8.refs_0_.refs_4_), channel_id=1, source_target_pairs={{0,4},{4,0},{8,12},{12,8},{16,20},{20,16},{24,28},{28,24},{1,5},{5... | collective-permute-start | bytes 3145736 | tf_op jit(solution)/shard_map/ppermute | solution.py:496
  84.2 10.2 %collective-permute-start.21 = (bf16[4,64,512]{2,1,0:T(8,128)(2,1)S(1)}, bf16[4,64,512]{2,1,0:T(8,128)(2,1)S(1)}, u32[]{:S(2)}, u32[]{:S(2)}) collective-permute-start(bf16[4,64,512]{2,1,0:T(8,128)(2,1)S(1)} %stack_planes.7.refs_4_.refs_0_), channel_id=1, source_target_pairs={{0,8},{4,20},{8,0},{12,28},{16,24},{20,4},{24,16},{28,12},{1,9},{5... | collective-permute-start | bytes 786440 | tf_op jit(solution)/shard_map/ppermute | solution.py:99
  85.8 8.6 %collective-permute-start.22 = (bf16[4,64,512]{2,1,0:T(8,128)(2,1)S(1)}, bf16[4,64,512]{2,1,0:T(8,128)(2,1)S(1)}, u32[]{:S(2)}, u32[]{:S(2)}) collective-permute-start(bf16[4,64,512]{2,1,0:T(8,128)(2,1)S(1)} %stack_planes.7.refs_4_.refs_0_), channel_id=1, source_target_pairs={{0,16},{4,12},{8,24},{12,4},{16,0},{20,28},{24,8},{28,20},{1,17},{... | collective-permute-start | bytes 786440 | tf_op jit(solution)/shard_map/ppermute | solution.py:99
  87.2 12.5 %collective-permute-start.23 = (bf16[4,64,512]{2,1,0:T(8,128)(2,1)S(1)}, bf16[4,64,512]{2,1,0:T(8,128)(2,1)S(1)}, u32[]{:S(2)}, u32[]{:S(2)}) collective-permute-start(bf16[4,64,512]{2,1,0:T(8,128)(2,1)S(1)} %stack_planes.7.refs_4_.refs_0_), channel_id=1, source_target_pairs={{0,24},{4,28},{8,16},{12,20},{16,8},{20,12},{24,0},{28,4},{1,25},{... | collective-permute-start | bytes 786440 | tf_op jit(solution)/shard_map/ppermute | solution.py:99
  87.8 4.7 %slice-start.1 = ((s8[8388608]{0:T(1024)(128)(4,1)}), s8[4194304]{0:T(1024)(128)(4,1)S(1)}, s32[]{:S(2)}) async-start(s8[8388608]{0:T(1024)(128)(4,1)} %bitcast.36), calls=%async_computation.1 | async-start | bytes 8388608
  99.8 6.4 %collective-permute-start.28 = (bf16[4,4,64,512]{3,2,1,0:T(8,128)(2,1)S(1)}, bf16[4,4,64,512]{3,2,1,0:T(8,128)(2,1)S(1)}, u32[]{:S(2)}, u32[]{:S(2)}) collective-permute-start(bf16[4,4,64,512]{3,2,1,0:T(8,128)(2,1)S(1)} %stack_planes.9.refs_4_.refs_0_), channel_id=1, source_target_pairs={{0,4},{4,0},{8,12},{12,8},{16,20},{20,16},{24,28},{28,24},{1,5},{5... | collective-permute-start | bytes 3145736 | tf_op jit(solution)/shard_map/ppermute | solution.py:496
  99.9 3.7 %collective-permute-start.31 = (bf16[4,64,512]{2,1,0:T(8,128)(2,1)S(1)}, bf16[4,64,512]{2,1,0:T(8,128)(2,1)S(1)}, u32[]{:S(2)}, u32[]{:S(2)}) collective-permute-start(bf16[4,64,512]{2,1,0:T(8,128)(2,1)S(1)} %get-tuple-element.47.refs_4_), channel_id=1, source_target_pairs={{0,4},{4,0},{8,12},{12,8},{16,20},{20,16},{24,28},{28,24},{1,5},{5... | collective-permute-start | bytes 786440 | tf_op jit(solution)/shard_map/ppermute | solution.py:496
  100.3 2.9 %collective-permute-start.29 = (bf16[4,64,512]{2,1,0:T(8,128)(2,1)S(1)}, bf16[4,64,512]{2,1,0:T(8,128)(2,1)S(1)}, u32[]{:S(2)}, u32[]{:S(2)}) collective-permute-start(bf16[4,64,512]{2,1,0:T(8,128)(2,1)S(1)} %get-tuple-element.49), channel_id=1, source_target_pairs={{0,4},{4,0},{8,12},{12,8},{16,20},{20,16},{24,28},{28,24},{1,5},{5... | collective-permute-start | bytes 786440 | tf_op jit(solution)/shard_map/ppermute | solution.py:496
  100.4 3.2 %collective-permute-start.30 = (bf16[4,64,512]{2,1,0:T(8,128)(2,1)S(1)}, bf16[4,64,512]{2,1,0:T(8,128)(2,1)S(1)}, u32[]{:S(2)}, u32[]{:S(2)}) collective-permute-start(bf16[4,64,512]{2,1,0:T(8,128)(2,1)S(1)} %get-tuple-element.51), channel_id=1, source_target_pairs={{0,4},{4,0},{8,12},{12,8},{16,20},{20,16},{24,28},{28,24},{1,5},{5... | collective-permute-start | bytes 786440 | tf_op jit(solution)/shard_map/ppermute | solution.py:496
  100.8 3.1 %collective-permute-start.32 = (bf16[4,64,512]{2,1,0:T(8,128)(2,1)S(1)}, bf16[4,64,512]{2,1,0:T(8,128)(2,1)S(1)}, u32[]{:S(2)}, u32[]{:S(2)}) collective-permute-start(bf16[4,64,512]{2,1,0:T(8,128)(2,1)S(1)} %get-tuple-element.53), channel_id=1, source_target_pairs={{0,4},{4,0},{8,12},{12,8},{16,20},{20,16},{24,28},{28,24},{1,5},{5... | collective-permute-start | bytes 786440 | tf_op jit(solution)/shard_map/ppermute | solution.py:496
  104.1 9.3 %collective-permute-start.33 = (bf16[4,64,512]{2,1,0:T(8,128)(2,1)S(1)}, bf16[4,64,512]{2,1,0:T(8,128)(2,1)S(1)}, u32[]{:S(2)}, u32[]{:S(2)}) collective-permute-start(bf16[4,64,512]{2,1,0:T(8,128)(2,1)S(1)} %get-tuple-element.56), channel_id=1, source_target_pairs={{0,16},{4,12},{8,24},{12,4},{16,0},{20,28},{24,8},{28,20},{1,17},{... | collective-permute-start | bytes 786440 | tf_op jit(solution)/shard_map/ppermute | solution.py:52
  104.6 9.2 %collective-permute-start.34 = (bf16[4,64,512]{2,1,0:T(8,128)(2,1)S(1)}, bf16[4,64,512]{2,1,0:T(8,128)(2,1)S(1)}, u32[]{:S(2)}, u32[]{:S(2)}) collective-permute-start(bf16[4,64,512]{2,1,0:T(8,128)(2,1)S(1)} %get-tuple-element.54.refs_4_), channel_id=1, source_target_pairs={{0,16},{4,12},{8,24},{12,4},{16,0},{20,28},{24,8},{28,20},{1,17},{... | collective-permute-start | bytes 786440 | tf_op jit(solution)/shard_map/ppermute | solution.py:52
  112.7 4.6 %collective-permute-start.35 = (bf16[4,64,512]{2,1,0:T(8,128)(2,1)S(1)}, bf16[4,64,512]{2,1,0:T(8,128)(2,1)S(1)}, u32[]{:S(2)}, u32[]{:S(2)}) collective-permute-start(bf16[4,64,512]{2,1,0:T(8,128)(2,1)S(1)} %get-tuple-element.57.refs_3_), channel_id=1, source_target_pairs={{0,4},{4,0},{8,12},{12,8},{16,20},{20,16},{24,28},{28,24},{1,5},{5... | collective-permute-start | bytes 786440 | tf_op jit(solution)/shard_map/ppermute | solution.py:496
  112.8 4.5 %collective-permute-start.36 = (bf16[4,64,512]{2,1,0:T(8,128)(2,1)S(1)}, bf16[4,64,512]{2,1,0:T(8,128)(2,1)S(1)}, u32[]{:S(2)}, u32[]{:S(2)}) collective-permute-start(bf16[4,64,512]{2,1,0:T(8,128)(2,1)S(1)} %get-tuple-element.60), channel_id=1, source_target_pairs={{0,4},{4,0},{8,12},{12,8},{16,20},{20,16},{24,28},{28,24},{1,5},{5... | collective-permute-start | bytes 786440 | tf_op jit(solution)/shard_map/ppermute | solution.py:496
  113.3 4.0 %collective-permute-start.37 = (bf16[4,64,512]{2,1,0:T(8,128)(2,1)S(1)}, bf16[4,64,512]{2,1,0:T(8,128)(2,1)S(1)}, u32[]{:S(2)}, u32[]{:S(2)}) collective-permute-start(bf16[4,64,512]{2,1,0:T(8,128)(2,1)S(1)} %get-tuple-element.62), channel_id=1, source_target_pairs={{0,4},{4,0},{8,12},{12,8},{16,20},{20,16},{24,28},{28,24},{1,5},{5... | collective-permute-start | bytes 786440 | tf_op jit(solution)/shard_map/ppermute | solution.py:496
  113.4 4.0 %collective-permute-start.38 = (bf16[4,64,512]{2,1,0:T(8,128)(2,1)S(1)}, bf16[4,64,512]{2,1,0:T(8,128)(2,1)S(1)}, u32[]{:S(2)}, u32[]{:S(2)}) collective-permute-start(bf16[4,64,512]{2,1,0:T(8,128)(2,1)S(1)} %get-tuple-element.64), channel_id=1, source_target_pairs={{0,4},{4,0},{8,12},{12,8},{16,20},{20,16},{24,28},{28,24},{1,5},{5... | collective-permute-start | bytes 786440 | tf_op jit(solution)/shard_map/ppermute | solution.py:496
  113.9 7.2 %collective-permute-start.42 = (bf16[4,64,512]{2,1,0:T(8,128)(2,1)S(1)}, bf16[4,64,512]{2,1,0:T(8,128)(2,1)S(1)}, u32[]{:S(2)}, u32[]{:S(2)}) collective-permute-start(bf16[4,64,512]{2,1,0:T(8,128)(2,1)S(1)} %add_terms.14.refs_4_), channel_id=1, source_target_pairs={{0,8},{4,20},{8,0},{12,28},{16,24},{20,4},{24,16},{28,12},{1,9},{5... | collective-permute-start | bytes 786440 | tf_op jit(solution)/shard_map/ppermute | solution.py:52
  117.6 9.2 %collective-permute-start.39 = (bf16[4,64,512]{2,1,0:T(8,128)(2,1)S(1)}, bf16[4,64,512]{2,1,0:T(8,128)(2,1)S(1)}, u32[]{:S(2)}, u32[]{:S(2)}) collective-permute-start(bf16[4,64,512]{2,1,0:T(8,128)(2,1)S(1)} %get-tuple-element.66), channel_id=1, source_target_pairs={{0,8},{4,20},{8,0},{12,28},{16,24},{20,4},{24,16},{28,12},{1,9},{5... | collective-permute-start | bytes 786440 | tf_op jit(solution)/shard_map/ppermute | solution.py:99
  118.2 11.3 %collective-permute-start.40 = (bf16[4,64,512]{2,1,0:T(8,128)(2,1)S(1)}, bf16[4,64,512]{2,1,0:T(8,128)(2,1)S(1)}, u32[]{:S(2)}, u32[]{:S(2)}) collective-permute-start(bf16[4,64,512]{2,1,0:T(8,128)(2,1)S(1)} %get-tuple-element.67), channel_id=1, source_target_pairs={{0,16},{4,12},{8,24},{12,4},{16,0},{20,28},{24,8},{28,20},{1,17},{... | collective-permute-start | bytes 786440 | tf_op jit(solution)/shard_map/ppermute | solution.py:99
  118.6 12.8 %collective-permute-start.41 = (bf16[4,64,512]{2,1,0:T(8,128)(2,1)S(1)}, bf16[4,64,512]{2,1,0:T(8,128)(2,1)S(1)}, u32[]{:S(2)}, u32[]{:S(2)}) collective-permute-start(bf16[4,64,512]{2,1,0:T(8,128)(2,1)S(1)} %get-tuple-element.68), channel_id=1, source_target_pairs={{0,24},{4,28},{8,16},{12,20},{16,8},{20,12},{24,0},{28,4},{1,25},{... | collective-permute-start | bytes 786440 | tf_op jit(solution)/shard_map/ppermute | solution.py:99
  121.3 14.9 %collective-permute-start.46 = (bf16[64,512]{1,0:T(8,128)(2,1)S(1)}, bf16[64,512]{1,0:T(8,128)(2,1)S(1)}, u32[]{:S(2)}, u32[]{:S(2)}) collective-permute-start(bf16[64,512]{1,0:T(8,128)(2,1)S(1)} %get-tuple-element.75), channel_id=1, source_target_pairs={{0,1},{1,2},{2,3},{3,0},{4,5},{5,6},{6,7},{7,4},{8,9},{9,10},{10,1... | collective-permute-start | bytes 196616 | tf_op jit(solution)/shard_map/ppermute | solution.py:107
  122.9 13.6 %collective-permute-start.47 = (bf16[64,512]{1,0:T(8,128)(2,1)S(1)}, bf16[64,512]{1,0:T(8,128)(2,1)S(1)}, u32[]{:S(2)}, u32[]{:S(2)}) collective-permute-start(bf16[64,512]{1,0:T(8,128)(2,1)S(1)} %get-tuple-element.74), channel_id=1, source_target_pairs={{0,2},{1,3},{2,0},{3,1},{4,6},{5,7},{6,4},{7,5},{8,10},{9,11},{10,... | collective-permute-start | bytes 196616 | tf_op jit(solution)/shard_map/ppermute | solution.py:107
  126.8 9.7 %collective-permute-start.48 = (bf16[64,512]{1,0:T(8,128)(2,1)S(1)}, bf16[64,512]{1,0:T(8,128)(2,1)S(1)}, u32[]{:S(2)}, u32[]{:S(2)}) collective-permute-start(bf16[64,512]{1,0:T(8,128)(2,1)S(1)} %get-tuple-element.73), channel_id=1, source_target_pairs={{0,3},{1,0},{2,1},{3,2},{4,7},{5,4},{6,5},{7,6},{8,11},{9,8},{10,9... | collective-permute-start | bytes 196616 | tf_op jit(solution)/shard_map/ppermute | solution.py:107
  131.6 7.1 %collective-permute-start.43 = (bf16[64,512]{1,0:T(8,128)(2,1)S(1)}, bf16[64,512]{1,0:T(8,128)(2,1)S(1)}, u32[]{:S(2)}, u32[]{:S(2)}) collective-permute-start(bf16[64,512]{1,0:T(8,128)(2,1)S(1)} %get-tuple-element.79), channel_id=1, source_target_pairs={{0,1},{1,2},{2,3},{3,0},{4,5},{5,6},{6,7},{7,4},{8,9},{9,10},{10,1... | collective-permute-start | bytes 196616 | tf_op jit(solution)/shard_map/ppermute | solution.py:107
  133.1 7.2 %collective-permute-start.44 = (bf16[64,512]{1,0:T(8,128)(2,1)S(1)}, bf16[64,512]{1,0:T(8,128)(2,1)S(1)}, u32[]{:S(2)}, u32[]{:S(2)}) collective-permute-start(bf16[64,512]{1,0:T(8,128)(2,1)S(1)} %get-tuple-element.78), channel_id=1, source_target_pairs={{0,2},{1,3},{2,0},{3,1},{4,6},{5,7},{6,4},{7,5},{8,10},{9,11},{10,... | collective-permute-start | bytes 196616 | tf_op jit(solution)/shard_map/ppermute | solution.py:107
  136.2 4.6 %collective-permute-start.45 = (bf16[64,512]{1,0:T(8,128)(2,1)S(1)}, bf16[64,512]{1,0:T(8,128)(2,1)S(1)}, u32[]{:S(2)}, u32[]{:S(2)}) collective-permute-start(bf16[64,512]{1,0:T(8,128)(2,1)S(1)} %get-tuple-element.77), channel_id=1, source_target_pairs={{0,3},{1,0},{2,1},{3,2},{4,7},{5,4},{6,5},{7,6},{8,11},{9,8},{10,9... | collective-permute-start | bytes 196616 | tf_op jit(solution)/shard_map/ppermute | solution.py:107
  136.6 7.1 %collective-permute-start.52 = (bf16[4,64,512]{2,1,0:T(8,128)(2,1)S(1)}, bf16[4,64,512]{2,1,0:T(8,128)(2,1)S(1)}, u32[]{:S(2)}, u32[]{:S(2)}) collective-permute-start(bf16[4,64,512]{2,1,0:T(8,128)(2,1)S(1)} %stack_planes.10.refs_4_.refs_1_), channel_id=1, source_target_pairs={{0,8},{4,20},{8,0},{12,28},{16,24},{20,4},{24,16},{28,12},{1,9},{5... | collective-permute-start | bytes 786440 | tf_op jit(solution)/shard_map/ppermute | solution.py:52
  140.8 9.3 %collective-permute-start.49 = (bf16[4,64,512]{2,1,0:T(8,128)(2,1)S(1)}, bf16[4,64,512]{2,1,0:T(8,128)(2,1)S(1)}, u32[]{:S(2)}, u32[]{:S(2)}) collective-permute-start(bf16[4,64,512]{2,1,0:T(8,128)(2,1)S(1)} %stack_planes.11.refs_1_), channel_id=1, source_target_pairs={{0,8},{4,20},{8,0},{12,28},{16,24},{20,4},{24,16},{28,12},{1,9},{5... | collective-permute-start | bytes 786440 | tf_op jit(solution)/shard_map/ppermute | solution.py:52
  143.0 8.0 %collective-permute-start.53 = (bf16[4,64,512]{2,1,0:T(8,128)(2,1)S(1)}, bf16[4,64,512]{2,1,0:T(8,128)(2,1)S(1)}, u32[]{:S(2)}, u32[]{:S(2)}) collective-permute-start(bf16[4,64,512]{2,1,0:T(8,128)(2,1)S(1)} %stack_planes.10.refs_4_.refs_1_), channel_id=1, source_target_pairs={{0,16},{4,12},{8,24},{12,4},{16,0},{20,28},{24,8},{28,20},{1,17},{... | collective-permute-start | bytes 786440 | tf_op jit(solution)/shard_map/ppermute | solution.py:52
  143.6 8.6 %collective-permute-start.54 = (bf16[4,64,512]{2,1,0:T(8,128)(2,1)S(1)}, bf16[4,64,512]{2,1,0:T(8,128)(2,1)S(1)}, u32[]{:S(2)}, u32[]{:S(2)}) collective-permute-start(bf16[4,64,512]{2,1,0:T(8,128)(2,1)S(1)} %collective-permute-done.52.refs_2_), channel_id=1, source_target_pairs={{0,16},{4,12},{8,24},{12,4},{16,0},{20,28},{24,8},{28,20},{1,17},{... | collective-permute-start | bytes 786440 | tf_op jit(solution)/shard_map/ppermute | solution.py:52
  145.1 10.0 %collective-permute-start.50 = (bf16[4,64,512]{2,1,0:T(8,128)(2,1)S(1)}, bf16[4,64,512]{2,1,0:T(8,128)(2,1)S(1)}, u32[]{:S(2)}, u32[]{:S(2)}) collective-permute-start(bf16[4,64,512]{2,1,0:T(8,128)(2,1)S(1)} %stack_planes.11.refs_1_), channel_id=1, source_target_pairs={{0,16},{4,12},{8,24},{12,4},{16,0},{20,28},{24,8},{28,20},{1,17},{... | collective-permute-start | bytes 786440 | tf_op jit(solution)/shard_map/ppermute | solution.py:52
  150.1 7.7 %collective-permute-start.51 = (bf16[4,64,512]{2,1,0:T(8,128)(2,1)S(1)}, bf16[4,64,512]{2,1,0:T(8,128)(2,1)S(1)}, u32[]{:S(2)}, u32[]{:S(2)}) collective-permute-start(bf16[4,64,512]{2,1,0:T(8,128)(2,1)S(1)} %collective-permute-done.49.refs_2_), channel_id=1, source_target_pairs={{0,16},{4,12},{8,24},{12,4},{16,0},{20,28},{24,8},{28,20},{1,17},{... | collective-permute-start | bytes 786440 | tf_op jit(solution)/shard_map/ppermute | solution.py:52
  158.9 2.0 %collective-permute-start.55 = (bf16[8,64,512]{2,1,0:T(8,128)(2,1)S(1)}, bf16[8,64,512]{2,1,0:T(8,128)(2,1)S(1)}, u32[]{:S(2)}, u32[]{:S(2)}) collective-permute-start(bf16[8,64,512]{2,1,0:T(8,128)(2,1)S(1)} %add_expert_rows.5), channel_id=1, source_target_pairs={{0,4},{4,0},{8,12},{12,8},{16,20},{20,16},{24,28},{28,24},{1,5},{5... | collective-permute-start | bytes 1572872 | tf_op jit(solution)/shard_map/ppermute | solution.py:496
  (2 other events, 9.4 us)

commit v10 on v9

--- a/solution.py
+++ b/solution.py
@@ -10,8 +10,8 @@
 GROUPS = 2
 DIRECT = ((0, 0, 0, 0), (0, 1, 1, 0))
 PICK_WAIT = (0, 0)
-HOP_WAIT = ((0, 1), (1, 0))
-ORDER = '001010110001001101101011'
+HOP_WAIT = ((0, 0), (0, 0))
+ORDER = '001010110000101011011011'
 
 
 def bit_orders(n_bits):
@@ -198,11 +198,11 @@
         return index, lax.div(owner, 2) == place.chip
 
 
-def project_kernel(make_place, parts, ahead, n_w, n_res, *refs):
+def project_kernel(make_place, parts, ahead, n_w, n_res, n_unread, *refs):
     context, other = refs[:2]
     weights = refs[2 : 2 + n_w]
     extra = refs[2 + n_w : 2 + n_w + n_res]
-    outs, (w_all, c_own, c_other, sems) = refs[2 + n_w + n_res : -4], refs[-4:]
+    outs, (w_all, c_own, c_other, sems) = refs[2 + n_w + n_res + n_unread : -4], refs[-4:]
     depth = weights[0].shape[0]
     place = make_place()
 
@@ -240,7 +240,7 @@
         copy.wait()
 
 
-def project(make_place, parts, ahead, own, other, weights, extra):
+def project(make_place, parts, ahead, own, other, weights, extra, unread):
     rows = own.shape[0]
     depth, half = weights[0].shape
     k = depth * len(weights)
@@ -248,9 +248,11 @@
     if ahead is not None:
         shapes.append(jax.ShapeDtypeStruct((2, rows, 2 * depth), own.dtype))
     return call(
-        lambda *refs: project_kernel(make_place, parts, ahead, len(weights), len(extra), *refs),
+        lambda *refs: project_kernel(
+            make_place, parts, ahead, len(weights), len(extra), len(unread), *refs
+        ),
         shapes,
-        [ANY, ANY] + [VMEM] * (len(weights) + len(extra)),
+        [ANY, ANY] + [VMEM] * (len(weights) + len(extra)) + [ANY] * len(unread),
         [VMEM] * len(shapes),
         "project",
         12,
@@ -260,7 +262,7 @@
             pltpu.VMEM((rows, k), jnp.bfloat16),
             pltpu.SemaphoreType.DMA((4, len(weights))),
         ],
-    )(own, other, *weights, *extra)
+    )(own, other, *weights, *extra, *unread)
 
 
 def project_last_kernel(columns, total, own, other, *refs):
@@ -396,43 +398,60 @@
     )(own, other, w_gate, w_up, after)
 
 
-def down_kernel(make_place, layout, order, s, counts, hid, wd, values, after, *outs):
+def scale_kernel(make_place, layouts, n_chip, counts, values, *outs):
+    place = make_place()
+    count = counts[place.expert]
+    rows, n_row = layouts[0].share, values.shape[1]
+    row_of = lax.broadcasted_iota(jnp.int32, (rows, n_row), 0)
+    at_of = lax.broadcasted_iota(jnp.int32, (rows, n_row), 1)
+    for layout, out in zip(layouts, outs):
+        for r in range(n_chip):
+            row = layout.first_row(place, r)
+            chosen = (at_of == row_of + row) & (lax.div(row, BLK) < count)
+            scale = jnp.sum(jnp.where(chosen, values[...], 0.0), axis=1, keepdims=True)
+            out[r * rows : (r + 1) * rows, :] = scale
+
+
+def scales(make_place, layouts, n_chip, counts, values):
+    shape = jax.ShapeDtypeStruct((n_chip * layouts[0].share, 1), jnp.float32)
+    return call(
+        lambda *refs: scale_kernel(make_place, layouts, n_chip, *refs),
+        [shape] * len(layouts),
+        [SMEM, VMEM],
+        [VMEM] * len(layouts),
+        "row_scales",
+        4,
+    )(counts, values)
+
+
+def down_kernel(make_place, layout, order, s, hid, wd, scale, after, *outs):
     n = len(order)
     n_z, rows, width = outs[0].shape
     place = make_place()
-    count = counts[place.expert]
-    n_row = values.shape[1]
-    row_of = lax.broadcasted_iota(jnp.int32, (rows, n_row), 0)
-    at_of = lax.broadcasted_iota(jnp.int32, (rows, n_row), 1)
-    scale = []
-    for r in range(n):
-        row = layout.first_row(place, r)
-        chosen = (at_of == row_of + row) & (lax.div(row, BLK) < count)
-        scale.append(jnp.sum(jnp.where(chosen, values[...], 0.0), axis=1, keepdims=True))
     for z in range(n_z):
         at = (place.ahead(z) * 2 + (place.side ^ s)) * width
         at = pl.ds(pl.multiple_of(at, width), width)
         part = jnp.dot(hid[...], wd[:, at], preferred_element_type=jnp.float32)
         for r in range(n):
-            value = part[r * rows : (r + 1) * rows] * scale[r]
+            value = part[r * rows : (r + 1) * rows] * scale[r * rows : (r + 1) * rows]
             outs[order[r]][z] = value.astype(jnp.bfloat16)
 
 
-def down(make_place, layout, order, s, n_z, width, counts, hid, w_down, values, after):
+def down(make_place, layout, order, s, n_z, width, hid, w_down, scale, after):
     n = len(order)
     return call(
         lambda *refs: down_kernel(make_place, layout, order, s, *refs),
         [jax.ShapeDtypeStruct((n_z, layout.share, width), jnp.bfloat16)] * n,
-        [SMEM] + [VMEM] * 3 + [ANY],
+        [VMEM] * 3 + [ANY],
         [VMEM] * n,
         "expert_down",
         8,
-    )(counts, hid, w_down, values, after)
+    )(hid, w_down, scale, after)
 
 
 def group_steps(layout, scope, tables, grains):
     make_place, n_dp, n_bits, n_expert, half, reverse, to_partner = scope
-    chosen, counts, values, w_gate, w_up, w_down = tables
+    chosen, scale, w_gate, w_up, w_down = tables
     n_chip = 1 << n_bits
     plain = list(range(n_chip))
     after = yield
@@ -454,7 +473,7 @@
 
     def downs(order, s):
         return down(
-            make_place, layout, order, s, n_expert, half, counts, hid, w_down, values, after
+            make_place, layout, order, s, n_expert, half, hid, w_down, scale[layout.group], after
         )
 
     theirs = downs(reverse, 1)
@@ -515,20 +534,20 @@
     def make_place():
         return Place(n_bits, n_expert)
 
+    layouts = [Layout(group, n_chip, local_blocks) for group in range(GROUPS)]
+    factors = scales(make_place, layouts, n_chip, block_counts, gate_values)
     last = n_chip - 1
     sides = (context, context_other)
-    (total,) = project(make_place, plain[:top], None, *sides, pieces[: 2 * top], ())
+    (total,) = project(make_place, plain[:top], None, *sides, pieces[: 2 * top], (), factors)
     total, columns = project(
-        make_place, plain[top:last], last, *sides, pieces[2 * top : 2 * last], (total,)
+        make_place, plain[top:last], last, *sides, pieces[2 * top : 2 * last], (total,), ()
     )
     attended = project_last(columns, total, residual_own, residual_other, pieces[2 * last :])
 
-    layouts = [Layout(group, n_chip, local_blocks) for group in range(GROUPS)]
     grains = attended.reshape(-1, share, half)
-    values = gate_values
 
     scope = (make_place, n_dp, n_bits, n_expert, half, reverse, to_partner)
-    tables = (chosen_blocks, block_counts, values, w_gate, w_up, w_down)
+    tables = (chosen_blocks, factors, w_gate, w_up, w_down)
     groups = [group_steps(layout, scope, tables, grains) for layout in layouts]
     for group in groups:
         next(group)

time: 162 us -> 161 us (level)
    ppermute x12, starting transfers between devices: 22.6 us -> 19.3 us  [swap_planes(): out.append(lax.ppermute(parts[k], 'expert', pairs))]
    ppermute x24, waiting for transfers between devices: 40.9 us -> 38.6 us  [exchange(): return lax.ppermute(value, 'dp', step_pairs(n_dp, step))]
    pallas_call x4, Pallas kernels: 7.29 us -> 5.13 us  [down(): call(lambda *refs: down_kernel(make_place, layout, order, s, *refs), [jax...]
  transfers between devices with their start and end apart: 56 -> 56, of which waited for: 26 -> 24; matrix products, arithmetic and copies ran while one was open for 2% -> 2% of each run, Pallas kernels for 16% -> 15%
where the time goes in v10:
time: 161 us
  starting transfers between devices  66.8 us (41%)
  waiting for transfers between devices  61.8 us (38%)
  Pallas kernels  29.2 us (18%)
  local copies, waits for them, and re-layouts  2.82 us (2%)
    ppermute x24, waiting for transfers between devices, exchange(): return lax.ppermute(value, 'dp', step_pairs(n_dp, step))  38.6 us
    ppermute x24, starting transfers between devices, exchange(): return lax.ppermute(value, 'dp', step_pairs(n_dp, step))  35.1 us
    ppermute x12, starting transfers between devices, swap_planes(): out.append(lax.ppermute(parts[k], 'expert', pairs))  19.3 us
    ppermute x6, waiting for transfers between devices, direct(): out.append(lax.ppermute(value, 'dp', pairs) if r else value)  10.1 us
    pallas_call x2, Pallas kernels, hidden_units(): call(lambda *refs: hidden_kernel(make_place, reverse, *refs), jax.ShapeDt...  9.29 us
    ppermute x6, starting transfers between devices, direct(): out.append(lax.ppermute(value, 'dp', pairs) if r else value)  7.65 us
    ppermute x12, waiting for transfers between devices, swap_planes(): out.append(lax.ppermute(parts[k], 'expert', pairs))  7.1 us
    ppermute x14, waiting for transfers between devices, to_partner(): return lax.ppermute(value, 'dp', pair)  6.04 us
  transfers between devices with their start and end apart: 56, of which 24 were waited for; matrix products, arithmetic and copies ran while one was open for 2% of the time, Pallas kernels for 15%

profile of v10, /device:TPU:0, one launch (start us, length us, event | category | flops | bytes accessed | tf_op | source)
XLA Modules:
  0.0 161.2 jit_solution(14646863775025422405)
XLA Ops:
  0.5 1.4 constant_dynamic-slice_fusion.2
  2.0 2.9 %collective-permute-start.4 = (bf16[512,512]{1,0:T(8,128)(2,1)S(1)}, bf16[512,512]{1,0:T(8,128)(2,1)S(1)}, u32[]{:S(2)}, u32[]{:S(2)}) collective-permute-start(bf16[512,512]{1,0:T(8,128)(2,1)S(1)} %get-tuple-element.76.refs_2_), channel_id=1, source_target_pairs={{0,8},{4,20},{8,0},{12,28},{16,24},{20,4},{24,16},{28,12},{1,9},{5... | collective-permute-start | bytes 1572872 | tf_op jit(solution)/shard_map/ppermute | solution.py:52
  4.9 3.1 %collective-permute-done.2.refs_3_ = bf16[512,512]{1,0:T(8,128)(2,1)S(1)} collective-permute-done((bf16[512,512]{1,0:T(8,128)(2,1)S(1)}, bf16[512,512]{1,0:T(8,128)(2,1)S(1)}, u32[]{:S(2)}, u32[]{:S(2)}) %collective-permute-start.2) | collective-permute-done | bytes 524320 | tf_op jit(solution)/shard_map/ppermute | solution.py:515
  8.0 2.9 %collective-permute-start.5 = (bf16[512,512]{1,0:T(8,128)(2,1)S(1)}, bf16[512,512]{1,0:T(8,128)(2,1)S(1)}, u32[]{:S(2)}, u32[]{:S(2)}) collective-permute-start(bf16[512,512]{1,0:T(8,128)(2,1)S(1)} %collective-permute-done.2.refs_3_), channel_id=1, source_target_pairs={{0,8},{4,20},{8,0},{12,28},{16,24},{20,4},{24,16},{28,12},{1,9},{5... | collective-permute-start | bytes 1572872 | tf_op jit(solution)/shard_map/ppermute | solution.py:52
  10.9 1.5 collective-permute-start.1
  12.4 1.3 constant_dynamic-slice_fusion
  13.7 0.9 collective-permute-start.3
  14.6 8.2 %collective-permute-done.5.refs_5_ = bf16[512,512]{1,0:T(8,128)(2,1)S(1)} collective-permute-done((bf16[512,512]{1,0:T(8,128)(2,1)S(1)}, bf16[512,512]{1,0:T(8,128)(2,1)S(1)}, u32[]{:S(2)}, u32[]{:S(2)}) %collective-permute-start.5) | collective-permute-done | bytes 524320 | tf_op jit(solution)/shard_map/ppermute | solution.py:52
  22.8 3.0 %collective-permute-start.7 = (bf16[512,512]{1,0:T(8,128)(2,1)S(1)}, bf16[512,512]{1,0:T(8,128)(2,1)S(1)}, u32[]{:S(2)}, u32[]{:S(2)}) collective-permute-start(bf16[512,512]{1,0:T(8,128)(2,1)S(1)} %collective-permute-done.4.refs_4_), channel_id=1, source_target_pairs={{0,16},{4,12},{8,24},{12,4},{16,0},{20,28},{24,8},{28,20},{1,17},{... | collective-permute-start | bytes 1572872 | tf_op jit(solution)/shard_map/ppermute | solution.py:52
  26.6 3.4 %project.2.refs_4_ = f32[2,512,512]{2,1,0:T(8,128)S(1)} custom-call(bf16[512,4096]{1,0:T(8,128)(2,1)S(1)} %copy-done, bf16[512,4096]{1,0:T(8,128)(2,1)} %collective-permute-done.refs_1_, bf16[512,512]{1,0:T(8,128)(2,1)S(1)} %get-tuple-element.76.refs_2_, bf16[512,512]{1,0:T(8,128)(2,1)S(1)} %collective-permute-done.2.refs_3_, ...), custom_call_target="tpu_custom_call" | custom-call | tf_op jit(solution)/shard_map/project/pallas_call | solution.py:250
  30.1 2.4 %project.3 = (f32[2,512,512]{2,1,0:T(8,128)S(1)}, bf16[2,512,1024]{2,1,0:T(8,128)(2,1)S(1)}) custom-call(bf16[512,4096]{1,0:T(8,128)(2,1)S(1)} %copy-done, bf16[512,4096]{1,0:T(8,128)(2,1)} %collective-permute-done.refs_1_, bf16[512,512]{1,0:T(8,128)(2,1)S(1)} %collective-permute-done.1.refs_2_, bf16[512,512]{1,0:T(8,128)(2,1)S(1)} %collective-permute-done.3.refs_3_, ...), custom_call_target="tpu_custom_call" | custom-call | tf_op jit(solution)/shard_map/project/pallas_call | solution.py:250
  32.5 1.8 %collective-permute-done.7.refs_0_ = bf16[512,512]{1,0:T(8,128)(2,1)S(1)} collective-permute-done((bf16[512,512]{1,0:T(8,128)(2,1)S(1)}, bf16[512,512]{1,0:T(8,128)(2,1)S(1)}, u32[]{:S(2)}, u32[]{:S(2)}) %collective-permute-start.7) | collective-permute-done | bytes 524320 | tf_op jit(solution)/shard_map/ppermute | solution.py:52
  34.3 5.6 %collective-permute-done.8.refs_1_ = bf16[512,512]{1,0:T(8,128)(2,1)S(1)} collective-permute-done((bf16[512,512]{1,0:T(8,128)(2,1)S(1)}, bf16[512,512]{1,0:T(8,128)(2,1)S(1)}, u32[]{:S(2)}, u32[]{:S(2)}) %collective-permute-start.8) | collective-permute-done | bytes 524320 | tf_op jit(solution)/shard_map/ppermute | solution.py:52
  40.0 1.2 project_last.1
  42.0 1.8 %collective-permute-start.9 = (bf16[4,64,512]{2,1,0:T(8,128)(2,1)S(1)}, bf16[4,64,512]{2,1,0:T(8,128)(2,1)S(1)}, u32[]{:S(2)}, u32[]{:S(2)}) collective-permute-start(bf16[4,64,512]{2,1,0:T(8,128)(2,1)S(1)} %get-tuple-element.44), channel_id=1, source_target_pairs={{0,16},{4,12},{8,24},{12,4},{16,0},{20,28},{24,8},{28,20},{1,17},{... | collective-permute-start | bytes 786440 | tf_op jit(solution)/shard_map/ppermute | solution.py:52
  44.1 4.3 %collective-permute-done.9.refs_1_ = bf16[4,64,512]{2,1,0:T(8,128)(2,1)S(1)} collective-permute-done((bf16[4,64,512]{2,1,0:T(8,128)(2,1)S(1)}, bf16[4,64,512]{2,1,0:T(8,128)(2,1)S(1)}, u32[]{:S(2)}, u32[]{:S(2)}) %collective-permute-start.9) | collective-permute-done | bytes 262176 | tf_op jit(solution)/shard_map/ppermute | solution.py:52
  48.6 1.8 %collective-permute-start.13 = (bf16[4,64,512]{2,1,0:T(8,128)(2,1)S(1)}, bf16[4,64,512]{2,1,0:T(8,128)(2,1)S(1)}, u32[]{:S(2)}, u32[]{:S(2)}) collective-permute-start(bf16[4,64,512]{2,1,0:T(8,128)(2,1)S(1)} %add_terms.9.refs_2_), channel_id=1, source_target_pairs={{0,8},{4,20},{8,0},{12,28},{16,24},{20,4},{24,16},{28,12},{1,9},{5... | collective-permute-start | bytes 786440 | tf_op jit(solution)/shard_map/ppermute | solution.py:52
  51.2 1.6 collective-permute-start.11
  52.7 4.2 %collective-permute-done.13.refs_2_ = bf16[4,64,512]{2,1,0:T(8,128)(2,1)S(1)} collective-permute-done((bf16[4,64,512]{2,1,0:T(8,128)(2,1)S(1)}, bf16[4,64,512]{2,1,0:T(8,128)(2,1)S(1)}, u32[]{:S(2)}, u32[]{:S(2)}) %collective-permute-start.13) | collective-permute-done | bytes 262176 | tf_op jit(solution)/shard_map/ppermute | solution.py:52
  57.1 2.1 %collective-permute-start.15 = (bf16[64,512]{1,0:T(8,128)(2,1)S(1)}, bf16[64,512]{1,0:T(8,128)(2,1)S(1)}, u32[]{:S(2)}, u32[]{:S(2)}) collective-permute-start(bf16[64,512]{1,0:T(8,128)(2,1)S(1)} %get-tuple-element.91), channel_id=1, source_target_pairs={{0,1},{1,2},{2,3},{3,0},{4,5},{5,6},{6,7},{7,4},{8,9},{9,10},{10,1... | collective-permute-start | bytes 196616 | tf_op jit(solution)/shard_map/ppermute | solution.py:107
  59.2 2.6 %collective-permute-start.16 = (bf16[64,512]{1,0:T(8,128)(2,1)S(1)}, bf16[64,512]{1,0:T(8,128)(2,1)S(1)}, u32[]{:S(2)}, u32[]{:S(2)}) collective-permute-start(bf16[64,512]{1,0:T(8,128)(2,1)S(1)} %get-tuple-element.90), channel_id=1, source_target_pairs={{0,2},{1,3},{2,0},{3,1},{4,6},{5,7},{6,4},{7,5},{8,10},{9,11},{10,... | collective-permute-start | bytes 196616 | tf_op jit(solution)/shard_map/ppermute | solution.py:107
  61.8 1.3 collective-permute-start.17
  63.1 2.1 %collective-permute-start.10 = (bf16[4,64,512]{2,1,0:T(8,128)(2,1)S(1)}, bf16[4,64,512]{2,1,0:T(8,128)(2,1)S(1)}, u32[]{:S(2)}, u32[]{:S(2)}) collective-permute-start(bf16[4,64,512]{2,1,0:T(8,128)(2,1)S(1)} %get-tuple-element.47), channel_id=1, source_target_pairs={{0,16},{4,12},{8,24},{12,4},{16,0},{20,28},{24,8},{28,20},{1,17},{... | collective-permute-start | bytes 786440 | tf_op jit(solution)/shard_map/ppermute | solution.py:52
  65.3 1.6 collective-permute-start.14
  67.6 2.1 %collective-permute-start.25 = (bf16[4,64,512]{2,1,0:T(8,128)(2,1)S(1)}, bf16[4,64,512]{2,1,0:T(8,128)(2,1)S(1)}, u32[]{:S(2)}, u32[]{:S(2)}) collective-permute-start(bf16[4,64,512]{2,1,0:T(8,128)(2,1)S(1)} %stack_planes.6.refs_3_.refs_0_), channel_id=1, source_target_pairs={{0,16},{4,12},{8,24},{12,4},{16,0},{20,28},{24,8},{28,20},{1,17},{... | collective-permute-start | bytes 786440 | tf_op jit(solution)/shard_map/ppermute | solution.py:52
  69.7 2.4 %collective-permute-done.10.refs_1_ = bf16[4,64,512]{2,1,0:T(8,128)(2,1)S(1)} collective-permute-done((bf16[4,64,512]{2,1,0:T(8,128)(2,1)S(1)}, bf16[4,64,512]{2,1,0:T(8,128)(2,1)S(1)}, u32[]{:S(2)}, u32[]{:S(2)}) %collective-permute-start.10) | collective-permute-done | bytes 262176 | tf_op jit(solution)/shard_map/ppermute | solution.py:52
  72.2 2.5 %collective-permute-done.24.refs_1_ = bf16[4,64,512]{2,1,0:T(8,128)(2,1)S(1)} collective-permute-done((bf16[4,64,512]{2,1,0:T(8,128)(2,1)S(1)}, bf16[4,64,512]{2,1,0:T(8,128)(2,1)S(1)}, u32[]{:S(2)}, u32[]{:S(2)}) %collective-permute-start.24) | collective-permute-done | bytes 262176 | tf_op jit(solution)/shard_map/ppermute | solution.py:52
  75.2 0.9 collective-permute-start.18
  76.1 3.0 %collective-permute-start.19 = (bf16[64,512]{1,0:T(8,128)(2,1)S(1)}, bf16[64,512]{1,0:T(8,128)(2,1)S(1)}, u32[]{:S(2)}, u32[]{:S(2)}) collective-permute-start(bf16[64,512]{1,0:T(8,128)(2,1)S(1)} %get-tuple-element.86), channel_id=1, source_target_pairs={{0,2},{1,3},{2,0},{3,1},{4,6},{5,7},{6,4},{7,5},{8,10},{9,11},{10,... | collective-permute-start | bytes 196616 | tf_op jit(solution)/shard_map/ppermute | solution.py:107
  79.1 2.3 %collective-permute-done.18.refs_1_ = bf16[64,512]{1,0:T(8,128)(2,1)S(1)} collective-permute-done((bf16[64,512]{1,0:T(8,128)(2,1)S(1)}, bf16[64,512]{1,0:T(8,128)(2,1)S(1)}, u32[]{:S(2)}, u32[]{:S(2)}) %collective-permute-start.18) | collective-permute-done | bytes 65568 | tf_op jit(solution)/shard_map/ppermute | solution.py:107
  81.4 1.3 collective-permute-done.19.refs_2_
  83.6 2.2 %collective-permute-start.21 = (bf16[4,64,512]{2,1,0:T(8,128)(2,1)S(1)}, bf16[4,64,512]{2,1,0:T(8,128)(2,1)S(1)}, u32[]{:S(2)}, u32[]{:S(2)}) collective-permute-start(bf16[4,64,512]{2,1,0:T(8,128)(2,1)S(1)} %stack_planes.7.refs_4_.refs_0_), channel_id=1, source_target_pairs={{0,8},{4,20},{8,0},{12,28},{16,24},{20,4},{24,16},{28,12},{1,9},{5... | collective-permute-start | bytes 786440 | tf_op jit(solution)/shard_map/ppermute | solution.py:99
  85.8 1.9 %collective-permute-start.22 = (bf16[4,64,512]{2,1,0:T(8,128)(2,1)S(1)}, bf16[4,64,512]{2,1,0:T(8,128)(2,1)S(1)}, u32[]{:S(2)}, u32[]{:S(2)}) collective-permute-start(bf16[4,64,512]{2,1,0:T(8,128)(2,1)S(1)} %stack_planes.7.refs_4_.refs_0_), channel_id=1, source_target_pairs={{0,16},{4,12},{8,24},{12,4},{16,0},{20,28},{24,8},{28,20},{1,17},{... | collective-permute-start | bytes 786440 | tf_op jit(solution)/shard_map/ppermute | solution.py:99
  87.8 4.6 %expert_hidden.2.refs_0_.refs_3_ = bf16[256,1024]{1,0:T(8,128)(2,1)S(1)} custom-call(bf16[4,4,64,512]{3,2,1,0:T(8,128)(2,1)S(1)} %stack_planes.8.refs_0_.refs_4_, bf16[4,4,64,512]{3,2,1,0:T(8,128)(2,1)S(1)} %collective-permute-done.27.refs_1_, bf16[4096,1024]{1,0:T(8,128)(2,1)S(1)} %bitcast.44, bf16[4096,1024]{1,0:T(8,128)(2,1)S(1)} %bitcast.48, ...), custom_call_target="tpu_custom_call" | custom-call | tf_op jit(solution)/shard_map/expert_hidden/pallas_call | solution.py:390
  92.5 1.3 expert_down.4
  93.8 1.3 expert_down.5
  95.1 4.6 %collective-permute-done.23.refs_3_ = bf16[4,64,512]{2,1,0:T(8,128)(2,1)S(1)} collective-permute-done((bf16[4,64,512]{2,1,0:T(8,128)(2,1)S(1)}, bf16[4,64,512]{2,1,0:T(8,128)(2,1)S(1)}, u32[]{:S(2)}, u32[]{:S(2)}) %collective-permute-start.23) | collective-permute-done | bytes 262176 | tf_op jit(solution)/shard_map/ppermute | solution.py:99
  100.8 2.0 %collective-permute-done.29.refs_1_ = bf16[4,64,512]{2,1,0:T(8,128)(2,1)S(1)} collective-permute-done((bf16[4,64,512]{2,1,0:T(8,128)(2,1)S(1)}, bf16[4,64,512]{2,1,0:T(8,128)(2,1)S(1)}, u32[]{:S(2)}, u32[]{:S(2)}) %collective-permute-start.29) | collective-permute-done | bytes 262176 | tf_op jit(solution)/shard_map/ppermute | solution.py:515
  103.4 1.6 collective-permute-start.37
  105.5 4.6 %expert_hidden.3.refs_3_.refs_0_ = bf16[256,1024]{1,0:T(8,128)(2,1)S(1)} custom-call(bf16[4,4,64,512]{3,2,1,0:T(8,128)(2,1)S(1)} %stack_planes.9.refs_4_.refs_0_, bf16[4,4,64,512]{3,2,1,0:T(8,128)(2,1)S(1)} %collective-permute-done.28.refs_1_, bf16[4096,1024]{1,0:T(8,128)(2,1)S(1)} %bitcast.45, bf16[4096,1024]{1,0:T(8,128)(2,1)S(1)} %bitcast.49, ...), custom_call_target="tpu_custom_call" | custom-call | tf_op jit(solution)/shard_map/expert_hidden/pallas_call | solution.py:390
  110.2 1.3 expert_down.6
  111.5 1.8 %collective-permute-start.39 = (bf16[4,64,512]{2,1,0:T(8,128)(2,1)S(1)}, bf16[4,64,512]{2,1,0:T(8,128)(2,1)S(1)}, u32[]{:S(2)}, u32[]{:S(2)}) collective-permute-start(bf16[4,64,512]{2,1,0:T(8,128)(2,1)S(1)} %add_terms.14.refs_3_), channel_id=1, source_target_pairs={{0,8},{4,20},{8,0},{12,28},{16,24},{20,4},{24,16},{28,12},{1,9},{5... | collective-permute-start | bytes 786440 | tf_op jit(solution)/shard_map/ppermute | solution.py:52
  114.4 1.3 expert_down.7
  115.6 2.3 %collective-permute-done.39.refs_3_ = bf16[4,64,512]{2,1,0:T(8,128)(2,1)S(1)} collective-permute-done((bf16[4,64,512]{2,1,0:T(8,128)(2,1)S(1)}, bf16[4,64,512]{2,1,0:T(8,128)(2,1)S(1)}, u32[]{:S(2)}, u32[]{:S(2)}) %collective-permute-start.39) | collective-permute-done | bytes 262176 | tf_op jit(solution)/shard_map/ppermute | solution.py:52
  118.4 1.8 %collective-permute-start.40 = (bf16[4,64,512]{2,1,0:T(8,128)(2,1)S(1)}, bf16[4,64,512]{2,1,0:T(8,128)(2,1)S(1)}, u32[]{:S(2)}, u32[]{:S(2)}) collective-permute-start(bf16[4,64,512]{2,1,0:T(8,128)(2,1)S(1)} %get-tuple-element.70), channel_id=1, source_target_pairs={{0,8},{4,20},{8,0},{12,28},{16,24},{20,4},{24,16},{28,12},{1,9},{5... | collective-permute-start | bytes 786440 | tf_op jit(solution)/shard_map/ppermute | solution.py:99
  120.4 1.5 collective-permute-start.42
  122.6 2.4 %collective-permute-start.47 = (bf16[64,512]{1,0:T(8,128)(2,1)S(1)}, bf16[64,512]{1,0:T(8,128)(2,1)S(1)}, u32[]{:S(2)}, u32[]{:S(2)}) collective-permute-start(bf16[64,512]{1,0:T(8,128)(2,1)S(1)} %get-tuple-element.78), channel_id=1, source_target_pairs={{0,2},{1,3},{2,0},{3,1},{4,6},{5,7},{6,4},{7,5},{8,10},{9,11},{10,... | collective-permute-start | bytes 196616 | tf_op jit(solution)/shard_map/ppermute | solution.py:107
  125.0 2.6 %collective-permute-done.40.refs_1_ = bf16[4,64,512]{2,1,0:T(8,128)(2,1)S(1)} collective-permute-done((bf16[4,64,512]{2,1,0:T(8,128)(2,1)S(1)}, bf16[4,64,512]{2,1,0:T(8,128)(2,1)S(1)}, u32[]{:S(2)}, u32[]{:S(2)}) %collective-permute-start.40) | collective-permute-done | bytes 262176 | tf_op jit(solution)/shard_map/ppermute | solution.py:99
  127.7 2.4 %collective-permute-start.48 = (bf16[64,512]{1,0:T(8,128)(2,1)S(1)}, bf16[64,512]{1,0:T(8,128)(2,1)S(1)}, u32[]{:S(2)}, u32[]{:S(2)}) collective-permute-start(bf16[64,512]{1,0:T(8,128)(2,1)S(1)} %get-tuple-element.77), channel_id=1, source_target_pairs={{0,3},{1,0},{2,1},{3,2},{4,7},{5,4},{6,5},{7,6},{8,11},{9,8},{10,9... | collective-permute-start | bytes 196616 | tf_op jit(solution)/shard_map/ppermute | solution.py:107
  130.1 2.8 %collective-permute-done.42.refs_3_ = bf16[4,64,512]{2,1,0:T(8,128)(2,1)S(1)} collective-permute-done((bf16[4,64,512]{2,1,0:T(8,128)(2,1)S(1)}, bf16[4,64,512]{2,1,0:T(8,128)(2,1)S(1)}, u32[]{:S(2)}, u32[]{:S(2)}) %collective-permute-start.42) | collective-permute-done | bytes 262176 | tf_op jit(solution)/shard_map/ppermute | solution.py:99
  133.7 2.4 %collective-permute-start.44 = (bf16[64,512]{1,0:T(8,128)(2,1)S(1)}, bf16[64,512]{1,0:T(8,128)(2,1)S(1)}, u32[]{:S(2)}, u32[]{:S(2)}) collective-permute-start(bf16[64,512]{1,0:T(8,128)(2,1)S(1)} %get-tuple-element.82), channel_id=1, source_target_pairs={{0,2},{1,3},{2,0},{3,1},{4,6},{5,7},{6,4},{7,5},{8,10},{9,11},{10,... | collective-permute-start | bytes 196616 | tf_op jit(solution)/shard_map/ppermute | solution.py:107
  137.0 1.1 collective-permute-start.52
  138.1 1.2 collective-permute-done.43.refs_1_
  139.3 1.3 collective-permute-done.44.refs_2_
  140.8 1.5 collective-permute-start.49
  142.3 1.3 collective-permute-start.53
  143.6 2.6 %collective-permute-start.54 = (bf16[4,64,512]{2,1,0:T(8,128)(2,1)S(1)}, bf16[4,64,512]{2,1,0:T(8,128)(2,1)S(1)}, u32[]{:S(2)}, u32[]{:S(2)}) collective-permute-start(bf16[4,64,512]{2,1,0:T(8,128)(2,1)S(1)} %collective-permute-done.52.refs_2_), channel_id=1, source_target_pairs={{0,16},{4,12},{8,24},{12,4},{16,0},{20,28},{24,8},{28,20},{1,17},{... | collective-permute-start | bytes 786440 | tf_op jit(solution)/shard_map/ppermute | solution.py:52
  146.2 3.8 %collective-permute-done.49.refs_2_ = bf16[4,64,512]{2,1,0:T(8,128)(2,1)S(1)} collective-permute-done((bf16[4,64,512]{2,1,0:T(8,128)(2,1)S(1)}, bf16[4,64,512]{2,1,0:T(8,128)(2,1)S(1)}, u32[]{:S(2)}, u32[]{:S(2)}) %collective-permute-start.49) | collective-permute-done | bytes 262176 | tf_op jit(solution)/shard_map/ppermute | solution.py:52
  150.1 2.7 %collective-permute-start.51 = (bf16[4,64,512]{2,1,0:T(8,128)(2,1)S(1)}, bf16[4,64,512]{2,1,0:T(8,128)(2,1)S(1)}, u32[]{:S(2)}, u32[]{:S(2)}) collective-permute-start(bf16[4,64,512]{2,1,0:T(8,128)(2,1)S(1)} %collective-permute-done.49.refs_2_), channel_id=1, source_target_pairs={{0,16},{4,12},{8,24},{12,4},{16,0},{20,28},{24,8},{28,20},{1,17},{... | collective-permute-start | bytes 786440 | tf_op jit(solution)/shard_map/ppermute | solution.py:52
  152.7 1.1 add_expert_rows.3.refs_5_
  154.3 2.8 %collective-permute-done.51.refs_4_ = bf16[4,64,512]{2,1,0:T(8,128)(2,1)S(1)} collective-permute-done((bf16[4,64,512]{2,1,0:T(8,128)(2,1)S(1)}, bf16[4,64,512]{2,1,0:T(8,128)(2,1)S(1)}, u32[]{:S(2)}, u32[]{:S(2)}) %collective-permute-start.51) | collective-permute-done | bytes 262176 | tf_op jit(solution)/shard_map/ppermute | solution.py:52
  157.1 1.0 add_expert_rows.5
  158.5 1.0 add_expert_rows.4.refs_0_
  160.1 1.1 join_halves.1
  (108 shorter events, 13.8 us)
Async XLA Ops:
  0.0 25.9 %copy-start.2 = (f32[1,512]{1,0:T(1,128)S(1)}, f32[1,512]{1,0:T(1,128)}, u32[]{:S(2)}) copy-start(f32[1,512]{1,0:T(1,128)} %refs_1_.1) | copy-start | bytes 6148
  0.0 25.9 %copy-start.3 = (s32[4]{0:T(128)S(1)}, s32[4]{0:T(128)}, u32[]{:S(2)}) copy-start(s32[4]{0:T(128)} %refs_0_.8) | copy-start | bytes 52
  0.0 25.9 %collective-permute-start = (bf16[512,4096]{1,0:T(8,128)(2,1)}, bf16[512,4096]{1,0:T(8,128)(2,1)}, u32[]{:S(2)}, u32[]{:S(2)}) collective-permute-start(bf16[512,4096]{1,0:T(8,128)(2,1)} %refs_0_.10), channel_id=1, source_target_pairs={{0,4},{4,0},{8,12},{12,8},{16,20},{20,16},{24,28},{28,24},{1,5},{5... | collective-permute-start | bytes 12582920 | tf_op jit(solution)/shard_map/ppermute | solution.py:515
  0.5 26.2 %copy-start = (bf16[512,4096]{1,0:T(8,128)(2,1)S(1)}, bf16[512,4096]{1,0:T(8,128)(2,1)}, u32[]{:S(2)}) copy-start(bf16[512,4096]{1,0:T(8,128)(2,1)} %refs_0_.10) | copy-start | bytes 12582916
  1.9 6.1 %collective-permute-start.2 = (bf16[512,512]{1,0:T(8,128)(2,1)S(1)}, bf16[512,512]{1,0:T(8,128)(2,1)S(1)}, u32[]{:S(2)}, u32[]{:S(2)}) collective-permute-start(bf16[512,512]{1,0:T(8,128)(2,1)S(1)} %get-tuple-element.75), channel_id=1, source_target_pairs={{0,4},{4,0},{8,12},{12,8},{16,20},{20,16},{24,28},{28,24},{1,5},{5... | collective-permute-start | bytes 1572872 | tf_op jit(solution)/shard_map/ppermute | solution.py:515
  2.0 11.7 %collective-permute-start.4 = (bf16[512,512]{1,0:T(8,128)(2,1)S(1)}, bf16[512,512]{1,0:T(8,128)(2,1)S(1)}, u32[]{:S(2)}, u32[]{:S(2)}) collective-permute-start(bf16[512,512]{1,0:T(8,128)(2,1)S(1)} %get-tuple-element.76.refs_2_), channel_id=1, source_target_pairs={{0,8},{4,20},{8,0},{12,28},{16,24},{20,4},{24,16},{28,12},{1,9},{5... | collective-permute-start | bytes 1572872 | tf_op jit(solution)/shard_map/ppermute | solution.py:52
  8.0 14.9 %collective-permute-start.5 = (bf16[512,512]{1,0:T(8,128)(2,1)S(1)}, bf16[512,512]{1,0:T(8,128)(2,1)S(1)}, u32[]{:S(2)}, u32[]{:S(2)}) collective-permute-start(bf16[512,512]{1,0:T(8,128)(2,1)S(1)} %collective-permute-done.2.refs_3_), channel_id=1, source_target_pairs={{0,8},{4,20},{8,0},{12,28},{16,24},{20,4},{24,16},{28,12},{1,9},{5... | collective-permute-start | bytes 1572872 | tf_op jit(solution)/shard_map/ppermute | solution.py:52
  10.9 19.2 %collective-permute-start.1 = (bf16[512,512]{1,0:T(8,128)(2,1)S(1)}, bf16[512,512]{1,0:T(8,128)(2,1)S(1)}, u32[]{:S(2)}, u32[]{:S(2)}) collective-permute-start(bf16[512,512]{1,0:T(8,128)(2,1)S(1)} %get-tuple-element.76.refs_2_), channel_id=1, source_target_pairs={{0,16},{4,12},{8,24},{12,4},{16,0},{20,28},{24,8},{28,20},{1,17},{... | collective-permute-start | bytes 1572872 | tf_op jit(solution)/shard_map/ppermute | solution.py:52
  13.7 18.8 %collective-permute-start.6 = (bf16[512,512]{1,0:T(8,128)(2,1)S(1)}, bf16[512,512]{1,0:T(8,128)(2,1)S(1)}, u32[]{:S(2)}, u32[]{:S(2)}) collective-permute-start(bf16[512,512]{1,0:T(8,128)(2,1)S(1)} %get-tuple-element.73), channel_id=1, source_target_pairs={{0,4},{4,0},{8,12},{12,8},{16,20},{20,16},{24,28},{28,24},{1,5},{5... | collective-permute-start | bytes 1572872 | tf_op jit(solution)/shard_map/ppermute | solution.py:515
  13.7 16.4 %collective-permute-start.3 = (bf16[512,512]{1,0:T(8,128)(2,1)S(1)}, bf16[512,512]{1,0:T(8,128)(2,1)S(1)}, u32[]{:S(2)}, u32[]{:S(2)}) collective-permute-start(bf16[512,512]{1,0:T(8,128)(2,1)S(1)} %collective-permute-done.2.refs_3_), channel_id=1, source_target_pairs={{0,16},{4,12},{8,24},{12,4},{16,0},{20,28},{24,8},{28,20},{1,17},{... | collective-permute-start | bytes 1572872 | tf_op jit(solution)/shard_map/ppermute | solution.py:52
  22.8 11.5 %collective-permute-start.7 = (bf16[512,512]{1,0:T(8,128)(2,1)S(1)}, bf16[512,512]{1,0:T(8,128)(2,1)S(1)}, u32[]{:S(2)}, u32[]{:S(2)}) collective-permute-start(bf16[512,512]{1,0:T(8,128)(2,1)S(1)} %collective-permute-done.4.refs_4_), channel_id=1, source_target_pairs={{0,16},{4,12},{8,24},{12,4},{16,0},{20,28},{24,8},{28,20},{1,17},{... | collective-permute-start | bytes 1572872 | tf_op jit(solution)/shard_map/ppermute | solution.py:52
  25.9 14.1 %collective-permute-start.8 = (bf16[512,512]{1,0:T(8,128)(2,1)S(1)}, bf16[512,512]{1,0:T(8,128)(2,1)S(1)}, u32[]{:S(2)}, u32[]{:S(2)}) collective-permute-start(bf16[512,512]{1,0:T(8,128)(2,1)S(1)} %collective-permute-done.5.refs_5_), channel_id=1, source_target_pairs={{0,16},{4,12},{8,24},{12,4},{16,0},{20,28},{24,8},{28,20},{1,17},{... | collective-permute-start | bytes 1572872 | tf_op jit(solution)/shard_map/ppermute | solution.py:52
  30.1 57.6 %slice-start.4 = ((s8[8388608]{0:T(1024)(128)(4,1)}), s8[4194304]{0:T(1024)(128)(4,1)S(1)}, s32[]{:S(2)}) async-start(s8[8388608]{0:T(1024)(128)(4,1)} %bitcast.46), calls=%async_computation.4 | async-start | bytes 8388608
  40.0 47.8 %slice-start.2 = ((s8[8388608]{0:T(1024)(128)(4,1)}), s8[4194304]{0:T(1024)(128)(4,1)S(1)}, s32[]{:S(2)}) async-start(s8[8388608]{0:T(1024)(128)(4,1)} %bitcast.42), calls=%async_computation.2 | async-start | bytes 8388608
  40.0 47.8 %slice-start.5 = ((s8[8388608]{0:T(1024)(128)(4,1)}), s8[4194304]{0:T(1024)(128)(4,1)S(1)}, s32[]{:S(2)}) async-start(s8[8388608]{0:T(1024)(128)(4,1)} %bitcast.46), calls=%async_computation.5 | async-start | bytes 8388608
  42.0 6.4 %collective-permute-start.9 = (bf16[4,64,512]{2,1,0:T(8,128)(2,1)S(1)}, bf16[4,64,512]{2,1,0:T(8,128)(2,1)S(1)}, u32[]{:S(2)}, u32[]{:S(2)}) collective-permute-start(bf16[4,64,512]{2,1,0:T(8,128)(2,1)S(1)} %get-tuple-element.44), channel_id=1, source_target_pairs={{0,16},{4,12},{8,24},{12,4},{16,0},{20,28},{24,8},{28,20},{1,17},{... | collective-permute-start | bytes 786440 | tf_op jit(solution)/shard_map/ppermute | solution.py:52
  43.9 8.9 %collective-permute-start.12 = (bf16[4,64,512]{2,1,0:T(8,128)(2,1)S(1)}, bf16[4,64,512]{2,1,0:T(8,128)(2,1)S(1)}, u32[]{:S(2)}, u32[]{:S(2)}) collective-permute-start(bf16[4,64,512]{2,1,0:T(8,128)(2,1)S(1)} %get-tuple-element.50), channel_id=1, source_target_pairs={{0,16},{4,12},{8,24},{12,4},{16,0},{20,28},{24,8},{28,20},{1,17},{... | collective-permute-start | bytes 786440 | tf_op jit(solution)/shard_map/ppermute | solution.py:52
  48.5 39.2 %slice-start.3 = ((s8[8388608]{0:T(1024)(128)(4,1)}), s8[4194304]{0:T(1024)(128)(4,1)S(1)}, s32[]{:S(2)}) async-start(s8[8388608]{0:T(1024)(128)(4,1)} %bitcast.42), calls=%async_computation.3 | async-start | bytes 8388608
  48.6 8.4 %collective-permute-start.13 = (bf16[4,64,512]{2,1,0:T(8,128)(2,1)S(1)}, bf16[4,64,512]{2,1,0:T(8,128)(2,1)S(1)}, u32[]{:S(2)}, u32[]{:S(2)}) collective-permute-start(bf16[4,64,512]{2,1,0:T(8,128)(2,1)S(1)} %add_terms.9.refs_2_), channel_id=1, source_target_pairs={{0,8},{4,20},{8,0},{12,28},{16,24},{20,4},{24,16},{28,12},{1,9},{5... | collective-permute-start | bytes 786440 | tf_op jit(solution)/shard_map/ppermute | solution.py:52
  51.2 14.0 %collective-permute-start.11 = (bf16[4,64,512]{2,1,0:T(8,128)(2,1)S(1)}, bf16[4,64,512]{2,1,0:T(8,128)(2,1)S(1)}, u32[]{:S(2)}, u32[]{:S(2)}) collective-permute-start(bf16[4,64,512]{2,1,0:T(8,128)(2,1)S(1)} %get-tuple-element.49), channel_id=1, source_target_pairs={{0,16},{4,12},{8,24},{12,4},{16,0},{20,28},{24,8},{28,20},{1,17},{... | collective-permute-start | bytes 786440 | tf_op jit(solution)/shard_map/ppermute | solution.py:52
  57.1 9.8 %collective-permute-start.15 = (bf16[64,512]{1,0:T(8,128)(2,1)S(1)}, bf16[64,512]{1,0:T(8,128)(2,1)S(1)}, u32[]{:S(2)}, u32[]{:S(2)}) collective-permute-start(bf16[64,512]{1,0:T(8,128)(2,1)S(1)} %get-tuple-element.91), channel_id=1, source_target_pairs={{0,1},{1,2},{2,3},{3,0},{4,5},{5,6},{6,7},{7,4},{8,9},{9,10},{10,1... | collective-permute-start | bytes 196616 | tf_op jit(solution)/shard_map/ppermute | solution.py:107
  59.2 7.6 %collective-permute-start.16 = (bf16[64,512]{1,0:T(8,128)(2,1)S(1)}, bf16[64,512]{1,0:T(8,128)(2,1)S(1)}, u32[]{:S(2)}, u32[]{:S(2)}) collective-permute-start(bf16[64,512]{1,0:T(8,128)(2,1)S(1)} %get-tuple-element.90), channel_id=1, source_target_pairs={{0,2},{1,3},{2,0},{3,1},{4,6},{5,7},{6,4},{7,5},{8,10},{9,11},{10,... | collective-permute-start | bytes 196616 | tf_op jit(solution)/shard_map/ppermute | solution.py:107
  61.8 5.1 %collective-permute-start.17 = (bf16[64,512]{1,0:T(8,128)(2,1)S(1)}, bf16[64,512]{1,0:T(8,128)(2,1)S(1)}, u32[]{:S(2)}, u32[]{:S(2)}) collective-permute-start(bf16[64,512]{1,0:T(8,128)(2,1)S(1)} %get-tuple-element.89), channel_id=1, source_target_pairs={{0,3},{1,0},{2,1},{3,2},{4,7},{5,4},{6,5},{7,6},{8,11},{9,8},{10,9... | collective-permute-start | bytes 196616 | tf_op jit(solution)/shard_map/ppermute | solution.py:107
  63.1 9.0 %collective-permute-start.10 = (bf16[4,64,512]{2,1,0:T(8,128)(2,1)S(1)}, bf16[4,64,512]{2,1,0:T(8,128)(2,1)S(1)}, u32[]{:S(2)}, u32[]{:S(2)}) collective-permute-start(bf16[4,64,512]{2,1,0:T(8,128)(2,1)S(1)} %get-tuple-element.47), channel_id=1, source_target_pairs={{0,16},{4,12},{8,24},{12,4},{16,0},{20,28},{24,8},{28,20},{1,17},{... | collective-permute-start | bytes 786440 | tf_op jit(solution)/shard_map/ppermute | solution.py:52
  65.3 6.8 %collective-permute-start.14 = (bf16[4,64,512]{2,1,0:T(8,128)(2,1)S(1)}, bf16[4,64,512]{2,1,0:T(8,128)(2,1)S(1)}, u32[]{:S(2)}, u32[]{:S(2)}) collective-permute-start(bf16[4,64,512]{2,1,0:T(8,128)(2,1)S(1)} %add_terms.11.refs_4_), channel_id=1, source_target_pairs={{0,8},{4,20},{8,0},{12,28},{16,24},{20,4},{24,16},{28,12},{1,9},{5... | collective-permute-start | bytes 786440 | tf_op jit(solution)/shard_map/ppermute | solution.py:52
  66.9 7.8 %collective-permute-start.24 = (bf16[4,64,512]{2,1,0:T(8,128)(2,1)S(1)}, bf16[4,64,512]{2,1,0:T(8,128)(2,1)S(1)}, u32[]{:S(2)}, u32[]{:S(2)}) collective-permute-start(bf16[4,64,512]{2,1,0:T(8,128)(2,1)S(1)} %stack_planes.6.refs_3_.refs_0_), channel_id=1, source_target_pairs={{0,8},{4,20},{8,0},{12,28},{16,24},{20,4},{24,16},{28,12},{1,9},{5... | collective-permute-start | bytes 786440 | tf_op jit(solution)/shard_map/ppermute | solution.py:52
  67.6 15.8 %collective-permute-start.25 = (bf16[4,64,512]{2,1,0:T(8,128)(2,1)S(1)}, bf16[4,64,512]{2,1,0:T(8,128)(2,1)S(1)}, u32[]{:S(2)}, u32[]{:S(2)}) collective-permute-start(bf16[4,64,512]{2,1,0:T(8,128)(2,1)S(1)} %stack_planes.6.refs_3_.refs_0_), channel_id=1, source_target_pairs={{0,16},{4,12},{8,24},{12,4},{16,0},{20,28},{24,8},{28,20},{1,17},{... | collective-permute-start | bytes 786440 | tf_op jit(solution)/shard_map/ppermute | solution.py:52
  74.7 8.8 %collective-permute-start.26 = (bf16[4,64,512]{2,1,0:T(8,128)(2,1)S(1)}, bf16[4,64,512]{2,1,0:T(8,128)(2,1)S(1)}, u32[]{:S(2)}, u32[]{:S(2)}) collective-permute-start(bf16[4,64,512]{2,1,0:T(8,128)(2,1)S(1)} %collective-permute-done.24.refs_1_), channel_id=1, source_target_pairs={{0,16},{4,12},{8,24},{12,4},{16,0},{20,28},{24,8},{28,20},{1,17},{... | collective-permute-start | bytes 786440 | tf_op jit(solution)/shard_map/ppermute | solution.py:52
  75.2 6.2 %collective-permute-start.18 = (bf16[64,512]{1,0:T(8,128)(2,1)S(1)}, bf16[64,512]{1,0:T(8,128)(2,1)S(1)}, u32[]{:S(2)}, u32[]{:S(2)}) collective-permute-start(bf16[64,512]{1,0:T(8,128)(2,1)S(1)} %get-tuple-element.87), channel_id=1, source_target_pairs={{0,1},{1,2},{2,3},{3,0},{4,5},{5,6},{6,7},{7,4},{8,9},{9,10},{10,1... | collective-permute-start | bytes 196616 | tf_op jit(solution)/shard_map/ppermute | solution.py:107
  76.1 6.7 %collective-permute-start.19 = (bf16[64,512]{1,0:T(8,128)(2,1)S(1)}, bf16[64,512]{1,0:T(8,128)(2,1)S(1)}, u32[]{:S(2)}, u32[]{:S(2)}) collective-permute-start(bf16[64,512]{1,0:T(8,128)(2,1)S(1)} %get-tuple-element.86), channel_id=1, source_target_pairs={{0,2},{1,3},{2,0},{3,1},{4,6},{5,7},{6,4},{7,5},{8,10},{9,11},{10,... | collective-permute-start | bytes 196616 | tf_op jit(solution)/shard_map/ppermute | solution.py:107
  79.1 4.3 %collective-permute-start.20 = (bf16[64,512]{1,0:T(8,128)(2,1)S(1)}, bf16[64,512]{1,0:T(8,128)(2,1)S(1)}, u32[]{:S(2)}, u32[]{:S(2)}) collective-permute-start(bf16[64,512]{1,0:T(8,128)(2,1)S(1)} %get-tuple-element.85), channel_id=1, source_target_pairs={{0,3},{1,0},{2,1},{3,2},{4,7},{5,4},{6,5},{7,6},{8,11},{9,8},{10,9... | collective-permute-start | bytes 196616 | tf_op jit(solution)/shard_map/ppermute | solution.py:107
  83.5 9.0 %slice-start = ((s8[8388608]{0:T(1024)(128)(4,1)}), s8[4194304]{0:T(1024)(128)(4,1)S(1)}, s32[]{:S(2)}) async-start(s8[8388608]{0:T(1024)(128)(4,1)} %bitcast.36), calls=%async_computation | async-start | bytes 8388608
  83.6 4.2 %collective-permute-start.27 = (bf16[4,4,64,512]{3,2,1,0:T(8,128)(2,1)S(1)}, bf16[4,4,64,512]{3,2,1,0:T(8,128)(2,1)S(1)}, u32[]{:S(2)}, u32[]{:S(2)}) collective-permute-start(bf16[4,4,64,512]{3,2,1,0:T(8,128)(2,1)S(1)} %stack_planes.8.refs_0_.refs_4_), channel_id=1, source_target_pairs={{0,4},{4,0},{8,12},{12,8},{16,20},{20,16},{24,28},{28,24},{1,5},{5... | collective-permute-start | bytes 3145736 | tf_op jit(solution)/shard_map/ppermute | solution.py:515
  83.6 11.4 %collective-permute-start.21 = (bf16[4,64,512]{2,1,0:T(8,128)(2,1)S(1)}, bf16[4,64,512]{2,1,0:T(8,128)(2,1)S(1)}, u32[]{:S(2)}, u32[]{:S(2)}) collective-permute-start(bf16[4,64,512]{2,1,0:T(8,128)(2,1)S(1)} %stack_planes.7.refs_4_.refs_0_), channel_id=1, source_target_pairs={{0,8},{4,20},{8,0},{12,28},{16,24},{20,4},{24,16},{28,12},{1,9},{5... | collective-permute-start | bytes 786440 | tf_op jit(solution)/shard_map/ppermute | solution.py:99
  85.8 9.3 %collective-permute-start.22 = (bf16[4,64,512]{2,1,0:T(8,128)(2,1)S(1)}, bf16[4,64,512]{2,1,0:T(8,128)(2,1)S(1)}, u32[]{:S(2)}, u32[]{:S(2)}) collective-permute-start(bf16[4,64,512]{2,1,0:T(8,128)(2,1)S(1)} %stack_planes.7.refs_4_.refs_0_), channel_id=1, source_target_pairs={{0,16},{4,12},{8,24},{12,4},{16,0},{20,28},{24,8},{28,20},{1,17},{... | collective-permute-start | bytes 786440 | tf_op jit(solution)/shard_map/ppermute | solution.py:99
  87.7 12.0 %collective-permute-start.23 = (bf16[4,64,512]{2,1,0:T(8,128)(2,1)S(1)}, bf16[4,64,512]{2,1,0:T(8,128)(2,1)S(1)}, u32[]{:S(2)}, u32[]{:S(2)}) collective-permute-start(bf16[4,64,512]{2,1,0:T(8,128)(2,1)S(1)} %stack_planes.7.refs_4_.refs_0_), channel_id=1, source_target_pairs={{0,24},{4,28},{8,16},{12,20},{16,8},{20,12},{24,0},{28,4},{1,25},{... | collective-permute-start | bytes 786440 | tf_op jit(solution)/shard_map/ppermute | solution.py:99
  99.8 5.7 %collective-permute-start.28 = (bf16[4,4,64,512]{3,2,1,0:T(8,128)(2,1)S(1)}, bf16[4,4,64,512]{3,2,1,0:T(8,128)(2,1)S(1)}, u32[]{:S(2)}, u32[]{:S(2)}) collective-permute-start(bf16[4,4,64,512]{3,2,1,0:T(8,128)(2,1)S(1)} %stack_planes.9.refs_4_.refs_0_), channel_id=1, source_target_pairs={{0,4},{4,0},{8,12},{12,8},{16,20},{20,16},{24,28},{28,24},{1,5},{5... | collective-permute-start | bytes 3145736 | tf_op jit(solution)/shard_map/ppermute | solution.py:515
  99.8 3.0 %collective-permute-start.29 = (bf16[4,64,512]{2,1,0:T(8,128)(2,1)S(1)}, bf16[4,64,512]{2,1,0:T(8,128)(2,1)S(1)}, u32[]{:S(2)}, u32[]{:S(2)}) collective-permute-start(bf16[4,64,512]{2,1,0:T(8,128)(2,1)S(1)} %get-tuple-element.54), channel_id=1, source_target_pairs={{0,4},{4,0},{8,12},{12,8},{16,20},{20,16},{24,28},{28,24},{1,5},{5... | collective-permute-start | bytes 786440 | tf_op jit(solution)/shard_map/ppermute | solution.py:515
  100.3 2.9 %collective-permute-start.30 = (bf16[4,64,512]{2,1,0:T(8,128)(2,1)S(1)}, bf16[4,64,512]{2,1,0:T(8,128)(2,1)S(1)}, u32[]{:S(2)}, u32[]{:S(2)}) collective-permute-start(bf16[4,64,512]{2,1,0:T(8,128)(2,1)S(1)} %get-tuple-element.56), channel_id=1, source_target_pairs={{0,4},{4,0},{8,12},{12,8},{16,20},{20,16},{24,28},{28,24},{1,5},{5... | collective-permute-start | bytes 786440 | tf_op jit(solution)/shard_map/ppermute | solution.py:515
  100.4 9.7 %collective-permute-start.31 = (bf16[4,64,512]{2,1,0:T(8,128)(2,1)S(1)}, bf16[4,64,512]{2,1,0:T(8,128)(2,1)S(1)}, u32[]{:S(2)}, u32[]{:S(2)}) collective-permute-start(bf16[4,64,512]{2,1,0:T(8,128)(2,1)S(1)} %get-tuple-element.59), channel_id=1, source_target_pairs={{0,4},{4,0},{8,12},{12,8},{16,20},{20,16},{24,28},{28,24},{1,5},{5... | collective-permute-start | bytes 786440 | tf_op jit(solution)/shard_map/ppermute | solution.py:515
  103.4 6.8 %collective-permute-start.32 = (bf16[4,64,512]{2,1,0:T(8,128)(2,1)S(1)}, bf16[4,64,512]{2,1,0:T(8,128)(2,1)S(1)}, u32[]{:S(2)}, u32[]{:S(2)}) collective-permute-start(bf16[4,64,512]{2,1,0:T(8,128)(2,1)S(1)} %get-tuple-element.60), channel_id=1, source_target_pairs={{0,16},{4,12},{8,24},{12,4},{16,0},{20,28},{24,8},{28,20},{1,17},{... | collective-permute-start | bytes 786440 | tf_op jit(solution)/shard_map/ppermute | solution.py:52
  103.4 10.4 %collective-permute-start.37 = (bf16[4,64,512]{2,1,0:T(8,128)(2,1)S(1)}, bf16[4,64,512]{2,1,0:T(8,128)(2,1)S(1)}, u32[]{:S(2)}, u32[]{:S(2)}) collective-permute-start(bf16[4,64,512]{2,1,0:T(8,128)(2,1)S(1)} %get-tuple-element.51.refs_3_), channel_id=1, source_target_pairs={{0,4},{4,0},{8,12},{12,8},{16,20},{20,16},{24,28},{28,24},{1,5},{5... | collective-permute-start | bytes 786440 | tf_op jit(solution)/shard_map/ppermute | solution.py:515
  105.0 8.9 %collective-permute-start.38 = (bf16[4,64,512]{2,1,0:T(8,128)(2,1)S(1)}, bf16[4,64,512]{2,1,0:T(8,128)(2,1)S(1)}, u32[]{:S(2)}, u32[]{:S(2)}) collective-permute-start(bf16[4,64,512]{2,1,0:T(8,128)(2,1)S(1)} %get-tuple-element.57.refs_4_), channel_id=1, source_target_pairs={{0,16},{4,12},{8,24},{12,4},{16,0},{20,28},{24,8},{28,20},{1,17},{... | collective-permute-start | bytes 786440 | tf_op jit(solution)/shard_map/ppermute | solution.py:52
  111.5 6.4 %collective-permute-start.39 = (bf16[4,64,512]{2,1,0:T(8,128)(2,1)S(1)}, bf16[4,64,512]{2,1,0:T(8,128)(2,1)S(1)}, u32[]{:S(2)}, u32[]{:S(2)}) collective-permute-start(bf16[4,64,512]{2,1,0:T(8,128)(2,1)S(1)} %add_terms.14.refs_3_), channel_id=1, source_target_pairs={{0,8},{4,20},{8,0},{12,28},{16,24},{20,4},{24,16},{28,12},{1,9},{5... | collective-permute-start | bytes 786440 | tf_op jit(solution)/shard_map/ppermute | solution.py:52
  113.4 4.8 %collective-permute-start.33 = (bf16[4,64,512]{2,1,0:T(8,128)(2,1)S(1)}, bf16[4,64,512]{2,1,0:T(8,128)(2,1)S(1)}, u32[]{:S(2)}, u32[]{:S(2)}) collective-permute-start(bf16[4,64,512]{2,1,0:T(8,128)(2,1)S(1)} %get-tuple-element.61.refs_3_), channel_id=1, source_target_pairs={{0,4},{4,0},{8,12},{12,8},{16,20},{20,16},{24,28},{28,24},{1,5},{5... | collective-permute-start | bytes 786440 | tf_op jit(solution)/shard_map/ppermute | solution.py:515
  113.4 4.8 %collective-permute-start.34 = (bf16[4,64,512]{2,1,0:T(8,128)(2,1)S(1)}, bf16[4,64,512]{2,1,0:T(8,128)(2,1)S(1)}, u32[]{:S(2)}, u32[]{:S(2)}) collective-permute-start(bf16[4,64,512]{2,1,0:T(8,128)(2,1)S(1)} %get-tuple-element.64), channel_id=1, source_target_pairs={{0,4},{4,0},{8,12},{12,8},{16,20},{20,16},{24,28},{28,24},{1,5},{5... | collective-permute-start | bytes 786440 | tf_op jit(solution)/shard_map/ppermute | solution.py:515
  113.9 4.3 %collective-permute-start.35 = (bf16[4,64,512]{2,1,0:T(8,128)(2,1)S(1)}, bf16[4,64,512]{2,1,0:T(8,128)(2,1)S(1)}, u32[]{:S(2)}, u32[]{:S(2)}) collective-permute-start(bf16[4,64,512]{2,1,0:T(8,128)(2,1)S(1)} %get-tuple-element.66), channel_id=1, source_target_pairs={{0,4},{4,0},{8,12},{12,8},{16,20},{20,16},{24,28},{28,24},{1,5},{5... | collective-permute-start | bytes 786440 | tf_op jit(solution)/shard_map/ppermute | solution.py:515
  113.9 4.3 %collective-permute-start.36 = (bf16[4,64,512]{2,1,0:T(8,128)(2,1)S(1)}, bf16[4,64,512]{2,1,0:T(8,128)(2,1)S(1)}, u32[]{:S(2)}, u32[]{:S(2)}) collective-permute-start(bf16[4,64,512]{2,1,0:T(8,128)(2,1)S(1)} %get-tuple-element.68), channel_id=1, source_target_pairs={{0,4},{4,0},{8,12},{12,8},{16,20},{20,16},{24,28},{28,24},{1,5},{5... | collective-permute-start | bytes 786440 | tf_op jit(solution)/shard_map/ppermute | solution.py:515
  118.4 9.2 %collective-permute-start.40 = (bf16[4,64,512]{2,1,0:T(8,128)(2,1)S(1)}, bf16[4,64,512]{2,1,0:T(8,128)(2,1)S(1)}, u32[]{:S(2)}, u32[]{:S(2)}) collective-permute-start(bf16[4,64,512]{2,1,0:T(8,128)(2,1)S(1)} %get-tuple-element.70), channel_id=1, source_target_pairs={{0,8},{4,20},{8,0},{12,28},{16,24},{20,4},{24,16},{28,12},{1,9},{5... | collective-permute-start | bytes 786440 | tf_op jit(solution)/shard_map/ppermute | solution.py:99
  120.2 9.9 %collective-permute-start.41 = (bf16[4,64,512]{2,1,0:T(8,128)(2,1)S(1)}, bf16[4,64,512]{2,1,0:T(8,128)(2,1)S(1)}, u32[]{:S(2)}, u32[]{:S(2)}) collective-permute-start(bf16[4,64,512]{2,1,0:T(8,128)(2,1)S(1)} %get-tuple-element.71), channel_id=1, source_target_pairs={{0,16},{4,12},{8,24},{12,4},{16,0},{20,28},{24,8},{28,20},{1,17},{... | collective-permute-start | bytes 786440 | tf_op jit(solution)/shard_map/ppermute | solution.py:99
  120.4 12.5 %collective-permute-start.42 = (bf16[4,64,512]{2,1,0:T(8,128)(2,1)S(1)}, bf16[4,64,512]{2,1,0:T(8,128)(2,1)S(1)}, u32[]{:S(2)}, u32[]{:S(2)}) collective-permute-start(bf16[4,64,512]{2,1,0:T(8,128)(2,1)S(1)} %get-tuple-element.72), channel_id=1, source_target_pairs={{0,24},{4,28},{8,16},{12,20},{16,8},{20,12},{24,0},{28,4},{1,25},{... | collective-permute-start | bytes 786440 | tf_op jit(solution)/shard_map/ppermute | solution.py:99
  122.0 14.1 %collective-permute-start.46 = (bf16[64,512]{1,0:T(8,128)(2,1)S(1)}, bf16[64,512]{1,0:T(8,128)(2,1)S(1)}, u32[]{:S(2)}, u32[]{:S(2)}) collective-permute-start(bf16[64,512]{1,0:T(8,128)(2,1)S(1)} %get-tuple-element.79), channel_id=1, source_target_pairs={{0,1},{1,2},{2,3},{3,0},{4,5},{5,6},{6,7},{7,4},{8,9},{9,10},{10,1... | collective-permute-start | bytes 196616 | tf_op jit(solution)/shard_map/ppermute | solution.py:107
  122.6 14.3 %collective-permute-start.47 = (bf16[64,512]{1,0:T(8,128)(2,1)S(1)}, bf16[64,512]{1,0:T(8,128)(2,1)S(1)}, u32[]{:S(2)}, u32[]{:S(2)}) collective-permute-start(bf16[64,512]{1,0:T(8,128)(2,1)S(1)} %get-tuple-element.78), channel_id=1, source_target_pairs={{0,2},{1,3},{2,0},{3,1},{4,6},{5,7},{6,4},{7,5},{8,10},{9,11},{10,... | collective-permute-start | bytes 196616 | tf_op jit(solution)/shard_map/ppermute | solution.py:107
  127.7 9.3 %collective-permute-start.48 = (bf16[64,512]{1,0:T(8,128)(2,1)S(1)}, bf16[64,512]{1,0:T(8,128)(2,1)S(1)}, u32[]{:S(2)}, u32[]{:S(2)}) collective-permute-start(bf16[64,512]{1,0:T(8,128)(2,1)S(1)} %get-tuple-element.77), channel_id=1, source_target_pairs={{0,3},{1,0},{2,1},{3,2},{4,7},{5,4},{6,5},{7,6},{8,11},{9,8},{10,9... | collective-permute-start | bytes 196616 | tf_op jit(solution)/shard_map/ppermute | solution.py:107
  133.1 6.2 %collective-permute-start.43 = (bf16[64,512]{1,0:T(8,128)(2,1)S(1)}, bf16[64,512]{1,0:T(8,128)(2,1)S(1)}, u32[]{:S(2)}, u32[]{:S(2)}) collective-permute-start(bf16[64,512]{1,0:T(8,128)(2,1)S(1)} %get-tuple-element.83), channel_id=1, source_target_pairs={{0,1},{1,2},{2,3},{3,0},{4,5},{5,6},{6,7},{7,4},{8,9},{9,10},{10,1... | collective-permute-start | bytes 196616 | tf_op jit(solution)/shard_map/ppermute | solution.py:107
  133.7 6.9 %collective-permute-start.44 = (bf16[64,512]{1,0:T(8,128)(2,1)S(1)}, bf16[64,512]{1,0:T(8,128)(2,1)S(1)}, u32[]{:S(2)}, u32[]{:S(2)}) collective-permute-start(bf16[64,512]{1,0:T(8,128)(2,1)S(1)} %get-tuple-element.82), channel_id=1, source_target_pairs={{0,2},{1,3},{2,0},{3,1},{4,6},{5,7},{6,4},{7,5},{8,10},{9,11},{10,... | collective-permute-start | bytes 196616 | tf_op jit(solution)/shard_map/ppermute | solution.py:107
  136.1 4.7 %collective-permute-start.45 = (bf16[64,512]{1,0:T(8,128)(2,1)S(1)}, bf16[64,512]{1,0:T(8,128)(2,1)S(1)}, u32[]{:S(2)}, u32[]{:S(2)}) collective-permute-start(bf16[64,512]{1,0:T(8,128)(2,1)S(1)} %get-tuple-element.81), channel_id=1, source_target_pairs={{0,3},{1,0},{2,1},{3,2},{4,7},{5,4},{6,5},{7,6},{8,11},{9,8},{10,9... | collective-permute-start | bytes 196616 | tf_op jit(solution)/shard_map/ppermute | solution.py:107
  137.0 6.6 %collective-permute-start.52 = (bf16[4,64,512]{2,1,0:T(8,128)(2,1)S(1)}, bf16[4,64,512]{2,1,0:T(8,128)(2,1)S(1)}, u32[]{:S(2)}, u32[]{:S(2)}) collective-permute-start(bf16[4,64,512]{2,1,0:T(8,128)(2,1)S(1)} %stack_planes.10.refs_4_.refs_1_), channel_id=1, source_target_pairs={{0,8},{4,20},{8,0},{12,28},{16,24},{20,4},{24,16},{28,12},{1,9},{5... | collective-permute-start | bytes 786440 | tf_op jit(solution)/shard_map/ppermute | solution.py:52
  140.8 9.2 %collective-permute-start.49 = (bf16[4,64,512]{2,1,0:T(8,128)(2,1)S(1)}, bf16[4,64,512]{2,1,0:T(8,128)(2,1)S(1)}, u32[]{:S(2)}, u32[]{:S(2)}) collective-permute-start(bf16[4,64,512]{2,1,0:T(8,128)(2,1)S(1)} %stack_planes.11.refs_1_), channel_id=1, source_target_pairs={{0,8},{4,20},{8,0},{12,28},{16,24},{20,4},{24,16},{28,12},{1,9},{5... | collective-permute-start | bytes 786440 | tf_op jit(solution)/shard_map/ppermute | solution.py:52
  142.3 10.4 %collective-permute-start.53 = (bf16[4,64,512]{2,1,0:T(8,128)(2,1)S(1)}, bf16[4,64,512]{2,1,0:T(8,128)(2,1)S(1)}, u32[]{:S(2)}, u32[]{:S(2)}) collective-permute-start(bf16[4,64,512]{2,1,0:T(8,128)(2,1)S(1)} %stack_planes.10.refs_4_.refs_1_), channel_id=1, source_target_pairs={{0,16},{4,12},{8,24},{12,4},{16,0},{20,28},{24,8},{28,20},{1,17},{... | collective-permute-start | bytes 786440 | tf_op jit(solution)/shard_map/ppermute | solution.py:52
  143.6 9.2 %collective-permute-start.54 = (bf16[4,64,512]{2,1,0:T(8,128)(2,1)S(1)}, bf16[4,64,512]{2,1,0:T(8,128)(2,1)S(1)}, u32[]{:S(2)}, u32[]{:S(2)}) collective-permute-start(bf16[4,64,512]{2,1,0:T(8,128)(2,1)S(1)} %collective-permute-done.52.refs_2_), channel_id=1, source_target_pairs={{0,16},{4,12},{8,24},{12,4},{16,0},{20,28},{24,8},{28,20},{1,17},{... | collective-permute-start | bytes 786440 | tf_op jit(solution)/shard_map/ppermute | solution.py:52
  146.2 8.1 %collective-permute-start.50 = (bf16[4,64,512]{2,1,0:T(8,128)(2,1)S(1)}, bf16[4,64,512]{2,1,0:T(8,128)(2,1)S(1)}, u32[]{:S(2)}, u32[]{:S(2)}) collective-permute-start(bf16[4,64,512]{2,1,0:T(8,128)(2,1)S(1)} %stack_planes.11.refs_1_), channel_id=1, source_target_pairs={{0,16},{4,12},{8,24},{12,4},{16,0},{20,28},{24,8},{28,20},{1,17},{... | collective-permute-start | bytes 786440 | tf_op jit(solution)/shard_map/ppermute | solution.py:52
  150.1 7.0 %collective-permute-start.51 = (bf16[4,64,512]{2,1,0:T(8,128)(2,1)S(1)}, bf16[4,64,512]{2,1,0:T(8,128)(2,1)S(1)}, u32[]{:S(2)}, u32[]{:S(2)}) collective-permute-start(bf16[4,64,512]{2,1,0:T(8,128)(2,1)S(1)} %collective-permute-done.49.refs_2_), channel_id=1, source_target_pairs={{0,16},{4,12},{8,24},{12,4},{16,0},{20,28},{24,8},{28,20},{1,17},{... | collective-permute-start | bytes 786440 | tf_op jit(solution)/shard_map/ppermute | solution.py:52
  158.1 2.0 %collective-permute-start.55 = (bf16[8,64,512]{2,1,0:T(8,128)(2,1)S(1)}, bf16[8,64,512]{2,1,0:T(8,128)(2,1)S(1)}, u32[]{:S(2)}, u32[]{:S(2)}) collective-permute-start(bf16[8,64,512]{2,1,0:T(8,128)(2,1)S(1)} %add_expert_rows.5), channel_id=1, source_target_pairs={{0,4},{4,0},{8,12},{12,8},{16,20},{20,16},{24,28},{28,24},{1,5},{5... | collective-permute-start | bytes 1572872 | tf_op jit(solution)/shard_map/ppermute | solution.py:515
  (2 other events, 13.4 us)

commit v11 on v10

--- a/solution.py
+++ b/solution.py
@@ -8,7 +8,7 @@
 BLK = 128
 CAP = 4
 GROUPS = 2
-DIRECT = ((0, 0, 0, 0), (0, 1, 1, 0))
+DIRECT = ((0, 0, 0, 0), (0, 1, 1, 1))
 PICK_WAIT = (0, 0)
 HOP_WAIT = ((0, 0), (0, 0))
 ORDER = '001010110000101011011011'

time: 161 us -> 163 us (1.012)
  waiting for transfers between devices: 61.8 us -> 65.5 us
  starting transfers between devices: 66.8 us -> 65 us
    ppermute x6 -> x9, waiting for transfers between devices: 10.1 us -> 17.4 us  [direct(): out.append(lax.ppermute(value, 'dp', pairs) if r else value)]
    ppermute x24 -> x21, starting transfers between devices: 35.1 us -> 29.4 us  [exchange(): return lax.ppermute(value, 'dp', step_pairs(n_dp, step))]
    ppermute x6 -> x9, starting transfers between devices: 7.65 us -> 11.2 us  [direct(): out.append(lax.ppermute(value, 'dp', pairs) if r else value)]
    ppermute x24 -> x21, waiting for transfers between devices: 38.6 us -> 35.7 us  [exchange(): return lax.ppermute(value, 'dp', step_pairs(n_dp, step))]
where the time goes in v11:
time: 163 us
  waiting for transfers between devices  65.5 us (40%)
  starting transfers between devices  65 us (40%)
  Pallas kernels  29.3 us (18%)
  local copies, waits for them, and re-layouts  2.81 us (2%)
    ppermute x21, waiting for transfers between devices, exchange(): return lax.ppermute(value, 'dp', step_pairs(n_dp, step))  35.7 us
    ppermute x21, starting transfers between devices, exchange(): return lax.ppermute(value, 'dp', step_pairs(n_dp, step))  29.4 us
    ppermute x12, starting transfers between devices, swap_planes(): out.append(lax.ppermute(parts[k], 'expert', pairs))  19.9 us
    ppermute x9, waiting for transfers between devices, direct(): out.append(lax.ppermute(value, 'dp', pairs) if r else value)  17.4 us
    ppermute x9, starting transfers between devices, direct(): out.append(lax.ppermute(value, 'dp', pairs) if r else value)  11.2 us
    pallas_call x2, Pallas kernels, hidden_units(): call(lambda *refs: hidden_kernel(make_place, reverse, *refs), jax.ShapeDt...  9.29 us
    ppermute x14, waiting for transfers between devices, to_partner(): return lax.ppermute(value, 'dp', pair)  6.32 us
    ppermute x12, waiting for transfers between devices, swap_planes(): out.append(lax.ppermute(parts[k], 'expert', pairs))  6.13 us
  transfers between devices with their start and end apart: 56, of which 24 were waited for; matrix products, arithmetic and copies ran while one was open for 2% of the time, Pallas kernels for 15%

profile of v11, /device:TPU:0, one launch (start us, length us, event | category | flops | bytes accessed | tf_op | source)
XLA Modules:
  0.0 163.2 jit_solution(17011408296774459131)
XLA Ops:
  0.5 1.4 constant_dynamic-slice_fusion.2
  2.0 2.9 %collective-permute-start.4 = (bf16[512,512]{1,0:T(8,128)(2,1)S(1)}, bf16[512,512]{1,0:T(8,128)(2,1)S(1)}, u32[]{:S(2)}, u32[]{:S(2)}) collective-permute-start(bf16[512,512]{1,0:T(8,128)(2,1)S(1)} %get-tuple-element.76.refs_2_), channel_id=1, source_target_pairs={{0,8},{4,20},{8,0},{12,28},{16,24},{20,4},{24,16},{28,12},{1,9},{5... | collective-permute-start | bytes 1572872 | tf_op jit(solution)/shard_map/ppermute | solution.py:52
  4.9 3.1 %collective-permute-done.2.refs_3_ = bf16[512,512]{1,0:T(8,128)(2,1)S(1)} collective-permute-done((bf16[512,512]{1,0:T(8,128)(2,1)S(1)}, bf16[512,512]{1,0:T(8,128)(2,1)S(1)}, u32[]{:S(2)}, u32[]{:S(2)}) %collective-permute-start.2) | collective-permute-done | bytes 524320 | tf_op jit(solution)/shard_map/ppermute | solution.py:515
  8.0 2.9 %collective-permute-start.5 = (bf16[512,512]{1,0:T(8,128)(2,1)S(1)}, bf16[512,512]{1,0:T(8,128)(2,1)S(1)}, u32[]{:S(2)}, u32[]{:S(2)}) collective-permute-start(bf16[512,512]{1,0:T(8,128)(2,1)S(1)} %collective-permute-done.2.refs_3_), channel_id=1, source_target_pairs={{0,8},{4,20},{8,0},{12,28},{16,24},{20,4},{24,16},{28,12},{1,9},{5... | collective-permute-start | bytes 1572872 | tf_op jit(solution)/shard_map/ppermute | solution.py:52
  10.9 1.5 collective-permute-start.1
  12.4 1.3 constant_dynamic-slice_fusion
  13.7 0.9 collective-permute-start.3
  14.6 8.2 %collective-permute-done.5.refs_5_ = bf16[512,512]{1,0:T(8,128)(2,1)S(1)} collective-permute-done((bf16[512,512]{1,0:T(8,128)(2,1)S(1)}, bf16[512,512]{1,0:T(8,128)(2,1)S(1)}, u32[]{:S(2)}, u32[]{:S(2)}) %collective-permute-start.5) | collective-permute-done | bytes 524320 | tf_op jit(solution)/shard_map/ppermute | solution.py:52
  22.8 3.0 %collective-permute-start.7 = (bf16[512,512]{1,0:T(8,128)(2,1)S(1)}, bf16[512,512]{1,0:T(8,128)(2,1)S(1)}, u32[]{:S(2)}, u32[]{:S(2)}) collective-permute-start(bf16[512,512]{1,0:T(8,128)(2,1)S(1)} %collective-permute-done.4.refs_4_), channel_id=1, source_target_pairs={{0,16},{4,12},{8,24},{12,4},{16,0},{20,28},{24,8},{28,20},{1,17},{... | collective-permute-start | bytes 1572872 | tf_op jit(solution)/shard_map/ppermute | solution.py:52
  26.6 3.4 %project.2.refs_4_ = f32[2,512,512]{2,1,0:T(8,128)S(1)} custom-call(bf16[512,4096]{1,0:T(8,128)(2,1)S(1)} %copy-done, bf16[512,4096]{1,0:T(8,128)(2,1)} %collective-permute-done.refs_1_, bf16[512,512]{1,0:T(8,128)(2,1)S(1)} %get-tuple-element.76.refs_2_, bf16[512,512]{1,0:T(8,128)(2,1)S(1)} %collective-permute-done.2.refs_3_, ...), custom_call_target="tpu_custom_call" | custom-call | tf_op jit(solution)/shard_map/project/pallas_call | solution.py:250
  30.1 2.4 %project.3 = (f32[2,512,512]{2,1,0:T(8,128)S(1)}, bf16[2,512,1024]{2,1,0:T(8,128)(2,1)S(1)}) custom-call(bf16[512,4096]{1,0:T(8,128)(2,1)S(1)} %copy-done, bf16[512,4096]{1,0:T(8,128)(2,1)} %collective-permute-done.refs_1_, bf16[512,512]{1,0:T(8,128)(2,1)S(1)} %collective-permute-done.1.refs_2_, bf16[512,512]{1,0:T(8,128)(2,1)S(1)} %collective-permute-done.3.refs_3_, ...), custom_call_target="tpu_custom_call" | custom-call | tf_op jit(solution)/shard_map/project/pallas_call | solution.py:250
  32.5 1.8 %collective-permute-done.7.refs_0_ = bf16[512,512]{1,0:T(8,128)(2,1)S(1)} collective-permute-done((bf16[512,512]{1,0:T(8,128)(2,1)S(1)}, bf16[512,512]{1,0:T(8,128)(2,1)S(1)}, u32[]{:S(2)}, u32[]{:S(2)}) %collective-permute-start.7) | collective-permute-done | bytes 524320 | tf_op jit(solution)/shard_map/ppermute | solution.py:52
  34.3 5.6 %collective-permute-done.8.refs_1_ = bf16[512,512]{1,0:T(8,128)(2,1)S(1)} collective-permute-done((bf16[512,512]{1,0:T(8,128)(2,1)S(1)}, bf16[512,512]{1,0:T(8,128)(2,1)S(1)}, u32[]{:S(2)}, u32[]{:S(2)}) %collective-permute-start.8) | collective-permute-done | bytes 524320 | tf_op jit(solution)/shard_map/ppermute | solution.py:52
  40.0 1.2 project_last.1
  42.0 1.8 %collective-permute-start.9 = (bf16[4,64,512]{2,1,0:T(8,128)(2,1)S(1)}, bf16[4,64,512]{2,1,0:T(8,128)(2,1)S(1)}, u32[]{:S(2)}, u32[]{:S(2)}) collective-permute-start(bf16[4,64,512]{2,1,0:T(8,128)(2,1)S(1)} %get-tuple-element.44), channel_id=1, source_target_pairs={{0,16},{4,12},{8,24},{12,4},{16,0},{20,28},{24,8},{28,20},{1,17},{... | collective-permute-start | bytes 786440 | tf_op jit(solution)/shard_map/ppermute | solution.py:52
  44.1 4.3 %collective-permute-done.9.refs_1_ = bf16[4,64,512]{2,1,0:T(8,128)(2,1)S(1)} collective-permute-done((bf16[4,64,512]{2,1,0:T(8,128)(2,1)S(1)}, bf16[4,64,512]{2,1,0:T(8,128)(2,1)S(1)}, u32[]{:S(2)}, u32[]{:S(2)}) %collective-permute-start.9) | collective-permute-done | bytes 262176 | tf_op jit(solution)/shard_map/ppermute | solution.py:52
  48.6 1.8 %collective-permute-start.13 = (bf16[4,64,512]{2,1,0:T(8,128)(2,1)S(1)}, bf16[4,64,512]{2,1,0:T(8,128)(2,1)S(1)}, u32[]{:S(2)}, u32[]{:S(2)}) collective-permute-start(bf16[4,64,512]{2,1,0:T(8,128)(2,1)S(1)} %add_terms.9.refs_2_), channel_id=1, source_target_pairs={{0,8},{4,20},{8,0},{12,28},{16,24},{20,4},{24,16},{28,12},{1,9},{5... | collective-permute-start | bytes 786440 | tf_op jit(solution)/shard_map/ppermute | solution.py:52
  51.2 1.6 collective-permute-start.11
  52.7 4.2 %collective-permute-done.13.refs_2_ = bf16[4,64,512]{2,1,0:T(8,128)(2,1)S(1)} collective-permute-done((bf16[4,64,512]{2,1,0:T(8,128)(2,1)S(1)}, bf16[4,64,512]{2,1,0:T(8,128)(2,1)S(1)}, u32[]{:S(2)}, u32[]{:S(2)}) %collective-permute-start.13) | collective-permute-done | bytes 262176 | tf_op jit(solution)/shard_map/ppermute | solution.py:52
  57.1 2.1 %collective-permute-start.15 = (bf16[64,512]{1,0:T(8,128)(2,1)S(1)}, bf16[64,512]{1,0:T(8,128)(2,1)S(1)}, u32[]{:S(2)}, u32[]{:S(2)}) collective-permute-start(bf16[64,512]{1,0:T(8,128)(2,1)S(1)} %get-tuple-element.91), channel_id=1, source_target_pairs={{0,1},{1,2},{2,3},{3,0},{4,5},{5,6},{6,7},{7,4},{8,9},{9,10},{10,1... | collective-permute-start | bytes 196616 | tf_op jit(solution)/shard_map/ppermute | solution.py:107
  59.2 2.6 %collective-permute-start.16 = (bf16[64,512]{1,0:T(8,128)(2,1)S(1)}, bf16[64,512]{1,0:T(8,128)(2,1)S(1)}, u32[]{:S(2)}, u32[]{:S(2)}) collective-permute-start(bf16[64,512]{1,0:T(8,128)(2,1)S(1)} %get-tuple-element.90), channel_id=1, source_target_pairs={{0,2},{1,3},{2,0},{3,1},{4,6},{5,7},{6,4},{7,5},{8,10},{9,11},{10,... | collective-permute-start | bytes 196616 | tf_op jit(solution)/shard_map/ppermute | solution.py:107
  61.8 1.3 collective-permute-start.17
  63.1 2.1 %collective-permute-start.10 = (bf16[4,64,512]{2,1,0:T(8,128)(2,1)S(1)}, bf16[4,64,512]{2,1,0:T(8,128)(2,1)S(1)}, u32[]{:S(2)}, u32[]{:S(2)}) collective-permute-start(bf16[4,64,512]{2,1,0:T(8,128)(2,1)S(1)} %get-tuple-element.47), channel_id=1, source_target_pairs={{0,16},{4,12},{8,24},{12,4},{16,0},{20,28},{24,8},{28,20},{1,17},{... | collective-permute-start | bytes 786440 | tf_op jit(solution)/shard_map/ppermute | solution.py:52
  65.3 1.6 collective-permute-start.14
  67.6 2.1 %collective-permute-start.25 = (bf16[4,64,512]{2,1,0:T(8,128)(2,1)S(1)}, bf16[4,64,512]{2,1,0:T(8,128)(2,1)S(1)}, u32[]{:S(2)}, u32[]{:S(2)}) collective-permute-start(bf16[4,64,512]{2,1,0:T(8,128)(2,1)S(1)} %stack_planes.6.refs_3_.refs_0_), channel_id=1, source_target_pairs={{0,16},{4,12},{8,24},{12,4},{16,0},{20,28},{24,8},{28,20},{1,17},{... | collective-permute-start | bytes 786440 | tf_op jit(solution)/shard_map/ppermute | solution.py:52
  69.7 2.4 %collective-permute-done.10.refs_1_ = bf16[4,64,512]{2,1,0:T(8,128)(2,1)S(1)} collective-permute-done((bf16[4,64,512]{2,1,0:T(8,128)(2,1)S(1)}, bf16[4,64,512]{2,1,0:T(8,128)(2,1)S(1)}, u32[]{:S(2)}, u32[]{:S(2)}) %collective-permute-start.10) | collective-permute-done | bytes 262176 | tf_op jit(solution)/shard_map/ppermute | solution.py:52
  72.2 2.5 %collective-permute-done.24.refs_1_ = bf16[4,64,512]{2,1,0:T(8,128)(2,1)S(1)} collective-permute-done((bf16[4,64,512]{2,1,0:T(8,128)(2,1)S(1)}, bf16[4,64,512]{2,1,0:T(8,128)(2,1)S(1)}, u32[]{:S(2)}, u32[]{:S(2)}) %collective-permute-start.24) | collective-permute-done | bytes 262176 | tf_op jit(solution)/shard_map/ppermute | solution.py:52
  75.2 0.9 collective-permute-start.18
  76.1 3.0 %collective-permute-start.19 = (bf16[64,512]{1,0:T(8,128)(2,1)S(1)}, bf16[64,512]{1,0:T(8,128)(2,1)S(1)}, u32[]{:S(2)}, u32[]{:S(2)}) collective-permute-start(bf16[64,512]{1,0:T(8,128)(2,1)S(1)} %get-tuple-element.86), channel_id=1, source_target_pairs={{0,2},{1,3},{2,0},{3,1},{4,6},{5,7},{6,4},{7,5},{8,10},{9,11},{10,... | collective-permute-start | bytes 196616 | tf_op jit(solution)/shard_map/ppermute | solution.py:107
  79.1 2.3 %collective-permute-done.18.refs_1_ = bf16[64,512]{1,0:T(8,128)(2,1)S(1)} collective-permute-done((bf16[64,512]{1,0:T(8,128)(2,1)S(1)}, bf16[64,512]{1,0:T(8,128)(2,1)S(1)}, u32[]{:S(2)}, u32[]{:S(2)}) %collective-permute-start.18) | collective-permute-done | bytes 65568 | tf_op jit(solution)/shard_map/ppermute | solution.py:107
  81.4 1.3 collective-permute-done.19.refs_2_
  83.6 2.2 %collective-permute-start.21 = (bf16[4,64,512]{2,1,0:T(8,128)(2,1)S(1)}, bf16[4,64,512]{2,1,0:T(8,128)(2,1)S(1)}, u32[]{:S(2)}, u32[]{:S(2)}) collective-permute-start(bf16[4,64,512]{2,1,0:T(8,128)(2,1)S(1)} %stack_planes.7.refs_4_.refs_0_), channel_id=1, source_target_pairs={{0,8},{4,20},{8,0},{12,28},{16,24},{20,4},{24,16},{28,12},{1,9},{5... | collective-permute-start | bytes 786440 | tf_op jit(solution)/shard_map/ppermute | solution.py:99
  85.8 1.9 %collective-permute-start.22 = (bf16[4,64,512]{2,1,0:T(8,128)(2,1)S(1)}, bf16[4,64,512]{2,1,0:T(8,128)(2,1)S(1)}, u32[]{:S(2)}, u32[]{:S(2)}) collective-permute-start(bf16[4,64,512]{2,1,0:T(8,128)(2,1)S(1)} %stack_planes.7.refs_4_.refs_0_), channel_id=1, source_target_pairs={{0,16},{4,12},{8,24},{12,4},{16,0},{20,28},{24,8},{28,20},{1,17},{... | collective-permute-start | bytes 786440 | tf_op jit(solution)/shard_map/ppermute | solution.py:99
  87.8 4.6 %expert_hidden.2.refs_0_.refs_3_ = bf16[256,1024]{1,0:T(8,128)(2,1)S(1)} custom-call(bf16[4,4,64,512]{3,2,1,0:T(8,128)(2,1)S(1)} %stack_planes.8.refs_0_.refs_4_, bf16[4,4,64,512]{3,2,1,0:T(8,128)(2,1)S(1)} %collective-permute-done.27.refs_1_, bf16[4096,1024]{1,0:T(8,128)(2,1)S(1)} %bitcast.44, bf16[4096,1024]{1,0:T(8,128)(2,1)S(1)} %bitcast.48, ...), custom_call_target="tpu_custom_call" | custom-call | tf_op jit(solution)/shard_map/expert_hidden/pallas_call | solution.py:390
  92.5 1.3 expert_down.4
  93.8 1.3 expert_down.5
  95.1 4.6 %collective-permute-done.23.refs_3_ = bf16[4,64,512]{2,1,0:T(8,128)(2,1)S(1)} collective-permute-done((bf16[4,64,512]{2,1,0:T(8,128)(2,1)S(1)}, bf16[4,64,512]{2,1,0:T(8,128)(2,1)S(1)}, u32[]{:S(2)}, u32[]{:S(2)}) %collective-permute-start.23) | collective-permute-done | bytes 262176 | tf_op jit(solution)/shard_map/ppermute | solution.py:99
  100.8 2.0 %collective-permute-done.29.refs_1_ = bf16[4,64,512]{2,1,0:T(8,128)(2,1)S(1)} collective-permute-done((bf16[4,64,512]{2,1,0:T(8,128)(2,1)S(1)}, bf16[4,64,512]{2,1,0:T(8,128)(2,1)S(1)}, u32[]{:S(2)}, u32[]{:S(2)}) %collective-permute-start.29) | collective-permute-done | bytes 262176 | tf_op jit(solution)/shard_map/ppermute | solution.py:515
  103.4 1.6 collective-permute-start.37
  105.5 4.6 %expert_hidden.3.refs_3_.refs_0_ = bf16[256,1024]{1,0:T(8,128)(2,1)S(1)} custom-call(bf16[4,4,64,512]{3,2,1,0:T(8,128)(2,1)S(1)} %stack_planes.9.refs_4_.refs_0_, bf16[4,4,64,512]{3,2,1,0:T(8,128)(2,1)S(1)} %collective-permute-done.28.refs_1_, bf16[4096,1024]{1,0:T(8,128)(2,1)S(1)} %bitcast.45, bf16[4096,1024]{1,0:T(8,128)(2,1)S(1)} %bitcast.49, ...), custom_call_target="tpu_custom_call" | custom-call | tf_op jit(solution)/shard_map/expert_hidden/pallas_call | solution.py:390
  110.2 1.3 expert_down.6
  111.5 1.8 %collective-permute-start.39 = (bf16[4,64,512]{2,1,0:T(8,128)(2,1)S(1)}, bf16[4,64,512]{2,1,0:T(8,128)(2,1)S(1)}, u32[]{:S(2)}, u32[]{:S(2)}) collective-permute-start(bf16[4,64,512]{2,1,0:T(8,128)(2,1)S(1)} %add_terms.14.refs_3_), channel_id=1, source_target_pairs={{0,8},{4,20},{8,0},{12,28},{16,24},{20,4},{24,16},{28,12},{1,9},{5... | collective-permute-start | bytes 786440 | tf_op jit(solution)/shard_map/ppermute | solution.py:52
  114.4 1.3 expert_down.7
  115.6 2.3 %collective-permute-done.39.refs_3_ = bf16[4,64,512]{2,1,0:T(8,128)(2,1)S(1)} collective-permute-done((bf16[4,64,512]{2,1,0:T(8,128)(2,1)S(1)}, bf16[4,64,512]{2,1,0:T(8,128)(2,1)S(1)}, u32[]{:S(2)}, u32[]{:S(2)}) %collective-permute-start.39) | collective-permute-done | bytes 262176 | tf_op jit(solution)/shard_map/ppermute | solution.py:52
  118.4 1.8 %collective-permute-start.40 = (bf16[4,64,512]{2,1,0:T(8,128)(2,1)S(1)}, bf16[4,64,512]{2,1,0:T(8,128)(2,1)S(1)}, u32[]{:S(2)}, u32[]{:S(2)}) collective-permute-start(bf16[4,64,512]{2,1,0:T(8,128)(2,1)S(1)} %get-tuple-element.70), channel_id=1, source_target_pairs={{0,8},{4,20},{8,0},{12,28},{16,24},{20,4},{24,16},{28,12},{1,9},{5... | collective-permute-start | bytes 786440 | tf_op jit(solution)/shard_map/ppermute | solution.py:99
  120.4 1.5 collective-permute-start.42
  122.6 2.4 %collective-permute-start.47 = (bf16[64,512]{1,0:T(8,128)(2,1)S(1)}, bf16[64,512]{1,0:T(8,128)(2,1)S(1)}, u32[]{:S(2)}, u32[]{:S(2)}) collective-permute-start(bf16[64,512]{1,0:T(8,128)(2,1)S(1)} %get-tuple-element.78), channel_id=1, source_target_pairs={{0,2},{1,3},{2,0},{3,1},{4,6},{5,7},{6,4},{7,5},{8,10},{9,11},{10,... | collective-permute-start | bytes 196616 | tf_op jit(solution)/shard_map/ppermute | solution.py:107
  125.0 2.6 %collective-permute-done.40.refs_1_ = bf16[4,64,512]{2,1,0:T(8,128)(2,1)S(1)} collective-permute-done((bf16[4,64,512]{2,1,0:T(8,128)(2,1)S(1)}, bf16[4,64,512]{2,1,0:T(8,128)(2,1)S(1)}, u32[]{:S(2)}, u32[]{:S(2)}) %collective-permute-start.40) | collective-permute-done | bytes 262176 | tf_op jit(solution)/shard_map/ppermute | solution.py:99
  127.7 2.4 %collective-permute-start.48 = (bf16[64,512]{1,0:T(8,128)(2,1)S(1)}, bf16[64,512]{1,0:T(8,128)(2,1)S(1)}, u32[]{:S(2)}, u32[]{:S(2)}) collective-permute-start(bf16[64,512]{1,0:T(8,128)(2,1)S(1)} %get-tuple-element.77), channel_id=1, source_target_pairs={{0,3},{1,0},{2,1},{3,2},{4,7},{5,4},{6,5},{7,6},{8,11},{9,8},{10,9... | collective-permute-start | bytes 196616 | tf_op jit(solution)/shard_map/ppermute | solution.py:107
  130.1 2.8 %collective-permute-done.42.refs_3_ = bf16[4,64,512]{2,1,0:T(8,128)(2,1)S(1)} collective-permute-done((bf16[4,64,512]{2,1,0:T(8,128)(2,1)S(1)}, bf16[4,64,512]{2,1,0:T(8,128)(2,1)S(1)}, u32[]{:S(2)}, u32[]{:S(2)}) %collective-permute-start.42) | collective-permute-done | bytes 262176 | tf_op jit(solution)/shard_map/ppermute | solution.py:99
  133.1 1.1 collective-permute-start.52
  134.8 3.9 %collective-permute-start.44 = (bf16[64,512]{1,0:T(8,128)(2,1)S(1)}, bf16[64,512]{1,0:T(8,128)(2,1)S(1)}, u32[]{:S(2)}, u32[]{:S(2)}) collective-permute-start(bf16[64,512]{1,0:T(8,128)(2,1)S(1)} %get-tuple-element.82), channel_id=1, source_target_pairs={{0,2},{1,3},{2,0},{3,1},{4,6},{5,7},{6,4},{7,5},{8,10},{9,11},{10,... | collective-permute-start | bytes 196616 | tf_op jit(solution)/shard_map/ppermute | solution.py:107
  139.5 2.1 %collective-permute-start.54 = (bf16[4,64,512]{2,1,0:T(8,128)(2,1)S(1)}, bf16[4,64,512]{2,1,0:T(8,128)(2,1)S(1)}, u32[]{:S(2)}, u32[]{:S(2)}) collective-permute-start(bf16[4,64,512]{2,1,0:T(8,128)(2,1)S(1)} %collective-permute-done.52.refs_2_), channel_id=1, source_target_pairs={{0,16},{4,12},{8,24},{12,4},{16,0},{20,28},{24,8},{28,20},{1,17},{... | collective-permute-start | bytes 786440 | tf_op jit(solution)/shard_map/ppermute | solution.py:52
  141.6 1.6 collective-permute-done.44.refs_2_
  143.5 1.5 collective-permute-start.50
  145.0 2.0 %collective-permute-start.51 = (bf16[4,64,512]{2,1,0:T(8,128)(2,1)S(1)}, bf16[4,64,512]{2,1,0:T(8,128)(2,1)S(1)}, u32[]{:S(2)}, u32[]{:S(2)}) collective-permute-start(bf16[4,64,512]{2,1,0:T(8,128)(2,1)S(1)} %stack_planes.11.refs_1_), channel_id=1, source_target_pairs={{0,24},{4,28},{8,16},{12,20},{16,8},{20,12},{24,0},{28,4},{1,25},{... | collective-permute-start | bytes 786440 | tf_op jit(solution)/shard_map/ppermute | solution.py:99
  147.0 3.7 %collective-permute-done.54.refs_4_ = bf16[4,64,512]{2,1,0:T(8,128)(2,1)S(1)} collective-permute-done((bf16[4,64,512]{2,1,0:T(8,128)(2,1)S(1)}, bf16[4,64,512]{2,1,0:T(8,128)(2,1)S(1)}, u32[]{:S(2)}, u32[]{:S(2)}) %collective-permute-start.54) | collective-permute-done | bytes 262176 | tf_op jit(solution)/shard_map/ppermute | solution.py:52
  150.7 1.1 add_expert_rows.3.refs_5_
  151.8 1.0 collective-permute-done.49.refs_2_
  152.7 6.4 %collective-permute-done.50.refs_3_ = bf16[4,64,512]{2,1,0:T(8,128)(2,1)S(1)} collective-permute-done((bf16[4,64,512]{2,1,0:T(8,128)(2,1)S(1)}, bf16[4,64,512]{2,1,0:T(8,128)(2,1)S(1)}, u32[]{:S(2)}, u32[]{:S(2)}) %collective-permute-start.50) | collective-permute-done | bytes 262176 | tf_op jit(solution)/shard_map/ppermute | solution.py:99
  159.1 1.0 add_expert_rows.5
  160.2 1.0 add_expert_rows.4.refs_0_
  161.3 0.9 collective-permute-done.55.refs_1_
  162.1 1.1 join_halves.1
  (108 shorter events, 12.4 us)
Async XLA Ops:
  0.0 25.9 %copy-start.2 = (f32[1,512]{1,0:T(1,128)S(1)}, f32[1,512]{1,0:T(1,128)}, u32[]{:S(2)}) copy-start(f32[1,512]{1,0:T(1,128)} %refs_1_.1) | copy-start | bytes 6148
  0.0 25.9 %copy-start.3 = (s32[4]{0:T(128)S(1)}, s32[4]{0:T(128)}, u32[]{:S(2)}) copy-start(s32[4]{0:T(128)} %refs_0_.8) | copy-start | bytes 52
  0.0 25.9 %collective-permute-start = (bf16[512,4096]{1,0:T(8,128)(2,1)}, bf16[512,4096]{1,0:T(8,128)(2,1)}, u32[]{:S(2)}, u32[]{:S(2)}) collective-permute-start(bf16[512,4096]{1,0:T(8,128)(2,1)} %refs_0_.10), channel_id=1, source_target_pairs={{0,4},{4,0},{8,12},{12,8},{16,20},{20,16},{24,28},{28,24},{1,5},{5... | collective-permute-start | bytes 12582920 | tf_op jit(solution)/shard_map/ppermute | solution.py:515
  0.5 26.2 %copy-start = (bf16[512,4096]{1,0:T(8,128)(2,1)S(1)}, bf16[512,4096]{1,0:T(8,128)(2,1)}, u32[]{:S(2)}) copy-start(bf16[512,4096]{1,0:T(8,128)(2,1)} %refs_0_.10) | copy-start | bytes 12582916
  1.9 6.1 %collective-permute-start.2 = (bf16[512,512]{1,0:T(8,128)(2,1)S(1)}, bf16[512,512]{1,0:T(8,128)(2,1)S(1)}, u32[]{:S(2)}, u32[]{:S(2)}) collective-permute-start(bf16[512,512]{1,0:T(8,128)(2,1)S(1)} %get-tuple-element.75), channel_id=1, source_target_pairs={{0,4},{4,0},{8,12},{12,8},{16,20},{20,16},{24,28},{28,24},{1,5},{5... | collective-permute-start | bytes 1572872 | tf_op jit(solution)/shard_map/ppermute | solution.py:515
  2.0 11.7 %collective-permute-start.4 = (bf16[512,512]{1,0:T(8,128)(2,1)S(1)}, bf16[512,512]{1,0:T(8,128)(2,1)S(1)}, u32[]{:S(2)}, u32[]{:S(2)}) collective-permute-start(bf16[512,512]{1,0:T(8,128)(2,1)S(1)} %get-tuple-element.76.refs_2_), channel_id=1, source_target_pairs={{0,8},{4,20},{8,0},{12,28},{16,24},{20,4},{24,16},{28,12},{1,9},{5... | collective-permute-start | bytes 1572872 | tf_op jit(solution)/shard_map/ppermute | solution.py:52
  8.0 14.9 %collective-permute-start.5 = (bf16[512,512]{1,0:T(8,128)(2,1)S(1)}, bf16[512,512]{1,0:T(8,128)(2,1)S(1)}, u32[]{:S(2)}, u32[]{:S(2)}) collective-permute-start(bf16[512,512]{1,0:T(8,128)(2,1)S(1)} %collective-permute-done.2.refs_3_), channel_id=1, source_target_pairs={{0,8},{4,20},{8,0},{12,28},{16,24},{20,4},{24,16},{28,12},{1,9},{5... | collective-permute-start | bytes 1572872 | tf_op jit(solution)/shard_map/ppermute | solution.py:52
  10.9 19.2 %collective-permute-start.1 = (bf16[512,512]{1,0:T(8,128)(2,1)S(1)}, bf16[512,512]{1,0:T(8,128)(2,1)S(1)}, u32[]{:S(2)}, u32[]{:S(2)}) collective-permute-start(bf16[512,512]{1,0:T(8,128)(2,1)S(1)} %get-tuple-element.76.refs_2_), channel_id=1, source_target_pairs={{0,16},{4,12},{8,24},{12,4},{16,0},{20,28},{24,8},{28,20},{1,17},{... | collective-permute-start | bytes 1572872 | tf_op jit(solution)/shard_map/ppermute | solution.py:52
  13.7 18.8 %collective-permute-start.6 = (bf16[512,512]{1,0:T(8,128)(2,1)S(1)}, bf16[512,512]{1,0:T(8,128)(2,1)S(1)}, u32[]{:S(2)}, u32[]{:S(2)}) collective-permute-start(bf16[512,512]{1,0:T(8,128)(2,1)S(1)} %get-tuple-element.73), channel_id=1, source_target_pairs={{0,4},{4,0},{8,12},{12,8},{16,20},{20,16},{24,28},{28,24},{1,5},{5... | collective-permute-start | bytes 1572872 | tf_op jit(solution)/shard_map/ppermute | solution.py:515
  13.7 16.4 %collective-permute-start.3 = (bf16[512,512]{1,0:T(8,128)(2,1)S(1)}, bf16[512,512]{1,0:T(8,128)(2,1)S(1)}, u32[]{:S(2)}, u32[]{:S(2)}) collective-permute-start(bf16[512,512]{1,0:T(8,128)(2,1)S(1)} %collective-permute-done.2.refs_3_), channel_id=1, source_target_pairs={{0,16},{4,12},{8,24},{12,4},{16,0},{20,28},{24,8},{28,20},{1,17},{... | collective-permute-start | bytes 1572872 | tf_op jit(solution)/shard_map/ppermute | solution.py:52
  22.8 11.5 %collective-permute-start.7 = (bf16[512,512]{1,0:T(8,128)(2,1)S(1)}, bf16[512,512]{1,0:T(8,128)(2,1)S(1)}, u32[]{:S(2)}, u32[]{:S(2)}) collective-permute-start(bf16[512,512]{1,0:T(8,128)(2,1)S(1)} %collective-permute-done.4.refs_4_), channel_id=1, source_target_pairs={{0,16},{4,12},{8,24},{12,4},{16,0},{20,28},{24,8},{28,20},{1,17},{... | collective-permute-start | bytes 1572872 | tf_op jit(solution)/shard_map/ppermute | solution.py:52
  25.9 14.1 %collective-permute-start.8 = (bf16[512,512]{1,0:T(8,128)(2,1)S(1)}, bf16[512,512]{1,0:T(8,128)(2,1)S(1)}, u32[]{:S(2)}, u32[]{:S(2)}) collective-permute-start(bf16[512,512]{1,0:T(8,128)(2,1)S(1)} %collective-permute-done.5.refs_5_), channel_id=1, source_target_pairs={{0,16},{4,12},{8,24},{12,4},{16,0},{20,28},{24,8},{28,20},{1,17},{... | collective-permute-start | bytes 1572872 | tf_op jit(solution)/shard_map/ppermute | solution.py:52
  30.1 57.6 %slice-start.4 = ((s8[8388608]{0:T(1024)(128)(4,1)}), s8[4194304]{0:T(1024)(128)(4,1)S(1)}, s32[]{:S(2)}) async-start(s8[8388608]{0:T(1024)(128)(4,1)} %bitcast.46), calls=%async_computation.4 | async-start | bytes 8388608
  40.0 47.8 %slice-start.2 = ((s8[8388608]{0:T(1024)(128)(4,1)}), s8[4194304]{0:T(1024)(128)(4,1)S(1)}, s32[]{:S(2)}) async-start(s8[8388608]{0:T(1024)(128)(4,1)} %bitcast.42), calls=%async_computation.2 | async-start | bytes 8388608
  40.0 47.8 %slice-start.5 = ((s8[8388608]{0:T(1024)(128)(4,1)}), s8[4194304]{0:T(1024)(128)(4,1)S(1)}, s32[]{:S(2)}) async-start(s8[8388608]{0:T(1024)(128)(4,1)} %bitcast.46), calls=%async_computation.5 | async-start | bytes 8388608
  42.0 6.4 %collective-permute-start.9 = (bf16[4,64,512]{2,1,0:T(8,128)(2,1)S(1)}, bf16[4,64,512]{2,1,0:T(8,128)(2,1)S(1)}, u32[]{:S(2)}, u32[]{:S(2)}) collective-permute-start(bf16[4,64,512]{2,1,0:T(8,128)(2,1)S(1)} %get-tuple-element.44), channel_id=1, source_target_pairs={{0,16},{4,12},{8,24},{12,4},{16,0},{20,28},{24,8},{28,20},{1,17},{... | collective-permute-start | bytes 786440 | tf_op jit(solution)/shard_map/ppermute | solution.py:52
  43.9 8.9 %collective-permute-start.12 = (bf16[4,64,512]{2,1,0:T(8,128)(2,1)S(1)}, bf16[4,64,512]{2,1,0:T(8,128)(2,1)S(1)}, u32[]{:S(2)}, u32[]{:S(2)}) collective-permute-start(bf16[4,64,512]{2,1,0:T(8,128)(2,1)S(1)} %get-tuple-element.50), channel_id=1, source_target_pairs={{0,16},{4,12},{8,24},{12,4},{16,0},{20,28},{24,8},{28,20},{1,17},{... | collective-permute-start | bytes 786440 | tf_op jit(solution)/shard_map/ppermute | solution.py:52
  48.5 39.2 %slice-start.3 = ((s8[8388608]{0:T(1024)(128)(4,1)}), s8[4194304]{0:T(1024)(128)(4,1)S(1)}, s32[]{:S(2)}) async-start(s8[8388608]{0:T(1024)(128)(4,1)} %bitcast.42), calls=%async_computation.3 | async-start | bytes 8388608
  48.6 8.4 %collective-permute-start.13 = (bf16[4,64,512]{2,1,0:T(8,128)(2,1)S(1)}, bf16[4,64,512]{2,1,0:T(8,128)(2,1)S(1)}, u32[]{:S(2)}, u32[]{:S(2)}) collective-permute-start(bf16[4,64,512]{2,1,0:T(8,128)(2,1)S(1)} %add_terms.9.refs_2_), channel_id=1, source_target_pairs={{0,8},{4,20},{8,0},{12,28},{16,24},{20,4},{24,16},{28,12},{1,9},{5... | collective-permute-start | bytes 786440 | tf_op jit(solution)/shard_map/ppermute | solution.py:52
  51.2 14.0 %collective-permute-start.11 = (bf16[4,64,512]{2,1,0:T(8,128)(2,1)S(1)}, bf16[4,64,512]{2,1,0:T(8,128)(2,1)S(1)}, u32[]{:S(2)}, u32[]{:S(2)}) collective-permute-start(bf16[4,64,512]{2,1,0:T(8,128)(2,1)S(1)} %get-tuple-element.49), channel_id=1, source_target_pairs={{0,16},{4,12},{8,24},{12,4},{16,0},{20,28},{24,8},{28,20},{1,17},{... | collective-permute-start | bytes 786440 | tf_op jit(solution)/shard_map/ppermute | solution.py:52
  57.1 9.8 %collective-permute-start.15 = (bf16[64,512]{1,0:T(8,128)(2,1)S(1)}, bf16[64,512]{1,0:T(8,128)(2,1)S(1)}, u32[]{:S(2)}, u32[]{:S(2)}) collective-permute-start(bf16[64,512]{1,0:T(8,128)(2,1)S(1)} %get-tuple-element.91), channel_id=1, source_target_pairs={{0,1},{1,2},{2,3},{3,0},{4,5},{5,6},{6,7},{7,4},{8,9},{9,10},{10,1... | collective-permute-start | bytes 196616 | tf_op jit(solution)/shard_map/ppermute | solution.py:107
  59.2 7.6 %collective-permute-start.16 = (bf16[64,512]{1,0:T(8,128)(2,1)S(1)}, bf16[64,512]{1,0:T(8,128)(2,1)S(1)}, u32[]{:S(2)}, u32[]{:S(2)}) collective-permute-start(bf16[64,512]{1,0:T(8,128)(2,1)S(1)} %get-tuple-element.90), channel_id=1, source_target_pairs={{0,2},{1,3},{2,0},{3,1},{4,6},{5,7},{6,4},{7,5},{8,10},{9,11},{10,... | collective-permute-start | bytes 196616 | tf_op jit(solution)/shard_map/ppermute | solution.py:107
  61.8 5.1 %collective-permute-start.17 = (bf16[64,512]{1,0:T(8,128)(2,1)S(1)}, bf16[64,512]{1,0:T(8,128)(2,1)S(1)}, u32[]{:S(2)}, u32[]{:S(2)}) collective-permute-start(bf16[64,512]{1,0:T(8,128)(2,1)S(1)} %get-tuple-element.89), channel_id=1, source_target_pairs={{0,3},{1,0},{2,1},{3,2},{4,7},{5,4},{6,5},{7,6},{8,11},{9,8},{10,9... | collective-permute-start | bytes 196616 | tf_op jit(solution)/shard_map/ppermute | solution.py:107
  63.1 9.0 %collective-permute-start.10 = (bf16[4,64,512]{2,1,0:T(8,128)(2,1)S(1)}, bf16[4,64,512]{2,1,0:T(8,128)(2,1)S(1)}, u32[]{:S(2)}, u32[]{:S(2)}) collective-permute-start(bf16[4,64,512]{2,1,0:T(8,128)(2,1)S(1)} %get-tuple-element.47), channel_id=1, source_target_pairs={{0,16},{4,12},{8,24},{12,4},{16,0},{20,28},{24,8},{28,20},{1,17},{... | collective-permute-start | bytes 786440 | tf_op jit(solution)/shard_map/ppermute | solution.py:52
  65.3 6.8 %collective-permute-start.14 = (bf16[4,64,512]{2,1,0:T(8,128)(2,1)S(1)}, bf16[4,64,512]{2,1,0:T(8,128)(2,1)S(1)}, u32[]{:S(2)}, u32[]{:S(2)}) collective-permute-start(bf16[4,64,512]{2,1,0:T(8,128)(2,1)S(1)} %add_terms.11.refs_4_), channel_id=1, source_target_pairs={{0,8},{4,20},{8,0},{12,28},{16,24},{20,4},{24,16},{28,12},{1,9},{5... | collective-permute-start | bytes 786440 | tf_op jit(solution)/shard_map/ppermute | solution.py:52
  66.9 7.8 %collective-permute-start.24 = (bf16[4,64,512]{2,1,0:T(8,128)(2,1)S(1)}, bf16[4,64,512]{2,1,0:T(8,128)(2,1)S(1)}, u32[]{:S(2)}, u32[]{:S(2)}) collective-permute-start(bf16[4,64,512]{2,1,0:T(8,128)(2,1)S(1)} %stack_planes.6.refs_3_.refs_0_), channel_id=1, source_target_pairs={{0,8},{4,20},{8,0},{12,28},{16,24},{20,4},{24,16},{28,12},{1,9},{5... | collective-permute-start | bytes 786440 | tf_op jit(solution)/shard_map/ppermute | solution.py:52
  67.6 15.8 %collective-permute-start.25 = (bf16[4,64,512]{2,1,0:T(8,128)(2,1)S(1)}, bf16[4,64,512]{2,1,0:T(8,128)(2,1)S(1)}, u32[]{:S(2)}, u32[]{:S(2)}) collective-permute-start(bf16[4,64,512]{2,1,0:T(8,128)(2,1)S(1)} %stack_planes.6.refs_3_.refs_0_), channel_id=1, source_target_pairs={{0,16},{4,12},{8,24},{12,4},{16,0},{20,28},{24,8},{28,20},{1,17},{... | collective-permute-start | bytes 786440 | tf_op jit(solution)/shard_map/ppermute | solution.py:52
  74.7 8.8 %collective-permute-start.26 = (bf16[4,64,512]{2,1,0:T(8,128)(2,1)S(1)}, bf16[4,64,512]{2,1,0:T(8,128)(2,1)S(1)}, u32[]{:S(2)}, u32[]{:S(2)}) collective-permute-start(bf16[4,64,512]{2,1,0:T(8,128)(2,1)S(1)} %collective-permute-done.24.refs_1_), channel_id=1, source_target_pairs={{0,16},{4,12},{8,24},{12,4},{16,0},{20,28},{24,8},{28,20},{1,17},{... | collective-permute-start | bytes 786440 | tf_op jit(solution)/shard_map/ppermute | solution.py:52
  75.2 6.2 %collective-permute-start.18 = (bf16[64,512]{1,0:T(8,128)(2,1)S(1)}, bf16[64,512]{1,0:T(8,128)(2,1)S(1)}, u32[]{:S(2)}, u32[]{:S(2)}) collective-permute-start(bf16[64,512]{1,0:T(8,128)(2,1)S(1)} %get-tuple-element.87), channel_id=1, source_target_pairs={{0,1},{1,2},{2,3},{3,0},{4,5},{5,6},{6,7},{7,4},{8,9},{9,10},{10,1... | collective-permute-start | bytes 196616 | tf_op jit(solution)/shard_map/ppermute | solution.py:107
  76.1 6.7 %collective-permute-start.19 = (bf16[64,512]{1,0:T(8,128)(2,1)S(1)}, bf16[64,512]{1,0:T(8,128)(2,1)S(1)}, u32[]{:S(2)}, u32[]{:S(2)}) collective-permute-start(bf16[64,512]{1,0:T(8,128)(2,1)S(1)} %get-tuple-element.86), channel_id=1, source_target_pairs={{0,2},{1,3},{2,0},{3,1},{4,6},{5,7},{6,4},{7,5},{8,10},{9,11},{10,... | collective-permute-start | bytes 196616 | tf_op jit(solution)/shard_map/ppermute | solution.py:107
  79.1 4.3 %collective-permute-start.20 = (bf16[64,512]{1,0:T(8,128)(2,1)S(1)}, bf16[64,512]{1,0:T(8,128)(2,1)S(1)}, u32[]{:S(2)}, u32[]{:S(2)}) collective-permute-start(bf16[64,512]{1,0:T(8,128)(2,1)S(1)} %get-tuple-element.85), channel_id=1, source_target_pairs={{0,3},{1,0},{2,1},{3,2},{4,7},{5,4},{6,5},{7,6},{8,11},{9,8},{10,9... | collective-permute-start | bytes 196616 | tf_op jit(solution)/shard_map/ppermute | solution.py:107
  83.5 9.0 %slice-start = ((s8[8388608]{0:T(1024)(128)(4,1)}), s8[4194304]{0:T(1024)(128)(4,1)S(1)}, s32[]{:S(2)}) async-start(s8[8388608]{0:T(1024)(128)(4,1)} %bitcast.36), calls=%async_computation | async-start | bytes 8388608
  83.6 4.2 %collective-permute-start.27 = (bf16[4,4,64,512]{3,2,1,0:T(8,128)(2,1)S(1)}, bf16[4,4,64,512]{3,2,1,0:T(8,128)(2,1)S(1)}, u32[]{:S(2)}, u32[]{:S(2)}) collective-permute-start(bf16[4,4,64,512]{3,2,1,0:T(8,128)(2,1)S(1)} %stack_planes.8.refs_0_.refs_4_), channel_id=1, source_target_pairs={{0,4},{4,0},{8,12},{12,8},{16,20},{20,16},{24,28},{28,24},{1,5},{5... | collective-permute-start | bytes 3145736 | tf_op jit(solution)/shard_map/ppermute | solution.py:515
  83.6 11.4 %collective-permute-start.21 = (bf16[4,64,512]{2,1,0:T(8,128)(2,1)S(1)}, bf16[4,64,512]{2,1,0:T(8,128)(2,1)S(1)}, u32[]{:S(2)}, u32[]{:S(2)}) collective-permute-start(bf16[4,64,512]{2,1,0:T(8,128)(2,1)S(1)} %stack_planes.7.refs_4_.refs_0_), channel_id=1, source_target_pairs={{0,8},{4,20},{8,0},{12,28},{16,24},{20,4},{24,16},{28,12},{1,9},{5... | collective-permute-start | bytes 786440 | tf_op jit(solution)/shard_map/ppermute | solution.py:99
  85.8 9.3 %collective-permute-start.22 = (bf16[4,64,512]{2,1,0:T(8,128)(2,1)S(1)}, bf16[4,64,512]{2,1,0:T(8,128)(2,1)S(1)}, u32[]{:S(2)}, u32[]{:S(2)}) collective-permute-start(bf16[4,64,512]{2,1,0:T(8,128)(2,1)S(1)} %stack_planes.7.refs_4_.refs_0_), channel_id=1, source_target_pairs={{0,16},{4,12},{8,24},{12,4},{16,0},{20,28},{24,8},{28,20},{1,17},{... | collective-permute-start | bytes 786440 | tf_op jit(solution)/shard_map/ppermute | solution.py:99
  87.7 12.0 %collective-permute-start.23 = (bf16[4,64,512]{2,1,0:T(8,128)(2,1)S(1)}, bf16[4,64,512]{2,1,0:T(8,128)(2,1)S(1)}, u32[]{:S(2)}, u32[]{:S(2)}) collective-permute-start(bf16[4,64,512]{2,1,0:T(8,128)(2,1)S(1)} %stack_planes.7.refs_4_.refs_0_), channel_id=1, source_target_pairs={{0,24},{4,28},{8,16},{12,20},{16,8},{20,12},{24,0},{28,4},{1,25},{... | collective-permute-start | bytes 786440 | tf_op jit(solution)/shard_map/ppermute | solution.py:99
  99.8 5.7 %collective-permute-start.28 = (bf16[4,4,64,512]{3,2,1,0:T(8,128)(2,1)S(1)}, bf16[4,4,64,512]{3,2,1,0:T(8,128)(2,1)S(1)}, u32[]{:S(2)}, u32[]{:S(2)}) collective-permute-start(bf16[4,4,64,512]{3,2,1,0:T(8,128)(2,1)S(1)} %stack_planes.9.refs_4_.refs_0_), channel_id=1, source_target_pairs={{0,4},{4,0},{8,12},{12,8},{16,20},{20,16},{24,28},{28,24},{1,5},{5... | collective-permute-start | bytes 3145736 | tf_op jit(solution)/shard_map/ppermute | solution.py:515
  99.8 3.0 %collective-permute-start.29 = (bf16[4,64,512]{2,1,0:T(8,128)(2,1)S(1)}, bf16[4,64,512]{2,1,0:T(8,128)(2,1)S(1)}, u32[]{:S(2)}, u32[]{:S(2)}) collective-permute-start(bf16[4,64,512]{2,1,0:T(8,128)(2,1)S(1)} %get-tuple-element.54), channel_id=1, source_target_pairs={{0,4},{4,0},{8,12},{12,8},{16,20},{20,16},{24,28},{28,24},{1,5},{5... | collective-permute-start | bytes 786440 | tf_op jit(solution)/shard_map/ppermute | solution.py:515
  100.3 2.9 %collective-permute-start.30 = (bf16[4,64,512]{2,1,0:T(8,128)(2,1)S(1)}, bf16[4,64,512]{2,1,0:T(8,128)(2,1)S(1)}, u32[]{:S(2)}, u32[]{:S(2)}) collective-permute-start(bf16[4,64,512]{2,1,0:T(8,128)(2,1)S(1)} %get-tuple-element.56), channel_id=1, source_target_pairs={{0,4},{4,0},{8,12},{12,8},{16,20},{20,16},{24,28},{28,24},{1,5},{5... | collective-permute-start | bytes 786440 | tf_op jit(solution)/shard_map/ppermute | solution.py:515
  100.4 9.7 %collective-permute-start.31 = (bf16[4,64,512]{2,1,0:T(8,128)(2,1)S(1)}, bf16[4,64,512]{2,1,0:T(8,128)(2,1)S(1)}, u32[]{:S(2)}, u32[]{:S(2)}) collective-permute-start(bf16[4,64,512]{2,1,0:T(8,128)(2,1)S(1)} %get-tuple-element.59), channel_id=1, source_target_pairs={{0,4},{4,0},{8,12},{12,8},{16,20},{20,16},{24,28},{28,24},{1,5},{5... | collective-permute-start | bytes 786440 | tf_op jit(solution)/shard_map/ppermute | solution.py:515
  103.4 6.8 %collective-permute-start.32 = (bf16[4,64,512]{2,1,0:T(8,128)(2,1)S(1)}, bf16[4,64,512]{2,1,0:T(8,128)(2,1)S(1)}, u32[]{:S(2)}, u32[]{:S(2)}) collective-permute-start(bf16[4,64,512]{2,1,0:T(8,128)(2,1)S(1)} %get-tuple-element.60), channel_id=1, source_target_pairs={{0,16},{4,12},{8,24},{12,4},{16,0},{20,28},{24,8},{28,20},{1,17},{... | collective-permute-start | bytes 786440 | tf_op jit(solution)/shard_map/ppermute | solution.py:52
  103.4 10.4 %collective-permute-start.37 = (bf16[4,64,512]{2,1,0:T(8,128)(2,1)S(1)}, bf16[4,64,512]{2,1,0:T(8,128)(2,1)S(1)}, u32[]{:S(2)}, u32[]{:S(2)}) collective-permute-start(bf16[4,64,512]{2,1,0:T(8,128)(2,1)S(1)} %get-tuple-element.51.refs_3_), channel_id=1, source_target_pairs={{0,4},{4,0},{8,12},{12,8},{16,20},{20,16},{24,28},{28,24},{1,5},{5... | collective-permute-start | bytes 786440 | tf_op jit(solution)/shard_map/ppermute | solution.py:515
  105.0 8.9 %collective-permute-start.38 = (bf16[4,64,512]{2,1,0:T(8,128)(2,1)S(1)}, bf16[4,64,512]{2,1,0:T(8,128)(2,1)S(1)}, u32[]{:S(2)}, u32[]{:S(2)}) collective-permute-start(bf16[4,64,512]{2,1,0:T(8,128)(2,1)S(1)} %get-tuple-element.57.refs_4_), channel_id=1, source_target_pairs={{0,16},{4,12},{8,24},{12,4},{16,0},{20,28},{24,8},{28,20},{1,17},{... | collective-permute-start | bytes 786440 | tf_op jit(solution)/shard_map/ppermute | solution.py:52
  111.5 6.4 %collective-permute-start.39 = (bf16[4,64,512]{2,1,0:T(8,128)(2,1)S(1)}, bf16[4,64,512]{2,1,0:T(8,128)(2,1)S(1)}, u32[]{:S(2)}, u32[]{:S(2)}) collective-permute-start(bf16[4,64,512]{2,1,0:T(8,128)(2,1)S(1)} %add_terms.14.refs_3_), channel_id=1, source_target_pairs={{0,8},{4,20},{8,0},{12,28},{16,24},{20,4},{24,16},{28,12},{1,9},{5... | collective-permute-start | bytes 786440 | tf_op jit(solution)/shard_map/ppermute | solution.py:52
  113.4 4.8 %collective-permute-start.33 = (bf16[4,64,512]{2,1,0:T(8,128)(2,1)S(1)}, bf16[4,64,512]{2,1,0:T(8,128)(2,1)S(1)}, u32[]{:S(2)}, u32[]{:S(2)}) collective-permute-start(bf16[4,64,512]{2,1,0:T(8,128)(2,1)S(1)} %get-tuple-element.61.refs_3_), channel_id=1, source_target_pairs={{0,4},{4,0},{8,12},{12,8},{16,20},{20,16},{24,28},{28,24},{1,5},{5... | collective-permute-start | bytes 786440 | tf_op jit(solution)/shard_map/ppermute | solution.py:515
  113.4 4.8 %collective-permute-start.34 = (bf16[4,64,512]{2,1,0:T(8,128)(2,1)S(1)}, bf16[4,64,512]{2,1,0:T(8,128)(2,1)S(1)}, u32[]{:S(2)}, u32[]{:S(2)}) collective-permute-start(bf16[4,64,512]{2,1,0:T(8,128)(2,1)S(1)} %get-tuple-element.64), channel_id=1, source_target_pairs={{0,4},{4,0},{8,12},{12,8},{16,20},{20,16},{24,28},{28,24},{1,5},{5... | collective-permute-start | bytes 786440 | tf_op jit(solution)/shard_map/ppermute | solution.py:515
  113.9 4.3 %collective-permute-start.35 = (bf16[4,64,512]{2,1,0:T(8,128)(2,1)S(1)}, bf16[4,64,512]{2,1,0:T(8,128)(2,1)S(1)}, u32[]{:S(2)}, u32[]{:S(2)}) collective-permute-start(bf16[4,64,512]{2,1,0:T(8,128)(2,1)S(1)} %get-tuple-element.66), channel_id=1, source_target_pairs={{0,4},{4,0},{8,12},{12,8},{16,20},{20,16},{24,28},{28,24},{1,5},{5... | collective-permute-start | bytes 786440 | tf_op jit(solution)/shard_map/ppermute | solution.py:515
  113.9 4.3 %collective-permute-start.36 = (bf16[4,64,512]{2,1,0:T(8,128)(2,1)S(1)}, bf16[4,64,512]{2,1,0:T(8,128)(2,1)S(1)}, u32[]{:S(2)}, u32[]{:S(2)}) collective-permute-start(bf16[4,64,512]{2,1,0:T(8,128)(2,1)S(1)} %get-tuple-element.68), channel_id=1, source_target_pairs={{0,4},{4,0},{8,12},{12,8},{16,20},{20,16},{24,28},{28,24},{1,5},{5... | collective-permute-start | bytes 786440 | tf_op jit(solution)/shard_map/ppermute | solution.py:515
  118.4 9.2 %collective-permute-start.40 = (bf16[4,64,512]{2,1,0:T(8,128)(2,1)S(1)}, bf16[4,64,512]{2,1,0:T(8,128)(2,1)S(1)}, u32[]{:S(2)}, u32[]{:S(2)}) collective-permute-start(bf16[4,64,512]{2,1,0:T(8,128)(2,1)S(1)} %get-tuple-element.70), channel_id=1, source_target_pairs={{0,8},{4,20},{8,0},{12,28},{16,24},{20,4},{24,16},{28,12},{1,9},{5... | collective-permute-start | bytes 786440 | tf_op jit(solution)/shard_map/ppermute | solution.py:99
  120.2 9.9 %collective-permute-start.41 = (bf16[4,64,512]{2,1,0:T(8,128)(2,1)S(1)}, bf16[4,64,512]{2,1,0:T(8,128)(2,1)S(1)}, u32[]{:S(2)}, u32[]{:S(2)}) collective-permute-start(bf16[4,64,512]{2,1,0:T(8,128)(2,1)S(1)} %get-tuple-element.71), channel_id=1, source_target_pairs={{0,16},{4,12},{8,24},{12,4},{16,0},{20,28},{24,8},{28,20},{1,17},{... | collective-permute-start | bytes 786440 | tf_op jit(solution)/shard_map/ppermute | solution.py:99
  120.4 12.5 %collective-permute-start.42 = (bf16[4,64,512]{2,1,0:T(8,128)(2,1)S(1)}, bf16[4,64,512]{2,1,0:T(8,128)(2,1)S(1)}, u32[]{:S(2)}, u32[]{:S(2)}) collective-permute-start(bf16[4,64,512]{2,1,0:T(8,128)(2,1)S(1)} %get-tuple-element.72), channel_id=1, source_target_pairs={{0,24},{4,28},{8,16},{12,20},{16,8},{20,12},{24,0},{28,4},{1,25},{... | collective-permute-start | bytes 786440 | tf_op jit(solution)/shard_map/ppermute | solution.py:99
  122.0 11.1 %collective-permute-start.46 = (bf16[64,512]{1,0:T(8,128)(2,1)S(1)}, bf16[64,512]{1,0:T(8,128)(2,1)S(1)}, u32[]{:S(2)}, u32[]{:S(2)}) collective-permute-start(bf16[64,512]{1,0:T(8,128)(2,1)S(1)} %get-tuple-element.79), channel_id=1, source_target_pairs={{0,1},{1,2},{2,3},{3,0},{4,5},{5,6},{6,7},{7,4},{8,9},{9,10},{10,1... | collective-permute-start | bytes 196616 | tf_op jit(solution)/shard_map/ppermute | solution.py:107
  122.6 10.4 %collective-permute-start.47 = (bf16[64,512]{1,0:T(8,128)(2,1)S(1)}, bf16[64,512]{1,0:T(8,128)(2,1)S(1)}, u32[]{:S(2)}, u32[]{:S(2)}) collective-permute-start(bf16[64,512]{1,0:T(8,128)(2,1)S(1)} %get-tuple-element.78), channel_id=1, source_target_pairs={{0,2},{1,3},{2,0},{3,1},{4,6},{5,7},{6,4},{7,5},{8,10},{9,11},{10,... | collective-permute-start | bytes 196616 | tf_op jit(solution)/shard_map/ppermute | solution.py:107
  127.7 5.4 %collective-permute-start.48 = (bf16[64,512]{1,0:T(8,128)(2,1)S(1)}, bf16[64,512]{1,0:T(8,128)(2,1)S(1)}, u32[]{:S(2)}, u32[]{:S(2)}) collective-permute-start(bf16[64,512]{1,0:T(8,128)(2,1)S(1)} %get-tuple-element.77), channel_id=1, source_target_pairs={{0,3},{1,0},{2,1},{3,2},{4,7},{5,4},{6,5},{7,6},{8,11},{9,8},{10,9... | collective-permute-start | bytes 196616 | tf_op jit(solution)/shard_map/ppermute | solution.py:107
  133.1 6.4 %collective-permute-start.52 = (bf16[4,64,512]{2,1,0:T(8,128)(2,1)S(1)}, bf16[4,64,512]{2,1,0:T(8,128)(2,1)S(1)}, u32[]{:S(2)}, u32[]{:S(2)}) collective-permute-start(bf16[4,64,512]{2,1,0:T(8,128)(2,1)S(1)} %stack_planes.10.refs_4_.refs_1_), channel_id=1, source_target_pairs={{0,8},{4,20},{8,0},{12,28},{16,24},{20,4},{24,16},{28,12},{1,9},{5... | collective-permute-start | bytes 786440 | tf_op jit(solution)/shard_map/ppermute | solution.py:52
  134.2 7.4 %collective-permute-start.43 = (bf16[64,512]{1,0:T(8,128)(2,1)S(1)}, bf16[64,512]{1,0:T(8,128)(2,1)S(1)}, u32[]{:S(2)}, u32[]{:S(2)}) collective-permute-start(bf16[64,512]{1,0:T(8,128)(2,1)S(1)} %get-tuple-element.83), channel_id=1, source_target_pairs={{0,1},{1,2},{2,3},{3,0},{4,5},{5,6},{6,7},{7,4},{8,9},{9,10},{10,1... | collective-permute-start | bytes 196616 | tf_op jit(solution)/shard_map/ppermute | solution.py:107
  134.8 8.4 %collective-permute-start.44 = (bf16[64,512]{1,0:T(8,128)(2,1)S(1)}, bf16[64,512]{1,0:T(8,128)(2,1)S(1)}, u32[]{:S(2)}, u32[]{:S(2)}) collective-permute-start(bf16[64,512]{1,0:T(8,128)(2,1)S(1)} %get-tuple-element.82), channel_id=1, source_target_pairs={{0,2},{1,3},{2,0},{3,1},{4,6},{5,7},{6,4},{7,5},{8,10},{9,11},{10,... | collective-permute-start | bytes 196616 | tf_op jit(solution)/shard_map/ppermute | solution.py:107
  138.7 4.7 %collective-permute-start.45 = (bf16[64,512]{1,0:T(8,128)(2,1)S(1)}, bf16[64,512]{1,0:T(8,128)(2,1)S(1)}, u32[]{:S(2)}, u32[]{:S(2)}) collective-permute-start(bf16[64,512]{1,0:T(8,128)(2,1)S(1)} %get-tuple-element.81), channel_id=1, source_target_pairs={{0,3},{1,0},{2,1},{3,2},{4,7},{5,4},{6,5},{7,6},{8,11},{9,8},{10,9... | collective-permute-start | bytes 196616 | tf_op jit(solution)/shard_map/ppermute | solution.py:107
  138.7 8.3 %collective-permute-start.53 = (bf16[4,64,512]{2,1,0:T(8,128)(2,1)S(1)}, bf16[4,64,512]{2,1,0:T(8,128)(2,1)S(1)}, u32[]{:S(2)}, u32[]{:S(2)}) collective-permute-start(bf16[4,64,512]{2,1,0:T(8,128)(2,1)S(1)} %stack_planes.10.refs_4_.refs_1_), channel_id=1, source_target_pairs={{0,16},{4,12},{8,24},{12,4},{16,0},{20,28},{24,8},{28,20},{1,17},{... | collective-permute-start | bytes 786440 | tf_op jit(solution)/shard_map/ppermute | solution.py:52
  139.5 11.1 %collective-permute-start.54 = (bf16[4,64,512]{2,1,0:T(8,128)(2,1)S(1)}, bf16[4,64,512]{2,1,0:T(8,128)(2,1)S(1)}, u32[]{:S(2)}, u32[]{:S(2)}) collective-permute-start(bf16[4,64,512]{2,1,0:T(8,128)(2,1)S(1)} %collective-permute-done.52.refs_2_), channel_id=1, source_target_pairs={{0,16},{4,12},{8,24},{12,4},{16,0},{20,28},{24,8},{28,20},{1,17},{... | collective-permute-start | bytes 786440 | tf_op jit(solution)/shard_map/ppermute | solution.py:52
  143.4 9.3 %collective-permute-start.49 = (bf16[4,64,512]{2,1,0:T(8,128)(2,1)S(1)}, bf16[4,64,512]{2,1,0:T(8,128)(2,1)S(1)}, u32[]{:S(2)}, u32[]{:S(2)}) collective-permute-start(bf16[4,64,512]{2,1,0:T(8,128)(2,1)S(1)} %stack_planes.11.refs_1_), channel_id=1, source_target_pairs={{0,8},{4,20},{8,0},{12,28},{16,24},{20,4},{24,16},{28,12},{1,9},{5... | collective-permute-start | bytes 786440 | tf_op jit(solution)/shard_map/ppermute | solution.py:99
  143.5 15.6 %collective-permute-start.50 = (bf16[4,64,512]{2,1,0:T(8,128)(2,1)S(1)}, bf16[4,64,512]{2,1,0:T(8,128)(2,1)S(1)}, u32[]{:S(2)}, u32[]{:S(2)}) collective-permute-start(bf16[4,64,512]{2,1,0:T(8,128)(2,1)S(1)} %stack_planes.11.refs_1_), channel_id=1, source_target_pairs={{0,16},{4,12},{8,24},{12,4},{16,0},{20,28},{24,8},{28,20},{1,17},{... | collective-permute-start | bytes 786440 | tf_op jit(solution)/shard_map/ppermute | solution.py:99
  145.0 14.1 %collective-permute-start.51 = (bf16[4,64,512]{2,1,0:T(8,128)(2,1)S(1)}, bf16[4,64,512]{2,1,0:T(8,128)(2,1)S(1)}, u32[]{:S(2)}, u32[]{:S(2)}) collective-permute-start(bf16[4,64,512]{2,1,0:T(8,128)(2,1)S(1)} %stack_planes.11.refs_1_), channel_id=1, source_target_pairs={{0,24},{4,28},{8,16},{12,20},{16,8},{20,12},{24,0},{28,4},{1,25},{... | collective-permute-start | bytes 786440 | tf_op jit(solution)/shard_map/ppermute | solution.py:99
  160.1 2.0 %collective-permute-start.55 = (bf16[8,64,512]{2,1,0:T(8,128)(2,1)S(1)}, bf16[8,64,512]{2,1,0:T(8,128)(2,1)S(1)}, u32[]{:S(2)}, u32[]{:S(2)}) collective-permute-start(bf16[8,64,512]{2,1,0:T(8,128)(2,1)S(1)} %add_expert_rows.5), channel_id=1, source_target_pairs={{0,4},{4,0},{8,12},{12,8},{16,20},{20,16},{24,28},{28,24},{1,5},{5... | collective-permute-start | bytes 1572872 | tf_op jit(solution)/shard_map/ppermute | solution.py:515
  (2 other events, 13.4 us)
